TPU v7x, 32 devices: a whole 2x2x4 slice. The times are simulated.
32 devices in a mesh: rows: 8 (over z, x), cols: 4 (over y, core).
Axes of the slice: x: 2, y: 2, z: 4, core: 2. Of those that a mesh axis runs over, the one named last changes fastest.
Arguments:
- block_list: int32 [64, 24], P('rows', 'cols'), may hold values from -1 to 63, as said below
- points: bfloat16 [16, 16384], P(None, 'rows'), may hold values from -4 to 4
- targets: float32 [32, 16384], P(None, 'rows'), may hold values from -6 to 6
Outputs:
- solution: float32 [32, 16384], P(None, 'rows')
- residual: float32 [32, 16384], P(None, 'rows')
Inputs may be any that keep to these rules, and one draw needn't show every extreme that they name: `block_list`: A non-empty entry j of block row i satisfies j <= i. Within the 6 slots of a block row held by one index of cols, the entries lie in different groups of 8 consecutive blocks. Of all slots held by one device (8 block rows of 6 slots), at most 6 name blocks of any one group of 8 consecutive blocks, and in every draw some device reaches 6.
All inputs are finite; a program needn't handle non-finite values.
Results may differ from a plain program's by a relative error of at most 0.0057.
Values may be sent and summed in bfloat16 or wider, within the bound.
No kernel may reach another device: no remote copies, remote signals or barrier semaphores. Data moves between devices by JAX's collectives and lax.ppermute only.
A program may use at most 64 MiB of HBM per device.

v0:
```python
import functools

import jax
import jax.numpy as jnp
from jax import lax
from jax.experimental import pallas as pl
from jax.experimental.pallas import tpu as pltpu
from jax.sharding import PartitionSpec as P

REG = 1.5
RADIUS = 0.25
GROUP = 4
RING = 3
STRIP = 64
LANES = 128
TINY = 1e-30
SHIFT = 0.375
DIRECT_ROWS = 8
RESIDENT_BYTES = 20 * 1024 * 1024

SMEM = pl.BlockSpec(memory_space=pltpu.SMEM)
VMEM = pl.BlockSpec(memory_space=pltpu.VMEM)
HBM = pl.BlockSpec(memory_space=pltpu.HBM)
F32 = jnp.float32
BF16 = jnp.bfloat16


def augment(x, first_ones):
    dim, n = x.shape
    norm = jnp.sum(x * x, axis=0, keepdims=True) / (RADIUS * RADIUS)
    high = norm.astype(BF16).astype(F32)
    rest = norm - high
    mid = rest.astype(BF16).astype(F32)
    low = rest - mid
    line = lax.broadcasted_iota(jnp.int32, (dim, n), 0)
    base = 3 if first_ones else 0
    ones_at = 0 if first_ones else 3
    tail = jnp.where((line >= ones_at) & (line < ones_at + 3), 1.0, 0.0)
    tail = jnp.where(line == base, high, tail)
    tail = jnp.where(line == base + 1, mid, tail)
    tail = jnp.where(line == base + 2, low, tail)
    return tail


def each_piece(pieces, row, visit):
    if len(pieces) == 1:

        def one(r, carry):
            visit(r, lambda *at: pieces[0][(r,) + at])
            return carry

        lax.fori_loop(0, pieces[0].shape[0], one, 0)
    else:
        for parity, ref in enumerate(pieces):
            for k in range(ref.shape[0]):
                visit(row ^ (2 * k + parity), lambda *at, ref=ref, k=k: ref[(k,) + at])


def build_kernel(cfg, place, direct, near_ref, *refs):
    n_pieces, nb, block_len, own_rows, block_rows, n_sub, count_rows, resident = cfg
    pieces, refs = refs[:n_pieces], refs[n_pieces:]
    k_hbm, ilist, jlist, groups, deg_ref = refs[:5]
    mlist, acc, lhs, rhs, counts_v, counts, count_sem = refs[5:12]
    kbuf, sems = (None, None) if resident else refs[12:]
    row, col = place[0], place[1]
    own_len = own_rows * block_len
    dim = near_ref.shape[0]
    scale = 1.0 / (RADIUS * RADIUS)

    def prepare(r, load):
        for k in range(own_rows):
            far = load(slice(None), slice(k * block_len, (k + 1) * block_len))
            rhs[r * own_rows + k, :dim, :] = far
            rhs[r * own_rows + k, dim:, :] = augment(far.astype(F32), False).astype(BF16)
        listed = load(slice(None), slice(own_len, own_len + LANES))
        counts_v[r] = listed.astype(F32)[:count_rows].astype(jnp.int32)

    each_piece(pieces, row, prepare)
    fetch = pltpu.make_async_copy(counts_v, counts, count_sem)
    fetch.start()
    for i in range(block_rows):
        near = near_ref[:, i * block_len:(i + 1) * block_len].astype(F32)
        full = jnp.concatenate([near * (-2.0 * scale), augment(near, True)], axis=0)
        lhs[i] = full.T.astype(BF16)
    acc[...] = jnp.zeros_like(acc)
    fetch.wait()

    def line(i, pos):
        me = row * block_rows + i

        def note(j, at):
            r, k = lax.div(j, own_rows), lax.rem(j, own_rows)
            name = r * block_rows + col * own_rows + k
            spot = k * nb + me
            mirrored = counts[r, lax.div(spot, LANES), lax.rem(spot, LANES)]
            m = direct[i, name] + jnp.where(name == me, 0, mirrored)
            ilist[at] = i
            jlist[at] = j
            mlist[at] = m
            return at + jnp.where(m > 0, 1, 0)

        return lax.fori_loop(0, n_sub, note, pos, unroll=8)

    pos = lax.fori_loop(0, block_rows, line, jnp.int32(0))
    for u in range(GROUP):
        ilist[pos + u] = 0
        jlist[pos + u] = 0
        mlist[pos + u] = 0
    total = lax.div(pos + (GROUP - 1), GROUP)
    groups[0] = total

    def copy_out(g):
        slot = lax.rem(g, RING)
        return pltpu.make_async_copy(kbuf.at[slot], k_hbm.at[g], sems.at[slot])

    def step(g, carry):
        slot, target = (g, k_hbm) if resident else (lax.rem(g, RING), kbuf)
        if not resident:

            @pl.when(g >= RING)
            def _():
                copy_out(g - RING).wait()

        for u in range(GROUP):
            i = ilist[g * GROUP + u]
            j = jlist[g * GROUP + u]
            m = mlist[g * GROUP + u].astype(F32)
            far = rhs[j]
            for s in range(block_len // STRIP):
                rows = slice(s * STRIP, (s + 1) * STRIP)
                d = jnp.dot(lhs[i, rows, :], far, preferred_element_type=F32)
                d = jnp.maximum(d, TINY)
                sc = d * lax.rsqrt(d)
                rem = jnp.maximum(1.0 - sc, 0.0)
                sq = rem * rem
                val = (sq * sq) * (sc * (4.0 * m) + m)
                target[slot, u, rows, :] = val.astype(BF16)
                half = val[:, :LANES]
                for h in range(1, block_len // LANES):
                    half = half + val[:, h * LANES:(h + 1) * LANES]
                acc[i, rows, :] += half
        if not resident:
            copy_out(g).start()
        return carry

    lax.fori_loop(0, total, step, 0)
    for i in range(block_rows):
        deg_ref[:, i * block_len:(i + 1) * block_len] = jnp.sum(acc[i].T, axis=0, keepdims=True)

    def drain(g, carry):
        copy_out(g).wait()
        return carry

    if not resident:
        lax.fori_loop(jnp.maximum(total - RING, 0), total, drain, 0)


def apply_kernel(cfg, place, ilist, jlist, groups, k_mat, *refs):
    n_pieces, n_cols, own_rows, block_len, products, resident = cfg
    pieces, refs = refs[:n_pieces], refs[n_pieces:]
    if products:
        inv_ref, t_ref, refs = refs[0], refs[1], refs[2:]
        s_refs, refs = refs[:n_cols], refs[n_cols:]
    z_refs, refs = refs[:n_cols], refs[n_cols:]
    w_all, z_acc = refs[:2]
    kbuf, sems = (None, None) if resident else refs[2:]
    row, col = place[0], place[1]
    total = groups[0]

    def copy_in(g):
        slot = lax.rem(g, RING)
        return pltpu.make_async_copy(k_mat.at[g], kbuf.at[slot], sems.at[slot])

    if not resident:
        for p in range(RING - 1):

            @pl.when(p < total)
            def _(p=p):
                copy_in(p).start()

    def place_piece(r, load):
        for k in range(own_rows):
            w_all[r * own_rows + k] = load(slice(None), slice(k * block_len, (k + 1) * block_len))

    each_piece(pieces, row, place_piece)
    z_acc[...] = jnp.zeros_like(z_acc)

    def step(g, carry):
        slot, source = (g, k_mat) if resident else (lax.rem(g, RING), kbuf)
        if not resident:

            @pl.when(g + (RING - 1) < total)
            def _():
                copy_in(g + (RING - 1)).start()

            copy_in(g).wait()
        parts = []
        for u in range(GROUP):
            parts.append(
                lax.dot_general(
                    w_all[jlist[g * GROUP + u]],
                    source[slot, u],
                    (((1,), (1,)), ((), ())),
                    preferred_element_type=F32,
                )
            )
        for u in range(GROUP):
            z_acc[ilist[g * GROUP + u]] += parts[u]
        return carry

    lax.fori_loop(0, total, step, 0)
    own_len = own_rows * block_len
    for e in range(n_cols):
        for k in range(own_rows):
            z_refs[e][:, k * block_len:(k + 1) * block_len] = z_acc[(col ^ e) * own_rows + k]
    if products:
        ts2 = jnp.zeros((t_ref.shape[0], 1), F32)
        s1s2 = jnp.zeros((t_ref.shape[0], 1), F32)
        for e in range(n_cols):
            at = pl.ds(pl.multiple_of((col ^ e) * own_len, LANES), own_len)
            scaled = z_refs[e][:, :own_len] * inv_ref[:, at]
            ts2 += jnp.sum(t_ref[:, at] * scaled, axis=1, keepdims=True)
            s1s2 += jnp.sum(s_refs[e][...] * scaled, axis=1, keepdims=True)
        t = t_ref[:, pl.ds(pl.multiple_of(col * own_len, LANES), own_len)]
        s1 = s_refs[0][...]
        tt = jnp.sum(t * t, axis=1, keepdims=True)
        ts1 = jnp.sum(t * s1, axis=1, keepdims=True)
        s1s1 = jnp.sum(s1 * s1, axis=1, keepdims=True)
        ts2 += SHIFT * ts1
        s1s2 += SHIFT * s1s1
        lane = lax.broadcasted_iota(jnp.int32, (t_ref.shape[0], LANES), 1)
        out = jnp.zeros(lane.shape, F32)
        for n, v in enumerate((tt, ts1, s1s1, ts2, s1s2)):
            out = jnp.where(lane == n, v, out)
        for e in range(n_cols):
            z_refs[e][:, own_len:] = out


def final_kernel(n_cols, place, t_ref, dots_a, dots_b, *refs):
    s1s, ends = refs[:n_cols], refs[n_cols:2 * n_cols]
    sol_ref, res_ref = refs[2 * n_cols:]
    own_len = s1s[0].shape[1]
    dots = dots_a[...] + dots_b[...]
    tt, ts1, s1s1, ts2, s1s2 = (dots[:, n:n + 1] for n in range(5))
    a1 = tt / (REG * tt + ts1)
    p = 1.0 - REG * a1
    new = p * p * tt - 2.0 * p * a1 * ts1 + a1 * a1 * s1s1
    u = p + new / tt
    dd = u * u * tt - 2.0 * u * a1 * ts1 + a1 * a1 * s1s1
    dmd = u * u * ts1 - u * a1 * (s1s1 + ts2) + a1 * a1 * s1s2
    a2 = new / (REG * dd + dmd)
    for e in range(n_cols):
        at = pl.ds(pl.multiple_of((place[1] ^ e) * own_len, LANES), own_len)
        t, s1, s2 = t_ref[:, at], s1s[e][...], ends[e][...]
        sol_ref[:, at] = (a1 + a2 * u) * t - (a2 * a1) * s1
        res_ref[:, at] = (p - a2 * REG * u) * t - (a1 + a2 * (u - REG * a1)) * s1 + (a2 * a1) * s2


def swap(x, axis, d):
    size = lax.axis_size(axis)
    return lax.ppermute(x, axis, [(i, i ^ d) for i in range(size)])


def from_cols(x):
    return [x] + [swap(x, "cols", e) for e in range(1, lax.axis_size("cols"))]


def from_rows(x):
    size = lax.axis_size("rows")
    if size > DIRECT_ROWS:
        return [lax.all_gather(x, "rows")]
    same = jnp.stack([x] + [swap(x, "rows", d) for d in range(2, size, 2)])
    return [same, swap(same, "rows", 1)]


def local(block_list, points, targets):
    n_rows = lax.axis_size("rows")
    n_cols = lax.axis_size("cols")
    row = lax.axis_index("rows")
    col = lax.axis_index("cols")
    block_rows, slots = block_list.shape
    dim, npoints = points.shape
    outputs = targets.shape[0]
    block_len = npoints // block_rows
    own_rows = block_rows // n_cols
    own_len = own_rows * block_len
    nb = block_rows * n_rows
    n_sub = own_rows * n_rows
    capacity = -(-block_rows * slots // n_rows)
    bound = min(block_rows * n_sub, n_cols * capacity * (n_rows + 1))
    n_groups = -(-bound // GROUP)
    list_len = n_groups * GROUP + GROUP
    place = jnp.stack([row, col])
    k_shape = (n_groups, GROUP, block_len, block_len)
    resident = 2 * n_groups * GROUP * block_len * block_len <= RESIDENT_BYTES
    limit = pltpu.CompilerParams(vmem_limit_bytes=24 * 1024 * 1024)
    ring = [] if resident else [
        pltpu.VMEM((RING, GROUP, block_len, block_len), BF16),
        pltpu.SemaphoreType.DMA((RING,)),
    ]
    k_spec = VMEM if resident else HBM

    def shape(*dims, dtype=F32):
        return jax.ShapeDtypeStruct(dims, dtype)

    lists = jnp.concatenate(from_cols(block_list), axis=1)
    names = jnp.arange(nb, dtype=jnp.int32)
    direct = jnp.sum((lists[:, :, None] == names).astype(jnp.int32), axis=1)
    own_counts = lax.dynamic_slice_in_dim(direct, col * own_rows, own_rows, 0)
    count_rows = -(-own_rows * nb // LANES)
    coded = own_counts.reshape(-1)
    coded = jnp.pad(coded, (0, dim * LANES - coded.shape[0])).reshape(dim, LANES).astype(BF16)
    own_points = lax.dynamic_slice_in_dim(points, col * own_len, own_len, 1)
    pieces = from_rows(jnp.concatenate([own_points, coded], axis=1))

    k_mat, ilist, jlist, groups, degree = pl.pallas_call(
        functools.partial(
            build_kernel,
                (len(pieces), nb, block_len, own_rows, block_rows, n_sub, count_rows, resident),
        ),
        out_shape=(
            pltpu.VMEM(k_shape, BF16) if resident else shape(*k_shape, dtype=BF16),
            shape(list_len, dtype=jnp.int32),
            shape(list_len, dtype=jnp.int32),
            shape(1, dtype=jnp.int32),
            shape(1, npoints),
        ),
        in_specs=[SMEM, SMEM, VMEM] + [VMEM] * len(pieces),
        out_specs=(k_spec, SMEM, SMEM, SMEM, VMEM),
        scratch_shapes=[
            pltpu.SMEM((list_len,), jnp.int32),
            pltpu.VMEM((block_rows, block_len, LANES), F32),
            pltpu.VMEM((block_rows, block_len, 2 * dim), BF16),
            pltpu.VMEM((n_sub, 2 * dim, block_len), BF16),
            pltpu.VMEM((n_rows, count_rows, LANES), jnp.int32),
            pltpu.SMEM((n_rows, count_rows, LANES), jnp.int32),
            pltpu.SemaphoreType.DMA,
            *ring,
        ],
        compiler_params=limit,
        name="build",
    )(place, direct, points, *pieces)

    if resident:
        k_mat = pltpu.with_memory_space_constraint(k_mat, pltpu.VMEM)

    def own(x):
        return lax.dynamic_slice_in_dim(x, col * own_len, own_len, 1)

    own_t = own(targets)
    inv = 1.0 / jnp.sqrt(1.0 + sum(from_cols(degree)))
    own_inv = own(inv)
    w1 = (own_t * own_inv).astype(BF16)

    def apply(w, s_pieces):
        pieces = from_rows(w)
        products = s_pieces is not None
        extra = [inv, targets, *s_pieces] if products else []
        width = own_len + LANES if products else own_len
        z = pl.pallas_call(
            functools.partial(
                apply_kernel, (len(pieces), n_cols, own_rows, block_len, products, resident)
            ),
            out_shape=[shape(outputs, width)] * n_cols,
            in_specs=[SMEM] * 4 + [k_spec] + [VMEM] * (len(pieces) + len(extra)),
            out_specs=[VMEM] * n_cols,
            scratch_shapes=[
                pltpu.VMEM((n_sub, outputs, block_len), BF16),
                pltpu.VMEM((block_rows, outputs, block_len), F32),
                *ring,
            ],
            compiler_params=limit,
            name="apply",
        )(place, ilist, jlist, groups, k_mat, *pieces, *extra)
        return sum([z[0]] + [swap(z[e], "cols", e) for e in range(1, n_cols)])

    s1 = apply(w1, None) * own_inv
    g = ((s1 - SHIFT * own_t) * own_inv).astype(BF16)
    s1_pieces = from_cols(s1)
    z2 = apply(g, s1_pieces)
    s2 = z2[:, :own_len] * own_inv + SHIFT * s1
    dots = z2[:, own_len:]
    if n_rows > DIRECT_ROWS:
        dots = [lax.psum(dots, "rows"), jnp.zeros_like(dots)]
    else:
        dots = dots + sum(swap(dots, "rows", d) for d in range(2, n_rows, 2))
        dots = [dots, swap(dots, "rows", 1)]

    return pl.pallas_call(
        functools.partial(final_kernel, n_cols),
        out_shape=(shape(outputs, npoints), shape(outputs, npoints)),
        in_specs=[SMEM] + [VMEM] * (3 + 2 * n_cols),
        out_specs=(VMEM, VMEM),
        name="final",
    )(place, targets, *dots, *s1_pieces, *from_cols(s2))


def solution(mesh):
    placed = (P("rows", "cols"), P(None, "rows"), P(None, "rows"))
    return jax.shard_map(
        local,
        mesh=mesh,
        in_specs=placed,
        out_specs=(P(None, "rows"), P(None, "rows")),
        check_vma=False,
    )
```

profile of v0, /device:TPU:0, one launch (start us, length us, event | category | flops | bytes accessed | tf_op | source)
XLA Modules:
  0.0 96.7 jit_solution(8262498090401652913)
XLA Ops:
  0.6 3.0 %collective-permute-start.1 = (s32[8,6]{1,0:T(8,128)}, s32[8,6]{1,0:T(8,128)S(1)}, u32[]{:S(2)}, u32[]{:S(2)}) collective-permute-start(s32[8,6]{1,0:T(8,128)} %param.3), channel_id=1, source_target_pairs={{0,2},{1,3},{2,0},{3,1},{4,6},{5,7},{6,4},{7,5},{8,10},{9,11},{10,... | collective-permute-start | bytes 584 | tf_op jit(solution)/shard_map/ppermute | solution.py:261
  3.9 0.7 constant_dynamic-slice_fusion.1
  4.6 0.9 collective-permute-done.1
  5.5 1.4 %collective-permute-done.2 = s32[8,6]{1,0:T(8,128)S(1)} collective-permute-done((s32[8,6]{1,0:T(8,128)}, s32[8,6]{1,0:T(8,128)S(1)}, u32[]{:S(2)}, u32[]{:S(2)}) %collective-permute-start.2) | collective-permute-done | bytes 224 | tf_op jit(solution)/shard_map/ppermute | solution.py:261
  6.9 0.8 pad_add_fusion
  7.9 2.6 %collective-permute-start.4 = (bf16[16,640]{1,0:T(8,128)(2,1)S(1)}, bf16[16,640]{1,0:T(8,128)(2,1)S(1)}, u32[]{:S(2)}, u32[]{:S(2)}) collective-permute-start(bf16[16,640]{1,0:T(8,128)(2,1)S(1)} %get-tuple-element.31), channel_id=1, source_target_pairs={{0,16},{4,20},{8,24},{12,28},{16,0},{20,4},{24,8},{28,12},{1,17},{... | collective-permute-start | bytes 61448 | tf_op jit(solution)/shard_map/ppermute | solution.py:261
  10.6 1.6 %collective-permute-start.3 = (bf16[16,640]{1,0:T(8,128)(2,1)S(1)}, bf16[16,640]{1,0:T(8,128)(2,1)S(1)}, u32[]{:S(2)}, u32[]{:S(2)}) collective-permute-start(bf16[16,640]{1,0:T(8,128)(2,1)S(1)} %get-tuple-element.31), channel_id=1, source_target_pairs={{0,8},{4,12},{8,0},{12,4},{16,24},{20,28},{24,16},{28,20},{1,9},{5... | collective-permute-start | bytes 61448 | tf_op jit(solution)/shard_map/ppermute | solution.py:261
  12.7 1.7 %collective-permute-done.3 = bf16[16,640]{1,0:T(8,128)(2,1)S(1)} collective-permute-done((bf16[16,640]{1,0:T(8,128)(2,1)S(1)}, bf16[16,640]{1,0:T(8,128)(2,1)S(1)}, u32[]{:S(2)}, u32[]{:S(2)}) %collective-permute-start.3) | collective-permute-done | bytes 20512 | tf_op jit(solution)/shard_map/ppermute | solution.py:261
  14.3 3.4 %collective-permute-done.5 = bf16[16,640]{1,0:T(8,128)(2,1)S(1)} collective-permute-done((bf16[16,640]{1,0:T(8,128)(2,1)S(1)}, bf16[16,640]{1,0:T(8,128)(2,1)S(1)}, u32[]{:S(2)}, u32[]{:S(2)}) %collective-permute-start.5) | collective-permute-done | bytes 20512 | tf_op jit(solution)/shard_map/ppermute | solution.py:261
  17.7 1.6 %collective-permute-start.6 = (bf16[4,16,640]{2,1,0:T(8,128)(2,1)S(1)}, bf16[4,16,640]{2,1,0:T(8,128)(2,1)S(1)}, u32[]{:S(2)}, u32[]{:S(2)}) collective-permute-start(bf16[4,16,640]{2,1,0:T(8,128)(2,1)S(1)} %pad_maximum_fusion.2.refs_0_), channel_id=1, source_target_pairs={{0,4},{4,0},{8,12},{12,8},{16,20},{20,16},{24,28},{28,24},{1,5},{5... | collective-permute-start | bytes 245768 | tf_op jit(solution)/shard_map/ppermute | solution.py:261
  19.4 2.9 %collective-permute-done.6.refs_1_ = bf16[4,16,640]{2,1,0:T(8,128)(2,1)S(1)} collective-permute-done((bf16[4,16,640]{2,1,0:T(8,128)(2,1)S(1)}, bf16[4,16,640]{2,1,0:T(8,128)(2,1)S(1)}, u32[]{:S(2)}, u32[]{:S(2)}) %collective-permute-start.6) | collective-permute-done | bytes 81952 | tf_op jit(solution)/shard_map/ppermute | solution.py:261
  22.2 0.8 copy-done.5
  23.1 9.1 %build.1 = (bf16[32,4,256,256]{3,2,1,0:T(8,128)(2,1)S(1)}, s32[132]{0:T(256)S(1)}, s32[132]{0:T(256)S(1)}, s32[1]{0:T(128)}, f32[1,2048]{1,0:T(1,128)S(1)}) custom-call(s32[2]{0:T(128)S(1)} %pad_add_fusion.1.place, s32[8,64]{1,0:T(8,128)S(1)} %convert_reduce_fusion.direct, bf16[16,2048]{1,0:T(8,128)(2,1)S(1)} %copy-done.5, ...), custom_call_target="tpu_custom_call" | custom-call | tf_op jit(solution)/shard_map/build/pallas_call | solution.py:316
  32.3 0.6 collective-permute-start.8
  33.0 1.2 %collective-permute-start.7 = (f32[1,2048]{1,0:T(1,128)S(1)}, f32[1,2048]{1,0:T(1,128)S(1)}, u32[]{:S(2)}, u32[]{:S(2)}) collective-permute-start(f32[1,2048]{1,0:T(1,128)S(1)} %get-tuple-element.19), channel_id=1, source_target_pairs={{0,1},{1,0},{2,3},{3,2},{4,5},{5,4},{6,7},{7,6},{8,9},{9,8},{10,11... | collective-permute-start | bytes 24584 | tf_op jit(solution)/shard_map/ppermute | solution.py:261
  34.2 1.2 %collective-permute-done.9 = f32[1,2048]{1,0:T(1,128)S(1)} collective-permute-done((f32[1,2048]{1,0:T(1,128)S(1)}, f32[1,2048]{1,0:T(1,128)S(1)}, u32[]{:S(2)}, u32[]{:S(2)}) %collective-permute-start.9) | collective-permute-done | bytes 8224 | tf_op jit(solution)/shard_map/ppermute | solution.py:261
  35.4 0.7 collective-permute-done.8
  36.1 0.9 multiply_convert_fusion.1
  36.9 0.8 collective-permute-start.10
  37.7 3.6 %collective-permute-start.12 = (bf16[32,512]{1,0:T(8,128)(2,1)S(1)}, bf16[32,512]{1,0:T(8,128)(2,1)S(1)}, u32[]{:S(2)}, u32[]{:S(2)}) collective-permute-start(bf16[32,512]{1,0:T(8,128)(2,1)S(1)} %multiply_convert_fusion.1), channel_id=1, source_target_pairs={{0,24},{4,28},{8,16},{12,20},{16,8},{20,12},{24,0},{28,4},{1,25},{... | collective-permute-start | bytes 98312 | tf_op jit(solution)/shard_map/ppermute | solution.py:261
  41.3 0.8 fusion.2
  42.2 1.4 %collective-permute-done.12 = bf16[32,512]{1,0:T(8,128)(2,1)S(1)} collective-permute-done((bf16[32,512]{1,0:T(8,128)(2,1)S(1)}, bf16[32,512]{1,0:T(8,128)(2,1)S(1)}, u32[]{:S(2)}, u32[]{:S(2)}) %collective-permute-start.12) | collective-permute-done | bytes 32800 | tf_op jit(solution)/shard_map/ppermute | solution.py:261
  43.6 1.0 %collective-permute-start.13 = (bf16[4,32,512]{2,1,0:T(8,128)(2,1)S(1)}, bf16[4,32,512]{2,1,0:T(8,128)(2,1)S(1)}, u32[]{:S(2)}, u32[]{:S(2)}) collective-permute-start(bf16[4,32,512]{2,1,0:T(8,128)(2,1)S(1)} %pad_maximum_fusion.refs_0_), channel_id=1, source_target_pairs={{0,4},{4,0},{8,12},{12,8},{16,20},{20,16},{24,28},{28,24},{1,5},{5... | collective-permute-start | bytes 393224 | tf_op jit(solution)/shard_map/ppermute | solution.py:261
  44.6 4.0 %collective-permute-done.13.refs_1_ = bf16[4,32,512]{2,1,0:T(8,128)(2,1)S(1)} collective-permute-done((bf16[4,32,512]{2,1,0:T(8,128)(2,1)S(1)}, bf16[4,32,512]{2,1,0:T(8,128)(2,1)S(1)}, u32[]{:S(2)}, u32[]{:S(2)}) %collective-permute-start.13) | collective-permute-done | bytes 131104 | tf_op jit(solution)/shard_map/ppermute | solution.py:261
  48.6 3.7 %apply.2 = (f32[32,512]{1,0:T(8,128)S(1)}, f32[32,512]{1,0:T(8,128)S(1)}, f32[32,512]{1,0:T(8,128)S(1)}, f32[32,512]{1,0:T(8,128)S(1)}) custom-call(s32[2]{0:T(128)S(1)} %pad_add_fusion.1.place, s32[132]{0:T(256)S(1)} %get-tuple-element.15.ilist, s32[132]{0:T(256)S(1)} %get-tuple-element.16.jlist, s32[1]{0:T(128)} %get-tuple-element.17.groups, ...), custom_call_target="tpu_custom_call" | custom-call | tf_op jit(solution)/shard_map/apply/pallas_call | solution.py:360
  53.1 1.2 %collective-permute-start.16 = (f32[32,512]{1,0:T(8,128)S(1)}, f32[32,512]{1,0:T(8,128)S(1)}, u32[]{:S(2)}, u32[]{:S(2)}) collective-permute-start(f32[32,512]{1,0:T(8,128)S(1)} %get-tuple-element.23), channel_id=1, source_target_pairs={{0,3},{1,2},{2,1},{3,0},{4,7},{5,6},{6,5},{7,4},{8,11},{9,10},{10,... | collective-permute-start | bytes 196616 | tf_op jit(solution)/shard_map/ppermute | solution.py:261
  54.3 3.1 %collective-permute-done.15 = f32[32,512]{1,0:T(8,128)S(1)} collective-permute-done((f32[32,512]{1,0:T(8,128)S(1)}, f32[32,512]{1,0:T(8,128)S(1)}, u32[]{:S(2)}, u32[]{:S(2)}) %collective-permute-start.15) | collective-permute-done | bytes 65568 | tf_op jit(solution)/shard_map/ppermute | solution.py:261
  57.9 3.5 %collective-permute-start.19 = (bf16[32,512]{1,0:T(8,128)(2,1)S(1)}, bf16[32,512]{1,0:T(8,128)(2,1)S(1)}, u32[]{:S(2)}, u32[]{:S(2)}) collective-permute-start(bf16[32,512]{1,0:T(8,128)(2,1)S(1)} %get-tuple-element.28), channel_id=1, source_target_pairs={{0,24},{4,28},{8,16},{12,20},{16,8},{20,12},{24,0},{28,4},{1,25},{... | collective-permute-start | bytes 98312 | tf_op jit(solution)/shard_map/ppermute | solution.py:261
  61.5 0.9 collective-permute-start.17
  62.4 1.3 %collective-permute-done.19 = bf16[32,512]{1,0:T(8,128)(2,1)S(1)} collective-permute-done((bf16[32,512]{1,0:T(8,128)(2,1)S(1)}, bf16[32,512]{1,0:T(8,128)(2,1)S(1)}, u32[]{:S(2)}, u32[]{:S(2)}) %collective-permute-start.19) | collective-permute-done | bytes 32800 | tf_op jit(solution)/shard_map/ppermute | solution.py:261
  63.7 2.6 %collective-permute-done.18 = bf16[32,512]{1,0:T(8,128)(2,1)S(1)} collective-permute-done((bf16[32,512]{1,0:T(8,128)(2,1)S(1)}, bf16[32,512]{1,0:T(8,128)(2,1)S(1)}, u32[]{:S(2)}, u32[]{:S(2)}) %collective-permute-start.18) | collective-permute-done | bytes 32800 | tf_op jit(solution)/shard_map/ppermute | solution.py:261
  66.3 0.8 collective-permute-start.20
  67.1 1.4 %collective-permute-start.22 = (f32[32,512]{1,0:T(8,128)S(1)}, f32[32,512]{1,0:T(8,128)S(1)}, u32[]{:S(2)}, u32[]{:S(2)}) collective-permute-start(f32[32,512]{1,0:T(8,128)S(1)} %get-tuple-element.29.refs_4_.refs_0_), channel_id=1, source_target_pairs={{0,2},{1,3},{2,0},{3,1},{4,6},{5,7},{6,4},{7,5},{8,10},{9,11},{10,... | collective-permute-start | bytes 196616 | tf_op jit(solution)/shard_map/ppermute | solution.py:261
  69.0 2.5 %collective-permute-done.23.refs_7_.refs_3_ = f32[32,512]{1,0:T(8,128)S(1)} collective-permute-done((f32[32,512]{1,0:T(8,128)S(1)}, f32[32,512]{1,0:T(8,128)S(1)}, u32[]{:S(2)}, u32[]{:S(2)}) %collective-permute-start.23) | collective-permute-done | bytes 65568 | tf_op jit(solution)/shard_map/ppermute | solution.py:261
  71.5 1.2 %collective-permute-done.22.refs_6_.refs_2_ = f32[32,512]{1,0:T(8,128)S(1)} collective-permute-done((f32[32,512]{1,0:T(8,128)S(1)}, f32[32,512]{1,0:T(8,128)S(1)}, u32[]{:S(2)}, u32[]{:S(2)}) %collective-permute-start.22) | collective-permute-done | bytes 65568 | tf_op jit(solution)/shard_map/ppermute | solution.py:261
  72.7 3.9 %apply.3 = (f32[32,640]{1,0:T(8,128)S(1)}, f32[32,640]{1,0:T(8,128)S(1)}, f32[32,640]{1,0:T(8,128)S(1)}, f32[32,640]{1,0:T(8,128)S(1)}) custom-call(s32[2]{0:T(128)S(1)} %pad_add_fusion.1.place, s32[132]{0:T(256)S(1)} %get-tuple-element.15.ilist, s32[132]{0:T(256)S(1)} %get-tuple-element.16.jlist, s32[1]{0:T(128)} %get-tuple-element.17.groups, ...), custom_call_target="tpu_custom_call" | custom-call | tf_op jit(solution)/shard_map/apply/pallas_call | solution.py:360
  76.8 1.0 %collective-permute-start.25 = (f32[32,640]{1,0:T(8,128)S(1)}, f32[32,640]{1,0:T(8,128)S(1)}, u32[]{:S(2)}, u32[]{:S(2)}) collective-permute-start(f32[32,640]{1,0:T(8,128)S(1)} %get-tuple-element.26), channel_id=1, source_target_pairs={{0,2},{1,3},{2,0},{3,1},{4,6},{5,7},{6,4},{7,5},{8,10},{9,11},{10,... | collective-permute-start | bytes 245768 | tf_op jit(solution)/shard_map/ppermute | solution.py:261
  77.8 0.8 collective-permute-start.26
  78.6 3.5 %collective-permute-done.25 = f32[32,640]{1,0:T(8,128)S(1)} collective-permute-done((f32[32,640]{1,0:T(8,128)S(1)}, f32[32,640]{1,0:T(8,128)S(1)}, u32[]{:S(2)}, u32[]{:S(2)}) %collective-permute-start.25) | collective-permute-done | bytes 81952 | tf_op jit(solution)/shard_map/ppermute | solution.py:261
  82.1 0.8 collective-permute-done.26
  82.9 1.4 %collective-permute-start.29 = (f32[32,128]{1,0:T(8,128)S(1)}, f32[32,128]{1,0:T(8,128)S(1)}, u32[]{:S(2)}, u32[]{:S(2)}) collective-permute-start(f32[32,128]{1,0:T(8,128)S(1)} %slice.8), channel_id=1, source_target_pairs={{0,24},{4,28},{8,16},{12,20},{16,8},{20,12},{24,0},{28,4},{1,25},{... | collective-permute-start | bytes 49160 | tf_op jit(solution)/shard_map/ppermute | solution.py:261
  84.3 0.8 collective-permute-start.28
  85.1 2.3 %collective-permute-start.27 = (f32[32,128]{1,0:T(8,128)S(1)}, f32[32,128]{1,0:T(8,128)S(1)}, u32[]{:S(2)}, u32[]{:S(2)}) collective-permute-start(f32[32,128]{1,0:T(8,128)S(1)} %slice.8), channel_id=1, source_target_pairs={{0,8},{4,12},{8,0},{12,4},{16,24},{20,28},{24,16},{28,20},{1,9},{5... | collective-permute-start | bytes 49160 | tf_op jit(solution)/shard_map/ppermute | solution.py:261
  87.5 1.1 %collective-permute-start.32 = (f32[32,512]{1,0:T(8,128)S(1)}, f32[32,512]{1,0:T(8,128)S(1)}, u32[]{:S(2)}, u32[]{:S(2)}) collective-permute-start(f32[32,512]{1,0:T(8,128)S(1)} %fusion.refs_4_), channel_id=1, source_target_pairs={{0,2},{1,3},{2,0},{3,1},{4,6},{5,7},{6,4},{7,5},{8,10},{9,11},{10,... | collective-permute-start | bytes 196616 | tf_op jit(solution)/shard_map/ppermute | solution.py:261
  88.6 0.8 collective-permute-start.31
  89.4 0.7 collective-permute-start.30
  90.1 3.1 %collective-permute-done.30.dots_b = f32[32,128]{1,0:T(8,128)S(1)} collective-permute-done((f32[32,128]{1,0:T(8,128)S(1)}, f32[32,128]{1,0:T(8,128)S(1)}, u32[]{:S(2)}, u32[]{:S(2)}) %collective-permute-start.30) | collective-permute-done | bytes 16416 | tf_op jit(solution)/shard_map/ppermute | solution.py:261
  94.5 2.3 %final.1 = (f32[32,2048]{1,0:T(8,128)}, f32[32,2048]{1,0:T(8,128)}) custom-call(s32[2]{0:T(128)} %copy-done.6, f32[32,2048]{1,0:T(8,128)} %t_ref.1, f32[32,128]{1,0:T(8,128)} %copy-done.8, f32[32,128]{1,0:T(8,128)} %copy-done.12, f32[32,512]{1,0:T(8,128)} %copy-done.1, f32[32,512]{1,0:T(8,128)} %copy-done.4, f32[32,512]{1,0:T(8,128)} %copy-done.3, ...), custom_call_target="tpu_custom_call" | custom-call | tf_op jit(solution)/shard_map/final/pallas_call | solution.py:389
  (70 shorter events, 4.5 us)
Async XLA Ops:
  0.6 57.3 %copy-start = (f32[32,2048]{1,0:T(8,128)S(1)}, f32[32,2048]{1,0:T(8,128)}, u32[]{:S(2)}) copy-start(f32[32,2048]{1,0:T(8,128)} %t_ref.1) | copy-start | bytes 786436
  0.6 4.8 %collective-permute-start.1 = (s32[8,6]{1,0:T(8,128)}, s32[8,6]{1,0:T(8,128)S(1)}, u32[]{:S(2)}, u32[]{:S(2)}) collective-permute-start(s32[8,6]{1,0:T(8,128)} %param.3), channel_id=1, source_target_pairs={{0,2},{1,3},{2,0},{3,1},{4,6},{5,7},{6,4},{7,5},{8,10},{9,11},{10,... | collective-permute-start | bytes 584 | tf_op jit(solution)/shard_map/ppermute | solution.py:261
  3.7 1.8 %collective-permute-start = (s32[8,6]{1,0:T(8,128)}, s32[8,6]{1,0:T(8,128)S(1)}, u32[]{:S(2)}, u32[]{:S(2)}) collective-permute-start(s32[8,6]{1,0:T(8,128)} %param.3), channel_id=1, source_target_pairs={{0,1},{1,0},{2,3},{3,2},{4,5},{5,4},{6,7},{7,6},{8,9},{9,8},{10,11... | collective-permute-start | bytes 584 | tf_op jit(solution)/shard_map/ppermute | solution.py:261
  3.7 3.2 %collective-permute-start.2 = (s32[8,6]{1,0:T(8,128)}, s32[8,6]{1,0:T(8,128)S(1)}, u32[]{:S(2)}, u32[]{:S(2)}) collective-permute-start(s32[8,6]{1,0:T(8,128)} %param.3), channel_id=1, source_target_pairs={{0,3},{1,2},{2,1},{3,0},{4,7},{5,6},{6,5},{7,4},{8,11},{9,10},{10,... | collective-permute-start | bytes 584 | tf_op jit(solution)/shard_map/ppermute | solution.py:261
  7.9 4.7 %collective-permute-start.4 = (bf16[16,640]{1,0:T(8,128)(2,1)S(1)}, bf16[16,640]{1,0:T(8,128)(2,1)S(1)}, u32[]{:S(2)}, u32[]{:S(2)}) collective-permute-start(bf16[16,640]{1,0:T(8,128)(2,1)S(1)} %get-tuple-element.31), channel_id=1, source_target_pairs={{0,16},{4,20},{8,24},{12,28},{16,0},{20,4},{24,8},{28,12},{1,17},{... | collective-permute-start | bytes 61448 | tf_op jit(solution)/shard_map/ppermute | solution.py:261
  10.6 3.8 %collective-permute-start.3 = (bf16[16,640]{1,0:T(8,128)(2,1)S(1)}, bf16[16,640]{1,0:T(8,128)(2,1)S(1)}, u32[]{:S(2)}, u32[]{:S(2)}) collective-permute-start(bf16[16,640]{1,0:T(8,128)(2,1)S(1)} %get-tuple-element.31), channel_id=1, source_target_pairs={{0,8},{4,12},{8,0},{12,4},{16,24},{20,28},{24,16},{28,20},{1,9},{5... | collective-permute-start | bytes 61448 | tf_op jit(solution)/shard_map/ppermute | solution.py:261
  12.1 5.6 %collective-permute-start.5 = (bf16[16,640]{1,0:T(8,128)(2,1)S(1)}, bf16[16,640]{1,0:T(8,128)(2,1)S(1)}, u32[]{:S(2)}, u32[]{:S(2)}) collective-permute-start(bf16[16,640]{1,0:T(8,128)(2,1)S(1)} %get-tuple-element.31), channel_id=1, source_target_pairs={{0,24},{4,28},{8,16},{12,20},{16,8},{20,12},{24,0},{28,4},{1,25},{... | collective-permute-start | bytes 61448 | tf_op jit(solution)/shard_map/ppermute | solution.py:261
  17.7 4.5 %collective-permute-start.6 = (bf16[4,16,640]{2,1,0:T(8,128)(2,1)S(1)}, bf16[4,16,640]{2,1,0:T(8,128)(2,1)S(1)}, u32[]{:S(2)}, u32[]{:S(2)}) collective-permute-start(bf16[4,16,640]{2,1,0:T(8,128)(2,1)S(1)} %pad_maximum_fusion.2.refs_0_), channel_id=1, source_target_pairs={{0,4},{4,0},{8,12},{12,8},{16,20},{20,16},{24,28},{28,24},{1,5},{5... | collective-permute-start | bytes 245768 | tf_op jit(solution)/shard_map/ppermute | solution.py:261
  19.4 57.3 %copy-start.6 = (s32[2]{0:T(128)}, s32[2]{0:T(128)S(1)}, u32[]{:S(2)}) copy-start(s32[2]{0:T(128)S(1)} %pad_add_fusion.1.place) | copy-start | bytes 28
  22.2 0.8 copy-start.5
  32.2 3.1 %collective-permute-start.9 = (f32[1,2048]{1,0:T(1,128)S(1)}, f32[1,2048]{1,0:T(1,128)S(1)}, u32[]{:S(2)}, u32[]{:S(2)}) collective-permute-start(f32[1,2048]{1,0:T(1,128)S(1)} %get-tuple-element.19), channel_id=1, source_target_pairs={{0,3},{1,2},{2,1},{3,0},{4,7},{5,6},{6,5},{7,4},{8,11},{9,10},{10,... | collective-permute-start | bytes 24584 | tf_op jit(solution)/shard_map/ppermute | solution.py:261
  32.3 3.7 %collective-permute-start.8 = (f32[1,2048]{1,0:T(1,128)S(1)}, f32[1,2048]{1,0:T(1,128)S(1)}, u32[]{:S(2)}, u32[]{:S(2)}) collective-permute-start(f32[1,2048]{1,0:T(1,128)S(1)} %get-tuple-element.19), channel_id=1, source_target_pairs={{0,2},{1,3},{2,0},{3,1},{4,6},{5,7},{6,4},{7,5},{8,10},{9,11},{10,... | collective-permute-start | bytes 24584 | tf_op jit(solution)/shard_map/ppermute | solution.py:261
  33.0 3.1 %collective-permute-start.7 = (f32[1,2048]{1,0:T(1,128)S(1)}, f32[1,2048]{1,0:T(1,128)S(1)}, u32[]{:S(2)}, u32[]{:S(2)}) collective-permute-start(f32[1,2048]{1,0:T(1,128)S(1)} %get-tuple-element.19), channel_id=1, source_target_pairs={{0,1},{1,0},{2,3},{3,2},{4,5},{5,4},{6,7},{7,6},{8,9},{9,8},{10,11... | collective-permute-start | bytes 24584 | tf_op jit(solution)/shard_map/ppermute | solution.py:261
  36.9 5.2 %collective-permute-start.11 = (bf16[32,512]{1,0:T(8,128)(2,1)S(1)}, bf16[32,512]{1,0:T(8,128)(2,1)S(1)}, u32[]{:S(2)}, u32[]{:S(2)}) collective-permute-start(bf16[32,512]{1,0:T(8,128)(2,1)S(1)} %multiply_convert_fusion.1), channel_id=1, source_target_pairs={{0,16},{4,20},{8,24},{12,28},{16,0},{20,4},{24,8},{28,12},{1,17},{... | collective-permute-start | bytes 98312 | tf_op jit(solution)/shard_map/ppermute | solution.py:261
  36.9 5.2 %collective-permute-start.10 = (bf16[32,512]{1,0:T(8,128)(2,1)S(1)}, bf16[32,512]{1,0:T(8,128)(2,1)S(1)}, u32[]{:S(2)}, u32[]{:S(2)}) collective-permute-start(bf16[32,512]{1,0:T(8,128)(2,1)S(1)} %multiply_convert_fusion.1), channel_id=1, source_target_pairs={{0,8},{4,12},{8,0},{12,4},{16,24},{20,28},{24,16},{28,20},{1,9},{5... | collective-permute-start | bytes 98312 | tf_op jit(solution)/shard_map/ppermute | solution.py:261
  37.7 5.8 %collective-permute-start.12 = (bf16[32,512]{1,0:T(8,128)(2,1)S(1)}, bf16[32,512]{1,0:T(8,128)(2,1)S(1)}, u32[]{:S(2)}, u32[]{:S(2)}) collective-permute-start(bf16[32,512]{1,0:T(8,128)(2,1)S(1)} %multiply_convert_fusion.1), channel_id=1, source_target_pairs={{0,24},{4,28},{8,16},{12,20},{16,8},{20,12},{24,0},{28,4},{1,25},{... | collective-permute-start | bytes 98312 | tf_op jit(solution)/shard_map/ppermute | solution.py:261
  43.6 5.0 %collective-permute-start.13 = (bf16[4,32,512]{2,1,0:T(8,128)(2,1)S(1)}, bf16[4,32,512]{2,1,0:T(8,128)(2,1)S(1)}, u32[]{:S(2)}, u32[]{:S(2)}) collective-permute-start(bf16[4,32,512]{2,1,0:T(8,128)(2,1)S(1)} %pad_maximum_fusion.refs_0_), channel_id=1, source_target_pairs={{0,4},{4,0},{8,12},{12,8},{16,20},{20,16},{24,28},{28,24},{1,5},{5... | collective-permute-start | bytes 393224 | tf_op jit(solution)/shard_map/ppermute | solution.py:261
  52.4 1.9 %collective-permute-start.14 = (f32[32,512]{1,0:T(8,128)S(1)}, f32[32,512]{1,0:T(8,128)S(1)}, u32[]{:S(2)}, u32[]{:S(2)}) collective-permute-start(f32[32,512]{1,0:T(8,128)S(1)} %get-tuple-element.21), channel_id=1, source_target_pairs={{0,1},{1,0},{2,3},{3,2},{4,5},{5,4},{6,7},{7,6},{8,9},{9,8},{10,11... | collective-permute-start | bytes 196616 | tf_op jit(solution)/shard_map/ppermute | solution.py:261
  52.4 5.0 %collective-permute-start.15 = (f32[32,512]{1,0:T(8,128)S(1)}, f32[32,512]{1,0:T(8,128)S(1)}, u32[]{:S(2)}, u32[]{:S(2)}) collective-permute-start(f32[32,512]{1,0:T(8,128)S(1)} %get-tuple-element.22), channel_id=1, source_target_pairs={{0,2},{1,3},{2,0},{3,1},{4,6},{5,7},{6,4},{7,5},{8,10},{9,11},{10,... | collective-permute-start | bytes 196616 | tf_op jit(solution)/shard_map/ppermute | solution.py:261
  53.1 4.8 %collective-permute-start.16 = (f32[32,512]{1,0:T(8,128)S(1)}, f32[32,512]{1,0:T(8,128)S(1)}, u32[]{:S(2)}, u32[]{:S(2)}) collective-permute-start(f32[32,512]{1,0:T(8,128)S(1)} %get-tuple-element.23), channel_id=1, source_target_pairs={{0,3},{1,2},{2,1},{3,0},{4,7},{5,6},{6,5},{7,4},{8,11},{9,10},{10,... | collective-permute-start | bytes 196616 | tf_op jit(solution)/shard_map/ppermute | solution.py:261
  57.9 35.3 %copy-start.1 = (f32[32,512]{1,0:T(8,128)}, f32[32,512]{1,0:T(8,128)S(1)}, u32[]{:S(2)}) copy-start(f32[32,512]{1,0:T(8,128)S(1)} %get-tuple-element.29.refs_4_.refs_0_) | copy-start | bytes 196612
  57.9 5.8 %collective-permute-start.19 = (bf16[32,512]{1,0:T(8,128)(2,1)S(1)}, bf16[32,512]{1,0:T(8,128)(2,1)S(1)}, u32[]{:S(2)}, u32[]{:S(2)}) collective-permute-start(bf16[32,512]{1,0:T(8,128)(2,1)S(1)} %get-tuple-element.28), channel_id=1, source_target_pairs={{0,24},{4,28},{8,16},{12,20},{16,8},{20,12},{24,0},{28,4},{1,25},{... | collective-permute-start | bytes 98312 | tf_op jit(solution)/shard_map/ppermute | solution.py:261
  61.5 4.8 %collective-permute-start.18 = (bf16[32,512]{1,0:T(8,128)(2,1)S(1)}, bf16[32,512]{1,0:T(8,128)(2,1)S(1)}, u32[]{:S(2)}, u32[]{:S(2)}) collective-permute-start(bf16[32,512]{1,0:T(8,128)(2,1)S(1)} %get-tuple-element.28), channel_id=1, source_target_pairs={{0,16},{4,20},{8,24},{12,28},{16,0},{20,4},{24,8},{28,12},{1,17},{... | collective-permute-start | bytes 98312 | tf_op jit(solution)/shard_map/ppermute | solution.py:261
  61.5 4.8 %collective-permute-start.17 = (bf16[32,512]{1,0:T(8,128)(2,1)S(1)}, bf16[32,512]{1,0:T(8,128)(2,1)S(1)}, u32[]{:S(2)}, u32[]{:S(2)}) collective-permute-start(bf16[32,512]{1,0:T(8,128)(2,1)S(1)} %get-tuple-element.28), channel_id=1, source_target_pairs={{0,8},{4,12},{8,0},{12,4},{16,24},{20,28},{24,16},{28,20},{1,9},{5... | collective-permute-start | bytes 98312 | tf_op jit(solution)/shard_map/ppermute | solution.py:261
  66.3 6.4 %collective-permute-start.20 = (bf16[4,32,512]{2,1,0:T(8,128)(2,1)S(1)}, bf16[4,32,512]{2,1,0:T(8,128)(2,1)S(1)}, u32[]{:S(2)}, u32[]{:S(2)}) collective-permute-start(bf16[4,32,512]{2,1,0:T(8,128)(2,1)S(1)} %pad_maximum_fusion.1.refs_0_), channel_id=1, source_target_pairs={{0,4},{4,0},{8,12},{12,8},{16,20},{20,16},{24,28},{28,24},{1,5},{5... | collective-permute-start | bytes 393224 | tf_op jit(solution)/shard_map/ppermute | solution.py:261
  67.1 4.4 %collective-permute-start.23 = (f32[32,512]{1,0:T(8,128)S(1)}, f32[32,512]{1,0:T(8,128)S(1)}, u32[]{:S(2)}, u32[]{:S(2)}) collective-permute-start(f32[32,512]{1,0:T(8,128)S(1)} %get-tuple-element.29.refs_4_.refs_0_), channel_id=1, source_target_pairs={{0,3},{1,2},{2,1},{3,0},{4,7},{5,6},{6,5},{7,4},{8,11},{9,10},{10,... | collective-permute-start | bytes 196616 | tf_op jit(solution)/shard_map/ppermute | solution.py:261
  67.1 5.6 %collective-permute-start.22 = (f32[32,512]{1,0:T(8,128)S(1)}, f32[32,512]{1,0:T(8,128)S(1)}, u32[]{:S(2)}, u32[]{:S(2)}) collective-permute-start(f32[32,512]{1,0:T(8,128)S(1)} %get-tuple-element.29.refs_4_.refs_0_), channel_id=1, source_target_pairs={{0,2},{1,3},{2,0},{3,1},{4,6},{5,7},{6,4},{7,5},{8,10},{9,11},{10,... | collective-permute-start | bytes 196616 | tf_op jit(solution)/shard_map/ppermute | solution.py:261
  68.5 4.2 %collective-permute-start.21 = (f32[32,512]{1,0:T(8,128)S(1)}, f32[32,512]{1,0:T(8,128)S(1)}, u32[]{:S(2)}, u32[]{:S(2)}) collective-permute-start(f32[32,512]{1,0:T(8,128)S(1)} %get-tuple-element.29.refs_4_.refs_0_), channel_id=1, source_target_pairs={{0,1},{1,0},{2,3},{3,2},{4,5},{5,4},{6,7},{7,6},{8,9},{9,8},{10,11... | collective-permute-start | bytes 196616 | tf_op jit(solution)/shard_map/ppermute | solution.py:261
  71.5 21.7 %copy-start.2 = (f32[32,512]{1,0:T(8,128)}, f32[32,512]{1,0:T(8,128)S(1)}, u32[]{:S(2)}) copy-start(f32[32,512]{1,0:T(8,128)S(1)} %collective-permute-done.23.refs_7_.refs_3_) | copy-start | bytes 196612
  72.7 20.5 %copy-start.3 = (f32[32,512]{1,0:T(8,128)}, f32[32,512]{1,0:T(8,128)S(1)}, u32[]{:S(2)}) copy-start(f32[32,512]{1,0:T(8,128)S(1)} %collective-permute-done.22.refs_6_.refs_2_) | copy-start | bytes 196612
  72.7 20.5 %copy-start.4 = (f32[32,512]{1,0:T(8,128)}, f32[32,512]{1,0:T(8,128)S(1)}, u32[]{:S(2)}) copy-start(f32[32,512]{1,0:T(8,128)S(1)} %collective-permute-done.21.refs_5_.refs_1_) | copy-start | bytes 196612
  76.7 2.0 %collective-permute-start.24 = (f32[32,640]{1,0:T(8,128)S(1)}, f32[32,640]{1,0:T(8,128)S(1)}, u32[]{:S(2)}, u32[]{:S(2)}) collective-permute-start(f32[32,640]{1,0:T(8,128)S(1)} %get-tuple-element.25), channel_id=1, source_target_pairs={{0,1},{1,0},{2,3},{3,2},{4,5},{5,4},{6,7},{7,6},{8,9},{9,8},{10,11... | collective-permute-start | bytes 245768 | tf_op jit(solution)/shard_map/ppermute | solution.py:261
  76.8 5.2 %collective-permute-start.25 = (f32[32,640]{1,0:T(8,128)S(1)}, f32[32,640]{1,0:T(8,128)S(1)}, u32[]{:S(2)}, u32[]{:S(2)}) collective-permute-start(f32[32,640]{1,0:T(8,128)S(1)} %get-tuple-element.26), channel_id=1, source_target_pairs={{0,2},{1,3},{2,0},{3,1},{4,6},{5,7},{6,4},{7,5},{8,10},{9,11},{10,... | collective-permute-start | bytes 245768 | tf_op jit(solution)/shard_map/ppermute | solution.py:261
  77.8 5.1 %collective-permute-start.26 = (f32[32,640]{1,0:T(8,128)S(1)}, f32[32,640]{1,0:T(8,128)S(1)}, u32[]{:S(2)}, u32[]{:S(2)}) collective-permute-start(f32[32,640]{1,0:T(8,128)S(1)} %get-tuple-element.27), channel_id=1, source_target_pairs={{0,3},{1,2},{2,1},{3,0},{4,7},{5,6},{6,5},{7,4},{8,11},{9,10},{10,... | collective-permute-start | bytes 245768 | tf_op jit(solution)/shard_map/ppermute | solution.py:261
  82.9 5.6 %collective-permute-start.29 = (f32[32,128]{1,0:T(8,128)S(1)}, f32[32,128]{1,0:T(8,128)S(1)}, u32[]{:S(2)}, u32[]{:S(2)}) collective-permute-start(f32[32,128]{1,0:T(8,128)S(1)} %slice.8), channel_id=1, source_target_pairs={{0,24},{4,28},{8,16},{12,20},{16,8},{20,12},{24,0},{28,4},{1,25},{... | collective-permute-start | bytes 49160 | tf_op jit(solution)/shard_map/ppermute | solution.py:261
  84.3 5.0 %collective-permute-start.28 = (f32[32,128]{1,0:T(8,128)S(1)}, f32[32,128]{1,0:T(8,128)S(1)}, u32[]{:S(2)}, u32[]{:S(2)}) collective-permute-start(f32[32,128]{1,0:T(8,128)S(1)} %slice.8), channel_id=1, source_target_pairs={{0,16},{4,20},{8,24},{12,28},{16,0},{20,4},{24,8},{28,12},{1,17},{... | collective-permute-start | bytes 49160 | tf_op jit(solution)/shard_map/ppermute | solution.py:261
  85.1 4.2 %collective-permute-start.27 = (f32[32,128]{1,0:T(8,128)S(1)}, f32[32,128]{1,0:T(8,128)S(1)}, u32[]{:S(2)}, u32[]{:S(2)}) collective-permute-start(f32[32,128]{1,0:T(8,128)S(1)} %slice.8), channel_id=1, source_target_pairs={{0,8},{4,12},{8,0},{12,4},{16,24},{20,28},{24,16},{28,20},{1,9},{5... | collective-permute-start | bytes 49160 | tf_op jit(solution)/shard_map/ppermute | solution.py:261
  87.4 5.8 %copy-start.7 = (f32[32,512]{1,0:T(8,128)}, f32[32,512]{1,0:T(8,128)S(1)}, u32[]{:S(2)}) copy-start(f32[32,512]{1,0:T(8,128)S(1)} %fusion.refs_4_) | copy-start | bytes 196612
  87.4 5.8 %collective-permute-start.33 = (f32[32,512]{1,0:T(8,128)S(1)}, f32[32,512]{1,0:T(8,128)S(1)}, u32[]{:S(2)}, u32[]{:S(2)}) collective-permute-start(f32[32,512]{1,0:T(8,128)S(1)} %fusion.refs_4_), channel_id=1, source_target_pairs={{0,3},{1,2},{2,1},{3,0},{4,7},{5,6},{6,5},{7,4},{8,11},{9,10},{10,... | collective-permute-start | bytes 196616 | tf_op jit(solution)/shard_map/ppermute | solution.py:261
  87.5 5.7 %collective-permute-start.32 = (f32[32,512]{1,0:T(8,128)S(1)}, f32[32,512]{1,0:T(8,128)S(1)}, u32[]{:S(2)}, u32[]{:S(2)}) collective-permute-start(f32[32,512]{1,0:T(8,128)S(1)} %fusion.refs_4_), channel_id=1, source_target_pairs={{0,2},{1,3},{2,0},{3,1},{4,6},{5,7},{6,4},{7,5},{8,10},{9,11},{10,... | collective-permute-start | bytes 196616 | tf_op jit(solution)/shard_map/ppermute | solution.py:261
  88.6 4.6 %collective-permute-start.31 = (f32[32,512]{1,0:T(8,128)S(1)}, f32[32,512]{1,0:T(8,128)S(1)}, u32[]{:S(2)}, u32[]{:S(2)}) collective-permute-start(f32[32,512]{1,0:T(8,128)S(1)} %fusion.refs_4_), channel_id=1, source_target_pairs={{0,1},{1,0},{2,3},{3,2},{4,5},{5,4},{6,7},{7,6},{8,9},{9,8},{10,11... | collective-permute-start | bytes 196616 | tf_op jit(solution)/shard_map/ppermute | solution.py:261
  89.3 3.9 %copy-start.8 = (f32[32,128]{1,0:T(8,128)}, f32[32,128]{1,0:T(8,128)S(1)}, u32[]{:S(2)}) copy-start(f32[32,128]{1,0:T(8,128)S(1)} %add_add_fusion.1.dots_a) | copy-start | bytes 49156
  89.4 3.8 %collective-permute-start.30 = (f32[32,128]{1,0:T(8,128)S(1)}, f32[32,128]{1,0:T(8,128)S(1)}, u32[]{:S(2)}, u32[]{:S(2)}) collective-permute-start(f32[32,128]{1,0:T(8,128)S(1)} %add_add_fusion.1.dots_a), channel_id=1, source_target_pairs={{0,4},{4,0},{8,12},{12,8},{16,20},{20,16},{24,28},{28,24},{1,5},{5... | collective-permute-start | bytes 49160 | tf_op jit(solution)/shard_map/ppermute | solution.py:261
  93.2 0.6 copy-start.12
  93.2 0.6 copy-start.9
  93.2 0.7 copy-start.10
  93.8 0.6 copy-start.11
where the time goes:
time: 97.2 us; the launch traced here: 96.7 us
  waiting for transfers between devices  36.5 us (38%)
  starting transfers between devices  34.6 us (36%)
  Pallas kernels  19 us (20%)
  local copies, waits for them, and re-layouts  2.9 us (3%)
  other arithmetic  2.81 us (3%)
    ppermute x34, waiting for transfers between devices, swap(): return lax.ppermute(x, axis, [(i, i ^ d) for i in range(size)])  36.5 us
    ppermute x34, starting transfers between devices, swap(): return lax.ppermute(x, axis, [(i, i ^ d) for i in range(size)])  34.6 us
    pallas_call x1, Pallas kernels, local(): pl.pallas_call(functools.partial(build_kernel, (len(pieces), nb, block_le...  9.13 us
    pallas_call x2, Pallas kernels, apply(): pl.pallas_call(functools.partial(apply_kernel, (len(pieces), n_cols, own_...  7.63 us
    pallas_call x1, Pallas kernels, local(): pl.pallas_call(functools.partial(final_kernel, n_cols), out_shape=(shape(...  2.27 us
    unnamed x26, local copies, waits for them, and re-layouts  2.08 us
  transfers between devices with their start and end apart: 34, of which 19 were waited for; matrix products, arithmetic and copies ran while one was open for 2% of the time, Pallas kernels for 0%

commit v1 on v0

--- a/solution.py
+++ b/solution.py
@@ -56,6 +56,11 @@
                 visit(row ^ (2 * k + parity), lambda *at, ref=ref, k=k: ref[(k,) + at])
 
 
+def by_col(refs):
+    own, across, pair = refs
+    return own, pair.at[0], across, pair.at[1]
+
+
 def build_kernel(cfg, place, direct, near_ref, *refs):
     n_pieces, nb, block_len, own_rows, block_rows, n_sub, count_rows, resident = cfg
     pieces, refs = refs[:n_pieces], refs[n_pieces:]
@@ -126,6 +131,7 @@
             j = jlist[g * GROUP + u]
             m = mlist[g * GROUP + u].astype(F32)
             far = rhs[j]
+            sums = jnp.zeros((8, block_len), F32)
             for s in range(block_len // STRIP):
                 rows = slice(s * STRIP, (s + 1) * STRIP)
                 d = jnp.dot(lhs[i, rows, :], far, preferred_element_type=F32)
@@ -135,17 +141,15 @@
                 sq = rem * rem
                 val = (sq * sq) * (sc * (4.0 * m) + m)
                 target[slot, u, rows, :] = val.astype(BF16)
-                half = val[:, :LANES]
-                for h in range(1, block_len // LANES):
-                    half = half + val[:, h * LANES:(h + 1) * LANES]
-                acc[i, rows, :] += half
+                for h in range(0, STRIP, 8):
+                    sums = sums + val[h:h + 8]
+            acc[j] += sums
         if not resident:
             copy_out(g).start()
         return carry
 
     lax.fori_loop(0, total, step, 0)
-    for i in range(block_rows):
-        deg_ref[:, i * block_len:(i + 1) * block_len] = jnp.sum(acc[i].T, axis=0, keepdims=True)
+    deg_ref[...] = jnp.sum(acc[...], axis=1)
 
     def drain(g, carry):
         copy_out(g).wait()
@@ -156,14 +160,15 @@
 
 
 def apply_kernel(cfg, place, ilist, jlist, groups, k_mat, *refs):
-    n_pieces, n_cols, own_rows, block_len, products, resident = cfg
+    n_pieces, n_cols, own_rows, block_len, first, resident = cfg
     pieces, refs = refs[:n_pieces], refs[n_pieces:]
-    if products:
-        inv_ref, t_ref, refs = refs[0], refs[1], refs[2:]
-        s_refs, refs = refs[:n_cols], refs[n_cols:]
-    z_refs, refs = refs[:n_cols], refs[n_cols:]
-    w_all, z_acc = refs[:2]
-    kbuf, sems = (None, None) if resident else refs[2:]
+    if first:
+        inv_ref, refs = refs[0], refs[1:]
+    else:
+        t_ref, s_refs, refs = refs[0], refs[1:4], refs[4:]
+    near, near_y, cross = refs[:3]
+    w_all, z_acc = refs[3:5]
+    kbuf, sems = (None, None) if resident else refs[5:]
     row, col = place[0], place[1]
     total = groups[0]
 
@@ -180,7 +185,10 @@
 
     def place_piece(r, load):
         for k in range(own_rows):
-            w_all[r * own_rows + k] = load(slice(None), slice(k * block_len, (k + 1) * block_len))
+            w = load(slice(None), slice(k * block_len, (k + 1) * block_len))
+            if first:
+                w = (w * inv_ref[pl.ds(r * own_rows + k, 1), :]).astype(BF16)
+            w_all[r * own_rows + k] = w
 
     each_piece(pieces, row, place_piece)
     z_acc[...] = jnp.zeros_like(z_acc)
@@ -210,36 +218,38 @@
 
     lax.fori_loop(0, total, step, 0)
     own_len = own_rows * block_len
+    z_refs = (near, cross.at[0], near_y, cross.at[1])
     for e in range(n_cols):
         for k in range(own_rows):
             z_refs[e][:, k * block_len:(k + 1) * block_len] = z_acc[(col ^ e) * own_rows + k]
-    if products:
-        ts2 = jnp.zeros((t_ref.shape[0], 1), F32)
-        s1s2 = jnp.zeros((t_ref.shape[0], 1), F32)
-        for e in range(n_cols):
+    if not first:
+        outputs = t_ref.shape[0]
+        ts2 = jnp.zeros((outputs, 1), F32)
+        s1s2 = jnp.zeros((outputs, 1), F32)
+        for e, packed in enumerate(by_col(s_refs)):
             at = pl.ds(pl.multiple_of((col ^ e) * own_len, LANES), own_len)
-            scaled = z_refs[e][:, :own_len] * inv_ref[:, at]
+            scaled = z_refs[e][:, :own_len] * packed[outputs:outputs + 1, :]
             ts2 += jnp.sum(t_ref[:, at] * scaled, axis=1, keepdims=True)
-            s1s2 += jnp.sum(s_refs[e][...] * scaled, axis=1, keepdims=True)
+            s1s2 += jnp.sum(packed[:outputs, :] * scaled, axis=1, keepdims=True)
         t = t_ref[:, pl.ds(pl.multiple_of(col * own_len, LANES), own_len)]
-        s1 = s_refs[0][...]
+        s1 = s_refs[0][:outputs, :]
         tt = jnp.sum(t * t, axis=1, keepdims=True)
         ts1 = jnp.sum(t * s1, axis=1, keepdims=True)
         s1s1 = jnp.sum(s1 * s1, axis=1, keepdims=True)
         ts2 += SHIFT * ts1
         s1s2 += SHIFT * s1s1
-        lane = lax.broadcasted_iota(jnp.int32, (t_ref.shape[0], LANES), 1)
+        lane = lax.broadcasted_iota(jnp.int32, (outputs, LANES), 1)
         out = jnp.zeros(lane.shape, F32)
         for n, v in enumerate((tt, ts1, s1s1, ts2, s1s2)):
             out = jnp.where(lane == n, v, out)
-        for e in range(n_cols):
-            z_refs[e][:, own_len:] = out
+        for ref in z_refs:
+            ref[:, own_len:] = out
 
 
 def final_kernel(n_cols, place, t_ref, dots_a, dots_b, *refs):
-    s1s, ends = refs[:n_cols], refs[n_cols:2 * n_cols]
-    sol_ref, res_ref = refs[2 * n_cols:]
-    own_len = s1s[0].shape[1]
+    s1s, s2s = by_col(refs[:3]), by_col(refs[3:6])
+    sol_ref, res_ref = refs[6:]
+    outputs, own_len = s2s[0].shape
     dots = dots_a[...] + dots_b[...]
     tt, ts1, s1s1, ts2, s1s2 = (dots[:, n:n + 1] for n in range(5))
     a1 = tt / (REG * tt + ts1)
@@ -251,7 +261,7 @@
     a2 = new / (REG * dd + dmd)
     for e in range(n_cols):
         at = pl.ds(pl.multiple_of((place[1] ^ e) * own_len, LANES), own_len)
-        t, s1, s2 = t_ref[:, at], s1s[e][...], ends[e][...]
+        t, s1, s2 = t_ref[:, at], s1s[e][:outputs, :], s2s[e][...]
         sol_ref[:, at] = (a1 + a2 * u) * t - (a2 * a1) * s1
         res_ref[:, at] = (p - a2 * REG * u) * t - (a1 + a2 * (u - REG * a1)) * s1 + (a2 * a1) * s2
 
@@ -261,15 +271,28 @@
     return lax.ppermute(x, axis, [(i, i ^ d) for i in range(size)])
 
 
-def from_cols(x):
-    return [x] + [swap(x, "cols", e) for e in range(1, lax.axis_size("cols"))]
-
-
-def from_rows(x):
-    size = lax.axis_size("rows")
-    if size > DIRECT_ROWS:
-        return [lax.all_gather(x, "rows")]
-    same = jnp.stack([x] + [swap(x, "rows", d) for d in range(2, size, 2)])
+def spread(x):
+    across = swap(x, "cols", 2)
+    return [x, across, swap(jnp.stack([x, across]), "cols", 1)]
+
+
+def shared(near, near_y, cross):
+    got = swap(cross, "cols", 1)
+    far = swap(near_y + got[1], "cols", 2)
+    return (near + got[0]) + far
+
+
+def pair_sum(parts):
+    while len(parts) > 1:
+        parts = [a + b for a, b in zip(parts[::2], parts[1::2])]
+    return parts[0]
+
+
+def along_z(x):
+    return [x] + [swap(x, "rows", d) for d in range(2, lax.axis_size("rows"), 2)]
+
+
+def across_x(same):
     return [same, swap(same, "rows", 1)]
 
 
@@ -303,15 +326,35 @@
     def shape(*dims, dtype=F32):
         return jax.ShapeDtypeStruct(dims, dtype)
 
-    lists = jnp.concatenate(from_cols(block_list), axis=1)
+    direct_rows = n_rows <= DIRECT_ROWS
+
+    def own(x):
+        return lax.dynamic_slice_in_dim(x, col * own_len, own_len, 1)
+
+    def from_rows(x):
+        return across_x(jnp.stack(along_z(x))) if direct_rows else [lax.all_gather(x, "rows")]
+
+    def total_rows(x):
+        if direct_rows:
+            return pair_sum(across_x(pair_sum(along_z(x))))
+        return lax.psum(x, "rows")
+
+    lists = jnp.concatenate([block_list, swap(block_list, "cols", 1)], axis=1)
+    lists = jnp.concatenate([lists, swap(lists, "cols", 2)], axis=1)
     names = jnp.arange(nb, dtype=jnp.int32)
     direct = jnp.sum((lists[:, :, None] == names).astype(jnp.int32), axis=1)
     own_counts = lax.dynamic_slice_in_dim(direct, col * own_rows, own_rows, 0)
     count_rows = -(-own_rows * nb // LANES)
     coded = own_counts.reshape(-1)
     coded = jnp.pad(coded, (0, dim * LANES - coded.shape[0])).reshape(dim, LANES).astype(BF16)
-    own_points = lax.dynamic_slice_in_dim(points, col * own_len, own_len, 1)
-    pieces = from_rows(jnp.concatenate([own_points, coded], axis=1))
+    packed = jnp.concatenate([own(points), coded], axis=1)
+    own_t = own(targets)
+    if direct_rows:
+        packed, early_t = lax.optimization_barrier((packed, own_t))
+        pieces = from_rows(packed)
+        t_stack = jnp.stack(along_z(early_t))
+    else:
+        pieces = from_rows(packed)
 
     k_mat, ilist, jlist, groups, degree = pl.pallas_call(
         functools.partial(
@@ -323,13 +366,13 @@
             shape(list_len, dtype=jnp.int32),
             shape(list_len, dtype=jnp.int32),
             shape(1, dtype=jnp.int32),
-            shape(1, npoints),
+            shape(n_sub, block_len),
         ),
         in_specs=[SMEM, SMEM, VMEM] + [VMEM] * len(pieces),
         out_specs=(k_spec, SMEM, SMEM, SMEM, VMEM),
         scratch_shapes=[
             pltpu.SMEM((list_len,), jnp.int32),
-            pltpu.VMEM((block_rows, block_len, LANES), F32),
+            pltpu.VMEM((n_sub, 8, block_len), F32),
             pltpu.VMEM((block_rows, block_len, 2 * dim), BF16),
             pltpu.VMEM((n_sub, 2 * dim, block_len), BF16),
             pltpu.VMEM((n_rows, count_rows, LANES), jnp.int32),
@@ -344,26 +387,21 @@
     if resident:
         k_mat = pltpu.with_memory_space_constraint(k_mat, pltpu.VMEM)
 
-    def own(x):
-        return lax.dynamic_slice_in_dim(x, col * own_len, own_len, 1)
-
-    own_t = own(targets)
-    inv = 1.0 / jnp.sqrt(1.0 + sum(from_cols(degree)))
-    own_inv = own(inv)
-    w1 = (own_t * own_inv).astype(BF16)
-
-    def apply(w, s_pieces):
-        pieces = from_rows(w)
-        products = s_pieces is not None
-        extra = [inv, targets, *s_pieces] if products else []
-        width = own_len + LANES if products else own_len
-        z = pl.pallas_call(
+    t_pieces = across_x(t_stack) if direct_rows else from_rows(own_t)
+    inv = 1.0 / jnp.sqrt(1.0 + total_rows(degree))
+    own_inv = lax.dynamic_slice_in_dim(inv, row * own_rows, own_rows, 0).reshape(1, own_len)
+
+    def apply(pieces, extra, width):
+        first = len(extra) == 1
+        return shared(*pl.pallas_call(
             functools.partial(
-                apply_kernel, (len(pieces), n_cols, own_rows, block_len, products, resident)
+                apply_kernel, (len(pieces), n_cols, own_rows, block_len, first, resident)
             ),
-            out_shape=[shape(outputs, width)] * n_cols,
+            out_shape=[
+                shape(outputs, width), shape(outputs, width), shape(2, outputs, width)
+            ],
             in_specs=[SMEM] * 4 + [k_spec] + [VMEM] * (len(pieces) + len(extra)),
-            out_specs=[VMEM] * n_cols,
+            out_specs=[VMEM] * 3,
             scratch_shapes=[
                 pltpu.VMEM((n_sub, outputs, block_len), BF16),
                 pltpu.VMEM((block_rows, outputs, block_len), F32),
@@ -371,28 +409,26 @@
             ],
             compiler_params=limit,
             name="apply",
-        )(place, ilist, jlist, groups, k_mat, *pieces, *extra)
-        return sum([z[0]] + [swap(z[e], "cols", e) for e in range(1, n_cols)])
-
-    s1 = apply(w1, None) * own_inv
+        )(place, ilist, jlist, groups, k_mat, *pieces, *extra))
+
+    s1 = apply(t_pieces, [inv], own_len) * own_inv
     g = ((s1 - SHIFT * own_t) * own_inv).astype(BF16)
-    s1_pieces = from_cols(s1)
-    z2 = apply(g, s1_pieces)
+    s1_all = spread(jnp.concatenate([s1, jnp.broadcast_to(own_inv, (8, own_len))], axis=0))
+    z2 = apply(from_rows(g), [targets, *s1_all], own_len + LANES)
     s2 = z2[:, :own_len] * own_inv + SHIFT * s1
     dots = z2[:, own_len:]
-    if n_rows > DIRECT_ROWS:
+    if direct_rows:
+        dots = across_x(pair_sum(along_z(dots)))
+    else:
         dots = [lax.psum(dots, "rows"), jnp.zeros_like(dots)]
-    else:
-        dots = dots + sum(swap(dots, "rows", d) for d in range(2, n_rows, 2))
-        dots = [dots, swap(dots, "rows", 1)]
 
     return pl.pallas_call(
         functools.partial(final_kernel, n_cols),
         out_shape=(shape(outputs, npoints), shape(outputs, npoints)),
-        in_specs=[SMEM] + [VMEM] * (3 + 2 * n_cols),
+        in_specs=[SMEM] + [VMEM] * 9,
         out_specs=(VMEM, VMEM),
         name="final",
-    )(place, targets, *dots, *s1_pieces, *from_cols(s2))
+    )(place, targets, *dots, *s1_all, *spread(s2))
 
 
 def solution(mesh):

time: 97.2 us -> 106 us (1.091)
  local copies, waits for them, and re-layouts: 2.9 us -> 15.3 us
  waiting for transfers between devices: 36.5 us -> 32.1 us
  Pallas kernels: 19 us -> 21.3 us
    unnamed x26 -> x28, local copies, waits for them, and re-layouts: 2.08 us -> 13.6 us
    ppermute x34 -> x30, waiting for transfers between devices: 36.5 us -> 32.1 us  [swap(): return lax.ppermute(x, axis, [(i, i ^ d) for i in range(size)])]
    dynamic_slice x1 -> x2, local copies, waits for them, and re-layouts: 0.01 us -> 1.56 us  [own(): return lax.dynamic_slice_in_dim(x, col * own_len, own_len, 1)]
    pallas_call x1, Pallas kernels: 9.13 us -> 10.3 us  [local(): pl.pallas_call(functools.partial(build_kernel, (len(pieces), nb, block_le...]
    ppermute x34 -> x30, starting transfers between devices: 34.6 us -> 34.1 us  [swap(): return lax.ppermute(x, axis, [(i, i ^ d) for i in range(size)])]
  transfers between devices with their start and end apart: 34 -> 30, of which waited for: 19 -> 18; matrix products, arithmetic and copies ran while one was open for 2% -> 2% of each run, Pallas kernels for 0% -> 10%
where the time goes in v1:
time: 106 us
  starting transfers between devices  34.1 us (32%)
  waiting for transfers between devices  32.1 us (30%)
  Pallas kernels  21.3 us (20%)
  local copies, waits for them, and re-layouts  15.3 us (14%)
  other arithmetic  1.91 us (2%)
    ppermute x30, starting transfers between devices, swap(): return lax.ppermute(x, axis, [(i, i ^ d) for i in range(size)])  34.1 us
    ppermute x30, waiting for transfers between devices, swap(): return lax.ppermute(x, axis, [(i, i ^ d) for i in range(size)])  32.1 us
    unnamed x28, local copies, waits for them, and re-layouts  13.6 us
    pallas_call x1, Pallas kernels, local(): pl.pallas_call(functools.partial(build_kernel, (len(pieces), nb, block_le...  10.3 us
    pallas_call x2, Pallas kernels, apply(): pl.pallas_call(functools.partial(apply_kernel, (len(pieces), n_cols, own_...  8.67 us
    pallas_call x1, Pallas kernels, local(): pl.pallas_call(functools.partial(final_kernel, n_cols), out_shape=(shape(...  2.34 us
  transfers between devices with their start and end apart: 30, of which 18 were waited for; matrix products, arithmetic and copies ran while one was open for 2% of the time, Pallas kernels for 10%

profile of v1, /device:TPU:0, one launch (start us, length us, event | category | flops | bytes accessed | tf_op | source)
XLA Modules:
  0.0 105.5 jit_solution(7367711699216329750)
XLA Ops:
  1.2 0.8 constant_dynamic-slice_fusion
  2.2 0.8 pad_add_fusion
  3.0 2.9 %collective-permute-start.1 = (s32[8,12]{1,0:T(8,128)S(1)}, s32[8,12]{1,0:T(8,128)S(1)}, u32[]{:S(2)}, u32[]{:S(2)}) collective-permute-start(s32[8,12]{1,0:T(8,128)S(1)} %pad_add_fusion), channel_id=1, source_target_pairs={{0,2},{1,3},{2,0},{3,1},{4,6},{5,7},{6,4},{7,5},{8,10},{9,11},{10,... | collective-permute-start | bytes 1160 | tf_op jit(solution)/shard_map/ppermute | solution.py:271
  5.8 0.7 constant_dynamic-slice_fusion.1
  6.5 0.9 collective-permute-done.1
  7.4 0.8 pad_add_fusion.1
  8.4 4.2 %collective-permute-start.4 = (bf16[16,640]{1,0:T(8,128)(2,1)S(1)}, bf16[16,640]{1,0:T(8,128)(2,1)S(1)}, u32[]{:S(2)}, u32[]{:S(2)}) collective-permute-start(bf16[16,640]{1,0:T(8,128)(2,1)S(1)} %pad_maximum_fusion.6), channel_id=1, source_target_pairs={{0,24},{4,28},{8,16},{12,20},{16,8},{20,12},{24,0},{28,4},{1,25},{... | collective-permute-start | bytes 61448 | tf_op jit(solution)/shard_map/ppermute | solution.py:271
  12.5 0.6 collective-permute-start.2
  13.2 3.7 %collective-permute-start.8 = (f32[32,512]{1,0:T(8,128)S(1)}, f32[32,512]{1,0:T(8,128)S(1)}, u32[]{:S(2)}, u32[]{:S(2)}) collective-permute-start(f32[32,512]{1,0:T(8,128)S(1)} %constant_dynamic-slice_fusion), channel_id=1, source_target_pairs={{0,24},{4,28},{8,16},{12,20},{16,8},{20,12},{24,0},{28,4},{1,25},{... | collective-permute-start | bytes 196616 | tf_op jit(solution)/shard_map/ppermute | solution.py:271
  16.9 0.6 collective-permute-start.6
  17.6 0.5 collective-permute-done.3
  18.2 1.6 %collective-permute-start.5 = (bf16[4,16,640]{2,1,0:T(8,128)(2,1)S(1)}, bf16[4,16,640]{2,1,0:T(8,128)(2,1)S(1)}, u32[]{:S(2)}, u32[]{:S(2)}) collective-permute-start(bf16[4,16,640]{2,1,0:T(8,128)(2,1)S(1)} %pad_maximum_fusion.4.refs_0_), channel_id=1, source_target_pairs={{0,4},{4,0},{8,12},{12,8},{16,20},{20,16},{24,28},{28,24},{1,5},{5... | collective-permute-start | bytes 245768 | tf_op jit(solution)/shard_map/ppermute | solution.py:271
  19.8 2.9 %collective-permute-done.5.refs_1_ = bf16[4,16,640]{2,1,0:T(8,128)(2,1)S(1)} collective-permute-done((bf16[4,16,640]{2,1,0:T(8,128)(2,1)S(1)}, bf16[4,16,640]{2,1,0:T(8,128)(2,1)S(1)}, u32[]{:S(2)}, u32[]{:S(2)}) %collective-permute-start.5) | collective-permute-done | bytes 81952 | tf_op jit(solution)/shard_map/ppermute | solution.py:271
  22.7 0.8 copy-done.6
  23.5 10.3 %build.1 = (bf16[32,4,256,256]{3,2,1,0:T(8,128)(2,1)S(1)}, s32[132]{0:T(256)S(1)}, s32[132]{0:T(256)S(1)}, s32[1]{0:T(128)}, f32[16,256]{1,0:T(8,128)S(1)}) custom-call(s32[2]{0:T(128)S(1)} %pad_add_fusion.2.place, s32[8,64]{1,0:T(8,128)S(1)} %convert_reduce_fusion.direct, bf16[16,2048]{1,0:T(8,128)(2,1)S(1)} %copy-done.6, ...), custom_call_target="tpu_custom_call" | custom-call | tf_op jit(solution)/shard_map/build/pallas_call | solution.py:359
  33.8 2.1 %collective-permute-start.12 = (f32[16,256]{1,0:T(8,128)S(1)}, f32[16,256]{1,0:T(8,128)S(1)}, u32[]{:S(2)}, u32[]{:S(2)}) collective-permute-start(f32[16,256]{1,0:T(8,128)S(1)} %get-tuple-element.21), channel_id=1, source_target_pairs={{0,24},{4,28},{8,16},{12,20},{16,8},{20,12},{24,0},{28,4},{1,25},{... | collective-permute-start | bytes 49160 | tf_op jit(solution)/shard_map/ppermute | solution.py:271
  35.9 2.3 %collective-permute-start.10 = (f32[16,256]{1,0:T(8,128)S(1)}, f32[16,256]{1,0:T(8,128)S(1)}, u32[]{:S(2)}, u32[]{:S(2)}) collective-permute-start(f32[16,256]{1,0:T(8,128)S(1)} %get-tuple-element.21), channel_id=1, source_target_pairs={{0,8},{4,12},{8,0},{12,4},{16,24},{20,28},{24,16},{28,20},{1,9},{5... | collective-permute-start | bytes 49160 | tf_op jit(solution)/shard_map/ppermute | solution.py:271
  38.7 0.7 collective-permute-done.12
  39.4 1.1 %collective-permute-done.11 = f32[16,256]{1,0:T(8,128)S(1)} collective-permute-done((f32[16,256]{1,0:T(8,128)S(1)}, f32[16,256]{1,0:T(8,128)S(1)}, u32[]{:S(2)}, u32[]{:S(2)}) %collective-permute-start.11) | collective-permute-done | bytes 16416 | tf_op jit(solution)/shard_map/ppermute | solution.py:271
  40.6 1.6 %collective-permute-start.13 = (f32[16,256]{1,0:T(8,128)S(1)}, f32[16,256]{1,0:T(8,128)S(1)}, u32[]{:S(2)}, u32[]{:S(2)}) collective-permute-start(f32[16,256]{1,0:T(8,128)S(1)} %add_add_fusion.1), channel_id=1, source_target_pairs={{0,4},{4,0},{8,12},{12,8},{16,20},{20,16},{24,28},{28,24},{1,5},{5... | collective-permute-start | bytes 49160 | tf_op jit(solution)/shard_map/ppermute | solution.py:271
  42.2 2.7 %collective-permute-done.13 = f32[16,256]{1,0:T(8,128)S(1)} collective-permute-done((f32[16,256]{1,0:T(8,128)S(1)}, f32[16,256]{1,0:T(8,128)S(1)}, u32[]{:S(2)}, u32[]{:S(2)}) %collective-permute-start.13) | collective-permute-done | bytes 16416 | tf_op jit(solution)/shard_map/ppermute | solution.py:271
  45.0 4.3 %apply.2 = (f32[32,512]{1,0:T(8,128)S(1)}, f32[32,512]{1,0:T(8,128)S(1)}, f32[2,32,512]{2,1,0:T(8,128)S(1)}) custom-call(s32[2]{0:T(128)S(1)} %pad_add_fusion.2.place, s32[132]{0:T(256)S(1)} %get-tuple-element.16.ilist, s32[132]{0:T(256)S(1)} %get-tuple-element.17.jlist, s32[1]{0:T(128)} %get-tuple-element.18.groups, ...), custom_call_target="tpu_custom_call" | custom-call | tf_op jit(solution)/shard_map/apply/pallas_call | solution.py:396
  49.3 5.7 %copy-done = bf16[32,4,256,256]{3,2,1,0:T(8,128)(2,1)} copy-done((bf16[32,4,256,256]{3,2,1,0:T(8,128)(2,1)}, bf16[32,4,256,256]{3,2,1,0:T(8,128)(2,1)S(1)}, u32[]{:S(2)}) %copy-start) | copy-done | bytes 16777240
  55.0 1.3 %collective-permute-done.14 = f32[2,32,512]{2,1,0:T(8,128)S(1)} collective-permute-done((f32[2,32,512]{2,1,0:T(8,128)S(1)}, f32[2,32,512]{2,1,0:T(8,128)S(1)}, u32[]{:S(2)}, u32[]{:S(2)}) %collective-permute-start.14) | collective-permute-done | bytes 131104 | tf_op jit(solution)/shard_map/ppermute | solution.py:271
  56.4 0.8 collective-permute-start.15
  57.2 3.5 %collective-permute-done.15 = f32[32,512]{1,0:T(8,128)S(1)} collective-permute-done((f32[32,512]{1,0:T(8,128)S(1)}, f32[32,512]{1,0:T(8,128)S(1)}, u32[]{:S(2)}, u32[]{:S(2)}) %collective-permute-start.15) | collective-permute-done | bytes 65568 | tf_op jit(solution)/shard_map/ppermute | solution.py:271
  60.8 0.8 collective-permute-start.20
  61.5 2.3 %collective-permute-start.18 = (bf16[32,512]{1,0:T(8,128)(2,1)S(1)}, bf16[32,512]{1,0:T(8,128)(2,1)S(1)}, u32[]{:S(2)}, u32[]{:S(2)}) collective-permute-start(bf16[32,512]{1,0:T(8,128)(2,1)S(1)} %get-tuple-element.28), channel_id=1, source_target_pairs={{0,24},{4,28},{8,16},{12,20},{16,8},{20,12},{24,0},{28,4},{1,25},{... | collective-permute-start | bytes 98312 | tf_op jit(solution)/shard_map/ppermute | solution.py:271
  63.8 2.1 %collective-permute-start.16 = (bf16[32,512]{1,0:T(8,128)(2,1)S(1)}, bf16[32,512]{1,0:T(8,128)(2,1)S(1)}, u32[]{:S(2)}, u32[]{:S(2)}) collective-permute-start(bf16[32,512]{1,0:T(8,128)(2,1)S(1)} %get-tuple-element.28), channel_id=1, source_target_pairs={{0,8},{4,12},{8,0},{12,4},{16,24},{20,28},{24,16},{28,20},{1,9},{5... | collective-permute-start | bytes 98312 | tf_op jit(solution)/shard_map/ppermute | solution.py:271
  66.0 1.5 %collective-permute-done.18 = bf16[32,512]{1,0:T(8,128)(2,1)S(1)} collective-permute-done((bf16[32,512]{1,0:T(8,128)(2,1)S(1)}, bf16[32,512]{1,0:T(8,128)(2,1)S(1)}, u32[]{:S(2)}, u32[]{:S(2)}) %collective-permute-start.18) | collective-permute-done | bytes 32800 | tf_op jit(solution)/shard_map/ppermute | solution.py:271
  67.6 1.1 %collective-permute-done.17 = bf16[32,512]{1,0:T(8,128)(2,1)S(1)} collective-permute-done((bf16[32,512]{1,0:T(8,128)(2,1)S(1)}, bf16[32,512]{1,0:T(8,128)(2,1)S(1)}, u32[]{:S(2)}, u32[]{:S(2)}) %collective-permute-start.17) | collective-permute-done | bytes 32800 | tf_op jit(solution)/shard_map/ppermute | solution.py:271
  68.7 0.7 collective-permute-start.19
  69.4 4.3 %collective-permute-done.19.refs_1_ = bf16[4,32,512]{2,1,0:T(8,128)(2,1)S(1)} collective-permute-done((bf16[4,32,512]{2,1,0:T(8,128)(2,1)S(1)}, bf16[4,32,512]{2,1,0:T(8,128)(2,1)S(1)}, u32[]{:S(2)}, u32[]{:S(2)}) %collective-permute-start.19) | collective-permute-done | bytes 131104 | tf_op jit(solution)/shard_map/ppermute | solution.py:271
  73.7 5.8 %copy-done.1 = bf16[32,4,256,256]{3,2,1,0:T(8,128)(2,1)S(1)} copy-done((bf16[32,4,256,256]{3,2,1,0:T(8,128)(2,1)S(1)}, bf16[32,4,256,256]{3,2,1,0:T(8,128)(2,1)}, u32[]{:S(2)}) %copy-start.1) | copy-done | bytes 16777240
  79.5 4.4 %apply.3 = (f32[32,640]{1,0:T(8,128)S(1)}, f32[32,640]{1,0:T(8,128)S(1)}, f32[2,32,640]{2,1,0:T(8,128)S(1)}) custom-call(s32[2]{0:T(128)S(1)} %pad_add_fusion.2.place, s32[132]{0:T(256)S(1)} %get-tuple-element.16.ilist, s32[132]{0:T(256)S(1)} %get-tuple-element.17.jlist, s32[1]{0:T(128)} %get-tuple-element.18.groups, ...), custom_call_target="tpu_custom_call" | custom-call | tf_op jit(solution)/shard_map/apply/pallas_call | solution.py:396
  84.0 1.4 %collective-permute-done.22 = f32[2,32,640]{2,1,0:T(8,128)S(1)} collective-permute-done((f32[2,32,640]{2,1,0:T(8,128)S(1)}, f32[2,32,640]{2,1,0:T(8,128)S(1)}, u32[]{:S(2)}, u32[]{:S(2)}) %collective-permute-start.22) | collective-permute-done | bytes 163872 | tf_op jit(solution)/shard_map/ppermute | solution.py:271
  85.4 0.6 collective-permute-start.23
  86.0 3.9 %collective-permute-done.23 = f32[32,640]{1,0:T(8,128)S(1)} collective-permute-done((f32[32,640]{1,0:T(8,128)S(1)}, f32[32,640]{1,0:T(8,128)S(1)}, u32[]{:S(2)}, u32[]{:S(2)}) %collective-permute-start.23) | collective-permute-done | bytes 81952 | tf_op jit(solution)/shard_map/ppermute | solution.py:271
  90.0 0.6 collective-permute-start.28
  90.6 1.4 %collective-permute-start.25 = (f32[32,128]{1,0:T(8,128)S(1)}, f32[32,128]{1,0:T(8,128)S(1)}, u32[]{:S(2)}, u32[]{:S(2)}) collective-permute-start(f32[32,128]{1,0:T(8,128)S(1)} %slice.28), channel_id=1, source_target_pairs={{0,16},{4,20},{8,24},{12,28},{16,0},{20,4},{24,8},{28,12},{1,17},{... | collective-permute-start | bytes 49160 | tf_op jit(solution)/shard_map/ppermute | solution.py:271
  92.0 2.3 %collective-permute-start.26 = (f32[32,128]{1,0:T(8,128)S(1)}, f32[32,128]{1,0:T(8,128)S(1)}, u32[]{:S(2)}, u32[]{:S(2)}) collective-permute-start(f32[32,128]{1,0:T(8,128)S(1)} %slice.28), channel_id=1, source_target_pairs={{0,24},{4,28},{8,16},{12,20},{16,8},{20,12},{24,0},{28,4},{1,25},{... | collective-permute-start | bytes 49160 | tf_op jit(solution)/shard_map/ppermute | solution.py:271
  94.5 0.8 collective-permute-done.25
  95.3 2.3 %collective-permute-done.26 = f32[32,128]{1,0:T(8,128)S(1)} collective-permute-done((f32[32,128]{1,0:T(8,128)S(1)}, f32[32,128]{1,0:T(8,128)S(1)}, u32[]{:S(2)}, u32[]{:S(2)}) %collective-permute-start.26) | collective-permute-done | bytes 16416 | tf_op jit(solution)/shard_map/ppermute | solution.py:271
  97.6 0.5 collective-permute-done.24
  98.1 1.6 %collective-permute-start.27 = (f32[32,128]{1,0:T(8,128)S(1)}, f32[32,128]{1,0:T(8,128)S(1)}, u32[]{:S(2)}, u32[]{:S(2)}) collective-permute-start(f32[32,128]{1,0:T(8,128)S(1)} %add_add_fusion.dots_a), channel_id=1, source_target_pairs={{0,4},{4,0},{8,12},{12,8},{16,20},{20,16},{24,28},{28,24},{1,5},{5... | collective-permute-start | bytes 49160 | tf_op jit(solution)/shard_map/ppermute | solution.py:271
  99.8 2.2 %collective-permute-done.27.dots_b = f32[32,128]{1,0:T(8,128)S(1)} collective-permute-done((f32[32,128]{1,0:T(8,128)S(1)}, f32[32,128]{1,0:T(8,128)S(1)}, u32[]{:S(2)}, u32[]{:S(2)}) %collective-permute-start.27) | collective-permute-done | bytes 16416 | tf_op jit(solution)/shard_map/ppermute | solution.py:271
  102.5 0.7 copy-done.10
  103.2 2.3 %final.1 = (f32[32,2048]{1,0:T(8,128)}, f32[32,2048]{1,0:T(8,128)}) custom-call(s32[2]{0:T(128)} %copy-done.7, f32[32,2048]{1,0:T(8,128)} %t_ref.1, f32[32,128]{1,0:T(8,128)} %copy-done.11, f32[32,128]{1,0:T(8,128)} %copy-done.12, f32[40,512]{1,0:T(8,128)} %copy-done.4, f32[40,512]{1,0:T(8,128)} %copy-done.3, f32[2,40,512]{2,1,0:T(8,128)} %copy-done.5, ...), custom_call_target="tpu_custom_call" | custom-call | tf_op jit(solution)/shard_map/final/pallas_call | solution.py:425
  (70 shorter events, 2.4 us)
Async XLA Ops:
  0.6 60.1 %copy-start.2 = (f32[32,2048]{1,0:T(8,128)S(1)}, f32[32,2048]{1,0:T(8,128)}, u32[]{:S(2)}) copy-start(f32[32,2048]{1,0:T(8,128)} %t_ref.1) | copy-start | bytes 786436
  0.6 1.6 %collective-permute-start = (s32[8,6]{1,0:T(8,128)}, s32[8,6]{1,0:T(8,128)S(1)}, u32[]{:S(2)}, u32[]{:S(2)}) collective-permute-start(s32[8,6]{1,0:T(8,128)} %param.3), channel_id=1, source_target_pairs={{0,1},{1,0},{2,3},{3,2},{4,5},{5,4},{6,7},{7,6},{8,9},{9,8},{10,11... | collective-permute-start | bytes 584 | tf_op jit(solution)/shard_map/ppermute | solution.py:271
  3.0 4.4 %collective-permute-start.1 = (s32[8,12]{1,0:T(8,128)S(1)}, s32[8,12]{1,0:T(8,128)S(1)}, u32[]{:S(2)}, u32[]{:S(2)}) collective-permute-start(s32[8,12]{1,0:T(8,128)S(1)} %pad_add_fusion), channel_id=1, source_target_pairs={{0,2},{1,3},{2,0},{3,1},{4,6},{5,7},{6,4},{7,5},{8,10},{9,11},{10,... | collective-permute-start | bytes 1160 | tf_op jit(solution)/shard_map/ppermute | solution.py:271
  8.4 8.6 %collective-permute-start.4 = (bf16[16,640]{1,0:T(8,128)(2,1)S(1)}, bf16[16,640]{1,0:T(8,128)(2,1)S(1)}, u32[]{:S(2)}, u32[]{:S(2)}) collective-permute-start(bf16[16,640]{1,0:T(8,128)(2,1)S(1)} %pad_maximum_fusion.6), channel_id=1, source_target_pairs={{0,24},{4,28},{8,16},{12,20},{16,8},{20,12},{24,0},{28,4},{1,25},{... | collective-permute-start | bytes 61448 | tf_op jit(solution)/shard_map/ppermute | solution.py:271
  12.5 5.6 %collective-permute-start.3 = (bf16[16,640]{1,0:T(8,128)(2,1)S(1)}, bf16[16,640]{1,0:T(8,128)(2,1)S(1)}, u32[]{:S(2)}, u32[]{:S(2)}) collective-permute-start(bf16[16,640]{1,0:T(8,128)(2,1)S(1)} %pad_maximum_fusion.6), channel_id=1, source_target_pairs={{0,16},{4,20},{8,24},{12,28},{16,0},{20,4},{24,8},{28,12},{1,17},{... | collective-permute-start | bytes 61448 | tf_op jit(solution)/shard_map/ppermute | solution.py:271
  12.5 5.6 %collective-permute-start.2 = (bf16[16,640]{1,0:T(8,128)(2,1)S(1)}, bf16[16,640]{1,0:T(8,128)(2,1)S(1)}, u32[]{:S(2)}, u32[]{:S(2)}) collective-permute-start(bf16[16,640]{1,0:T(8,128)(2,1)S(1)} %pad_maximum_fusion.6), channel_id=1, source_target_pairs={{0,8},{4,12},{8,0},{12,4},{16,24},{20,28},{24,16},{28,20},{1,9},{5... | collective-permute-start | bytes 61448 | tf_op jit(solution)/shard_map/ppermute | solution.py:271
  13.2 22.8 %collective-permute-start.8 = (f32[32,512]{1,0:T(8,128)S(1)}, f32[32,512]{1,0:T(8,128)S(1)}, u32[]{:S(2)}, u32[]{:S(2)}) collective-permute-start(f32[32,512]{1,0:T(8,128)S(1)} %constant_dynamic-slice_fusion), channel_id=1, source_target_pairs={{0,24},{4,28},{8,16},{12,20},{16,8},{20,12},{24,0},{28,4},{1,25},{... | collective-permute-start | bytes 196616 | tf_op jit(solution)/shard_map/ppermute | solution.py:271
  16.9 21.4 %collective-permute-start.7 = (f32[32,512]{1,0:T(8,128)S(1)}, f32[32,512]{1,0:T(8,128)S(1)}, u32[]{:S(2)}, u32[]{:S(2)}) collective-permute-start(f32[32,512]{1,0:T(8,128)S(1)} %constant_dynamic-slice_fusion), channel_id=1, source_target_pairs={{0,16},{4,20},{8,24},{12,28},{16,0},{20,4},{24,8},{28,12},{1,17},{... | collective-permute-start | bytes 196616 | tf_op jit(solution)/shard_map/ppermute | solution.py:271
  16.9 21.4 %collective-permute-start.6 = (f32[32,512]{1,0:T(8,128)S(1)}, f32[32,512]{1,0:T(8,128)S(1)}, u32[]{:S(2)}, u32[]{:S(2)}) collective-permute-start(f32[32,512]{1,0:T(8,128)S(1)} %constant_dynamic-slice_fusion), channel_id=1, source_target_pairs={{0,8},{4,12},{8,0},{12,4},{16,24},{20,28},{24,16},{28,20},{1,9},{5... | collective-permute-start | bytes 196616 | tf_op jit(solution)/shard_map/ppermute | solution.py:271
  18.2 4.5 %collective-permute-start.5 = (bf16[4,16,640]{2,1,0:T(8,128)(2,1)S(1)}, bf16[4,16,640]{2,1,0:T(8,128)(2,1)S(1)}, u32[]{:S(2)}, u32[]{:S(2)}) collective-permute-start(bf16[4,16,640]{2,1,0:T(8,128)(2,1)S(1)} %pad_maximum_fusion.4.refs_0_), channel_id=1, source_target_pairs={{0,4},{4,0},{8,12},{12,8},{16,20},{20,16},{24,28},{28,24},{1,5},{5... | collective-permute-start | bytes 245768 | tf_op jit(solution)/shard_map/ppermute | solution.py:271
  19.8 64.1 %copy-start.7 = (s32[2]{0:T(128)}, s32[2]{0:T(128)S(1)}, u32[]{:S(2)}) copy-start(s32[2]{0:T(128)S(1)} %pad_add_fusion.2.place) | copy-start | bytes 28
  22.7 0.8 copy-start.6
  33.8 5.6 %collective-permute-start.12 = (f32[16,256]{1,0:T(8,128)S(1)}, f32[16,256]{1,0:T(8,128)S(1)}, u32[]{:S(2)}, u32[]{:S(2)}) collective-permute-start(f32[16,256]{1,0:T(8,128)S(1)} %get-tuple-element.21), channel_id=1, source_target_pairs={{0,24},{4,28},{8,16},{12,20},{16,8},{20,12},{24,0},{28,4},{1,25},{... | collective-permute-start | bytes 49160 | tf_op jit(solution)/shard_map/ppermute | solution.py:271
  35.9 4.6 %collective-permute-start.11 = (f32[16,256]{1,0:T(8,128)S(1)}, f32[16,256]{1,0:T(8,128)S(1)}, u32[]{:S(2)}, u32[]{:S(2)}) collective-permute-start(f32[16,256]{1,0:T(8,128)S(1)} %get-tuple-element.21), channel_id=1, source_target_pairs={{0,16},{4,20},{8,24},{12,28},{16,0},{20,4},{24,8},{28,12},{1,17},{... | collective-permute-start | bytes 49160 | tf_op jit(solution)/shard_map/ppermute | solution.py:271
  35.9 4.6 %collective-permute-start.10 = (f32[16,256]{1,0:T(8,128)S(1)}, f32[16,256]{1,0:T(8,128)S(1)}, u32[]{:S(2)}, u32[]{:S(2)}) collective-permute-start(f32[16,256]{1,0:T(8,128)S(1)} %get-tuple-element.21), channel_id=1, source_target_pairs={{0,8},{4,12},{8,0},{12,4},{16,24},{20,28},{24,16},{28,20},{1,9},{5... | collective-permute-start | bytes 49160 | tf_op jit(solution)/shard_map/ppermute | solution.py:271
  38.3 6.6 %collective-permute-start.9 = (f32[4,32,512]{2,1,0:T(8,128)S(1)}, f32[4,32,512]{2,1,0:T(8,128)S(1)}, u32[]{:S(2)}, u32[]{:S(2)}) collective-permute-start(f32[4,32,512]{2,1,0:T(8,128)S(1)} %pad_maximum_fusion.refs_0_), channel_id=1, source_target_pairs={{0,4},{4,0},{8,12},{12,8},{16,20},{20,16},{24,28},{28,24},{1,5},{5... | collective-permute-start | bytes 786440 | tf_op jit(solution)/shard_map/ppermute | solution.py:271
  40.6 4.3 %collective-permute-start.13 = (f32[16,256]{1,0:T(8,128)S(1)}, f32[16,256]{1,0:T(8,128)S(1)}, u32[]{:S(2)}, u32[]{:S(2)}) collective-permute-start(f32[16,256]{1,0:T(8,128)S(1)} %add_add_fusion.1), channel_id=1, source_target_pairs={{0,4},{4,0},{8,12},{12,8},{16,20},{20,16},{24,28},{28,24},{1,5},{5... | collective-permute-start | bytes 49160 | tf_op jit(solution)/shard_map/ppermute | solution.py:271
  49.3 5.8 %copy-start = (bf16[32,4,256,256]{3,2,1,0:T(8,128)(2,1)}, bf16[32,4,256,256]{3,2,1,0:T(8,128)(2,1)S(1)}, u32[]{:S(2)}) copy-start(bf16[32,4,256,256]{3,2,1,0:T(8,128)(2,1)S(1)} %get-tuple-element.19.k_mat) | copy-start | bytes 50331652
  55.0 1.3 %collective-permute-start.14 = (f32[2,32,512]{2,1,0:T(8,128)S(1)}, f32[2,32,512]{2,1,0:T(8,128)S(1)}, u32[]{:S(2)}, u32[]{:S(2)}) collective-permute-start(f32[2,32,512]{2,1,0:T(8,128)S(1)} %get-tuple-element.23), channel_id=1, source_target_pairs={{0,1},{1,0},{2,3},{3,2},{4,5},{5,4},{6,7},{7,6},{8,9},{9,8},{10,11... | collective-permute-start | bytes 393224 | tf_op jit(solution)/shard_map/ppermute | solution.py:271
  56.4 4.3 %collective-permute-start.15 = (f32[32,512]{1,0:T(8,128)S(1)}, f32[32,512]{1,0:T(8,128)S(1)}, u32[]{:S(2)}, u32[]{:S(2)}) collective-permute-start(f32[32,512]{1,0:T(8,128)S(1)} %fusion.4), channel_id=1, source_target_pairs={{0,2},{1,3},{2,0},{3,1},{4,6},{5,7},{6,4},{7,5},{8,10},{9,11},{10,... | collective-permute-start | bytes 196616 | tf_op jit(solution)/shard_map/ppermute | solution.py:271
  60.8 41.2 %copy-start.4 = (f32[40,512]{1,0:T(8,128)}, f32[40,512]{1,0:T(8,128)S(1)}, u32[]{:S(2)}) copy-start(f32[40,512]{1,0:T(8,128)S(1)} %get-tuple-element.31.refs_3_.refs_0_) | copy-start | bytes 245764
  60.8 5.2 %collective-permute-start.20 = (f32[40,512]{1,0:T(8,128)S(1)}, f32[40,512]{1,0:T(8,128)S(1)}, u32[]{:S(2)}, u32[]{:S(2)}) collective-permute-start(f32[40,512]{1,0:T(8,128)S(1)} %get-tuple-element.31.refs_3_.refs_0_), channel_id=1, source_target_pairs={{0,2},{1,3},{2,0},{3,1},{4,6},{5,7},{6,4},{7,5},{8,10},{9,11},{10,... | collective-permute-start | bytes 245768 | tf_op jit(solution)/shard_map/ppermute | solution.py:271
  61.5 6.0 %collective-permute-start.18 = (bf16[32,512]{1,0:T(8,128)(2,1)S(1)}, bf16[32,512]{1,0:T(8,128)(2,1)S(1)}, u32[]{:S(2)}, u32[]{:S(2)}) collective-permute-start(bf16[32,512]{1,0:T(8,128)(2,1)S(1)} %get-tuple-element.28), channel_id=1, source_target_pairs={{0,24},{4,28},{8,16},{12,20},{16,8},{20,12},{24,0},{28,4},{1,25},{... | collective-permute-start | bytes 98312 | tf_op jit(solution)/shard_map/ppermute | solution.py:271
  63.8 4.8 %collective-permute-start.17 = (bf16[32,512]{1,0:T(8,128)(2,1)S(1)}, bf16[32,512]{1,0:T(8,128)(2,1)S(1)}, u32[]{:S(2)}, u32[]{:S(2)}) collective-permute-start(bf16[32,512]{1,0:T(8,128)(2,1)S(1)} %get-tuple-element.28), channel_id=1, source_target_pairs={{0,16},{4,20},{8,24},{12,28},{16,0},{20,4},{24,8},{28,12},{1,17},{... | collective-permute-start | bytes 98312 | tf_op jit(solution)/shard_map/ppermute | solution.py:271
  63.8 4.8 %collective-permute-start.16 = (bf16[32,512]{1,0:T(8,128)(2,1)S(1)}, bf16[32,512]{1,0:T(8,128)(2,1)S(1)}, u32[]{:S(2)}, u32[]{:S(2)}) collective-permute-start(bf16[32,512]{1,0:T(8,128)(2,1)S(1)} %get-tuple-element.28), channel_id=1, source_target_pairs={{0,8},{4,12},{8,0},{12,4},{16,24},{20,28},{24,16},{28,20},{1,9},{5... | collective-permute-start | bytes 98312 | tf_op jit(solution)/shard_map/ppermute | solution.py:271
  65.9 36.0 %copy-start.3 = (f32[40,512]{1,0:T(8,128)}, f32[40,512]{1,0:T(8,128)S(1)}, u32[]{:S(2)}) copy-start(f32[40,512]{1,0:T(8,128)S(1)} %collective-permute-done.20.refs_4_.refs_1_) | copy-start | bytes 245764
  66.0 7.8 %collective-permute-start.21 = (f32[2,40,512]{2,1,0:T(8,128)S(1)}, f32[2,40,512]{2,1,0:T(8,128)S(1)}, u32[]{:S(2)}, u32[]{:S(2)}) collective-permute-start(f32[2,40,512]{2,1,0:T(8,128)S(1)} %pad_maximum_fusion.1), channel_id=1, source_target_pairs={{0,1},{1,0},{2,3},{3,2},{4,5},{5,4},{6,7},{7,6},{8,9},{9,8},{10,11... | collective-permute-start | bytes 491528 | tf_op jit(solution)/shard_map/ppermute | solution.py:271
  68.7 5.0 %collective-permute-start.19 = (bf16[4,32,512]{2,1,0:T(8,128)(2,1)S(1)}, bf16[4,32,512]{2,1,0:T(8,128)(2,1)S(1)}, u32[]{:S(2)}, u32[]{:S(2)}) collective-permute-start(bf16[4,32,512]{2,1,0:T(8,128)(2,1)S(1)} %pad_maximum_fusion.2.refs_0_), channel_id=1, source_target_pairs={{0,4},{4,0},{8,12},{12,8},{16,20},{20,16},{24,28},{28,24},{1,5},{5... | collective-permute-start | bytes 393224 | tf_op jit(solution)/shard_map/ppermute | solution.py:271
  73.7 5.8 %copy-start.1 = (bf16[32,4,256,256]{3,2,1,0:T(8,128)(2,1)S(1)}, bf16[32,4,256,256]{3,2,1,0:T(8,128)(2,1)}, u32[]{:S(2)}) copy-start(bf16[32,4,256,256]{3,2,1,0:T(8,128)(2,1)} %copy-done) | copy-start | bytes 50331652
  79.5 22.5 %copy-start.5 = (f32[2,40,512]{2,1,0:T(8,128)}, f32[2,40,512]{2,1,0:T(8,128)S(1)}, u32[]{:S(2)}) copy-start(f32[2,40,512]{2,1,0:T(8,128)S(1)} %collective-permute-done.21.refs_5_.refs_2_) | copy-start | bytes 491524
  83.9 1.5 %collective-permute-start.22 = (f32[2,32,640]{2,1,0:T(8,128)S(1)}, f32[2,32,640]{2,1,0:T(8,128)S(1)}, u32[]{:S(2)}, u32[]{:S(2)}) collective-permute-start(f32[2,32,640]{2,1,0:T(8,128)S(1)} %get-tuple-element.26), channel_id=1, source_target_pairs={{0,1},{1,0},{2,3},{3,2},{4,5},{5,4},{6,7},{7,6},{8,9},{9,8},{10,11... | collective-permute-start | bytes 491528 | tf_op jit(solution)/shard_map/ppermute | solution.py:271
  85.4 4.6 %collective-permute-start.23 = (f32[32,640]{1,0:T(8,128)S(1)}, f32[32,640]{1,0:T(8,128)S(1)}, u32[]{:S(2)}, u32[]{:S(2)}) collective-permute-start(f32[32,640]{1,0:T(8,128)S(1)} %fusion), channel_id=1, source_target_pairs={{0,2},{1,3},{2,0},{3,1},{4,6},{5,7},{6,4},{7,5},{8,10},{9,11},{10,... | collective-permute-start | bytes 245768 | tf_op jit(solution)/shard_map/ppermute | solution.py:271
  90.0 12.0 %copy-start.8 = (f32[32,512]{1,0:T(8,128)}, f32[32,512]{1,0:T(8,128)S(1)}, u32[]{:S(2)}) copy-start(f32[32,512]{1,0:T(8,128)S(1)} %fusion.3.refs_3_) | copy-start | bytes 196612
  90.0 4.4 %collective-permute-start.28 = (f32[32,512]{1,0:T(8,128)S(1)}, f32[32,512]{1,0:T(8,128)S(1)}, u32[]{:S(2)}, u32[]{:S(2)}) collective-permute-start(f32[32,512]{1,0:T(8,128)S(1)} %fusion.3.refs_3_), channel_id=1, source_target_pairs={{0,2},{1,3},{2,0},{3,1},{4,6},{5,7},{6,4},{7,5},{8,10},{9,11},{10,... | collective-permute-start | bytes 196616 | tf_op jit(solution)/shard_map/ppermute | solution.py:271
  90.6 4.6 %collective-permute-start.25 = (f32[32,128]{1,0:T(8,128)S(1)}, f32[32,128]{1,0:T(8,128)S(1)}, u32[]{:S(2)}, u32[]{:S(2)}) collective-permute-start(f32[32,128]{1,0:T(8,128)S(1)} %slice.28), channel_id=1, source_target_pairs={{0,16},{4,20},{8,24},{12,28},{16,0},{20,4},{24,8},{28,12},{1,17},{... | collective-permute-start | bytes 49160 | tf_op jit(solution)/shard_map/ppermute | solution.py:271
  92.0 5.5 %collective-permute-start.26 = (f32[32,128]{1,0:T(8,128)S(1)}, f32[32,128]{1,0:T(8,128)S(1)}, u32[]{:S(2)}, u32[]{:S(2)}) collective-permute-start(f32[32,128]{1,0:T(8,128)S(1)} %slice.28), channel_id=1, source_target_pairs={{0,24},{4,28},{8,16},{12,20},{16,8},{20,12},{24,0},{28,4},{1,25},{... | collective-permute-start | bytes 49160 | tf_op jit(solution)/shard_map/ppermute | solution.py:271
  94.4 3.7 %collective-permute-start.24 = (f32[32,128]{1,0:T(8,128)S(1)}, f32[32,128]{1,0:T(8,128)S(1)}, u32[]{:S(2)}, u32[]{:S(2)}) collective-permute-start(f32[32,128]{1,0:T(8,128)S(1)} %slice.28), channel_id=1, source_target_pairs={{0,8},{4,12},{8,0},{12,4},{16,24},{20,28},{24,16},{28,20},{1,9},{5... | collective-permute-start | bytes 49160 | tf_op jit(solution)/shard_map/ppermute | solution.py:271
  94.4 7.6 %copy-start.9 = (f32[32,512]{1,0:T(8,128)}, f32[32,512]{1,0:T(8,128)S(1)}, u32[]{:S(2)}) copy-start(f32[32,512]{1,0:T(8,128)S(1)} %collective-permute-done.28.refs_4_) | copy-start | bytes 196612
  94.4 7.5 %collective-permute-start.29 = (f32[2,32,512]{2,1,0:T(8,128)S(1)}, f32[2,32,512]{2,1,0:T(8,128)S(1)}, u32[]{:S(2)}, u32[]{:S(2)}) collective-permute-start(f32[2,32,512]{2,1,0:T(8,128)S(1)} %pad_maximum_fusion.3), channel_id=1, source_target_pairs={{0,1},{1,0},{2,3},{3,2},{4,5},{5,4},{6,7},{7,6},{8,9},{9,8},{10,11... | collective-permute-start | bytes 393224 | tf_op jit(solution)/shard_map/ppermute | solution.py:271
  98.1 3.9 %copy-start.11 = (f32[32,128]{1,0:T(8,128)}, f32[32,128]{1,0:T(8,128)S(1)}, u32[]{:S(2)}) copy-start(f32[32,128]{1,0:T(8,128)S(1)} %add_add_fusion.dots_a) | copy-start | bytes 49156
  98.1 3.8 %collective-permute-start.27 = (f32[32,128]{1,0:T(8,128)S(1)}, f32[32,128]{1,0:T(8,128)S(1)}, u32[]{:S(2)}, u32[]{:S(2)}) collective-permute-start(f32[32,128]{1,0:T(8,128)S(1)} %add_add_fusion.dots_a), channel_id=1, source_target_pairs={{0,4},{4,0},{8,12},{12,8},{16,20},{20,16},{24,28},{28,24},{1,5},{5... | collective-permute-start | bytes 49160 | tf_op jit(solution)/shard_map/ppermute | solution.py:271
  101.9 0.6 copy-start.12
  102.5 0.7 copy-start.10

commit v2 on v1

--- a/solution.py
+++ b/solution.py
@@ -23,6 +23,12 @@
 HBM = pl.BlockSpec(memory_space=pltpu.HBM)
 F32 = jnp.float32
 BF16 = jnp.bfloat16
+
+
+def pair_sum(parts):
+    while len(parts) > 1:
+        parts = [a + b for a, b in zip(parts[::2], parts[1::2])]
+    return parts[0]
 
 
 def augment(x, first_ones):
@@ -61,15 +67,17 @@
     return own, pair.at[0], across, pair.at[1]
 
 
-def build_kernel(cfg, place, direct, near_ref, *refs):
+def build_kernel(cfg, place, direct, near_hbm, *refs):
     n_pieces, nb, block_len, own_rows, block_rows, n_sub, count_rows, resident = cfg
     pieces, refs = refs[:n_pieces], refs[n_pieces:]
     k_hbm, ilist, jlist, groups, deg_ref = refs[:5]
-    mlist, acc, lhs, rhs, counts_v, counts, count_sem = refs[5:12]
-    kbuf, sems = (None, None) if resident else refs[12:]
+    mlist, acc, lhs, rhs, near_ref, counts_v, counts, count_sem, near_sem = refs[5:14]
+    kbuf, sems = (None, None) if resident else refs[14:]
+    near_copy = pltpu.make_async_copy(near_hbm, near_ref, near_sem)
+    near_copy.start()
     row, col = place[0], place[1]
     own_len = own_rows * block_len
-    dim = near_ref.shape[0]
+    dim = near_hbm.shape[0]
     scale = 1.0 / (RADIUS * RADIUS)
 
     def prepare(r, load):
@@ -83,6 +91,7 @@
     each_piece(pieces, row, prepare)
     fetch = pltpu.make_async_copy(counts_v, counts, count_sem)
     fetch.start()
+    near_copy.wait()
     for i in range(block_rows):
         near = near_ref[:, i * block_len:(i + 1) * block_len].astype(F32)
         full = jnp.concatenate([near * (-2.0 * scale), augment(near, True)], axis=0)
@@ -90,23 +99,23 @@
     acc[...] = jnp.zeros_like(acc)
     fetch.wait()
 
-    def line(i, pos):
+    pos = jnp.int32(0)
+    for i in range(block_rows):
         me = row * block_rows + i
-
-        def note(j, at):
-            r, k = lax.div(j, own_rows), lax.rem(j, own_rows)
-            name = r * block_rows + col * own_rows + k
-            spot = k * nb + me
-            mirrored = counts[r, lax.div(spot, LANES), lax.rem(spot, LANES)]
-            m = direct[i, name] + jnp.where(name == me, 0, mirrored)
-            ilist[at] = i
-            jlist[at] = j
-            mlist[at] = m
-            return at + jnp.where(m > 0, 1, 0)
-
-        return lax.fori_loop(0, n_sub, note, pos, unroll=8)
-
-    pos = lax.fori_loop(0, block_rows, line, jnp.int32(0))
+        spots = [k * nb + me for k in range(own_rows)]
+        spots = [(lax.shift_right_logical(p, 7), p & (LANES - 1)) for p in spots]
+
+        def note(r, at, i=i, me=me, spots=spots):
+            for k in range(own_rows):
+                name = r * block_rows + col * own_rows + k
+                m = direct[i, name] + jnp.where(name == me, 0, counts[r, spots[k][0], spots[k][1]])
+                ilist[at] = i
+                jlist[at] = r * own_rows + k
+                mlist[at] = m
+                at = at + jnp.where(m > 0, 1, 0)
+            return at
+
+        pos = lax.fori_loop(0, n_sub // own_rows, note, pos, unroll=4)
     for u in range(GROUP):
         ilist[pos + u] = 0
         jlist[pos + u] = 0
@@ -167,6 +176,8 @@
     else:
         t_ref, s_refs, refs = refs[0], refs[1:4], refs[4:]
     near, near_y, cross = refs[:3]
+    if not first:
+        dot_ref, refs = refs[3], refs[:3] + refs[4:]
     w_all, z_acc = refs[3:5]
     kbuf, sems = (None, None) if resident else refs[5:]
     row, col = place[0], place[1]
@@ -228,7 +239,7 @@
         s1s2 = jnp.zeros((outputs, 1), F32)
         for e, packed in enumerate(by_col(s_refs)):
             at = pl.ds(pl.multiple_of((col ^ e) * own_len, LANES), own_len)
-            scaled = z_refs[e][:, :own_len] * packed[outputs:outputs + 1, :]
+            scaled = z_refs[e][...] * packed[outputs:outputs + 1, :]
             ts2 += jnp.sum(t_ref[:, at] * scaled, axis=1, keepdims=True)
             s1s2 += jnp.sum(packed[:outputs, :] * scaled, axis=1, keepdims=True)
         t = t_ref[:, pl.ds(pl.multiple_of(col * own_len, LANES), own_len)]
@@ -242,15 +253,14 @@
         out = jnp.zeros(lane.shape, F32)
         for n, v in enumerate((tt, ts1, s1s1, ts2, s1s2)):
             out = jnp.where(lane == n, v, out)
-        for ref in z_refs:
-            ref[:, own_len:] = out
-
-
-def final_kernel(n_cols, place, t_ref, dots_a, dots_b, *refs):
+        dot_ref[...] = out
+
+
+def final_kernel(n_cols, place, t_ref, *refs):
     s1s, s2s = by_col(refs[:3]), by_col(refs[3:6])
     sol_ref, res_ref = refs[6:]
-    outputs, own_len = s2s[0].shape
-    dots = dots_a[...] + dots_b[...]
+    outputs, own_len = s2s[0].shape[0], s2s[0].shape[1] - LANES
+    dots = pair_sum([ref[:, own_len:] for ref in s2s])
     tt, ts1, s1s1, ts2, s1s2 = (dots[:, n:n + 1] for n in range(5))
     a1 = tt / (REG * tt + ts1)
     p = 1.0 - REG * a1
@@ -261,7 +271,7 @@
     a2 = new / (REG * dd + dmd)
     for e in range(n_cols):
         at = pl.ds(pl.multiple_of((place[1] ^ e) * own_len, LANES), own_len)
-        t, s1, s2 = t_ref[:, at], s1s[e][:outputs, :], s2s[e][...]
+        t, s1, s2 = t_ref[:, at], s1s[e][:outputs, :], s2s[e][:, :own_len]
         sol_ref[:, at] = (a1 + a2 * u) * t - (a2 * a1) * s1
         res_ref[:, at] = (p - a2 * REG * u) * t - (a1 + a2 * (u - REG * a1)) * s1 + (a2 * a1) * s2
 
@@ -280,12 +290,6 @@
     got = swap(cross, "cols", 1)
     far = swap(near_y + got[1], "cols", 2)
     return (near + got[0]) + far
-
-
-def pair_sum(parts):
-    while len(parts) > 1:
-        parts = [a + b for a, b in zip(parts[::2], parts[1::2])]
-    return parts[0]
 
 
 def along_z(x):
@@ -316,7 +320,7 @@
     place = jnp.stack([row, col])
     k_shape = (n_groups, GROUP, block_len, block_len)
     resident = 2 * n_groups * GROUP * block_len * block_len <= RESIDENT_BYTES
-    limit = pltpu.CompilerParams(vmem_limit_bytes=24 * 1024 * 1024)
+    limit = pltpu.CompilerParams(vmem_limit_bytes=(8 if resident else 32) * 1024 * 1024)
     ring = [] if resident else [
         pltpu.VMEM((RING, GROUP, block_len, block_len), BF16),
         pltpu.SemaphoreType.DMA((RING,)),
@@ -339,10 +343,9 @@
             return pair_sum(across_x(pair_sum(along_z(x))))
         return lax.psum(x, "rows")
 
-    lists = jnp.concatenate([block_list, swap(block_list, "cols", 1)], axis=1)
-    lists = jnp.concatenate([lists, swap(lists, "cols", 2)], axis=1)
+    lists = [block_list] + [swap(block_list, "cols", e) for e in range(1, n_cols)]
     names = jnp.arange(nb, dtype=jnp.int32)
-    direct = jnp.sum((lists[:, :, None] == names).astype(jnp.int32), axis=1)
+    direct = sum(jnp.sum((x[:, :, None] == names).astype(jnp.int32), axis=1) for x in lists)
     own_counts = lax.dynamic_slice_in_dim(direct, col * own_rows, own_rows, 0)
     count_rows = -(-own_rows * nb // LANES)
     coded = own_counts.reshape(-1)
@@ -353,6 +356,8 @@
         packed, early_t = lax.optimization_barrier((packed, own_t))
         pieces = from_rows(packed)
         t_stack = jnp.stack(along_z(early_t))
+        *pieces, t_stack = lax.optimization_barrier((*pieces, t_stack))
+        t_pieces = across_x(t_stack)
     else:
         pieces = from_rows(packed)
 
@@ -368,40 +373,50 @@
             shape(1, dtype=jnp.int32),
             shape(n_sub, block_len),
         ),
-        in_specs=[SMEM, SMEM, VMEM] + [VMEM] * len(pieces),
+        in_specs=[SMEM, SMEM, HBM] + [VMEM] * len(pieces),
         out_specs=(k_spec, SMEM, SMEM, SMEM, VMEM),
         scratch_shapes=[
             pltpu.SMEM((list_len,), jnp.int32),
             pltpu.VMEM((n_sub, 8, block_len), F32),
             pltpu.VMEM((block_rows, block_len, 2 * dim), BF16),
             pltpu.VMEM((n_sub, 2 * dim, block_len), BF16),
+            pltpu.VMEM((dim, npoints), BF16),
             pltpu.VMEM((n_rows, count_rows, LANES), jnp.int32),
             pltpu.SMEM((n_rows, count_rows, LANES), jnp.int32),
+            pltpu.SemaphoreType.DMA,
             pltpu.SemaphoreType.DMA,
             *ring,
         ],
         compiler_params=limit,
+        cost_estimate=pl.CostEstimate(
+            flops=2 * 2 * dim * bound * block_len * block_len,
+            bytes_accessed=2 * bound * block_len * block_len,
+            transcendentals=bound * block_len * block_len,
+        ),
         name="build",
-    )(place, direct, points, *pieces)
+    )(place, direct, pltpu.with_memory_space_constraint(points, pltpu.HBM), *pieces)
 
     if resident:
         k_mat = pltpu.with_memory_space_constraint(k_mat, pltpu.VMEM)
 
-    t_pieces = across_x(t_stack) if direct_rows else from_rows(own_t)
+    if direct_rows:
+        degree, *t_pieces = lax.optimization_barrier((degree, *t_pieces))
+    else:
+        t_pieces = from_rows(own_t)
     inv = 1.0 / jnp.sqrt(1.0 + total_rows(degree))
     own_inv = lax.dynamic_slice_in_dim(inv, row * own_rows, own_rows, 0).reshape(1, own_len)
 
-    def apply(pieces, extra, width):
+    def apply(pieces, extra):
         first = len(extra) == 1
-        return shared(*pl.pallas_call(
+        out = [shape(outputs, own_len), shape(outputs, own_len), shape(2, outputs, own_len)]
+        out += [] if first else [shape(outputs, LANES)]
+        return pl.pallas_call(
             functools.partial(
                 apply_kernel, (len(pieces), n_cols, own_rows, block_len, first, resident)
             ),
-            out_shape=[
-                shape(outputs, width), shape(outputs, width), shape(2, outputs, width)
-            ],
+            out_shape=out,
             in_specs=[SMEM] * 4 + [k_spec] + [VMEM] * (len(pieces) + len(extra)),
-            out_specs=[VMEM] * 3,
+            out_specs=[VMEM] * len(out),
             scratch_shapes=[
                 pltpu.VMEM((n_sub, outputs, block_len), BF16),
                 pltpu.VMEM((block_rows, outputs, block_len), F32),
@@ -409,26 +424,29 @@
             ],
             compiler_params=limit,
             name="apply",
-        )(place, ilist, jlist, groups, k_mat, *pieces, *extra))
-
-    s1 = apply(t_pieces, [inv], own_len) * own_inv
+        )(place, ilist, jlist, groups, k_mat, *pieces, *extra)
+
+    s1 = shared(*apply(t_pieces, [inv])) * own_inv
     g = ((s1 - SHIFT * own_t) * own_inv).astype(BF16)
     s1_all = spread(jnp.concatenate([s1, jnp.broadcast_to(own_inv, (8, own_len))], axis=0))
-    z2 = apply(from_rows(g), [targets, *s1_all], own_len + LANES)
-    s2 = z2[:, :own_len] * own_inv + SHIFT * s1
-    dots = z2[:, own_len:]
+    *z2, dots = apply(from_rows(g), [targets, *s1_all])
     if direct_rows:
-        dots = across_x(pair_sum(along_z(dots)))
+        dots = pair_sum(along_z(pair_sum(across_x(dots))))
     else:
-        dots = [lax.psum(dots, "rows"), jnp.zeros_like(dots)]
+        dots = lax.psum(dots, "rows")
+    s2 = shared(*z2) * own_inv + SHIFT * s1
+    ends = spread(jnp.concatenate([s2, dots], axis=1))
+    s1_all, ends = [
+        [pltpu.with_memory_space_constraint(x, pltpu.VMEM) for x in xs] for xs in (s1_all, ends)
+    ]
 
     return pl.pallas_call(
         functools.partial(final_kernel, n_cols),
         out_shape=(shape(outputs, npoints), shape(outputs, npoints)),
-        in_specs=[SMEM] + [VMEM] * 9,
+        in_specs=[SMEM] + [VMEM] * 7,
         out_specs=(VMEM, VMEM),
         name="final",
-    )(place, targets, *dots, *s1_all, *spread(s2))
+    )(place, targets, *s1_all, *ends)
 
 
 def solution(mesh):

time: 106 us -> 103 us (0.972)
  waiting for transfers between devices: 32.1 us -> 34.9 us
  Pallas kernels: 21.3 us -> 19.3 us
  other arithmetic: 1.91 us -> 0.62 us
  starting transfers between devices: 34.1 us -> 32.9 us
  local copies, waits for them, and re-layouts: 15.3 us -> 14.2 us
    ppermute x30 -> x31, waiting for transfers between devices: 32.1 us -> 34.9 us  [swap(): return lax.ppermute(x, axis, [(i, i ^ d) for i in range(size)])]
    concatenate x2 -> x0, other arithmetic: 1.52 us -> none  [the longest x1 0.76 us: local(): lists = jnp.concatenate([lists, swap(lists, 'cols', 2)], axis=1)]
    unnamed x28 -> x11, local copies, waits for them, and re-layouts: 13.6 us -> 12.3 us
    pallas_call x1, Pallas kernels: 10.3 us -> 9.12 us  [local(): pl.pallas_call(functools.partial(build_kernel, (len(pieces), nb, block_le...]
    ppermute x30 -> x31, starting transfers between devices: 34.1 us -> 32.9 us  [swap(): return lax.ppermute(x, axis, [(i, i ^ d) for i in range(size)])]
  transfers between devices with their start and end apart: 30 -> 31, of which waited for: 18 -> 18; matrix products, arithmetic and copies ran while one was open for 2% -> 3% of each run, Pallas kernels for 10% -> 9%
where the time goes in v2:
time: 103 us
  waiting for transfers between devices  34.9 us (34%)
  starting transfers between devices  32.9 us (32%)
  Pallas kernels  19.3 us (19%)
  local copies, waits for them, and re-layouts  14.2 us (14%)
    ppermute x31, waiting for transfers between devices, swap(): return lax.ppermute(x, axis, [(i, i ^ d) for i in range(size)])  34.9 us
    ppermute x31, starting transfers between devices, swap(): return lax.ppermute(x, axis, [(i, i ^ d) for i in range(size)])  32.9 us
    unnamed x11, local copies, waits for them, and re-layouts  12.3 us
    pallas_call x1, Pallas kernels, local(): pl.pallas_call(functools.partial(build_kernel, (len(pieces), nb, block_le...  9.12 us
    pallas_call x2, Pallas kernels, apply(): pl.pallas_call(functools.partial(apply_kernel, (len(pieces), n_cols, own_...  8.13 us
    pallas_call x1, Pallas kernels, local(): pl.pallas_call(functools.partial(final_kernel, n_cols), out_shape=(shape(...  2.08 us
  transfers between devices with their start and end apart: 31, of which 18 were waited for; matrix products, arithmetic and copies ran while one was open for 3% of the time, Pallas kernels for 9%

profile of v2, /device:TPU:0, one launch (start us, length us, event | category | flops | bytes accessed | tf_op | source)
XLA Modules:
  0.0 102.8 jit_solution(10097520524548510427)
XLA Ops:
  0.6 0.5 collective-permute-start
  1.1 2.6 %collective-permute-start.2 = (s32[8,6]{1,0:T(8,128)}, s32[8,6]{1,0:T(8,128)S(1)}, u32[]{:S(2)}, u32[]{:S(2)}) collective-permute-start(s32[8,6]{1,0:T(8,128)} %param.3), channel_id=1, source_target_pairs={{0,3},{1,2},{2,1},{3,0},{4,7},{5,6},{6,5},{7,4},{8,11},{9,10},{10,... | collective-permute-start | bytes 584 | tf_op jit(solution)/shard_map/ppermute | solution.py:281
  3.8 0.8 copy.5
  4.7 0.7 constant_dynamic-slice_fusion.1
  5.5 0.8 constant_dynamic-slice_fusion
  6.6 1.0 collective-permute-done.1
  7.8 0.1 reshape.16
  7.9 3.7 %collective-permute-start.5 = (bf16[16,640]{1,0:T(8,128)(2,1)S(1)}, bf16[16,640]{1,0:T(8,128)(2,1)S(1)}, u32[]{:S(2)}, u32[]{:S(2)}) collective-permute-start(bf16[16,640]{1,0:T(8,128)(2,1)S(1)} %pad_maximum_fusion.7), channel_id=1, source_target_pairs={{0,24},{4,28},{8,16},{12,20},{16,8},{20,12},{24,0},{28,4},{1,25},{... | collective-permute-start | bytes 61448 | tf_op jit(solution)/shard_map/ppermute | solution.py:281
  11.6 0.8 collective-permute-start.3
  12.3 3.6 %collective-permute-start.9 = (f32[32,512]{1,0:T(8,128)S(1)}, f32[32,512]{1,0:T(8,128)S(1)}, u32[]{:S(2)}, u32[]{:S(2)}) collective-permute-start(f32[32,512]{1,0:T(8,128)S(1)} %constant_dynamic-slice_fusion), channel_id=1, source_target_pairs={{0,24},{4,28},{8,16},{12,20},{16,8},{20,12},{24,0},{28,4},{1,25},{... | collective-permute-start | bytes 196616 | tf_op jit(solution)/shard_map/ppermute | solution.py:281
  15.9 0.8 collective-permute-start.7
  16.8 1.6 %collective-permute-start.6 = (bf16[4,16,640]{2,1,0:T(8,128)(2,1)S(1)}, bf16[4,16,640]{2,1,0:T(8,128)(2,1)S(1)}, u32[]{:S(2)}, u32[]{:S(2)}) collective-permute-start(bf16[4,16,640]{2,1,0:T(8,128)(2,1)S(1)} %pad_maximum_fusion.4.refs_0_), channel_id=1, source_target_pairs={{0,4},{4,0},{8,12},{12,8},{16,20},{20,16},{24,28},{28,24},{1,5},{5... | collective-permute-start | bytes 245768 | tf_op jit(solution)/shard_map/ppermute | solution.py:281
  18.3 0.2 collective-permute-done.9
  18.5 2.6 %collective-permute-done.8 = f32[32,512]{1,0:T(8,128)S(1)} collective-permute-done((f32[32,512]{1,0:T(8,128)S(1)}, f32[32,512]{1,0:T(8,128)S(1)}, u32[]{:S(2)}, u32[]{:S(2)}) %collective-permute-start.8) | collective-permute-done | bytes 65568 | tf_op jit(solution)/shard_map/ppermute | solution.py:281
  21.1 0.1 collective-permute-done.6.refs_1_
  21.3 1.5 %collective-permute-start.10 = (f32[4,32,512]{2,1,0:T(8,128)S(1)}, f32[4,32,512]{2,1,0:T(8,128)S(1)}, u32[]{:S(2)}, u32[]{:S(2)}) collective-permute-start(f32[4,32,512]{2,1,0:T(8,128)S(1)} %pad_maximum_fusion.refs_0_), channel_id=1, source_target_pairs={{0,4},{4,0},{8,12},{12,8},{16,20},{20,16},{24,28},{28,24},{1,5},{5... | collective-permute-start | bytes 786440 | tf_op jit(solution)/shard_map/ppermute | solution.py:281
  22.8 9.1 %build.1 = (bf16[32,4,256,256]{3,2,1,0:T(8,128)(2,1)S(1)}, s32[132]{0:T(256)S(1)}, s32[132]{0:T(256)S(1)}, s32[1]{0:T(128)}, f32[16,256]{1,0:T(8,128)S(1)}) custom-call(s32[2]{0:T(128)S(1)} %pad_add_fusion.place, s32[8,64]{1,0:T(8,128)S(1)} %add_add_fusion.2.direct, bf16[16,2048]{1,0:T(8,128)(2,1)} %near_hbm.1, ...), custom_call_target="tpu_custom_call" | custom-call | flops 536870912 | bytes 16777216 | tf_op jit(solution)/shard_map/build/pallas_call | solution.py:364
  32.0 4.4 %collective-permute-start.13 = (f32[16,256]{1,0:T(8,128)S(1)}, f32[16,256]{1,0:T(8,128)S(1)}, u32[]{:S(2)}, u32[]{:S(2)}) collective-permute-start(f32[16,256]{1,0:T(8,128)S(1)} %get-tuple-element.34), channel_id=1, source_target_pairs={{0,24},{4,28},{8,16},{12,20},{16,8},{20,12},{24,0},{28,4},{1,25},{... | collective-permute-start | bytes 49160 | tf_op jit(solution)/shard_map/ppermute | solution.py:281
  36.3 0.6 collective-permute-start.11
  37.0 1.1 %collective-permute-done.13 = f32[16,256]{1,0:T(8,128)S(1)} collective-permute-done((f32[16,256]{1,0:T(8,128)S(1)}, f32[16,256]{1,0:T(8,128)S(1)}, u32[]{:S(2)}, u32[]{:S(2)}) %collective-permute-start.13) | collective-permute-done | bytes 16416 | tf_op jit(solution)/shard_map/ppermute | solution.py:281
  38.0 2.9 %collective-permute-done.12 = f32[16,256]{1,0:T(8,128)S(1)} collective-permute-done((f32[16,256]{1,0:T(8,128)S(1)}, f32[16,256]{1,0:T(8,128)S(1)}, u32[]{:S(2)}, u32[]{:S(2)}) %collective-permute-start.12) | collective-permute-done | bytes 16416 | tf_op jit(solution)/shard_map/ppermute | solution.py:281
  41.1 3.7 %collective-permute-done.14 = f32[16,256]{1,0:T(8,128)S(1)} collective-permute-done((f32[16,256]{1,0:T(8,128)S(1)}, f32[16,256]{1,0:T(8,128)S(1)}, u32[]{:S(2)}, u32[]{:S(2)}) %collective-permute-start.14) | collective-permute-done | bytes 16416 | tf_op jit(solution)/shard_map/ppermute | solution.py:281
  44.8 4.0 %apply.2 = (f32[32,512]{1,0:T(8,128)S(1)}, f32[32,512]{1,0:T(8,128)S(1)}, f32[2,32,512]{2,1,0:T(8,128)S(1)}) custom-call(s32[2]{0:T(128)S(1)} %pad_add_fusion.place, s32[132]{0:T(256)S(1)} %get-tuple-element.26.ilist, s32[132]{0:T(256)S(1)} %get-tuple-element.27.jlist, s32[1]{0:T(128)} %get-tuple-element.28.groups, ...), custom_call_target="tpu_custom_call" | custom-call | tf_op jit(solution)/shard_map/apply/pallas_call | solution.py:413
  48.8 5.7 %copy-done = bf16[32,4,256,256]{3,2,1,0:T(8,128)(2,1)} copy-done((bf16[32,4,256,256]{3,2,1,0:T(8,128)(2,1)}, bf16[32,4,256,256]{3,2,1,0:T(8,128)(2,1)S(1)}, u32[]{:S(2)}) %copy-start) | copy-done | bytes 16777240
  54.5 1.3 %collective-permute-done.15 = f32[2,32,512]{2,1,0:T(8,128)S(1)} collective-permute-done((f32[2,32,512]{2,1,0:T(8,128)S(1)}, f32[2,32,512]{2,1,0:T(8,128)S(1)}, u32[]{:S(2)}, u32[]{:S(2)}) %collective-permute-start.15) | collective-permute-done | bytes 131104 | tf_op jit(solution)/shard_map/ppermute | solution.py:281
  56.0 4.2 %collective-permute-done.16 = f32[32,512]{1,0:T(8,128)S(1)} collective-permute-done((f32[32,512]{1,0:T(8,128)S(1)}, f32[32,512]{1,0:T(8,128)S(1)}, u32[]{:S(2)}, u32[]{:S(2)}) %collective-permute-start.16) | collective-permute-done | bytes 65568 | tf_op jit(solution)/shard_map/ppermute | solution.py:281
  60.3 0.2 collective-permute-start.17
  60.5 1.5 %collective-permute-start.21 = (bf16[32,512]{1,0:T(8,128)(2,1)S(1)}, bf16[32,512]{1,0:T(8,128)(2,1)S(1)}, u32[]{:S(2)}, u32[]{:S(2)}) collective-permute-start(bf16[32,512]{1,0:T(8,128)(2,1)S(1)} %get-tuple-element.42), channel_id=1, source_target_pairs={{0,24},{4,28},{8,16},{12,20},{16,8},{20,12},{24,0},{28,4},{1,25},{... | collective-permute-start | bytes 98312 | tf_op jit(solution)/shard_map/ppermute | solution.py:281
  62.0 0.3 collective-permute-start.20
  62.3 2.6 %collective-permute-start.19 = (bf16[32,512]{1,0:T(8,128)(2,1)S(1)}, bf16[32,512]{1,0:T(8,128)(2,1)S(1)}, u32[]{:S(2)}, u32[]{:S(2)}) collective-permute-start(bf16[32,512]{1,0:T(8,128)(2,1)S(1)} %get-tuple-element.42), channel_id=1, source_target_pairs={{0,8},{4,12},{8,0},{12,4},{16,24},{20,28},{24,16},{28,20},{1,9},{5... | collective-permute-start | bytes 98312 | tf_op jit(solution)/shard_map/ppermute | solution.py:281
  65.0 1.4 %collective-permute-done.21 = bf16[32,512]{1,0:T(8,128)(2,1)S(1)} collective-permute-done((bf16[32,512]{1,0:T(8,128)(2,1)S(1)}, bf16[32,512]{1,0:T(8,128)(2,1)S(1)}, u32[]{:S(2)}, u32[]{:S(2)}) %collective-permute-start.21) | collective-permute-done | bytes 32800 | tf_op jit(solution)/shard_map/ppermute | solution.py:281
  66.4 0.4 collective-permute-done.20
  66.8 0.3 collective-permute-done.19
  67.2 0.1 collective-permute-start.22
  67.3 4.9 %collective-permute-done.22.refs_1_ = bf16[4,32,512]{2,1,0:T(8,128)(2,1)S(1)} collective-permute-done((bf16[4,32,512]{2,1,0:T(8,128)(2,1)S(1)}, bf16[4,32,512]{2,1,0:T(8,128)(2,1)S(1)}, u32[]{:S(2)}, u32[]{:S(2)}) %collective-permute-start.22) | collective-permute-done | bytes 131104 | tf_op jit(solution)/shard_map/ppermute | solution.py:281
  72.2 5.8 %copy-done.1 = bf16[32,4,256,256]{3,2,1,0:T(8,128)(2,1)S(1)} copy-done((bf16[32,4,256,256]{3,2,1,0:T(8,128)(2,1)S(1)}, bf16[32,4,256,256]{3,2,1,0:T(8,128)(2,1)}, u32[]{:S(2)}) %copy-start.1) | copy-done | bytes 16777240
  78.0 4.1 %apply.3 = (f32[32,512]{1,0:T(8,128)S(1)}, f32[32,512]{1,0:T(8,128)S(1)}, f32[2,32,512]{2,1,0:T(8,128)S(1)}, f32[32,128]{1,0:T(8,128)S(1)}) custom-call(s32[2]{0:T(128)S(1)} %pad_add_fusion.place, s32[132]{0:T(256)S(1)} %get-tuple-element.26.ilist, s32[132]{0:T(256)S(1)} %get-tuple-element.27.jlist, s32[1]{0:T(128)} %get-tuple-element.28.groups, ...), custom_call_target="tpu_custom_call" | custom-call | tf_op jit(solution)/shard_map/apply/pallas_call | solution.py:413
  82.3 3.7 %collective-permute-done.25 = f32[32,128]{1,0:T(8,128)S(1)} collective-permute-done((f32[32,128]{1,0:T(8,128)S(1)}, f32[32,128]{1,0:T(8,128)S(1)}, u32[]{:S(2)}, u32[]{:S(2)}) %collective-permute-start.25) | collective-permute-done | bytes 16416 | tf_op jit(solution)/shard_map/ppermute | solution.py:281
  86.0 2.3 %collective-permute-start.28 = (f32[32,128]{1,0:T(8,128)S(1)}, f32[32,128]{1,0:T(8,128)S(1)}, u32[]{:S(2)}, u32[]{:S(2)}) collective-permute-start(f32[32,128]{1,0:T(8,128)S(1)} %add.87), channel_id=1, source_target_pairs={{0,24},{4,28},{8,16},{12,20},{16,8},{20,12},{24,0},{28,4},{1,25},{... | collective-permute-start | bytes 49160 | tf_op jit(solution)/shard_map/ppermute | solution.py:281
  88.3 0.3 collective-permute-start.27
  88.6 1.8 %collective-permute-start.26 = (f32[32,128]{1,0:T(8,128)S(1)}, f32[32,128]{1,0:T(8,128)S(1)}, u32[]{:S(2)}, u32[]{:S(2)}) collective-permute-start(f32[32,128]{1,0:T(8,128)S(1)} %add.87), channel_id=1, source_target_pairs={{0,8},{4,12},{8,0},{12,4},{16,24},{20,28},{24,16},{28,20},{1,9},{5... | collective-permute-start | bytes 49160 | tf_op jit(solution)/shard_map/ppermute | solution.py:281
  90.4 1.7 %collective-permute-start.24 = (f32[32,512]{1,0:T(8,128)S(1)}, f32[32,512]{1,0:T(8,128)S(1)}, u32[]{:S(2)}, u32[]{:S(2)}) collective-permute-start(f32[32,512]{1,0:T(8,128)S(1)} %fusion), channel_id=1, source_target_pairs={{0,2},{1,3},{2,0},{3,1},{4,6},{5,7},{6,4},{7,5},{8,10},{9,11},{10,... | collective-permute-start | bytes 196616 | tf_op jit(solution)/shard_map/ppermute | solution.py:281
  92.1 0.9 collective-permute-done.27
  93.0 1.8 %collective-permute-done.24 = f32[32,512]{1,0:T(8,128)S(1)} collective-permute-done((f32[32,512]{1,0:T(8,128)S(1)}, f32[32,512]{1,0:T(8,128)S(1)}, u32[]{:S(2)}, u32[]{:S(2)}) %collective-permute-start.24) | collective-permute-done | bytes 65568 | tf_op jit(solution)/shard_map/ppermute | solution.py:281
  94.8 1.7 %collective-permute-start.29 = (f32[32,640]{1,0:T(8,128)S(1)}, f32[32,640]{1,0:T(8,128)S(1)}, u32[]{:S(2)}, u32[]{:S(2)}) collective-permute-start(f32[32,640]{1,0:T(8,128)S(1)} %get-tuple-element.45.refs_3_), channel_id=1, source_target_pairs={{0,2},{1,3},{2,0},{3,1},{4,6},{5,7},{6,4},{7,5},{8,10},{9,11},{10,... | collective-permute-start | bytes 245768 | tf_op jit(solution)/shard_map/ppermute | solution.py:281
  96.4 2.9 %collective-permute-done.29.refs_4_ = f32[32,640]{1,0:T(8,128)S(1)} collective-permute-done((f32[32,640]{1,0:T(8,128)S(1)}, f32[32,640]{1,0:T(8,128)S(1)}, u32[]{:S(2)}, u32[]{:S(2)}) %collective-permute-start.29) | collective-permute-done | bytes 81952 | tf_op jit(solution)/shard_map/ppermute | solution.py:281
  99.4 1.4 %collective-permute-done.30.refs_5_ = f32[2,32,640]{2,1,0:T(8,128)S(1)} collective-permute-done((f32[2,32,640]{2,1,0:T(8,128)S(1)}, f32[2,32,640]{2,1,0:T(8,128)S(1)}, u32[]{:S(2)}, u32[]{:S(2)}) %collective-permute-start.30) | collective-permute-done | bytes 163872 | tf_op jit(solution)/shard_map/ppermute | solution.py:281
  100.8 2.1 %final.1 = (f32[32,2048]{1,0:T(8,128)}, f32[32,2048]{1,0:T(8,128)}) custom-call(s32[2]{0:T(128)} %copy-done.3, f32[32,2048]{1,0:T(8,128)} %t_ref.1, f32[40,512]{1,0:T(8,128)S(1)} %get-tuple-element.47.refs_3_.refs_0_, f32[40,512]{1,0:T(8,128)S(1)} %collective-permute-done.17.refs_4_.refs_1_, f32[2,40,512]{2,1,0:T(8,128)S(1)} %collective-permute-done.18.refs_5_.refs_2_, ...), custom_call_target="tpu_custom_call" | custom-call | tf_op jit(solution)/shard_map/final/pallas_call | solution.py:443
  (60 shorter events, 1.4 us)
Async XLA Ops:
  0.6 5.7 %collective-permute-start = (s32[8,6]{1,0:T(8,128)}, s32[8,6]{1,0:T(8,128)S(1)}, u32[]{:S(2)}, u32[]{:S(2)}) collective-permute-start(s32[8,6]{1,0:T(8,128)} %param.3), channel_id=1, source_target_pairs={{0,1},{1,0},{2,3},{3,2},{4,5},{5,4},{6,7},{7,6},{8,9},{9,8},{10,11... | collective-permute-start | bytes 584 | tf_op jit(solution)/shard_map/ppermute | solution.py:281
  1.1 5.3 %collective-permute-start.2 = (s32[8,6]{1,0:T(8,128)}, s32[8,6]{1,0:T(8,128)S(1)}, u32[]{:S(2)}, u32[]{:S(2)}) collective-permute-start(s32[8,6]{1,0:T(8,128)} %param.3), channel_id=1, source_target_pairs={{0,3},{1,2},{2,1},{3,0},{4,7},{5,6},{6,5},{7,4},{8,11},{9,10},{10,... | collective-permute-start | bytes 584 | tf_op jit(solution)/shard_map/ppermute | solution.py:281
  3.8 3.8 %collective-permute-start.1 = (s32[8,6]{1,0:T(8,128)}, s32[8,6]{1,0:T(8,128)S(1)}, u32[]{:S(2)}, u32[]{:S(2)}) collective-permute-start(s32[8,6]{1,0:T(8,128)} %param.3), channel_id=1, source_target_pairs={{0,2},{1,3},{2,0},{3,1},{4,6},{5,7},{6,4},{7,5},{8,10},{9,11},{10,... | collective-permute-start | bytes 584 | tf_op jit(solution)/shard_map/ppermute | solution.py:281
  7.9 8.1 %collective-permute-start.5 = (bf16[16,640]{1,0:T(8,128)(2,1)S(1)}, bf16[16,640]{1,0:T(8,128)(2,1)S(1)}, u32[]{:S(2)}, u32[]{:S(2)}) collective-permute-start(bf16[16,640]{1,0:T(8,128)(2,1)S(1)} %pad_maximum_fusion.7), channel_id=1, source_target_pairs={{0,24},{4,28},{8,16},{12,20},{16,8},{20,12},{24,0},{28,4},{1,25},{... | collective-permute-start | bytes 61448 | tf_op jit(solution)/shard_map/ppermute | solution.py:281
  11.6 5.2 %collective-permute-start.4 = (bf16[16,640]{1,0:T(8,128)(2,1)S(1)}, bf16[16,640]{1,0:T(8,128)(2,1)S(1)}, u32[]{:S(2)}, u32[]{:S(2)}) collective-permute-start(bf16[16,640]{1,0:T(8,128)(2,1)S(1)} %pad_maximum_fusion.7), channel_id=1, source_target_pairs={{0,16},{4,20},{8,24},{12,28},{16,0},{20,4},{24,8},{28,12},{1,17},{... | collective-permute-start | bytes 61448 | tf_op jit(solution)/shard_map/ppermute | solution.py:281
  11.6 5.2 %collective-permute-start.3 = (bf16[16,640]{1,0:T(8,128)(2,1)S(1)}, bf16[16,640]{1,0:T(8,128)(2,1)S(1)}, u32[]{:S(2)}, u32[]{:S(2)}) collective-permute-start(bf16[16,640]{1,0:T(8,128)(2,1)S(1)} %pad_maximum_fusion.7), channel_id=1, source_target_pairs={{0,8},{4,12},{8,0},{12,4},{16,24},{20,28},{24,16},{28,20},{1,9},{5... | collective-permute-start | bytes 61448 | tf_op jit(solution)/shard_map/ppermute | solution.py:281
  12.3 6.2 %collective-permute-start.9 = (f32[32,512]{1,0:T(8,128)S(1)}, f32[32,512]{1,0:T(8,128)S(1)}, u32[]{:S(2)}, u32[]{:S(2)}) collective-permute-start(f32[32,512]{1,0:T(8,128)S(1)} %constant_dynamic-slice_fusion), channel_id=1, source_target_pairs={{0,24},{4,28},{8,16},{12,20},{16,8},{20,12},{24,0},{28,4},{1,25},{... | collective-permute-start | bytes 196616 | tf_op jit(solution)/shard_map/ppermute | solution.py:281
  15.9 5.2 %collective-permute-start.8 = (f32[32,512]{1,0:T(8,128)S(1)}, f32[32,512]{1,0:T(8,128)S(1)}, u32[]{:S(2)}, u32[]{:S(2)}) collective-permute-start(f32[32,512]{1,0:T(8,128)S(1)} %constant_dynamic-slice_fusion), channel_id=1, source_target_pairs={{0,16},{4,20},{8,24},{12,28},{16,0},{20,4},{24,8},{28,12},{1,17},{... | collective-permute-start | bytes 196616 | tf_op jit(solution)/shard_map/ppermute | solution.py:281
  15.9 5.2 %collective-permute-start.7 = (f32[32,512]{1,0:T(8,128)S(1)}, f32[32,512]{1,0:T(8,128)S(1)}, u32[]{:S(2)}, u32[]{:S(2)}) collective-permute-start(f32[32,512]{1,0:T(8,128)S(1)} %constant_dynamic-slice_fusion), channel_id=1, source_target_pairs={{0,8},{4,12},{8,0},{12,4},{16,24},{20,28},{24,16},{28,20},{1,9},{5... | collective-permute-start | bytes 196616 | tf_op jit(solution)/shard_map/ppermute | solution.py:281
  16.8 4.5 %collective-permute-start.6 = (bf16[4,16,640]{2,1,0:T(8,128)(2,1)S(1)}, bf16[4,16,640]{2,1,0:T(8,128)(2,1)S(1)}, u32[]{:S(2)}, u32[]{:S(2)}) collective-permute-start(bf16[4,16,640]{2,1,0:T(8,128)(2,1)S(1)} %pad_maximum_fusion.4.refs_0_), channel_id=1, source_target_pairs={{0,4},{4,0},{8,12},{12,8},{16,20},{20,16},{24,28},{28,24},{1,5},{5... | collective-permute-start | bytes 245768 | tf_op jit(solution)/shard_map/ppermute | solution.py:281
  21.3 10.7 %collective-permute-start.10 = (f32[4,32,512]{2,1,0:T(8,128)S(1)}, f32[4,32,512]{2,1,0:T(8,128)S(1)}, u32[]{:S(2)}, u32[]{:S(2)}) collective-permute-start(f32[4,32,512]{2,1,0:T(8,128)S(1)} %pad_maximum_fusion.refs_0_), channel_id=1, source_target_pairs={{0,4},{4,0},{8,12},{12,8},{16,20},{20,16},{24,28},{28,24},{1,5},{5... | collective-permute-start | bytes 786440 | tf_op jit(solution)/shard_map/ppermute | solution.py:281
  22.8 49.4 %copy-start.3 = (s32[2]{0:T(128)}, s32[2]{0:T(128)S(1)}, u32[]{:S(2)}) copy-start(s32[2]{0:T(128)S(1)} %pad_add_fusion.place) | copy-start | bytes 28
  22.8 37.4 %copy-start.2 = (f32[32,2048]{1,0:T(8,128)S(1)}, f32[32,2048]{1,0:T(8,128)}, u32[]{:S(2)}) copy-start(f32[32,2048]{1,0:T(8,128)} %t_ref.1) | copy-start | bytes 786436
  32.0 6.1 %collective-permute-start.13 = (f32[16,256]{1,0:T(8,128)S(1)}, f32[16,256]{1,0:T(8,128)S(1)}, u32[]{:S(2)}, u32[]{:S(2)}) collective-permute-start(f32[16,256]{1,0:T(8,128)S(1)} %get-tuple-element.34), channel_id=1, source_target_pairs={{0,24},{4,28},{8,16},{12,20},{16,8},{20,12},{24,0},{28,4},{1,25},{... | collective-permute-start | bytes 49160 | tf_op jit(solution)/shard_map/ppermute | solution.py:281
  36.3 4.6 %collective-permute-start.12 = (f32[16,256]{1,0:T(8,128)S(1)}, f32[16,256]{1,0:T(8,128)S(1)}, u32[]{:S(2)}, u32[]{:S(2)}) collective-permute-start(f32[16,256]{1,0:T(8,128)S(1)} %get-tuple-element.34), channel_id=1, source_target_pairs={{0,16},{4,20},{8,24},{12,28},{16,0},{20,4},{24,8},{28,12},{1,17},{... | collective-permute-start | bytes 49160 | tf_op jit(solution)/shard_map/ppermute | solution.py:281
  36.3 4.6 %collective-permute-start.11 = (f32[16,256]{1,0:T(8,128)S(1)}, f32[16,256]{1,0:T(8,128)S(1)}, u32[]{:S(2)}, u32[]{:S(2)}) collective-permute-start(f32[16,256]{1,0:T(8,128)S(1)} %get-tuple-element.34), channel_id=1, source_target_pairs={{0,8},{4,12},{8,0},{12,4},{16,24},{20,28},{24,16},{28,20},{1,9},{5... | collective-permute-start | bytes 49160 | tf_op jit(solution)/shard_map/ppermute | solution.py:281
  41.0 3.8 %collective-permute-start.14 = (f32[16,256]{1,0:T(8,128)S(1)}, f32[16,256]{1,0:T(8,128)S(1)}, u32[]{:S(2)}, u32[]{:S(2)}) collective-permute-start(f32[16,256]{1,0:T(8,128)S(1)} %add_add_fusion.1), channel_id=1, source_target_pairs={{0,4},{4,0},{8,12},{12,8},{16,20},{20,16},{24,28},{28,24},{1,5},{5... | collective-permute-start | bytes 49160 | tf_op jit(solution)/shard_map/ppermute | solution.py:281
  48.8 5.7 %copy-start = (bf16[32,4,256,256]{3,2,1,0:T(8,128)(2,1)}, bf16[32,4,256,256]{3,2,1,0:T(8,128)(2,1)S(1)}, u32[]{:S(2)}) copy-start(bf16[32,4,256,256]{3,2,1,0:T(8,128)(2,1)S(1)} %get-tuple-element.29.k_mat) | copy-start | bytes 50331652
  54.5 1.3 %collective-permute-start.15 = (f32[2,32,512]{2,1,0:T(8,128)S(1)}, f32[2,32,512]{2,1,0:T(8,128)S(1)}, u32[]{:S(2)}, u32[]{:S(2)}) collective-permute-start(f32[2,32,512]{2,1,0:T(8,128)S(1)} %get-tuple-element.36), channel_id=1, source_target_pairs={{0,1},{1,0},{2,3},{3,2},{4,5},{5,4},{6,7},{7,6},{8,9},{9,8},{10,11... | collective-permute-start | bytes 393224 | tf_op jit(solution)/shard_map/ppermute | solution.py:281
  55.9 4.3 %collective-permute-start.16 = (f32[32,512]{1,0:T(8,128)S(1)}, f32[32,512]{1,0:T(8,128)S(1)}, u32[]{:S(2)}, u32[]{:S(2)}) collective-permute-start(f32[32,512]{1,0:T(8,128)S(1)} %fusion.5), channel_id=1, source_target_pairs={{0,2},{1,3},{2,0},{3,1},{4,6},{5,7},{6,4},{7,5},{8,10},{9,11},{10,... | collective-permute-start | bytes 196616 | tf_op jit(solution)/shard_map/ppermute | solution.py:281
  60.3 4.6 %collective-permute-start.17 = (f32[40,512]{1,0:T(8,128)S(1)}, f32[40,512]{1,0:T(8,128)S(1)}, u32[]{:S(2)}, u32[]{:S(2)}) collective-permute-start(f32[40,512]{1,0:T(8,128)S(1)} %get-tuple-element.47.refs_3_.refs_0_), channel_id=1, source_target_pairs={{0,2},{1,3},{2,0},{3,1},{4,6},{5,7},{6,4},{7,5},{8,10},{9,11},{10,... | collective-permute-start | bytes 245768 | tf_op jit(solution)/shard_map/ppermute | solution.py:281
  60.5 5.9 %collective-permute-start.21 = (bf16[32,512]{1,0:T(8,128)(2,1)S(1)}, bf16[32,512]{1,0:T(8,128)(2,1)S(1)}, u32[]{:S(2)}, u32[]{:S(2)}) collective-permute-start(bf16[32,512]{1,0:T(8,128)(2,1)S(1)} %get-tuple-element.42), channel_id=1, source_target_pairs={{0,24},{4,28},{8,16},{12,20},{16,8},{20,12},{24,0},{28,4},{1,25},{... | collective-permute-start | bytes 98312 | tf_op jit(solution)/shard_map/ppermute | solution.py:281
  62.0 4.8 %collective-permute-start.20 = (bf16[32,512]{1,0:T(8,128)(2,1)S(1)}, bf16[32,512]{1,0:T(8,128)(2,1)S(1)}, u32[]{:S(2)}, u32[]{:S(2)}) collective-permute-start(bf16[32,512]{1,0:T(8,128)(2,1)S(1)} %get-tuple-element.42), channel_id=1, source_target_pairs={{0,16},{4,20},{8,24},{12,28},{16,0},{20,4},{24,8},{28,12},{1,17},{... | collective-permute-start | bytes 98312 | tf_op jit(solution)/shard_map/ppermute | solution.py:281
  62.3 4.9 %collective-permute-start.19 = (bf16[32,512]{1,0:T(8,128)(2,1)S(1)}, bf16[32,512]{1,0:T(8,128)(2,1)S(1)}, u32[]{:S(2)}, u32[]{:S(2)}) collective-permute-start(bf16[32,512]{1,0:T(8,128)(2,1)S(1)} %get-tuple-element.42), channel_id=1, source_target_pairs={{0,8},{4,12},{8,0},{12,4},{16,24},{20,28},{24,16},{28,20},{1,9},{5... | collective-permute-start | bytes 98312 | tf_op jit(solution)/shard_map/ppermute | solution.py:281
  64.9 7.3 %collective-permute-start.18 = (f32[2,40,512]{2,1,0:T(8,128)S(1)}, f32[2,40,512]{2,1,0:T(8,128)S(1)}, u32[]{:S(2)}, u32[]{:S(2)}) collective-permute-start(f32[2,40,512]{2,1,0:T(8,128)S(1)} %pad_maximum_fusion.1), channel_id=1, source_target_pairs={{0,1},{1,0},{2,3},{3,2},{4,5},{5,4},{6,7},{7,6},{8,9},{9,8},{10,11... | collective-permute-start | bytes 491528 | tf_op jit(solution)/shard_map/ppermute | solution.py:281
  67.2 5.0 %collective-permute-start.22 = (bf16[4,32,512]{2,1,0:T(8,128)(2,1)S(1)}, bf16[4,32,512]{2,1,0:T(8,128)(2,1)S(1)}, u32[]{:S(2)}, u32[]{:S(2)}) collective-permute-start(bf16[4,32,512]{2,1,0:T(8,128)(2,1)S(1)} %pad_maximum_fusion.3.refs_0_), channel_id=1, source_target_pairs={{0,4},{4,0},{8,12},{12,8},{16,20},{20,16},{24,28},{28,24},{1,5},{5... | collective-permute-start | bytes 393224 | tf_op jit(solution)/shard_map/ppermute | solution.py:281
  72.2 5.8 %copy-start.1 = (bf16[32,4,256,256]{3,2,1,0:T(8,128)(2,1)S(1)}, bf16[32,4,256,256]{3,2,1,0:T(8,128)(2,1)}, u32[]{:S(2)}) copy-start(bf16[32,4,256,256]{3,2,1,0:T(8,128)(2,1)} %copy-done) | copy-start | bytes 50331652
  82.1 8.3 %collective-permute-start.23 = (f32[2,32,512]{2,1,0:T(8,128)S(1)}, f32[2,32,512]{2,1,0:T(8,128)S(1)}, u32[]{:S(2)}, u32[]{:S(2)}) collective-permute-start(f32[2,32,512]{2,1,0:T(8,128)S(1)} %get-tuple-element.39), channel_id=1, source_target_pairs={{0,1},{1,0},{2,3},{3,2},{4,5},{5,4},{6,7},{7,6},{8,9},{9,8},{10,11... | collective-permute-start | bytes 393224 | tf_op jit(solution)/shard_map/ppermute | solution.py:281
  82.2 3.8 %collective-permute-start.25 = (f32[32,128]{1,0:T(8,128)S(1)}, f32[32,128]{1,0:T(8,128)S(1)}, u32[]{:S(2)}, u32[]{:S(2)}) collective-permute-start(f32[32,128]{1,0:T(8,128)S(1)} %get-tuple-element.41), channel_id=1, source_target_pairs={{0,4},{4,0},{8,12},{12,8},{16,20},{20,16},{24,28},{28,24},{1,5},{5... | collective-permute-start | bytes 49160 | tf_op jit(solution)/shard_map/ppermute | solution.py:281
  86.0 6.1 %collective-permute-start.28 = (f32[32,128]{1,0:T(8,128)S(1)}, f32[32,128]{1,0:T(8,128)S(1)}, u32[]{:S(2)}, u32[]{:S(2)}) collective-permute-start(f32[32,128]{1,0:T(8,128)S(1)} %add.87), channel_id=1, source_target_pairs={{0,24},{4,28},{8,16},{12,20},{16,8},{20,12},{24,0},{28,4},{1,25},{... | collective-permute-start | bytes 49160 | tf_op jit(solution)/shard_map/ppermute | solution.py:281
  88.3 4.6 %collective-permute-start.27 = (f32[32,128]{1,0:T(8,128)S(1)}, f32[32,128]{1,0:T(8,128)S(1)}, u32[]{:S(2)}, u32[]{:S(2)}) collective-permute-start(f32[32,128]{1,0:T(8,128)S(1)} %add.87), channel_id=1, source_target_pairs={{0,16},{4,20},{8,24},{12,28},{16,0},{20,4},{24,8},{28,12},{1,17},{... | collective-permute-start | bytes 49160 | tf_op jit(solution)/shard_map/ppermute | solution.py:281
  88.6 4.4 %collective-permute-start.26 = (f32[32,128]{1,0:T(8,128)S(1)}, f32[32,128]{1,0:T(8,128)S(1)}, u32[]{:S(2)}, u32[]{:S(2)}) collective-permute-start(f32[32,128]{1,0:T(8,128)S(1)} %add.87), channel_id=1, source_target_pairs={{0,8},{4,12},{8,0},{12,4},{16,24},{20,28},{24,16},{28,20},{1,9},{5... | collective-permute-start | bytes 49160 | tf_op jit(solution)/shard_map/ppermute | solution.py:281
  90.4 4.3 %collective-permute-start.24 = (f32[32,512]{1,0:T(8,128)S(1)}, f32[32,512]{1,0:T(8,128)S(1)}, u32[]{:S(2)}, u32[]{:S(2)}) collective-permute-start(f32[32,512]{1,0:T(8,128)S(1)} %fusion), channel_id=1, source_target_pairs={{0,2},{1,3},{2,0},{3,1},{4,6},{5,7},{6,4},{7,5},{8,10},{9,11},{10,... | collective-permute-start | bytes 196616 | tf_op jit(solution)/shard_map/ppermute | solution.py:281
  94.8 4.5 %collective-permute-start.29 = (f32[32,640]{1,0:T(8,128)S(1)}, f32[32,640]{1,0:T(8,128)S(1)}, u32[]{:S(2)}, u32[]{:S(2)}) collective-permute-start(f32[32,640]{1,0:T(8,128)S(1)} %get-tuple-element.45.refs_3_), channel_id=1, source_target_pairs={{0,2},{1,3},{2,0},{3,1},{4,6},{5,7},{6,4},{7,5},{8,10},{9,11},{10,... | collective-permute-start | bytes 245768 | tf_op jit(solution)/shard_map/ppermute | solution.py:281
  99.3 1.5 %collective-permute-start.30 = (f32[2,32,640]{2,1,0:T(8,128)S(1)}, f32[2,32,640]{2,1,0:T(8,128)S(1)}, u32[]{:S(2)}, u32[]{:S(2)}) collective-permute-start(f32[2,32,640]{2,1,0:T(8,128)S(1)} %pad_maximum_fusion.2), channel_id=1, source_target_pairs={{0,1},{1,0},{2,3},{3,2},{4,5},{5,4},{6,7},{7,6},{8,9},{9,8},{10,11... | collective-permute-start | bytes 491528 | tf_op jit(solution)/shard_map/ppermute | solution.py:281

commit v3 on v2

v3 whole, which is shorter than its diff:
```python
import functools
from typing import NamedTuple

import jax
import jax.numpy as jnp
from jax import lax
from jax.experimental import pallas as pl
from jax.experimental.pallas import tpu as pltpu
from jax.sharding import PartitionSpec as P

REG = 1.5
RADIUS = 0.25
GROUP_BITS = 2
GROUP = 1 << GROUP_BITS
CODE_BITS = 12
CODE = 1 << CODE_BITS
RING = 3
STRIP = 64
LANES = 128
TINY = 1e-30
SHIFT = 0.375
DIRECT_ROWS = 8
RESIDENT_BYTES = 20 * 1024 * 1024

SMEM = pl.BlockSpec(memory_space=pltpu.SMEM)
VMEM = pl.BlockSpec(memory_space=pltpu.VMEM)
HBM = pl.BlockSpec(memory_space=pltpu.HBM)
F32 = jnp.float32
BF16 = jnp.bfloat16


def pair_sum(parts):
    while len(parts) > 1:
        parts = [a + b for a, b in zip(parts[::2], parts[1::2])]
    return parts[0]


class Sizes(NamedTuple):
    parts: int
    resident: bool
    nb: int
    block_len: int
    own_rows: int
    block_rows: int
    count_rows: int


def augment(x, first_ones):
    dim, n = x.shape
    norm = jnp.sum(x * x, axis=0, keepdims=True) / (RADIUS * RADIUS)
    high = norm.astype(BF16).astype(F32)
    rest = norm - high
    mid = rest.astype(BF16).astype(F32)
    low = rest - mid
    line = lax.broadcasted_iota(jnp.int32, (dim, n), 0)
    base = 3 if first_ones else 0
    ones_at = 0 if first_ones else 3
    tail = jnp.where((line >= ones_at) & (line < ones_at + 3), 1.0, 0.0)
    tail = jnp.where(line == base, high, tail)
    tail = jnp.where(line == base + 1, mid, tail)
    tail = jnp.where(line == base + 2, low, tail)
    return tail


def row_of(cfg, place, part, z):
    if cfg.parts == 1:
        return z
    return 2 * z + (place[0] & 1 if part == 0 else 1 - (place[0] & 1))


def slot_of(cfg, place, n):
    return n if cfg.parts == 1 else lax.shift_right_logical(place[0], 1) ^ n


def build_kernel(cfg, part, place, direct, *refs):
    last = part == cfg.parts - 1
    if part == 0:
        near_hbm, piece, refs = refs[0], refs[1], refs[2:]
        k_mat, listed, deg_ref, lhs = refs[:4]
        near_ref, near_sem, refs = refs[4], refs[5], refs[6:]
        near_copy = pltpu.make_async_copy(near_hbm, near_ref, near_sem)
        near_copy.start()
    else:
        lhs, first_deg, piece = refs[:3]
        k_mat, listed, deg_ref = refs[3:6]
        refs = refs[6:]
    mlist, acc, rhs, counts_v, counts, count_sem = refs[:6]
    kbuf, sems = (None, None) if cfg.resident else refs[6:]
    row, col = place[0], place[1]
    own_rows, block_len, nb = cfg.own_rows, cfg.block_len, cfg.nb
    own_len = own_rows * block_len
    dim, held = piece.shape[1], piece.shape[0]
    scale = 1.0 / (RADIUS * RADIUS)

    def prepare(n, carry):
        z = slot_of(cfg, place, n)
        for k in range(own_rows):
            far = piece[n, :, k * block_len:(k + 1) * block_len]
            rhs[z * own_rows + k, :dim, :] = far
            rhs[z * own_rows + k, dim:, :] = augment(far.astype(F32), False).astype(BF16)
        named = piece[n, :, own_len:own_len + LANES]
        counts_v[z] = named.astype(F32)[:cfg.count_rows].astype(jnp.int32)
        return carry

    lax.fori_loop(0, held, prepare, 0, unroll=held <= 4)
    fetch = pltpu.make_async_copy(counts_v, counts, count_sem)
    fetch.start()
    if part == 0:
        near_copy.wait()
        for i in range(cfg.block_rows):
            near = near_ref[:, i * block_len:(i + 1) * block_len].astype(F32)
            full = jnp.concatenate([near * (-2.0 * scale), augment(near, True)], axis=0)
            lhs[i] = full.T.astype(BF16)
    acc[...] = jnp.zeros_like(acc)
    fetch.wait()

    pos = jnp.int32(0)
    for i in range(cfg.block_rows):
        me = row * cfg.block_rows + i
        spots = [k * nb + me for k in range(own_rows)]
        spots = [(lax.shift_right_logical(p, 7), p & (LANES - 1)) for p in spots]

        def note(z, at, i=i, me=me, spots=spots):
            for k in range(own_rows):
                name = row_of(cfg, place, part, z) * cfg.block_rows + col * own_rows + k
                m = direct[i, name] + jnp.where(name == me, 0, counts[z, spots[k][0], spots[k][1]])
                listed[at + 1] = i * CODE + z * own_rows + k
                mlist[at] = m
                at = at + jnp.where(m > 0, 1, 0)
            return at

        pos = lax.fori_loop(0, held, note, pos, unroll=4)
    for u in range(GROUP):
        listed[pos + u + 1] = 0
        mlist[pos + u] = 0
    total = lax.shift_right_logical(pos + (GROUP - 1), GROUP_BITS)
    listed[0] = total

    def copy_out(g):
        slot = lax.rem(g, RING)
        return pltpu.make_async_copy(kbuf.at[slot], k_mat.at[g], sems.at[slot])

    def step(g, carry):
        slot, target = (g, k_mat) if cfg.resident else (lax.rem(g, RING), kbuf)
        if not cfg.resident:

            @pl.when(g >= RING)
            def _():
                copy_out(g - RING).wait()

        for u in range(GROUP):
            code = listed[g * GROUP + u + 1]
            i, j = lax.shift_right_logical(code, CODE_BITS), code & (CODE - 1)
            m = mlist[g * GROUP + u].astype(F32)
            far = rhs[j]
            sums = jnp.zeros((8, block_len), F32)
            for s in range(block_len // STRIP):
                rows = slice(s * STRIP, (s + 1) * STRIP)
                d = jnp.dot(lhs[i, rows, :], far, preferred_element_type=F32)
                d = jnp.maximum(d, TINY)
                sc = d * lax.rsqrt(d)
                rem = jnp.maximum(1.0 - sc, 0.0)
                sq = rem * rem
                val = (sq * sq) * (sc * (4.0 * m) + m)
                target[slot, u, rows, :] = val.astype(BF16)
                for h in range(0, STRIP, 8):
                    sums = sums + val[h:h + 8]
            acc[j] += sums
        if not cfg.resident:
            copy_out(g).start()
        return carry

    lax.fori_loop(0, total, step, 0)
    if cfg.parts == 1 or not last:
        deg_ref[...] = jnp.sum(acc[...], axis=1)
    else:
        second = jnp.sum(acc[...], axis=1)
        for z in range(held):
            rows = slice(z * own_rows, (z + 1) * own_rows)
            for p, deg in enumerate((first_deg[rows, :], second[rows])):
                at = row_of(cfg, place, p, z) * own_rows
                for k in range(own_rows):
                    deg_ref[pl.ds(at + k, 1), :] = deg[k:k + 1]

    def drain(g, carry):
        copy_out(g).wait()
        return carry

    if not cfg.resident:
        lax.fori_loop(jnp.maximum(total - RING, 0), total, drain, 0)


def apply_kernel(cfg, parts, scaled, carried, finish, extra_k, place, *refs):
    n = len(parts)
    lists, ks, pieces, refs = refs[:n], refs[n:2 * n], refs[2 * n:3 * n], refs[3 * n + extra_k:]
    if scaled:
        inv_ref, refs = refs[0], refs[1:]
    if carried:
        z_in, refs = refs[0], refs[1:]
    products = finish and not scaled
    if products:
        t_ref, s_refs, refs = refs[0], refs[1:5], refs[5:]
    if finish:
        near, near_y, cross, refs = refs[0], refs[1], refs[2], refs[3:]
        if products:
            dot_ref, refs = refs[0], refs[1:]
        z_acc, refs = refs[0], refs[1:]
    else:
        z_acc, refs = refs[0], refs[1:]
    w_all, refs = refs[0], refs[1:]
    kbuf, sems = (None, None) if cfg.resident else refs
    col = place[1]
    own_rows, block_len = cfg.own_rows, cfg.block_len

    z_acc[...] = z_in[...] if carried else jnp.zeros_like(z_acc)
    for part, listed, k_mat, piece in zip(parts, lists, ks, pieces):
        total = listed[0]
        held = piece.shape[0]

        def copy_in(g, k_mat=k_mat):
            slot = lax.rem(g, RING)
            return pltpu.make_async_copy(k_mat.at[g], kbuf.at[slot], sems.at[slot])

        if not cfg.resident:
            for p in range(RING - 1):

                @pl.when(p < total)
                def _(p=p, copy_in=copy_in):
                    copy_in(p).start()

        def prepare(n, carry, part=part, piece=piece):
            z = slot_of(cfg, place, n)
            for k in range(own_rows):
                w = piece[n, :, k * block_len:(k + 1) * block_len]
                if scaled:
                    at = row_of(cfg, place, part, z) * own_rows + k
                    w = (w * inv_ref[pl.ds(at, 1), :]).astype(BF16)
                w_all[z * own_rows + k] = w
            return carry

        lax.fori_loop(0, held, prepare, 0, unroll=held <= 4)

        def step(g, carry, total=total, listed=listed, k_mat=k_mat, copy_in=copy_in):
            slot, source = (g, k_mat) if cfg.resident else (lax.rem(g, RING), kbuf)
            if not cfg.resident:

                @pl.when(g + (RING - 1) < total)
                def _():
                    copy_in(g + (RING - 1)).start()

                copy_in(g).wait()
            codes = [listed[g * GROUP + u + 1] for u in range(GROUP)]
            terms = [
                lax.dot_general(
                    w_all[code & (CODE - 1)],
                    source[slot, u],
                    (((1,), (1,)), ((), ())),
                    preferred_element_type=F32,
                )
                for u, code in enumerate(codes)
            ]
            for code, term in zip(codes, terms):
                z_acc[lax.shift_right_logical(code, CODE_BITS)] += term
            return carry

        lax.fori_loop(0, total, step, 0)
    if not finish:
        return
    own_len = own_rows * block_len
    z_refs = (near, cross.at[0], near_y, cross.at[1])
    for e in range(4):
        for k in range(own_rows):
            z_refs[e][:, k * block_len:(k + 1) * block_len] = z_acc[(col ^ e) * own_rows + k]
    if products:
        outputs = t_ref.shape[0]
        ts2 = jnp.zeros((outputs, 1), F32)
        s1s2 = jnp.zeros((outputs, 1), F32)
        for e, packed in enumerate(s_refs):
            at = pl.ds(pl.multiple_of((col ^ e) * own_len, LANES), own_len)
            grown = z_refs[e][...] * packed[outputs:outputs + 1, :]
            ts2 += jnp.sum(t_ref[:, at] * grown, axis=1, keepdims=True)
            s1s2 += jnp.sum(packed[:outputs, :] * grown, axis=1, keepdims=True)
        t = t_ref[:, pl.ds(pl.multiple_of(col * own_len, LANES), own_len)]
        s1 = s_refs[0][:outputs, :]
        tt = jnp.sum(t * t, axis=1, keepdims=True)
        ts1 = jnp.sum(t * s1, axis=1, keepdims=True)
        s1s1 = jnp.sum(s1 * s1, axis=1, keepdims=True)
        ts2 += SHIFT * ts1
        s1s2 += SHIFT * s1s1
        lane = lax.broadcasted_iota(jnp.int32, (outputs, LANES), 1)
        out = jnp.zeros(lane.shape, F32)
        for n, v in enumerate((tt, ts1, s1s1, ts2, s1s2)):
            out = jnp.where(lane == n, v, out)
        dot_ref[...] = out


def final_kernel(n_cols, place, t_ref, *refs):
    s1s, s2s = refs[:4], refs[4:8]
    sol_ref, res_ref = refs[8:]
    outputs, own_len = s2s[0].shape[0], s2s[0].shape[1] - LANES
    dots = pair_sum([ref[:, own_len:] for ref in s2s])
    tt, ts1, s1s1, ts2, s1s2 = (dots[:, n:n + 1] for n in range(5))
    a1 = tt / (REG * tt + ts1)
    p = 1.0 - REG * a1
    new = p * p * tt - 2.0 * p * a1 * ts1 + a1 * a1 * s1s1
    u = p + new / tt
    dd = u * u * tt - 2.0 * u * a1 * ts1 + a1 * a1 * s1s1
    dmd = u * u * ts1 - u * a1 * (s1s1 + ts2) + a1 * a1 * s1s2
    a2 = new / (REG * dd + dmd)
    for e in range(n_cols):
        at = pl.ds(pl.multiple_of((place[1] ^ e) * own_len, LANES), own_len)
        t, s1, s2 = t_ref[:, at], s1s[e][:outputs, :], s2s[e][:, :own_len]
        sol_ref[:, at] = (a1 + a2 * u) * t - (a2 * a1) * s1
        res_ref[:, at] = (p - a2 * REG * u) * t - (a1 + a2 * (u - REG * a1)) * s1 + (a2 * a1) * s2


def swap(x, axis, d):
    size = lax.axis_size(axis)
    return lax.ppermute(x, axis, [(i, i ^ d) for i in range(size)])


def half_shared(near, near_y, cross):
    got = swap(cross, "cols", 1)
    return near + got[0], near_y + got[1]


def shared(near, near_y):
    return near + swap(near_y, "cols", 2)


def along_z(x):
    return [x] + [swap(x, "rows", d) for d in range(2, lax.axis_size("rows"), 2)]


def across_x(same):
    return [same, swap(same, "rows", 1)]


def direct_cols(x):
    return [x] + [swap(x, "cols", e) for e in range(1, 4)]


def local(block_list, points, targets):
    n_rows = lax.axis_size("rows")
    n_cols = lax.axis_size("cols")
    row = lax.axis_index("rows")
    col = lax.axis_index("cols")
    block_rows, slots = block_list.shape
    dim, npoints = points.shape
    outputs = targets.shape[0]
    block_len = npoints // block_rows
    own_rows = block_rows // n_cols
    own_len = own_rows * block_len
    nb = block_rows * n_rows
    n_sub = own_rows * n_rows
    capacity = -(-block_rows * slots // n_rows)
    direct_rows = n_rows <= DIRECT_ROWS
    parts = 2 if direct_rows else 1
    n_part = n_sub // parts
    bound = min(block_rows * n_part, n_cols * capacity * (n_rows + 1))
    n_groups = -(-bound // GROUP)
    list_len = n_groups * GROUP + GROUP + 1
    place = jnp.stack([row, col])
    k_shape = (n_groups, GROUP, block_len, block_len)
    resident = parts * 2 * n_groups * GROUP * block_len * block_len <= RESIDENT_BYTES
    limit = pltpu.CompilerParams(vmem_limit_bytes=(8 if resident else 32) * 1024 * 1024)
    ring = [] if resident else [
        pltpu.VMEM((RING, GROUP, block_len, block_len), BF16),
        pltpu.SemaphoreType.DMA((RING,)),
    ]
    k_spec = VMEM if resident else HBM
    cfg = Sizes(
        parts, resident, nb, block_len, own_rows, block_rows, -(-own_rows * nb // LANES)
    )

    def shape(*dims, dtype=F32):
        return jax.ShapeDtypeStruct(dims, dtype)

    def own(x):
        return lax.dynamic_slice_in_dim(x, col * own_len, own_len, 1)

    def total_rows(x):
        if direct_rows:
            return pair_sum(across_x(pair_sum(along_z(x))))
        return lax.psum(x, "rows")

    lists = direct_cols(block_list)
    names = jnp.arange(nb, dtype=jnp.int32)
    direct = sum(jnp.sum((x[:, :, None] == names).astype(jnp.int32), axis=1) for x in lists)
    own_counts = lax.dynamic_slice_in_dim(direct, col * own_rows, own_rows, 0)
    coded = own_counts.reshape(-1)
    coded = jnp.pad(coded, (0, dim * LANES - coded.shape[0])).reshape(dim, LANES).astype(BF16)
    packed = jnp.concatenate([own(points), coded], axis=1)
    own_t = own(targets)

    def build(part, *operands):
        first, last = part == 0, part == parts - 1
        out = [
            pltpu.VMEM(k_shape, BF16) if resident else shape(*k_shape, dtype=BF16),
            shape(list_len, dtype=jnp.int32),
            shape(n_sub if last else n_part, block_len),
        ]
        out += [shape(block_rows, block_len, 2 * dim, dtype=BF16)] if first else []
        k_mat, *rest = pl.pallas_call(
            functools.partial(build_kernel, cfg, part),
            out_shape=out,
            in_specs=[SMEM, SMEM] + ([HBM, VMEM] if first else [VMEM] * 3),
            out_specs=[k_spec, SMEM] + [VMEM] * (len(out) - 2),
            scratch_shapes=([
                pltpu.VMEM((dim, npoints), BF16),
                pltpu.SemaphoreType.DMA,
            ] if first else []) + [
                pltpu.SMEM((list_len,), jnp.int32),
                pltpu.VMEM((n_part, 8, block_len), F32),
                pltpu.VMEM((n_part, 2 * dim, block_len), BF16),
                pltpu.VMEM((n_part // own_rows, cfg.count_rows, LANES), jnp.int32),
                pltpu.SMEM((n_part // own_rows, cfg.count_rows, LANES), jnp.int32),
                pltpu.SemaphoreType.DMA,
                *ring,
            ],
            compiler_params=limit,
            cost_estimate=pl.CostEstimate(
                flops=2 * 2 * dim * bound * block_len * block_len,
                bytes_accessed=2 * bound * block_len * block_len,
                transcendentals=bound * block_len * block_len,
            ),
            name="build",
        )(place, direct, *operands)
        if resident:
            k_mat = pltpu.with_memory_space_constraint(k_mat, pltpu.VMEM)
        return k_mat, *rest

    near = pltpu.with_memory_space_constraint(points, pltpu.HBM)
    if direct_rows:
        packed, early_t = lax.optimization_barrier((packed, own_t))
        same, other = across_x(jnp.stack(along_z(packed)))
        t_same = along_z(early_t)
        k0, list0, degree, lhs = build(0, near, same)
        degree, other, *t_same = lax.optimization_barrier((degree, other, *t_same))
        t_same, t_other = across_x(jnp.stack(t_same))
        other, t_same = lax.optimization_barrier((other, t_same))
        k1, list1, degree = build(1, lhs, degree, other)
        degree, t_other = lax.optimization_barrier((degree, t_other))
        t_pieces, k_mats, k_lists = [t_same, t_other], [k0, k1], [list0, list1]
    else:
        k0, list0, degree, _ = build(0, near, lax.all_gather(packed, "rows"))
        t_pieces, k_mats, k_lists = [lax.all_gather(own_t, "rows")], [k0], [list0]
    inv = 1.0 / jnp.sqrt(1.0 + total_rows(degree))
    own_inv = lax.dynamic_slice_in_dim(inv, row * own_rows, own_rows, 0).reshape(1, own_len)

    def apply(use, pieces, finish=True, inv=None, z_in=None, products=()):
        spare = [k for p, k in enumerate(k_mats) if p not in use]
        operands = [k_lists[p] for p in use] + [k_mats[p] for p in use] + pieces + spare
        specs = [SMEM] * len(use) + [k_spec] * len(use) + [VMEM] * len(pieces) + [k_spec] * len(spare)
        more = [x for x in (inv, z_in) if x is not None] + list(products)
        z_shape = (block_rows, outputs, block_len)
        if finish:
            out = [shape(outputs, own_len), shape(outputs, own_len), shape(2, outputs, own_len)]
            out += [shape(outputs, LANES)] if products else []
        else:
            out = [shape(*z_shape)]
        return pl.pallas_call(
            functools.partial(
                apply_kernel, cfg, use, inv is not None, z_in is not None, finish, len(spare)
            ),
            out_shape=out,
            in_specs=[SMEM] + specs + [VMEM] * len(more),
            out_specs=[VMEM] * len(out),
            scratch_shapes=([pltpu.VMEM(z_shape, F32)] if finish else []) + [
                pltpu.VMEM((n_part, outputs, block_len), BF16),
                *ring,
            ],
            compiler_params=limit,
            cost_estimate=pl.CostEstimate(
                flops=2 * len(use) * bound * outputs * block_len * block_len,
                bytes_accessed=len(use) * bound * block_len * block_len,
                transcendentals=0,
            ),
            name="apply",
        )(place, *operands, *more)

    s1 = shared(*half_shared(*apply(tuple(range(parts)), t_pieces, inv=inv))) * own_inv
    g = ((s1 - SHIFT * own_t) * own_inv).astype(BF16)
    s1_packed = jnp.concatenate([s1, jnp.broadcast_to(own_inv, (8, own_len))], axis=0)
    if direct_rows:
        g_same = jnp.stack(along_z(g))
        g_same, s1_packed = lax.optimization_barrier((g_same, s1_packed))
        _, g_other = across_x(g_same)
        s1_all = direct_cols(s1_packed)
        (z_part,) = apply((0,), [g_same], finish=False)
        z_part, g_other, *s1_all = lax.optimization_barrier((z_part, g_other, *s1_all))
        *z2, dots = apply((1,), [g_other], z_in=z_part, products=[targets, *s1_all])
        z2 = half_shared(*z2)
        dots = pair_sum(across_x(dots))
        dots, *z2 = lax.optimization_barrier((dots, *z2))
        s2 = shared(*z2)
        dots = pair_sum(along_z(dots))
    else:
        s1_all = direct_cols(s1_packed)
        *z2, dots = apply((0,), [lax.all_gather(g, "rows")], products=[targets, *s1_all])
        s2 = shared(*half_shared(*z2))
        dots = lax.psum(dots, "rows")
    s2 = s2 * own_inv + SHIFT * s1
    ends = direct_cols(jnp.concatenate([s2, dots], axis=1))
    s1_all, ends = [
        [pltpu.with_memory_space_constraint(x, pltpu.VMEM) for x in xs] for xs in (s1_all, ends)
    ]

    return pl.pallas_call(
        functools.partial(final_kernel, n_cols),
        out_shape=(shape(outputs, npoints), shape(outputs, npoints)),
        in_specs=[SMEM] + [VMEM] * 9,
        out_specs=(VMEM, VMEM),
        name="final",
    )(place, targets, *s1_all, *ends)


def solution(mesh):
    placed = (P("rows", "cols"), P(None, "rows"), P(None, "rows"))
    return jax.shard_map(
        local,
        mesh=mesh,
        in_specs=placed,
        out_specs=(P(None, "rows"), P(None, "rows")),
        check_vma=False,
    )
```

time: 103 us -> 96.9 us (0.941)
  waiting for transfers between devices: 34.9 us -> 25.2 us
  starting transfers between devices: 32.9 us -> 38.8 us
  local copies, waits for them, and re-layouts: 14.2 us -> 10.9 us
    ppermute x31 -> x33, waiting for transfers between devices: 34.9 us -> 25.2 us  [swap(): return lax.ppermute(x, axis, [(i, i ^ d) for i in range(size)])]
    ppermute x31 -> x33, starting transfers between devices: 32.9 us -> 38.8 us  [swap(): return lax.ppermute(x, axis, [(i, i ^ d) for i in range(size)])]
    unnamed x11 -> x17, local copies, waits for them, and re-layouts: 12.3 us -> 8.99 us
    pallas_call x3 -> x5, Pallas kernels: 17.2 us -> 18.1 us  [the longest x2 10.8 us: build(): pl.pallas_call(functools.partial(build_kernel, cfg, part), out_shape=out,...]
  transfers between devices with their start and end apart: 31 -> 33, of which waited for: 18 -> 15; matrix products, arithmetic and copies ran while one was open for 3% -> 3% of each run, Pallas kernels for 9% -> 13%
where the time goes in v3:
time: 96.9 us; the launch traced here: 96.7 us
  starting transfers between devices  38.8 us (40%)
  waiting for transfers between devices  25.2 us (26%)
  Pallas kernels  20.2 us (21%)
  local copies, waits for them, and re-layouts  10.9 us (11%)
    ppermute x33, starting transfers between devices, swap(): return lax.ppermute(x, axis, [(i, i ^ d) for i in range(size)])  38.8 us
    ppermute x33, waiting for transfers between devices, swap(): return lax.ppermute(x, axis, [(i, i ^ d) for i in range(size)])  25.2 us
    pallas_call x2, Pallas kernels, build(): pl.pallas_call(functools.partial(build_kernel, cfg, part), out_shape=out,...  10.8 us
    unnamed x17, local copies, waits for them, and re-layouts  8.99 us
    pallas_call x3, Pallas kernels, apply(): pl.pallas_call(functools.partial(apply_kernel, cfg, use, inv is not None,...  7.36 us
    pallas_call x1, Pallas kernels, local(): pl.pallas_call(functools.partial(final_kernel, n_cols), out_shape=(shape(...  2.08 us
  transfers between devices with their start and end apart: 33, of which 15 were waited for; matrix products, arithmetic and copies ran while one was open for 3% of the time, Pallas kernels for 13%

profile of v3, /device:TPU:0, one launch (start us, length us, event | category | flops | bytes accessed | tf_op | source)
XLA Modules:
  0.0 96.7 jit_solution(11509911245130404134)
XLA Ops:
  0.6 2.5 %collective-permute-start.2 = (s32[8,6]{1,0:T(8,128)}, s32[8,6]{1,0:T(8,128)S(1)}, u32[]{:S(2)}, u32[]{:S(2)}) collective-permute-start(s32[8,6]{1,0:T(8,128)} %param.3), channel_id=1, source_target_pairs={{0,3},{1,2},{2,1},{3,0},{4,7},{5,6},{6,5},{7,4},{8,11},{9,10},{10,... | collective-permute-start | bytes 584 | tf_op jit(solution)/shard_map/ppermute | solution.py:319
  3.1 0.6 collective-permute-start.1
  3.8 0.8 copy.5
  4.7 0.7 constant_dynamic-slice_fusion.1
  5.4 0.8 constant_dynamic-slice_fusion
  6.4 0.5 collective-permute-done.1
  7.4 1.6 %collective-permute-start.3 = (bf16[16,640]{1,0:T(8,128)(2,1)S(1)}, bf16[16,640]{1,0:T(8,128)(2,1)S(1)}, u32[]{:S(2)}, u32[]{:S(2)}) collective-permute-start(bf16[16,640]{1,0:T(8,128)(2,1)S(1)} %pad_maximum_fusion.5), channel_id=1, source_target_pairs={{0,8},{4,12},{8,0},{12,4},{16,24},{20,28},{24,16},{28,20},{1,9},{5... | collective-permute-start | bytes 61448 | tf_op jit(solution)/shard_map/ppermute | solution.py:319
  9.0 2.6 %collective-permute-start.4 = (bf16[16,640]{1,0:T(8,128)(2,1)S(1)}, bf16[16,640]{1,0:T(8,128)(2,1)S(1)}, u32[]{:S(2)}, u32[]{:S(2)}) collective-permute-start(bf16[16,640]{1,0:T(8,128)(2,1)S(1)} %pad_maximum_fusion.5), channel_id=1, source_target_pairs={{0,16},{4,20},{8,24},{12,28},{16,0},{20,4},{24,8},{28,12},{1,17},{... | collective-permute-start | bytes 61448 | tf_op jit(solution)/shard_map/ppermute | solution.py:319
  11.8 0.7 collective-permute-start.7
  12.5 3.5 %collective-permute-start.8 = (f32[32,512]{1,0:T(8,128)S(1)}, f32[32,512]{1,0:T(8,128)S(1)}, u32[]{:S(2)}, u32[]{:S(2)}) collective-permute-start(f32[32,512]{1,0:T(8,128)S(1)} %constant_dynamic-slice_fusion), channel_id=1, source_target_pairs={{0,16},{4,20},{8,24},{12,28},{16,0},{20,4},{24,8},{28,12},{1,17},{... | collective-permute-start | bytes 196616 | tf_op jit(solution)/shard_map/ppermute | solution.py:319
  16.2 1.1 %collective-permute-done.5 = bf16[16,640]{1,0:T(8,128)(2,1)S(1)} collective-permute-done((bf16[16,640]{1,0:T(8,128)(2,1)S(1)}, bf16[16,640]{1,0:T(8,128)(2,1)S(1)}, u32[]{:S(2)}, u32[]{:S(2)}) %collective-permute-start.5) | collective-permute-done | bytes 20512 | tf_op jit(solution)/shard_map/ppermute | solution.py:319
  17.3 1.6 %collective-permute-start.6 = (bf16[4,16,640]{2,1,0:T(8,128)(2,1)S(1)}, bf16[4,16,640]{2,1,0:T(8,128)(2,1)S(1)}, u32[]{:S(2)}, u32[]{:S(2)}) collective-permute-start(bf16[4,16,640]{2,1,0:T(8,128)(2,1)S(1)} %pad_maximum_fusion.2.refs_1_), channel_id=1, source_target_pairs={{0,4},{4,0},{8,12},{12,8},{16,20},{20,16},{24,28},{28,24},{1,5},{5... | collective-permute-start | bytes 245768 | tf_op jit(solution)/shard_map/ppermute | solution.py:319
  18.9 5.6 %build.2 = (bf16[16,4,256,256]{3,2,1,0:T(8,128)(2,1)S(1)}, s32[69]{0:T(128)S(1)}, f32[8,256]{1,0:T(8,128)S(1)}, bf16[8,256,32]{2,1,0:T(8,128)(2,1)S(1)}) custom-call(s32[2]{0:T(128)S(1)} %pad_add_fusion.place, s32[8,64]{1,0:T(8,128)S(1)} %add_add_fusion.2.direct, bf16[16,2048]{1,0:T(8,128)(2,1)} %refs_0_.1, bf16[4,16,640]{2,1,0:T(8,128)(2,1)S(1)} %pad_maximum_fusion.2.refs_1_), custom_call_target="tpu_custom_call" | custom-call | flops 268435456 | bytes 8388608 | tf_op jit(solution)/shard_map/build/pallas_call | solution.py:404
  24.7 0.6 collective-permute-start.10
  25.2 5.2 %build.3 = (bf16[16,4,256,256]{3,2,1,0:T(8,128)(2,1)S(1)}, s32[69]{0:T(128)S(1)}, f32[16,256]{1,0:T(8,128)S(1)}) custom-call(s32[2]{0:T(128)S(1)} %pad_add_fusion.place, s32[8,64]{1,0:T(8,128)S(1)} %add_add_fusion.2.direct, bf16[8,256,32]{2,1,0:T(8,128)(2,1)S(1)} %get-tuple-element.42.refs_0_, f32[8,256]{1,0:T(8,128)S(1)} %get-tuple-element.45.refs_1_, ...), custom_call_target="tpu_custom_call" | custom-call | flops 268435456 | bytes 8388608 | tf_op jit(solution)/shard_map/build/pallas_call | solution.py:404
  30.4 0.9 collective-permute-done.10.refs_5_
  31.3 2.3 %collective-permute-start.12 = (f32[16,256]{1,0:T(8,128)S(1)}, f32[16,256]{1,0:T(8,128)S(1)}, u32[]{:S(2)}, u32[]{:S(2)}) collective-permute-start(f32[16,256]{1,0:T(8,128)S(1)} %get-tuple-element.57), channel_id=1, source_target_pairs={{0,16},{4,20},{8,24},{12,28},{16,0},{20,4},{24,8},{28,12},{1,17},{... | collective-permute-start | bytes 49160 | tf_op jit(solution)/shard_map/ppermute | solution.py:319
  33.6 2.1 %collective-permute-start.13 = (f32[16,256]{1,0:T(8,128)S(1)}, f32[16,256]{1,0:T(8,128)S(1)}, u32[]{:S(2)}, u32[]{:S(2)}) collective-permute-start(f32[16,256]{1,0:T(8,128)S(1)} %get-tuple-element.57), channel_id=1, source_target_pairs={{0,24},{4,28},{8,16},{12,20},{16,8},{20,12},{24,0},{28,4},{1,25},{... | collective-permute-start | bytes 49160 | tf_op jit(solution)/shard_map/ppermute | solution.py:319
  35.7 0.2 collective-permute-done.12
  36.0 3.2 %collective-permute-done.13 = f32[16,256]{1,0:T(8,128)S(1)} collective-permute-done((f32[16,256]{1,0:T(8,128)S(1)}, f32[16,256]{1,0:T(8,128)S(1)}, u32[]{:S(2)}, u32[]{:S(2)}) %collective-permute-start.13) | collective-permute-done | bytes 16416 | tf_op jit(solution)/shard_map/ppermute | solution.py:319
  39.2 1.2 %collective-permute-start.14 = (f32[16,256]{1,0:T(8,128)S(1)}, f32[16,256]{1,0:T(8,128)S(1)}, u32[]{:S(2)}, u32[]{:S(2)}) collective-permute-start(f32[16,256]{1,0:T(8,128)S(1)} %add_add_fusion.1), channel_id=1, source_target_pairs={{0,4},{4,0},{8,12},{12,8},{16,20},{20,16},{24,28},{28,24},{1,5},{5... | collective-permute-start | bytes 49160 | tf_op jit(solution)/shard_map/ppermute | solution.py:319
  40.3 2.6 %collective-permute-done.14 = f32[16,256]{1,0:T(8,128)S(1)} collective-permute-done((f32[16,256]{1,0:T(8,128)S(1)}, f32[16,256]{1,0:T(8,128)S(1)}, u32[]{:S(2)}, u32[]{:S(2)}) %collective-permute-start.14) | collective-permute-done | bytes 16416 | tf_op jit(solution)/shard_map/ppermute | solution.py:319
  43.0 3.4 %apply.3 = (f32[32,512]{1,0:T(8,128)S(1)}, f32[32,512]{1,0:T(8,128)S(1)}, f32[2,32,512]{2,1,0:T(8,128)S(1)}) custom-call(s32[2]{0:T(128)S(1)} %pad_add_fusion.place, s32[69]{0:T(128)S(1)} %get-tuple-element.40.refs_0_, s32[69]{0:T(128)S(1)} %get-tuple-element.52.refs_1_.refs_0_, bf16[16,4,256,256]{3,2,1,0:T(8,128)(2,1)S(1)} %get-tuple-element.41.refs_2_.refs_1_.refs_3_, ...), custom_call_target="tpu_custom_call" | custom-call | flops 536870912 | bytes 8388608 | tf_op jit(solution)/shard_map/apply/pallas_call | solution.py:462
  46.4 1.3 %collective-permute-done.15 = f32[2,32,512]{2,1,0:T(8,128)S(1)} collective-permute-done((f32[2,32,512]{2,1,0:T(8,128)S(1)}, f32[2,32,512]{2,1,0:T(8,128)S(1)}, u32[]{:S(2)}, u32[]{:S(2)}) %collective-permute-start.15) | collective-permute-done | bytes 131104 | tf_op jit(solution)/shard_map/ppermute | solution.py:319
  47.8 2.1 %collective-permute-start.16 = (f32[32,512]{1,0:T(8,128)S(1)}, f32[32,512]{1,0:T(8,128)S(1)}, u32[]{:S(2)}, u32[]{:S(2)}) collective-permute-start(f32[32,512]{1,0:T(8,128)S(1)} %fusion.2), channel_id=1, source_target_pairs={{0,2},{1,3},{2,0},{3,1},{4,6},{5,7},{6,4},{7,5},{8,10},{9,11},{10,... | collective-permute-start | bytes 196616 | tf_op jit(solution)/shard_map/ppermute | solution.py:319
  49.9 2.4 %collective-permute-done.16 = f32[32,512]{1,0:T(8,128)S(1)} collective-permute-done((f32[32,512]{1,0:T(8,128)S(1)}, f32[32,512]{1,0:T(8,128)S(1)}, u32[]{:S(2)}, u32[]{:S(2)}) %collective-permute-start.16) | collective-permute-done | bytes 65568 | tf_op jit(solution)/shard_map/ppermute | solution.py:319
  52.4 2.2 %collective-permute-start.18 = (bf16[32,512]{1,0:T(8,128)(2,1)S(1)}, bf16[32,512]{1,0:T(8,128)(2,1)S(1)}, u32[]{:S(2)}, u32[]{:S(2)}) collective-permute-start(bf16[32,512]{1,0:T(8,128)(2,1)S(1)} %get-tuple-element.76), channel_id=1, source_target_pairs={{0,16},{4,20},{8,24},{12,28},{16,0},{20,4},{24,8},{28,12},{1,17},{... | collective-permute-start | bytes 98312 | tf_op jit(solution)/shard_map/ppermute | solution.py:319
  54.6 2.2 %collective-permute-start.19 = (bf16[32,512]{1,0:T(8,128)(2,1)S(1)}, bf16[32,512]{1,0:T(8,128)(2,1)S(1)}, u32[]{:S(2)}, u32[]{:S(2)}) collective-permute-start(bf16[32,512]{1,0:T(8,128)(2,1)S(1)} %get-tuple-element.76), channel_id=1, source_target_pairs={{0,24},{4,28},{8,16},{12,20},{16,8},{20,12},{24,0},{28,4},{1,25},{... | collective-permute-start | bytes 98312 | tf_op jit(solution)/shard_map/ppermute | solution.py:319
  56.8 0.6 collective-permute-done.18
  57.4 2.9 %collective-permute-done.19 = bf16[32,512]{1,0:T(8,128)(2,1)S(1)} collective-permute-done((bf16[32,512]{1,0:T(8,128)(2,1)S(1)}, bf16[32,512]{1,0:T(8,128)(2,1)S(1)}, u32[]{:S(2)}, u32[]{:S(2)}) %collective-permute-start.19) | collective-permute-done | bytes 32800 | tf_op jit(solution)/shard_map/ppermute | solution.py:319
  60.4 1.0 %collective-permute-start.20 = (bf16[4,32,512]{2,1,0:T(8,128)(2,1)S(1)}, bf16[4,32,512]{2,1,0:T(8,128)(2,1)S(1)}, u32[]{:S(2)}, u32[]{:S(2)}) collective-permute-start(bf16[4,32,512]{2,1,0:T(8,128)(2,1)S(1)} %pad_maximum_fusion.1.refs_2_), channel_id=1, source_target_pairs={{0,4},{4,0},{8,12},{12,8},{16,20},{20,16},{24,28},{28,24},{1,5},{5... | collective-permute-start | bytes 393224 | tf_op jit(solution)/shard_map/ppermute | solution.py:319
  61.4 1.6 %collective-permute-start.22 = (f32[40,512]{1,0:T(8,128)S(1)}, f32[40,512]{1,0:T(8,128)S(1)}, u32[]{:S(2)}, u32[]{:S(2)}) collective-permute-start(f32[40,512]{1,0:T(8,128)S(1)} %pad_maximum_fusion.3.refs_6_.refs_0_), channel_id=1, source_target_pairs={{0,2},{1,3},{2,0},{3,1},{4,6},{5,7},{6,4},{7,5},{8,10},{9,11},{10,... | collective-permute-start | bytes 245768 | tf_op jit(solution)/shard_map/ppermute | solution.py:319
  63.0 0.3 collective-permute-start.23
  63.3 3.4 %copy-done.1 = bf16[16,4,256,256]{3,2,1,0:T(8,128)(2,1)S(1)} copy-done((bf16[16,4,256,256]{3,2,1,0:T(8,128)(2,1)S(1)}, bf16[16,4,256,256]{3,2,1,0:T(8,128)(2,1)}, u32[]{:S(2)}) %copy-start.1) | copy-done | bytes 8388632
  66.6 3.4 %copy-done.3 = bf16[16,4,256,256]{3,2,1,0:T(8,128)(2,1)S(1)} copy-done((bf16[16,4,256,256]{3,2,1,0:T(8,128)(2,1)S(1)}, bf16[16,4,256,256]{3,2,1,0:T(8,128)(2,1)}, u32[]{:S(2)}) %copy-start.3) | copy-done | bytes 8388632
  70.0 1.9 %apply.4.refs_4_ = f32[8,32,256]{2,1,0:T(8,128)S(1)} custom-call(s32[2]{0:T(128)S(1)} %pad_add_fusion.place, s32[69]{0:T(128)S(1)} %get-tuple-element.40.refs_0_, bf16[16,4,256,256]{3,2,1,0:T(8,128)(2,1)S(1)} %copy-done.1, bf16[4,32,512]{2,1,0:T(8,128)(2,1)S(1)} %pad_maximum_fusion.1.refs_2_, bf16[16,4,256,256]{3,2,1,0:T(8,128)(2,1)S(1)} %copy-done.3), custom_call_target="tpu_custom_call" | custom-call | flops 268435456 | bytes 4194304 | tf_op jit(solution)/shard_map/apply/pallas_call | solution.py:462
  72.0 1.4 %copy-done.4 = bf16[16,4,256,256]{3,2,1,0:T(8,128)(2,1)S(1)} copy-done((bf16[16,4,256,256]{3,2,1,0:T(8,128)(2,1)S(1)}, bf16[16,4,256,256]{3,2,1,0:T(8,128)(2,1)}, u32[]{:S(2)}) %copy-start.4) | copy-done | bytes 8388632
  73.4 2.1 %apply.5 = (f32[32,512]{1,0:T(8,128)S(1)}, f32[32,512]{1,0:T(8,128)S(1)}, f32[2,32,512]{2,1,0:T(8,128)S(1)}, f32[32,128]{1,0:T(8,128)S(1)}) custom-call(s32[2]{0:T(128)S(1)} %pad_add_fusion.place, s32[69]{0:T(128)S(1)} %get-tuple-element.52.refs_1_.refs_0_, bf16[16,4,256,256]{3,2,1,0:T(8,128)(2,1)S(1)} %copy-done.4, ...), custom_call_target="tpu_custom_call" | custom-call | flops 268435456 | bytes 4194304 | tf_op jit(solution)/shard_map/apply/pallas_call | solution.py:462
  75.6 1.3 %collective-permute-start.24 = (f32[32,128]{1,0:T(8,128)S(1)}, f32[32,128]{1,0:T(8,128)S(1)}, u32[]{:S(2)}, u32[]{:S(2)}) collective-permute-start(f32[32,128]{1,0:T(8,128)S(1)} %get-tuple-element.69), channel_id=1, source_target_pairs={{0,4},{4,0},{8,12},{12,8},{16,20},{20,16},{24,28},{28,24},{1,5},{5... | collective-permute-start | bytes 49160 | tf_op jit(solution)/shard_map/ppermute | solution.py:319
  76.9 2.5 %collective-permute-done.24 = f32[32,128]{1,0:T(8,128)S(1)} collective-permute-done((f32[32,128]{1,0:T(8,128)S(1)}, f32[32,128]{1,0:T(8,128)S(1)}, u32[]{:S(2)}, u32[]{:S(2)}) %collective-permute-start.24) | collective-permute-done | bytes 16416 | tf_op jit(solution)/shard_map/ppermute | solution.py:319
  79.5 2.9 %collective-permute-start.28 = (f32[32,128]{1,0:T(8,128)S(1)}, f32[32,128]{1,0:T(8,128)S(1)}, u32[]{:S(2)}, u32[]{:S(2)}) collective-permute-start(f32[32,128]{1,0:T(8,128)S(1)} %add.83), channel_id=1, source_target_pairs={{0,16},{4,20},{8,24},{12,28},{16,0},{20,4},{24,8},{28,12},{1,17},{... | collective-permute-start | bytes 49160 | tf_op jit(solution)/shard_map/ppermute | solution.py:319
  82.4 1.5 %collective-permute-start.29 = (f32[32,128]{1,0:T(8,128)S(1)}, f32[32,128]{1,0:T(8,128)S(1)}, u32[]{:S(2)}, u32[]{:S(2)}) collective-permute-start(f32[32,128]{1,0:T(8,128)S(1)} %add.83), channel_id=1, source_target_pairs={{0,24},{4,28},{8,16},{12,20},{16,8},{20,12},{24,0},{28,4},{1,25},{... | collective-permute-start | bytes 49160 | tf_op jit(solution)/shard_map/ppermute | solution.py:319
  83.9 1.8 %collective-permute-start.26 = (f32[32,512]{1,0:T(8,128)S(1)}, f32[32,512]{1,0:T(8,128)S(1)}, u32[]{:S(2)}, u32[]{:S(2)}) collective-permute-start(f32[32,512]{1,0:T(8,128)S(1)} %get-tuple-element.74), channel_id=1, source_target_pairs={{0,2},{1,3},{2,0},{3,1},{4,6},{5,7},{6,4},{7,5},{8,10},{9,11},{10,... | collective-permute-start | bytes 196616 | tf_op jit(solution)/shard_map/ppermute | solution.py:319
  85.7 2.3 %collective-permute-done.29 = f32[32,128]{1,0:T(8,128)S(1)} collective-permute-done((f32[32,128]{1,0:T(8,128)S(1)}, f32[32,128]{1,0:T(8,128)S(1)}, u32[]{:S(2)}, u32[]{:S(2)}) %collective-permute-start.29) | collective-permute-done | bytes 16416 | tf_op jit(solution)/shard_map/ppermute | solution.py:319
  88.2 1.9 %collective-permute-start.31 = (f32[32,640]{1,0:T(8,128)S(1)}, f32[32,640]{1,0:T(8,128)S(1)}, u32[]{:S(2)}, u32[]{:S(2)}) collective-permute-start(f32[32,640]{1,0:T(8,128)S(1)} %pad_maximum_fusion.4.refs_4_), channel_id=1, source_target_pairs={{0,2},{1,3},{2,0},{3,1},{4,6},{5,7},{6,4},{7,5},{8,10},{9,11},{10,... | collective-permute-start | bytes 245768 | tf_op jit(solution)/shard_map/ppermute | solution.py:319
  90.2 3.0 %collective-permute-done.31.refs_6_ = f32[32,640]{1,0:T(8,128)S(1)} collective-permute-done((f32[32,640]{1,0:T(8,128)S(1)}, f32[32,640]{1,0:T(8,128)S(1)}, u32[]{:S(2)}, u32[]{:S(2)}) %collective-permute-start.31) | collective-permute-done | bytes 81952 | tf_op jit(solution)/shard_map/ppermute | solution.py:319
  93.2 1.4 %collective-permute-done.32.refs_7_ = f32[32,640]{1,0:T(8,128)S(1)} collective-permute-done((f32[32,640]{1,0:T(8,128)S(1)}, f32[32,640]{1,0:T(8,128)S(1)}, u32[]{:S(2)}, u32[]{:S(2)}) %collective-permute-start.32) | collective-permute-done | bytes 81952 | tf_op jit(solution)/shard_map/ppermute | solution.py:319
  94.6 2.1 %final.1 = (f32[32,2048]{1,0:T(8,128)}, f32[32,2048]{1,0:T(8,128)}) custom-call(s32[2]{0:T(128)} %copy-done.6, f32[32,2048]{1,0:T(8,128)} %t_ref.1, f32[40,512]{1,0:T(8,128)S(1)} %pad_maximum_fusion.3.refs_6_.refs_0_, f32[40,512]{1,0:T(8,128)S(1)} %collective-permute-done.21.refs_7_.refs_1_, f32[40,512]{1,0:T(8,128)S(1)} %collective-permute-done.22.refs_8_.refs_2_, ...), custom_call_target="tpu_custom_call" | custom-call | tf_op jit(solution)/shard_map/final/pallas_call | solution.py:509
  (70 shorter events, 2.1 us)
Async XLA Ops:
  0.6 5.6 %collective-permute-start.2 = (s32[8,6]{1,0:T(8,128)}, s32[8,6]{1,0:T(8,128)S(1)}, u32[]{:S(2)}, u32[]{:S(2)}) collective-permute-start(s32[8,6]{1,0:T(8,128)} %param.3), channel_id=1, source_target_pairs={{0,3},{1,2},{2,1},{3,0},{4,7},{5,6},{6,5},{7,4},{8,11},{9,10},{10,... | collective-permute-start | bytes 584 | tf_op jit(solution)/shard_map/ppermute | solution.py:319
  3.1 3.8 %collective-permute-start.1 = (s32[8,6]{1,0:T(8,128)}, s32[8,6]{1,0:T(8,128)S(1)}, u32[]{:S(2)}, u32[]{:S(2)}) collective-permute-start(s32[8,6]{1,0:T(8,128)} %param.3), channel_id=1, source_target_pairs={{0,2},{1,3},{2,0},{3,1},{4,6},{5,7},{6,4},{7,5},{8,10},{9,11},{10,... | collective-permute-start | bytes 584 | tf_op jit(solution)/shard_map/ppermute | solution.py:319
  3.7 3.3 %collective-permute-start = (s32[8,6]{1,0:T(8,128)}, s32[8,6]{1,0:T(8,128)S(1)}, u32[]{:S(2)}, u32[]{:S(2)}) collective-permute-start(s32[8,6]{1,0:T(8,128)} %param.3), channel_id=1, source_target_pairs={{0,1},{1,0},{2,3},{3,2},{4,5},{5,4},{6,7},{7,6},{8,9},{9,8},{10,11... | collective-permute-start | bytes 584 | tf_op jit(solution)/shard_map/ppermute | solution.py:319
  7.4 8.6 %collective-permute-start.3 = (bf16[16,640]{1,0:T(8,128)(2,1)S(1)}, bf16[16,640]{1,0:T(8,128)(2,1)S(1)}, u32[]{:S(2)}, u32[]{:S(2)}) collective-permute-start(bf16[16,640]{1,0:T(8,128)(2,1)S(1)} %pad_maximum_fusion.5), channel_id=1, source_target_pairs={{0,8},{4,12},{8,0},{12,4},{16,24},{20,28},{24,16},{28,20},{1,9},{5... | collective-permute-start | bytes 61448 | tf_op jit(solution)/shard_map/ppermute | solution.py:319
  9.0 7.2 %collective-permute-start.4 = (bf16[16,640]{1,0:T(8,128)(2,1)S(1)}, bf16[16,640]{1,0:T(8,128)(2,1)S(1)}, u32[]{:S(2)}, u32[]{:S(2)}) collective-permute-start(bf16[16,640]{1,0:T(8,128)(2,1)S(1)} %pad_maximum_fusion.5), channel_id=1, source_target_pairs={{0,16},{4,20},{8,24},{12,28},{16,0},{20,4},{24,8},{28,12},{1,17},{... | collective-permute-start | bytes 61448 | tf_op jit(solution)/shard_map/ppermute | solution.py:319
  11.6 5.7 %collective-permute-start.5 = (bf16[16,640]{1,0:T(8,128)(2,1)S(1)}, bf16[16,640]{1,0:T(8,128)(2,1)S(1)}, u32[]{:S(2)}, u32[]{:S(2)}) collective-permute-start(bf16[16,640]{1,0:T(8,128)(2,1)S(1)} %pad_maximum_fusion.5), channel_id=1, source_target_pairs={{0,24},{4,28},{8,16},{12,20},{16,8},{20,12},{24,0},{28,4},{1,25},{... | collective-permute-start | bytes 61448 | tf_op jit(solution)/shard_map/ppermute | solution.py:319
  11.8 12.8 %collective-permute-start.7 = (f32[32,512]{1,0:T(8,128)S(1)}, f32[32,512]{1,0:T(8,128)S(1)}, u32[]{:S(2)}, u32[]{:S(2)}) collective-permute-start(f32[32,512]{1,0:T(8,128)S(1)} %constant_dynamic-slice_fusion), channel_id=1, source_target_pairs={{0,8},{4,12},{8,0},{12,4},{16,24},{20,28},{24,16},{28,20},{1,9},{5... | collective-permute-start | bytes 196616 | tf_op jit(solution)/shard_map/ppermute | solution.py:319
  12.5 12.1 %collective-permute-start.8 = (f32[32,512]{1,0:T(8,128)S(1)}, f32[32,512]{1,0:T(8,128)S(1)}, u32[]{:S(2)}, u32[]{:S(2)}) collective-permute-start(f32[32,512]{1,0:T(8,128)S(1)} %constant_dynamic-slice_fusion), channel_id=1, source_target_pairs={{0,16},{4,20},{8,24},{12,28},{16,0},{20,4},{24,8},{28,12},{1,17},{... | collective-permute-start | bytes 196616 | tf_op jit(solution)/shard_map/ppermute | solution.py:319
  16.0 8.6 %collective-permute-start.9 = (f32[32,512]{1,0:T(8,128)S(1)}, f32[32,512]{1,0:T(8,128)S(1)}, u32[]{:S(2)}, u32[]{:S(2)}) collective-permute-start(f32[32,512]{1,0:T(8,128)S(1)} %constant_dynamic-slice_fusion), channel_id=1, source_target_pairs={{0,24},{4,28},{8,16},{12,20},{16,8},{20,12},{24,0},{28,4},{1,25},{... | collective-permute-start | bytes 196616 | tf_op jit(solution)/shard_map/ppermute | solution.py:319
  17.3 7.3 %collective-permute-start.6 = (bf16[4,16,640]{2,1,0:T(8,128)(2,1)S(1)}, bf16[4,16,640]{2,1,0:T(8,128)(2,1)S(1)}, u32[]{:S(2)}, u32[]{:S(2)}) collective-permute-start(bf16[4,16,640]{2,1,0:T(8,128)(2,1)S(1)} %pad_maximum_fusion.2.refs_1_), channel_id=1, source_target_pairs={{0,4},{4,0},{8,12},{12,8},{16,20},{20,16},{24,28},{28,24},{1,5},{5... | collective-permute-start | bytes 245768 | tf_op jit(solution)/shard_map/ppermute | solution.py:319
  18.9 53.0 %copy-start.6 = (s32[2]{0:T(128)}, s32[2]{0:T(128)S(1)}, u32[]{:S(2)}) copy-start(s32[2]{0:T(128)S(1)} %pad_add_fusion.place) | copy-start | bytes 28
  24.6 21.8 %copy-start = (bf16[16,4,256,256]{3,2,1,0:T(8,128)(2,1)}, bf16[16,4,256,256]{3,2,1,0:T(8,128)(2,1)S(1)}, u32[]{:S(2)}) copy-start(bf16[16,4,256,256]{3,2,1,0:T(8,128)(2,1)S(1)} %get-tuple-element.41.refs_2_.refs_1_.refs_3_) | copy-start | bytes 25165828
  24.7 6.7 %collective-permute-start.10 = (f32[4,32,512]{2,1,0:T(8,128)S(1)}, f32[4,32,512]{2,1,0:T(8,128)S(1)}, u32[]{:S(2)}, u32[]{:S(2)}) collective-permute-start(f32[4,32,512]{2,1,0:T(8,128)S(1)} %pad_maximum_fusion.refs_4_), channel_id=1, source_target_pairs={{0,4},{4,0},{8,12},{12,8},{16,20},{20,16},{24,28},{28,24},{1,5},{5... | collective-permute-start | bytes 786440 | tf_op jit(solution)/shard_map/ppermute | solution.py:319
  30.4 15.9 %copy-start.2 = (bf16[16,4,256,256]{3,2,1,0:T(8,128)(2,1)}, bf16[16,4,256,256]{3,2,1,0:T(8,128)(2,1)S(1)}, u32[]{:S(2)}) copy-start(bf16[16,4,256,256]{3,2,1,0:T(8,128)(2,1)S(1)} %get-tuple-element.53.refs_3_.refs_1_) | copy-start | bytes 25165828
  31.3 4.4 %collective-permute-start.11 = (f32[16,256]{1,0:T(8,128)S(1)}, f32[16,256]{1,0:T(8,128)S(1)}, u32[]{:S(2)}, u32[]{:S(2)}) collective-permute-start(f32[16,256]{1,0:T(8,128)S(1)} %get-tuple-element.57), channel_id=1, source_target_pairs={{0,8},{4,12},{8,0},{12,4},{16,24},{20,28},{24,16},{28,20},{1,9},{5... | collective-permute-start | bytes 49160 | tf_op jit(solution)/shard_map/ppermute | solution.py:319
  31.3 4.6 %collective-permute-start.12 = (f32[16,256]{1,0:T(8,128)S(1)}, f32[16,256]{1,0:T(8,128)S(1)}, u32[]{:S(2)}, u32[]{:S(2)}) collective-permute-start(f32[16,256]{1,0:T(8,128)S(1)} %get-tuple-element.57), channel_id=1, source_target_pairs={{0,16},{4,20},{8,24},{12,28},{16,0},{20,4},{24,8},{28,12},{1,17},{... | collective-permute-start | bytes 49160 | tf_op jit(solution)/shard_map/ppermute | solution.py:319
  33.6 5.5 %collective-permute-start.13 = (f32[16,256]{1,0:T(8,128)S(1)}, f32[16,256]{1,0:T(8,128)S(1)}, u32[]{:S(2)}, u32[]{:S(2)}) collective-permute-start(f32[16,256]{1,0:T(8,128)S(1)} %get-tuple-element.57), channel_id=1, source_target_pairs={{0,24},{4,28},{8,16},{12,20},{16,8},{20,12},{24,0},{28,4},{1,25},{... | collective-permute-start | bytes 49160 | tf_op jit(solution)/shard_map/ppermute | solution.py:319
  39.2 3.8 %collective-permute-start.14 = (f32[16,256]{1,0:T(8,128)S(1)}, f32[16,256]{1,0:T(8,128)S(1)}, u32[]{:S(2)}, u32[]{:S(2)}) collective-permute-start(f32[16,256]{1,0:T(8,128)S(1)} %add_add_fusion.1), channel_id=1, source_target_pairs={{0,4},{4,0},{8,12},{12,8},{16,20},{20,16},{24,28},{28,24},{1,5},{5... | collective-permute-start | bytes 49160 | tf_op jit(solution)/shard_map/ppermute | solution.py:319
  43.0 9.3 %copy-start.5 = (f32[32,2048]{1,0:T(8,128)S(1)}, f32[32,2048]{1,0:T(8,128)}, u32[]{:S(2)}) copy-start(f32[32,2048]{1,0:T(8,128)} %t_ref.1) | copy-start | bytes 786436
  46.4 1.4 %collective-permute-start.15 = (f32[2,32,512]{2,1,0:T(8,128)S(1)}, f32[2,32,512]{2,1,0:T(8,128)S(1)}, u32[]{:S(2)}, u32[]{:S(2)}) collective-permute-start(f32[2,32,512]{2,1,0:T(8,128)S(1)} %get-tuple-element.59), channel_id=1, source_target_pairs={{0,1},{1,0},{2,3},{3,2},{4,5},{5,4},{6,7},{7,6},{8,9},{9,8},{10,11... | collective-permute-start | bytes 393224 | tf_op jit(solution)/shard_map/ppermute | solution.py:319
  47.8 4.5 %collective-permute-start.16 = (f32[32,512]{1,0:T(8,128)S(1)}, f32[32,512]{1,0:T(8,128)S(1)}, u32[]{:S(2)}, u32[]{:S(2)}) collective-permute-start(f32[32,512]{1,0:T(8,128)S(1)} %fusion.2), channel_id=1, source_target_pairs={{0,2},{1,3},{2,0},{3,1},{4,6},{5,7},{6,4},{7,5},{8,10},{9,11},{10,... | collective-permute-start | bytes 196616 | tf_op jit(solution)/shard_map/ppermute | solution.py:319
  52.3 4.5 %collective-permute-start.17 = (bf16[32,512]{1,0:T(8,128)(2,1)S(1)}, bf16[32,512]{1,0:T(8,128)(2,1)S(1)}, u32[]{:S(2)}, u32[]{:S(2)}) collective-permute-start(bf16[32,512]{1,0:T(8,128)(2,1)S(1)} %get-tuple-element.76), channel_id=1, source_target_pairs={{0,8},{4,12},{8,0},{12,4},{16,24},{20,28},{24,16},{28,20},{1,9},{5... | collective-permute-start | bytes 98312 | tf_op jit(solution)/shard_map/ppermute | solution.py:319
  52.4 5.0 %collective-permute-start.18 = (bf16[32,512]{1,0:T(8,128)(2,1)S(1)}, bf16[32,512]{1,0:T(8,128)(2,1)S(1)}, u32[]{:S(2)}, u32[]{:S(2)}) collective-permute-start(bf16[32,512]{1,0:T(8,128)(2,1)S(1)} %get-tuple-element.76), channel_id=1, source_target_pairs={{0,16},{4,20},{8,24},{12,28},{16,0},{20,4},{24,8},{28,12},{1,17},{... | collective-permute-start | bytes 98312 | tf_op jit(solution)/shard_map/ppermute | solution.py:319
  54.6 5.7 %collective-permute-start.19 = (bf16[32,512]{1,0:T(8,128)(2,1)S(1)}, bf16[32,512]{1,0:T(8,128)(2,1)S(1)}, u32[]{:S(2)}, u32[]{:S(2)}) collective-permute-start(bf16[32,512]{1,0:T(8,128)(2,1)S(1)} %get-tuple-element.76), channel_id=1, source_target_pairs={{0,24},{4,28},{8,16},{12,20},{16,8},{20,12},{24,0},{28,4},{1,25},{... | collective-permute-start | bytes 98312 | tf_op jit(solution)/shard_map/ppermute | solution.py:319
  60.4 11.6 %collective-permute-start.20 = (bf16[4,32,512]{2,1,0:T(8,128)(2,1)S(1)}, bf16[4,32,512]{2,1,0:T(8,128)(2,1)S(1)}, u32[]{:S(2)}, u32[]{:S(2)}) collective-permute-start(bf16[4,32,512]{2,1,0:T(8,128)(2,1)S(1)} %pad_maximum_fusion.1.refs_2_), channel_id=1, source_target_pairs={{0,4},{4,0},{8,12},{12,8},{16,20},{20,16},{24,28},{28,24},{1,5},{5... | collective-permute-start | bytes 393224 | tf_op jit(solution)/shard_map/ppermute | solution.py:319
  61.4 10.6 %collective-permute-start.21 = (f32[40,512]{1,0:T(8,128)S(1)}, f32[40,512]{1,0:T(8,128)S(1)}, u32[]{:S(2)}, u32[]{:S(2)}) collective-permute-start(f32[40,512]{1,0:T(8,128)S(1)} %pad_maximum_fusion.3.refs_6_.refs_0_), channel_id=1, source_target_pairs={{0,1},{1,0},{2,3},{3,2},{4,5},{5,4},{6,7},{7,6},{8,9},{9,8},{10,11... | collective-permute-start | bytes 245768 | tf_op jit(solution)/shard_map/ppermute | solution.py:319
  61.4 10.6 %collective-permute-start.22 = (f32[40,512]{1,0:T(8,128)S(1)}, f32[40,512]{1,0:T(8,128)S(1)}, u32[]{:S(2)}, u32[]{:S(2)}) collective-permute-start(f32[40,512]{1,0:T(8,128)S(1)} %pad_maximum_fusion.3.refs_6_.refs_0_), channel_id=1, source_target_pairs={{0,2},{1,3},{2,0},{3,1},{4,6},{5,7},{6,4},{7,5},{8,10},{9,11},{10,... | collective-permute-start | bytes 245768 | tf_op jit(solution)/shard_map/ppermute | solution.py:319
  63.0 9.0 %collective-permute-start.23 = (f32[40,512]{1,0:T(8,128)S(1)}, f32[40,512]{1,0:T(8,128)S(1)}, u32[]{:S(2)}, u32[]{:S(2)}) collective-permute-start(f32[40,512]{1,0:T(8,128)S(1)} %pad_maximum_fusion.3.refs_6_.refs_0_), channel_id=1, source_target_pairs={{0,3},{1,2},{2,1},{3,0},{4,7},{5,6},{6,5},{7,4},{8,11},{9,10},{10,... | collective-permute-start | bytes 245768 | tf_op jit(solution)/shard_map/ppermute | solution.py:319
  63.2 3.4 %copy-start.1 = (bf16[16,4,256,256]{3,2,1,0:T(8,128)(2,1)S(1)}, bf16[16,4,256,256]{3,2,1,0:T(8,128)(2,1)}, u32[]{:S(2)}) copy-start(bf16[16,4,256,256]{3,2,1,0:T(8,128)(2,1)} %copy-done) | copy-start | bytes 25165828
  66.6 3.4 %copy-start.3 = (bf16[16,4,256,256]{3,2,1,0:T(8,128)(2,1)S(1)}, bf16[16,4,256,256]{3,2,1,0:T(8,128)(2,1)}, u32[]{:S(2)}) copy-start(bf16[16,4,256,256]{3,2,1,0:T(8,128)(2,1)} %copy-done.2) | copy-start | bytes 25165828
  70.0 3.4 %copy-start.4 = (bf16[16,4,256,256]{3,2,1,0:T(8,128)(2,1)S(1)}, bf16[16,4,256,256]{3,2,1,0:T(8,128)(2,1)}, u32[]{:S(2)}) copy-start(bf16[16,4,256,256]{3,2,1,0:T(8,128)(2,1)} %copy-done.2) | copy-start | bytes 25165828
  75.5 3.9 %collective-permute-start.25 = (f32[2,32,512]{2,1,0:T(8,128)S(1)}, f32[2,32,512]{2,1,0:T(8,128)S(1)}, u32[]{:S(2)}, u32[]{:S(2)}) collective-permute-start(f32[2,32,512]{2,1,0:T(8,128)S(1)} %get-tuple-element.71), channel_id=1, source_target_pairs={{0,1},{1,0},{2,3},{3,2},{4,5},{5,4},{6,7},{7,6},{8,9},{9,8},{10,11... | collective-permute-start | bytes 393224 | tf_op jit(solution)/shard_map/ppermute | solution.py:319
  75.6 3.8 %collective-permute-start.24 = (f32[32,128]{1,0:T(8,128)S(1)}, f32[32,128]{1,0:T(8,128)S(1)}, u32[]{:S(2)}, u32[]{:S(2)}) collective-permute-start(f32[32,128]{1,0:T(8,128)S(1)} %get-tuple-element.69), channel_id=1, source_target_pairs={{0,4},{4,0},{8,12},{12,8},{16,20},{20,16},{24,28},{28,24},{1,5},{5... | collective-permute-start | bytes 49160 | tf_op jit(solution)/shard_map/ppermute | solution.py:319
  79.4 6.3 %collective-permute-start.27 = (f32[32,128]{1,0:T(8,128)S(1)}, f32[32,128]{1,0:T(8,128)S(1)}, u32[]{:S(2)}, u32[]{:S(2)}) collective-permute-start(f32[32,128]{1,0:T(8,128)S(1)} %add.83), channel_id=1, source_target_pairs={{0,8},{4,12},{8,0},{12,4},{16,24},{20,28},{24,16},{28,20},{1,9},{5... | collective-permute-start | bytes 49160 | tf_op jit(solution)/shard_map/ppermute | solution.py:319
  79.5 6.2 %collective-permute-start.28 = (f32[32,128]{1,0:T(8,128)S(1)}, f32[32,128]{1,0:T(8,128)S(1)}, u32[]{:S(2)}, u32[]{:S(2)}) collective-permute-start(f32[32,128]{1,0:T(8,128)S(1)} %add.83), channel_id=1, source_target_pairs={{0,16},{4,20},{8,24},{12,28},{16,0},{20,4},{24,8},{28,12},{1,17},{... | collective-permute-start | bytes 49160 | tf_op jit(solution)/shard_map/ppermute | solution.py:319
  82.4 5.5 %collective-permute-start.29 = (f32[32,128]{1,0:T(8,128)S(1)}, f32[32,128]{1,0:T(8,128)S(1)}, u32[]{:S(2)}, u32[]{:S(2)}) collective-permute-start(f32[32,128]{1,0:T(8,128)S(1)} %add.83), channel_id=1, source_target_pairs={{0,24},{4,28},{8,16},{12,20},{16,8},{20,12},{24,0},{28,4},{1,25},{... | collective-permute-start | bytes 49160 | tf_op jit(solution)/shard_map/ppermute | solution.py:319
  83.9 4.3 %collective-permute-start.26 = (f32[32,512]{1,0:T(8,128)S(1)}, f32[32,512]{1,0:T(8,128)S(1)}, u32[]{:S(2)}, u32[]{:S(2)}) collective-permute-start(f32[32,512]{1,0:T(8,128)S(1)} %get-tuple-element.74), channel_id=1, source_target_pairs={{0,2},{1,3},{2,0},{3,1},{4,6},{5,7},{6,4},{7,5},{8,10},{9,11},{10,... | collective-permute-start | bytes 196616 | tf_op jit(solution)/shard_map/ppermute | solution.py:319
  88.2 2.0 %collective-permute-start.30 = (f32[32,640]{1,0:T(8,128)S(1)}, f32[32,640]{1,0:T(8,128)S(1)}, u32[]{:S(2)}, u32[]{:S(2)}) collective-permute-start(f32[32,640]{1,0:T(8,128)S(1)} %pad_maximum_fusion.4.refs_4_), channel_id=1, source_target_pairs={{0,1},{1,0},{2,3},{3,2},{4,5},{5,4},{6,7},{7,6},{8,9},{9,8},{10,11... | collective-permute-start | bytes 245768 | tf_op jit(solution)/shard_map/ppermute | solution.py:319
  88.2 4.9 %collective-permute-start.31 = (f32[32,640]{1,0:T(8,128)S(1)}, f32[32,640]{1,0:T(8,128)S(1)}, u32[]{:S(2)}, u32[]{:S(2)}) collective-permute-start(f32[32,640]{1,0:T(8,128)S(1)} %pad_maximum_fusion.4.refs_4_), channel_id=1, source_target_pairs={{0,2},{1,3},{2,0},{3,1},{4,6},{5,7},{6,4},{7,5},{8,10},{9,11},{10,... | collective-permute-start | bytes 245768 | tf_op jit(solution)/shard_map/ppermute | solution.py:319
  90.1 4.5 %collective-permute-start.32 = (f32[32,640]{1,0:T(8,128)S(1)}, f32[32,640]{1,0:T(8,128)S(1)}, u32[]{:S(2)}, u32[]{:S(2)}) collective-permute-start(f32[32,640]{1,0:T(8,128)S(1)} %pad_maximum_fusion.4.refs_4_), channel_id=1, source_target_pairs={{0,3},{1,2},{2,1},{3,0},{4,7},{5,6},{6,5},{7,4},{8,11},{9,10},{10,... | collective-permute-start | bytes 245768 | tf_op jit(solution)/shard_map/ppermute | solution.py:319

commit v4 on v3

--- a/solution.py
+++ b/solution.py
@@ -20,6 +20,7 @@
 TINY = 1e-30
 SHIFT = 0.375
 DIRECT_ROWS = 8
+ROOM_GROUPS = 8
 RESIDENT_BYTES = 20 * 1024 * 1024
 
 SMEM = pl.BlockSpec(memory_space=pltpu.SMEM)
@@ -37,6 +38,7 @@
 
 class Sizes(NamedTuple):
     parts: int
+    part_groups: int
     resident: bool
     nb: int
     block_len: int
@@ -81,9 +83,9 @@
         near_copy = pltpu.make_async_copy(near_hbm, near_ref, near_sem)
         near_copy.start()
     else:
-        lhs, first_deg, piece = refs[:3]
-        k_mat, listed, deg_ref = refs[3:6]
-        refs = refs[6:]
+        lhs, first_deg, piece, _ = refs[:4]
+        k_mat, listed, deg_ref = refs[4:7]
+        refs = refs[7:]
     mlist, acc, rhs, counts_v, counts, count_sem = refs[:6]
     kbuf, sems = (None, None) if cfg.resident else refs[6:]
     row, col = place[0], place[1]
@@ -140,8 +142,10 @@
         slot = lax.rem(g, RING)
         return pltpu.make_async_copy(kbuf.at[slot], k_mat.at[g], sems.at[slot])
 
+    base = part * cfg.part_groups
+
     def step(g, carry):
-        slot, target = (g, k_mat) if cfg.resident else (lax.rem(g, RING), kbuf)
+        slot, target = (base + g, k_mat) if cfg.resident else (lax.rem(g, RING), kbuf)
         if not cfg.resident:
 
             @pl.when(g >= RING)
@@ -190,9 +194,9 @@
         lax.fori_loop(jnp.maximum(total - RING, 0), total, drain, 0)
 
 
-def apply_kernel(cfg, parts, scaled, carried, finish, extra_k, place, *refs):
+def apply_kernel(cfg, parts, scaled, carried, finish, place, k_mat, *refs):
     n = len(parts)
-    lists, ks, pieces, refs = refs[:n], refs[n:2 * n], refs[2 * n:3 * n], refs[3 * n + extra_k:]
+    lists, pieces, refs = refs[:n], refs[n:2 * n], refs[2 * n:]
     if scaled:
         inv_ref, refs = refs[0], refs[1:]
     if carried:
@@ -213,11 +217,12 @@
     own_rows, block_len = cfg.own_rows, cfg.block_len
 
     z_acc[...] = z_in[...] if carried else jnp.zeros_like(z_acc)
-    for part, listed, k_mat, piece in zip(parts, lists, ks, pieces):
+    for part, listed, piece in zip(parts, lists, pieces):
         total = listed[0]
+        base = part * cfg.part_groups
         held = piece.shape[0]
 
-        def copy_in(g, k_mat=k_mat):
+        def copy_in(g):
             slot = lax.rem(g, RING)
             return pltpu.make_async_copy(k_mat.at[g], kbuf.at[slot], sems.at[slot])
 
@@ -240,8 +245,8 @@
 
         lax.fori_loop(0, held, prepare, 0, unroll=held <= 4)
 
-        def step(g, carry, total=total, listed=listed, k_mat=k_mat, copy_in=copy_in):
-            slot, source = (g, k_mat) if cfg.resident else (lax.rem(g, RING), kbuf)
+        def step(g, carry, total=total, listed=listed, base=base, copy_in=copy_in):
+            slot, source = (base + g, k_mat) if cfg.resident else (lax.rem(g, RING), kbuf)
             if not cfg.resident:
 
                 @pl.when(g + (RING - 1) < total)
@@ -294,6 +299,15 @@
         dot_ref[...] = out
 
 
+def first_kernel(near, far, inv_ref, t_ref, k_mat, s_ref, g_ref):
+    outputs = t_ref.shape[0]
+    inv = inv_ref[...]
+    s = (near[...] + far[...]) * inv
+    s_ref[:outputs, :] = s
+    s_ref[outputs:, :] = jnp.broadcast_to(inv, (8, inv.shape[1]))
+    g_ref[...] = ((s - SHIFT * t_ref[...]) * inv).astype(BF16)
+
+
 def final_kernel(n_cols, place, t_ref, *refs):
     s1s, s2s = refs[:4], refs[4:8]
     sol_ref, res_ref = refs[8:]
@@ -361,8 +375,9 @@
     n_groups = -(-bound // GROUP)
     list_len = n_groups * GROUP + GROUP + 1
     place = jnp.stack([row, col])
-    k_shape = (n_groups, GROUP, block_len, block_len)
     resident = parts * 2 * n_groups * GROUP * block_len * block_len <= RESIDENT_BYTES
+    room = ROOM_GROUPS if resident else 0
+    k_shape = (parts * n_groups + room, GROUP, block_len, block_len)
     limit = pltpu.CompilerParams(vmem_limit_bytes=(8 if resident else 32) * 1024 * 1024)
     ring = [] if resident else [
         pltpu.VMEM((RING, GROUP, block_len, block_len), BF16),
@@ -370,7 +385,7 @@
     ]
     k_spec = VMEM if resident else HBM
     cfg = Sizes(
-        parts, resident, nb, block_len, own_rows, block_rows, -(-own_rows * nb // LANES)
+        parts, n_groups, resident, nb, block_len, own_rows, block_rows, -(-own_rows * nb // LANES)
     )
 
     def shape(*dims, dtype=F32):
@@ -404,7 +419,7 @@
         k_mat, *rest = pl.pallas_call(
             functools.partial(build_kernel, cfg, part),
             out_shape=out,
-            in_specs=[SMEM, SMEM] + ([HBM, VMEM] if first else [VMEM] * 3),
+            in_specs=[SMEM, SMEM] + ([HBM, VMEM] if first else [VMEM] * 3 + [k_spec]),
             out_specs=[k_spec, SMEM] + [VMEM] * (len(out) - 2),
             scratch_shapes=([
                 pltpu.VMEM((dim, npoints), BF16),
@@ -419,6 +434,7 @@
                 *ring,
             ],
             compiler_params=limit,
+            input_output_aliases={} if first else {5: 0},
             cost_estimate=pl.CostEstimate(
                 flops=2 * 2 * dim * bound * block_len * block_len,
                 bytes_accessed=2 * bound * block_len * block_len,
@@ -435,23 +451,22 @@
         packed, early_t = lax.optimization_barrier((packed, own_t))
         same, other = across_x(jnp.stack(along_z(packed)))
         t_same = along_z(early_t)
-        k0, list0, degree, lhs = build(0, near, same)
+        k_mat, list0, degree, lhs = build(0, near, same)
         degree, other, *t_same = lax.optimization_barrier((degree, other, *t_same))
         t_same, t_other = across_x(jnp.stack(t_same))
         other, t_same = lax.optimization_barrier((other, t_same))
-        k1, list1, degree = build(1, lhs, degree, other)
+        k_mat, list1, degree = build(1, lhs, degree, other, k_mat)
         degree, t_other = lax.optimization_barrier((degree, t_other))
-        t_pieces, k_mats, k_lists = [t_same, t_other], [k0, k1], [list0, list1]
+        t_pieces, k_lists = [t_same, t_other], [list0, list1]
     else:
-        k0, list0, degree, _ = build(0, near, lax.all_gather(packed, "rows"))
-        t_pieces, k_mats, k_lists = [lax.all_gather(own_t, "rows")], [k0], [list0]
+        k_mat, list0, degree, _ = build(0, near, lax.all_gather(packed, "rows"))
+        t_pieces, k_lists = [lax.all_gather(own_t, "rows")], [list0]
     inv = 1.0 / jnp.sqrt(1.0 + total_rows(degree))
     own_inv = lax.dynamic_slice_in_dim(inv, row * own_rows, own_rows, 0).reshape(1, own_len)
 
     def apply(use, pieces, finish=True, inv=None, z_in=None, products=()):
-        spare = [k for p, k in enumerate(k_mats) if p not in use]
-        operands = [k_lists[p] for p in use] + [k_mats[p] for p in use] + pieces + spare
-        specs = [SMEM] * len(use) + [k_spec] * len(use) + [VMEM] * len(pieces) + [k_spec] * len(spare)
+        operands = [k_mat] + [k_lists[p] for p in use] + pieces
+        specs = [k_spec] + [SMEM] * len(use) + [VMEM] * len(pieces)
         more = [x for x in (inv, z_in) if x is not None] + list(products)
         z_shape = (block_rows, outputs, block_len)
         if finish:
@@ -461,7 +476,7 @@
             out = [shape(*z_shape)]
         return pl.pallas_call(
             functools.partial(
-                apply_kernel, cfg, use, inv is not None, z_in is not None, finish, len(spare)
+                apply_kernel, cfg, use, inv is not None, z_in is not None, finish
             ),
             out_shape=out,
             in_specs=[SMEM] + specs + [VMEM] * len(more),
@@ -479,9 +494,16 @@
             name="apply",
         )(place, *operands, *more)
 
-    s1 = shared(*half_shared(*apply(tuple(range(parts)), t_pieces, inv=inv))) * own_inv
-    g = ((s1 - SHIFT * own_t) * own_inv).astype(BF16)
-    s1_packed = jnp.concatenate([s1, jnp.broadcast_to(own_inv, (8, own_len))], axis=0)
+    z1, z1_y = half_shared(*apply(tuple(range(parts)), t_pieces, inv=inv))
+    s1_packed, g = pl.pallas_call(
+        first_kernel,
+        out_shape=(shape(outputs + 8, own_len), shape(outputs, own_len, dtype=BF16)),
+        in_specs=[VMEM] * 4 + [k_spec],
+        out_specs=(VMEM, VMEM),
+        compiler_params=limit,
+        name="first",
+    )(z1, swap(z1_y, "cols", 2), own_inv, own_t, k_mat)
+    s1 = s1_packed[:outputs]
     if direct_rows:
         g_same = jnp.stack(along_z(g))
         g_same, s1_packed = lax.optimization_barrier((g_same, s1_packed))
@@ -490,11 +512,9 @@
         (z_part,) = apply((0,), [g_same], finish=False)
         z_part, g_other, *s1_all = lax.optimization_barrier((z_part, g_other, *s1_all))
         *z2, dots = apply((1,), [g_other], z_in=z_part, products=[targets, *s1_all])
-        z2 = half_shared(*z2)
+        dots = pair_sum(along_z(dots))
+        s2 = shared(*half_shared(*z2))
         dots = pair_sum(across_x(dots))
-        dots, *z2 = lax.optimization_barrier((dots, *z2))
-        s2 = shared(*z2)
-        dots = pair_sum(along_z(dots))
     else:
         s1_all = direct_cols(s1_packed)
         *z2, dots = apply((0,), [lax.all_gather(g, "rows")], products=[targets, *s1_all])

time: 96.9 us -> 100 us (1.032)
  local copies, waits for them, and re-layouts: 10.9 us -> 16.7 us
  starting transfers between devices: 38.8 us -> 34.1 us
  waiting for transfers between devices: 25.2 us -> 28 us
    unnamed x17 -> x14, local copies, waits for them, and re-layouts: 8.99 us -> 14.8 us
    ppermute x33, starting transfers between devices: 38.8 us -> 34.1 us  [swap(): return lax.ppermute(x, axis, [(i, i ^ d) for i in range(size)])]
    ppermute x33, waiting for transfers between devices: 25.2 us -> 28 us  [swap(): return lax.ppermute(x, axis, [(i, i ^ d) for i in range(size)])]
  transfers between devices with their start and end apart: 33 -> 33, of which waited for: 15 -> 17; matrix products, arithmetic and copies ran while one was open for 3% -> 3% of each run, Pallas kernels for 13% -> 13%
where the time goes in v4:
time: 100 us
  starting transfers between devices  34.1 us (34%)
  waiting for transfers between devices  28 us (28%)
  Pallas kernels  20.2 us (20%)
  local copies, waits for them, and re-layouts  16.7 us (17%)
    ppermute x33, starting transfers between devices, swap(): return lax.ppermute(x, axis, [(i, i ^ d) for i in range(size)])  34.1 us
    ppermute x33, waiting for transfers between devices, swap(): return lax.ppermute(x, axis, [(i, i ^ d) for i in range(size)])  28 us
    unnamed x14, local copies, waits for them, and re-layouts  14.8 us
    pallas_call x2, Pallas kernels, build(): pl.pallas_call(functools.partial(build_kernel, cfg, part), out_shape=out,...  10.8 us
    pallas_call x3, Pallas kernels, apply(): pl.pallas_call(functools.partial(apply_kernel, cfg, use, inv is not None,...  7.33 us
    pallas_call x1, Pallas kernels, local(): pl.pallas_call(functools.partial(final_kernel, n_cols), out_shape=(shape(...  2.09 us
  transfers between devices with their start and end apart: 33, of which 17 were waited for; matrix products, arithmetic and copies ran while one was open for 3% of the time, Pallas kernels for 13%

profile of v4, /device:TPU:0, one launch (start us, length us, event | category | flops | bytes accessed | tf_op | source)
XLA Modules:
  0.0 100.4 jit_solution(2686569324443728723)
XLA Ops:
  0.6 0.5 collective-permute-start
  1.1 2.6 %collective-permute-start.2 = (s32[8,6]{1,0:T(8,128)}, s32[8,6]{1,0:T(8,128)S(1)}, u32[]{:S(2)}, u32[]{:S(2)}) collective-permute-start(s32[8,6]{1,0:T(8,128)} %param.3), channel_id=1, source_target_pairs={{0,3},{1,2},{2,1},{3,0},{4,7},{5,6},{6,5},{7,4},{8,11},{9,10},{10,... | collective-permute-start | bytes 584 | tf_op jit(solution)/shard_map/ppermute | solution.py:333
  3.8 0.8 copy.6
  4.7 0.7 constant_dynamic-slice_fusion.1
  5.5 0.8 constant_dynamic-slice_fusion.t_ref
  6.6 1.0 collective-permute-done.1
  7.9 3.7 %collective-permute-start.5 = (bf16[16,640]{1,0:T(8,128)(2,1)S(1)}, bf16[16,640]{1,0:T(8,128)(2,1)S(1)}, u32[]{:S(2)}, u32[]{:S(2)}) collective-permute-start(bf16[16,640]{1,0:T(8,128)(2,1)S(1)} %pad_maximum_fusion.4), channel_id=1, source_target_pairs={{0,24},{4,28},{8,16},{12,20},{16,8},{20,12},{24,0},{28,4},{1,25},{... | collective-permute-start | bytes 61448 | tf_op jit(solution)/shard_map/ppermute | solution.py:333
  11.6 0.8 collective-permute-start.3
  12.3 3.6 %collective-permute-start.9 = (f32[32,512]{1,0:T(8,128)S(1)}, f32[32,512]{1,0:T(8,128)S(1)}, u32[]{:S(2)}, u32[]{:S(2)}) collective-permute-start(f32[32,512]{1,0:T(8,128)S(1)} %constant_dynamic-slice_fusion.t_ref), channel_id=1, source_target_pairs={{0,24},{4,28},{8,16},{12,20},{16,8},{20,12},{24,0},{28,4},{1,25},{... | collective-permute-start | bytes 196616 | tf_op jit(solution)/shard_map/ppermute | solution.py:333
  15.9 0.8 collective-permute-start.7
  16.8 1.6 %collective-permute-start.6 = (bf16[4,16,640]{2,1,0:T(8,128)(2,1)S(1)}, bf16[4,16,640]{2,1,0:T(8,128)(2,1)S(1)}, u32[]{:S(2)}, u32[]{:S(2)}) collective-permute-start(bf16[4,16,640]{2,1,0:T(8,128)(2,1)S(1)} %pad_maximum_fusion.2.refs_1_), channel_id=1, source_target_pairs={{0,4},{4,0},{8,12},{12,8},{16,20},{20,16},{24,28},{28,24},{1,5},{5... | collective-permute-start | bytes 245768 | tf_op jit(solution)/shard_map/ppermute | solution.py:333
  18.4 5.6 %build.2 = (bf16[40,4,256,256]{3,2,1,0:T(8,128)(2,1)S(1)}, s32[69]{0:T(128)S(1)}, f32[8,256]{1,0:T(8,128)S(1)}, bf16[8,256,32]{2,1,0:T(8,128)(2,1)S(1)}) custom-call(s32[2]{0:T(128)S(1)} %pad_add_fusion.place, s32[8,64]{1,0:T(8,128)S(1)} %add_add_fusion.2.direct, bf16[16,2048]{1,0:T(8,128)(2,1)} %refs_0_.1, bf16[4,16,640]{2,1,0:T(8,128)(2,1)S(1)} %pad_maximum_fusion.2.refs_1_), custom_call_target="tpu_custom_call" | custom-call | flops 268435456 | bytes 8388608 | tf_op jit(solution)/shard_map/build/pallas_call | solution.py:419
  24.1 0.6 collective-permute-start.10
  24.7 5.2 %build.3 = (bf16[40,4,256,256]{3,2,1,0:T(8,128)(2,1)S(1)}, s32[69]{0:T(128)S(1)}, f32[16,256]{1,0:T(8,128)S(1)}) custom-call(s32[2]{0:T(128)S(1)} %pad_add_fusion.place, s32[8,64]{1,0:T(8,128)S(1)} %add_add_fusion.2.direct, bf16[8,256,32]{2,1,0:T(8,128)(2,1)S(1)} %get-tuple-element.39.refs_0_, ...), custom_call_target="tpu_custom_call", output_to_operand_aliasing={{0}: (5, {})} | custom-call | flops 268435456 | bytes 8388608 | tf_op jit(solution)/shard_map/build/pallas_call | solution.py:419
  29.9 0.6 collective-permute-done.10.refs_3_
  30.5 4.2 %collective-permute-start.13 = (f32[16,256]{1,0:T(8,128)S(1)}, f32[16,256]{1,0:T(8,128)S(1)}, u32[]{:S(2)}, u32[]{:S(2)}) collective-permute-start(f32[16,256]{1,0:T(8,128)S(1)} %get-tuple-element.56), channel_id=1, source_target_pairs={{0,24},{4,28},{8,16},{12,20},{16,8},{20,12},{24,0},{28,4},{1,25},{... | collective-permute-start | bytes 49160 | tf_op jit(solution)/shard_map/ppermute | solution.py:333
  34.7 0.6 collective-permute-start.11
  35.3 1.1 %collective-permute-done.13 = f32[16,256]{1,0:T(8,128)S(1)} collective-permute-done((f32[16,256]{1,0:T(8,128)S(1)}, f32[16,256]{1,0:T(8,128)S(1)}, u32[]{:S(2)}, u32[]{:S(2)}) %collective-permute-start.13) | collective-permute-done | bytes 16416 | tf_op jit(solution)/shard_map/ppermute | solution.py:333
  36.4 2.9 %collective-permute-done.12 = f32[16,256]{1,0:T(8,128)S(1)} collective-permute-done((f32[16,256]{1,0:T(8,128)S(1)}, f32[16,256]{1,0:T(8,128)S(1)}, u32[]{:S(2)}, u32[]{:S(2)}) %collective-permute-start.12) | collective-permute-done | bytes 16416 | tf_op jit(solution)/shard_map/ppermute | solution.py:333
  39.8 3.4 %collective-permute-done.14 = f32[16,256]{1,0:T(8,128)S(1)} collective-permute-done((f32[16,256]{1,0:T(8,128)S(1)}, f32[16,256]{1,0:T(8,128)S(1)}, u32[]{:S(2)}, u32[]{:S(2)}) %collective-permute-start.14) | collective-permute-done | bytes 16416 | tf_op jit(solution)/shard_map/ppermute | solution.py:333
  43.2 3.3 %apply.3 = (f32[32,512]{1,0:T(8,128)S(1)}, f32[32,512]{1,0:T(8,128)S(1)}, f32[2,32,512]{2,1,0:T(8,128)S(1)}) custom-call(s32[2]{0:T(128)S(1)} %pad_add_fusion.place, bf16[40,4,256,256]{3,2,1,0:T(8,128)(2,1)S(1)} %get-tuple-element.50.k_mat, s32[69]{0:T(128)S(1)} %get-tuple-element.51.refs_0_, s32[69]{0:T(128)S(1)} %get-tuple-element.52.refs_1_.refs_0_, ...), custom_call_target="tpu_custom_call" | custom-call | flops 536870912 | bytes 8388608 | tf_op jit(solution)/shard_map/apply/pallas_call | solution.py:477
  46.5 7.0 %copy-done = bf16[40,4,256,256]{3,2,1,0:T(8,128)(2,1)} copy-done((bf16[40,4,256,256]{3,2,1,0:T(8,128)(2,1)}, bf16[40,4,256,256]{3,2,1,0:T(8,128)(2,1)S(1)}, u32[]{:S(2)}) %copy-start) | copy-done | bytes 20971544
  53.5 1.3 %collective-permute-done.15 = f32[2,32,512]{2,1,0:T(8,128)S(1)} collective-permute-done((f32[2,32,512]{2,1,0:T(8,128)S(1)}, f32[2,32,512]{2,1,0:T(8,128)S(1)}, u32[]{:S(2)}, u32[]{:S(2)}) %collective-permute-start.15) | collective-permute-done | bytes 131104 | tf_op jit(solution)/shard_map/ppermute | solution.py:333
  55.0 4.2 %collective-permute-done.16.far = f32[32,512]{1,0:T(8,128)S(1)} collective-permute-done((f32[32,512]{1,0:T(8,128)S(1)}, f32[32,512]{1,0:T(8,128)S(1)}, u32[]{:S(2)}, u32[]{:S(2)}) %collective-permute-start.16) | collective-permute-done | bytes 65568 | tf_op jit(solution)/shard_map/ppermute | solution.py:333
  59.2 7.0 %copy-done.1 = bf16[40,4,256,256]{3,2,1,0:T(8,128)(2,1)S(1)} copy-done((bf16[40,4,256,256]{3,2,1,0:T(8,128)(2,1)S(1)}, bf16[40,4,256,256]{3,2,1,0:T(8,128)(2,1)}, u32[]{:S(2)}) %copy-start.1) | copy-done | bytes 20971544
  66.2 1.5 %collective-permute-start.19 = (bf16[32,512]{1,0:T(8,128)(2,1)S(1)}, bf16[32,512]{1,0:T(8,128)(2,1)S(1)}, u32[]{:S(2)}, u32[]{:S(2)}) collective-permute-start(bf16[32,512]{1,0:T(8,128)(2,1)S(1)} %get-tuple-element.60), channel_id=1, source_target_pairs={{0,24},{4,28},{8,16},{12,20},{16,8},{20,12},{24,0},{28,4},{1,25},{... | collective-permute-start | bytes 98312 | tf_op jit(solution)/shard_map/ppermute | solution.py:333
  67.8 0.6 collective-permute-start.18
  68.4 2.3 %collective-permute-start.17 = (bf16[32,512]{1,0:T(8,128)(2,1)S(1)}, bf16[32,512]{1,0:T(8,128)(2,1)S(1)}, u32[]{:S(2)}, u32[]{:S(2)}) collective-permute-start(bf16[32,512]{1,0:T(8,128)(2,1)S(1)} %get-tuple-element.60), channel_id=1, source_target_pairs={{0,8},{4,12},{8,0},{12,4},{16,24},{20,28},{24,16},{28,20},{1,9},{5... | collective-permute-start | bytes 98312 | tf_op jit(solution)/shard_map/ppermute | solution.py:333
  70.7 1.3 %collective-permute-done.19 = bf16[32,512]{1,0:T(8,128)(2,1)S(1)} collective-permute-done((bf16[32,512]{1,0:T(8,128)(2,1)S(1)}, bf16[32,512]{1,0:T(8,128)(2,1)S(1)}, u32[]{:S(2)}, u32[]{:S(2)}) %collective-permute-start.19) | collective-permute-done | bytes 32800 | tf_op jit(solution)/shard_map/ppermute | solution.py:333
  72.0 0.6 collective-permute-done.18
  73.4 1.9 %collective-permute-start.22 = (f32[40,512]{1,0:T(8,128)S(1)}, f32[40,512]{1,0:T(8,128)S(1)}, u32[]{:S(2)}, u32[]{:S(2)}) collective-permute-start(f32[40,512]{1,0:T(8,128)S(1)} %get-tuple-element.64.refs_4_.refs_0_), channel_id=1, source_target_pairs={{0,2},{1,3},{2,0},{3,1},{4,6},{5,7},{6,4},{7,5},{8,10},{9,11},{10,... | collective-permute-start | bytes 245768 | tf_op jit(solution)/shard_map/ppermute | solution.py:333
  75.3 1.9 %apply.4.refs_2_ = f32[8,32,256]{2,1,0:T(8,128)S(1)} custom-call(s32[2]{0:T(128)S(1)} %pad_add_fusion.place, bf16[40,4,256,256]{3,2,1,0:T(8,128)(2,1)S(1)} %copy-done.2, s32[69]{0:T(128)S(1)} %get-tuple-element.51.refs_0_, bf16[4,32,512]{2,1,0:T(8,128)(2,1)S(1)} %pad_maximum_fusion.1.refs_1_), custom_call_target="tpu_custom_call" | custom-call | flops 268435456 | bytes 4194304 | tf_op jit(solution)/shard_map/apply/pallas_call | solution.py:477
  77.3 0.5 collective-permute-done.23.refs_7_.refs_3_
  77.8 2.1 %collective-permute-done.22.refs_6_.refs_2_ = f32[40,512]{1,0:T(8,128)S(1)} collective-permute-done((f32[40,512]{1,0:T(8,128)S(1)}, f32[40,512]{1,0:T(8,128)S(1)}, u32[]{:S(2)}, u32[]{:S(2)}) %collective-permute-start.22) | collective-permute-done | bytes 81952 | tf_op jit(solution)/shard_map/ppermute | solution.py:333
  79.9 2.1 %apply.5 = (f32[32,512]{1,0:T(8,128)S(1)}, f32[32,512]{1,0:T(8,128)S(1)}, f32[2,32,512]{2,1,0:T(8,128)S(1)}, f32[32,128]{1,0:T(8,128)S(1)}) custom-call(s32[2]{0:T(128)S(1)} %pad_add_fusion.place, bf16[40,4,256,256]{3,2,1,0:T(8,128)(2,1)S(1)} %copy-done.2, s32[69]{0:T(128)S(1)} %get-tuple-element.52.refs_1_.refs_0_, ...), custom_call_target="tpu_custom_call" | custom-call | flops 268435456 | bytes 4194304 | tf_op jit(solution)/shard_map/apply/pallas_call | solution.py:477
  82.0 2.3 %collective-permute-start.28 = (f32[32,128]{1,0:T(8,128)S(1)}, f32[32,128]{1,0:T(8,128)S(1)}, u32[]{:S(2)}, u32[]{:S(2)}) collective-permute-start(f32[32,128]{1,0:T(8,128)S(1)} %get-tuple-element.73), channel_id=1, source_target_pairs={{0,24},{4,28},{8,16},{12,20},{16,8},{20,12},{24,0},{28,4},{1,25},{... | collective-permute-start | bytes 49160 | tf_op jit(solution)/shard_map/ppermute | solution.py:333
  84.3 0.8 collective-permute-start.27
  85.1 1.3 %collective-permute-start.26 = (f32[32,128]{1,0:T(8,128)S(1)}, f32[32,128]{1,0:T(8,128)S(1)}, u32[]{:S(2)}, u32[]{:S(2)}) collective-permute-start(f32[32,128]{1,0:T(8,128)S(1)} %get-tuple-element.73), channel_id=1, source_target_pairs={{0,8},{4,12},{8,0},{12,4},{16,24},{20,28},{24,16},{28,20},{1,9},{5... | collective-permute-start | bytes 49160 | tf_op jit(solution)/shard_map/ppermute | solution.py:333
  86.5 0.8 collective-permute-start.25
  87.3 0.5 collective-permute-done.28
  87.8 1.3 %collective-permute-done.27 = f32[32,128]{1,0:T(8,128)S(1)} collective-permute-done((f32[32,128]{1,0:T(8,128)S(1)}, f32[32,128]{1,0:T(8,128)S(1)}, u32[]{:S(2)}, u32[]{:S(2)}) %collective-permute-start.27) | collective-permute-done | bytes 16416 | tf_op jit(solution)/shard_map/ppermute | solution.py:333
  89.1 0.6 collective-permute-start.29
  89.6 3.2 %collective-permute-done.29 = f32[32,128]{1,0:T(8,128)S(1)} collective-permute-done((f32[32,128]{1,0:T(8,128)S(1)}, f32[32,128]{1,0:T(8,128)S(1)}, u32[]{:S(2)}, u32[]{:S(2)}) %collective-permute-start.29) | collective-permute-done | bytes 16416 | tf_op jit(solution)/shard_map/ppermute | solution.py:333
  93.0 0.6 collective-permute-start.31
  93.6 1.2 %collective-permute-start.30 = (f32[32,640]{1,0:T(8,128)S(1)}, f32[32,640]{1,0:T(8,128)S(1)}, u32[]{:S(2)}, u32[]{:S(2)}) collective-permute-start(f32[32,640]{1,0:T(8,128)S(1)} %pad_maximum_fusion.3.refs_4_), channel_id=1, source_target_pairs={{0,1},{1,0},{2,3},{3,2},{4,5},{5,4},{6,7},{7,6},{8,9},{9,8},{10,11... | collective-permute-start | bytes 245768 | tf_op jit(solution)/shard_map/ppermute | solution.py:333
  94.9 2.3 %collective-permute-done.32.refs_7_ = f32[32,640]{1,0:T(8,128)S(1)} collective-permute-done((f32[32,640]{1,0:T(8,128)S(1)}, f32[32,640]{1,0:T(8,128)S(1)}, u32[]{:S(2)}, u32[]{:S(2)}) %collective-permute-start.32) | collective-permute-done | bytes 81952 | tf_op jit(solution)/shard_map/ppermute | solution.py:333
  97.1 1.2 %collective-permute-done.31.refs_6_ = f32[32,640]{1,0:T(8,128)S(1)} collective-permute-done((f32[32,640]{1,0:T(8,128)S(1)}, f32[32,640]{1,0:T(8,128)S(1)}, u32[]{:S(2)}, u32[]{:S(2)}) %collective-permute-start.31) | collective-permute-done | bytes 81952 | tf_op jit(solution)/shard_map/ppermute | solution.py:333
  98.3 2.1 %final.1 = (f32[32,2048]{1,0:T(8,128)}, f32[32,2048]{1,0:T(8,128)}) custom-call(s32[2]{0:T(128)} %copy-done.4, f32[32,2048]{1,0:T(8,128)} %t_ref.1, f32[40,512]{1,0:T(8,128)S(1)} %get-tuple-element.64.refs_4_.refs_0_, f32[40,512]{1,0:T(8,128)S(1)} %collective-permute-done.21.refs_5_.refs_1_, f32[40,512]{1,0:T(8,128)S(1)} %collective-permute-done.22.refs_6_.refs_2_, ...), custom_call_target="tpu_custom_call" | custom-call | tf_op jit(solution)/shard_map/final/pallas_call | solution.py:529
  (65 shorter events, 2.5 us)
Async XLA Ops:
  0.6 5.7 %collective-permute-start = (s32[8,6]{1,0:T(8,128)}, s32[8,6]{1,0:T(8,128)S(1)}, u32[]{:S(2)}, u32[]{:S(2)}) collective-permute-start(s32[8,6]{1,0:T(8,128)} %param.3), channel_id=1, source_target_pairs={{0,1},{1,0},{2,3},{3,2},{4,5},{5,4},{6,7},{7,6},{8,9},{9,8},{10,11... | collective-permute-start | bytes 584 | tf_op jit(solution)/shard_map/ppermute | solution.py:333
  1.1 5.3 %collective-permute-start.2 = (s32[8,6]{1,0:T(8,128)}, s32[8,6]{1,0:T(8,128)S(1)}, u32[]{:S(2)}, u32[]{:S(2)}) collective-permute-start(s32[8,6]{1,0:T(8,128)} %param.3), channel_id=1, source_target_pairs={{0,3},{1,2},{2,1},{3,0},{4,7},{5,6},{6,5},{7,4},{8,11},{9,10},{10,... | collective-permute-start | bytes 584 | tf_op jit(solution)/shard_map/ppermute | solution.py:333
  3.8 3.8 %collective-permute-start.1 = (s32[8,6]{1,0:T(8,128)}, s32[8,6]{1,0:T(8,128)S(1)}, u32[]{:S(2)}, u32[]{:S(2)}) collective-permute-start(s32[8,6]{1,0:T(8,128)} %param.3), channel_id=1, source_target_pairs={{0,2},{1,3},{2,0},{3,1},{4,6},{5,7},{6,4},{7,5},{8,10},{9,11},{10,... | collective-permute-start | bytes 584 | tf_op jit(solution)/shard_map/ppermute | solution.py:333
  7.9 8.1 %collective-permute-start.5 = (bf16[16,640]{1,0:T(8,128)(2,1)S(1)}, bf16[16,640]{1,0:T(8,128)(2,1)S(1)}, u32[]{:S(2)}, u32[]{:S(2)}) collective-permute-start(bf16[16,640]{1,0:T(8,128)(2,1)S(1)} %pad_maximum_fusion.4), channel_id=1, source_target_pairs={{0,24},{4,28},{8,16},{12,20},{16,8},{20,12},{24,0},{28,4},{1,25},{... | collective-permute-start | bytes 61448 | tf_op jit(solution)/shard_map/ppermute | solution.py:333
  11.6 5.2 %collective-permute-start.4 = (bf16[16,640]{1,0:T(8,128)(2,1)S(1)}, bf16[16,640]{1,0:T(8,128)(2,1)S(1)}, u32[]{:S(2)}, u32[]{:S(2)}) collective-permute-start(bf16[16,640]{1,0:T(8,128)(2,1)S(1)} %pad_maximum_fusion.4), channel_id=1, source_target_pairs={{0,16},{4,20},{8,24},{12,28},{16,0},{20,4},{24,8},{28,12},{1,17},{... | collective-permute-start | bytes 61448 | tf_op jit(solution)/shard_map/ppermute | solution.py:333
  11.6 5.2 %collective-permute-start.3 = (bf16[16,640]{1,0:T(8,128)(2,1)S(1)}, bf16[16,640]{1,0:T(8,128)(2,1)S(1)}, u32[]{:S(2)}, u32[]{:S(2)}) collective-permute-start(bf16[16,640]{1,0:T(8,128)(2,1)S(1)} %pad_maximum_fusion.4), channel_id=1, source_target_pairs={{0,8},{4,12},{8,0},{12,4},{16,24},{20,28},{24,16},{28,20},{1,9},{5... | collective-permute-start | bytes 61448 | tf_op jit(solution)/shard_map/ppermute | solution.py:333
  12.3 11.7 %collective-permute-start.9 = (f32[32,512]{1,0:T(8,128)S(1)}, f32[32,512]{1,0:T(8,128)S(1)}, u32[]{:S(2)}, u32[]{:S(2)}) collective-permute-start(f32[32,512]{1,0:T(8,128)S(1)} %constant_dynamic-slice_fusion.t_ref), channel_id=1, source_target_pairs={{0,24},{4,28},{8,16},{12,20},{16,8},{20,12},{24,0},{28,4},{1,25},{... | collective-permute-start | bytes 196616 | tf_op jit(solution)/shard_map/ppermute | solution.py:333
  15.9 8.1 %collective-permute-start.8 = (f32[32,512]{1,0:T(8,128)S(1)}, f32[32,512]{1,0:T(8,128)S(1)}, u32[]{:S(2)}, u32[]{:S(2)}) collective-permute-start(f32[32,512]{1,0:T(8,128)S(1)} %constant_dynamic-slice_fusion.t_ref), channel_id=1, source_target_pairs={{0,16},{4,20},{8,24},{12,28},{16,0},{20,4},{24,8},{28,12},{1,17},{... | collective-permute-start | bytes 196616 | tf_op jit(solution)/shard_map/ppermute | solution.py:333
  15.9 8.1 %collective-permute-start.7 = (f32[32,512]{1,0:T(8,128)S(1)}, f32[32,512]{1,0:T(8,128)S(1)}, u32[]{:S(2)}, u32[]{:S(2)}) collective-permute-start(f32[32,512]{1,0:T(8,128)S(1)} %constant_dynamic-slice_fusion.t_ref), channel_id=1, source_target_pairs={{0,8},{4,12},{8,0},{12,4},{16,24},{20,28},{24,16},{28,20},{1,9},{5... | collective-permute-start | bytes 196616 | tf_op jit(solution)/shard_map/ppermute | solution.py:333
  16.8 7.3 %collective-permute-start.6 = (bf16[4,16,640]{2,1,0:T(8,128)(2,1)S(1)}, bf16[4,16,640]{2,1,0:T(8,128)(2,1)S(1)}, u32[]{:S(2)}, u32[]{:S(2)}) collective-permute-start(bf16[4,16,640]{2,1,0:T(8,128)(2,1)S(1)} %pad_maximum_fusion.2.refs_1_), channel_id=1, source_target_pairs={{0,4},{4,0},{8,12},{12,8},{16,20},{20,16},{24,28},{28,24},{1,5},{5... | collective-permute-start | bytes 245768 | tf_op jit(solution)/shard_map/ppermute | solution.py:333
  18.4 61.5 %copy-start.4 = (s32[2]{0:T(128)}, s32[2]{0:T(128)S(1)}, u32[]{:S(2)}) copy-start(s32[2]{0:T(128)S(1)} %pad_add_fusion.place) | copy-start | bytes 28
  24.1 6.4 %collective-permute-start.10 = (f32[4,32,512]{2,1,0:T(8,128)S(1)}, f32[4,32,512]{2,1,0:T(8,128)S(1)}, u32[]{:S(2)}, u32[]{:S(2)}) collective-permute-start(f32[4,32,512]{2,1,0:T(8,128)S(1)} %pad_maximum_fusion.refs_2_), channel_id=1, source_target_pairs={{0,4},{4,0},{8,12},{12,8},{16,20},{20,16},{24,28},{28,24},{1,5},{5... | collective-permute-start | bytes 786440 | tf_op jit(solution)/shard_map/ppermute | solution.py:333
  30.5 5.9 %collective-permute-start.13 = (f32[16,256]{1,0:T(8,128)S(1)}, f32[16,256]{1,0:T(8,128)S(1)}, u32[]{:S(2)}, u32[]{:S(2)}) collective-permute-start(f32[16,256]{1,0:T(8,128)S(1)} %get-tuple-element.56), channel_id=1, source_target_pairs={{0,24},{4,28},{8,16},{12,20},{16,8},{20,12},{24,0},{28,4},{1,25},{... | collective-permute-start | bytes 49160 | tf_op jit(solution)/shard_map/ppermute | solution.py:333
  34.7 4.6 %collective-permute-start.12 = (f32[16,256]{1,0:T(8,128)S(1)}, f32[16,256]{1,0:T(8,128)S(1)}, u32[]{:S(2)}, u32[]{:S(2)}) collective-permute-start(f32[16,256]{1,0:T(8,128)S(1)} %get-tuple-element.56), channel_id=1, source_target_pairs={{0,16},{4,20},{8,24},{12,28},{16,0},{20,4},{24,8},{28,12},{1,17},{... | collective-permute-start | bytes 49160 | tf_op jit(solution)/shard_map/ppermute | solution.py:333
  34.7 4.6 %collective-permute-start.11 = (f32[16,256]{1,0:T(8,128)S(1)}, f32[16,256]{1,0:T(8,128)S(1)}, u32[]{:S(2)}, u32[]{:S(2)}) collective-permute-start(f32[16,256]{1,0:T(8,128)S(1)} %get-tuple-element.56), channel_id=1, source_target_pairs={{0,8},{4,12},{8,0},{12,4},{16,24},{20,28},{24,16},{28,20},{1,9},{5... | collective-permute-start | bytes 49160 | tf_op jit(solution)/shard_map/ppermute | solution.py:333
  39.4 3.8 %collective-permute-start.14 = (f32[16,256]{1,0:T(8,128)S(1)}, f32[16,256]{1,0:T(8,128)S(1)}, u32[]{:S(2)}, u32[]{:S(2)}) collective-permute-start(f32[16,256]{1,0:T(8,128)S(1)} %add_add_fusion.1), channel_id=1, source_target_pairs={{0,4},{4,0},{8,12},{12,8},{16,20},{20,16},{24,28},{28,24},{1,5},{5... | collective-permute-start | bytes 49160 | tf_op jit(solution)/shard_map/ppermute | solution.py:333
  46.5 7.0 %copy-start = (bf16[40,4,256,256]{3,2,1,0:T(8,128)(2,1)}, bf16[40,4,256,256]{3,2,1,0:T(8,128)(2,1)S(1)}, u32[]{:S(2)}) copy-start(bf16[40,4,256,256]{3,2,1,0:T(8,128)(2,1)S(1)} %get-tuple-element.50.k_mat) | copy-start | bytes 62914564
  53.5 1.3 %collective-permute-start.15 = (f32[2,32,512]{2,1,0:T(8,128)S(1)}, f32[2,32,512]{2,1,0:T(8,128)S(1)}, u32[]{:S(2)}, u32[]{:S(2)}) collective-permute-start(f32[2,32,512]{2,1,0:T(8,128)S(1)} %get-tuple-element.58), channel_id=1, source_target_pairs={{0,1},{1,0},{2,3},{3,2},{4,5},{5,4},{6,7},{7,6},{8,9},{9,8},{10,11... | collective-permute-start | bytes 393224 | tf_op jit(solution)/shard_map/ppermute | solution.py:333
  54.9 4.3 %collective-permute-start.16 = (f32[32,512]{1,0:T(8,128)S(1)}, f32[32,512]{1,0:T(8,128)S(1)}, u32[]{:S(2)}, u32[]{:S(2)}) collective-permute-start(f32[32,512]{1,0:T(8,128)S(1)} %get-tuple-element.74), channel_id=1, source_target_pairs={{0,2},{1,3},{2,0},{3,1},{4,6},{5,7},{6,4},{7,5},{8,10},{9,11},{10,... | collective-permute-start | bytes 196616 | tf_op jit(solution)/shard_map/ppermute | solution.py:333
  59.2 7.0 %copy-start.1 = (bf16[40,4,256,256]{3,2,1,0:T(8,128)(2,1)S(1)}, bf16[40,4,256,256]{3,2,1,0:T(8,128)(2,1)}, u32[]{:S(2)}) copy-start(bf16[40,4,256,256]{3,2,1,0:T(8,128)(2,1)} %copy-done) | copy-start | bytes 62914564
  66.2 9.1 %copy-start.2 = (bf16[40,4,256,256]{3,2,1,0:T(8,128)(2,1)S(1)}, bf16[40,4,256,256]{3,2,1,0:T(8,128)(2,1)}, u32[]{:S(2)}) copy-start(bf16[40,4,256,256]{3,2,1,0:T(8,128)(2,1)} %copy-done) | copy-start | bytes 62914564
  66.2 13.7 %copy-start.3 = (f32[32,2048]{1,0:T(8,128)S(1)}, f32[32,2048]{1,0:T(8,128)}, u32[]{:S(2)}) copy-start(f32[32,2048]{1,0:T(8,128)} %t_ref.1) | copy-start | bytes 786436
  66.2 5.8 %collective-permute-start.19 = (bf16[32,512]{1,0:T(8,128)(2,1)S(1)}, bf16[32,512]{1,0:T(8,128)(2,1)S(1)}, u32[]{:S(2)}, u32[]{:S(2)}) collective-permute-start(bf16[32,512]{1,0:T(8,128)(2,1)S(1)} %get-tuple-element.60), channel_id=1, source_target_pairs={{0,24},{4,28},{8,16},{12,20},{16,8},{20,12},{24,0},{28,4},{1,25},{... | collective-permute-start | bytes 98312 | tf_op jit(solution)/shard_map/ppermute | solution.py:333
  67.8 4.8 %collective-permute-start.18 = (bf16[32,512]{1,0:T(8,128)(2,1)S(1)}, bf16[32,512]{1,0:T(8,128)(2,1)S(1)}, u32[]{:S(2)}, u32[]{:S(2)}) collective-permute-start(bf16[32,512]{1,0:T(8,128)(2,1)S(1)} %get-tuple-element.60), channel_id=1, source_target_pairs={{0,16},{4,20},{8,24},{12,28},{16,0},{20,4},{24,8},{28,12},{1,17},{... | collective-permute-start | bytes 98312 | tf_op jit(solution)/shard_map/ppermute | solution.py:333
  68.4 4.5 %collective-permute-start.17 = (bf16[32,512]{1,0:T(8,128)(2,1)S(1)}, bf16[32,512]{1,0:T(8,128)(2,1)S(1)}, u32[]{:S(2)}, u32[]{:S(2)}) collective-permute-start(bf16[32,512]{1,0:T(8,128)(2,1)S(1)} %get-tuple-element.60), channel_id=1, source_target_pairs={{0,8},{4,12},{8,0},{12,4},{16,24},{20,28},{24,16},{28,20},{1,9},{5... | collective-permute-start | bytes 98312 | tf_op jit(solution)/shard_map/ppermute | solution.py:333
  72.9 6.9 %collective-permute-start.20 = (bf16[4,32,512]{2,1,0:T(8,128)(2,1)S(1)}, bf16[4,32,512]{2,1,0:T(8,128)(2,1)S(1)}, u32[]{:S(2)}, u32[]{:S(2)}) collective-permute-start(bf16[4,32,512]{2,1,0:T(8,128)(2,1)S(1)} %pad_maximum_fusion.1.refs_1_), channel_id=1, source_target_pairs={{0,4},{4,0},{8,12},{12,8},{16,20},{20,16},{24,28},{28,24},{1,5},{5... | collective-permute-start | bytes 393224 | tf_op jit(solution)/shard_map/ppermute | solution.py:333
  73.4 4.4 %collective-permute-start.23 = (f32[40,512]{1,0:T(8,128)S(1)}, f32[40,512]{1,0:T(8,128)S(1)}, u32[]{:S(2)}, u32[]{:S(2)}) collective-permute-start(f32[40,512]{1,0:T(8,128)S(1)} %get-tuple-element.64.refs_4_.refs_0_), channel_id=1, source_target_pairs={{0,3},{1,2},{2,1},{3,0},{4,7},{5,6},{6,5},{7,4},{8,11},{9,10},{10,... | collective-permute-start | bytes 245768 | tf_op jit(solution)/shard_map/ppermute | solution.py:333
  73.4 6.5 %collective-permute-start.22 = (f32[40,512]{1,0:T(8,128)S(1)}, f32[40,512]{1,0:T(8,128)S(1)}, u32[]{:S(2)}, u32[]{:S(2)}) collective-permute-start(f32[40,512]{1,0:T(8,128)S(1)} %get-tuple-element.64.refs_4_.refs_0_), channel_id=1, source_target_pairs={{0,2},{1,3},{2,0},{3,1},{4,6},{5,7},{6,4},{7,5},{8,10},{9,11},{10,... | collective-permute-start | bytes 245768 | tf_op jit(solution)/shard_map/ppermute | solution.py:333
  75.2 4.6 %collective-permute-start.21 = (f32[40,512]{1,0:T(8,128)S(1)}, f32[40,512]{1,0:T(8,128)S(1)}, u32[]{:S(2)}, u32[]{:S(2)}) collective-permute-start(f32[40,512]{1,0:T(8,128)S(1)} %get-tuple-element.64.refs_4_.refs_0_), channel_id=1, source_target_pairs={{0,1},{1,0},{2,3},{3,2},{4,5},{5,4},{6,7},{7,6},{8,9},{9,8},{10,11... | collective-permute-start | bytes 245768 | tf_op jit(solution)/shard_map/ppermute | solution.py:333
  81.9 4.5 %collective-permute-start.24 = (f32[2,32,512]{2,1,0:T(8,128)S(1)}, f32[2,32,512]{2,1,0:T(8,128)S(1)}, u32[]{:S(2)}, u32[]{:S(2)}) collective-permute-start(f32[2,32,512]{2,1,0:T(8,128)S(1)} %get-tuple-element.71), channel_id=1, source_target_pairs={{0,1},{1,0},{2,3},{3,2},{4,5},{5,4},{6,7},{7,6},{8,9},{9,8},{10,11... | collective-permute-start | bytes 393224 | tf_op jit(solution)/shard_map/ppermute | solution.py:333
  82.0 5.8 %collective-permute-start.28 = (f32[32,128]{1,0:T(8,128)S(1)}, f32[32,128]{1,0:T(8,128)S(1)}, u32[]{:S(2)}, u32[]{:S(2)}) collective-permute-start(f32[32,128]{1,0:T(8,128)S(1)} %get-tuple-element.73), channel_id=1, source_target_pairs={{0,24},{4,28},{8,16},{12,20},{16,8},{20,12},{24,0},{28,4},{1,25},{... | collective-permute-start | bytes 49160 | tf_op jit(solution)/shard_map/ppermute | solution.py:333
  84.3 4.7 %collective-permute-start.27 = (f32[32,128]{1,0:T(8,128)S(1)}, f32[32,128]{1,0:T(8,128)S(1)}, u32[]{:S(2)}, u32[]{:S(2)}) collective-permute-start(f32[32,128]{1,0:T(8,128)S(1)} %get-tuple-element.73), channel_id=1, source_target_pairs={{0,16},{4,20},{8,24},{12,28},{16,0},{20,4},{24,8},{28,12},{1,17},{... | collective-permute-start | bytes 49160 | tf_op jit(solution)/shard_map/ppermute | solution.py:333
  85.1 3.9 %collective-permute-start.26 = (f32[32,128]{1,0:T(8,128)S(1)}, f32[32,128]{1,0:T(8,128)S(1)}, u32[]{:S(2)}, u32[]{:S(2)}) collective-permute-start(f32[32,128]{1,0:T(8,128)S(1)} %get-tuple-element.73), channel_id=1, source_target_pairs={{0,8},{4,12},{8,0},{12,4},{16,24},{20,28},{24,16},{28,20},{1,9},{5... | collective-permute-start | bytes 49160 | tf_op jit(solution)/shard_map/ppermute | solution.py:333
  86.5 6.4 %collective-permute-start.25 = (f32[32,512]{1,0:T(8,128)S(1)}, f32[32,512]{1,0:T(8,128)S(1)}, u32[]{:S(2)}, u32[]{:S(2)}) collective-permute-start(f32[32,512]{1,0:T(8,128)S(1)} %fusion), channel_id=1, source_target_pairs={{0,2},{1,3},{2,0},{3,1},{4,6},{5,7},{6,4},{7,5},{8,10},{9,11},{10,... | collective-permute-start | bytes 196616 | tf_op jit(solution)/shard_map/ppermute | solution.py:333
  89.1 3.8 %collective-permute-start.29 = (f32[32,128]{1,0:T(8,128)S(1)}, f32[32,128]{1,0:T(8,128)S(1)}, u32[]{:S(2)}, u32[]{:S(2)}) collective-permute-start(f32[32,128]{1,0:T(8,128)S(1)} %add_add_fusion), channel_id=1, source_target_pairs={{0,4},{4,0},{8,12},{12,8},{16,20},{20,16},{24,28},{28,24},{1,5},{5... | collective-permute-start | bytes 49160 | tf_op jit(solution)/shard_map/ppermute | solution.py:333
  92.9 4.2 %collective-permute-start.32 = (f32[32,640]{1,0:T(8,128)S(1)}, f32[32,640]{1,0:T(8,128)S(1)}, u32[]{:S(2)}, u32[]{:S(2)}) collective-permute-start(f32[32,640]{1,0:T(8,128)S(1)} %pad_maximum_fusion.3.refs_4_), channel_id=1, source_target_pairs={{0,3},{1,2},{2,1},{3,0},{4,7},{5,6},{6,5},{7,4},{8,11},{9,10},{10,... | collective-permute-start | bytes 245768 | tf_op jit(solution)/shard_map/ppermute | solution.py:333
  93.0 5.3 %collective-permute-start.31 = (f32[32,640]{1,0:T(8,128)S(1)}, f32[32,640]{1,0:T(8,128)S(1)}, u32[]{:S(2)}, u32[]{:S(2)}) collective-permute-start(f32[32,640]{1,0:T(8,128)S(1)} %pad_maximum_fusion.3.refs_4_), channel_id=1, source_target_pairs={{0,2},{1,3},{2,0},{3,1},{4,6},{5,7},{6,4},{7,5},{8,10},{9,11},{10,... | collective-permute-start | bytes 245768 | tf_op jit(solution)/shard_map/ppermute | solution.py:333
  93.6 4.7 %collective-permute-start.30 = (f32[32,640]{1,0:T(8,128)S(1)}, f32[32,640]{1,0:T(8,128)S(1)}, u32[]{:S(2)}, u32[]{:S(2)}) collective-permute-start(f32[32,640]{1,0:T(8,128)S(1)} %pad_maximum_fusion.3.refs_4_), channel_id=1, source_target_pairs={{0,1},{1,0},{2,3},{3,2},{4,5},{5,4},{6,7},{7,6},{8,9},{9,8},{10,11... | collective-permute-start | bytes 245768 | tf_op jit(solution)/shard_map/ppermute | solution.py:333

commit v5 on v4

--- a/solution.py
+++ b/solution.py
@@ -15,12 +15,11 @@
 CODE_BITS = 12
 CODE = 1 << CODE_BITS
 RING = 3
-STRIP = 64
+STRIP = 32
 LANES = 128
 TINY = 1e-30
 SHIFT = 0.375
 DIRECT_ROWS = 8
-ROOM_GROUPS = 8
 RESIDENT_BYTES = 20 * 1024 * 1024
 
 SMEM = pl.BlockSpec(memory_space=pltpu.SMEM)
@@ -156,12 +155,11 @@
             code = listed[g * GROUP + u + 1]
             i, j = lax.shift_right_logical(code, CODE_BITS), code & (CODE - 1)
             m = mlist[g * GROUP + u].astype(F32)
-            far = rhs[j]
+            dist = jnp.dot(lhs[i], rhs[j], preferred_element_type=F32)
             sums = jnp.zeros((8, block_len), F32)
             for s in range(block_len // STRIP):
                 rows = slice(s * STRIP, (s + 1) * STRIP)
-                d = jnp.dot(lhs[i, rows, :], far, preferred_element_type=F32)
-                d = jnp.maximum(d, TINY)
+                d = jnp.maximum(dist[rows], TINY)
                 sc = d * lax.rsqrt(d)
                 rem = jnp.maximum(1.0 - sc, 0.0)
                 sq = rem * rem
@@ -194,6 +192,10 @@
         lax.fori_loop(jnp.maximum(total - RING, 0), total, drain, 0)
 
 
+def pieces_of(own, got):
+    return own.at[0], got.at[0], own.at[1], got.at[1]
+
+
 def apply_kernel(cfg, parts, scaled, carried, finish, place, k_mat, *refs):
     n = len(parts)
     lists, pieces, refs = refs[:n], refs[n:2 * n], refs[2 * n:]
@@ -203,12 +205,12 @@
         z_in, refs = refs[0], refs[1:]
     products = finish and not scaled
     if products:
-        t_ref, s_refs, refs = refs[0], refs[1:5], refs[5:]
-    if finish:
-        near, near_y, cross, refs = refs[0], refs[1], refs[2], refs[3:]
-        if products:
-            dot_ref, refs = refs[0], refs[1:]
-        z_acc, refs = refs[0], refs[1:]
+        t_ref, s_refs, refs = refs[0], pieces_of(refs[1], refs[2]), refs[3:]
+    if products:
+        near, near_y, cross, dot_ref, z_acc, refs = *refs[:5], refs[5:]
+        z_refs = (near, cross.at[0], near_y, cross.at[1])
+    elif finish:
+        near, cross, z_acc, refs = *refs[:3], refs[3:]
     else:
         z_acc, refs = refs[0], refs[1:]
     w_all, refs = refs[0], refs[1:]
@@ -272,7 +274,16 @@
     if not finish:
         return
     own_len = own_rows * block_len
-    z_refs = (near, cross.at[0], near_y, cross.at[1])
+    if scaled:
+        outputs = (near.shape[0] - 8) // 2
+        z_refs = [
+            ref.at[pl.ds(outputs * h, outputs)] for h in range(2) for ref in (near, cross)
+        ]
+        for k in range(own_rows):
+            cols = slice(k * block_len, (k + 1) * block_len)
+            mine = inv_ref[pl.ds(place[0] * own_rows + k, 1), :]
+            near[2 * outputs:, cols] = jnp.broadcast_to(mine, (8, block_len))
+        cross[2 * outputs:, :] = jnp.zeros((8, own_len), F32)
     for e in range(4):
         for k in range(own_rows):
             z_refs[e][:, k * block_len:(k + 1) * block_len] = z_acc[(col ^ e) * own_rows + k]
@@ -299,20 +310,12 @@
         dot_ref[...] = out
 
 
-def first_kernel(near, far, inv_ref, t_ref, k_mat, s_ref, g_ref):
-    outputs = t_ref.shape[0]
-    inv = inv_ref[...]
-    s = (near[...] + far[...]) * inv
-    s_ref[:outputs, :] = s
-    s_ref[outputs:, :] = jnp.broadcast_to(inv, (8, inv.shape[1]))
-    g_ref[...] = ((s - SHIFT * t_ref[...]) * inv).astype(BF16)
-
-
-def final_kernel(n_cols, place, t_ref, *refs):
-    s1s, s2s = refs[:4], refs[4:8]
-    sol_ref, res_ref = refs[8:]
-    outputs, own_len = s2s[0].shape[0], s2s[0].shape[1] - LANES
-    dots = pair_sum([ref[:, own_len:] for ref in s2s])
+def final_kernel(place, t_ref, s1_own, s1_got, *refs):
+    s2s, all_dots = refs[:4], refs[4:8]
+    sol_hbm, res_hbm, sol_ref, res_ref, sems = refs[8:]
+    s1s = pieces_of(s1_own, s1_got)
+    outputs, own_len = s2s[0].shape
+    dots = pair_sum([ref[...] for ref in all_dots])
     tt, ts1, s1s1, ts2, s1s2 = (dots[:, n:n + 1] for n in range(5))
     a1 = tt / (REG * tt + ts1)
     p = 1.0 - REG * a1
@@ -321,25 +324,25 @@
     dd = u * u * tt - 2.0 * u * a1 * ts1 + a1 * a1 * s1s1
     dmd = u * u * ts1 - u * a1 * (s1s1 + ts2) + a1 * a1 * s1s2
     a2 = new / (REG * dd + dmd)
-    for e in range(n_cols):
+    sol_t, sol_1 = a1 + a2 * u, a2 * a1
+    res_t, res_1 = p - a2 * REG * u, a1 + a2 * (u - REG * a1)
+    copies = []
+    for e in range(4):
         at = pl.ds(pl.multiple_of((place[1] ^ e) * own_len, LANES), own_len)
-        t, s1, s2 = t_ref[:, at], s1s[e][:outputs, :], s2s[e][:, :own_len]
-        sol_ref[:, at] = (a1 + a2 * u) * t - (a2 * a1) * s1
-        res_ref[:, at] = (p - a2 * REG * u) * t - (a1 + a2 * (u - REG * a1)) * s1 + (a2 * a1) * s2
+        t, s1, s2 = t_ref[:, at], s1s[e][:outputs, :], s2s[e][...]
+        sol_ref[e] = sol_t * t - sol_1 * s1
+        res_ref[e] = res_t * t - res_1 * s1 + sol_1 * s2
+        for n, (ref, hbm) in enumerate(((sol_ref, sol_hbm), (res_ref, res_hbm))):
+            copy = pltpu.make_async_copy(ref.at[e], hbm.at[:, at], sems.at[n, e])
+            copy.start()
+            copies.append(copy)
+    for copy in copies:
+        copy.wait()
 
 
 def swap(x, axis, d):
     size = lax.axis_size(axis)
     return lax.ppermute(x, axis, [(i, i ^ d) for i in range(size)])
-
-
-def half_shared(near, near_y, cross):
-    got = swap(cross, "cols", 1)
-    return near + got[0], near_y + got[1]
-
-
-def shared(near, near_y):
-    return near + swap(near_y, "cols", 2)
 
 
 def along_z(x):
@@ -376,8 +379,7 @@
     list_len = n_groups * GROUP + GROUP + 1
     place = jnp.stack([row, col])
     resident = parts * 2 * n_groups * GROUP * block_len * block_len <= RESIDENT_BYTES
-    room = ROOM_GROUPS if resident else 0
-    k_shape = (parts * n_groups + room, GROUP, block_len, block_len)
+    k_shape = (parts * n_groups, GROUP, block_len, block_len)
     limit = pltpu.CompilerParams(vmem_limit_bytes=(8 if resident else 32) * 1024 * 1024)
     ring = [] if resident else [
         pltpu.VMEM((RING, GROUP, block_len, block_len), BF16),
@@ -462,16 +464,17 @@
         k_mat, list0, degree, _ = build(0, near, lax.all_gather(packed, "rows"))
         t_pieces, k_lists = [lax.all_gather(own_t, "rows")], [list0]
     inv = 1.0 / jnp.sqrt(1.0 + total_rows(degree))
-    own_inv = lax.dynamic_slice_in_dim(inv, row * own_rows, own_rows, 0).reshape(1, own_len)
 
     def apply(use, pieces, finish=True, inv=None, z_in=None, products=()):
         operands = [k_mat] + [k_lists[p] for p in use] + pieces
         specs = [k_spec] + [SMEM] * len(use) + [VMEM] * len(pieces)
         more = [x for x in (inv, z_in) if x is not None] + list(products)
         z_shape = (block_rows, outputs, block_len)
-        if finish:
+        if products:
             out = [shape(outputs, own_len), shape(outputs, own_len), shape(2, outputs, own_len)]
-            out += [shape(outputs, LANES)] if products else []
+            out += [shape(outputs, LANES)]
+        elif finish:
+            out = [shape(2 * outputs + 8, own_len)] * 2
         else:
             out = [shape(*z_shape)]
         return pl.pallas_call(
@@ -494,45 +497,56 @@
             name="apply",
         )(place, *operands, *more)
 
-    z1, z1_y = half_shared(*apply(tuple(range(parts)), t_pieces, inv=inv))
-    s1_packed, g = pl.pallas_call(
-        first_kernel,
-        out_shape=(shape(outputs + 8, own_len), shape(outputs, own_len, dtype=BF16)),
-        in_specs=[VMEM] * 4 + [k_spec],
-        out_specs=(VMEM, VMEM),
-        compiler_params=limit,
-        name="first",
-    )(z1, swap(z1_y, "cols", 2), own_inv, own_t, k_mat)
-    s1 = s1_packed[:outputs]
+    near_z, cross_z = apply(tuple(range(parts)), t_pieces, inv=inv)
+    half = near_z + swap(cross_z, "cols", 1)
+    far = swap(half, "cols", 2)
+    lo, hi, tail = slice(0, outputs), slice(outputs, 2 * outputs), slice(2 * outputs, None)
+    own_inv, far_inv = half[2 * outputs:2 * outputs + 1], far[2 * outputs:2 * outputs + 1]
+    s1 = (half[lo] + far[hi]) * own_inv
+    g = ((s1 - SHIFT * own_t) * own_inv).astype(BF16)
+    s1_own = jnp.stack([
+        jnp.concatenate([s1, half[tail]], axis=0),
+        jnp.concatenate([(half[hi] + far[lo]) * far_inv, far[tail]], axis=0),
+    ])
+    held_t = pltpu.with_memory_space_constraint(targets, pltpu.VMEM)
     if direct_rows:
         g_same = jnp.stack(along_z(g))
-        g_same, s1_packed = lax.optimization_barrier((g_same, s1_packed))
+        g_same, s1_own = lax.optimization_barrier((g_same, s1_own))
         _, g_other = across_x(g_same)
-        s1_all = direct_cols(s1_packed)
+        s1_got = swap(s1_own, "cols", 1)
         (z_part,) = apply((0,), [g_same], finish=False)
-        z_part, g_other, *s1_all = lax.optimization_barrier((z_part, g_other, *s1_all))
-        *z2, dots = apply((1,), [g_other], z_in=z_part, products=[targets, *s1_all])
+        z_part, g_other, s1_got = lax.optimization_barrier((z_part, g_other, s1_got))
+        near_z, near_y, cross_z, dots = apply(
+            (1,), [g_other], z_in=z_part, products=[held_t, s1_own, s1_got]
+        )
         dots = pair_sum(along_z(dots))
-        s2 = shared(*half_shared(*z2))
-        dots = pair_sum(across_x(dots))
     else:
-        s1_all = direct_cols(s1_packed)
-        *z2, dots = apply((0,), [lax.all_gather(g, "rows")], products=[targets, *s1_all])
-        s2 = shared(*half_shared(*z2))
-        dots = lax.psum(dots, "rows")
-    s2 = s2 * own_inv + SHIFT * s1
-    ends = direct_cols(jnp.concatenate([s2, dots], axis=1))
-    s1_all, ends = [
-        [pltpu.with_memory_space_constraint(x, pltpu.VMEM) for x in xs] for xs in (s1_all, ends)
+        s1_got = swap(s1_own, "cols", 1)
+        near_z, near_y, cross_z, dots = apply(
+            (0,), [lax.all_gather(g, "rows")], products=[held_t, s1_own, s1_got]
+        )
+    got = swap(cross_z, "cols", 1)
+    z2 = near_z + got[0] + swap(near_y + got[1], "cols", 2)
+    s2 = direct_cols(z2 * own_inv + SHIFT * s1)
+    dots = pair_sum(across_x(dots)) if direct_rows else lax.psum(dots, "rows")
+    dots = direct_cols(dots)
+    ends = [
+        pltpu.with_memory_space_constraint(x, pltpu.VMEM) for x in (s1_own, s1_got, *s2, *dots)
     ]
 
     return pl.pallas_call(
-        functools.partial(final_kernel, n_cols),
+        final_kernel,
         out_shape=(shape(outputs, npoints), shape(outputs, npoints)),
-        in_specs=[SMEM] + [VMEM] * 9,
-        out_specs=(VMEM, VMEM),
+        in_specs=[SMEM] + [VMEM] * 11,
+        out_specs=(HBM, HBM),
+        scratch_shapes=[
+            pltpu.VMEM((4, outputs, own_len), F32),
+            pltpu.VMEM((4, outputs, own_len), F32),
+            pltpu.SemaphoreType.DMA((2, 4)),
+        ],
+        compiler_params=limit,
         name="final",
-    )(place, targets, *s1_all, *ends)
+    )(place, held_t, *ends)
 
 
 def solution(mesh):

time: 100 us -> 87.6 us (0.88); the launches traced: 100 us -> 87 us
  local copies, waits for them, and re-layouts: 16.7 us -> 2.75 us
    unnamed x14 -> x3, local copies, waits for them, and re-layouts: 14.8 us -> 0.84 us
    ppermute x33 -> x34, starting transfers between devices: 34.1 us -> 35 us  [swap(): return lax.ppermute(x, axis, [(i, i ^ d) for i in range(size)])]
    pallas_call x2 -> x1, Pallas kernels: 2.11 us -> 1.71 us  [local(): pl.pallas_call(final_kernel, out_shape=(shape(outputs, npoints), shape(ou...]
    ppermute x33 -> x34, waiting for transfers between devices: 28 us -> 28 us  [swap(): return lax.ppermute(x, axis, [(i, i ^ d) for i in range(size)])]
  transfers between devices with their start and end apart: 33 -> 34, of which waited for: 17 -> 18; matrix products, arithmetic and copies ran while one was open for 3% -> 3% of each run, Pallas kernels for 13% -> 15%
where the time goes in v5:
time: 87.6 us; the launch traced here: 87 us
  starting transfers between devices  35 us (40%)
  waiting for transfers between devices  28 us (32%)
  Pallas kernels  19.9 us (23%)
  local copies, waits for them, and re-layouts  2.75 us (3%)
    ppermute x34, starting transfers between devices, swap(): return lax.ppermute(x, axis, [(i, i ^ d) for i in range(size)])  35 us
    ppermute x34, waiting for transfers between devices, swap(): return lax.ppermute(x, axis, [(i, i ^ d) for i in range(size)])  28 us
    pallas_call x2, Pallas kernels, build(): pl.pallas_call(functools.partial(build_kernel, cfg, part), out_shape=out,...  10.8 us
    pallas_call x3, Pallas kernels, apply(): pl.pallas_call(functools.partial(apply_kernel, cfg, use, inv is not None,...  7.36 us
  transfers between devices with their start and end apart: 34, of which 18 were waited for; matrix products, arithmetic and copies ran while one was open for 3% of the time, Pallas kernels for 15%

profile of v5, /device:TPU:0, one launch (start us, length us, event | category | flops | bytes accessed | tf_op | source)
XLA Modules:
  0.0 87.0 jit_solution(3484943152225602309)
XLA Ops:
  0.6 0.5 collective-permute-start
  1.1 2.6 %collective-permute-start.2 = (s32[8,6]{1,0:T(8,128)}, s32[8,6]{1,0:T(8,128)S(1)}, u32[]{:S(2)}, u32[]{:S(2)}) collective-permute-start(s32[8,6]{1,0:T(8,128)} %param.3), channel_id=1, source_target_pairs={{0,3},{1,2},{2,1},{3,0},{4,7},{5,6},{6,5},{7,4},{8,11},{9,10},{10,... | collective-permute-start | bytes 584 | tf_op jit(solution)/shard_map/ppermute | solution.py:345
  3.8 0.8 copy.6
  4.7 0.7 constant_dynamic-slice_fusion.1
  5.5 0.8 constant_dynamic-slice_fusion
  6.6 1.0 %collective-permute-done.1 = s32[8,6]{1,0:T(8,128)S(1)} collective-permute-done((s32[8,6]{1,0:T(8,128)}, s32[8,6]{1,0:T(8,128)S(1)}, u32[]{:S(2)}, u32[]{:S(2)}) %collective-permute-start.1) | collective-permute-done | bytes 224 | tf_op jit(solution)/shard_map/ppermute | solution.py:345
  7.9 3.7 %collective-permute-start.5 = (bf16[16,640]{1,0:T(8,128)(2,1)S(1)}, bf16[16,640]{1,0:T(8,128)(2,1)S(1)}, u32[]{:S(2)}, u32[]{:S(2)}) collective-permute-start(bf16[16,640]{1,0:T(8,128)(2,1)S(1)} %pad_maximum_fusion.4), channel_id=1, source_target_pairs={{0,24},{4,28},{8,16},{12,20},{16,8},{20,12},{24,0},{28,4},{1,25},{... | collective-permute-start | bytes 61448 | tf_op jit(solution)/shard_map/ppermute | solution.py:345
  11.6 0.8 collective-permute-start.3
  12.3 3.6 %collective-permute-start.9 = (f32[32,512]{1,0:T(8,128)S(1)}, f32[32,512]{1,0:T(8,128)S(1)}, u32[]{:S(2)}, u32[]{:S(2)}) collective-permute-start(f32[32,512]{1,0:T(8,128)S(1)} %constant_dynamic-slice_fusion), channel_id=1, source_target_pairs={{0,24},{4,28},{8,16},{12,20},{16,8},{20,12},{24,0},{28,4},{1,25},{... | collective-permute-start | bytes 196616 | tf_op jit(solution)/shard_map/ppermute | solution.py:345
  15.9 0.8 collective-permute-start.7
  16.8 1.6 %collective-permute-start.6 = (bf16[4,16,640]{2,1,0:T(8,128)(2,1)S(1)}, bf16[4,16,640]{2,1,0:T(8,128)(2,1)S(1)}, u32[]{:S(2)}, u32[]{:S(2)}) collective-permute-start(bf16[4,16,640]{2,1,0:T(8,128)(2,1)S(1)} %pad_maximum_fusion.3.refs_1_), channel_id=1, source_target_pairs={{0,4},{4,0},{8,12},{12,8},{16,20},{20,16},{24,28},{28,24},{1,5},{5... | collective-permute-start | bytes 245768 | tf_op jit(solution)/shard_map/ppermute | solution.py:345
  18.4 5.6 %build.2 = (bf16[32,4,256,256]{3,2,1,0:T(8,128)(2,1)S(1)}, s32[69]{0:T(128)S(1)}, f32[8,256]{1,0:T(8,128)S(1)}, bf16[8,256,32]{2,1,0:T(8,128)(2,1)S(1)}) custom-call(s32[2]{0:T(128)S(1)} %pad_add_fusion.place, s32[8,64]{1,0:T(8,128)S(1)} %add_add_fusion.2.direct, bf16[16,2048]{1,0:T(8,128)(2,1)} %refs_0_.1, bf16[4,16,640]{2,1,0:T(8,128)(2,1)S(1)} %pad_maximum_fusion.3.refs_1_), custom_call_target="tpu_custom_call" | custom-call | flops 268435456 | bytes 8388608 | tf_op jit(solution)/shard_map/build/pallas_call | solution.py:421
  24.2 5.2 %build.3 = (bf16[32,4,256,256]{3,2,1,0:T(8,128)(2,1)S(1)}, s32[69]{0:T(128)S(1)}, f32[16,256]{1,0:T(8,128)S(1)}) custom-call(s32[2]{0:T(128)S(1)} %pad_add_fusion.place, s32[8,64]{1,0:T(8,128)S(1)} %add_add_fusion.2.direct, bf16[8,256,32]{2,1,0:T(8,128)(2,1)S(1)} %get-tuple-element.33.refs_0_, ...), custom_call_target="tpu_custom_call", output_to_operand_aliasing={{0}: (5, {})} | custom-call | flops 268435456 | bytes 8388608 | tf_op jit(solution)/shard_map/build/pallas_call | solution.py:421
  29.4 1.1 %collective-permute-done.10.refs_3_ = f32[4,32,512]{2,1,0:T(8,128)S(1)} collective-permute-done((f32[4,32,512]{2,1,0:T(8,128)S(1)}, f32[4,32,512]{2,1,0:T(8,128)S(1)}, u32[]{:S(2)}, u32[]{:S(2)}) %collective-permute-start.10) | collective-permute-done | bytes 262176 | tf_op jit(solution)/shard_map/ppermute | solution.py:345
  30.5 3.6 %collective-permute-start.13 = (f32[16,256]{1,0:T(8,128)S(1)}, f32[16,256]{1,0:T(8,128)S(1)}, u32[]{:S(2)}, u32[]{:S(2)}) collective-permute-start(f32[16,256]{1,0:T(8,128)S(1)} %get-tuple-element.50), channel_id=1, source_target_pairs={{0,24},{4,28},{8,16},{12,20},{16,8},{20,12},{24,0},{28,4},{1,25},{... | collective-permute-start | bytes 49160 | tf_op jit(solution)/shard_map/ppermute | solution.py:345
  34.1 0.8 collective-permute-start.11
  34.9 1.1 %collective-permute-done.13 = f32[16,256]{1,0:T(8,128)S(1)} collective-permute-done((f32[16,256]{1,0:T(8,128)S(1)}, f32[16,256]{1,0:T(8,128)S(1)}, u32[]{:S(2)}, u32[]{:S(2)}) %collective-permute-start.13) | collective-permute-done | bytes 16416 | tf_op jit(solution)/shard_map/ppermute | solution.py:345
  36.1 2.7 %collective-permute-done.12 = f32[16,256]{1,0:T(8,128)S(1)} collective-permute-done((f32[16,256]{1,0:T(8,128)S(1)}, f32[16,256]{1,0:T(8,128)S(1)}, u32[]{:S(2)}, u32[]{:S(2)}) %collective-permute-start.12) | collective-permute-done | bytes 16416 | tf_op jit(solution)/shard_map/ppermute | solution.py:345
  38.8 1.0 %collective-permute-start.14 = (f32[16,256]{1,0:T(8,128)S(1)}, f32[16,256]{1,0:T(8,128)S(1)}, u32[]{:S(2)}, u32[]{:S(2)}) collective-permute-start(f32[16,256]{1,0:T(8,128)S(1)} %add_add_fusion.1), channel_id=1, source_target_pairs={{0,4},{4,0},{8,12},{12,8},{16,20},{20,16},{24,28},{28,24},{1,5},{5... | collective-permute-start | bytes 49160 | tf_op jit(solution)/shard_map/ppermute | solution.py:345
  39.8 2.8 %collective-permute-done.14 = f32[16,256]{1,0:T(8,128)S(1)} collective-permute-done((f32[16,256]{1,0:T(8,128)S(1)}, f32[16,256]{1,0:T(8,128)S(1)}, u32[]{:S(2)}, u32[]{:S(2)}) %collective-permute-start.14) | collective-permute-done | bytes 16416 | tf_op jit(solution)/shard_map/ppermute | solution.py:345
  42.6 3.3 %apply.3 = (f32[72,512]{1,0:T(8,128)S(1)}, f32[72,512]{1,0:T(8,128)S(1)}) custom-call(s32[2]{0:T(128)S(1)} %pad_add_fusion.place, bf16[32,4,256,256]{3,2,1,0:T(8,128)(2,1)S(1)} %get-tuple-element.44.k_mat, s32[69]{0:T(128)S(1)} %get-tuple-element.45.refs_0_, s32[69]{0:T(128)S(1)} %get-tuple-element.46.refs_1_.refs_0_, ...), custom_call_target="tpu_custom_call" | custom-call | flops 536870912 | bytes 8388608 | tf_op jit(solution)/shard_map/apply/pallas_call | solution.py:480
  46.0 1.4 %collective-permute-done.15 = f32[72,512]{1,0:T(8,128)S(1)} collective-permute-done((f32[72,512]{1,0:T(8,128)S(1)}, f32[72,512]{1,0:T(8,128)S(1)}, u32[]{:S(2)}, u32[]{:S(2)}) %collective-permute-start.15) | collective-permute-done | bytes 147488 | tf_op jit(solution)/shard_map/ppermute | solution.py:345
  47.4 0.4 collective-permute-start.16
  47.9 5.5 %collective-permute-done.16 = f32[72,512]{1,0:T(8,128)S(1)} collective-permute-done((f32[72,512]{1,0:T(8,128)S(1)}, f32[72,512]{1,0:T(8,128)S(1)}, u32[]{:S(2)}, u32[]{:S(2)}) %collective-permute-start.16) | collective-permute-done | bytes 147488 | tf_op jit(solution)/shard_map/ppermute | solution.py:345
  53.4 1.5 %collective-permute-start.19 = (bf16[32,512]{1,0:T(8,128)(2,1)S(1)}, bf16[32,512]{1,0:T(8,128)(2,1)S(1)}, u32[]{:S(2)}, u32[]{:S(2)}) collective-permute-start(bf16[32,512]{1,0:T(8,128)(2,1)S(1)} %get-tuple-element.62), channel_id=1, source_target_pairs={{0,24},{4,28},{8,16},{12,20},{16,8},{20,12},{24,0},{28,4},{1,25},{... | collective-permute-start | bytes 98312 | tf_op jit(solution)/shard_map/ppermute | solution.py:345
  55.0 0.9 %collective-permute-start.18 = (bf16[32,512]{1,0:T(8,128)(2,1)S(1)}, bf16[32,512]{1,0:T(8,128)(2,1)S(1)}, u32[]{:S(2)}, u32[]{:S(2)}) collective-permute-start(bf16[32,512]{1,0:T(8,128)(2,1)S(1)} %get-tuple-element.62), channel_id=1, source_target_pairs={{0,16},{4,20},{8,24},{12,28},{16,0},{20,4},{24,8},{28,12},{1,17},{... | collective-permute-start | bytes 98312 | tf_op jit(solution)/shard_map/ppermute | solution.py:345
  55.9 2.0 %collective-permute-start.17 = (bf16[32,512]{1,0:T(8,128)(2,1)S(1)}, bf16[32,512]{1,0:T(8,128)(2,1)S(1)}, u32[]{:S(2)}, u32[]{:S(2)}) collective-permute-start(bf16[32,512]{1,0:T(8,128)(2,1)S(1)} %get-tuple-element.62), channel_id=1, source_target_pairs={{0,8},{4,12},{8,0},{12,4},{16,24},{20,28},{24,16},{28,20},{1,9},{5... | collective-permute-start | bytes 98312 | tf_op jit(solution)/shard_map/ppermute | solution.py:345
  57.9 1.4 %collective-permute-done.19 = bf16[32,512]{1,0:T(8,128)(2,1)S(1)} collective-permute-done((bf16[32,512]{1,0:T(8,128)(2,1)S(1)}, bf16[32,512]{1,0:T(8,128)(2,1)S(1)}, u32[]{:S(2)}, u32[]{:S(2)}) %collective-permute-start.19) | collective-permute-done | bytes 32800 | tf_op jit(solution)/shard_map/ppermute | solution.py:345
  59.4 0.4 collective-permute-done.18
  60.2 0.7 collective-permute-start.20
  61.0 1.9 %apply.4.refs_2_ = f32[8,32,256]{2,1,0:T(8,128)S(1)} custom-call(s32[2]{0:T(128)S(1)} %pad_add_fusion.place, bf16[32,4,256,256]{3,2,1,0:T(8,128)(2,1)S(1)} %get-tuple-element.44.k_mat, s32[69]{0:T(128)S(1)} %get-tuple-element.45.refs_0_, bf16[4,32,512]{2,1,0:T(8,128)(2,1)S(1)} %pad_maximum_fusion.2.refs_1_), custom_call_target="tpu_custom_call" | custom-call | flops 268435456 | bytes 4194304 | tf_op jit(solution)/shard_map/apply/pallas_call | solution.py:480
  62.9 3.2 %collective-permute-done.20.refs_1_ = bf16[4,32,512]{2,1,0:T(8,128)(2,1)S(1)} collective-permute-done((bf16[4,32,512]{2,1,0:T(8,128)(2,1)S(1)}, bf16[4,32,512]{2,1,0:T(8,128)(2,1)S(1)}, u32[]{:S(2)}, u32[]{:S(2)}) %collective-permute-start.20) | collective-permute-done | bytes 131104 | tf_op jit(solution)/shard_map/ppermute | solution.py:345
  66.1 2.1 %apply.5 = (f32[32,512]{1,0:T(8,128)S(1)}, f32[32,512]{1,0:T(8,128)S(1)}, f32[2,32,512]{2,1,0:T(8,128)S(1)}, f32[32,128]{1,0:T(8,128)S(1)}) custom-call(s32[2]{0:T(128)S(1)} %pad_add_fusion.place, bf16[32,4,256,256]{3,2,1,0:T(8,128)(2,1)S(1)} %get-tuple-element.44.k_mat, s32[69]{0:T(128)S(1)} %get-tuple-element.46.refs_1_.refs_0_, ...), custom_call_target="tpu_custom_call" | custom-call | flops 268435456 | bytes 4194304 | tf_op jit(solution)/shard_map/apply/pallas_call | solution.py:480
  68.3 1.3 %collective-permute-done.22 = f32[2,32,512]{2,1,0:T(8,128)S(1)} collective-permute-done((f32[2,32,512]{2,1,0:T(8,128)S(1)}, f32[2,32,512]{2,1,0:T(8,128)S(1)}, u32[]{:S(2)}, u32[]{:S(2)}) %collective-permute-start.22) | collective-permute-done | bytes 131104 | tf_op jit(solution)/shard_map/ppermute | solution.py:345
  69.9 2.5 %collective-permute-start.29 = (f32[32,128]{1,0:T(8,128)S(1)}, f32[32,128]{1,0:T(8,128)S(1)}, u32[]{:S(2)}, u32[]{:S(2)}) collective-permute-start(f32[32,128]{1,0:T(8,128)S(1)} %get-tuple-element.61), channel_id=1, source_target_pairs={{0,24},{4,28},{8,16},{12,20},{16,8},{20,12},{24,0},{28,4},{1,25},{... | collective-permute-start | bytes 49160 | tf_op jit(solution)/shard_map/ppermute | solution.py:345
  72.3 0.9 %collective-permute-start.28 = (f32[32,128]{1,0:T(8,128)S(1)}, f32[32,128]{1,0:T(8,128)S(1)}, u32[]{:S(2)}, u32[]{:S(2)}) collective-permute-start(f32[32,128]{1,0:T(8,128)S(1)} %get-tuple-element.61), channel_id=1, source_target_pairs={{0,16},{4,20},{8,24},{12,28},{16,0},{20,4},{24,8},{28,12},{1,17},{... | collective-permute-start | bytes 49160 | tf_op jit(solution)/shard_map/ppermute | solution.py:345
  73.2 1.0 %collective-permute-start.27 = (f32[32,128]{1,0:T(8,128)S(1)}, f32[32,128]{1,0:T(8,128)S(1)}, u32[]{:S(2)}, u32[]{:S(2)}) collective-permute-start(f32[32,128]{1,0:T(8,128)S(1)} %get-tuple-element.61), channel_id=1, source_target_pairs={{0,8},{4,12},{8,0},{12,4},{16,24},{20,28},{24,16},{28,20},{1,9},{5... | collective-permute-start | bytes 49160 | tf_op jit(solution)/shard_map/ppermute | solution.py:345
  74.3 0.6 collective-permute-start.26
  74.9 1.4 %collective-permute-start.25 = (f32[32,512]{1,0:T(8,128)S(1)}, f32[32,512]{1,0:T(8,128)S(1)}, u32[]{:S(2)}, u32[]{:S(2)}) collective-permute-start(f32[32,512]{1,0:T(8,128)S(1)} %fusion.4.refs_0_), channel_id=1, source_target_pairs={{0,2},{1,3},{2,0},{3,1},{4,6},{5,7},{6,4},{7,5},{8,10},{9,11},{10,... | collective-permute-start | bytes 196616 | tf_op jit(solution)/shard_map/ppermute | solution.py:345
  76.4 0.6 collective-permute-done.28
  77.1 1.1 %collective-permute-start.30 = (f32[32,128]{1,0:T(8,128)S(1)}, f32[32,128]{1,0:T(8,128)S(1)}, u32[]{:S(2)}, u32[]{:S(2)}) collective-permute-start(f32[32,128]{1,0:T(8,128)S(1)} %add_add_fusion), channel_id=1, source_target_pairs={{0,4},{4,0},{8,12},{12,8},{16,20},{20,16},{24,28},{28,24},{1,5},{5... | collective-permute-start | bytes 49160 | tf_op jit(solution)/shard_map/ppermute | solution.py:345
  78.2 2.7 %collective-permute-done.30 = f32[32,128]{1,0:T(8,128)S(1)} collective-permute-done((f32[32,128]{1,0:T(8,128)S(1)}, f32[32,128]{1,0:T(8,128)S(1)}, u32[]{:S(2)}, u32[]{:S(2)}) %collective-permute-start.30) | collective-permute-done | bytes 16416 | tf_op jit(solution)/shard_map/ppermute | solution.py:345
  80.9 2.0 %collective-permute-start.32 = (f32[32,128]{1,0:T(8,128)S(1)}, f32[32,128]{1,0:T(8,128)S(1)}, u32[]{:S(2)}, u32[]{:S(2)}) collective-permute-start(f32[32,128]{1,0:T(8,128)S(1)} %add.86.refs_4_), channel_id=1, source_target_pairs={{0,2},{1,3},{2,0},{3,1},{4,6},{5,7},{6,4},{7,5},{8,10},{9,11},{10,... | collective-permute-start | bytes 49160 | tf_op jit(solution)/shard_map/ppermute | solution.py:345
  83.0 1.1 %collective-permute-done.33.refs_7_ = f32[32,128]{1,0:T(8,128)S(1)} collective-permute-done((f32[32,128]{1,0:T(8,128)S(1)}, f32[32,128]{1,0:T(8,128)S(1)}, u32[]{:S(2)}, u32[]{:S(2)}) %collective-permute-start.33) | collective-permute-done | bytes 16416 | tf_op jit(solution)/shard_map/ppermute | solution.py:345
  84.1 0.3 collective-permute-start.31
  84.4 0.4 collective-permute-done.32.refs_6_
  84.8 0.5 collective-permute-done.31.refs_5_
  85.3 1.7 %final.1 = (f32[32,2048]{1,0:T(8,128)}, f32[32,2048]{1,0:T(8,128)}) custom-call(s32[2]{0:T(128)S(1)} %pad_add_fusion.place, f32[32,2048]{1,0:T(8,128)S(1)} %copy-done, f32[2,40,512]{2,1,0:T(8,128)S(1)} %pad_maximum_fusion.1.refs_4_.s1_own, f32[2,40,512]{2,1,0:T(8,128)S(1)} %collective-permute-done.21.refs_5_.s1_got, f32[32,512]{1,0:T(8,128)S(1)} %fusion.4.refs_0_, ...), custom_call_target="tpu_custom_call" | custom-call | tf_op jit(solution)/shard_map/final/pallas_call | solution.py:537
  (61 shorter events, 2.1 us)
Async XLA Ops:
  0.6 5.7 %collective-permute-start = (s32[8,6]{1,0:T(8,128)}, s32[8,6]{1,0:T(8,128)S(1)}, u32[]{:S(2)}, u32[]{:S(2)}) collective-permute-start(s32[8,6]{1,0:T(8,128)} %param.3), channel_id=1, source_target_pairs={{0,1},{1,0},{2,3},{3,2},{4,5},{5,4},{6,7},{7,6},{8,9},{9,8},{10,11... | collective-permute-start | bytes 584 | tf_op jit(solution)/shard_map/ppermute | solution.py:345
  1.1 5.3 %collective-permute-start.2 = (s32[8,6]{1,0:T(8,128)}, s32[8,6]{1,0:T(8,128)S(1)}, u32[]{:S(2)}, u32[]{:S(2)}) collective-permute-start(s32[8,6]{1,0:T(8,128)} %param.3), channel_id=1, source_target_pairs={{0,3},{1,2},{2,1},{3,0},{4,7},{5,6},{6,5},{7,4},{8,11},{9,10},{10,... | collective-permute-start | bytes 584 | tf_op jit(solution)/shard_map/ppermute | solution.py:345
  3.8 3.8 %collective-permute-start.1 = (s32[8,6]{1,0:T(8,128)}, s32[8,6]{1,0:T(8,128)S(1)}, u32[]{:S(2)}, u32[]{:S(2)}) collective-permute-start(s32[8,6]{1,0:T(8,128)} %param.3), channel_id=1, source_target_pairs={{0,2},{1,3},{2,0},{3,1},{4,6},{5,7},{6,4},{7,5},{8,10},{9,11},{10,... | collective-permute-start | bytes 584 | tf_op jit(solution)/shard_map/ppermute | solution.py:345
  7.9 8.1 %collective-permute-start.5 = (bf16[16,640]{1,0:T(8,128)(2,1)S(1)}, bf16[16,640]{1,0:T(8,128)(2,1)S(1)}, u32[]{:S(2)}, u32[]{:S(2)}) collective-permute-start(bf16[16,640]{1,0:T(8,128)(2,1)S(1)} %pad_maximum_fusion.4), channel_id=1, source_target_pairs={{0,24},{4,28},{8,16},{12,20},{16,8},{20,12},{24,0},{28,4},{1,25},{... | collective-permute-start | bytes 61448 | tf_op jit(solution)/shard_map/ppermute | solution.py:345
  11.6 5.2 %collective-permute-start.4 = (bf16[16,640]{1,0:T(8,128)(2,1)S(1)}, bf16[16,640]{1,0:T(8,128)(2,1)S(1)}, u32[]{:S(2)}, u32[]{:S(2)}) collective-permute-start(bf16[16,640]{1,0:T(8,128)(2,1)S(1)} %pad_maximum_fusion.4), channel_id=1, source_target_pairs={{0,16},{4,20},{8,24},{12,28},{16,0},{20,4},{24,8},{28,12},{1,17},{... | collective-permute-start | bytes 61448 | tf_op jit(solution)/shard_map/ppermute | solution.py:345
  11.6 5.2 %collective-permute-start.3 = (bf16[16,640]{1,0:T(8,128)(2,1)S(1)}, bf16[16,640]{1,0:T(8,128)(2,1)S(1)}, u32[]{:S(2)}, u32[]{:S(2)}) collective-permute-start(bf16[16,640]{1,0:T(8,128)(2,1)S(1)} %pad_maximum_fusion.4), channel_id=1, source_target_pairs={{0,8},{4,12},{8,0},{12,4},{16,24},{20,28},{24,16},{28,20},{1,9},{5... | collective-permute-start | bytes 61448 | tf_op jit(solution)/shard_map/ppermute | solution.py:345
  12.3 11.7 %collective-permute-start.9 = (f32[32,512]{1,0:T(8,128)S(1)}, f32[32,512]{1,0:T(8,128)S(1)}, u32[]{:S(2)}, u32[]{:S(2)}) collective-permute-start(f32[32,512]{1,0:T(8,128)S(1)} %constant_dynamic-slice_fusion), channel_id=1, source_target_pairs={{0,24},{4,28},{8,16},{12,20},{16,8},{20,12},{24,0},{28,4},{1,25},{... | collective-permute-start | bytes 196616 | tf_op jit(solution)/shard_map/ppermute | solution.py:345
  15.9 8.1 %collective-permute-start.8 = (f32[32,512]{1,0:T(8,128)S(1)}, f32[32,512]{1,0:T(8,128)S(1)}, u32[]{:S(2)}, u32[]{:S(2)}) collective-permute-start(f32[32,512]{1,0:T(8,128)S(1)} %constant_dynamic-slice_fusion), channel_id=1, source_target_pairs={{0,16},{4,20},{8,24},{12,28},{16,0},{20,4},{24,8},{28,12},{1,17},{... | collective-permute-start | bytes 196616 | tf_op jit(solution)/shard_map/ppermute | solution.py:345
  15.9 8.1 %collective-permute-start.7 = (f32[32,512]{1,0:T(8,128)S(1)}, f32[32,512]{1,0:T(8,128)S(1)}, u32[]{:S(2)}, u32[]{:S(2)}) collective-permute-start(f32[32,512]{1,0:T(8,128)S(1)} %constant_dynamic-slice_fusion), channel_id=1, source_target_pairs={{0,8},{4,12},{8,0},{12,4},{16,24},{20,28},{24,16},{28,20},{1,9},{5... | collective-permute-start | bytes 196616 | tf_op jit(solution)/shard_map/ppermute | solution.py:345
  16.8 7.3 %collective-permute-start.6 = (bf16[4,16,640]{2,1,0:T(8,128)(2,1)S(1)}, bf16[4,16,640]{2,1,0:T(8,128)(2,1)S(1)}, u32[]{:S(2)}, u32[]{:S(2)}) collective-permute-start(bf16[4,16,640]{2,1,0:T(8,128)(2,1)S(1)} %pad_maximum_fusion.3.refs_1_), channel_id=1, source_target_pairs={{0,4},{4,0},{8,12},{12,8},{16,20},{20,16},{24,28},{28,24},{1,5},{5... | collective-permute-start | bytes 245768 | tf_op jit(solution)/shard_map/ppermute | solution.py:345
  24.1 6.4 %collective-permute-start.10 = (f32[4,32,512]{2,1,0:T(8,128)S(1)}, f32[4,32,512]{2,1,0:T(8,128)S(1)}, u32[]{:S(2)}, u32[]{:S(2)}) collective-permute-start(f32[4,32,512]{2,1,0:T(8,128)S(1)} %pad_maximum_fusion.refs_2_), channel_id=1, source_target_pairs={{0,4},{4,0},{8,12},{12,8},{16,20},{20,16},{24,28},{28,24},{1,5},{5... | collective-permute-start | bytes 786440 | tf_op jit(solution)/shard_map/ppermute | solution.py:345
  24.2 29.2 %copy-start = (f32[32,2048]{1,0:T(8,128)S(1)}, f32[32,2048]{1,0:T(8,128)}, u32[]{:S(2)}) copy-start(f32[32,2048]{1,0:T(8,128)} %t_ref.1) | copy-start | bytes 786436
  30.5 5.5 %collective-permute-start.13 = (f32[16,256]{1,0:T(8,128)S(1)}, f32[16,256]{1,0:T(8,128)S(1)}, u32[]{:S(2)}, u32[]{:S(2)}) collective-permute-start(f32[16,256]{1,0:T(8,128)S(1)} %get-tuple-element.50), channel_id=1, source_target_pairs={{0,24},{4,28},{8,16},{12,20},{16,8},{20,12},{24,0},{28,4},{1,25},{... | collective-permute-start | bytes 49160 | tf_op jit(solution)/shard_map/ppermute | solution.py:345
  34.1 4.6 %collective-permute-start.12 = (f32[16,256]{1,0:T(8,128)S(1)}, f32[16,256]{1,0:T(8,128)S(1)}, u32[]{:S(2)}, u32[]{:S(2)}) collective-permute-start(f32[16,256]{1,0:T(8,128)S(1)} %get-tuple-element.50), channel_id=1, source_target_pairs={{0,16},{4,20},{8,24},{12,28},{16,0},{20,4},{24,8},{28,12},{1,17},{... | collective-permute-start | bytes 49160 | tf_op jit(solution)/shard_map/ppermute | solution.py:345
  34.1 4.6 %collective-permute-start.11 = (f32[16,256]{1,0:T(8,128)S(1)}, f32[16,256]{1,0:T(8,128)S(1)}, u32[]{:S(2)}, u32[]{:S(2)}) collective-permute-start(f32[16,256]{1,0:T(8,128)S(1)} %get-tuple-element.50), channel_id=1, source_target_pairs={{0,8},{4,12},{8,0},{12,4},{16,24},{20,28},{24,16},{28,20},{1,9},{5... | collective-permute-start | bytes 49160 | tf_op jit(solution)/shard_map/ppermute | solution.py:345
  38.8 3.8 %collective-permute-start.14 = (f32[16,256]{1,0:T(8,128)S(1)}, f32[16,256]{1,0:T(8,128)S(1)}, u32[]{:S(2)}, u32[]{:S(2)}) collective-permute-start(f32[16,256]{1,0:T(8,128)S(1)} %add_add_fusion.1), channel_id=1, source_target_pairs={{0,4},{4,0},{8,12},{12,8},{16,20},{20,16},{24,28},{28,24},{1,5},{5... | collective-permute-start | bytes 49160 | tf_op jit(solution)/shard_map/ppermute | solution.py:345
  46.0 1.4 %collective-permute-start.15 = (f32[72,512]{1,0:T(8,128)S(1)}, f32[72,512]{1,0:T(8,128)S(1)}, u32[]{:S(2)}, u32[]{:S(2)}) collective-permute-start(f32[72,512]{1,0:T(8,128)S(1)} %get-tuple-element.52), channel_id=1, source_target_pairs={{0,1},{1,0},{2,3},{3,2},{4,5},{5,4},{6,7},{7,6},{8,9},{9,8},{10,11... | collective-permute-start | bytes 442376 | tf_op jit(solution)/shard_map/ppermute | solution.py:345
  47.4 6.0 %collective-permute-start.16 = (f32[72,512]{1,0:T(8,128)S(1)}, f32[72,512]{1,0:T(8,128)S(1)}, u32[]{:S(2)}, u32[]{:S(2)}) collective-permute-start(f32[72,512]{1,0:T(8,128)S(1)} %add.76), channel_id=1, source_target_pairs={{0,2},{1,3},{2,0},{3,1},{4,6},{5,7},{6,4},{7,5},{8,10},{9,11},{10,... | collective-permute-start | bytes 442376 | tf_op jit(solution)/shard_map/ppermute | solution.py:345
  53.4 5.9 %collective-permute-start.19 = (bf16[32,512]{1,0:T(8,128)(2,1)S(1)}, bf16[32,512]{1,0:T(8,128)(2,1)S(1)}, u32[]{:S(2)}, u32[]{:S(2)}) collective-permute-start(bf16[32,512]{1,0:T(8,128)(2,1)S(1)} %get-tuple-element.62), channel_id=1, source_target_pairs={{0,24},{4,28},{8,16},{12,20},{16,8},{20,12},{24,0},{28,4},{1,25},{... | collective-permute-start | bytes 98312 | tf_op jit(solution)/shard_map/ppermute | solution.py:345
  55.0 4.8 %collective-permute-start.18 = (bf16[32,512]{1,0:T(8,128)(2,1)S(1)}, bf16[32,512]{1,0:T(8,128)(2,1)S(1)}, u32[]{:S(2)}, u32[]{:S(2)}) collective-permute-start(bf16[32,512]{1,0:T(8,128)(2,1)S(1)} %get-tuple-element.62), channel_id=1, source_target_pairs={{0,16},{4,20},{8,24},{12,28},{16,0},{20,4},{24,8},{28,12},{1,17},{... | collective-permute-start | bytes 98312 | tf_op jit(solution)/shard_map/ppermute | solution.py:345
  55.9 4.3 %collective-permute-start.17 = (bf16[32,512]{1,0:T(8,128)(2,1)S(1)}, bf16[32,512]{1,0:T(8,128)(2,1)S(1)}, u32[]{:S(2)}, u32[]{:S(2)}) collective-permute-start(bf16[32,512]{1,0:T(8,128)(2,1)S(1)} %get-tuple-element.62), channel_id=1, source_target_pairs={{0,8},{4,12},{8,0},{12,4},{16,24},{20,28},{24,16},{28,20},{1,9},{5... | collective-permute-start | bytes 98312 | tf_op jit(solution)/shard_map/ppermute | solution.py:345
  60.1 6.0 %collective-permute-start.21 = (f32[2,40,512]{2,1,0:T(8,128)S(1)}, f32[2,40,512]{2,1,0:T(8,128)S(1)}, u32[]{:S(2)}, u32[]{:S(2)}) collective-permute-start(f32[2,40,512]{2,1,0:T(8,128)S(1)} %pad_maximum_fusion.1.refs_4_.s1_own), channel_id=1, source_target_pairs={{0,1},{1,0},{2,3},{3,2},{4,5},{5,4},{6,7},{7,6},{8,9},{9,8},{10,11... | collective-permute-start | bytes 491528 | tf_op jit(solution)/shard_map/ppermute | solution.py:345
  60.2 5.9 %collective-permute-start.20 = (bf16[4,32,512]{2,1,0:T(8,128)(2,1)S(1)}, bf16[4,32,512]{2,1,0:T(8,128)(2,1)S(1)}, u32[]{:S(2)}, u32[]{:S(2)}) collective-permute-start(bf16[4,32,512]{2,1,0:T(8,128)(2,1)S(1)} %pad_maximum_fusion.2.refs_1_), channel_id=1, source_target_pairs={{0,4},{4,0},{8,12},{12,8},{16,20},{20,16},{24,28},{28,24},{1,5},{5... | collective-permute-start | bytes 393224 | tf_op jit(solution)/shard_map/ppermute | solution.py:345
  68.2 1.4 %collective-permute-start.22 = (f32[2,32,512]{2,1,0:T(8,128)S(1)}, f32[2,32,512]{2,1,0:T(8,128)S(1)}, u32[]{:S(2)}, u32[]{:S(2)}) collective-permute-start(f32[2,32,512]{2,1,0:T(8,128)S(1)} %get-tuple-element.59), channel_id=1, source_target_pairs={{0,1},{1,0},{2,3},{3,2},{4,5},{5,4},{6,7},{7,6},{8,9},{9,8},{10,11... | collective-permute-start | bytes 393224 | tf_op jit(solution)/shard_map/ppermute | solution.py:345
  69.7 4.6 %collective-permute-start.23 = (f32[32,512]{1,0:T(8,128)S(1)}, f32[32,512]{1,0:T(8,128)S(1)}, u32[]{:S(2)}, u32[]{:S(2)}) collective-permute-start(f32[32,512]{1,0:T(8,128)S(1)} %fusion), channel_id=1, source_target_pairs={{0,2},{1,3},{2,0},{3,1},{4,6},{5,7},{6,4},{7,5},{8,10},{9,11},{10,... | collective-permute-start | bytes 196616 | tf_op jit(solution)/shard_map/ppermute | solution.py:345
  69.9 6.5 %collective-permute-start.29 = (f32[32,128]{1,0:T(8,128)S(1)}, f32[32,128]{1,0:T(8,128)S(1)}, u32[]{:S(2)}, u32[]{:S(2)}) collective-permute-start(f32[32,128]{1,0:T(8,128)S(1)} %get-tuple-element.61), channel_id=1, source_target_pairs={{0,24},{4,28},{8,16},{12,20},{16,8},{20,12},{24,0},{28,4},{1,25},{... | collective-permute-start | bytes 49160 | tf_op jit(solution)/shard_map/ppermute | solution.py:345
  72.3 4.6 %collective-permute-start.28 = (f32[32,128]{1,0:T(8,128)S(1)}, f32[32,128]{1,0:T(8,128)S(1)}, u32[]{:S(2)}, u32[]{:S(2)}) collective-permute-start(f32[32,128]{1,0:T(8,128)S(1)} %get-tuple-element.61), channel_id=1, source_target_pairs={{0,16},{4,20},{8,24},{12,28},{16,0},{20,4},{24,8},{28,12},{1,17},{... | collective-permute-start | bytes 49160 | tf_op jit(solution)/shard_map/ppermute | solution.py:345
  73.2 3.9 %collective-permute-start.27 = (f32[32,128]{1,0:T(8,128)S(1)}, f32[32,128]{1,0:T(8,128)S(1)}, u32[]{:S(2)}, u32[]{:S(2)}) collective-permute-start(f32[32,128]{1,0:T(8,128)S(1)} %get-tuple-element.61), channel_id=1, source_target_pairs={{0,8},{4,12},{8,0},{12,4},{16,24},{20,28},{24,16},{28,20},{1,9},{5... | collective-permute-start | bytes 49160 | tf_op jit(solution)/shard_map/ppermute | solution.py:345
  74.3 11.0 %collective-permute-start.26 = (f32[32,512]{1,0:T(8,128)S(1)}, f32[32,512]{1,0:T(8,128)S(1)}, u32[]{:S(2)}, u32[]{:S(2)}) collective-permute-start(f32[32,512]{1,0:T(8,128)S(1)} %fusion.4.refs_0_), channel_id=1, source_target_pairs={{0,3},{1,2},{2,1},{3,0},{4,7},{5,6},{6,5},{7,4},{8,11},{9,10},{10,... | collective-permute-start | bytes 196616 | tf_op jit(solution)/shard_map/ppermute | solution.py:345
  74.9 10.4 %collective-permute-start.25 = (f32[32,512]{1,0:T(8,128)S(1)}, f32[32,512]{1,0:T(8,128)S(1)}, u32[]{:S(2)}, u32[]{:S(2)}) collective-permute-start(f32[32,512]{1,0:T(8,128)S(1)} %fusion.4.refs_0_), channel_id=1, source_target_pairs={{0,2},{1,3},{2,0},{3,1},{4,6},{5,7},{6,4},{7,5},{8,10},{9,11},{10,... | collective-permute-start | bytes 196616 | tf_op jit(solution)/shard_map/ppermute | solution.py:345
  76.3 9.0 %collective-permute-start.24 = (f32[32,512]{1,0:T(8,128)S(1)}, f32[32,512]{1,0:T(8,128)S(1)}, u32[]{:S(2)}, u32[]{:S(2)}) collective-permute-start(f32[32,512]{1,0:T(8,128)S(1)} %fusion.4.refs_0_), channel_id=1, source_target_pairs={{0,1},{1,0},{2,3},{3,2},{4,5},{5,4},{6,7},{7,6},{8,9},{9,8},{10,11... | collective-permute-start | bytes 196616 | tf_op jit(solution)/shard_map/ppermute | solution.py:345
  77.1 3.8 %collective-permute-start.30 = (f32[32,128]{1,0:T(8,128)S(1)}, f32[32,128]{1,0:T(8,128)S(1)}, u32[]{:S(2)}, u32[]{:S(2)}) collective-permute-start(f32[32,128]{1,0:T(8,128)S(1)} %add_add_fusion), channel_id=1, source_target_pairs={{0,4},{4,0},{8,12},{12,8},{16,20},{20,16},{24,28},{28,24},{1,5},{5... | collective-permute-start | bytes 49160 | tf_op jit(solution)/shard_map/ppermute | solution.py:345
  80.9 3.2 %collective-permute-start.33 = (f32[32,128]{1,0:T(8,128)S(1)}, f32[32,128]{1,0:T(8,128)S(1)}, u32[]{:S(2)}, u32[]{:S(2)}) collective-permute-start(f32[32,128]{1,0:T(8,128)S(1)} %add.86.refs_4_), channel_id=1, source_target_pairs={{0,3},{1,2},{2,1},{3,0},{4,7},{5,6},{6,5},{7,4},{8,11},{9,10},{10,... | collective-permute-start | bytes 49160 | tf_op jit(solution)/shard_map/ppermute | solution.py:345
  80.9 3.8 %collective-permute-start.32 = (f32[32,128]{1,0:T(8,128)S(1)}, f32[32,128]{1,0:T(8,128)S(1)}, u32[]{:S(2)}, u32[]{:S(2)}) collective-permute-start(f32[32,128]{1,0:T(8,128)S(1)} %add.86.refs_4_), channel_id=1, source_target_pairs={{0,2},{1,3},{2,0},{3,1},{4,6},{5,7},{6,4},{7,5},{8,10},{9,11},{10,... | collective-permute-start | bytes 49160 | tf_op jit(solution)/shard_map/ppermute | solution.py:345
  84.1 1.2 %collective-permute-start.31 = (f32[32,128]{1,0:T(8,128)S(1)}, f32[32,128]{1,0:T(8,128)S(1)}, u32[]{:S(2)}, u32[]{:S(2)}) collective-permute-start(f32[32,128]{1,0:T(8,128)S(1)} %add.86.refs_4_), channel_id=1, source_target_pairs={{0,1},{1,0},{2,3},{3,2},{4,5},{5,4},{6,7},{7,6},{8,9},{9,8},{10,11... | collective-permute-start | bytes 49160 | tf_op jit(solution)/shard_map/ppermute | solution.py:345

commit v6 on v5

--- a/solution.py
+++ b/solution.py
@@ -206,11 +206,9 @@
     products = finish and not scaled
     if products:
         t_ref, s_refs, refs = refs[0], pieces_of(refs[1], refs[2]), refs[3:]
-    if products:
-        near, near_y, cross, dot_ref, z_acc, refs = *refs[:5], refs[5:]
+    if finish:
+        near, near_y, cross, extra, z_acc, refs = *refs[:5], refs[5:]
         z_refs = (near, cross.at[0], near_y, cross.at[1])
-    elif finish:
-        near, cross, z_acc, refs = *refs[:3], refs[3:]
     else:
         z_acc, refs = refs[0], refs[1:]
     w_all, refs = refs[0], refs[1:]
@@ -275,15 +273,9 @@
         return
     own_len = own_rows * block_len
     if scaled:
-        outputs = (near.shape[0] - 8) // 2
-        z_refs = [
-            ref.at[pl.ds(outputs * h, outputs)] for h in range(2) for ref in (near, cross)
-        ]
         for k in range(own_rows):
-            cols = slice(k * block_len, (k + 1) * block_len)
             mine = inv_ref[pl.ds(place[0] * own_rows + k, 1), :]
-            near[2 * outputs:, cols] = jnp.broadcast_to(mine, (8, block_len))
-        cross[2 * outputs:, :] = jnp.zeros((8, own_len), F32)
+            extra[:, k * block_len:(k + 1) * block_len] = jnp.broadcast_to(mine, (8, block_len))
     for e in range(4):
         for k in range(own_rows):
             z_refs[e][:, k * block_len:(k + 1) * block_len] = z_acc[(col ^ e) * own_rows + k]
@@ -307,14 +299,14 @@
         out = jnp.zeros(lane.shape, F32)
         for n, v in enumerate((tt, ts1, s1s1, ts2, s1s2)):
             out = jnp.where(lane == n, v, out)
-        dot_ref[...] = out
+        extra[...] = out
 
 
 def final_kernel(place, t_ref, s1_own, s1_got, *refs):
-    s2s, all_dots = refs[:4], refs[4:8]
-    sol_hbm, res_hbm, sol_ref, res_ref, sems = refs[8:]
+    grown, all_dots = pieces_of(refs[0], refs[1]), refs[2:6]
+    sol_hbm, res_hbm, sol_ref, res_ref, sems = refs[6:]
     s1s = pieces_of(s1_own, s1_got)
-    outputs, own_len = s2s[0].shape
+    outputs, own_len = grown[0].shape
     dots = pair_sum([ref[...] for ref in all_dots])
     tt, ts1, s1s1, ts2, s1s2 = (dots[:, n:n + 1] for n in range(5))
     a1 = tt / (REG * tt + ts1)
@@ -329,7 +321,8 @@
     copies = []
     for e in range(4):
         at = pl.ds(pl.multiple_of((place[1] ^ e) * own_len, LANES), own_len)
-        t, s1, s2 = t_ref[:, at], s1s[e][:outputs, :], s2s[e][...]
+        t, s1 = t_ref[:, at], s1s[e][:outputs, :]
+        s2 = grown[e][...] + SHIFT * s1
         sol_ref[e] = sol_t * t - sol_1 * s1
         res_ref[e] = res_t * t - res_1 * s1 + sol_1 * s2
         for n, (ref, hbm) in enumerate(((sol_ref, sol_hbm), (res_ref, res_hbm))):
@@ -470,11 +463,9 @@
         specs = [k_spec] + [SMEM] * len(use) + [VMEM] * len(pieces)
         more = [x for x in (inv, z_in) if x is not None] + list(products)
         z_shape = (block_rows, outputs, block_len)
-        if products:
-            out = [shape(outputs, own_len), shape(outputs, own_len), shape(2, outputs, own_len)]
-            out += [shape(outputs, LANES)]
-        elif finish:
-            out = [shape(2 * outputs + 8, own_len)] * 2
+        if finish:
+            out = [shape(outputs, own_len)] * 2 + [shape(2, outputs, own_len)]
+            out += [shape(outputs, LANES) if products else shape(8, own_len)]
         else:
             out = [shape(*z_shape)]
         return pl.pallas_call(
@@ -497,16 +488,17 @@
             name="apply",
         )(place, *operands, *more)
 
-    near_z, cross_z = apply(tuple(range(parts)), t_pieces, inv=inv)
-    half = near_z + swap(cross_z, "cols", 1)
-    far = swap(half, "cols", 2)
-    lo, hi, tail = slice(0, outputs), slice(outputs, 2 * outputs), slice(2 * outputs, None)
-    own_inv, far_inv = half[2 * outputs:2 * outputs + 1], far[2 * outputs:2 * outputs + 1]
-    s1 = (half[lo] + far[hi]) * own_inv
+    near_z, near_y, cross_z, tail = apply(tuple(range(parts)), t_pieces, inv=inv)
+    got = swap(cross_z, "cols", 1)
+    half, half_y = near_z + got[0], near_y + got[1]
+    own_inv = tail[:1]
+    s1 = (half + swap(half_y, "cols", 2)) * own_inv
     g = ((s1 - SHIFT * own_t) * own_inv).astype(BF16)
+    g, half, half_y = lax.optimization_barrier((g, half, half_y))
+    far = swap(jnp.concatenate([half, tail], axis=0), "cols", 2)
     s1_own = jnp.stack([
-        jnp.concatenate([s1, half[tail]], axis=0),
-        jnp.concatenate([(half[hi] + far[lo]) * far_inv, far[tail]], axis=0),
+        jnp.concatenate([s1, tail], axis=0),
+        jnp.concatenate([(half_y + far[:outputs]) * far[outputs:outputs + 1], far[outputs:]], axis=0),
     ])
     held_t = pltpu.with_memory_space_constraint(targets, pltpu.VMEM)
     if direct_rows:
@@ -516,28 +508,32 @@
         s1_got = swap(s1_own, "cols", 1)
         (z_part,) = apply((0,), [g_same], finish=False)
         z_part, g_other, s1_got = lax.optimization_barrier((z_part, g_other, s1_got))
-        near_z, near_y, cross_z, dots = apply(
+        *z2, dots = apply(
             (1,), [g_other], z_in=z_part, products=[held_t, s1_own, s1_got]
         )
         dots = pair_sum(along_z(dots))
     else:
         s1_got = swap(s1_own, "cols", 1)
-        near_z, near_y, cross_z, dots = apply(
+        *z2, dots = apply(
             (0,), [lax.all_gather(g, "rows")], products=[held_t, s1_own, s1_got]
         )
-    got = swap(cross_z, "cols", 1)
-    z2 = near_z + got[0] + swap(near_y + got[1], "cols", 2)
-    s2 = direct_cols(z2 * own_inv + SHIFT * s1)
+    got = swap(z2[2], "cols", 1)
+    halves = jnp.stack([z2[0] + got[0], z2[1] + got[1]])
+    halves = lax.reduce_precision(halves, 8, 7)
+    far = swap(halves.astype(BF16), "cols", 2).astype(F32)
+    grown = jnp.stack([
+        (halves[0] + far[1]) * own_inv,
+        (halves[1] + far[0]) * s1_own[1, outputs:outputs + 1],
+    ])
     dots = pair_sum(across_x(dots)) if direct_rows else lax.psum(dots, "rows")
     dots = direct_cols(dots)
-    ends = [
-        pltpu.with_memory_space_constraint(x, pltpu.VMEM) for x in (s1_own, s1_got, *s2, *dots)
-    ]
+    ends = (s1_own, s1_got, grown, swap(grown, "cols", 1), *dots)
+    ends = [pltpu.with_memory_space_constraint(x, pltpu.VMEM) for x in ends]
 
     return pl.pallas_call(
         final_kernel,
         out_shape=(shape(outputs, npoints), shape(outputs, npoints)),
-        in_specs=[SMEM] + [VMEM] * 11,
+        in_specs=[SMEM] + [VMEM] * 9,
         out_specs=(HBM, HBM),
         scratch_shapes=[
             pltpu.VMEM((4, outputs, own_len), F32),

time: 87.6 us -> 86.7 us (0.990)
  starting transfers between devices: 35 us -> 36.3 us
  Pallas kernels: 19.9 us -> 18.7 us
    ppermute x34 -> x33, starting transfers between devices: 35 us -> 36.3 us  [swap(): return lax.ppermute(x, axis, [(i, i ^ d) for i in range(size)])]
    ppermute x34 -> x33, waiting for transfers between devices: 28 us -> 27.3 us  [swap(): return lax.ppermute(x, axis, [(i, i ^ d) for i in range(size)])]
  transfers between devices with their start and end apart: 34 -> 33, of which waited for: 18 -> 17; matrix products, arithmetic and copies ran while one was open for 3% -> 3% of each run, Pallas kernels for 15% -> 14%
where the time goes in v6:
time: 86.7 us; the launch traced here: 86.6 us
  starting transfers between devices  36.3 us (42%)
  waiting for transfers between devices  27.3 us (31%)
  Pallas kernels  18.7 us (22%)
  local copies, waits for them, and re-layouts  2.74 us (3%)
    ppermute x33, starting transfers between devices, swap(): return lax.ppermute(x, axis, [(i, i ^ d) for i in range(size)])  36.3 us
    ppermute x33, waiting for transfers between devices, swap(): return lax.ppermute(x, axis, [(i, i ^ d) for i in range(size)])  27.3 us
    pallas_call x2, Pallas kernels, build(): pl.pallas_call(functools.partial(build_kernel, cfg, part), out_shape=out,...  10.2 us
    pallas_call x3, Pallas kernels, apply(): pl.pallas_call(functools.partial(apply_kernel, cfg, use, inv is not None,...  6.81 us
  transfers between devices with their start and end apart: 33, of which 17 were waited for; matrix products, arithmetic and copies ran while one was open for 3% of the time, Pallas kernels for 14%

profile of v6, /device:TPU:0, one launch (start us, length us, event | category | flops | bytes accessed | tf_op | source)
XLA Modules:
  0.0 86.6 jit_solution(11085435528725573137)
XLA Ops:
  0.6 0.5 collective-permute-start
  1.1 2.6 %collective-permute-start.2 = (s32[8,6]{1,0:T(8,128)}, s32[8,6]{1,0:T(8,128)S(1)}, u32[]{:S(2)}, u32[]{:S(2)}) collective-permute-start(s32[8,6]{1,0:T(8,128)} %param.3), channel_id=1, source_target_pairs={{0,3},{1,2},{2,1},{3,0},{4,7},{5,6},{6,5},{7,4},{8,11},{9,10},{10,... | collective-permute-start | bytes 584 | tf_op jit(solution)/shard_map/ppermute | solution.py:338
  3.8 0.8 copy.6
  4.7 0.7 constant_dynamic-slice_fusion.1
  5.5 0.8 constant_dynamic-slice_fusion
  6.6 1.0 %collective-permute-done.1 = s32[8,6]{1,0:T(8,128)S(1)} collective-permute-done((s32[8,6]{1,0:T(8,128)}, s32[8,6]{1,0:T(8,128)S(1)}, u32[]{:S(2)}, u32[]{:S(2)}) %collective-permute-start.1) | collective-permute-done | bytes 224 | tf_op jit(solution)/shard_map/ppermute | solution.py:338
  7.9 3.7 %collective-permute-start.5 = (bf16[16,640]{1,0:T(8,128)(2,1)S(1)}, bf16[16,640]{1,0:T(8,128)(2,1)S(1)}, u32[]{:S(2)}, u32[]{:S(2)}) collective-permute-start(bf16[16,640]{1,0:T(8,128)(2,1)S(1)} %pad_maximum_fusion.7), channel_id=1, source_target_pairs={{0,24},{4,28},{8,16},{12,20},{16,8},{20,12},{24,0},{28,4},{1,25},{... | collective-permute-start | bytes 61448 | tf_op jit(solution)/shard_map/ppermute | solution.py:338
  11.6 0.8 collective-permute-start.3
  12.3 3.6 %collective-permute-start.9 = (f32[32,512]{1,0:T(8,128)S(1)}, f32[32,512]{1,0:T(8,128)S(1)}, u32[]{:S(2)}, u32[]{:S(2)}) collective-permute-start(f32[32,512]{1,0:T(8,128)S(1)} %constant_dynamic-slice_fusion), channel_id=1, source_target_pairs={{0,24},{4,28},{8,16},{12,20},{16,8},{20,12},{24,0},{28,4},{1,25},{... | collective-permute-start | bytes 196616 | tf_op jit(solution)/shard_map/ppermute | solution.py:338
  15.9 0.8 collective-permute-start.7
  16.8 1.6 %collective-permute-start.6 = (bf16[4,16,640]{2,1,0:T(8,128)(2,1)S(1)}, bf16[4,16,640]{2,1,0:T(8,128)(2,1)S(1)}, u32[]{:S(2)}, u32[]{:S(2)}) collective-permute-start(bf16[4,16,640]{2,1,0:T(8,128)(2,1)S(1)} %pad_maximum_fusion.6.refs_1_), channel_id=1, source_target_pairs={{0,4},{4,0},{8,12},{12,8},{16,20},{20,16},{24,28},{28,24},{1,5},{5... | collective-permute-start | bytes 245768 | tf_op jit(solution)/shard_map/ppermute | solution.py:338
  18.4 5.0 %build.2 = (bf16[32,4,256,256]{3,2,1,0:T(8,128)(2,1)S(1)}, s32[69]{0:T(128)S(1)}, f32[8,256]{1,0:T(8,128)S(1)}, bf16[8,256,32]{2,1,0:T(8,128)(2,1)S(1)}) custom-call(s32[2]{0:T(128)S(1)} %pad_add_fusion.place, s32[8,64]{1,0:T(8,128)S(1)} %add_add_fusion.2.direct, bf16[16,2048]{1,0:T(8,128)(2,1)} %refs_0_.1, bf16[4,16,640]{2,1,0:T(8,128)(2,1)S(1)} %pad_maximum_fusion.6.refs_1_), custom_call_target="tpu_custom_call" | custom-call | flops 268435456 | bytes 8388608 | tf_op jit(solution)/shard_map/build/pallas_call | solution.py:414
  23.5 1.2 %collective-permute-start.10 = (f32[4,32,512]{2,1,0:T(8,128)S(1)}, f32[4,32,512]{2,1,0:T(8,128)S(1)}, u32[]{:S(2)}, u32[]{:S(2)}) collective-permute-start(f32[4,32,512]{2,1,0:T(8,128)S(1)} %pad_maximum_fusion.refs_2_), channel_id=1, source_target_pairs={{0,4},{4,0},{8,12},{12,8},{16,20},{20,16},{24,28},{28,24},{1,5},{5... | collective-permute-start | bytes 786440 | tf_op jit(solution)/shard_map/ppermute | solution.py:338
  24.7 5.2 %build.3 = (bf16[32,4,256,256]{3,2,1,0:T(8,128)(2,1)S(1)}, s32[69]{0:T(128)S(1)}, f32[16,256]{1,0:T(8,128)S(1)}) custom-call(s32[2]{0:T(128)S(1)} %pad_add_fusion.place, s32[8,64]{1,0:T(8,128)S(1)} %add_add_fusion.2.direct, bf16[8,256,32]{2,1,0:T(8,128)(2,1)S(1)} %get-tuple-element.38.refs_0_, ...), custom_call_target="tpu_custom_call", output_to_operand_aliasing={{0}: (5, {})} | custom-call | flops 268435456 | bytes 8388608 | tf_op jit(solution)/shard_map/build/pallas_call | solution.py:414
  30.0 3.9 %collective-permute-start.13 = (f32[16,256]{1,0:T(8,128)S(1)}, f32[16,256]{1,0:T(8,128)S(1)}, u32[]{:S(2)}, u32[]{:S(2)}) collective-permute-start(f32[16,256]{1,0:T(8,128)S(1)} %get-tuple-element.55), channel_id=1, source_target_pairs={{0,24},{4,28},{8,16},{12,20},{16,8},{20,12},{24,0},{28,4},{1,25},{... | collective-permute-start | bytes 49160 | tf_op jit(solution)/shard_map/ppermute | solution.py:338
  33.9 0.6 collective-permute-start.11
  34.4 1.1 %collective-permute-done.13 = f32[16,256]{1,0:T(8,128)S(1)} collective-permute-done((f32[16,256]{1,0:T(8,128)S(1)}, f32[16,256]{1,0:T(8,128)S(1)}, u32[]{:S(2)}, u32[]{:S(2)}) %collective-permute-start.13) | collective-permute-done | bytes 16416 | tf_op jit(solution)/shard_map/ppermute | solution.py:338
  35.6 2.9 %collective-permute-done.12 = f32[16,256]{1,0:T(8,128)S(1)} collective-permute-done((f32[16,256]{1,0:T(8,128)S(1)}, f32[16,256]{1,0:T(8,128)S(1)}, u32[]{:S(2)}, u32[]{:S(2)}) %collective-permute-start.12) | collective-permute-done | bytes 16416 | tf_op jit(solution)/shard_map/ppermute | solution.py:338
  38.5 0.4 collective-permute-start.14
  38.9 3.5 %collective-permute-done.14 = f32[16,256]{1,0:T(8,128)S(1)} collective-permute-done((f32[16,256]{1,0:T(8,128)S(1)}, f32[16,256]{1,0:T(8,128)S(1)}, u32[]{:S(2)}, u32[]{:S(2)}) %collective-permute-start.14) | collective-permute-done | bytes 16416 | tf_op jit(solution)/shard_map/ppermute | solution.py:338
  42.3 3.1 %apply.3 = (f32[32,512]{1,0:T(8,128)S(1)}, f32[32,512]{1,0:T(8,128)S(1)}, f32[2,32,512]{2,1,0:T(8,128)S(1)}, f32[8,512]{1,0:T(8,128)S(1)}) custom-call(s32[2]{0:T(128)S(1)} %pad_add_fusion.place, bf16[32,4,256,256]{3,2,1,0:T(8,128)(2,1)S(1)} %get-tuple-element.49.k_mat, s32[69]{0:T(128)S(1)} %get-tuple-element.50.refs_0_, ...), custom_call_target="tpu_custom_call" | custom-call | flops 536870912 | bytes 8388608 | tf_op jit(solution)/shard_map/apply/pallas_call | solution.py:471
  45.5 1.3 %collective-permute-done.15 = f32[2,32,512]{2,1,0:T(8,128)S(1)} collective-permute-done((f32[2,32,512]{2,1,0:T(8,128)S(1)}, f32[2,32,512]{2,1,0:T(8,128)S(1)}, u32[]{:S(2)}, u32[]{:S(2)}) %collective-permute-start.15) | collective-permute-done | bytes 131104 | tf_op jit(solution)/shard_map/ppermute | solution.py:338
  46.8 1.3 %collective-permute-start.16 = (f32[32,512]{1,0:T(8,128)S(1)}, f32[32,512]{1,0:T(8,128)S(1)}, u32[]{:S(2)}, u32[]{:S(2)}) collective-permute-start(f32[32,512]{1,0:T(8,128)S(1)} %fusion.8), channel_id=1, source_target_pairs={{0,2},{1,3},{2,0},{3,1},{4,6},{5,7},{6,4},{7,5},{8,10},{9,11},{10,... | collective-permute-start | bytes 196616 | tf_op jit(solution)/shard_map/ppermute | solution.py:338
  48.2 3.0 %collective-permute-done.16 = f32[32,512]{1,0:T(8,128)S(1)} collective-permute-done((f32[32,512]{1,0:T(8,128)S(1)}, f32[32,512]{1,0:T(8,128)S(1)}, u32[]{:S(2)}, u32[]{:S(2)}) %collective-permute-start.16) | collective-permute-done | bytes 65568 | tf_op jit(solution)/shard_map/ppermute | solution.py:338
  51.2 1.8 %collective-permute-start.19 = (bf16[32,512]{1,0:T(8,128)(2,1)S(1)}, bf16[32,512]{1,0:T(8,128)(2,1)S(1)}, u32[]{:S(2)}, u32[]{:S(2)}) collective-permute-start(bf16[32,512]{1,0:T(8,128)(2,1)S(1)} %get-tuple-element.60), channel_id=1, source_target_pairs={{0,24},{4,28},{8,16},{12,20},{16,8},{20,12},{24,0},{28,4},{1,25},{... | collective-permute-start | bytes 98312 | tf_op jit(solution)/shard_map/ppermute | solution.py:338
  53.0 0.6 collective-permute-start.18
  53.6 2.0 %collective-permute-start.17 = (bf16[32,512]{1,0:T(8,128)(2,1)S(1)}, bf16[32,512]{1,0:T(8,128)(2,1)S(1)}, u32[]{:S(2)}, u32[]{:S(2)}) collective-permute-start(bf16[32,512]{1,0:T(8,128)(2,1)S(1)} %get-tuple-element.60), channel_id=1, source_target_pairs={{0,8},{4,12},{8,0},{12,4},{16,24},{20,28},{24,16},{28,20},{1,9},{5... | collective-permute-start | bytes 98312 | tf_op jit(solution)/shard_map/ppermute | solution.py:338
  55.7 1.3 %collective-permute-start.20 = (f32[40,512]{1,0:T(8,128)S(1)}, f32[40,512]{1,0:T(8,128)S(1)}, u32[]{:S(2)}, u32[]{:S(2)}) collective-permute-start(f32[40,512]{1,0:T(8,128)S(1)} %get-tuple-element.82), channel_id=1, source_target_pairs={{0,2},{1,3},{2,0},{3,1},{4,6},{5,7},{6,4},{7,5},{8,10},{9,11},{10,... | collective-permute-start | bytes 245768 | tf_op jit(solution)/shard_map/ppermute | solution.py:338
  57.1 0.8 collective-permute-done.18
  57.9 2.2 %collective-permute-done.20 = f32[40,512]{1,0:T(8,128)S(1)} collective-permute-done((f32[40,512]{1,0:T(8,128)S(1)}, f32[40,512]{1,0:T(8,128)S(1)}, u32[]{:S(2)}, u32[]{:S(2)}) %collective-permute-start.20) | collective-permute-done | bytes 81952 | tf_op jit(solution)/shard_map/ppermute | solution.py:338
  60.3 0.4 collective-permute-start.21
  60.7 1.7 %apply.4.refs_2_ = f32[8,32,256]{2,1,0:T(8,128)S(1)} custom-call(s32[2]{0:T(128)S(1)} %pad_add_fusion.place, bf16[32,4,256,256]{3,2,1,0:T(8,128)(2,1)S(1)} %get-tuple-element.49.k_mat, s32[69]{0:T(128)S(1)} %get-tuple-element.50.refs_0_, bf16[4,32,512]{2,1,0:T(8,128)(2,1)S(1)} %pad_maximum_fusion.2.refs_1_), custom_call_target="tpu_custom_call" | custom-call | flops 268435456 | bytes 4194304 | tf_op jit(solution)/shard_map/apply/pallas_call | solution.py:471
  62.4 3.8 %collective-permute-done.21.refs_1_ = bf16[4,32,512]{2,1,0:T(8,128)(2,1)S(1)} collective-permute-done((bf16[4,32,512]{2,1,0:T(8,128)(2,1)S(1)}, bf16[4,32,512]{2,1,0:T(8,128)(2,1)S(1)}, u32[]{:S(2)}, u32[]{:S(2)}) %collective-permute-start.21) | collective-permute-done | bytes 131104 | tf_op jit(solution)/shard_map/ppermute | solution.py:338
  66.2 2.1 %apply.5 = (f32[32,512]{1,0:T(8,128)S(1)}, f32[32,512]{1,0:T(8,128)S(1)}, f32[2,32,512]{2,1,0:T(8,128)S(1)}, f32[32,128]{1,0:T(8,128)S(1)}) custom-call(s32[2]{0:T(128)S(1)} %pad_add_fusion.place, bf16[32,4,256,256]{3,2,1,0:T(8,128)(2,1)S(1)} %get-tuple-element.49.k_mat, s32[69]{0:T(128)S(1)} %get-tuple-element.51.refs_1_.refs_0_, ...), custom_call_target="tpu_custom_call" | custom-call | flops 268435456 | bytes 4194304 | tf_op jit(solution)/shard_map/apply/pallas_call | solution.py:471
  68.4 1.3 %collective-permute-done.23 = f32[2,32,512]{2,1,0:T(8,128)S(1)} collective-permute-done((f32[2,32,512]{2,1,0:T(8,128)S(1)}, f32[2,32,512]{2,1,0:T(8,128)S(1)}, u32[]{:S(2)}, u32[]{:S(2)}) %collective-permute-start.23) | collective-permute-done | bytes 131104 | tf_op jit(solution)/shard_map/ppermute | solution.py:338
  69.8 1.4 %collective-permute-start.24 = (bf16[2,32,512]{2,1,0:T(8,128)(2,1)S(1)}, bf16[2,32,512]{2,1,0:T(8,128)(2,1)S(1)}, u32[]{:S(2)}, u32[]{:S(2)}) collective-permute-start(bf16[2,32,512]{2,1,0:T(8,128)(2,1)S(1)} %get-tuple-element.78), channel_id=1, source_target_pairs={{0,2},{1,3},{2,0},{3,1},{4,6},{5,7},{6,4},{7,5},{8,10},{9,11},{10,... | collective-permute-start | bytes 196616 | tf_op jit(solution)/shard_map/ppermute | solution.py:338
  71.1 1.2 %collective-permute-start.28 = (f32[32,128]{1,0:T(8,128)S(1)}, f32[32,128]{1,0:T(8,128)S(1)}, u32[]{:S(2)}, u32[]{:S(2)}) collective-permute-start(f32[32,128]{1,0:T(8,128)S(1)} %get-tuple-element.71), channel_id=1, source_target_pairs={{0,24},{4,28},{8,16},{12,20},{16,8},{20,12},{24,0},{28,4},{1,25},{... | collective-permute-start | bytes 49160 | tf_op jit(solution)/shard_map/ppermute | solution.py:338
  72.3 0.8 collective-permute-start.27
  73.1 2.5 %collective-permute-start.26 = (f32[32,128]{1,0:T(8,128)S(1)}, f32[32,128]{1,0:T(8,128)S(1)}, u32[]{:S(2)}, u32[]{:S(2)}) collective-permute-start(f32[32,128]{1,0:T(8,128)S(1)} %get-tuple-element.71), channel_id=1, source_target_pairs={{0,8},{4,12},{8,0},{12,4},{16,24},{20,28},{24,16},{28,20},{1,9},{5... | collective-permute-start | bytes 49160 | tf_op jit(solution)/shard_map/ppermute | solution.py:338
  75.7 1.1 %collective-permute-done.28 = f32[32,128]{1,0:T(8,128)S(1)} collective-permute-done((f32[32,128]{1,0:T(8,128)S(1)}, f32[32,128]{1,0:T(8,128)S(1)}, u32[]{:S(2)}, u32[]{:S(2)}) %collective-permute-start.28) | collective-permute-done | bytes 16416 | tf_op jit(solution)/shard_map/ppermute | solution.py:338
  76.9 0.3 collective-permute-done.26
  77.2 1.2 %collective-permute-start.29 = (f32[32,128]{1,0:T(8,128)S(1)}, f32[32,128]{1,0:T(8,128)S(1)}, u32[]{:S(2)}, u32[]{:S(2)}) collective-permute-start(f32[32,128]{1,0:T(8,128)S(1)} %add_add_fusion), channel_id=1, source_target_pairs={{0,4},{4,0},{8,12},{12,8},{16,20},{20,16},{24,28},{28,24},{1,5},{5... | collective-permute-start | bytes 49160 | tf_op jit(solution)/shard_map/ppermute | solution.py:338
  78.5 2.6 %collective-permute-done.29 = f32[32,128]{1,0:T(8,128)S(1)} collective-permute-done((f32[32,128]{1,0:T(8,128)S(1)}, f32[32,128]{1,0:T(8,128)S(1)}, u32[]{:S(2)}, u32[]{:S(2)}) %collective-permute-start.29) | collective-permute-done | bytes 16416 | tf_op jit(solution)/shard_map/ppermute | solution.py:338
  81.1 1.4 %collective-permute-start.31 = (f32[32,128]{1,0:T(8,128)S(1)}, f32[32,128]{1,0:T(8,128)S(1)}, u32[]{:S(2)}, u32[]{:S(2)}) collective-permute-start(f32[32,128]{1,0:T(8,128)S(1)} %add.92.refs_2_), channel_id=1, source_target_pairs={{0,2},{1,3},{2,0},{3,1},{4,6},{5,7},{6,4},{7,5},{8,10},{9,11},{10,... | collective-permute-start | bytes 49160 | tf_op jit(solution)/shard_map/ppermute | solution.py:338
  82.4 0.5 collective-permute-start.30
  82.9 1.3 %collective-permute-done.32.refs_5_ = f32[32,128]{1,0:T(8,128)S(1)} collective-permute-done((f32[32,128]{1,0:T(8,128)S(1)}, f32[32,128]{1,0:T(8,128)S(1)}, u32[]{:S(2)}, u32[]{:S(2)}) %collective-permute-start.32) | collective-permute-done | bytes 16416 | tf_op jit(solution)/shard_map/ppermute | solution.py:338
  84.2 0.6 collective-permute-done.31.refs_4_
  84.9 1.7 %final.1 = (f32[32,2048]{1,0:T(8,128)}, f32[32,2048]{1,0:T(8,128)}) custom-call(s32[2]{0:T(128)S(1)} %pad_add_fusion.place, f32[32,2048]{1,0:T(8,128)S(1)} %copy-done, f32[2,40,512]{2,1,0:T(8,128)S(1)} %pad_maximum_fusion.1.refs_4_.s1_own, f32[2,40,512]{2,1,0:T(8,128)S(1)} %collective-permute-done.22.refs_5_.s1_got, ...), custom_call_target="tpu_custom_call" | custom-call | tf_op jit(solution)/shard_map/final/pallas_call | solution.py:533
  (64 shorter events, 1.7 us)
Async XLA Ops:
  0.6 5.7 %collective-permute-start = (s32[8,6]{1,0:T(8,128)}, s32[8,6]{1,0:T(8,128)S(1)}, u32[]{:S(2)}, u32[]{:S(2)}) collective-permute-start(s32[8,6]{1,0:T(8,128)} %param.3), channel_id=1, source_target_pairs={{0,1},{1,0},{2,3},{3,2},{4,5},{5,4},{6,7},{7,6},{8,9},{9,8},{10,11... | collective-permute-start | bytes 584 | tf_op jit(solution)/shard_map/ppermute | solution.py:338
  1.1 5.3 %collective-permute-start.2 = (s32[8,6]{1,0:T(8,128)}, s32[8,6]{1,0:T(8,128)S(1)}, u32[]{:S(2)}, u32[]{:S(2)}) collective-permute-start(s32[8,6]{1,0:T(8,128)} %param.3), channel_id=1, source_target_pairs={{0,3},{1,2},{2,1},{3,0},{4,7},{5,6},{6,5},{7,4},{8,11},{9,10},{10,... | collective-permute-start | bytes 584 | tf_op jit(solution)/shard_map/ppermute | solution.py:338
  3.8 3.8 %collective-permute-start.1 = (s32[8,6]{1,0:T(8,128)}, s32[8,6]{1,0:T(8,128)S(1)}, u32[]{:S(2)}, u32[]{:S(2)}) collective-permute-start(s32[8,6]{1,0:T(8,128)} %param.3), channel_id=1, source_target_pairs={{0,2},{1,3},{2,0},{3,1},{4,6},{5,7},{6,4},{7,5},{8,10},{9,11},{10,... | collective-permute-start | bytes 584 | tf_op jit(solution)/shard_map/ppermute | solution.py:338
  7.9 8.1 %collective-permute-start.5 = (bf16[16,640]{1,0:T(8,128)(2,1)S(1)}, bf16[16,640]{1,0:T(8,128)(2,1)S(1)}, u32[]{:S(2)}, u32[]{:S(2)}) collective-permute-start(bf16[16,640]{1,0:T(8,128)(2,1)S(1)} %pad_maximum_fusion.7), channel_id=1, source_target_pairs={{0,24},{4,28},{8,16},{12,20},{16,8},{20,12},{24,0},{28,4},{1,25},{... | collective-permute-start | bytes 61448 | tf_op jit(solution)/shard_map/ppermute | solution.py:338
  11.6 5.2 %collective-permute-start.4 = (bf16[16,640]{1,0:T(8,128)(2,1)S(1)}, bf16[16,640]{1,0:T(8,128)(2,1)S(1)}, u32[]{:S(2)}, u32[]{:S(2)}) collective-permute-start(bf16[16,640]{1,0:T(8,128)(2,1)S(1)} %pad_maximum_fusion.7), channel_id=1, source_target_pairs={{0,16},{4,20},{8,24},{12,28},{16,0},{20,4},{24,8},{28,12},{1,17},{... | collective-permute-start | bytes 61448 | tf_op jit(solution)/shard_map/ppermute | solution.py:338
  11.6 5.2 %collective-permute-start.3 = (bf16[16,640]{1,0:T(8,128)(2,1)S(1)}, bf16[16,640]{1,0:T(8,128)(2,1)S(1)}, u32[]{:S(2)}, u32[]{:S(2)}) collective-permute-start(bf16[16,640]{1,0:T(8,128)(2,1)S(1)} %pad_maximum_fusion.7), channel_id=1, source_target_pairs={{0,8},{4,12},{8,0},{12,4},{16,24},{20,28},{24,16},{28,20},{1,9},{5... | collective-permute-start | bytes 61448 | tf_op jit(solution)/shard_map/ppermute | solution.py:338
  12.3 11.1 %collective-permute-start.9 = (f32[32,512]{1,0:T(8,128)S(1)}, f32[32,512]{1,0:T(8,128)S(1)}, u32[]{:S(2)}, u32[]{:S(2)}) collective-permute-start(f32[32,512]{1,0:T(8,128)S(1)} %constant_dynamic-slice_fusion), channel_id=1, source_target_pairs={{0,24},{4,28},{8,16},{12,20},{16,8},{20,12},{24,0},{28,4},{1,25},{... | collective-permute-start | bytes 196616 | tf_op jit(solution)/shard_map/ppermute | solution.py:338
  15.9 7.5 %collective-permute-start.8 = (f32[32,512]{1,0:T(8,128)S(1)}, f32[32,512]{1,0:T(8,128)S(1)}, u32[]{:S(2)}, u32[]{:S(2)}) collective-permute-start(f32[32,512]{1,0:T(8,128)S(1)} %constant_dynamic-slice_fusion), channel_id=1, source_target_pairs={{0,16},{4,20},{8,24},{12,28},{16,0},{20,4},{24,8},{28,12},{1,17},{... | collective-permute-start | bytes 196616 | tf_op jit(solution)/shard_map/ppermute | solution.py:338
  15.9 7.5 %collective-permute-start.7 = (f32[32,512]{1,0:T(8,128)S(1)}, f32[32,512]{1,0:T(8,128)S(1)}, u32[]{:S(2)}, u32[]{:S(2)}) collective-permute-start(f32[32,512]{1,0:T(8,128)S(1)} %constant_dynamic-slice_fusion), channel_id=1, source_target_pairs={{0,8},{4,12},{8,0},{12,4},{16,24},{20,28},{24,16},{28,20},{1,9},{5... | collective-permute-start | bytes 196616 | tf_op jit(solution)/shard_map/ppermute | solution.py:338
  16.8 6.7 %collective-permute-start.6 = (bf16[4,16,640]{2,1,0:T(8,128)(2,1)S(1)}, bf16[4,16,640]{2,1,0:T(8,128)(2,1)S(1)}, u32[]{:S(2)}, u32[]{:S(2)}) collective-permute-start(bf16[4,16,640]{2,1,0:T(8,128)(2,1)S(1)} %pad_maximum_fusion.6.refs_1_), channel_id=1, source_target_pairs={{0,4},{4,0},{8,12},{12,8},{16,20},{20,16},{24,28},{28,24},{1,5},{5... | collective-permute-start | bytes 245768 | tf_op jit(solution)/shard_map/ppermute | solution.py:338
  23.5 6.4 %collective-permute-start.10 = (f32[4,32,512]{2,1,0:T(8,128)S(1)}, f32[4,32,512]{2,1,0:T(8,128)S(1)}, u32[]{:S(2)}, u32[]{:S(2)}) collective-permute-start(f32[4,32,512]{2,1,0:T(8,128)S(1)} %pad_maximum_fusion.refs_2_), channel_id=1, source_target_pairs={{0,4},{4,0},{8,12},{12,8},{16,20},{20,16},{24,28},{28,24},{1,5},{5... | collective-permute-start | bytes 786440 | tf_op jit(solution)/shard_map/ppermute | solution.py:338
  24.7 26.5 %copy-start = (f32[32,2048]{1,0:T(8,128)S(1)}, f32[32,2048]{1,0:T(8,128)}, u32[]{:S(2)}) copy-start(f32[32,2048]{1,0:T(8,128)} %t_ref.1) | copy-start | bytes 786436
  30.0 5.6 %collective-permute-start.13 = (f32[16,256]{1,0:T(8,128)S(1)}, f32[16,256]{1,0:T(8,128)S(1)}, u32[]{:S(2)}, u32[]{:S(2)}) collective-permute-start(f32[16,256]{1,0:T(8,128)S(1)} %get-tuple-element.55), channel_id=1, source_target_pairs={{0,24},{4,28},{8,16},{12,20},{16,8},{20,12},{24,0},{28,4},{1,25},{... | collective-permute-start | bytes 49160 | tf_op jit(solution)/shard_map/ppermute | solution.py:338
  33.9 4.6 %collective-permute-start.12 = (f32[16,256]{1,0:T(8,128)S(1)}, f32[16,256]{1,0:T(8,128)S(1)}, u32[]{:S(2)}, u32[]{:S(2)}) collective-permute-start(f32[16,256]{1,0:T(8,128)S(1)} %get-tuple-element.55), channel_id=1, source_target_pairs={{0,16},{4,20},{8,24},{12,28},{16,0},{20,4},{24,8},{28,12},{1,17},{... | collective-permute-start | bytes 49160 | tf_op jit(solution)/shard_map/ppermute | solution.py:338
  33.9 4.6 %collective-permute-start.11 = (f32[16,256]{1,0:T(8,128)S(1)}, f32[16,256]{1,0:T(8,128)S(1)}, u32[]{:S(2)}, u32[]{:S(2)}) collective-permute-start(f32[16,256]{1,0:T(8,128)S(1)} %get-tuple-element.55), channel_id=1, source_target_pairs={{0,8},{4,12},{8,0},{12,4},{16,24},{20,28},{24,16},{28,20},{1,9},{5... | collective-permute-start | bytes 49160 | tf_op jit(solution)/shard_map/ppermute | solution.py:338
  38.5 3.8 %collective-permute-start.14 = (f32[16,256]{1,0:T(8,128)S(1)}, f32[16,256]{1,0:T(8,128)S(1)}, u32[]{:S(2)}, u32[]{:S(2)}) collective-permute-start(f32[16,256]{1,0:T(8,128)S(1)} %add_add_fusion.1), channel_id=1, source_target_pairs={{0,4},{4,0},{8,12},{12,8},{16,20},{20,16},{24,28},{28,24},{1,5},{5... | collective-permute-start | bytes 49160 | tf_op jit(solution)/shard_map/ppermute | solution.py:338
  45.4 1.4 %collective-permute-start.15 = (f32[2,32,512]{2,1,0:T(8,128)S(1)}, f32[2,32,512]{2,1,0:T(8,128)S(1)}, u32[]{:S(2)}, u32[]{:S(2)}) collective-permute-start(f32[2,32,512]{2,1,0:T(8,128)S(1)} %get-tuple-element.57), channel_id=1, source_target_pairs={{0,1},{1,0},{2,3},{3,2},{4,5},{5,4},{6,7},{7,6},{8,9},{9,8},{10,11... | collective-permute-start | bytes 393224 | tf_op jit(solution)/shard_map/ppermute | solution.py:338
  46.8 4.3 %collective-permute-start.16 = (f32[32,512]{1,0:T(8,128)S(1)}, f32[32,512]{1,0:T(8,128)S(1)}, u32[]{:S(2)}, u32[]{:S(2)}) collective-permute-start(f32[32,512]{1,0:T(8,128)S(1)} %fusion.8), channel_id=1, source_target_pairs={{0,2},{1,3},{2,0},{3,1},{4,6},{5,7},{6,4},{7,5},{8,10},{9,11},{10,... | collective-permute-start | bytes 196616 | tf_op jit(solution)/shard_map/ppermute | solution.py:338
  51.2 5.9 %collective-permute-start.19 = (bf16[32,512]{1,0:T(8,128)(2,1)S(1)}, bf16[32,512]{1,0:T(8,128)(2,1)S(1)}, u32[]{:S(2)}, u32[]{:S(2)}) collective-permute-start(bf16[32,512]{1,0:T(8,128)(2,1)S(1)} %get-tuple-element.60), channel_id=1, source_target_pairs={{0,24},{4,28},{8,16},{12,20},{16,8},{20,12},{24,0},{28,4},{1,25},{... | collective-permute-start | bytes 98312 | tf_op jit(solution)/shard_map/ppermute | solution.py:338
  53.0 4.9 %collective-permute-start.18 = (bf16[32,512]{1,0:T(8,128)(2,1)S(1)}, bf16[32,512]{1,0:T(8,128)(2,1)S(1)}, u32[]{:S(2)}, u32[]{:S(2)}) collective-permute-start(bf16[32,512]{1,0:T(8,128)(2,1)S(1)} %get-tuple-element.60), channel_id=1, source_target_pairs={{0,16},{4,20},{8,24},{12,28},{16,0},{20,4},{24,8},{28,12},{1,17},{... | collective-permute-start | bytes 98312 | tf_op jit(solution)/shard_map/ppermute | solution.py:338
  53.6 4.3 %collective-permute-start.17 = (bf16[32,512]{1,0:T(8,128)(2,1)S(1)}, bf16[32,512]{1,0:T(8,128)(2,1)S(1)}, u32[]{:S(2)}, u32[]{:S(2)}) collective-permute-start(bf16[32,512]{1,0:T(8,128)(2,1)S(1)} %get-tuple-element.60), channel_id=1, source_target_pairs={{0,8},{4,12},{8,0},{12,4},{16,24},{20,28},{24,16},{28,20},{1,9},{5... | collective-permute-start | bytes 98312 | tf_op jit(solution)/shard_map/ppermute | solution.py:338
  55.7 4.5 %collective-permute-start.20 = (f32[40,512]{1,0:T(8,128)S(1)}, f32[40,512]{1,0:T(8,128)S(1)}, u32[]{:S(2)}, u32[]{:S(2)}) collective-permute-start(f32[40,512]{1,0:T(8,128)S(1)} %get-tuple-element.82), channel_id=1, source_target_pairs={{0,2},{1,3},{2,0},{3,1},{4,6},{5,7},{6,4},{7,5},{8,10},{9,11},{10,... | collective-permute-start | bytes 245768 | tf_op jit(solution)/shard_map/ppermute | solution.py:338
  60.2 6.0 %collective-permute-start.22 = (f32[2,40,512]{2,1,0:T(8,128)S(1)}, f32[2,40,512]{2,1,0:T(8,128)S(1)}, u32[]{:S(2)}, u32[]{:S(2)}) collective-permute-start(f32[2,40,512]{2,1,0:T(8,128)S(1)} %pad_maximum_fusion.1.refs_4_.s1_own), channel_id=1, source_target_pairs={{0,1},{1,0},{2,3},{3,2},{4,5},{5,4},{6,7},{7,6},{8,9},{9,8},{10,11... | collective-permute-start | bytes 491528 | tf_op jit(solution)/shard_map/ppermute | solution.py:338
  60.3 5.9 %collective-permute-start.21 = (bf16[4,32,512]{2,1,0:T(8,128)(2,1)S(1)}, bf16[4,32,512]{2,1,0:T(8,128)(2,1)S(1)}, u32[]{:S(2)}, u32[]{:S(2)}) collective-permute-start(bf16[4,32,512]{2,1,0:T(8,128)(2,1)S(1)} %pad_maximum_fusion.2.refs_1_), channel_id=1, source_target_pairs={{0,4},{4,0},{8,12},{12,8},{16,20},{20,16},{24,28},{28,24},{1,5},{5... | collective-permute-start | bytes 393224 | tf_op jit(solution)/shard_map/ppermute | solution.py:338
  68.3 1.4 %collective-permute-start.23 = (f32[2,32,512]{2,1,0:T(8,128)S(1)}, f32[2,32,512]{2,1,0:T(8,128)S(1)}, u32[]{:S(2)}, u32[]{:S(2)}) collective-permute-start(f32[2,32,512]{2,1,0:T(8,128)S(1)} %get-tuple-element.69), channel_id=1, source_target_pairs={{0,1},{1,0},{2,3},{3,2},{4,5},{5,4},{6,7},{7,6},{8,9},{9,8},{10,11... | collective-permute-start | bytes 393224 | tf_op jit(solution)/shard_map/ppermute | solution.py:338
  69.8 5.7 %collective-permute-start.24 = (bf16[2,32,512]{2,1,0:T(8,128)(2,1)S(1)}, bf16[2,32,512]{2,1,0:T(8,128)(2,1)S(1)}, u32[]{:S(2)}, u32[]{:S(2)}) collective-permute-start(bf16[2,32,512]{2,1,0:T(8,128)(2,1)S(1)} %get-tuple-element.78), channel_id=1, source_target_pairs={{0,2},{1,3},{2,0},{3,1},{4,6},{5,7},{6,4},{7,5},{8,10},{9,11},{10,... | collective-permute-start | bytes 196616 | tf_op jit(solution)/shard_map/ppermute | solution.py:338
  71.1 5.6 %collective-permute-start.28 = (f32[32,128]{1,0:T(8,128)S(1)}, f32[32,128]{1,0:T(8,128)S(1)}, u32[]{:S(2)}, u32[]{:S(2)}) collective-permute-start(f32[32,128]{1,0:T(8,128)S(1)} %get-tuple-element.71), channel_id=1, source_target_pairs={{0,24},{4,28},{8,16},{12,20},{16,8},{20,12},{24,0},{28,4},{1,25},{... | collective-permute-start | bytes 49160 | tf_op jit(solution)/shard_map/ppermute | solution.py:338
  72.3 4.6 %collective-permute-start.27 = (f32[32,128]{1,0:T(8,128)S(1)}, f32[32,128]{1,0:T(8,128)S(1)}, u32[]{:S(2)}, u32[]{:S(2)}) collective-permute-start(f32[32,128]{1,0:T(8,128)S(1)} %get-tuple-element.71), channel_id=1, source_target_pairs={{0,16},{4,20},{8,24},{12,28},{16,0},{20,4},{24,8},{28,12},{1,17},{... | collective-permute-start | bytes 49160 | tf_op jit(solution)/shard_map/ppermute | solution.py:338
  73.1 4.2 %collective-permute-start.26 = (f32[32,128]{1,0:T(8,128)S(1)}, f32[32,128]{1,0:T(8,128)S(1)}, u32[]{:S(2)}, u32[]{:S(2)}) collective-permute-start(f32[32,128]{1,0:T(8,128)S(1)} %get-tuple-element.71), channel_id=1, source_target_pairs={{0,8},{4,12},{8,0},{12,4},{16,24},{20,28},{24,16},{28,20},{1,9},{5... | collective-permute-start | bytes 49160 | tf_op jit(solution)/shard_map/ppermute | solution.py:338
  75.6 9.3 %collective-permute-start.25 = (f32[2,32,512]{2,1,0:T(8,128)S(1)}, f32[2,32,512]{2,1,0:T(8,128)S(1)}, u32[]{:S(2)}, u32[]{:S(2)}) collective-permute-start(f32[2,32,512]{2,1,0:T(8,128)S(1)} %pad_maximum_fusion.3.refs_0_), channel_id=1, source_target_pairs={{0,1},{1,0},{2,3},{3,2},{4,5},{5,4},{6,7},{7,6},{8,9},{9,8},{10,11... | collective-permute-start | bytes 393224 | tf_op jit(solution)/shard_map/ppermute | solution.py:338
  77.2 3.8 %collective-permute-start.29 = (f32[32,128]{1,0:T(8,128)S(1)}, f32[32,128]{1,0:T(8,128)S(1)}, u32[]{:S(2)}, u32[]{:S(2)}) collective-permute-start(f32[32,128]{1,0:T(8,128)S(1)} %add_add_fusion), channel_id=1, source_target_pairs={{0,4},{4,0},{8,12},{12,8},{16,20},{20,16},{24,28},{28,24},{1,5},{5... | collective-permute-start | bytes 49160 | tf_op jit(solution)/shard_map/ppermute | solution.py:338
  81.1 3.2 %collective-permute-start.32 = (f32[32,128]{1,0:T(8,128)S(1)}, f32[32,128]{1,0:T(8,128)S(1)}, u32[]{:S(2)}, u32[]{:S(2)}) collective-permute-start(f32[32,128]{1,0:T(8,128)S(1)} %add.92.refs_2_), channel_id=1, source_target_pairs={{0,3},{1,2},{2,1},{3,0},{4,7},{5,6},{6,5},{7,4},{8,11},{9,10},{10,... | collective-permute-start | bytes 49160 | tf_op jit(solution)/shard_map/ppermute | solution.py:338
  81.1 3.8 %collective-permute-start.31 = (f32[32,128]{1,0:T(8,128)S(1)}, f32[32,128]{1,0:T(8,128)S(1)}, u32[]{:S(2)}, u32[]{:S(2)}) collective-permute-start(f32[32,128]{1,0:T(8,128)S(1)} %add.92.refs_2_), channel_id=1, source_target_pairs={{0,2},{1,3},{2,0},{3,1},{4,6},{5,7},{6,4},{7,5},{8,10},{9,11},{10,... | collective-permute-start | bytes 49160 | tf_op jit(solution)/shard_map/ppermute | solution.py:338
  82.4 2.4 %collective-permute-start.30 = (f32[32,128]{1,0:T(8,128)S(1)}, f32[32,128]{1,0:T(8,128)S(1)}, u32[]{:S(2)}, u32[]{:S(2)}) collective-permute-start(f32[32,128]{1,0:T(8,128)S(1)} %add.92.refs_2_), channel_id=1, source_target_pairs={{0,1},{1,0},{2,3},{3,2},{4,5},{5,4},{6,7},{7,6},{8,9},{9,8},{10,11... | collective-permute-start | bytes 49160 | tf_op jit(solution)/shard_map/ppermute | solution.py:338

commit v7 on v6

--- a/solution.py
+++ b/solution.py
@@ -196,110 +196,120 @@
     return own.at[0], got.at[0], own.at[1], got.at[1]
 
 
-def apply_kernel(cfg, parts, scaled, carried, finish, place, k_mat, *refs):
-    n = len(parts)
-    lists, pieces, refs = refs[:n], refs[n:2 * n], refs[2 * n:]
-    if scaled:
-        inv_ref, refs = refs[0], refs[1:]
-    if carried:
-        z_in, refs = refs[0], refs[1:]
-    products = finish and not scaled
-    if products:
-        t_ref, s_refs, refs = refs[0], pieces_of(refs[1], refs[2]), refs[3:]
-    if finish:
-        near, near_y, cross, extra, z_acc, refs = *refs[:5], refs[5:]
-        z_refs = (near, cross.at[0], near_y, cross.at[1])
-    else:
-        z_acc, refs = refs[0], refs[1:]
-    w_all, refs = refs[0], refs[1:]
-    kbuf, sems = (None, None) if cfg.resident else refs
+def walk(cfg, part, listed, k_mat, kbuf, sems, product, total_ref, by_row):
+    total = listed[0]
+    base = part * cfg.part_groups
+
+    def copy_in(g):
+        slot = lax.rem(g, RING)
+        return pltpu.make_async_copy(k_mat.at[g], kbuf.at[slot], sems.at[slot])
+
+    if not cfg.resident:
+        for p in range(RING - 1):
+
+            @pl.when(p < total)
+            def _(p=p):
+                copy_in(p).start()
+
+    def step(g, carry):
+        slot, source = (base + g, k_mat) if cfg.resident else (lax.rem(g, RING), kbuf)
+        if not cfg.resident:
+
+            @pl.when(g + (RING - 1) < total)
+            def _():
+                copy_in(g + (RING - 1)).start()
+
+            copy_in(g).wait()
+        codes = [listed[g * GROUP + u + 1] for u in range(GROUP)]
+        pairs = [(lax.shift_right_logical(code, CODE_BITS), code & (CODE - 1)) for code in codes]
+        terms = [product(i, j, source[slot, u]) for u, (i, j) in enumerate(pairs)]
+        for (i, j), term in zip(pairs, terms):
+            total_ref[i if by_row else j] += term
+        return carry
+
+    lax.fori_loop(0, total, step, 0)
+
+
+def first_kernel(cfg, place, k_mat, *refs):
+    n = cfg.parts
+    lists, pieces, inv_ref, refs = refs[:n], refs[n:2 * n], refs[2 * n], refs[2 * n + 1:]
+    near, near_y, cross, own_inv, z_acc, w_all, *ring = refs
+    kbuf, sems = ring or (None, None)
     col = place[1]
     own_rows, block_len = cfg.own_rows, cfg.block_len
-
-    z_acc[...] = z_in[...] if carried else jnp.zeros_like(z_acc)
-    for part, listed, piece in zip(parts, lists, pieces):
-        total = listed[0]
-        base = part * cfg.part_groups
+    z_acc[...] = jnp.zeros_like(z_acc)
+    for part, (listed, piece) in enumerate(zip(lists, pieces)):
         held = piece.shape[0]
 
-        def copy_in(g):
-            slot = lax.rem(g, RING)
-            return pltpu.make_async_copy(k_mat.at[g], kbuf.at[slot], sems.at[slot])
-
-        if not cfg.resident:
-            for p in range(RING - 1):
-
-                @pl.when(p < total)
-                def _(p=p, copy_in=copy_in):
-                    copy_in(p).start()
-
-        def prepare(n, carry, part=part, piece=piece):
-            z = slot_of(cfg, place, n)
+        def prepare(m, carry, part=part, piece=piece):
+            z = slot_of(cfg, place, m)
             for k in range(own_rows):
-                w = piece[n, :, k * block_len:(k + 1) * block_len]
-                if scaled:
-                    at = row_of(cfg, place, part, z) * own_rows + k
-                    w = (w * inv_ref[pl.ds(at, 1), :]).astype(BF16)
-                w_all[z * own_rows + k] = w
+                w = piece[m, :, k * block_len:(k + 1) * block_len]
+                at = row_of(cfg, place, part, z) * own_rows + k
+                w_all[z * own_rows + k] = (w * inv_ref[pl.ds(at, 1), :]).astype(BF16)
             return carry
 
         lax.fori_loop(0, held, prepare, 0, unroll=held <= 4)
 
-        def step(g, carry, total=total, listed=listed, base=base, copy_in=copy_in):
-            slot, source = (base + g, k_mat) if cfg.resident else (lax.rem(g, RING), kbuf)
-            if not cfg.resident:
-
-                @pl.when(g + (RING - 1) < total)
-                def _():
-                    copy_in(g + (RING - 1)).start()
-
-                copy_in(g).wait()
-            codes = [listed[g * GROUP + u + 1] for u in range(GROUP)]
-            terms = [
-                lax.dot_general(
-                    w_all[code & (CODE - 1)],
-                    source[slot, u],
-                    (((1,), (1,)), ((), ())),
-                    preferred_element_type=F32,
-                )
-                for u, code in enumerate(codes)
-            ]
-            for code, term in zip(codes, terms):
-                z_acc[lax.shift_right_logical(code, CODE_BITS)] += term
-            return carry
-
-        lax.fori_loop(0, total, step, 0)
-    if not finish:
-        return
-    own_len = own_rows * block_len
-    if scaled:
+        def product(i, j, block):
+            return lax.dot_general(
+                w_all[j], block, (((1,), (1,)), ((), ())), preferred_element_type=F32
+            )
+
+        walk(cfg, part, listed, k_mat, kbuf, sems, product, z_acc, True)
+    for k in range(own_rows):
+        cols = slice(k * block_len, (k + 1) * block_len)
+        mine = inv_ref[pl.ds(place[0] * own_rows + k, 1), :]
+        own_inv[:, cols] = jnp.broadcast_to(mine, (8, block_len))
+        for e, ref in enumerate((near, cross.at[0], near_y, cross.at[1])):
+            ref[:, cols] = z_acc[(col ^ e) * own_rows + k]
+
+
+def second_kernel(cfg, part, place, k_mat, listed, t_ref, s1_own, s1_got, out, z_acc, w_all, *ring):
+    kbuf, sems = ring or (None, None)
+    own_rows, block_len = cfg.own_rows, cfg.block_len
+    outputs = t_ref.shape[0]
+    for e, packed in enumerate(pieces_of(s1_own, s1_got)):
+        share = place[1] ^ e
         for k in range(own_rows):
-            mine = inv_ref[pl.ds(place[0] * own_rows + k, 1), :]
-            extra[:, k * block_len:(k + 1) * block_len] = jnp.broadcast_to(mine, (8, block_len))
-    for e in range(4):
+            cols = slice(k * block_len, (k + 1) * block_len)
+            i = share * own_rows + k
+            t = t_ref[:, pl.ds(pl.multiple_of(i * block_len, LANES), block_len)]
+            g = (packed[:outputs, cols] - SHIFT * t) * packed[outputs:outputs + 1, cols]
+            w_all[i] = g.astype(BF16)
+    z_acc[...] = jnp.zeros_like(z_acc)
+
+    def product(i, j, block):
+        return jnp.dot(w_all[i], block, preferred_element_type=F32)
+
+    walk(cfg, part, listed, k_mat, kbuf, sems, product, z_acc, False)
+
+    def hand_out(m, carry):
+        z = slot_of(cfg, place, m)
         for k in range(own_rows):
-            z_refs[e][:, k * block_len:(k + 1) * block_len] = z_acc[(col ^ e) * own_rows + k]
-    if products:
-        outputs = t_ref.shape[0]
-        ts2 = jnp.zeros((outputs, 1), F32)
-        s1s2 = jnp.zeros((outputs, 1), F32)
-        for e, packed in enumerate(s_refs):
-            at = pl.ds(pl.multiple_of((col ^ e) * own_len, LANES), own_len)
-            grown = z_refs[e][...] * packed[outputs:outputs + 1, :]
-            ts2 += jnp.sum(t_ref[:, at] * grown, axis=1, keepdims=True)
-            s1s2 += jnp.sum(packed[:outputs, :] * grown, axis=1, keepdims=True)
-        t = t_ref[:, pl.ds(pl.multiple_of(col * own_len, LANES), own_len)]
-        s1 = s_refs[0][:outputs, :]
-        tt = jnp.sum(t * t, axis=1, keepdims=True)
-        ts1 = jnp.sum(t * s1, axis=1, keepdims=True)
-        s1s1 = jnp.sum(s1 * s1, axis=1, keepdims=True)
-        ts2 += SHIFT * ts1
-        s1s2 += SHIFT * s1s1
-        lane = lax.broadcasted_iota(jnp.int32, (outputs, LANES), 1)
-        out = jnp.zeros(lane.shape, F32)
-        for n, v in enumerate((tt, ts1, s1s1, ts2, s1s2)):
-            out = jnp.where(lane == n, v, out)
-        extra[...] = out
+            out[m, :, k * block_len:(k + 1) * block_len] = z_acc[z * own_rows + k].astype(out.dtype)
+        return carry
+
+    held = out.shape[0]
+    lax.fori_loop(0, held, hand_out, 0, unroll=held <= 4)
+
+
+def product_kernel(place, t_ref, s1_own, *refs):
+    zs, grown_ref, dot_ref = refs[:-2], refs[-2], refs[-1]
+    outputs, own_len = grown_ref.shape
+    z = zs[0][...].astype(F32)
+    for ref in zs[1:]:
+        z = z + ref[...].astype(F32)
+    grown = z * s1_own[0, outputs:outputs + 1, :]
+    grown_ref[...] = grown
+    s1 = s1_own[0, :outputs, :]
+    s2 = grown + SHIFT * s1
+    t = t_ref[:, pl.ds(pl.multiple_of(place[1] * own_len, LANES), own_len)]
+    lane = lax.broadcasted_iota(jnp.int32, (outputs, LANES), 1)
+    out = jnp.zeros(lane.shape, F32)
+    for n, (a, b) in enumerate(((t, t), (t, s1), (s1, s1), (t, s2), (s1, s2))):
+        out = jnp.where(lane == n, jnp.sum(a * b, axis=1, keepdims=True), out)
+    dot_ref[...] = out
 
 
 def final_kernel(place, t_ref, s1_own, s1_got, *refs):
@@ -458,76 +468,77 @@
         t_pieces, k_lists = [lax.all_gather(own_t, "rows")], [list0]
     inv = 1.0 / jnp.sqrt(1.0 + total_rows(degree))
 
-    def apply(use, pieces, finish=True, inv=None, z_in=None, products=()):
-        operands = [k_mat] + [k_lists[p] for p in use] + pieces
-        specs = [k_spec] + [SMEM] * len(use) + [VMEM] * len(pieces)
-        more = [x for x in (inv, z_in) if x is not None] + list(products)
-        z_shape = (block_rows, outputs, block_len)
-        if finish:
-            out = [shape(outputs, own_len)] * 2 + [shape(2, outputs, own_len)]
-            out += [shape(outputs, LANES) if products else shape(8, own_len)]
-        else:
-            out = [shape(*z_shape)]
+    def cost(n):
+        return pl.CostEstimate(
+            flops=2 * n * bound * outputs * block_len * block_len,
+            bytes_accessed=n * bound * block_len * block_len,
+            transcendentals=0,
+        )
+
+    near_z, near_y, cross_z, tail = pl.pallas_call(
+        functools.partial(first_kernel, cfg),
+        out_shape=[shape(outputs, own_len)] * 2 + [shape(2, outputs, own_len), shape(8, own_len)],
+        in_specs=[SMEM, k_spec] + [SMEM] * parts + [VMEM] * (parts + 1),
+        out_specs=[VMEM] * 4,
+        scratch_shapes=[
+            pltpu.VMEM((block_rows, outputs, block_len), F32),
+            pltpu.VMEM((n_part, outputs, block_len), BF16),
+            *ring,
+        ],
+        compiler_params=limit,
+        cost_estimate=cost(parts),
+        name="first",
+    )(place, k_mat, *k_lists, *t_pieces, inv)
+
+    got = swap(cross_z, "cols", 1)
+    half = jnp.concatenate([near_z + got[0], near_y + got[1], tail], axis=0)
+    far = swap(half, "cols", 2)
+    lo, hi, end = slice(0, outputs), slice(outputs, 2 * outputs), slice(2 * outputs, None)
+    s1_own = jnp.stack([
+        jnp.concatenate([(half[lo] + far[hi]) * tail[:1], tail], axis=0),
+        jnp.concatenate([(half[hi] + far[lo]) * far[end][:1], far[end]], axis=0),
+    ])
+    s1_got = swap(s1_own, "cols", 1)
+    held_t = pltpu.with_memory_space_constraint(targets, pltpu.VMEM)
+
+    def second(part, dtype):
         return pl.pallas_call(
-            functools.partial(
-                apply_kernel, cfg, use, inv is not None, z_in is not None, finish
-            ),
-            out_shape=out,
-            in_specs=[SMEM] + specs + [VMEM] * len(more),
-            out_specs=[VMEM] * len(out),
-            scratch_shapes=([pltpu.VMEM(z_shape, F32)] if finish else []) + [
-                pltpu.VMEM((n_part, outputs, block_len), BF16),
+            functools.partial(second_kernel, cfg, part),
+            out_shape=shape(n_part // own_rows, outputs, own_len, dtype=dtype),
+            in_specs=[SMEM, k_spec, SMEM] + [VMEM] * 3,
+            out_specs=VMEM,
+            scratch_shapes=[
+                pltpu.VMEM((n_part, outputs, block_len), F32),
+                pltpu.VMEM((block_rows, outputs, block_len), BF16),
                 *ring,
             ],
             compiler_params=limit,
-            cost_estimate=pl.CostEstimate(
-                flops=2 * len(use) * bound * outputs * block_len * block_len,
-                bytes_accessed=len(use) * bound * block_len * block_len,
-                transcendentals=0,
-            ),
-            name="apply",
-        )(place, *operands, *more)
-
-    near_z, near_y, cross_z, tail = apply(tuple(range(parts)), t_pieces, inv=inv)
-    got = swap(cross_z, "cols", 1)
-    half, half_y = near_z + got[0], near_y + got[1]
-    own_inv = tail[:1]
-    s1 = (half + swap(half_y, "cols", 2)) * own_inv
-    g = ((s1 - SHIFT * own_t) * own_inv).astype(BF16)
-    g, half, half_y = lax.optimization_barrier((g, half, half_y))
-    far = swap(jnp.concatenate([half, tail], axis=0), "cols", 2)
-    s1_own = jnp.stack([
-        jnp.concatenate([s1, tail], axis=0),
-        jnp.concatenate([(half_y + far[:outputs]) * far[outputs:outputs + 1], far[outputs:]], axis=0),
-    ])
-    held_t = pltpu.with_memory_space_constraint(targets, pltpu.VMEM)
+            cost_estimate=cost(1),
+            name="second",
+        )(place, k_mat, k_lists[part], held_t, s1_own, s1_got)
+
     if direct_rows:
-        g_same = jnp.stack(along_z(g))
-        g_same, s1_own = lax.optimization_barrier((g_same, s1_own))
-        _, g_other = across_x(g_same)
-        s1_got = swap(s1_own, "cols", 1)
-        (z_part,) = apply((0,), [g_same], finish=False)
-        z_part, g_other, s1_got = lax.optimization_barrier((z_part, g_other, s1_got))
-        *z2, dots = apply(
-            (1,), [g_other], z_in=z_part, products=[held_t, s1_own, s1_got]
-        )
-        dots = pair_sum(along_z(dots))
+        z2_other = swap(second(1, BF16), "rows", 1)
+        z2_same = second(0, F32)
+        z2_same, z2_other = lax.optimization_barrier((z2_same, z2_other))
+        z2 = z2_same + z2_other.astype(F32)
+        z2 = [z2[0]] + [swap(z2[n].astype(BF16), "rows", 2 * n) for n in range(1, n_rows // 2)]
     else:
-        s1_got = swap(s1_own, "cols", 1)
-        *z2, dots = apply(
-            (0,), [lax.all_gather(g, "rows")], products=[held_t, s1_own, s1_got]
-        )
-    got = swap(z2[2], "cols", 1)
-    halves = jnp.stack([z2[0] + got[0], z2[1] + got[1]])
-    halves = lax.reduce_precision(halves, 8, 7)
-    far = swap(halves.astype(BF16), "cols", 2).astype(F32)
-    grown = jnp.stack([
-        (halves[0] + far[1]) * own_inv,
-        (halves[1] + far[0]) * s1_own[1, outputs:outputs + 1],
-    ])
-    dots = pair_sum(across_x(dots)) if direct_rows else lax.psum(dots, "rows")
-    dots = direct_cols(dots)
-    ends = (s1_own, s1_got, grown, swap(grown, "cols", 1), *dots)
+        z2 = [lax.psum_scatter(second(0, F32), "rows", scatter_dimension=0)]
+    grown, dots = pl.pallas_call(
+        product_kernel,
+        out_shape=(shape(outputs, own_len), shape(outputs, LANES)),
+        in_specs=[SMEM] + [VMEM] * (2 + len(z2)),
+        out_specs=(VMEM, VMEM),
+        compiler_params=limit,
+        name="products",
+    )(place, held_t, s1_own, *z2)
+    if direct_rows:
+        dots = pair_sum(across_x(pair_sum(along_z(dots))))
+    else:
+        dots = lax.psum(dots, "rows")
+    grown = jnp.stack([grown, swap(grown, "cols", 2)])
+    ends = (s1_own, s1_got, grown, swap(grown, "cols", 1), *direct_cols(dots))
     ends = [pltpu.with_memory_space_constraint(x, pltpu.VMEM) for x in ends]
 
     return pl.pallas_call(

time: 86.7 us -> 87.7 us (1.012)
    ppermute x33 -> x31, waiting for transfers between devices: 27.3 us -> 27.8 us  [swap(): return lax.ppermute(x, axis, [(i, i ^ d) for i in range(size)])]
    ppermute x33 -> x31, starting transfers between devices: 36.3 us -> 36.6 us  [swap(): return lax.ppermute(x, axis, [(i, i ^ d) for i in range(size)])]
    pallas_call x3 -> x4, Pallas kernels: 6.81 us -> 6.79 us  [the longest x1 3.08 us: local(): pl.pallas_call(functools.partial(first_kernel, cfg), out_shape=[shape(out...]
  transfers between devices with their start and end apart: 33 -> 31, of which waited for: 17 -> 17; matrix products, arithmetic and copies ran while one was open for 3% -> 3% of each run, Pallas kernels for 14% -> 14%
where the time goes in v7:
time: 87.7 us; the launch traced here: 87.4 us
  starting transfers between devices  36.6 us (42%)
  waiting for transfers between devices  27.8 us (32%)
  Pallas kernels  18.7 us (21%)
  local copies, waits for them, and re-layouts  2.76 us (3%)
    ppermute x31, starting transfers between devices, swap(): return lax.ppermute(x, axis, [(i, i ^ d) for i in range(size)])  36.6 us
    ppermute x31, waiting for transfers between devices, swap(): return lax.ppermute(x, axis, [(i, i ^ d) for i in range(size)])  27.8 us
    pallas_call x2, Pallas kernels, build(): pl.pallas_call(functools.partial(build_kernel, cfg, part), out_shape=out,...  10.2 us
    pallas_call x1, Pallas kernels, local(): pl.pallas_call(functools.partial(first_kernel, cfg), out_shape=[shape(out...  3.08 us
    pallas_call x2, Pallas kernels, second(): pl.pallas_call(functools.partial(second_kernel, cfg, part), out_shape=sha...  3.06 us
  transfers between devices with their start and end apart: 31, of which 17 were waited for; matrix products, arithmetic and copies ran while one was open for 3% of the time, Pallas kernels for 14%

profile of v7, /device:TPU:0, one launch (start us, length us, event | category | flops | bytes accessed | tf_op | source)
XLA Modules:
  0.0 87.4 jit_solution(15304577345564195924)
XLA Ops:
  0.6 0.5 collective-permute-start
  1.1 2.6 %collective-permute-start.2 = (s32[8,6]{1,0:T(8,128)}, s32[8,6]{1,0:T(8,128)S(1)}, u32[]{:S(2)}, u32[]{:S(2)}) collective-permute-start(s32[8,6]{1,0:T(8,128)} %param.3), channel_id=1, source_target_pairs={{0,3},{1,2},{2,1},{3,0},{4,7},{5,6},{6,5},{7,4},{8,11},{9,10},{10,... | collective-permute-start | bytes 584 | tf_op jit(solution)/shard_map/ppermute | solution.py:348
  3.8 0.8 copy.6
  4.7 0.7 constant_dynamic-slice_fusion.1
  5.5 0.8 constant_dynamic-slice_fusion
  6.6 1.0 %collective-permute-done.1 = s32[8,6]{1,0:T(8,128)S(1)} collective-permute-done((s32[8,6]{1,0:T(8,128)}, s32[8,6]{1,0:T(8,128)S(1)}, u32[]{:S(2)}, u32[]{:S(2)}) %collective-permute-start.1) | collective-permute-done | bytes 224 | tf_op jit(solution)/shard_map/ppermute | solution.py:348
  7.9 3.7 %collective-permute-start.5 = (bf16[16,640]{1,0:T(8,128)(2,1)S(1)}, bf16[16,640]{1,0:T(8,128)(2,1)S(1)}, u32[]{:S(2)}, u32[]{:S(2)}) collective-permute-start(bf16[16,640]{1,0:T(8,128)(2,1)S(1)} %pad_maximum_fusion.5), channel_id=1, source_target_pairs={{0,24},{4,28},{8,16},{12,20},{16,8},{20,12},{24,0},{28,4},{1,25},{... | collective-permute-start | bytes 61448 | tf_op jit(solution)/shard_map/ppermute | solution.py:348
  11.6 0.8 collective-permute-start.3
  12.3 3.6 %collective-permute-start.9 = (f32[32,512]{1,0:T(8,128)S(1)}, f32[32,512]{1,0:T(8,128)S(1)}, u32[]{:S(2)}, u32[]{:S(2)}) collective-permute-start(f32[32,512]{1,0:T(8,128)S(1)} %constant_dynamic-slice_fusion), channel_id=1, source_target_pairs={{0,24},{4,28},{8,16},{12,20},{16,8},{20,12},{24,0},{28,4},{1,25},{... | collective-permute-start | bytes 196616 | tf_op jit(solution)/shard_map/ppermute | solution.py:348
  15.9 0.8 collective-permute-start.7
  16.8 1.6 %collective-permute-start.6 = (bf16[4,16,640]{2,1,0:T(8,128)(2,1)S(1)}, bf16[4,16,640]{2,1,0:T(8,128)(2,1)S(1)}, u32[]{:S(2)}, u32[]{:S(2)}) collective-permute-start(bf16[4,16,640]{2,1,0:T(8,128)(2,1)S(1)} %pad_maximum_fusion.4.refs_1_), channel_id=1, source_target_pairs={{0,4},{4,0},{8,12},{12,8},{16,20},{20,16},{24,28},{28,24},{1,5},{5... | collective-permute-start | bytes 245768 | tf_op jit(solution)/shard_map/ppermute | solution.py:348
  18.4 5.6 %build.2 = (bf16[32,4,256,256]{3,2,1,0:T(8,128)(2,1)S(1)}, s32[69]{0:T(128)S(1)}, f32[8,256]{1,0:T(8,128)S(1)}, bf16[8,256,32]{2,1,0:T(8,128)(2,1)S(1)}) custom-call(s32[2]{0:T(128)S(1)} %pad_add_fusion.place, s32[8,64]{1,0:T(8,128)S(1)} %add_add_fusion.2.direct, bf16[16,2048]{1,0:T(8,128)(2,1)} %refs_0_.1, bf16[4,16,640]{2,1,0:T(8,128)(2,1)S(1)} %pad_maximum_fusion.4.refs_1_), custom_call_target="tpu_custom_call" | custom-call | flops 268435456 | bytes 8388608 | tf_op jit(solution)/shard_map/build/pallas_call | solution.py:424
  24.1 0.6 collective-permute-start.10
  24.7 4.6 %build.3 = (bf16[32,4,256,256]{3,2,1,0:T(8,128)(2,1)S(1)}, s32[69]{0:T(128)S(1)}, f32[16,256]{1,0:T(8,128)S(1)}) custom-call(s32[2]{0:T(128)S(1)} %pad_add_fusion.place, s32[8,64]{1,0:T(8,128)S(1)} %add_add_fusion.2.direct, bf16[8,256,32]{2,1,0:T(8,128)(2,1)S(1)} %get-tuple-element.30.refs_0_, ...), custom_call_target="tpu_custom_call", output_to_operand_aliasing={{0}: (5, {})} | custom-call | flops 268435456 | bytes 8388608 | tf_op jit(solution)/shard_map/build/pallas_call | solution.py:424
  29.3 1.2 %collective-permute-done.10.refs_3_ = f32[4,32,512]{2,1,0:T(8,128)S(1)} collective-permute-done((f32[4,32,512]{2,1,0:T(8,128)S(1)}, f32[4,32,512]{2,1,0:T(8,128)S(1)}, u32[]{:S(2)}, u32[]{:S(2)}) %collective-permute-start.10) | collective-permute-done | bytes 262176 | tf_op jit(solution)/shard_map/ppermute | solution.py:348
  30.5 3.6 %collective-permute-start.13 = (f32[16,256]{1,0:T(8,128)S(1)}, f32[16,256]{1,0:T(8,128)S(1)}, u32[]{:S(2)}, u32[]{:S(2)}) collective-permute-start(f32[16,256]{1,0:T(8,128)S(1)} %get-tuple-element.47), channel_id=1, source_target_pairs={{0,24},{4,28},{8,16},{12,20},{16,8},{20,12},{24,0},{28,4},{1,25},{... | collective-permute-start | bytes 49160 | tf_op jit(solution)/shard_map/ppermute | solution.py:348
  34.1 0.8 collective-permute-start.11
  34.9 1.1 %collective-permute-done.13 = f32[16,256]{1,0:T(8,128)S(1)} collective-permute-done((f32[16,256]{1,0:T(8,128)S(1)}, f32[16,256]{1,0:T(8,128)S(1)}, u32[]{:S(2)}, u32[]{:S(2)}) %collective-permute-start.13) | collective-permute-done | bytes 16416 | tf_op jit(solution)/shard_map/ppermute | solution.py:348
  36.1 2.7 %collective-permute-done.12 = f32[16,256]{1,0:T(8,128)S(1)} collective-permute-done((f32[16,256]{1,0:T(8,128)S(1)}, f32[16,256]{1,0:T(8,128)S(1)}, u32[]{:S(2)}, u32[]{:S(2)}) %collective-permute-start.12) | collective-permute-done | bytes 16416 | tf_op jit(solution)/shard_map/ppermute | solution.py:348
  38.8 1.6 %collective-permute-start.14 = (f32[16,256]{1,0:T(8,128)S(1)}, f32[16,256]{1,0:T(8,128)S(1)}, u32[]{:S(2)}, u32[]{:S(2)}) collective-permute-start(f32[16,256]{1,0:T(8,128)S(1)} %add_add_fusion.1), channel_id=1, source_target_pairs={{0,4},{4,0},{8,12},{12,8},{16,20},{20,16},{24,28},{28,24},{1,5},{5... | collective-permute-start | bytes 49160 | tf_op jit(solution)/shard_map/ppermute | solution.py:348
  40.4 2.2 %collective-permute-done.14 = f32[16,256]{1,0:T(8,128)S(1)} collective-permute-done((f32[16,256]{1,0:T(8,128)S(1)}, f32[16,256]{1,0:T(8,128)S(1)}, u32[]{:S(2)}, u32[]{:S(2)}) %collective-permute-start.14) | collective-permute-done | bytes 16416 | tf_op jit(solution)/shard_map/ppermute | solution.py:348
  42.6 3.1 %first.1 = (f32[32,512]{1,0:T(8,128)S(1)}, f32[32,512]{1,0:T(8,128)S(1)}, f32[2,32,512]{2,1,0:T(8,128)S(1)}, f32[8,512]{1,0:T(8,128)S(1)}) custom-call(s32[2]{0:T(128)S(1)} %pad_add_fusion.place, bf16[32,4,256,256]{3,2,1,0:T(8,128)(2,1)S(1)} %get-tuple-element.41.k_mat, s32[69]{0:T(128)S(1)} %get-tuple-element.42.refs_0_.listed, ...), custom_call_target="tpu_custom_call" | custom-call | flops 536870912 | bytes 8388608 | tf_op jit(solution)/shard_map/first/pallas_call | solution.py:478
  45.8 1.3 %collective-permute-done.15 = f32[2,32,512]{2,1,0:T(8,128)S(1)} collective-permute-done((f32[2,32,512]{2,1,0:T(8,128)S(1)}, f32[2,32,512]{2,1,0:T(8,128)S(1)}, u32[]{:S(2)}, u32[]{:S(2)}) %collective-permute-start.15) | collective-permute-done | bytes 131104 | tf_op jit(solution)/shard_map/ppermute | solution.py:348
  47.2 1.6 %collective-permute-start.16 = (f32[72,512]{1,0:T(8,128)S(1)}, f32[72,512]{1,0:T(8,128)S(1)}, u32[]{:S(2)}, u32[]{:S(2)}) collective-permute-start(f32[72,512]{1,0:T(8,128)S(1)} %pad_maximum_fusion.2), channel_id=1, source_target_pairs={{0,2},{1,3},{2,0},{3,1},{4,6},{5,7},{6,4},{7,5},{8,10},{9,11},{10,... | collective-permute-start | bytes 442376 | tf_op jit(solution)/shard_map/ppermute | solution.py:348
  48.7 4.4 %collective-permute-done.16 = f32[72,512]{1,0:T(8,128)S(1)} collective-permute-done((f32[72,512]{1,0:T(8,128)S(1)}, f32[72,512]{1,0:T(8,128)S(1)}, u32[]{:S(2)}, u32[]{:S(2)}) %collective-permute-start.16) | collective-permute-done | bytes 147488 | tf_op jit(solution)/shard_map/ppermute | solution.py:348
  53.3 1.4 %collective-permute-done.17.s1_got = f32[2,40,512]{2,1,0:T(8,128)S(1)} collective-permute-done((f32[2,40,512]{2,1,0:T(8,128)S(1)}, f32[2,40,512]{2,1,0:T(8,128)S(1)}, u32[]{:S(2)}, u32[]{:S(2)}) %collective-permute-start.17) | collective-permute-done | bytes 163872 | tf_op jit(solution)/shard_map/ppermute | solution.py:348
  54.7 1.4 %second.3 = bf16[4,32,512]{2,1,0:T(8,128)(2,1)S(1)} custom-call(s32[2]{0:T(128)S(1)} %pad_add_fusion.place, bf16[32,4,256,256]{3,2,1,0:T(8,128)(2,1)S(1)} %get-tuple-element.41.k_mat, s32[69]{0:T(128)S(1)} %get-tuple-element.43.refs_1_.listed, f32[32,2048]{1,0:T(8,128)S(1)} %copy-done, f32[2,40,512]{2,1,0:T(8,128)S(1)} %pad_maximum_fusion.1.s1_own, ...), custom_call_target="tpu_custom_call" | custom-call | flops 268435456 | bytes 4194304 | tf_op jit(solution)/shard_map/second/pallas_call | solution.py:505
  56.1 2.1 %collective-permute-start.18 = (bf16[4,32,512]{2,1,0:T(8,128)(2,1)S(1)}, bf16[4,32,512]{2,1,0:T(8,128)(2,1)S(1)}, u32[]{:S(2)}, u32[]{:S(2)}) collective-permute-start(bf16[4,32,512]{2,1,0:T(8,128)(2,1)S(1)} %second.3), channel_id=1, source_target_pairs={{0,4},{4,0},{8,12},{12,8},{16,20},{20,16},{24,28},{28,24},{1,5},{5... | collective-permute-start | bytes 393224 | tf_op jit(solution)/shard_map/ppermute | solution.py:348
  58.1 1.6 %second.2 = f32[4,32,512]{2,1,0:T(8,128)S(1)} custom-call(s32[2]{0:T(128)S(1)} %pad_add_fusion.place, bf16[32,4,256,256]{3,2,1,0:T(8,128)(2,1)S(1)} %get-tuple-element.41.k_mat, s32[69]{0:T(128)S(1)} %get-tuple-element.42.refs_0_.listed, f32[32,2048]{1,0:T(8,128)S(1)} %copy-done, f32[2,40,512]{2,1,0:T(8,128)S(1)} %pad_maximum_fusion.1.s1_own, ...), custom_call_target="tpu_custom_call" | custom-call | flops 268435456 | bytes 4194304 | tf_op jit(solution)/shard_map/second/pallas_call | solution.py:505
  59.8 2.2 %collective-permute-done.18 = bf16[4,32,512]{2,1,0:T(8,128)(2,1)S(1)} collective-permute-done((bf16[4,32,512]{2,1,0:T(8,128)(2,1)S(1)}, bf16[4,32,512]{2,1,0:T(8,128)(2,1)S(1)}, u32[]{:S(2)}, u32[]{:S(2)}) %collective-permute-start.18) | collective-permute-done | bytes 131104 | tf_op jit(solution)/shard_map/ppermute | solution.py:348
  62.0 1.5 %collective-permute-start.21 = (bf16[32,512]{1,0:T(8,128)(2,1)S(1)}, bf16[32,512]{1,0:T(8,128)(2,1)S(1)}, u32[]{:S(2)}, u32[]{:S(2)}) collective-permute-start(bf16[32,512]{1,0:T(8,128)(2,1)S(1)} %get-tuple-element.60), channel_id=1, source_target_pairs={{0,24},{4,28},{8,16},{12,20},{16,8},{20,12},{24,0},{28,4},{1,25},{... | collective-permute-start | bytes 98312 | tf_op jit(solution)/shard_map/ppermute | solution.py:348
  63.5 1.1 %collective-permute-start.20 = (bf16[32,512]{1,0:T(8,128)(2,1)S(1)}, bf16[32,512]{1,0:T(8,128)(2,1)S(1)}, u32[]{:S(2)}, u32[]{:S(2)}) collective-permute-start(bf16[32,512]{1,0:T(8,128)(2,1)S(1)} %get-tuple-element.61), channel_id=1, source_target_pairs={{0,16},{4,20},{8,24},{12,28},{16,0},{20,4},{24,8},{28,12},{1,17},{... | collective-permute-start | bytes 98312 | tf_op jit(solution)/shard_map/ppermute | solution.py:348
  64.6 1.8 %collective-permute-start.19 = (bf16[32,512]{1,0:T(8,128)(2,1)S(1)}, bf16[32,512]{1,0:T(8,128)(2,1)S(1)}, u32[]{:S(2)}, u32[]{:S(2)}) collective-permute-start(bf16[32,512]{1,0:T(8,128)(2,1)S(1)} %get-tuple-element.62), channel_id=1, source_target_pairs={{0,8},{4,12},{8,0},{12,4},{16,24},{20,28},{24,16},{28,20},{1,9},{5... | collective-permute-start | bytes 98312 | tf_op jit(solution)/shard_map/ppermute | solution.py:348
  66.5 1.7 %collective-permute-done.21.refs_3_ = bf16[32,512]{1,0:T(8,128)(2,1)S(1)} collective-permute-done((bf16[32,512]{1,0:T(8,128)(2,1)S(1)}, bf16[32,512]{1,0:T(8,128)(2,1)S(1)}, u32[]{:S(2)}, u32[]{:S(2)}) %collective-permute-start.21) | collective-permute-done | bytes 32800 | tf_op jit(solution)/shard_map/ppermute | solution.py:348
  68.8 0.7 products.1
  69.5 1.2 %collective-permute-start.22 = (f32[32,512]{1,0:T(8,128)S(1)}, f32[32,512]{1,0:T(8,128)S(1)}, u32[]{:S(2)}, u32[]{:S(2)}) collective-permute-start(f32[32,512]{1,0:T(8,128)S(1)} %get-tuple-element.54), channel_id=1, source_target_pairs={{0,2},{1,3},{2,0},{3,1},{4,6},{5,7},{6,4},{7,5},{8,10},{9,11},{10,... | collective-permute-start | bytes 196616 | tf_op jit(solution)/shard_map/ppermute | solution.py:348
  70.7 2.6 %collective-permute-start.26 = (f32[32,128]{1,0:T(8,128)S(1)}, f32[32,128]{1,0:T(8,128)S(1)}, u32[]{:S(2)}, u32[]{:S(2)}) collective-permute-start(f32[32,128]{1,0:T(8,128)S(1)} %get-tuple-element.55), channel_id=1, source_target_pairs={{0,24},{4,28},{8,16},{12,20},{16,8},{20,12},{24,0},{28,4},{1,25},{... | collective-permute-start | bytes 49160 | tf_op jit(solution)/shard_map/ppermute | solution.py:348
  73.2 0.8 collective-permute-start.25
  74.0 1.0 %collective-permute-start.24 = (f32[32,128]{1,0:T(8,128)S(1)}, f32[32,128]{1,0:T(8,128)S(1)}, u32[]{:S(2)}, u32[]{:S(2)}) collective-permute-start(f32[32,128]{1,0:T(8,128)S(1)} %get-tuple-element.55), channel_id=1, source_target_pairs={{0,8},{4,12},{8,0},{12,4},{16,24},{20,28},{24,16},{28,20},{1,9},{5... | collective-permute-start | bytes 49160 | tf_op jit(solution)/shard_map/ppermute | solution.py:348
  75.2 1.1 %collective-permute-done.26 = f32[32,128]{1,0:T(8,128)S(1)} collective-permute-done((f32[32,128]{1,0:T(8,128)S(1)}, f32[32,128]{1,0:T(8,128)S(1)}, u32[]{:S(2)}, u32[]{:S(2)}) %collective-permute-start.26) | collective-permute-done | bytes 16416 | tf_op jit(solution)/shard_map/ppermute | solution.py:348
  76.2 1.7 %collective-permute-done.25 = f32[32,128]{1,0:T(8,128)S(1)} collective-permute-done((f32[32,128]{1,0:T(8,128)S(1)}, f32[32,128]{1,0:T(8,128)S(1)}, u32[]{:S(2)}, u32[]{:S(2)}) %collective-permute-start.25) | collective-permute-done | bytes 16416 | tf_op jit(solution)/shard_map/ppermute | solution.py:348
  77.9 0.7 collective-permute-start.27
  78.7 3.1 %collective-permute-done.27 = f32[32,128]{1,0:T(8,128)S(1)} collective-permute-done((f32[32,128]{1,0:T(8,128)S(1)}, f32[32,128]{1,0:T(8,128)S(1)}, u32[]{:S(2)}, u32[]{:S(2)}) %collective-permute-start.27) | collective-permute-done | bytes 16416 | tf_op jit(solution)/shard_map/ppermute | solution.py:348
  81.8 0.9 %collective-permute-start.29 = (f32[32,128]{1,0:T(8,128)S(1)}, f32[32,128]{1,0:T(8,128)S(1)}, u32[]{:S(2)}, u32[]{:S(2)}) collective-permute-start(f32[32,128]{1,0:T(8,128)S(1)} %add.78.refs_2_), channel_id=1, source_target_pairs={{0,2},{1,3},{2,0},{3,1},{4,6},{5,7},{6,4},{7,5},{8,10},{9,11},{10,... | collective-permute-start | bytes 49160 | tf_op jit(solution)/shard_map/ppermute | solution.py:348
  82.7 0.9 %collective-permute-start.28 = (f32[32,128]{1,0:T(8,128)S(1)}, f32[32,128]{1,0:T(8,128)S(1)}, u32[]{:S(2)}, u32[]{:S(2)}) collective-permute-start(f32[32,128]{1,0:T(8,128)S(1)} %add.78.refs_2_), channel_id=1, source_target_pairs={{0,1},{1,0},{2,3},{3,2},{4,5},{5,4},{6,7},{7,6},{8,9},{9,8},{10,11... | collective-permute-start | bytes 49160 | tf_op jit(solution)/shard_map/ppermute | solution.py:348
  83.6 1.3 %collective-permute-done.30.refs_5_ = f32[32,128]{1,0:T(8,128)S(1)} collective-permute-done((f32[32,128]{1,0:T(8,128)S(1)}, f32[32,128]{1,0:T(8,128)S(1)}, u32[]{:S(2)}, u32[]{:S(2)}) %collective-permute-start.30) | collective-permute-done | bytes 16416 | tf_op jit(solution)/shard_map/ppermute | solution.py:348
  84.9 0.8 collective-permute-done.29.refs_4_
  85.7 1.7 %final.1 = (f32[32,2048]{1,0:T(8,128)}, f32[32,2048]{1,0:T(8,128)}) custom-call(s32[2]{0:T(128)S(1)} %pad_add_fusion.place, f32[32,2048]{1,0:T(8,128)S(1)} %copy-done, f32[2,40,512]{2,1,0:T(8,128)S(1)} %pad_maximum_fusion.1.s1_own, f32[2,40,512]{2,1,0:T(8,128)S(1)} %collective-permute-done.17.s1_got, f32[2,32,512]{2,1,0:T(8,128)S(1)} %pad_maximum_fusion.3.refs_0_, ...), custom_call_target="tpu_custom_call" | custom-call | tf_op jit(solution)/shard_map/final/pallas_call | solution.py:544
  (57 shorter events, 2.0 us)
Async XLA Ops:
  0.6 5.7 %collective-permute-start = (s32[8,6]{1,0:T(8,128)}, s32[8,6]{1,0:T(8,128)S(1)}, u32[]{:S(2)}, u32[]{:S(2)}) collective-permute-start(s32[8,6]{1,0:T(8,128)} %param.3), channel_id=1, source_target_pairs={{0,1},{1,0},{2,3},{3,2},{4,5},{5,4},{6,7},{7,6},{8,9},{9,8},{10,11... | collective-permute-start | bytes 584 | tf_op jit(solution)/shard_map/ppermute | solution.py:348
  1.1 5.3 %collective-permute-start.2 = (s32[8,6]{1,0:T(8,128)}, s32[8,6]{1,0:T(8,128)S(1)}, u32[]{:S(2)}, u32[]{:S(2)}) collective-permute-start(s32[8,6]{1,0:T(8,128)} %param.3), channel_id=1, source_target_pairs={{0,3},{1,2},{2,1},{3,0},{4,7},{5,6},{6,5},{7,4},{8,11},{9,10},{10,... | collective-permute-start | bytes 584 | tf_op jit(solution)/shard_map/ppermute | solution.py:348
  3.8 3.8 %collective-permute-start.1 = (s32[8,6]{1,0:T(8,128)}, s32[8,6]{1,0:T(8,128)S(1)}, u32[]{:S(2)}, u32[]{:S(2)}) collective-permute-start(s32[8,6]{1,0:T(8,128)} %param.3), channel_id=1, source_target_pairs={{0,2},{1,3},{2,0},{3,1},{4,6},{5,7},{6,4},{7,5},{8,10},{9,11},{10,... | collective-permute-start | bytes 584 | tf_op jit(solution)/shard_map/ppermute | solution.py:348
  7.9 8.1 %collective-permute-start.5 = (bf16[16,640]{1,0:T(8,128)(2,1)S(1)}, bf16[16,640]{1,0:T(8,128)(2,1)S(1)}, u32[]{:S(2)}, u32[]{:S(2)}) collective-permute-start(bf16[16,640]{1,0:T(8,128)(2,1)S(1)} %pad_maximum_fusion.5), channel_id=1, source_target_pairs={{0,24},{4,28},{8,16},{12,20},{16,8},{20,12},{24,0},{28,4},{1,25},{... | collective-permute-start | bytes 61448 | tf_op jit(solution)/shard_map/ppermute | solution.py:348
  11.6 5.2 %collective-permute-start.4 = (bf16[16,640]{1,0:T(8,128)(2,1)S(1)}, bf16[16,640]{1,0:T(8,128)(2,1)S(1)}, u32[]{:S(2)}, u32[]{:S(2)}) collective-permute-start(bf16[16,640]{1,0:T(8,128)(2,1)S(1)} %pad_maximum_fusion.5), channel_id=1, source_target_pairs={{0,16},{4,20},{8,24},{12,28},{16,0},{20,4},{24,8},{28,12},{1,17},{... | collective-permute-start | bytes 61448 | tf_op jit(solution)/shard_map/ppermute | solution.py:348
  11.6 5.2 %collective-permute-start.3 = (bf16[16,640]{1,0:T(8,128)(2,1)S(1)}, bf16[16,640]{1,0:T(8,128)(2,1)S(1)}, u32[]{:S(2)}, u32[]{:S(2)}) collective-permute-start(bf16[16,640]{1,0:T(8,128)(2,1)S(1)} %pad_maximum_fusion.5), channel_id=1, source_target_pairs={{0,8},{4,12},{8,0},{12,4},{16,24},{20,28},{24,16},{28,20},{1,9},{5... | collective-permute-start | bytes 61448 | tf_op jit(solution)/shard_map/ppermute | solution.py:348
  12.3 11.7 %collective-permute-start.9 = (f32[32,512]{1,0:T(8,128)S(1)}, f32[32,512]{1,0:T(8,128)S(1)}, u32[]{:S(2)}, u32[]{:S(2)}) collective-permute-start(f32[32,512]{1,0:T(8,128)S(1)} %constant_dynamic-slice_fusion), channel_id=1, source_target_pairs={{0,24},{4,28},{8,16},{12,20},{16,8},{20,12},{24,0},{28,4},{1,25},{... | collective-permute-start | bytes 196616 | tf_op jit(solution)/shard_map/ppermute | solution.py:348
  15.9 8.1 %collective-permute-start.8 = (f32[32,512]{1,0:T(8,128)S(1)}, f32[32,512]{1,0:T(8,128)S(1)}, u32[]{:S(2)}, u32[]{:S(2)}) collective-permute-start(f32[32,512]{1,0:T(8,128)S(1)} %constant_dynamic-slice_fusion), channel_id=1, source_target_pairs={{0,16},{4,20},{8,24},{12,28},{16,0},{20,4},{24,8},{28,12},{1,17},{... | collective-permute-start | bytes 196616 | tf_op jit(solution)/shard_map/ppermute | solution.py:348
  15.9 8.1 %collective-permute-start.7 = (f32[32,512]{1,0:T(8,128)S(1)}, f32[32,512]{1,0:T(8,128)S(1)}, u32[]{:S(2)}, u32[]{:S(2)}) collective-permute-start(f32[32,512]{1,0:T(8,128)S(1)} %constant_dynamic-slice_fusion), channel_id=1, source_target_pairs={{0,8},{4,12},{8,0},{12,4},{16,24},{20,28},{24,16},{28,20},{1,9},{5... | collective-permute-start | bytes 196616 | tf_op jit(solution)/shard_map/ppermute | solution.py:348
  16.8 7.3 %collective-permute-start.6 = (bf16[4,16,640]{2,1,0:T(8,128)(2,1)S(1)}, bf16[4,16,640]{2,1,0:T(8,128)(2,1)S(1)}, u32[]{:S(2)}, u32[]{:S(2)}) collective-permute-start(bf16[4,16,640]{2,1,0:T(8,128)(2,1)S(1)} %pad_maximum_fusion.4.refs_1_), channel_id=1, source_target_pairs={{0,4},{4,0},{8,12},{12,8},{16,20},{20,16},{24,28},{28,24},{1,5},{5... | collective-permute-start | bytes 245768 | tf_op jit(solution)/shard_map/ppermute | solution.py:348
  24.1 6.4 %collective-permute-start.10 = (f32[4,32,512]{2,1,0:T(8,128)S(1)}, f32[4,32,512]{2,1,0:T(8,128)S(1)}, u32[]{:S(2)}, u32[]{:S(2)}) collective-permute-start(f32[4,32,512]{2,1,0:T(8,128)S(1)} %pad_maximum_fusion.refs_2_), channel_id=1, source_target_pairs={{0,4},{4,0},{8,12},{12,8},{16,20},{20,16},{24,28},{28,24},{1,5},{5... | collective-permute-start | bytes 786440 | tf_op jit(solution)/shard_map/ppermute | solution.py:348
  24.7 30.0 %copy-start = (f32[32,2048]{1,0:T(8,128)S(1)}, f32[32,2048]{1,0:T(8,128)}, u32[]{:S(2)}) copy-start(f32[32,2048]{1,0:T(8,128)} %t_ref.7) | copy-start | bytes 786436
  30.5 5.5 %collective-permute-start.13 = (f32[16,256]{1,0:T(8,128)S(1)}, f32[16,256]{1,0:T(8,128)S(1)}, u32[]{:S(2)}, u32[]{:S(2)}) collective-permute-start(f32[16,256]{1,0:T(8,128)S(1)} %get-tuple-element.47), channel_id=1, source_target_pairs={{0,24},{4,28},{8,16},{12,20},{16,8},{20,12},{24,0},{28,4},{1,25},{... | collective-permute-start | bytes 49160 | tf_op jit(solution)/shard_map/ppermute | solution.py:348
  34.1 4.6 %collective-permute-start.12 = (f32[16,256]{1,0:T(8,128)S(1)}, f32[16,256]{1,0:T(8,128)S(1)}, u32[]{:S(2)}, u32[]{:S(2)}) collective-permute-start(f32[16,256]{1,0:T(8,128)S(1)} %get-tuple-element.47), channel_id=1, source_target_pairs={{0,16},{4,20},{8,24},{12,28},{16,0},{20,4},{24,8},{28,12},{1,17},{... | collective-permute-start | bytes 49160 | tf_op jit(solution)/shard_map/ppermute | solution.py:348
  34.1 4.6 %collective-permute-start.11 = (f32[16,256]{1,0:T(8,128)S(1)}, f32[16,256]{1,0:T(8,128)S(1)}, u32[]{:S(2)}, u32[]{:S(2)}) collective-permute-start(f32[16,256]{1,0:T(8,128)S(1)} %get-tuple-element.47), channel_id=1, source_target_pairs={{0,8},{4,12},{8,0},{12,4},{16,24},{20,28},{24,16},{28,20},{1,9},{5... | collective-permute-start | bytes 49160 | tf_op jit(solution)/shard_map/ppermute | solution.py:348
  38.8 3.8 %collective-permute-start.14 = (f32[16,256]{1,0:T(8,128)S(1)}, f32[16,256]{1,0:T(8,128)S(1)}, u32[]{:S(2)}, u32[]{:S(2)}) collective-permute-start(f32[16,256]{1,0:T(8,128)S(1)} %add_add_fusion.1), channel_id=1, source_target_pairs={{0,4},{4,0},{8,12},{12,8},{16,20},{20,16},{24,28},{28,24},{1,5},{5... | collective-permute-start | bytes 49160 | tf_op jit(solution)/shard_map/ppermute | solution.py:348
  45.7 1.4 %collective-permute-start.15 = (f32[2,32,512]{2,1,0:T(8,128)S(1)}, f32[2,32,512]{2,1,0:T(8,128)S(1)}, u32[]{:S(2)}, u32[]{:S(2)}) collective-permute-start(f32[2,32,512]{2,1,0:T(8,128)S(1)} %get-tuple-element.49), channel_id=1, source_target_pairs={{0,1},{1,0},{2,3},{3,2},{4,5},{5,4},{6,7},{7,6},{8,9},{9,8},{10,11... | collective-permute-start | bytes 393224 | tf_op jit(solution)/shard_map/ppermute | solution.py:348
  47.2 6.0 %collective-permute-start.16 = (f32[72,512]{1,0:T(8,128)S(1)}, f32[72,512]{1,0:T(8,128)S(1)}, u32[]{:S(2)}, u32[]{:S(2)}) collective-permute-start(f32[72,512]{1,0:T(8,128)S(1)} %pad_maximum_fusion.2), channel_id=1, source_target_pairs={{0,2},{1,3},{2,0},{3,1},{4,6},{5,7},{6,4},{7,5},{8,10},{9,11},{10,... | collective-permute-start | bytes 442376 | tf_op jit(solution)/shard_map/ppermute | solution.py:348
  53.2 1.5 %collective-permute-start.17 = (f32[2,40,512]{2,1,0:T(8,128)S(1)}, f32[2,40,512]{2,1,0:T(8,128)S(1)}, u32[]{:S(2)}, u32[]{:S(2)}) collective-permute-start(f32[2,40,512]{2,1,0:T(8,128)S(1)} %pad_maximum_fusion.1.s1_own), channel_id=1, source_target_pairs={{0,1},{1,0},{2,3},{3,2},{4,5},{5,4},{6,7},{7,6},{8,9},{9,8},{10,11... | collective-permute-start | bytes 491528 | tf_op jit(solution)/shard_map/ppermute | solution.py:348
  56.1 5.9 %collective-permute-start.18 = (bf16[4,32,512]{2,1,0:T(8,128)(2,1)S(1)}, bf16[4,32,512]{2,1,0:T(8,128)(2,1)S(1)}, u32[]{:S(2)}, u32[]{:S(2)}) collective-permute-start(bf16[4,32,512]{2,1,0:T(8,128)(2,1)S(1)} %second.3), channel_id=1, source_target_pairs={{0,4},{4,0},{8,12},{12,8},{16,20},{20,16},{24,28},{28,24},{1,5},{5... | collective-permute-start | bytes 393224 | tf_op jit(solution)/shard_map/ppermute | solution.py:348
  62.0 6.1 %collective-permute-start.21 = (bf16[32,512]{1,0:T(8,128)(2,1)S(1)}, bf16[32,512]{1,0:T(8,128)(2,1)S(1)}, u32[]{:S(2)}, u32[]{:S(2)}) collective-permute-start(bf16[32,512]{1,0:T(8,128)(2,1)S(1)} %get-tuple-element.60), channel_id=1, source_target_pairs={{0,24},{4,28},{8,16},{12,20},{16,8},{20,12},{24,0},{28,4},{1,25},{... | collective-permute-start | bytes 98312 | tf_op jit(solution)/shard_map/ppermute | solution.py:348
  63.5 5.0 %collective-permute-start.20 = (bf16[32,512]{1,0:T(8,128)(2,1)S(1)}, bf16[32,512]{1,0:T(8,128)(2,1)S(1)}, u32[]{:S(2)}, u32[]{:S(2)}) collective-permute-start(bf16[32,512]{1,0:T(8,128)(2,1)S(1)} %get-tuple-element.61), channel_id=1, source_target_pairs={{0,16},{4,20},{8,24},{12,28},{16,0},{20,4},{24,8},{28,12},{1,17},{... | collective-permute-start | bytes 98312 | tf_op jit(solution)/shard_map/ppermute | solution.py:348
  64.6 4.2 %collective-permute-start.19 = (bf16[32,512]{1,0:T(8,128)(2,1)S(1)}, bf16[32,512]{1,0:T(8,128)(2,1)S(1)}, u32[]{:S(2)}, u32[]{:S(2)}) collective-permute-start(bf16[32,512]{1,0:T(8,128)(2,1)S(1)} %get-tuple-element.62), channel_id=1, source_target_pairs={{0,8},{4,12},{8,0},{12,4},{16,24},{20,28},{24,16},{28,20},{1,9},{5... | collective-permute-start | bytes 98312 | tf_op jit(solution)/shard_map/ppermute | solution.py:348
  69.5 5.6 %collective-permute-start.22 = (f32[32,512]{1,0:T(8,128)S(1)}, f32[32,512]{1,0:T(8,128)S(1)}, u32[]{:S(2)}, u32[]{:S(2)}) collective-permute-start(f32[32,512]{1,0:T(8,128)S(1)} %get-tuple-element.54), channel_id=1, source_target_pairs={{0,2},{1,3},{2,0},{3,1},{4,6},{5,7},{6,4},{7,5},{8,10},{9,11},{10,... | collective-permute-start | bytes 196616 | tf_op jit(solution)/shard_map/ppermute | solution.py:348
  70.7 5.5 %collective-permute-start.26 = (f32[32,128]{1,0:T(8,128)S(1)}, f32[32,128]{1,0:T(8,128)S(1)}, u32[]{:S(2)}, u32[]{:S(2)}) collective-permute-start(f32[32,128]{1,0:T(8,128)S(1)} %get-tuple-element.55), channel_id=1, source_target_pairs={{0,24},{4,28},{8,16},{12,20},{16,8},{20,12},{24,0},{28,4},{1,25},{... | collective-permute-start | bytes 49160 | tf_op jit(solution)/shard_map/ppermute | solution.py:348
  73.2 4.7 %collective-permute-start.25 = (f32[32,128]{1,0:T(8,128)S(1)}, f32[32,128]{1,0:T(8,128)S(1)}, u32[]{:S(2)}, u32[]{:S(2)}) collective-permute-start(f32[32,128]{1,0:T(8,128)S(1)} %get-tuple-element.55), channel_id=1, source_target_pairs={{0,16},{4,20},{8,24},{12,28},{16,0},{20,4},{24,8},{28,12},{1,17},{... | collective-permute-start | bytes 49160 | tf_op jit(solution)/shard_map/ppermute | solution.py:348
  74.0 3.9 %collective-permute-start.24 = (f32[32,128]{1,0:T(8,128)S(1)}, f32[32,128]{1,0:T(8,128)S(1)}, u32[]{:S(2)}, u32[]{:S(2)}) collective-permute-start(f32[32,128]{1,0:T(8,128)S(1)} %get-tuple-element.55), channel_id=1, source_target_pairs={{0,8},{4,12},{8,0},{12,4},{16,24},{20,28},{24,16},{28,20},{1,9},{5... | collective-permute-start | bytes 49160 | tf_op jit(solution)/shard_map/ppermute | solution.py:348
  75.1 10.6 %collective-permute-start.23 = (f32[2,32,512]{2,1,0:T(8,128)S(1)}, f32[2,32,512]{2,1,0:T(8,128)S(1)}, u32[]{:S(2)}, u32[]{:S(2)}) collective-permute-start(f32[2,32,512]{2,1,0:T(8,128)S(1)} %pad_maximum_fusion.3.refs_0_), channel_id=1, source_target_pairs={{0,1},{1,0},{2,3},{3,2},{4,5},{5,4},{6,7},{7,6},{8,9},{9,8},{10,11... | collective-permute-start | bytes 393224 | tf_op jit(solution)/shard_map/ppermute | solution.py:348
  77.9 3.8 %collective-permute-start.27 = (f32[32,128]{1,0:T(8,128)S(1)}, f32[32,128]{1,0:T(8,128)S(1)}, u32[]{:S(2)}, u32[]{:S(2)}) collective-permute-start(f32[32,128]{1,0:T(8,128)S(1)} %add_add_fusion), channel_id=1, source_target_pairs={{0,4},{4,0},{8,12},{12,8},{16,20},{20,16},{24,28},{28,24},{1,5},{5... | collective-permute-start | bytes 49160 | tf_op jit(solution)/shard_map/ppermute | solution.py:348
  81.8 3.2 %collective-permute-start.30 = (f32[32,128]{1,0:T(8,128)S(1)}, f32[32,128]{1,0:T(8,128)S(1)}, u32[]{:S(2)}, u32[]{:S(2)}) collective-permute-start(f32[32,128]{1,0:T(8,128)S(1)} %add.78.refs_2_), channel_id=1, source_target_pairs={{0,3},{1,2},{2,1},{3,0},{4,7},{5,6},{6,5},{7,4},{8,11},{9,10},{10,... | collective-permute-start | bytes 49160 | tf_op jit(solution)/shard_map/ppermute | solution.py:348
  81.8 3.9 %collective-permute-start.29 = (f32[32,128]{1,0:T(8,128)S(1)}, f32[32,128]{1,0:T(8,128)S(1)}, u32[]{:S(2)}, u32[]{:S(2)}) collective-permute-start(f32[32,128]{1,0:T(8,128)S(1)} %add.78.refs_2_), channel_id=1, source_target_pairs={{0,2},{1,3},{2,0},{3,1},{4,6},{5,7},{6,4},{7,5},{8,10},{9,11},{10,... | collective-permute-start | bytes 49160 | tf_op jit(solution)/shard_map/ppermute | solution.py:348
  82.7 3.0 %collective-permute-start.28 = (f32[32,128]{1,0:T(8,128)S(1)}, f32[32,128]{1,0:T(8,128)S(1)}, u32[]{:S(2)}, u32[]{:S(2)}) collective-permute-start(f32[32,128]{1,0:T(8,128)S(1)} %add.78.refs_2_), channel_id=1, source_target_pairs={{0,1},{1,0},{2,3},{3,2},{4,5},{5,4},{6,7},{7,6},{8,9},{9,8},{10,11... | collective-permute-start | bytes 49160 | tf_op jit(solution)/shard_map/ppermute | solution.py:348

commit v8 on v7

--- a/solution.py
+++ b/solution.py
@@ -232,8 +232,9 @@
 
 def first_kernel(cfg, place, k_mat, *refs):
     n = cfg.parts
-    lists, pieces, inv_ref, refs = refs[:n], refs[n:2 * n], refs[2 * n], refs[2 * n + 1:]
-    near, near_y, cross, own_inv, z_acc, w_all, *ring = refs
+    lists, pieces, refs = refs[:n], refs[n:2 * n], refs[2 * n:]
+    lent, refs = (refs[:n], refs[n:]) if n > 1 else (None, refs)
+    inv_ref, near, near_y, cross, own_inv, z_acc, w_all, *ring = refs
     kbuf, sems = ring or (None, None)
     col = place[1]
     own_rows, block_len = cfg.own_rows, cfg.block_len
@@ -241,15 +242,32 @@
     for part, (listed, piece) in enumerate(zip(lists, pieces)):
         held = piece.shape[0]
 
-        def prepare(m, carry, part=part, piece=piece):
+        def prepare(m, load, part=part):
             z = slot_of(cfg, place, m)
             for k in range(own_rows):
-                w = piece[m, :, k * block_len:(k + 1) * block_len]
+                w = load(slice(k * block_len, (k + 1) * block_len))
                 at = row_of(cfg, place, part, z) * own_rows + k
                 w_all[z * own_rows + k] = (w * inv_ref[pl.ds(at, 1), :]).astype(BF16)
-            return carry
-
-        lax.fori_loop(0, held, prepare, 0, unroll=held <= 4)
+
+        if lent is None:
+
+            def one(m, carry, piece=piece, prepare=prepare):
+                prepare(m, lambda cols: piece[m, :, cols])
+                return carry
+
+            lax.fori_loop(0, held, one, 0)
+        else:
+            own_len = own_rows * block_len
+
+            @pl.when(col & 1 == 1)
+            def _(piece=piece, prepare=prepare):
+                for m in range(held):
+                    prepare(m, lambda cols, m=m: piece[m, :, own_len:][:, cols])
+
+            @pl.when(col & 1 == 0)
+            def _(piece=lent[part], prepare=prepare):
+                for m in range(held):
+                    prepare(m, lambda cols, m=m: piece[m, :, cols])
 
         def product(i, j, block):
             return lax.dot_general(
@@ -313,11 +331,11 @@
 
 
 def final_kernel(place, t_ref, s1_own, s1_got, *refs):
-    grown, all_dots = pieces_of(refs[0], refs[1]), refs[2:6]
-    sol_hbm, res_hbm, sol_ref, res_ref, sems = refs[6:]
+    grown, all_dots = pieces_of(refs[0], refs[1]), refs[2:4]
+    sol_hbm, res_hbm, sol_ref, res_ref, sems = refs[4:]
     s1s = pieces_of(s1_own, s1_got)
     outputs, own_len = grown[0].shape
-    dots = pair_sum([ref[...] for ref in all_dots])
+    dots = jnp.where(place[1] & 1 == 1, all_dots[0][...], all_dots[1][...])
     tt, ts1, s1s1, ts2, s1s2 = (dots[:, n:n + 1] for n in range(5))
     a1 = tt / (REG * tt + ts1)
     p = 1.0 - REG * a1
@@ -346,6 +364,21 @@
 def swap(x, axis, d):
     size = lax.axis_size(axis)
     return lax.ppermute(x, axis, [(i, i ^ d) for i in range(size)])
+
+
+def odd_swap(x, row_d, col_d):
+    n_rows, n_cols = lax.axis_size("rows"), lax.axis_size("cols")
+    pairs = [
+        (r * n_cols + c, (r ^ row_d) * n_cols + (c ^ col_d))
+        for r in range(n_rows)
+        for c in range(1, n_cols, 2)
+    ]
+    return lax.ppermute(x, ("rows", "cols"), pairs)
+
+
+def lend(x):
+    size = lax.axis_size("cols")
+    return lax.ppermute(x, "cols", [(c, c ^ 1) for c in range(1, size, 2)])
 
 
 def along_z(x):
@@ -411,7 +444,6 @@
     coded = own_counts.reshape(-1)
     coded = jnp.pad(coded, (0, dim * LANES - coded.shape[0])).reshape(dim, LANES).astype(BF16)
     packed = jnp.concatenate([own(points), coded], axis=1)
-    own_t = own(targets)
 
     def build(part, *operands):
         first, last = part == 0, part == parts - 1
@@ -453,19 +485,22 @@
 
     near = pltpu.with_memory_space_constraint(points, pltpu.HBM)
     if direct_rows:
-        packed, early_t = lax.optimization_barrier((packed, own_t))
+        both_t = lax.dynamic_slice_in_dim(targets, (col - (col & 1)) * own_len, 2 * own_len, 1)
+        packed, both_t = lax.optimization_barrier((packed, both_t))
         same, other = across_x(jnp.stack(along_z(packed)))
-        t_same = along_z(early_t)
+        t_same = [both_t] + [odd_swap(both_t, d, 0) for d in range(2, n_rows, 2)]
         k_mat, list0, degree, lhs = build(0, near, same)
         degree, other, *t_same = lax.optimization_barrier((degree, other, *t_same))
-        t_same, t_other = across_x(jnp.stack(t_same))
+        t_same = jnp.stack(t_same)
+        t_other = odd_swap(t_same, 1, 0)
         other, t_same = lax.optimization_barrier((other, t_same))
         k_mat, list1, degree = build(1, lhs, degree, other, k_mat)
         degree, t_other = lax.optimization_barrier((degree, t_other))
-        t_pieces, k_lists = [t_same, t_other], [list0, list1]
+        t_pieces = [t_same, t_other, lend(t_same), lend(t_other)]
+        k_lists = [list0, list1]
     else:
         k_mat, list0, degree, _ = build(0, near, lax.all_gather(packed, "rows"))
-        t_pieces, k_lists = [lax.all_gather(own_t, "rows")], [list0]
+        t_pieces, k_lists = [lax.all_gather(own(targets), "rows")], [list0]
     inv = 1.0 / jnp.sqrt(1.0 + total_rows(degree))
 
     def cost(n):
@@ -478,7 +513,7 @@
     near_z, near_y, cross_z, tail = pl.pallas_call(
         functools.partial(first_kernel, cfg),
         out_shape=[shape(outputs, own_len)] * 2 + [shape(2, outputs, own_len), shape(8, own_len)],
-        in_specs=[SMEM, k_spec] + [SMEM] * parts + [VMEM] * (parts + 1),
+        in_specs=[SMEM, k_spec] + [SMEM] * parts + [VMEM] * (len(t_pieces) + 1),
         out_specs=[VMEM] * 4,
         scratch_shapes=[
             pltpu.VMEM((block_rows, outputs, block_len), F32),
@@ -534,17 +569,20 @@
         name="products",
     )(place, held_t, s1_own, *z2)
     if direct_rows:
-        dots = pair_sum(across_x(pair_sum(along_z(dots))))
+        dots = dots + swap(dots, "cols", 1)
+        dots = pair_sum([dots] + [odd_swap(dots, d, 0) for d in range(2, n_rows, 2)])
+        dots = pair_sum([dots, odd_swap(dots, 1, 0), odd_swap(dots, 0, 2), odd_swap(dots, 1, 2)])
+        dots = [dots, lend(dots)]
     else:
-        dots = lax.psum(dots, "rows")
+        dots = [lax.psum(dots, ("rows", "cols"))] * 2
     grown = jnp.stack([grown, swap(grown, "cols", 2)])
-    ends = (s1_own, s1_got, grown, swap(grown, "cols", 1), *direct_cols(dots))
+    ends = (s1_own, s1_got, grown, swap(grown, "cols", 1), *dots)
     ends = [pltpu.with_memory_space_constraint(x, pltpu.VMEM) for x in ends]
 
     return pl.pallas_call(
         final_kernel,
         out_shape=(shape(outputs, npoints), shape(outputs, npoints)),
-        in_specs=[SMEM] + [VMEM] * 9,
+        in_specs=[SMEM] + [VMEM] * 7,
         out_specs=(HBM, HBM),
         scratch_shapes=[
             pltpu.VMEM((4, outputs, own_len), F32),

time: 87.7 us -> 101 us (1.15)
  starting transfers between devices: 36.6 us -> 52 us
  waiting for transfers between devices: 27.8 us -> 25.5 us
    ppermute x0 -> x13, starting transfers between devices: none -> 10.5 us  [the longest x10 6.65 us: odd_swap(): return lax.ppermute(x, ('rows', 'cols'), pairs)]
    ppermute x31 -> x21, starting transfers between devices: 36.6 us -> 41.5 us  [swap(): return lax.ppermute(x, axis, [(i, i ^ d) for i in range(size)])]
    ppermute x31 -> x21, waiting for transfers between devices: 27.8 us -> 23.3 us  [swap(): return lax.ppermute(x, axis, [(i, i ^ d) for i in range(size)])]
    ppermute x0 -> x13, waiting for transfers between devices: none -> 2.27 us  [the longest x3 2.25 us: lend(): return lax.ppermute(x, 'cols', [(c, c ^ 1) for c in range(1, size, 2)])]
  transfers between devices with their start and end apart: 31 -> 34, of which waited for: 17 -> 15; matrix products, arithmetic and copies ran while one was open for 3% -> 3% of each run, Pallas kernels for 14% -> 12%
where the time goes in v8:
time: 101 us
  starting transfers between devices  52 us (51%)
  waiting for transfers between devices  25.5 us (25%)
  Pallas kernels  18.8 us (19%)
  local copies, waits for them, and re-layouts  2.83 us (3%)
    ppermute x21, starting transfers between devices, swap(): return lax.ppermute(x, axis, [(i, i ^ d) for i in range(size)])  41.5 us
    ppermute x21, waiting for transfers between devices, swap(): return lax.ppermute(x, axis, [(i, i ^ d) for i in range(size)])  23.3 us
    pallas_call x2, Pallas kernels, build(): pl.pallas_call(functools.partial(build_kernel, cfg, part), out_shape=out,...  10.2 us
    ppermute x10, starting transfers between devices, odd_swap(): return lax.ppermute(x, ('rows', 'cols'), pairs)  6.65 us
    ppermute x3, starting transfers between devices, lend(): return lax.ppermute(x, 'cols', [(c, c ^ 1) for c in range(1, size, 2)])  3.88 us
    pallas_call x1, Pallas kernels, local(): pl.pallas_call(functools.partial(first_kernel, cfg), out_shape=[shape(out...  3.11 us
    pallas_call x2, Pallas kernels, second(): pl.pallas_call(functools.partial(second_kernel, cfg, part), out_shape=sha...  3.06 us
    ppermute x3, waiting for transfers between devices, lend(): return lax.ppermute(x, 'cols', [(c, c ^ 1) for c in range(1, size, 2)])  2.25 us
  transfers between devices with their start and end apart: 34, of which 15 were waited for; matrix products, arithmetic and copies ran while one was open for 3% of the time, Pallas kernels for 12%

profile of v8, /device:TPU:0, one launch (start us, length us, event | category | flops | bytes accessed | tf_op | source)
XLA Modules:
  0.0 100.7 jit_solution(9438391160737966326)
XLA Ops:
  1.1 2.6 %collective-permute-start.2 = (s32[8,6]{1,0:T(8,128)}, s32[8,6]{1,0:T(8,128)S(1)}, u32[]{:S(2)}, u32[]{:S(2)}) collective-permute-start(s32[8,6]{1,0:T(8,128)} %param.3), channel_id=1, source_target_pairs={{0,3},{1,2},{2,1},{3,0},{4,7},{5,6},{6,5},{7,4},{8,11},{9,10},{10,... | collective-permute-start | bytes 584 | tf_op jit(solution)/shard_map/ppermute | solution.py:366
  3.8 0.8 copy.6
  4.7 0.7 constant_dynamic-slice_fusion.1
  5.5 0.9 constant_dynamic-slice_fusion
  6.7 0.9 collective-permute-done.1
  7.9 3.7 %collective-permute-start.5 = (bf16[16,640]{1,0:T(8,128)(2,1)S(1)}, bf16[16,640]{1,0:T(8,128)(2,1)S(1)}, u32[]{:S(2)}, u32[]{:S(2)}) collective-permute-start(bf16[16,640]{1,0:T(8,128)(2,1)S(1)} %pad_maximum_fusion.5), channel_id=1, source_target_pairs={{0,24},{4,28},{8,16},{12,20},{16,8},{20,12},{24,0},{28,4},{1,25},{... | collective-permute-start | bytes 61448 | tf_op jit(solution)/shard_map/ppermute | solution.py:366
  11.6 0.8 collective-permute-start.3
  13.0 0.7 collective-permute-start.8
  13.7 0.7 collective-permute-start.7
  14.4 1.9 %collective-permute-done.4 = bf16[16,640]{1,0:T(8,128)(2,1)S(1)} collective-permute-done((bf16[16,640]{1,0:T(8,128)(2,1)S(1)}, bf16[16,640]{1,0:T(8,128)(2,1)S(1)}, u32[]{:S(2)}, u32[]{:S(2)}) %collective-permute-start.4) | collective-permute-done | bytes 20512 | tf_op jit(solution)/shard_map/ppermute | solution.py:366
  16.3 1.6 %collective-permute-start.6 = (bf16[4,16,640]{2,1,0:T(8,128)(2,1)S(1)}, bf16[4,16,640]{2,1,0:T(8,128)(2,1)S(1)}, u32[]{:S(2)}, u32[]{:S(2)}) collective-permute-start(bf16[4,16,640]{2,1,0:T(8,128)(2,1)S(1)} %pad_maximum_fusion.4.refs_1_), channel_id=1, source_target_pairs={{0,4},{4,0},{8,12},{12,8},{16,20},{20,16},{24,28},{28,24},{1,5},{5... | collective-permute-start | bytes 245768 | tf_op jit(solution)/shard_map/ppermute | solution.py:366
  17.9 5.0 %build.2 = (bf16[32,4,256,256]{3,2,1,0:T(8,128)(2,1)S(1)}, s32[69]{0:T(128)S(1)}, f32[8,256]{1,0:T(8,128)S(1)}, bf16[8,256,32]{2,1,0:T(8,128)(2,1)S(1)}) custom-call(s32[2]{0:T(128)S(1)} %pad_add_fusion.place, s32[8,64]{1,0:T(8,128)S(1)} %add_add_fusion.3.direct, bf16[16,2048]{1,0:T(8,128)(2,1)} %refs_0_.1, bf16[4,16,640]{2,1,0:T(8,128)(2,1)S(1)} %pad_maximum_fusion.4.refs_1_), custom_call_target="tpu_custom_call" | custom-call | flops 268435456 | bytes 8388608 | tf_op jit(solution)/shard_map/build/pallas_call | solution.py:456
  23.0 0.7 collective-permute-start.10
  23.7 1.3 %collective-permute-start.11 = (f32[4,32,1024]{2,1,0:T(8,128)S(1)}, f32[4,32,1024]{2,1,0:T(8,128)S(1)}, u32[]{:S(2)}, u32[]{:S(2)}) collective-permute-start(f32[4,32,1024]{2,1,0:T(8,128)S(1)} %pad_maximum_fusion.refs_2_), channel_id=1, source_target_pairs={{1,0},{3,2},{5,4},{7,6},{9,8},{11,10},{13,12},{15,14},{17,16},{19,... | collective-permute-start | bytes 1572872 | tf_op jit(solution)/shard_map/ppermute | solution.py:381
  25.0 5.2 %build.3 = (bf16[32,4,256,256]{3,2,1,0:T(8,128)(2,1)S(1)}, s32[69]{0:T(128)S(1)}, f32[16,256]{1,0:T(8,128)S(1)}) custom-call(s32[2]{0:T(128)S(1)} %pad_add_fusion.place, s32[8,64]{1,0:T(8,128)S(1)} %add_add_fusion.3.direct, bf16[8,256,32]{2,1,0:T(8,128)(2,1)S(1)} %get-tuple-element.30.refs_0_, ...), custom_call_target="tpu_custom_call", output_to_operand_aliasing={{0}: (5, {})} | custom-call | flops 268435456 | bytes 8388608 | tf_op jit(solution)/shard_map/build/pallas_call | solution.py:456
  30.3 1.3 %collective-permute-start.12 = (f32[4,32,1024]{2,1,0:T(8,128)S(1)}, f32[4,32,1024]{2,1,0:T(8,128)S(1)}, u32[]{:S(2)}, u32[]{:S(2)}) collective-permute-start(f32[4,32,1024]{2,1,0:T(8,128)S(1)} %collective-permute-done.10.refs_3_), channel_id=1, source_target_pairs={{1,0},{3,2},{5,4},{7,6},{9,8},{11,10},{13,12},{15,14},{17,16},{19,... | collective-permute-start | bytes 1572872 | tf_op jit(solution)/shard_map/ppermute | solution.py:381
  31.6 1.8 %collective-permute-start.15 = (f32[16,256]{1,0:T(8,128)S(1)}, f32[16,256]{1,0:T(8,128)S(1)}, u32[]{:S(2)}, u32[]{:S(2)}) collective-permute-start(f32[16,256]{1,0:T(8,128)S(1)} %get-tuple-element.47), channel_id=1, source_target_pairs={{0,24},{4,28},{8,16},{12,20},{16,8},{20,12},{24,0},{28,4},{1,25},{... | collective-permute-start | bytes 49160 | tf_op jit(solution)/shard_map/ppermute | solution.py:366
  33.4 1.7 %collective-permute-start.14 = (f32[16,256]{1,0:T(8,128)S(1)}, f32[16,256]{1,0:T(8,128)S(1)}, u32[]{:S(2)}, u32[]{:S(2)}) collective-permute-start(f32[16,256]{1,0:T(8,128)S(1)} %get-tuple-element.47), channel_id=1, source_target_pairs={{0,16},{4,20},{8,24},{12,28},{16,0},{20,4},{24,8},{28,12},{1,17},{... | collective-permute-start | bytes 49160 | tf_op jit(solution)/shard_map/ppermute | solution.py:366
  35.1 0.9 collective-permute-start.13
  36.0 1.1 %collective-permute-done.15 = f32[16,256]{1,0:T(8,128)S(1)} collective-permute-done((f32[16,256]{1,0:T(8,128)S(1)}, f32[16,256]{1,0:T(8,128)S(1)}, u32[]{:S(2)}, u32[]{:S(2)}) %collective-permute-start.15) | collective-permute-done | bytes 16416 | tf_op jit(solution)/shard_map/ppermute | solution.py:366
  37.2 0.9 collective-permute-done.14
  38.0 0.8 collective-permute-done.13
  39.5 3.2 %collective-permute-done.16 = f32[16,256]{1,0:T(8,128)S(1)} collective-permute-done((f32[16,256]{1,0:T(8,128)S(1)}, f32[16,256]{1,0:T(8,128)S(1)}, u32[]{:S(2)}, u32[]{:S(2)}) %collective-permute-start.16) | collective-permute-done | bytes 16416 | tf_op jit(solution)/shard_map/ppermute | solution.py:366
  42.7 3.1 %first.1 = (f32[32,512]{1,0:T(8,128)S(1)}, f32[32,512]{1,0:T(8,128)S(1)}, f32[2,32,512]{2,1,0:T(8,128)S(1)}, f32[8,512]{1,0:T(8,128)S(1)}) custom-call(s32[2]{0:T(128)S(1)} %pad_add_fusion.place, bf16[32,4,256,256]{3,2,1,0:T(8,128)(2,1)S(1)} %get-tuple-element.41.k_mat, s32[69]{0:T(128)S(1)} %get-tuple-element.42.refs_0_.listed, ...), custom_call_target="tpu_custom_call" | custom-call | flops 536870912 | bytes 8388608 | tf_op jit(solution)/shard_map/first/pallas_call | solution.py:513
  45.8 5.4 %collective-permute-start.17 = (f32[2,32,512]{2,1,0:T(8,128)S(1)}, f32[2,32,512]{2,1,0:T(8,128)S(1)}, u32[]{:S(2)}, u32[]{:S(2)}) collective-permute-start(f32[2,32,512]{2,1,0:T(8,128)S(1)} %get-tuple-element.49), channel_id=1, source_target_pairs={{0,1},{1,0},{2,3},{3,2},{4,5},{5,4},{6,7},{7,6},{8,9},{9,8},{10,11... | collective-permute-start | bytes 393224 | tf_op jit(solution)/shard_map/ppermute | solution.py:366
  51.3 1.0 collective-permute-done.17
  52.3 1.0 %collective-permute-start.18 = (f32[72,512]{1,0:T(8,128)S(1)}, f32[72,512]{1,0:T(8,128)S(1)}, u32[]{:S(2)}, u32[]{:S(2)}) collective-permute-start(f32[72,512]{1,0:T(8,128)S(1)} %pad_maximum_fusion.2), channel_id=1, source_target_pairs={{0,2},{1,3},{2,0},{3,1},{4,6},{5,7},{6,4},{7,5},{8,10},{9,11},{10,... | collective-permute-start | bytes 442376 | tf_op jit(solution)/shard_map/ppermute | solution.py:366
  53.3 5.2 %collective-permute-done.18 = f32[72,512]{1,0:T(8,128)S(1)} collective-permute-done((f32[72,512]{1,0:T(8,128)S(1)}, f32[72,512]{1,0:T(8,128)S(1)}, u32[]{:S(2)}, u32[]{:S(2)}) %collective-permute-start.18) | collective-permute-done | bytes 147488 | tf_op jit(solution)/shard_map/ppermute | solution.py:366
  58.6 1.4 %collective-permute-done.19.s1_got = f32[2,40,512]{2,1,0:T(8,128)S(1)} collective-permute-done((f32[2,40,512]{2,1,0:T(8,128)S(1)}, f32[2,40,512]{2,1,0:T(8,128)S(1)}, u32[]{:S(2)}, u32[]{:S(2)}) %collective-permute-start.19) | collective-permute-done | bytes 163872 | tf_op jit(solution)/shard_map/ppermute | solution.py:366
  60.0 1.6 %second.3 = bf16[4,32,512]{2,1,0:T(8,128)(2,1)S(1)} custom-call(s32[2]{0:T(128)S(1)} %pad_add_fusion.place, bf16[32,4,256,256]{3,2,1,0:T(8,128)(2,1)S(1)} %get-tuple-element.41.k_mat, s32[69]{0:T(128)S(1)} %get-tuple-element.43.refs_1_.listed, f32[32,2048]{1,0:T(8,128)S(1)} %copy-done, f32[2,40,512]{2,1,0:T(8,128)S(1)} %pad_maximum_fusion.1.s1_own, ...), custom_call_target="tpu_custom_call" | custom-call | flops 268435456 | bytes 4194304 | tf_op jit(solution)/shard_map/second/pallas_call | solution.py:540
  61.6 1.0 collective-permute-start.20
  62.6 1.4 %second.2 = f32[4,32,512]{2,1,0:T(8,128)S(1)} custom-call(s32[2]{0:T(128)S(1)} %pad_add_fusion.place, bf16[32,4,256,256]{3,2,1,0:T(8,128)(2,1)S(1)} %get-tuple-element.41.k_mat, s32[69]{0:T(128)S(1)} %get-tuple-element.42.refs_0_.listed, f32[32,2048]{1,0:T(8,128)S(1)} %copy-done, f32[2,40,512]{2,1,0:T(8,128)S(1)} %pad_maximum_fusion.1.s1_own, ...), custom_call_target="tpu_custom_call" | custom-call | flops 268435456 | bytes 4194304 | tf_op jit(solution)/shard_map/second/pallas_call | solution.py:540
  64.0 3.2 %collective-permute-done.20 = bf16[4,32,512]{2,1,0:T(8,128)(2,1)S(1)} collective-permute-done((bf16[4,32,512]{2,1,0:T(8,128)(2,1)S(1)}, bf16[4,32,512]{2,1,0:T(8,128)(2,1)S(1)}, u32[]{:S(2)}, u32[]{:S(2)}) %collective-permute-start.20) | collective-permute-done | bytes 131104 | tf_op jit(solution)/shard_map/ppermute | solution.py:366
  67.3 1.3 %collective-permute-start.23 = (bf16[32,512]{1,0:T(8,128)(2,1)S(1)}, bf16[32,512]{1,0:T(8,128)(2,1)S(1)}, u32[]{:S(2)}, u32[]{:S(2)}) collective-permute-start(bf16[32,512]{1,0:T(8,128)(2,1)S(1)} %get-tuple-element.60), channel_id=1, source_target_pairs={{0,24},{4,28},{8,16},{12,20},{16,8},{20,12},{24,0},{28,4},{1,25},{... | collective-permute-start | bytes 98312 | tf_op jit(solution)/shard_map/ppermute | solution.py:366
  68.6 0.7 collective-permute-start.22
  69.3 2.4 %collective-permute-start.21 = (bf16[32,512]{1,0:T(8,128)(2,1)S(1)}, bf16[32,512]{1,0:T(8,128)(2,1)S(1)}, u32[]{:S(2)}, u32[]{:S(2)}) collective-permute-start(bf16[32,512]{1,0:T(8,128)(2,1)S(1)} %get-tuple-element.62), channel_id=1, source_target_pairs={{0,8},{4,12},{8,0},{12,4},{16,24},{20,28},{24,16},{28,20},{1,9},{5... | collective-permute-start | bytes 98312 | tf_op jit(solution)/shard_map/ppermute | solution.py:366
  71.8 1.3 %collective-permute-done.23.refs_3_ = bf16[32,512]{1,0:T(8,128)(2,1)S(1)} collective-permute-done((bf16[32,512]{1,0:T(8,128)(2,1)S(1)}, bf16[32,512]{1,0:T(8,128)(2,1)S(1)}, u32[]{:S(2)}, u32[]{:S(2)}) %collective-permute-start.23) | collective-permute-done | bytes 32800 | tf_op jit(solution)/shard_map/ppermute | solution.py:366
  73.1 0.7 collective-permute-done.22.refs_2_
  74.5 1.2 %collective-permute-done.26 = f32[32,128]{1,0:T(8,128)S(1)} collective-permute-done((f32[32,128]{1,0:T(8,128)S(1)}, f32[32,128]{1,0:T(8,128)S(1)}, u32[]{:S(2)}, u32[]{:S(2)}) %collective-permute-start.26) | collective-permute-done | bytes 16416 | tf_op jit(solution)/shard_map/ppermute | solution.py:366
  76.4 0.7 collective-permute-start.28
  77.0 0.7 collective-permute-start.27
  77.7 1.8 %collective-permute-start.24 = (f32[32,512]{1,0:T(8,128)S(1)}, f32[32,512]{1,0:T(8,128)S(1)}, u32[]{:S(2)}, u32[]{:S(2)}) collective-permute-start(f32[32,512]{1,0:T(8,128)S(1)} %get-tuple-element.54), channel_id=1, source_target_pairs={{0,2},{1,3},{2,0},{3,1},{4,6},{5,7},{6,4},{7,5},{8,10},{9,11},{10,... | collective-permute-start | bytes 196616 | tf_op jit(solution)/shard_map/ppermute | solution.py:366
  79.5 0.7 collective-permute-start.32
  80.2 0.7 collective-permute-start.31
  82.0 13.4 %collective-permute-start.25 = (f32[2,32,512]{2,1,0:T(8,128)S(1)}, f32[2,32,512]{2,1,0:T(8,128)S(1)}, u32[]{:S(2)}, u32[]{:S(2)}) collective-permute-start(f32[2,32,512]{2,1,0:T(8,128)S(1)} %pad_maximum_fusion.3.refs_0_), channel_id=1, source_target_pairs={{0,1},{1,0},{2,3},{3,2},{4,5},{5,4},{6,7},{7,6},{8,9},{9,8},{10,11... | collective-permute-start | bytes 393224 | tf_op jit(solution)/shard_map/ppermute | solution.py:366
  95.5 1.3 %collective-permute-start.33 = (f32[32,128]{1,0:T(8,128)S(1)}, f32[32,128]{1,0:T(8,128)S(1)}, u32[]{:S(2)}, u32[]{:S(2)}) collective-permute-start(f32[32,128]{1,0:T(8,128)S(1)} %add_add_fusion.refs_2_), channel_id=1, source_target_pairs={{1,0},{3,2},{5,4},{7,6},{9,8},{11,10},{13,12},{15,14},{17,16},{19,... | collective-permute-start | bytes 49160 | tf_op jit(solution)/shard_map/ppermute | solution.py:381
  96.8 2.2 %collective-permute-done.33.refs_3_ = f32[32,128]{1,0:T(8,128)S(1)} collective-permute-done((f32[32,128]{1,0:T(8,128)S(1)}, f32[32,128]{1,0:T(8,128)S(1)}, u32[]{:S(2)}, u32[]{:S(2)}) %collective-permute-start.33) | collective-permute-done | bytes 16416 | tf_op jit(solution)/shard_map/ppermute | solution.py:381
  99.0 1.7 %final.1 = (f32[32,2048]{1,0:T(8,128)}, f32[32,2048]{1,0:T(8,128)}) custom-call(s32[2]{0:T(128)S(1)} %pad_add_fusion.place, f32[32,2048]{1,0:T(8,128)S(1)} %copy-done, f32[2,40,512]{2,1,0:T(8,128)S(1)} %pad_maximum_fusion.1.s1_own, f32[2,40,512]{2,1,0:T(8,128)S(1)} %collective-permute-done.19.s1_got, f32[2,32,512]{2,1,0:T(8,128)S(1)} %pad_maximum_fusion.3.refs_0_, ...), custom_call_target="tpu_custom_call" | custom-call | tf_op jit(solution)/shard_map/final/pallas_call | solution.py:582
  (64 shorter events, 5.5 us)
Async XLA Ops:
  0.6 5.8 %collective-permute-start = (s32[8,6]{1,0:T(8,128)}, s32[8,6]{1,0:T(8,128)S(1)}, u32[]{:S(2)}, u32[]{:S(2)}) collective-permute-start(s32[8,6]{1,0:T(8,128)} %param.3), channel_id=1, source_target_pairs={{0,1},{1,0},{2,3},{3,2},{4,5},{5,4},{6,7},{7,6},{8,9},{9,8},{10,11... | collective-permute-start | bytes 584 | tf_op jit(solution)/shard_map/ppermute | solution.py:366
  1.1 5.4 %collective-permute-start.2 = (s32[8,6]{1,0:T(8,128)}, s32[8,6]{1,0:T(8,128)S(1)}, u32[]{:S(2)}, u32[]{:S(2)}) collective-permute-start(s32[8,6]{1,0:T(8,128)} %param.3), channel_id=1, source_target_pairs={{0,3},{1,2},{2,1},{3,0},{4,7},{5,6},{6,5},{7,4},{8,11},{9,10},{10,... | collective-permute-start | bytes 584 | tf_op jit(solution)/shard_map/ppermute | solution.py:366
  3.8 3.8 %collective-permute-start.1 = (s32[8,6]{1,0:T(8,128)}, s32[8,6]{1,0:T(8,128)S(1)}, u32[]{:S(2)}, u32[]{:S(2)}) collective-permute-start(s32[8,6]{1,0:T(8,128)} %param.3), channel_id=1, source_target_pairs={{0,2},{1,3},{2,0},{3,1},{4,6},{5,7},{6,4},{7,5},{8,10},{9,11},{10,... | collective-permute-start | bytes 584 | tf_op jit(solution)/shard_map/ppermute | solution.py:366
  7.9 5.8 %collective-permute-start.5 = (bf16[16,640]{1,0:T(8,128)(2,1)S(1)}, bf16[16,640]{1,0:T(8,128)(2,1)S(1)}, u32[]{:S(2)}, u32[]{:S(2)}) collective-permute-start(bf16[16,640]{1,0:T(8,128)(2,1)S(1)} %pad_maximum_fusion.5), channel_id=1, source_target_pairs={{0,24},{4,28},{8,16},{12,20},{16,8},{20,12},{24,0},{28,4},{1,25},{... | collective-permute-start | bytes 61448 | tf_op jit(solution)/shard_map/ppermute | solution.py:366
  11.6 4.7 %collective-permute-start.4 = (bf16[16,640]{1,0:T(8,128)(2,1)S(1)}, bf16[16,640]{1,0:T(8,128)(2,1)S(1)}, u32[]{:S(2)}, u32[]{:S(2)}) collective-permute-start(bf16[16,640]{1,0:T(8,128)(2,1)S(1)} %pad_maximum_fusion.5), channel_id=1, source_target_pairs={{0,16},{4,20},{8,24},{12,28},{16,0},{20,4},{24,8},{28,12},{1,17},{... | collective-permute-start | bytes 61448 | tf_op jit(solution)/shard_map/ppermute | solution.py:366
  11.6 4.7 %collective-permute-start.3 = (bf16[16,640]{1,0:T(8,128)(2,1)S(1)}, bf16[16,640]{1,0:T(8,128)(2,1)S(1)}, u32[]{:S(2)}, u32[]{:S(2)}) collective-permute-start(bf16[16,640]{1,0:T(8,128)(2,1)S(1)} %pad_maximum_fusion.5), channel_id=1, source_target_pairs={{0,8},{4,12},{8,0},{12,4},{16,24},{20,28},{24,16},{28,20},{1,9},{5... | collective-permute-start | bytes 61448 | tf_op jit(solution)/shard_map/ppermute | solution.py:366
  12.3 10.6 %collective-permute-start.9 = (f32[32,1024]{1,0:T(8,128)S(1)}, f32[32,1024]{1,0:T(8,128)S(1)}, u32[]{:S(2)}, u32[]{:S(2)}) collective-permute-start(f32[32,1024]{1,0:T(8,128)S(1)} %constant_dynamic-slice_fusion), channel_id=1, source_target_pairs={{1,25},{3,27},{5,29},{7,31},{9,17},{11,19},{13,21},{15,23},{17,9},... | collective-permute-start | bytes 393224 | tf_op jit(solution)/shard_map/ppermute | solution.py:376
  13.0 10.0 %collective-permute-start.8 = (f32[32,1024]{1,0:T(8,128)S(1)}, f32[32,1024]{1,0:T(8,128)S(1)}, u32[]{:S(2)}, u32[]{:S(2)}) collective-permute-start(f32[32,1024]{1,0:T(8,128)S(1)} %constant_dynamic-slice_fusion), channel_id=1, source_target_pairs={{1,17},{3,19},{5,21},{7,23},{9,25},{11,27},{13,29},{15,31},{17,1},... | collective-permute-start | bytes 393224 | tf_op jit(solution)/shard_map/ppermute | solution.py:376
  13.7 9.3 %collective-permute-start.7 = (f32[32,1024]{1,0:T(8,128)S(1)}, f32[32,1024]{1,0:T(8,128)S(1)}, u32[]{:S(2)}, u32[]{:S(2)}) collective-permute-start(f32[32,1024]{1,0:T(8,128)S(1)} %constant_dynamic-slice_fusion), channel_id=1, source_target_pairs={{1,9},{3,11},{5,13},{7,15},{9,1},{11,3},{13,5},{15,7},{17,25},{19,... | collective-permute-start | bytes 393224 | tf_op jit(solution)/shard_map/ppermute | solution.py:376
  16.3 6.7 %collective-permute-start.6 = (bf16[4,16,640]{2,1,0:T(8,128)(2,1)S(1)}, bf16[4,16,640]{2,1,0:T(8,128)(2,1)S(1)}, u32[]{:S(2)}, u32[]{:S(2)}) collective-permute-start(bf16[4,16,640]{2,1,0:T(8,128)(2,1)S(1)} %pad_maximum_fusion.4.refs_1_), channel_id=1, source_target_pairs={{0,4},{4,0},{8,12},{12,8},{16,20},{20,16},{24,28},{28,24},{1,5},{5... | collective-permute-start | bytes 245768 | tf_op jit(solution)/shard_map/ppermute | solution.py:366
  23.0 7.2 %collective-permute-start.10 = (f32[4,32,1024]{2,1,0:T(8,128)S(1)}, f32[4,32,1024]{2,1,0:T(8,128)S(1)}, u32[]{:S(2)}, u32[]{:S(2)}) collective-permute-start(f32[4,32,1024]{2,1,0:T(8,128)S(1)} %pad_maximum_fusion.refs_2_), channel_id=1, source_target_pairs={{1,5},{3,7},{5,1},{7,3},{9,13},{11,15},{13,9},{15,11},{17,21},{19,... | collective-permute-start | bytes 1572872 | tf_op jit(solution)/shard_map/ppermute | solution.py:376
  23.7 18.9 %collective-permute-start.11 = (f32[4,32,1024]{2,1,0:T(8,128)S(1)}, f32[4,32,1024]{2,1,0:T(8,128)S(1)}, u32[]{:S(2)}, u32[]{:S(2)}) collective-permute-start(f32[4,32,1024]{2,1,0:T(8,128)S(1)} %pad_maximum_fusion.refs_2_), channel_id=1, source_target_pairs={{1,0},{3,2},{5,4},{7,6},{9,8},{11,10},{13,12},{15,14},{17,16},{19,... | collective-permute-start | bytes 1572872 | tf_op jit(solution)/shard_map/ppermute | solution.py:381
  25.0 35.0 %copy-start = (f32[32,2048]{1,0:T(8,128)S(1)}, f32[32,2048]{1,0:T(8,128)}, u32[]{:S(2)}) copy-start(f32[32,2048]{1,0:T(8,128)} %t_ref.7) | copy-start | bytes 786436
  30.3 12.4 %collective-permute-start.12 = (f32[4,32,1024]{2,1,0:T(8,128)S(1)}, f32[4,32,1024]{2,1,0:T(8,128)S(1)}, u32[]{:S(2)}, u32[]{:S(2)}) collective-permute-start(f32[4,32,1024]{2,1,0:T(8,128)S(1)} %collective-permute-done.10.refs_3_), channel_id=1, source_target_pairs={{1,0},{3,2},{5,4},{7,6},{9,8},{11,10},{13,12},{15,14},{17,16},{19,... | collective-permute-start | bytes 1572872 | tf_op jit(solution)/shard_map/ppermute | solution.py:381
  31.6 5.6 %collective-permute-start.15 = (f32[16,256]{1,0:T(8,128)S(1)}, f32[16,256]{1,0:T(8,128)S(1)}, u32[]{:S(2)}, u32[]{:S(2)}) collective-permute-start(f32[16,256]{1,0:T(8,128)S(1)} %get-tuple-element.47), channel_id=1, source_target_pairs={{0,24},{4,28},{8,16},{12,20},{16,8},{20,12},{24,0},{28,4},{1,25},{... | collective-permute-start | bytes 49160 | tf_op jit(solution)/shard_map/ppermute | solution.py:366
  33.4 4.6 %collective-permute-start.14 = (f32[16,256]{1,0:T(8,128)S(1)}, f32[16,256]{1,0:T(8,128)S(1)}, u32[]{:S(2)}, u32[]{:S(2)}) collective-permute-start(f32[16,256]{1,0:T(8,128)S(1)} %get-tuple-element.47), channel_id=1, source_target_pairs={{0,16},{4,20},{8,24},{12,28},{16,0},{20,4},{24,8},{28,12},{1,17},{... | collective-permute-start | bytes 49160 | tf_op jit(solution)/shard_map/ppermute | solution.py:366
  35.1 3.7 %collective-permute-start.13 = (f32[16,256]{1,0:T(8,128)S(1)}, f32[16,256]{1,0:T(8,128)S(1)}, u32[]{:S(2)}, u32[]{:S(2)}) collective-permute-start(f32[16,256]{1,0:T(8,128)S(1)} %get-tuple-element.47), channel_id=1, source_target_pairs={{0,8},{4,12},{8,0},{12,4},{16,24},{20,28},{24,16},{28,20},{1,9},{5... | collective-permute-start | bytes 49160 | tf_op jit(solution)/shard_map/ppermute | solution.py:366
  38.9 3.8 %collective-permute-start.16 = (f32[16,256]{1,0:T(8,128)S(1)}, f32[16,256]{1,0:T(8,128)S(1)}, u32[]{:S(2)}, u32[]{:S(2)}) collective-permute-start(f32[16,256]{1,0:T(8,128)S(1)} %add_add_fusion.2), channel_id=1, source_target_pairs={{0,4},{4,0},{8,12},{12,8},{16,20},{20,16},{24,28},{28,24},{1,5},{5... | collective-permute-start | bytes 49160 | tf_op jit(solution)/shard_map/ppermute | solution.py:366
  45.8 6.4 %collective-permute-start.17 = (f32[2,32,512]{2,1,0:T(8,128)S(1)}, f32[2,32,512]{2,1,0:T(8,128)S(1)}, u32[]{:S(2)}, u32[]{:S(2)}) collective-permute-start(f32[2,32,512]{2,1,0:T(8,128)S(1)} %get-tuple-element.49), channel_id=1, source_target_pairs={{0,1},{1,0},{2,3},{3,2},{4,5},{5,4},{6,7},{7,6},{8,9},{9,8},{10,11... | collective-permute-start | bytes 393224 | tf_op jit(solution)/shard_map/ppermute | solution.py:366
  52.3 6.2 %collective-permute-start.18 = (f32[72,512]{1,0:T(8,128)S(1)}, f32[72,512]{1,0:T(8,128)S(1)}, u32[]{:S(2)}, u32[]{:S(2)}) collective-permute-start(f32[72,512]{1,0:T(8,128)S(1)} %pad_maximum_fusion.2), channel_id=1, source_target_pairs={{0,2},{1,3},{2,0},{3,1},{4,6},{5,7},{6,4},{7,5},{8,10},{9,11},{10,... | collective-permute-start | bytes 442376 | tf_op jit(solution)/shard_map/ppermute | solution.py:366
  58.5 1.5 %collective-permute-start.19 = (f32[2,40,512]{2,1,0:T(8,128)S(1)}, f32[2,40,512]{2,1,0:T(8,128)S(1)}, u32[]{:S(2)}, u32[]{:S(2)}) collective-permute-start(f32[2,40,512]{2,1,0:T(8,128)S(1)} %pad_maximum_fusion.1.s1_own), channel_id=1, source_target_pairs={{0,1},{1,0},{2,3},{3,2},{4,5},{5,4},{6,7},{7,6},{8,9},{9,8},{10,11... | collective-permute-start | bytes 491528 | tf_op jit(solution)/shard_map/ppermute | solution.py:366
  61.6 5.6 %collective-permute-start.20 = (bf16[4,32,512]{2,1,0:T(8,128)(2,1)S(1)}, bf16[4,32,512]{2,1,0:T(8,128)(2,1)S(1)}, u32[]{:S(2)}, u32[]{:S(2)}) collective-permute-start(bf16[4,32,512]{2,1,0:T(8,128)(2,1)S(1)} %second.3), channel_id=1, source_target_pairs={{0,4},{4,0},{8,12},{12,8},{16,20},{20,16},{24,28},{28,24},{1,5},{5... | collective-permute-start | bytes 393224 | tf_op jit(solution)/shard_map/ppermute | solution.py:366
  67.3 5.8 %collective-permute-start.23 = (bf16[32,512]{1,0:T(8,128)(2,1)S(1)}, bf16[32,512]{1,0:T(8,128)(2,1)S(1)}, u32[]{:S(2)}, u32[]{:S(2)}) collective-permute-start(bf16[32,512]{1,0:T(8,128)(2,1)S(1)} %get-tuple-element.60), channel_id=1, source_target_pairs={{0,24},{4,28},{8,16},{12,20},{16,8},{20,12},{24,0},{28,4},{1,25},{... | collective-permute-start | bytes 98312 | tf_op jit(solution)/shard_map/ppermute | solution.py:366
  68.6 5.2 %collective-permute-start.22 = (bf16[32,512]{1,0:T(8,128)(2,1)S(1)}, bf16[32,512]{1,0:T(8,128)(2,1)S(1)}, u32[]{:S(2)}, u32[]{:S(2)}) collective-permute-start(bf16[32,512]{1,0:T(8,128)(2,1)S(1)} %get-tuple-element.61), channel_id=1, source_target_pairs={{0,16},{4,20},{8,24},{12,28},{16,0},{20,4},{24,8},{28,12},{1,17},{... | collective-permute-start | bytes 98312 | tf_op jit(solution)/shard_map/ppermute | solution.py:366
  69.3 4.5 %collective-permute-start.21 = (bf16[32,512]{1,0:T(8,128)(2,1)S(1)}, bf16[32,512]{1,0:T(8,128)(2,1)S(1)}, u32[]{:S(2)}, u32[]{:S(2)}) collective-permute-start(bf16[32,512]{1,0:T(8,128)(2,1)S(1)} %get-tuple-element.62), channel_id=1, source_target_pairs={{0,8},{4,12},{8,0},{12,4},{16,24},{20,28},{24,16},{28,20},{1,9},{5... | collective-permute-start | bytes 98312 | tf_op jit(solution)/shard_map/ppermute | solution.py:366
  74.4 1.2 %collective-permute-start.26 = (f32[32,128]{1,0:T(8,128)S(1)}, f32[32,128]{1,0:T(8,128)S(1)}, u32[]{:S(2)}, u32[]{:S(2)}) collective-permute-start(f32[32,128]{1,0:T(8,128)S(1)} %get-tuple-element.55), channel_id=1, source_target_pairs={{0,1},{1,0},{2,3},{3,2},{4,5},{5,4},{6,7},{7,6},{8,9},{9,8},{10,11... | collective-permute-start | bytes 49160 | tf_op jit(solution)/shard_map/ppermute | solution.py:366
  75.7 3.8 %collective-permute-start.29 = (f32[32,128]{1,0:T(8,128)S(1)}, f32[32,128]{1,0:T(8,128)S(1)}, u32[]{:S(2)}, u32[]{:S(2)}) collective-permute-start(f32[32,128]{1,0:T(8,128)S(1)} %add.87), channel_id=1, source_target_pairs={{1,25},{3,27},{5,29},{7,31},{9,17},{11,19},{13,21},{15,23},{17,9},... | collective-permute-start | bytes 49160 | tf_op jit(solution)/shard_map/ppermute | solution.py:376
  76.4 3.1 %collective-permute-start.28 = (f32[32,128]{1,0:T(8,128)S(1)}, f32[32,128]{1,0:T(8,128)S(1)}, u32[]{:S(2)}, u32[]{:S(2)}) collective-permute-start(f32[32,128]{1,0:T(8,128)S(1)} %add.87), channel_id=1, source_target_pairs={{1,17},{3,19},{5,21},{7,23},{9,25},{11,27},{13,29},{15,31},{17,1},... | collective-permute-start | bytes 49160 | tf_op jit(solution)/shard_map/ppermute | solution.py:376
  77.0 2.5 %collective-permute-start.27 = (f32[32,128]{1,0:T(8,128)S(1)}, f32[32,128]{1,0:T(8,128)S(1)}, u32[]{:S(2)}, u32[]{:S(2)}) collective-permute-start(f32[32,128]{1,0:T(8,128)S(1)} %add.87), channel_id=1, source_target_pairs={{1,9},{3,11},{5,13},{7,15},{9,1},{11,3},{13,5},{15,7},{17,25},{19,... | collective-permute-start | bytes 49160 | tf_op jit(solution)/shard_map/ppermute | solution.py:376
  77.7 4.3 %collective-permute-start.24 = (f32[32,512]{1,0:T(8,128)S(1)}, f32[32,512]{1,0:T(8,128)S(1)}, u32[]{:S(2)}, u32[]{:S(2)}) collective-permute-start(f32[32,512]{1,0:T(8,128)S(1)} %get-tuple-element.54), channel_id=1, source_target_pairs={{0,2},{1,3},{2,0},{3,1},{4,6},{5,7},{6,4},{7,5},{8,10},{9,11},{10,... | collective-permute-start | bytes 196616 | tf_op jit(solution)/shard_map/ppermute | solution.py:366
  79.5 15.9 %collective-permute-start.32 = (f32[32,128]{1,0:T(8,128)S(1)}, f32[32,128]{1,0:T(8,128)S(1)}, u32[]{:S(2)}, u32[]{:S(2)}) collective-permute-start(f32[32,128]{1,0:T(8,128)S(1)} %add_add_fusion.1), channel_id=1, source_target_pairs={{1,7},{3,5},{5,3},{7,1},{9,15},{11,13},{13,11},{15,9},{17,23},{19,... | collective-permute-start | bytes 49160 | tf_op jit(solution)/shard_map/ppermute | solution.py:376
  80.2 15.3 %collective-permute-start.31 = (f32[32,128]{1,0:T(8,128)S(1)}, f32[32,128]{1,0:T(8,128)S(1)}, u32[]{:S(2)}, u32[]{:S(2)}) collective-permute-start(f32[32,128]{1,0:T(8,128)S(1)} %add_add_fusion.1), channel_id=1, source_target_pairs={{1,3},{3,1},{5,7},{7,5},{9,11},{11,9},{13,15},{15,13},{17,19},{19,... | collective-permute-start | bytes 49160 | tf_op jit(solution)/shard_map/ppermute | solution.py:376
  80.9 14.6 %collective-permute-start.30 = (f32[32,128]{1,0:T(8,128)S(1)}, f32[32,128]{1,0:T(8,128)S(1)}, u32[]{:S(2)}, u32[]{:S(2)}) collective-permute-start(f32[32,128]{1,0:T(8,128)S(1)} %add_add_fusion.1), channel_id=1, source_target_pairs={{1,5},{3,7},{5,1},{7,3},{9,13},{11,15},{13,9},{15,11},{17,21},{19,... | collective-permute-start | bytes 49160 | tf_op jit(solution)/shard_map/ppermute | solution.py:376
  82.0 17.0 %collective-permute-start.25 = (f32[2,32,512]{2,1,0:T(8,128)S(1)}, f32[2,32,512]{2,1,0:T(8,128)S(1)}, u32[]{:S(2)}, u32[]{:S(2)}) collective-permute-start(f32[2,32,512]{2,1,0:T(8,128)S(1)} %pad_maximum_fusion.3.refs_0_), channel_id=1, source_target_pairs={{0,1},{1,0},{2,3},{3,2},{4,5},{5,4},{6,7},{7,6},{8,9},{9,8},{10,11... | collective-permute-start | bytes 393224 | tf_op jit(solution)/shard_map/ppermute | solution.py:366
  95.5 3.5 %collective-permute-start.33 = (f32[32,128]{1,0:T(8,128)S(1)}, f32[32,128]{1,0:T(8,128)S(1)}, u32[]{:S(2)}, u32[]{:S(2)}) collective-permute-start(f32[32,128]{1,0:T(8,128)S(1)} %add_add_fusion.refs_2_), channel_id=1, source_target_pairs={{1,0},{3,2},{5,4},{7,6},{9,8},{11,10},{13,12},{15,14},{17,16},{19,... | collective-permute-start | bytes 49160 | tf_op jit(solution)/shard_map/ppermute | solution.py:381

commit v9 on v7

--- a/solution.py
+++ b/solution.py
@@ -85,13 +85,18 @@
         lhs, first_deg, piece, _ = refs[:4]
         k_mat, listed, deg_ref = refs[4:7]
         refs = refs[7:]
-    mlist, acc, rhs, counts_v, counts, count_sem = refs[:6]
-    kbuf, sems = (None, None) if cfg.resident else refs[6:]
+    mlist, acc, rhs, dist, counts_v, counts, count_sem = refs[:7]
+    kbuf, sems = (None, None) if cfg.resident else refs[7:]
     row, col = place[0], place[1]
     own_rows, block_len, nb = cfg.own_rows, cfg.block_len, cfg.nb
     own_len = own_rows * block_len
     dim, held = piece.shape[1], piece.shape[0]
     scale = 1.0 / (RADIUS * RADIUS)
+
+    def count(n, carry):
+        named = piece[n, :, own_len:own_len + LANES]
+        counts_v[slot_of(cfg, place, n)] = named.astype(F32)[:cfg.count_rows].astype(jnp.int32)
+        return carry
 
     def prepare(n, carry):
         z = slot_of(cfg, place, n)
@@ -99,20 +104,19 @@
             far = piece[n, :, k * block_len:(k + 1) * block_len]
             rhs[z * own_rows + k, :dim, :] = far
             rhs[z * own_rows + k, dim:, :] = augment(far.astype(F32), False).astype(BF16)
-        named = piece[n, :, own_len:own_len + LANES]
-        counts_v[z] = named.astype(F32)[:cfg.count_rows].astype(jnp.int32)
         return carry
 
-    lax.fori_loop(0, held, prepare, 0, unroll=held <= 4)
+    lax.fori_loop(0, held, count, 0, unroll=held <= 4)
     fetch = pltpu.make_async_copy(counts_v, counts, count_sem)
     fetch.start()
+    lax.fori_loop(0, held, prepare, 0, unroll=held <= 4)
+    acc[...] = jnp.zeros_like(acc)
     if part == 0:
         near_copy.wait()
         for i in range(cfg.block_rows):
             near = near_ref[:, i * block_len:(i + 1) * block_len].astype(F32)
             full = jnp.concatenate([near * (-2.0 * scale), augment(near, True)], axis=0)
             lhs[i] = full.T.astype(BF16)
-    acc[...] = jnp.zeros_like(acc)
     fetch.wait()
 
     pos = jnp.int32(0)
@@ -130,7 +134,11 @@
                 at = at + jnp.where(m > 0, 1, 0)
             return at
 
-        pos = lax.fori_loop(0, held, note, pos, unroll=4)
+        if held <= 4:
+            for z in range(held):
+                pos = note(z, pos)
+        else:
+            pos = lax.fori_loop(0, held, note, pos, unroll=4)
     for u in range(GROUP):
         listed[pos + u + 1] = 0
         mlist[pos + u] = 0
@@ -143,6 +151,13 @@
 
     base = part * cfg.part_groups
 
+    def distances(e, slot):
+        code = listed[e + 1]
+        i, j = lax.shift_right_logical(code, CODE_BITS), code & (CODE - 1)
+        dist[slot] = jnp.dot(lhs[i], rhs[j], preferred_element_type=F32)
+
+    distances(0, 0)
+
     def step(g, carry):
         slot, target = (base + g, k_mat) if cfg.resident else (lax.rem(g, RING), kbuf)
         if not cfg.resident:
@@ -152,14 +167,13 @@
                 copy_out(g - RING).wait()
 
         for u in range(GROUP):
-            code = listed[g * GROUP + u + 1]
-            i, j = lax.shift_right_logical(code, CODE_BITS), code & (CODE - 1)
+            distances(g * GROUP + u + 1, (u + 1) % 2)
+            j = listed[g * GROUP + u + 1] & (CODE - 1)
             m = mlist[g * GROUP + u].astype(F32)
-            dist = jnp.dot(lhs[i], rhs[j], preferred_element_type=F32)
             sums = jnp.zeros((8, block_len), F32)
             for s in range(block_len // STRIP):
                 rows = slice(s * STRIP, (s + 1) * STRIP)
-                d = jnp.maximum(dist[rows], TINY)
+                d = jnp.maximum(dist[u % 2, rows, :], TINY)
                 sc = d * lax.rsqrt(d)
                 rem = jnp.maximum(1.0 - sc, 0.0)
                 sq = rem * rem
@@ -433,6 +447,7 @@
                 pltpu.SMEM((list_len,), jnp.int32),
                 pltpu.VMEM((n_part, 8, block_len), F32),
                 pltpu.VMEM((n_part, 2 * dim, block_len), BF16),
+                pltpu.VMEM((2, block_len, block_len), F32),
                 pltpu.VMEM((n_part // own_rows, cfg.count_rows, LANES), jnp.int32),
                 pltpu.SMEM((n_part // own_rows, cfg.count_rows, LANES), jnp.int32),
                 pltpu.SemaphoreType.DMA,

time: 87.7 us -> 87.2 us (level)
  starting transfers between devices: 36.6 us -> 34.8 us
    ppermute x31, starting transfers between devices: 36.6 us -> 34.8 us  [swap(): return lax.ppermute(x, axis, [(i, i ^ d) for i in range(size)])]
  transfers between devices with their start and end apart: 31 -> 31, of which waited for: 17 -> 18; matrix products, arithmetic and copies ran while one was open for 3% -> 3% of each run, Pallas kernels for 14% -> 14%
where the time goes in v9:
time: 87.2 us; the launch traced here: 87 us
  starting transfers between devices  34.8 us (40%)
  waiting for transfers between devices  28.5 us (33%)
  Pallas kernels  19.5 us (22%)
  local copies, waits for them, and re-layouts  2.76 us (3%)
    ppermute x31, starting transfers between devices, swap(): return lax.ppermute(x, axis, [(i, i ^ d) for i in range(size)])  34.8 us
    ppermute x31, waiting for transfers between devices, swap(): return lax.ppermute(x, axis, [(i, i ^ d) for i in range(size)])  28.5 us
    pallas_call x2, Pallas kernels, build(): pl.pallas_call(functools.partial(build_kernel, cfg, part), out_shape=out,...  10.5 us
    pallas_call x1, Pallas kernels, local(): pl.pallas_call(functools.partial(first_kernel, cfg), out_shape=[shape(out...  3.35 us
    pallas_call x2, Pallas kernels, second(): pl.pallas_call(functools.partial(second_kernel, cfg, part), out_shape=sha...  3.26 us
  transfers between devices with their start and end apart: 31, of which 18 were waited for; matrix products, arithmetic and copies ran while one was open for 3% of the time, Pallas kernels for 14%

profile of v9, /device:TPU:0, one launch (start us, length us, event | category | flops | bytes accessed | tf_op | source)
XLA Modules:
  0.0 87.0 jit_solution(3747035101977919095)
XLA Ops:
  0.6 0.5 collective-permute-start
  1.1 2.6 %collective-permute-start.2 = (s32[8,6]{1,0:T(8,128)}, s32[8,6]{1,0:T(8,128)S(1)}, u32[]{:S(2)}, u32[]{:S(2)}) collective-permute-start(s32[8,6]{1,0:T(8,128)} %param.3), channel_id=1, source_target_pairs={{0,3},{1,2},{2,1},{3,0},{4,7},{5,6},{6,5},{7,4},{8,11},{9,10},{10,... | collective-permute-start | bytes 584 | tf_op jit(solution)/shard_map/ppermute | solution.py:362
  3.8 0.8 copy.6
  4.7 0.7 constant_dynamic-slice_fusion.1
  5.5 0.8 constant_dynamic-slice_fusion
  6.6 1.0 %collective-permute-done.1 = s32[8,6]{1,0:T(8,128)S(1)} collective-permute-done((s32[8,6]{1,0:T(8,128)}, s32[8,6]{1,0:T(8,128)S(1)}, u32[]{:S(2)}, u32[]{:S(2)}) %collective-permute-start.1) | collective-permute-done | bytes 224 | tf_op jit(solution)/shard_map/ppermute | solution.py:362
  7.9 3.7 %collective-permute-start.5 = (bf16[16,640]{1,0:T(8,128)(2,1)S(1)}, bf16[16,640]{1,0:T(8,128)(2,1)S(1)}, u32[]{:S(2)}, u32[]{:S(2)}) collective-permute-start(bf16[16,640]{1,0:T(8,128)(2,1)S(1)} %pad_maximum_fusion.5), channel_id=1, source_target_pairs={{0,24},{4,28},{8,16},{12,20},{16,8},{20,12},{24,0},{28,4},{1,25},{... | collective-permute-start | bytes 61448 | tf_op jit(solution)/shard_map/ppermute | solution.py:362
  11.6 0.8 collective-permute-start.3
  12.3 3.6 %collective-permute-start.9 = (f32[32,512]{1,0:T(8,128)S(1)}, f32[32,512]{1,0:T(8,128)S(1)}, u32[]{:S(2)}, u32[]{:S(2)}) collective-permute-start(f32[32,512]{1,0:T(8,128)S(1)} %constant_dynamic-slice_fusion), channel_id=1, source_target_pairs={{0,24},{4,28},{8,16},{12,20},{16,8},{20,12},{24,0},{28,4},{1,25},{... | collective-permute-start | bytes 196616 | tf_op jit(solution)/shard_map/ppermute | solution.py:362
  15.9 0.8 collective-permute-start.7
  16.8 1.6 %collective-permute-start.6 = (bf16[4,16,640]{2,1,0:T(8,128)(2,1)S(1)}, bf16[4,16,640]{2,1,0:T(8,128)(2,1)S(1)}, u32[]{:S(2)}, u32[]{:S(2)}) collective-permute-start(bf16[4,16,640]{2,1,0:T(8,128)(2,1)S(1)} %pad_maximum_fusion.4.refs_1_), channel_id=1, source_target_pairs={{0,4},{4,0},{8,12},{12,8},{16,20},{20,16},{24,28},{28,24},{1,5},{5... | collective-permute-start | bytes 245768 | tf_op jit(solution)/shard_map/ppermute | solution.py:362
  18.4 5.5 %build.2 = (bf16[32,4,256,256]{3,2,1,0:T(8,128)(2,1)S(1)}, s32[69]{0:T(128)S(1)}, f32[8,256]{1,0:T(8,128)S(1)}, bf16[8,256,32]{2,1,0:T(8,128)(2,1)S(1)}) custom-call(s32[2]{0:T(128)S(1)} %pad_add_fusion.place, s32[8,64]{1,0:T(8,128)S(1)} %add_add_fusion.2.direct, bf16[16,2048]{1,0:T(8,128)(2,1)} %refs_0_.1, bf16[4,16,640]{2,1,0:T(8,128)(2,1)S(1)} %pad_maximum_fusion.4.refs_1_), custom_call_target="tpu_custom_call" | custom-call | flops 268435456 | bytes 8388608 | tf_op jit(solution)/shard_map/build/pallas_call | solution.py:438
  24.1 5.0 %build.3 = (bf16[32,4,256,256]{3,2,1,0:T(8,128)(2,1)S(1)}, s32[69]{0:T(128)S(1)}, f32[16,256]{1,0:T(8,128)S(1)}) custom-call(s32[2]{0:T(128)S(1)} %pad_add_fusion.place, s32[8,64]{1,0:T(8,128)S(1)} %add_add_fusion.2.direct, bf16[8,256,32]{2,1,0:T(8,128)(2,1)S(1)} %get-tuple-element.30.refs_0_, ...), custom_call_target="tpu_custom_call", output_to_operand_aliasing={{0}: (5, {})} | custom-call | flops 268435456 | bytes 8388608 | tf_op jit(solution)/shard_map/build/pallas_call | solution.py:438
  29.1 1.3 %collective-permute-done.10.refs_3_ = f32[4,32,512]{2,1,0:T(8,128)S(1)} collective-permute-done((f32[4,32,512]{2,1,0:T(8,128)S(1)}, f32[4,32,512]{2,1,0:T(8,128)S(1)}, u32[]{:S(2)}, u32[]{:S(2)}) %collective-permute-start.10) | collective-permute-done | bytes 262176 | tf_op jit(solution)/shard_map/ppermute | solution.py:362
  30.4 3.3 %collective-permute-start.13 = (f32[16,256]{1,0:T(8,128)S(1)}, f32[16,256]{1,0:T(8,128)S(1)}, u32[]{:S(2)}, u32[]{:S(2)}) collective-permute-start(f32[16,256]{1,0:T(8,128)S(1)} %get-tuple-element.47), channel_id=1, source_target_pairs={{0,24},{4,28},{8,16},{12,20},{16,8},{20,12},{24,0},{28,4},{1,25},{... | collective-permute-start | bytes 49160 | tf_op jit(solution)/shard_map/ppermute | solution.py:362
  33.7 1.1 %collective-permute-start.11 = (f32[16,256]{1,0:T(8,128)S(1)}, f32[16,256]{1,0:T(8,128)S(1)}, u32[]{:S(2)}, u32[]{:S(2)}) collective-permute-start(f32[16,256]{1,0:T(8,128)S(1)} %get-tuple-element.47), channel_id=1, source_target_pairs={{0,8},{4,12},{8,0},{12,4},{16,24},{20,28},{24,16},{28,20},{1,9},{5... | collective-permute-start | bytes 49160 | tf_op jit(solution)/shard_map/ppermute | solution.py:362
  34.8 1.1 %collective-permute-done.13 = f32[16,256]{1,0:T(8,128)S(1)} collective-permute-done((f32[16,256]{1,0:T(8,128)S(1)}, f32[16,256]{1,0:T(8,128)S(1)}, u32[]{:S(2)}, u32[]{:S(2)}) %collective-permute-start.13) | collective-permute-done | bytes 16416 | tf_op jit(solution)/shard_map/ppermute | solution.py:362
  35.9 2.4 %collective-permute-done.12 = f32[16,256]{1,0:T(8,128)S(1)} collective-permute-done((f32[16,256]{1,0:T(8,128)S(1)}, f32[16,256]{1,0:T(8,128)S(1)}, u32[]{:S(2)}, u32[]{:S(2)}) %collective-permute-start.12) | collective-permute-done | bytes 16416 | tf_op jit(solution)/shard_map/ppermute | solution.py:362
  38.3 0.9 %collective-permute-start.14 = (f32[16,256]{1,0:T(8,128)S(1)}, f32[16,256]{1,0:T(8,128)S(1)}, u32[]{:S(2)}, u32[]{:S(2)}) collective-permute-start(f32[16,256]{1,0:T(8,128)S(1)} %add_add_fusion.1), channel_id=1, source_target_pairs={{0,4},{4,0},{8,12},{12,8},{16,20},{20,16},{24,28},{28,24},{1,5},{5... | collective-permute-start | bytes 49160 | tf_op jit(solution)/shard_map/ppermute | solution.py:362
  39.3 2.9 %collective-permute-done.14 = f32[16,256]{1,0:T(8,128)S(1)} collective-permute-done((f32[16,256]{1,0:T(8,128)S(1)}, f32[16,256]{1,0:T(8,128)S(1)}, u32[]{:S(2)}, u32[]{:S(2)}) %collective-permute-start.14) | collective-permute-done | bytes 16416 | tf_op jit(solution)/shard_map/ppermute | solution.py:362
  42.2 3.3 %first.1 = (f32[32,512]{1,0:T(8,128)S(1)}, f32[32,512]{1,0:T(8,128)S(1)}, f32[2,32,512]{2,1,0:T(8,128)S(1)}, f32[8,512]{1,0:T(8,128)S(1)}) custom-call(s32[2]{0:T(128)S(1)} %pad_add_fusion.place, bf16[32,4,256,256]{3,2,1,0:T(8,128)(2,1)S(1)} %get-tuple-element.41.k_mat, s32[69]{0:T(128)S(1)} %get-tuple-element.42.refs_0_.listed, ...), custom_call_target="tpu_custom_call" | custom-call | flops 536870912 | bytes 8388608 | tf_op jit(solution)/shard_map/first/pallas_call | solution.py:493
  45.6 1.3 %collective-permute-done.15 = f32[2,32,512]{2,1,0:T(8,128)S(1)} collective-permute-done((f32[2,32,512]{2,1,0:T(8,128)S(1)}, f32[2,32,512]{2,1,0:T(8,128)S(1)}, u32[]{:S(2)}, u32[]{:S(2)}) %collective-permute-start.15) | collective-permute-done | bytes 131104 | tf_op jit(solution)/shard_map/ppermute | solution.py:362
  47.0 1.7 %collective-permute-start.16 = (f32[72,512]{1,0:T(8,128)S(1)}, f32[72,512]{1,0:T(8,128)S(1)}, u32[]{:S(2)}, u32[]{:S(2)}) collective-permute-start(f32[72,512]{1,0:T(8,128)S(1)} %pad_maximum_fusion.2), channel_id=1, source_target_pairs={{0,2},{1,3},{2,0},{3,1},{4,6},{5,7},{6,4},{7,5},{8,10},{9,11},{10,... | collective-permute-start | bytes 442376 | tf_op jit(solution)/shard_map/ppermute | solution.py:362
  48.6 4.3 %collective-permute-done.16 = f32[72,512]{1,0:T(8,128)S(1)} collective-permute-done((f32[72,512]{1,0:T(8,128)S(1)}, f32[72,512]{1,0:T(8,128)S(1)}, u32[]{:S(2)}, u32[]{:S(2)}) %collective-permute-start.16) | collective-permute-done | bytes 147488 | tf_op jit(solution)/shard_map/ppermute | solution.py:362
  53.1 1.4 %collective-permute-done.17.s1_got = f32[2,40,512]{2,1,0:T(8,128)S(1)} collective-permute-done((f32[2,40,512]{2,1,0:T(8,128)S(1)}, f32[2,40,512]{2,1,0:T(8,128)S(1)}, u32[]{:S(2)}, u32[]{:S(2)}) %collective-permute-start.17) | collective-permute-done | bytes 163872 | tf_op jit(solution)/shard_map/ppermute | solution.py:362
  54.5 1.6 %second.3 = bf16[4,32,512]{2,1,0:T(8,128)(2,1)S(1)} custom-call(s32[2]{0:T(128)S(1)} %pad_add_fusion.place, bf16[32,4,256,256]{3,2,1,0:T(8,128)(2,1)S(1)} %get-tuple-element.41.k_mat, s32[69]{0:T(128)S(1)} %get-tuple-element.43.refs_1_.listed, f32[32,2048]{1,0:T(8,128)S(1)} %copy-done, f32[2,40,512]{2,1,0:T(8,128)S(1)} %pad_maximum_fusion.1.s1_own, ...), custom_call_target="tpu_custom_call" | custom-call | flops 268435456 | bytes 4194304 | tf_op jit(solution)/shard_map/second/pallas_call | solution.py:520
  56.1 1.1 %collective-permute-start.18 = (bf16[4,32,512]{2,1,0:T(8,128)(2,1)S(1)}, bf16[4,32,512]{2,1,0:T(8,128)(2,1)S(1)}, u32[]{:S(2)}, u32[]{:S(2)}) collective-permute-start(bf16[4,32,512]{2,1,0:T(8,128)(2,1)S(1)} %second.3), channel_id=1, source_target_pairs={{0,4},{4,0},{8,12},{12,8},{16,20},{20,16},{24,28},{28,24},{1,5},{5... | collective-permute-start | bytes 393224 | tf_op jit(solution)/shard_map/ppermute | solution.py:362
  57.3 1.6 %second.2 = f32[4,32,512]{2,1,0:T(8,128)S(1)} custom-call(s32[2]{0:T(128)S(1)} %pad_add_fusion.place, bf16[32,4,256,256]{3,2,1,0:T(8,128)(2,1)S(1)} %get-tuple-element.41.k_mat, s32[69]{0:T(128)S(1)} %get-tuple-element.42.refs_0_.listed, f32[32,2048]{1,0:T(8,128)S(1)} %copy-done, f32[2,40,512]{2,1,0:T(8,128)S(1)} %pad_maximum_fusion.1.s1_own, ...), custom_call_target="tpu_custom_call" | custom-call | flops 268435456 | bytes 4194304 | tf_op jit(solution)/shard_map/second/pallas_call | solution.py:520
  58.9 2.8 %collective-permute-done.18 = bf16[4,32,512]{2,1,0:T(8,128)(2,1)S(1)} collective-permute-done((bf16[4,32,512]{2,1,0:T(8,128)(2,1)S(1)}, bf16[4,32,512]{2,1,0:T(8,128)(2,1)S(1)}, u32[]{:S(2)}, u32[]{:S(2)}) %collective-permute-start.18) | collective-permute-done | bytes 131104 | tf_op jit(solution)/shard_map/ppermute | solution.py:362
  61.8 1.3 %collective-permute-start.21 = (bf16[32,512]{1,0:T(8,128)(2,1)S(1)}, bf16[32,512]{1,0:T(8,128)(2,1)S(1)}, u32[]{:S(2)}, u32[]{:S(2)}) collective-permute-start(bf16[32,512]{1,0:T(8,128)(2,1)S(1)} %get-tuple-element.60), channel_id=1, source_target_pairs={{0,24},{4,28},{8,16},{12,20},{16,8},{20,12},{24,0},{28,4},{1,25},{... | collective-permute-start | bytes 98312 | tf_op jit(solution)/shard_map/ppermute | solution.py:362
  63.0 1.1 %collective-permute-start.20 = (bf16[32,512]{1,0:T(8,128)(2,1)S(1)}, bf16[32,512]{1,0:T(8,128)(2,1)S(1)}, u32[]{:S(2)}, u32[]{:S(2)}) collective-permute-start(bf16[32,512]{1,0:T(8,128)(2,1)S(1)} %get-tuple-element.61), channel_id=1, source_target_pairs={{0,16},{4,20},{8,24},{12,28},{16,0},{20,4},{24,8},{28,12},{1,17},{... | collective-permute-start | bytes 98312 | tf_op jit(solution)/shard_map/ppermute | solution.py:362
  64.2 2.1 %collective-permute-start.19 = (bf16[32,512]{1,0:T(8,128)(2,1)S(1)}, bf16[32,512]{1,0:T(8,128)(2,1)S(1)}, u32[]{:S(2)}, u32[]{:S(2)}) collective-permute-start(bf16[32,512]{1,0:T(8,128)(2,1)S(1)} %get-tuple-element.62), channel_id=1, source_target_pairs={{0,8},{4,12},{8,0},{12,4},{16,24},{20,28},{24,16},{28,20},{1,9},{5... | collective-permute-start | bytes 98312 | tf_op jit(solution)/shard_map/ppermute | solution.py:362
  66.2 1.6 %collective-permute-done.21.refs_3_ = bf16[32,512]{1,0:T(8,128)(2,1)S(1)} collective-permute-done((bf16[32,512]{1,0:T(8,128)(2,1)S(1)}, bf16[32,512]{1,0:T(8,128)(2,1)S(1)}, u32[]{:S(2)}, u32[]{:S(2)}) %collective-permute-start.21) | collective-permute-done | bytes 32800 | tf_op jit(solution)/shard_map/ppermute | solution.py:362
  68.0 0.3 collective-permute-done.19.refs_1_
  68.4 0.7 products.1
  69.0 1.6 %collective-permute-start.22 = (f32[32,512]{1,0:T(8,128)S(1)}, f32[32,512]{1,0:T(8,128)S(1)}, u32[]{:S(2)}, u32[]{:S(2)}) collective-permute-start(f32[32,512]{1,0:T(8,128)S(1)} %get-tuple-element.54), channel_id=1, source_target_pairs={{0,2},{1,3},{2,0},{3,1},{4,6},{5,7},{6,4},{7,5},{8,10},{9,11},{10,... | collective-permute-start | bytes 196616 | tf_op jit(solution)/shard_map/ppermute | solution.py:362
  70.6 2.2 %collective-permute-start.26 = (f32[32,128]{1,0:T(8,128)S(1)}, f32[32,128]{1,0:T(8,128)S(1)}, u32[]{:S(2)}, u32[]{:S(2)}) collective-permute-start(f32[32,128]{1,0:T(8,128)S(1)} %get-tuple-element.55), channel_id=1, source_target_pairs={{0,24},{4,28},{8,16},{12,20},{16,8},{20,12},{24,0},{28,4},{1,25},{... | collective-permute-start | bytes 49160 | tf_op jit(solution)/shard_map/ppermute | solution.py:362
  72.8 1.1 %collective-permute-start.25 = (f32[32,128]{1,0:T(8,128)S(1)}, f32[32,128]{1,0:T(8,128)S(1)}, u32[]{:S(2)}, u32[]{:S(2)}) collective-permute-start(f32[32,128]{1,0:T(8,128)S(1)} %get-tuple-element.55), channel_id=1, source_target_pairs={{0,16},{4,20},{8,24},{12,28},{16,0},{20,4},{24,8},{28,12},{1,17},{... | collective-permute-start | bytes 49160 | tf_op jit(solution)/shard_map/ppermute | solution.py:362
  73.9 1.0 %collective-permute-start.24 = (f32[32,128]{1,0:T(8,128)S(1)}, f32[32,128]{1,0:T(8,128)S(1)}, u32[]{:S(2)}, u32[]{:S(2)}) collective-permute-start(f32[32,128]{1,0:T(8,128)S(1)} %get-tuple-element.55), channel_id=1, source_target_pairs={{0,8},{4,12},{8,0},{12,4},{16,24},{20,28},{24,16},{28,20},{1,9},{5... | collective-permute-start | bytes 49160 | tf_op jit(solution)/shard_map/ppermute | solution.py:362
  75.1 1.1 %collective-permute-done.26 = f32[32,128]{1,0:T(8,128)S(1)} collective-permute-done((f32[32,128]{1,0:T(8,128)S(1)}, f32[32,128]{1,0:T(8,128)S(1)}, u32[]{:S(2)}, u32[]{:S(2)}) %collective-permute-start.26) | collective-permute-done | bytes 16416 | tf_op jit(solution)/shard_map/ppermute | solution.py:362
  76.1 1.3 %collective-permute-done.25 = f32[32,128]{1,0:T(8,128)S(1)} collective-permute-done((f32[32,128]{1,0:T(8,128)S(1)}, f32[32,128]{1,0:T(8,128)S(1)}, u32[]{:S(2)}, u32[]{:S(2)}) %collective-permute-start.25) | collective-permute-done | bytes 16416 | tf_op jit(solution)/shard_map/ppermute | solution.py:362
  77.7 0.5 collective-permute-start.27
  78.2 3.3 %collective-permute-done.27 = f32[32,128]{1,0:T(8,128)S(1)} collective-permute-done((f32[32,128]{1,0:T(8,128)S(1)}, f32[32,128]{1,0:T(8,128)S(1)}, u32[]{:S(2)}, u32[]{:S(2)}) %collective-permute-start.27) | collective-permute-done | bytes 16416 | tf_op jit(solution)/shard_map/ppermute | solution.py:362
  81.5 0.7 collective-permute-start.29
  82.2 1.1 %collective-permute-start.28 = (f32[32,128]{1,0:T(8,128)S(1)}, f32[32,128]{1,0:T(8,128)S(1)}, u32[]{:S(2)}, u32[]{:S(2)}) collective-permute-start(f32[32,128]{1,0:T(8,128)S(1)} %add.78.refs_2_), channel_id=1, source_target_pairs={{0,1},{1,0},{2,3},{3,2},{4,5},{5,4},{6,7},{7,6},{8,9},{9,8},{10,11... | collective-permute-start | bytes 49160 | tf_op jit(solution)/shard_map/ppermute | solution.py:362
  83.3 1.3 %collective-permute-done.30.refs_5_ = f32[32,128]{1,0:T(8,128)S(1)} collective-permute-done((f32[32,128]{1,0:T(8,128)S(1)}, f32[32,128]{1,0:T(8,128)S(1)}, u32[]{:S(2)}, u32[]{:S(2)}) %collective-permute-start.30) | collective-permute-done | bytes 16416 | tf_op jit(solution)/shard_map/ppermute | solution.py:362
  84.7 0.6 collective-permute-done.29.refs_4_
  85.3 1.7 %final.1 = (f32[32,2048]{1,0:T(8,128)}, f32[32,2048]{1,0:T(8,128)}) custom-call(s32[2]{0:T(128)S(1)} %pad_add_fusion.place, f32[32,2048]{1,0:T(8,128)S(1)} %copy-done, f32[2,40,512]{2,1,0:T(8,128)S(1)} %pad_maximum_fusion.1.s1_own, f32[2,40,512]{2,1,0:T(8,128)S(1)} %collective-permute-done.17.s1_got, f32[2,32,512]{2,1,0:T(8,128)S(1)} %pad_maximum_fusion.3.refs_0_, ...), custom_call_target="tpu_custom_call" | custom-call | tf_op jit(solution)/shard_map/final/pallas_call | solution.py:559
  (57 shorter events, 1.8 us)
Async XLA Ops:
  0.6 5.7 %collective-permute-start = (s32[8,6]{1,0:T(8,128)}, s32[8,6]{1,0:T(8,128)S(1)}, u32[]{:S(2)}, u32[]{:S(2)}) collective-permute-start(s32[8,6]{1,0:T(8,128)} %param.3), channel_id=1, source_target_pairs={{0,1},{1,0},{2,3},{3,2},{4,5},{5,4},{6,7},{7,6},{8,9},{9,8},{10,11... | collective-permute-start | bytes 584 | tf_op jit(solution)/shard_map/ppermute | solution.py:362
  1.1 5.3 %collective-permute-start.2 = (s32[8,6]{1,0:T(8,128)}, s32[8,6]{1,0:T(8,128)S(1)}, u32[]{:S(2)}, u32[]{:S(2)}) collective-permute-start(s32[8,6]{1,0:T(8,128)} %param.3), channel_id=1, source_target_pairs={{0,3},{1,2},{2,1},{3,0},{4,7},{5,6},{6,5},{7,4},{8,11},{9,10},{10,... | collective-permute-start | bytes 584 | tf_op jit(solution)/shard_map/ppermute | solution.py:362
  3.8 3.8 %collective-permute-start.1 = (s32[8,6]{1,0:T(8,128)}, s32[8,6]{1,0:T(8,128)S(1)}, u32[]{:S(2)}, u32[]{:S(2)}) collective-permute-start(s32[8,6]{1,0:T(8,128)} %param.3), channel_id=1, source_target_pairs={{0,2},{1,3},{2,0},{3,1},{4,6},{5,7},{6,4},{7,5},{8,10},{9,11},{10,... | collective-permute-start | bytes 584 | tf_op jit(solution)/shard_map/ppermute | solution.py:362
  7.9 8.1 %collective-permute-start.5 = (bf16[16,640]{1,0:T(8,128)(2,1)S(1)}, bf16[16,640]{1,0:T(8,128)(2,1)S(1)}, u32[]{:S(2)}, u32[]{:S(2)}) collective-permute-start(bf16[16,640]{1,0:T(8,128)(2,1)S(1)} %pad_maximum_fusion.5), channel_id=1, source_target_pairs={{0,24},{4,28},{8,16},{12,20},{16,8},{20,12},{24,0},{28,4},{1,25},{... | collective-permute-start | bytes 61448 | tf_op jit(solution)/shard_map/ppermute | solution.py:362
  11.6 5.2 %collective-permute-start.4 = (bf16[16,640]{1,0:T(8,128)(2,1)S(1)}, bf16[16,640]{1,0:T(8,128)(2,1)S(1)}, u32[]{:S(2)}, u32[]{:S(2)}) collective-permute-start(bf16[16,640]{1,0:T(8,128)(2,1)S(1)} %pad_maximum_fusion.5), channel_id=1, source_target_pairs={{0,16},{4,20},{8,24},{12,28},{16,0},{20,4},{24,8},{28,12},{1,17},{... | collective-permute-start | bytes 61448 | tf_op jit(solution)/shard_map/ppermute | solution.py:362
  11.6 5.2 %collective-permute-start.3 = (bf16[16,640]{1,0:T(8,128)(2,1)S(1)}, bf16[16,640]{1,0:T(8,128)(2,1)S(1)}, u32[]{:S(2)}, u32[]{:S(2)}) collective-permute-start(bf16[16,640]{1,0:T(8,128)(2,1)S(1)} %pad_maximum_fusion.5), channel_id=1, source_target_pairs={{0,8},{4,12},{8,0},{12,4},{16,24},{20,28},{24,16},{28,20},{1,9},{5... | collective-permute-start | bytes 61448 | tf_op jit(solution)/shard_map/ppermute | solution.py:362
  12.3 11.6 %collective-permute-start.9 = (f32[32,512]{1,0:T(8,128)S(1)}, f32[32,512]{1,0:T(8,128)S(1)}, u32[]{:S(2)}, u32[]{:S(2)}) collective-permute-start(f32[32,512]{1,0:T(8,128)S(1)} %constant_dynamic-slice_fusion), channel_id=1, source_target_pairs={{0,24},{4,28},{8,16},{12,20},{16,8},{20,12},{24,0},{28,4},{1,25},{... | collective-permute-start | bytes 196616 | tf_op jit(solution)/shard_map/ppermute | solution.py:362
  15.9 8.0 %collective-permute-start.8 = (f32[32,512]{1,0:T(8,128)S(1)}, f32[32,512]{1,0:T(8,128)S(1)}, u32[]{:S(2)}, u32[]{:S(2)}) collective-permute-start(f32[32,512]{1,0:T(8,128)S(1)} %constant_dynamic-slice_fusion), channel_id=1, source_target_pairs={{0,16},{4,20},{8,24},{12,28},{16,0},{20,4},{24,8},{28,12},{1,17},{... | collective-permute-start | bytes 196616 | tf_op jit(solution)/shard_map/ppermute | solution.py:362
  15.9 8.0 %collective-permute-start.7 = (f32[32,512]{1,0:T(8,128)S(1)}, f32[32,512]{1,0:T(8,128)S(1)}, u32[]{:S(2)}, u32[]{:S(2)}) collective-permute-start(f32[32,512]{1,0:T(8,128)S(1)} %constant_dynamic-slice_fusion), channel_id=1, source_target_pairs={{0,8},{4,12},{8,0},{12,4},{16,24},{20,28},{24,16},{28,20},{1,9},{5... | collective-permute-start | bytes 196616 | tf_op jit(solution)/shard_map/ppermute | solution.py:362
  16.8 7.2 %collective-permute-start.6 = (bf16[4,16,640]{2,1,0:T(8,128)(2,1)S(1)}, bf16[4,16,640]{2,1,0:T(8,128)(2,1)S(1)}, u32[]{:S(2)}, u32[]{:S(2)}) collective-permute-start(bf16[4,16,640]{2,1,0:T(8,128)(2,1)S(1)} %pad_maximum_fusion.4.refs_1_), channel_id=1, source_target_pairs={{0,4},{4,0},{8,12},{12,8},{16,20},{20,16},{24,28},{28,24},{1,5},{5... | collective-permute-start | bytes 245768 | tf_op jit(solution)/shard_map/ppermute | solution.py:362
  24.0 6.4 %collective-permute-start.10 = (f32[4,32,512]{2,1,0:T(8,128)S(1)}, f32[4,32,512]{2,1,0:T(8,128)S(1)}, u32[]{:S(2)}, u32[]{:S(2)}) collective-permute-start(f32[4,32,512]{2,1,0:T(8,128)S(1)} %pad_maximum_fusion.refs_2_), channel_id=1, source_target_pairs={{0,4},{4,0},{8,12},{12,8},{16,20},{20,16},{24,28},{28,24},{1,5},{5... | collective-permute-start | bytes 786440 | tf_op jit(solution)/shard_map/ppermute | solution.py:362
  24.1 30.4 %copy-start = (f32[32,2048]{1,0:T(8,128)S(1)}, f32[32,2048]{1,0:T(8,128)}, u32[]{:S(2)}) copy-start(f32[32,2048]{1,0:T(8,128)} %t_ref.7) | copy-start | bytes 786436
  30.4 5.5 %collective-permute-start.13 = (f32[16,256]{1,0:T(8,128)S(1)}, f32[16,256]{1,0:T(8,128)S(1)}, u32[]{:S(2)}, u32[]{:S(2)}) collective-permute-start(f32[16,256]{1,0:T(8,128)S(1)} %get-tuple-element.47), channel_id=1, source_target_pairs={{0,24},{4,28},{8,16},{12,20},{16,8},{20,12},{24,0},{28,4},{1,25},{... | collective-permute-start | bytes 49160 | tf_op jit(solution)/shard_map/ppermute | solution.py:362
  33.7 4.6 %collective-permute-start.12 = (f32[16,256]{1,0:T(8,128)S(1)}, f32[16,256]{1,0:T(8,128)S(1)}, u32[]{:S(2)}, u32[]{:S(2)}) collective-permute-start(f32[16,256]{1,0:T(8,128)S(1)} %get-tuple-element.47), channel_id=1, source_target_pairs={{0,16},{4,20},{8,24},{12,28},{16,0},{20,4},{24,8},{28,12},{1,17},{... | collective-permute-start | bytes 49160 | tf_op jit(solution)/shard_map/ppermute | solution.py:362
  33.7 4.6 %collective-permute-start.11 = (f32[16,256]{1,0:T(8,128)S(1)}, f32[16,256]{1,0:T(8,128)S(1)}, u32[]{:S(2)}, u32[]{:S(2)}) collective-permute-start(f32[16,256]{1,0:T(8,128)S(1)} %get-tuple-element.47), channel_id=1, source_target_pairs={{0,8},{4,12},{8,0},{12,4},{16,24},{20,28},{24,16},{28,20},{1,9},{5... | collective-permute-start | bytes 49160 | tf_op jit(solution)/shard_map/ppermute | solution.py:362
  38.3 3.8 %collective-permute-start.14 = (f32[16,256]{1,0:T(8,128)S(1)}, f32[16,256]{1,0:T(8,128)S(1)}, u32[]{:S(2)}, u32[]{:S(2)}) collective-permute-start(f32[16,256]{1,0:T(8,128)S(1)} %add_add_fusion.1), channel_id=1, source_target_pairs={{0,4},{4,0},{8,12},{12,8},{16,20},{20,16},{24,28},{28,24},{1,5},{5... | collective-permute-start | bytes 49160 | tf_op jit(solution)/shard_map/ppermute | solution.py:362
  45.5 1.4 %collective-permute-start.15 = (f32[2,32,512]{2,1,0:T(8,128)S(1)}, f32[2,32,512]{2,1,0:T(8,128)S(1)}, u32[]{:S(2)}, u32[]{:S(2)}) collective-permute-start(f32[2,32,512]{2,1,0:T(8,128)S(1)} %get-tuple-element.49), channel_id=1, source_target_pairs={{0,1},{1,0},{2,3},{3,2},{4,5},{5,4},{6,7},{7,6},{8,9},{9,8},{10,11... | collective-permute-start | bytes 393224 | tf_op jit(solution)/shard_map/ppermute | solution.py:362
  47.0 6.0 %collective-permute-start.16 = (f32[72,512]{1,0:T(8,128)S(1)}, f32[72,512]{1,0:T(8,128)S(1)}, u32[]{:S(2)}, u32[]{:S(2)}) collective-permute-start(f32[72,512]{1,0:T(8,128)S(1)} %pad_maximum_fusion.2), channel_id=1, source_target_pairs={{0,2},{1,3},{2,0},{3,1},{4,6},{5,7},{6,4},{7,5},{8,10},{9,11},{10,... | collective-permute-start | bytes 442376 | tf_op jit(solution)/shard_map/ppermute | solution.py:362
  53.0 1.5 %collective-permute-start.17 = (f32[2,40,512]{2,1,0:T(8,128)S(1)}, f32[2,40,512]{2,1,0:T(8,128)S(1)}, u32[]{:S(2)}, u32[]{:S(2)}) collective-permute-start(f32[2,40,512]{2,1,0:T(8,128)S(1)} %pad_maximum_fusion.1.s1_own), channel_id=1, source_target_pairs={{0,1},{1,0},{2,3},{3,2},{4,5},{5,4},{6,7},{7,6},{8,9},{9,8},{10,11... | collective-permute-start | bytes 491528 | tf_op jit(solution)/shard_map/ppermute | solution.py:362
  56.1 5.6 %collective-permute-start.18 = (bf16[4,32,512]{2,1,0:T(8,128)(2,1)S(1)}, bf16[4,32,512]{2,1,0:T(8,128)(2,1)S(1)}, u32[]{:S(2)}, u32[]{:S(2)}) collective-permute-start(bf16[4,32,512]{2,1,0:T(8,128)(2,1)S(1)} %second.3), channel_id=1, source_target_pairs={{0,4},{4,0},{8,12},{12,8},{16,20},{20,16},{24,28},{28,24},{1,5},{5... | collective-permute-start | bytes 393224 | tf_op jit(solution)/shard_map/ppermute | solution.py:362
  61.8 6.0 %collective-permute-start.21 = (bf16[32,512]{1,0:T(8,128)(2,1)S(1)}, bf16[32,512]{1,0:T(8,128)(2,1)S(1)}, u32[]{:S(2)}, u32[]{:S(2)}) collective-permute-start(bf16[32,512]{1,0:T(8,128)(2,1)S(1)} %get-tuple-element.60), channel_id=1, source_target_pairs={{0,24},{4,28},{8,16},{12,20},{16,8},{20,12},{24,0},{28,4},{1,25},{... | collective-permute-start | bytes 98312 | tf_op jit(solution)/shard_map/ppermute | solution.py:362
  63.0 5.0 %collective-permute-start.20 = (bf16[32,512]{1,0:T(8,128)(2,1)S(1)}, bf16[32,512]{1,0:T(8,128)(2,1)S(1)}, u32[]{:S(2)}, u32[]{:S(2)}) collective-permute-start(bf16[32,512]{1,0:T(8,128)(2,1)S(1)} %get-tuple-element.61), channel_id=1, source_target_pairs={{0,16},{4,20},{8,24},{12,28},{16,0},{20,4},{24,8},{28,12},{1,17},{... | collective-permute-start | bytes 98312 | tf_op jit(solution)/shard_map/ppermute | solution.py:362
  64.2 4.2 %collective-permute-start.19 = (bf16[32,512]{1,0:T(8,128)(2,1)S(1)}, bf16[32,512]{1,0:T(8,128)(2,1)S(1)}, u32[]{:S(2)}, u32[]{:S(2)}) collective-permute-start(bf16[32,512]{1,0:T(8,128)(2,1)S(1)} %get-tuple-element.62), channel_id=1, source_target_pairs={{0,8},{4,12},{8,0},{12,4},{16,24},{20,28},{24,16},{28,20},{1,9},{5... | collective-permute-start | bytes 98312 | tf_op jit(solution)/shard_map/ppermute | solution.py:362
  69.0 6.0 %collective-permute-start.22 = (f32[32,512]{1,0:T(8,128)S(1)}, f32[32,512]{1,0:T(8,128)S(1)}, u32[]{:S(2)}, u32[]{:S(2)}) collective-permute-start(f32[32,512]{1,0:T(8,128)S(1)} %get-tuple-element.54), channel_id=1, source_target_pairs={{0,2},{1,3},{2,0},{3,1},{4,6},{5,7},{6,4},{7,5},{8,10},{9,11},{10,... | collective-permute-start | bytes 196616 | tf_op jit(solution)/shard_map/ppermute | solution.py:362
  70.6 5.5 %collective-permute-start.26 = (f32[32,128]{1,0:T(8,128)S(1)}, f32[32,128]{1,0:T(8,128)S(1)}, u32[]{:S(2)}, u32[]{:S(2)}) collective-permute-start(f32[32,128]{1,0:T(8,128)S(1)} %get-tuple-element.55), channel_id=1, source_target_pairs={{0,24},{4,28},{8,16},{12,20},{16,8},{20,12},{24,0},{28,4},{1,25},{... | collective-permute-start | bytes 49160 | tf_op jit(solution)/shard_map/ppermute | solution.py:362
  72.8 4.6 %collective-permute-start.25 = (f32[32,128]{1,0:T(8,128)S(1)}, f32[32,128]{1,0:T(8,128)S(1)}, u32[]{:S(2)}, u32[]{:S(2)}) collective-permute-start(f32[32,128]{1,0:T(8,128)S(1)} %get-tuple-element.55), channel_id=1, source_target_pairs={{0,16},{4,20},{8,24},{12,28},{16,0},{20,4},{24,8},{28,12},{1,17},{... | collective-permute-start | bytes 49160 | tf_op jit(solution)/shard_map/ppermute | solution.py:362
  73.9 3.7 %collective-permute-start.24 = (f32[32,128]{1,0:T(8,128)S(1)}, f32[32,128]{1,0:T(8,128)S(1)}, u32[]{:S(2)}, u32[]{:S(2)}) collective-permute-start(f32[32,128]{1,0:T(8,128)S(1)} %get-tuple-element.55), channel_id=1, source_target_pairs={{0,8},{4,12},{8,0},{12,4},{16,24},{20,28},{24,16},{28,20},{1,9},{5... | collective-permute-start | bytes 49160 | tf_op jit(solution)/shard_map/ppermute | solution.py:362
  75.0 10.3 %collective-permute-start.23 = (f32[2,32,512]{2,1,0:T(8,128)S(1)}, f32[2,32,512]{2,1,0:T(8,128)S(1)}, u32[]{:S(2)}, u32[]{:S(2)}) collective-permute-start(f32[2,32,512]{2,1,0:T(8,128)S(1)} %pad_maximum_fusion.3.refs_0_), channel_id=1, source_target_pairs={{0,1},{1,0},{2,3},{3,2},{4,5},{5,4},{6,7},{7,6},{8,9},{9,8},{10,11... | collective-permute-start | bytes 393224 | tf_op jit(solution)/shard_map/ppermute | solution.py:362
  77.7 3.8 %collective-permute-start.27 = (f32[32,128]{1,0:T(8,128)S(1)}, f32[32,128]{1,0:T(8,128)S(1)}, u32[]{:S(2)}, u32[]{:S(2)}) collective-permute-start(f32[32,128]{1,0:T(8,128)S(1)} %add_add_fusion), channel_id=1, source_target_pairs={{0,4},{4,0},{8,12},{12,8},{16,20},{20,16},{24,28},{28,24},{1,5},{5... | collective-permute-start | bytes 49160 | tf_op jit(solution)/shard_map/ppermute | solution.py:362
  81.5 3.2 %collective-permute-start.30 = (f32[32,128]{1,0:T(8,128)S(1)}, f32[32,128]{1,0:T(8,128)S(1)}, u32[]{:S(2)}, u32[]{:S(2)}) collective-permute-start(f32[32,128]{1,0:T(8,128)S(1)} %add.78.refs_2_), channel_id=1, source_target_pairs={{0,3},{1,2},{2,1},{3,0},{4,7},{5,6},{6,5},{7,4},{8,11},{9,10},{10,... | collective-permute-start | bytes 49160 | tf_op jit(solution)/shard_map/ppermute | solution.py:362
  81.5 3.8 %collective-permute-start.29 = (f32[32,128]{1,0:T(8,128)S(1)}, f32[32,128]{1,0:T(8,128)S(1)}, u32[]{:S(2)}, u32[]{:S(2)}) collective-permute-start(f32[32,128]{1,0:T(8,128)S(1)} %add.78.refs_2_), channel_id=1, source_target_pairs={{0,2},{1,3},{2,0},{3,1},{4,6},{5,7},{6,4},{7,5},{8,10},{9,11},{10,... | collective-permute-start | bytes 49160 | tf_op jit(solution)/shard_map/ppermute | solution.py:362
  82.2 3.1 %collective-permute-start.28 = (f32[32,128]{1,0:T(8,128)S(1)}, f32[32,128]{1,0:T(8,128)S(1)}, u32[]{:S(2)}, u32[]{:S(2)}) collective-permute-start(f32[32,128]{1,0:T(8,128)S(1)} %add.78.refs_2_), channel_id=1, source_target_pairs={{0,1},{1,0},{2,3},{3,2},{4,5},{5,4},{6,7},{7,6},{8,9},{9,8},{10,11... | collective-permute-start | bytes 49160 | tf_op jit(solution)/shard_map/ppermute | solution.py:362

commit v10 on v9

--- a/solution.py
+++ b/solution.py
@@ -308,21 +308,56 @@
     lax.fori_loop(0, held, hand_out, 0, unroll=held <= 4)
 
 
-def product_kernel(place, t_ref, s1_own, *refs):
-    zs, grown_ref, dot_ref = refs[:-2], refs[-2], refs[-1]
+N_DOTS = 5
+
+
+def meet_kernel(cfg, place, z_same, z_other, t_same, inv_ref, s1_own, *refs):
+    gs, (own_z, own_dots, *outs) = refs[:4], refs[4:]
+    own_rows, block_len = cfg.own_rows, cfg.block_len
+    outputs, own_len = own_z.shape
+    tz = jnp.zeros((outputs, 1), F32)
+    gz = jnp.zeros((outputs, 1), F32)
+    for n in range(4):
+        z = z_same[n] + z_other[n].astype(F32)
+        if n == 0:
+            own_z[...] = z
+        else:
+            outs[n - 1][:, :own_len] = z.astype(BF16)
+        gz += jnp.sum(gs[n][...].astype(F32) * z, axis=1, keepdims=True)
+        at = row_of(cfg, place, 0, slot_of(cfg, place, n)) * own_rows
+        for k in range(own_rows):
+            cols = slice(k * block_len, (k + 1) * block_len)
+            scaled = t_same[n, :, cols] * inv_ref[pl.ds(at + k, 1), :]
+            tz += jnp.sum(scaled * z[:, cols], axis=1, keepdims=True)
+    t, s1 = t_same[0], s1_own[0, :outputs, :]
+    tt = jnp.sum(t * t, axis=1, keepdims=True)
+    ts1 = jnp.sum(t * s1, axis=1, keepdims=True)
+    s1s1 = jnp.sum(s1 * s1, axis=1, keepdims=True)
+    dots = (tt, ts1, s1s1, tz + SHIFT * ts1, gz + SHIFT * (tz + s1s1))
+    lane = lax.broadcasted_iota(jnp.int32, (outputs, LANES), 1)
+    tile = jnp.zeros(lane.shape, F32)
+    for n, v in enumerate(dots):
+        for part in range(3):
+            head = v.astype(BF16).astype(F32)
+            tile = jnp.where(lane == part * N_DOTS + n, head, tile)
+            v = v - head
+    own_dots[...] = tile.astype(BF16)
+    for out in outs:
+        out[:, own_len:] = tile.astype(BF16)
+
+
+def product_kernel(own_z, own_dots, s1_own, *refs):
+    got, grown_ref, dot_ref = refs[:3], refs[3], refs[4]
     outputs, own_len = grown_ref.shape
-    z = zs[0][...].astype(F32)
-    for ref in zs[1:]:
-        z = z + ref[...].astype(F32)
-    grown = z * s1_own[0, outputs:outputs + 1, :]
-    grown_ref[...] = grown
-    s1 = s1_own[0, :outputs, :]
-    s2 = grown + SHIFT * s1
-    t = t_ref[:, pl.ds(pl.multiple_of(place[1] * own_len, LANES), own_len)]
-    lane = lax.broadcasted_iota(jnp.int32, (outputs, LANES), 1)
-    out = jnp.zeros(lane.shape, F32)
-    for n, (a, b) in enumerate(((t, t), (t, s1), (s1, s1), (t, s2), (s1, s2))):
-        out = jnp.where(lane == n, jnp.sum(a * b, axis=1, keepdims=True), out)
+    z = own_z[...]
+    for ref in got:
+        z = z + ref[:, :own_len].astype(F32)
+    grown_ref[...] = z * s1_own[0, outputs:outputs + 1, :]
+    tiles = [own_dots[...]] + [ref[:, own_len:] for ref in got]
+    total = pair_sum([tile.astype(F32) for tile in tiles])
+    out = total
+    for part in range(1, 3):
+        out = out + pltpu.roll(total, LANES - part * N_DOTS, 1)
     dot_ref[...] = out
 
 
@@ -533,26 +568,40 @@
         )(place, k_mat, k_lists[part], held_t, s1_own, s1_got)
 
     if direct_rows:
-        z2_other = swap(second(1, BF16), "rows", 1)
+        g = ((s1_own[0, :outputs] - SHIFT * own_t) * tail[:1]).astype(BF16)
+        z2_other, g = lax.optimization_barrier((second(1, BF16), g))
+        z2_other = swap(z2_other, "rows", 1)
+        gs = along_z(g)
         z2_same = second(0, F32)
-        z2_same, z2_other = lax.optimization_barrier((z2_same, z2_other))
-        z2 = z2_same + z2_other.astype(F32)
-        z2 = [z2[0]] + [swap(z2[n].astype(BF16), "rows", 2 * n) for n in range(1, n_rows // 2)]
+        z2_same, z2_other, *gs = lax.optimization_barrier((z2_same, z2_other, *gs))
+        row_piece = shape(outputs, own_len + LANES, dtype=BF16)
+        own_z, own_dots, *sends = pl.pallas_call(
+            functools.partial(meet_kernel, cfg),
+            out_shape=[shape(outputs, own_len), shape(outputs, LANES, dtype=BF16)] + [row_piece] * 3,
+            in_specs=[SMEM] + [VMEM] * 9,
+            out_specs=[VMEM] * 5,
+            compiler_params=limit,
+            name="meet",
+        )(place, z2_same, z2_other, t_pieces[0], inv, s1_own, *gs)
+        grown, dots = pl.pallas_call(
+            product_kernel,
+            out_shape=(shape(outputs, own_len), shape(outputs, LANES)),
+            in_specs=[VMEM] * 6,
+            out_specs=(VMEM, VMEM),
+            compiler_params=limit,
+            name="products",
+        )(own_z, own_dots, s1_own, *[swap(x, "rows", 2 * n + 2) for n, x in enumerate(sends)])
+        dots = pair_sum(across_x(dots))
     else:
-        z2 = [lax.psum_scatter(second(0, F32), "rows", scatter_dimension=0)]
-    grown, dots = pl.pallas_call(
-        product_kernel,
-        out_shape=(shape(outputs, own_len), shape(outputs, LANES)),
-        in_specs=[SMEM] + [VMEM] * (2 + len(z2)),
-        out_specs=(VMEM, VMEM),
-        compiler_params=limit,
-        name="products",
-    )(place, held_t, s1_own, *z2)
-    if direct_rows:
-        dots = pair_sum(across_x(pair_sum(along_z(dots))))
-    else:
-        dots = lax.psum(dots, "rows")
+        z2 = lax.psum_scatter(second(0, F32), "rows", scatter_dimension=0)
+        grown = z2 * tail[:1]
+        own_s1 = s1_own[0, :outputs]
+        own_t, s2 = own(targets), grown + SHIFT * own_s1
+        dots = [(own_t, own_t), (own_t, own_s1), (own_s1, own_s1), (own_t, s2), (own_s1, s2)]
+        dots = jnp.stack([jnp.sum(x * y, axis=1) for x, y in dots], axis=1)
+        dots = lax.psum(jnp.pad(dots, ((0, 0), (0, LANES - N_DOTS))), "rows")
     grown = jnp.stack([grown, swap(grown, "cols", 2)])
+    grown, dots = lax.optimization_barrier((grown, dots))
     ends = (s1_own, s1_got, grown, swap(grown, "cols", 1), *direct_cols(dots))
     ends = [pltpu.with_memory_space_constraint(x, pltpu.VMEM) for x in ends]
 

time: 87.2 us -> 85.2 us (0.977)
  waiting for transfers between devices: 28.5 us -> 25.6 us
  starting transfers between devices: 34.8 us -> 37.6 us
  Pallas kernels: 19.5 us -> 17.6 us
    ppermute x31, waiting for transfers between devices: 28.5 us -> 25.6 us  [swap(): return lax.ppermute(x, axis, [(i, i ^ d) for i in range(size)])]
    ppermute x31, starting transfers between devices: 34.8 us -> 37.6 us  [swap(): return lax.ppermute(x, axis, [(i, i ^ d) for i in range(size)])]
    pallas_call x2, Pallas kernels: 10.5 us -> 9.46 us  [build(): pl.pallas_call(functools.partial(build_kernel, cfg, part), out_shape=out,...]
  transfers between devices with their start and end apart: 31 -> 31, of which waited for: 18 -> 16; matrix products, arithmetic and copies ran while one was open for 3% -> 3% of each run, Pallas kernels for 14% -> 13%
where the time goes in v10:
time: 85.2 us; the launch traced here: 85 us
  starting transfers between devices  37.6 us (44%)
  waiting for transfers between devices  25.6 us (30%)
  Pallas kernels  17.6 us (21%)
  local copies, waits for them, and re-layouts  2.74 us (3%)
    ppermute x31, starting transfers between devices, swap(): return lax.ppermute(x, axis, [(i, i ^ d) for i in range(size)])  37.6 us
    ppermute x31, waiting for transfers between devices, swap(): return lax.ppermute(x, axis, [(i, i ^ d) for i in range(size)])  25.6 us
    pallas_call x2, Pallas kernels, build(): pl.pallas_call(functools.partial(build_kernel, cfg, part), out_shape=out,...  9.46 us
    pallas_call x2, Pallas kernels, second(): pl.pallas_call(functools.partial(second_kernel, cfg, part), out_shape=sha...  2.85 us
    pallas_call x1, Pallas kernels, local(): pl.pallas_call(functools.partial(first_kernel, cfg), out_shape=[shape(out...  2.81 us
  transfers between devices with their start and end apart: 31, of which 16 were waited for; matrix products, arithmetic and copies ran while one was open for 3% of the time, Pallas kernels for 13%

profile of v10, /device:TPU:0, one launch (start us, length us, event | category | flops | bytes accessed | tf_op | source)
XLA Modules:
  0.0 85.0 jit_solution(2849826953220105723)
XLA Ops:
  0.6 0.5 collective-permute-start
  1.1 2.6 %collective-permute-start.2 = (s32[8,6]{1,0:T(8,128)}, s32[8,6]{1,0:T(8,128)S(1)}, u32[]{:S(2)}, u32[]{:S(2)}) collective-permute-start(s32[8,6]{1,0:T(8,128)} %param.3), channel_id=1, source_target_pairs={{0,3},{1,2},{2,1},{3,0},{4,7},{5,6},{6,5},{7,4},{8,11},{9,10},{10,... | collective-permute-start | bytes 584 | tf_op jit(solution)/shard_map/ppermute | solution.py:397
  3.8 0.8 copy.6
  4.7 0.7 constant_dynamic-slice_fusion.1
  5.5 0.8 constant_dynamic-slice_fusion
  6.6 1.0 %collective-permute-done.1 = s32[8,6]{1,0:T(8,128)S(1)} collective-permute-done((s32[8,6]{1,0:T(8,128)}, s32[8,6]{1,0:T(8,128)S(1)}, u32[]{:S(2)}, u32[]{:S(2)}) %collective-permute-start.1) | collective-permute-done | bytes 224 | tf_op jit(solution)/shard_map/ppermute | solution.py:397
  7.9 3.7 %collective-permute-start.5 = (bf16[16,640]{1,0:T(8,128)(2,1)S(1)}, bf16[16,640]{1,0:T(8,128)(2,1)S(1)}, u32[]{:S(2)}, u32[]{:S(2)}) collective-permute-start(bf16[16,640]{1,0:T(8,128)(2,1)S(1)} %pad_maximum_fusion.5), channel_id=1, source_target_pairs={{0,24},{4,28},{8,16},{12,20},{16,8},{20,12},{24,0},{28,4},{1,25},{... | collective-permute-start | bytes 61448 | tf_op jit(solution)/shard_map/ppermute | solution.py:397
  11.6 0.8 collective-permute-start.3
  12.3 3.6 %collective-permute-start.9 = (f32[32,512]{1,0:T(8,128)S(1)}, f32[32,512]{1,0:T(8,128)S(1)}, u32[]{:S(2)}, u32[]{:S(2)}) collective-permute-start(f32[32,512]{1,0:T(8,128)S(1)} %constant_dynamic-slice_fusion), channel_id=1, source_target_pairs={{0,24},{4,28},{8,16},{12,20},{16,8},{20,12},{24,0},{28,4},{1,25},{... | collective-permute-start | bytes 196616 | tf_op jit(solution)/shard_map/ppermute | solution.py:397
  15.9 0.8 collective-permute-start.7
  16.8 1.6 %collective-permute-start.6 = (bf16[4,16,640]{2,1,0:T(8,128)(2,1)S(1)}, bf16[4,16,640]{2,1,0:T(8,128)(2,1)S(1)}, u32[]{:S(2)}, u32[]{:S(2)}) collective-permute-start(bf16[4,16,640]{2,1,0:T(8,128)(2,1)S(1)} %pad_maximum_fusion.4.refs_1_), channel_id=1, source_target_pairs={{0,4},{4,0},{8,12},{12,8},{16,20},{20,16},{24,28},{28,24},{1,5},{5... | collective-permute-start | bytes 245768 | tf_op jit(solution)/shard_map/ppermute | solution.py:397
  18.4 5.0 %build.2 = (bf16[32,4,256,256]{3,2,1,0:T(8,128)(2,1)S(1)}, s32[69]{0:T(128)S(1)}, f32[8,256]{1,0:T(8,128)S(1)}, bf16[8,256,32]{2,1,0:T(8,128)(2,1)S(1)}) custom-call(s32[2]{0:T(128)S(1)} %pad_add_fusion.place, s32[8,64]{1,0:T(8,128)S(1)} %add_add_fusion.1.direct, bf16[16,2048]{1,0:T(8,128)(2,1)} %refs_0_.1, bf16[4,16,640]{2,1,0:T(8,128)(2,1)S(1)} %pad_maximum_fusion.4.refs_1_), custom_call_target="tpu_custom_call" | custom-call | flops 268435456 | bytes 8388608 | tf_op jit(solution)/shard_map/build/pallas_call | solution.py:473
  23.4 1.1 %collective-permute-start.10 = (f32[4,32,512]{2,1,0:T(8,128)S(1)}, f32[4,32,512]{2,1,0:T(8,128)S(1)}, u32[]{:S(2)}, u32[]{:S(2)}) collective-permute-start(f32[4,32,512]{2,1,0:T(8,128)S(1)} %pad_maximum_fusion.refs_2_.t_same), channel_id=1, source_target_pairs={{0,4},{4,0},{8,12},{12,8},{16,20},{20,16},{24,28},{28,24},{1,5},{5... | collective-permute-start | bytes 786440 | tf_op jit(solution)/shard_map/ppermute | solution.py:397
  24.6 4.5 %build.3 = (bf16[32,4,256,256]{3,2,1,0:T(8,128)(2,1)S(1)}, s32[69]{0:T(128)S(1)}, f32[16,256]{1,0:T(8,128)S(1)}) custom-call(s32[2]{0:T(128)S(1)} %pad_add_fusion.place, s32[8,64]{1,0:T(8,128)S(1)} %add_add_fusion.1.direct, bf16[8,256,32]{2,1,0:T(8,128)(2,1)S(1)} %get-tuple-element.43.refs_0_, ...), custom_call_target="tpu_custom_call", output_to_operand_aliasing={{0}: (5, {})} | custom-call | flops 268435456 | bytes 8388608 | tf_op jit(solution)/shard_map/build/pallas_call | solution.py:473
  29.1 0.8 collective-permute-done.10.refs_3_
  29.9 4.1 %collective-permute-start.13 = (f32[16,256]{1,0:T(8,128)S(1)}, f32[16,256]{1,0:T(8,128)S(1)}, u32[]{:S(2)}, u32[]{:S(2)}) collective-permute-start(f32[16,256]{1,0:T(8,128)S(1)} %get-tuple-element.60), channel_id=1, source_target_pairs={{0,24},{4,28},{8,16},{12,20},{16,8},{20,12},{24,0},{28,4},{1,25},{... | collective-permute-start | bytes 49160 | tf_op jit(solution)/shard_map/ppermute | solution.py:397
  34.0 0.6 collective-permute-start.11
  34.6 1.1 %collective-permute-done.13 = f32[16,256]{1,0:T(8,128)S(1)} collective-permute-done((f32[16,256]{1,0:T(8,128)S(1)}, f32[16,256]{1,0:T(8,128)S(1)}, u32[]{:S(2)}, u32[]{:S(2)}) %collective-permute-start.13) | collective-permute-done | bytes 16416 | tf_op jit(solution)/shard_map/ppermute | solution.py:397
  35.7 2.9 %collective-permute-done.12 = f32[16,256]{1,0:T(8,128)S(1)} collective-permute-done((f32[16,256]{1,0:T(8,128)S(1)}, f32[16,256]{1,0:T(8,128)S(1)}, u32[]{:S(2)}, u32[]{:S(2)}) %collective-permute-start.12) | collective-permute-done | bytes 16416 | tf_op jit(solution)/shard_map/ppermute | solution.py:397
  38.7 0.8 collective-permute-start.14
  39.5 3.0 %collective-permute-done.14 = f32[16,256]{1,0:T(8,128)S(1)} collective-permute-done((f32[16,256]{1,0:T(8,128)S(1)}, f32[16,256]{1,0:T(8,128)S(1)}, u32[]{:S(2)}, u32[]{:S(2)}) %collective-permute-start.14) | collective-permute-done | bytes 16416 | tf_op jit(solution)/shard_map/ppermute | solution.py:397
  42.5 2.8 %first.1 = (f32[32,512]{1,0:T(8,128)S(1)}, f32[32,512]{1,0:T(8,128)S(1)}, f32[2,32,512]{2,1,0:T(8,128)S(1)}, f32[8,512]{1,0:T(8,128)S(1)}) custom-call(s32[2]{0:T(128)S(1)} %pad_add_fusion.place, bf16[32,4,256,256]{3,2,1,0:T(8,128)(2,1)S(1)} %get-tuple-element.54.k_mat, s32[69]{0:T(128)S(1)} %get-tuple-element.55.refs_0_.listed, ...), custom_call_target="tpu_custom_call" | custom-call | flops 536870912 | bytes 8388608 | tf_op jit(solution)/shard_map/first/pallas_call | solution.py:528
  45.4 1.3 %collective-permute-done.15 = f32[2,32,512]{2,1,0:T(8,128)S(1)} collective-permute-done((f32[2,32,512]{2,1,0:T(8,128)S(1)}, f32[2,32,512]{2,1,0:T(8,128)S(1)}, u32[]{:S(2)}, u32[]{:S(2)}) %collective-permute-start.15) | collective-permute-done | bytes 131104 | tf_op jit(solution)/shard_map/ppermute | solution.py:397
  46.8 1.9 %collective-permute-start.16 = (f32[72,512]{1,0:T(8,128)S(1)}, f32[72,512]{1,0:T(8,128)S(1)}, u32[]{:S(2)}, u32[]{:S(2)}) collective-permute-start(f32[72,512]{1,0:T(8,128)S(1)} %pad_maximum_fusion.2), channel_id=1, source_target_pairs={{0,2},{1,3},{2,0},{3,1},{4,6},{5,7},{6,4},{7,5},{8,10},{9,11},{10,... | collective-permute-start | bytes 442376 | tf_op jit(solution)/shard_map/ppermute | solution.py:397
  48.6 4.2 %collective-permute-done.16 = f32[72,512]{1,0:T(8,128)S(1)} collective-permute-done((f32[72,512]{1,0:T(8,128)S(1)}, f32[72,512]{1,0:T(8,128)S(1)}, u32[]{:S(2)}, u32[]{:S(2)}) %collective-permute-start.16) | collective-permute-done | bytes 147488 | tf_op jit(solution)/shard_map/ppermute | solution.py:397
  53.0 1.3 %collective-permute-done.17.s1_got = f32[2,40,512]{2,1,0:T(8,128)S(1)} collective-permute-done((f32[2,40,512]{2,1,0:T(8,128)S(1)}, f32[2,40,512]{2,1,0:T(8,128)S(1)}, u32[]{:S(2)}, u32[]{:S(2)}) %collective-permute-start.17) | collective-permute-done | bytes 163872 | tf_op jit(solution)/shard_map/ppermute | solution.py:397
  54.3 1.4 %second.3 = bf16[4,32,512]{2,1,0:T(8,128)(2,1)S(1)} custom-call(s32[2]{0:T(128)S(1)} %pad_add_fusion.place, bf16[32,4,256,256]{3,2,1,0:T(8,128)(2,1)S(1)} %get-tuple-element.54.k_mat, s32[69]{0:T(128)S(1)} %get-tuple-element.56.refs_1_.listed, f32[32,2048]{1,0:T(8,128)S(1)} %copy-done, f32[2,40,512]{2,1,0:T(8,128)S(1)} %pad_maximum_fusion.1.s1_own, ...), custom_call_target="tpu_custom_call" | custom-call | flops 268435456 | bytes 4194304 | tf_op jit(solution)/shard_map/second/pallas_call | solution.py:555
  55.7 1.6 %collective-permute-start.18 = (bf16[4,32,512]{2,1,0:T(8,128)(2,1)S(1)}, bf16[4,32,512]{2,1,0:T(8,128)(2,1)S(1)}, u32[]{:S(2)}, u32[]{:S(2)}) collective-permute-start(bf16[4,32,512]{2,1,0:T(8,128)(2,1)S(1)} %second.3), channel_id=1, source_target_pairs={{0,4},{4,0},{8,12},{12,8},{16,20},{20,16},{24,28},{28,24},{1,5},{5... | collective-permute-start | bytes 393224 | tf_op jit(solution)/shard_map/ppermute | solution.py:397
  57.3 1.4 %collective-permute-start.21 = (bf16[32,512]{1,0:T(8,128)(2,1)S(1)}, bf16[32,512]{1,0:T(8,128)(2,1)S(1)}, u32[]{:S(2)}, u32[]{:S(2)}) collective-permute-start(bf16[32,512]{1,0:T(8,128)(2,1)S(1)} %fusion.2.refs_0_), channel_id=1, source_target_pairs={{0,24},{4,28},{8,16},{12,20},{16,8},{20,12},{24,0},{28,4},{1,25},{... | collective-permute-start | bytes 98312 | tf_op jit(solution)/shard_map/ppermute | solution.py:397
  58.7 0.6 collective-permute-start.20
  59.3 2.4 %collective-permute-start.19 = (bf16[32,512]{1,0:T(8,128)(2,1)S(1)}, bf16[32,512]{1,0:T(8,128)(2,1)S(1)}, u32[]{:S(2)}, u32[]{:S(2)}) collective-permute-start(bf16[32,512]{1,0:T(8,128)(2,1)S(1)} %fusion.2.refs_0_), channel_id=1, source_target_pairs={{0,8},{4,12},{8,0},{12,4},{16,24},{20,28},{24,16},{28,20},{1,9},{5... | collective-permute-start | bytes 98312 | tf_op jit(solution)/shard_map/ppermute | solution.py:397
  61.7 1.4 %second.2.z_same = f32[4,32,512]{2,1,0:T(8,128)S(1)} custom-call(s32[2]{0:T(128)S(1)} %pad_add_fusion.place, bf16[32,4,256,256]{3,2,1,0:T(8,128)(2,1)S(1)} %get-tuple-element.54.k_mat, s32[69]{0:T(128)S(1)} %get-tuple-element.55.refs_0_.listed, f32[32,2048]{1,0:T(8,128)S(1)} %copy-done, f32[2,40,512]{2,1,0:T(8,128)S(1)} %pad_maximum_fusion.1.s1_own, ...), custom_call_target="tpu_custom_call" | custom-call | flops 268435456 | bytes 4194304 | tf_op jit(solution)/shard_map/second/pallas_call | solution.py:555
  63.4 0.3 collective-permute-done.20.refs_2_
  63.7 0.3 collective-permute-done.19.refs_1_
  64.0 0.7 meet.1
  64.7 1.7 %collective-permute-start.22 = (bf16[32,640]{1,0:T(8,128)(2,1)S(1)}, bf16[32,640]{1,0:T(8,128)(2,1)S(1)}, u32[]{:S(2)}, u32[]{:S(2)}) collective-permute-start(bf16[32,640]{1,0:T(8,128)(2,1)S(1)} %get-tuple-element.75), channel_id=1, source_target_pairs={{0,8},{4,12},{8,0},{12,4},{16,24},{20,28},{24,16},{28,20},{1,9},{5... | collective-permute-start | bytes 122888 | tf_op jit(solution)/shard_map/ppermute | solution.py:397
  66.4 1.2 %collective-permute-start.23 = (bf16[32,640]{1,0:T(8,128)(2,1)S(1)}, bf16[32,640]{1,0:T(8,128)(2,1)S(1)}, u32[]{:S(2)}, u32[]{:S(2)}) collective-permute-start(bf16[32,640]{1,0:T(8,128)(2,1)S(1)} %get-tuple-element.76), channel_id=1, source_target_pairs={{0,16},{4,20},{8,24},{12,28},{16,0},{20,4},{24,8},{28,12},{1,17},{... | collective-permute-start | bytes 122888 | tf_op jit(solution)/shard_map/ppermute | solution.py:397
  67.7 1.5 %collective-permute-start.24 = (bf16[32,640]{1,0:T(8,128)(2,1)S(1)}, bf16[32,640]{1,0:T(8,128)(2,1)S(1)}, u32[]{:S(2)}, u32[]{:S(2)}) collective-permute-start(bf16[32,640]{1,0:T(8,128)(2,1)S(1)} %get-tuple-element.77), channel_id=1, source_target_pairs={{0,24},{4,28},{8,16},{12,20},{16,8},{20,12},{24,0},{28,4},{1,25},{... | collective-permute-start | bytes 122888 | tf_op jit(solution)/shard_map/ppermute | solution.py:397
  69.2 2.5 %collective-permute-done.23.refs_1_ = bf16[32,640]{1,0:T(8,128)(2,1)S(1)} collective-permute-done((bf16[32,640]{1,0:T(8,128)(2,1)S(1)}, bf16[32,640]{1,0:T(8,128)(2,1)S(1)}, u32[]{:S(2)}, u32[]{:S(2)}) %collective-permute-start.23) | collective-permute-done | bytes 40992 | tf_op jit(solution)/shard_map/ppermute | solution.py:397
  71.6 1.9 %collective-permute-done.24.refs_2_ = bf16[32,640]{1,0:T(8,128)(2,1)S(1)} collective-permute-done((bf16[32,640]{1,0:T(8,128)(2,1)S(1)}, bf16[32,640]{1,0:T(8,128)(2,1)S(1)}, u32[]{:S(2)}, u32[]{:S(2)}) %collective-permute-start.24) | collective-permute-done | bytes 40992 | tf_op jit(solution)/shard_map/ppermute | solution.py:397
  73.6 1.4 %collective-permute-start.25 = (f32[32,512]{1,0:T(8,128)S(1)}, f32[32,512]{1,0:T(8,128)S(1)}, u32[]{:S(2)}, u32[]{:S(2)}) collective-permute-start(f32[32,512]{1,0:T(8,128)S(1)} %get-tuple-element.78), channel_id=1, source_target_pairs={{0,2},{1,3},{2,0},{3,1},{4,6},{5,7},{6,4},{7,5},{8,10},{9,11},{10,... | collective-permute-start | bytes 196616 | tf_op jit(solution)/shard_map/ppermute | solution.py:397
  75.0 1.3 %collective-permute-start.26 = (f32[32,128]{1,0:T(8,128)S(1)}, f32[32,128]{1,0:T(8,128)S(1)}, u32[]{:S(2)}, u32[]{:S(2)}) collective-permute-start(f32[32,128]{1,0:T(8,128)S(1)} %get-tuple-element.79), channel_id=1, source_target_pairs={{0,4},{4,0},{8,12},{12,8},{16,20},{20,16},{24,28},{28,24},{1,5},{5... | collective-permute-start | bytes 49160 | tf_op jit(solution)/shard_map/ppermute | solution.py:397
  76.3 2.4 %collective-permute-done.26 = f32[32,128]{1,0:T(8,128)S(1)} collective-permute-done((f32[32,128]{1,0:T(8,128)S(1)}, f32[32,128]{1,0:T(8,128)S(1)}, u32[]{:S(2)}, u32[]{:S(2)}) %collective-permute-start.26) | collective-permute-done | bytes 16416 | tf_op jit(solution)/shard_map/ppermute | solution.py:397
  78.8 0.8 collective-permute-start.30
  79.6 1.4 %collective-permute-start.29 = (f32[32,128]{1,0:T(8,128)S(1)}, f32[32,128]{1,0:T(8,128)S(1)}, u32[]{:S(2)}, u32[]{:S(2)}) collective-permute-start(f32[32,128]{1,0:T(8,128)S(1)} %add.62.refs_2_), channel_id=1, source_target_pairs={{0,2},{1,3},{2,0},{3,1},{4,6},{5,7},{6,4},{7,5},{8,10},{9,11},{10,... | collective-permute-start | bytes 49160 | tf_op jit(solution)/shard_map/ppermute | solution.py:397
  81.0 1.1 %collective-permute-done.30.refs_5_ = f32[32,128]{1,0:T(8,128)S(1)} collective-permute-done((f32[32,128]{1,0:T(8,128)S(1)}, f32[32,128]{1,0:T(8,128)S(1)}, u32[]{:S(2)}, u32[]{:S(2)}) %collective-permute-start.30) | collective-permute-done | bytes 16416 | tf_op jit(solution)/shard_map/ppermute | solution.py:397
  82.1 1.3 %collective-permute-done.29.refs_4_ = f32[32,128]{1,0:T(8,128)S(1)} collective-permute-done((f32[32,128]{1,0:T(8,128)S(1)}, f32[32,128]{1,0:T(8,128)S(1)}, u32[]{:S(2)}, u32[]{:S(2)}) %collective-permute-start.29) | collective-permute-done | bytes 16416 | tf_op jit(solution)/shard_map/ppermute | solution.py:397
  83.3 1.7 %final.1 = (f32[32,2048]{1,0:T(8,128)}, f32[32,2048]{1,0:T(8,128)}) custom-call(s32[2]{0:T(128)S(1)} %pad_add_fusion.place, f32[32,2048]{1,0:T(8,128)S(1)} %copy-done, f32[2,40,512]{2,1,0:T(8,128)S(1)} %pad_maximum_fusion.1.s1_own, f32[2,40,512]{2,1,0:T(8,128)S(1)} %collective-permute-done.17.s1_got, f32[2,32,512]{2,1,0:T(8,128)S(1)} %pad_maximum_fusion.3.refs_0_, ...), custom_call_target="tpu_custom_call" | custom-call | tf_op jit(solution)/shard_map/final/pallas_call | solution.py:608
  (55 shorter events, 1.5 us)
Async XLA Ops:
  0.6 5.7 %collective-permute-start = (s32[8,6]{1,0:T(8,128)}, s32[8,6]{1,0:T(8,128)S(1)}, u32[]{:S(2)}, u32[]{:S(2)}) collective-permute-start(s32[8,6]{1,0:T(8,128)} %param.3), channel_id=1, source_target_pairs={{0,1},{1,0},{2,3},{3,2},{4,5},{5,4},{6,7},{7,6},{8,9},{9,8},{10,11... | collective-permute-start | bytes 584 | tf_op jit(solution)/shard_map/ppermute | solution.py:397
  1.1 5.3 %collective-permute-start.2 = (s32[8,6]{1,0:T(8,128)}, s32[8,6]{1,0:T(8,128)S(1)}, u32[]{:S(2)}, u32[]{:S(2)}) collective-permute-start(s32[8,6]{1,0:T(8,128)} %param.3), channel_id=1, source_target_pairs={{0,3},{1,2},{2,1},{3,0},{4,7},{5,6},{6,5},{7,4},{8,11},{9,10},{10,... | collective-permute-start | bytes 584 | tf_op jit(solution)/shard_map/ppermute | solution.py:397
  3.8 3.8 %collective-permute-start.1 = (s32[8,6]{1,0:T(8,128)}, s32[8,6]{1,0:T(8,128)S(1)}, u32[]{:S(2)}, u32[]{:S(2)}) collective-permute-start(s32[8,6]{1,0:T(8,128)} %param.3), channel_id=1, source_target_pairs={{0,2},{1,3},{2,0},{3,1},{4,6},{5,7},{6,4},{7,5},{8,10},{9,11},{10,... | collective-permute-start | bytes 584 | tf_op jit(solution)/shard_map/ppermute | solution.py:397
  7.9 8.1 %collective-permute-start.5 = (bf16[16,640]{1,0:T(8,128)(2,1)S(1)}, bf16[16,640]{1,0:T(8,128)(2,1)S(1)}, u32[]{:S(2)}, u32[]{:S(2)}) collective-permute-start(bf16[16,640]{1,0:T(8,128)(2,1)S(1)} %pad_maximum_fusion.5), channel_id=1, source_target_pairs={{0,24},{4,28},{8,16},{12,20},{16,8},{20,12},{24,0},{28,4},{1,25},{... | collective-permute-start | bytes 61448 | tf_op jit(solution)/shard_map/ppermute | solution.py:397
  11.6 5.2 %collective-permute-start.4 = (bf16[16,640]{1,0:T(8,128)(2,1)S(1)}, bf16[16,640]{1,0:T(8,128)(2,1)S(1)}, u32[]{:S(2)}, u32[]{:S(2)}) collective-permute-start(bf16[16,640]{1,0:T(8,128)(2,1)S(1)} %pad_maximum_fusion.5), channel_id=1, source_target_pairs={{0,16},{4,20},{8,24},{12,28},{16,0},{20,4},{24,8},{28,12},{1,17},{... | collective-permute-start | bytes 61448 | tf_op jit(solution)/shard_map/ppermute | solution.py:397
  11.6 5.2 %collective-permute-start.3 = (bf16[16,640]{1,0:T(8,128)(2,1)S(1)}, bf16[16,640]{1,0:T(8,128)(2,1)S(1)}, u32[]{:S(2)}, u32[]{:S(2)}) collective-permute-start(bf16[16,640]{1,0:T(8,128)(2,1)S(1)} %pad_maximum_fusion.5), channel_id=1, source_target_pairs={{0,8},{4,12},{8,0},{12,4},{16,24},{20,28},{24,16},{28,20},{1,9},{5... | collective-permute-start | bytes 61448 | tf_op jit(solution)/shard_map/ppermute | solution.py:397
  12.3 11.0 %collective-permute-start.9 = (f32[32,512]{1,0:T(8,128)S(1)}, f32[32,512]{1,0:T(8,128)S(1)}, u32[]{:S(2)}, u32[]{:S(2)}) collective-permute-start(f32[32,512]{1,0:T(8,128)S(1)} %constant_dynamic-slice_fusion), channel_id=1, source_target_pairs={{0,24},{4,28},{8,16},{12,20},{16,8},{20,12},{24,0},{28,4},{1,25},{... | collective-permute-start | bytes 196616 | tf_op jit(solution)/shard_map/ppermute | solution.py:397
  15.9 7.4 %collective-permute-start.8 = (f32[32,512]{1,0:T(8,128)S(1)}, f32[32,512]{1,0:T(8,128)S(1)}, u32[]{:S(2)}, u32[]{:S(2)}) collective-permute-start(f32[32,512]{1,0:T(8,128)S(1)} %constant_dynamic-slice_fusion), channel_id=1, source_target_pairs={{0,16},{4,20},{8,24},{12,28},{16,0},{20,4},{24,8},{28,12},{1,17},{... | collective-permute-start | bytes 196616 | tf_op jit(solution)/shard_map/ppermute | solution.py:397
  15.9 7.4 %collective-permute-start.7 = (f32[32,512]{1,0:T(8,128)S(1)}, f32[32,512]{1,0:T(8,128)S(1)}, u32[]{:S(2)}, u32[]{:S(2)}) collective-permute-start(f32[32,512]{1,0:T(8,128)S(1)} %constant_dynamic-slice_fusion), channel_id=1, source_target_pairs={{0,8},{4,12},{8,0},{12,4},{16,24},{20,28},{24,16},{28,20},{1,9},{5... | collective-permute-start | bytes 196616 | tf_op jit(solution)/shard_map/ppermute | solution.py:397
  16.8 6.6 %collective-permute-start.6 = (bf16[4,16,640]{2,1,0:T(8,128)(2,1)S(1)}, bf16[4,16,640]{2,1,0:T(8,128)(2,1)S(1)}, u32[]{:S(2)}, u32[]{:S(2)}) collective-permute-start(bf16[4,16,640]{2,1,0:T(8,128)(2,1)S(1)} %pad_maximum_fusion.4.refs_1_), channel_id=1, source_target_pairs={{0,4},{4,0},{8,12},{12,8},{16,20},{20,16},{24,28},{28,24},{1,5},{5... | collective-permute-start | bytes 245768 | tf_op jit(solution)/shard_map/ppermute | solution.py:397
  23.4 6.4 %collective-permute-start.10 = (f32[4,32,512]{2,1,0:T(8,128)S(1)}, f32[4,32,512]{2,1,0:T(8,128)S(1)}, u32[]{:S(2)}, u32[]{:S(2)}) collective-permute-start(f32[4,32,512]{2,1,0:T(8,128)S(1)} %pad_maximum_fusion.refs_2_.t_same), channel_id=1, source_target_pairs={{0,4},{4,0},{8,12},{12,8},{16,20},{20,16},{24,28},{28,24},{1,5},{5... | collective-permute-start | bytes 786440 | tf_op jit(solution)/shard_map/ppermute | solution.py:397
  24.6 28.4 %copy-start = (f32[32,2048]{1,0:T(8,128)S(1)}, f32[32,2048]{1,0:T(8,128)}, u32[]{:S(2)}) copy-start(f32[32,2048]{1,0:T(8,128)} %t_ref.5) | copy-start | bytes 786436
  29.9 5.9 %collective-permute-start.13 = (f32[16,256]{1,0:T(8,128)S(1)}, f32[16,256]{1,0:T(8,128)S(1)}, u32[]{:S(2)}, u32[]{:S(2)}) collective-permute-start(f32[16,256]{1,0:T(8,128)S(1)} %get-tuple-element.60), channel_id=1, source_target_pairs={{0,24},{4,28},{8,16},{12,20},{16,8},{20,12},{24,0},{28,4},{1,25},{... | collective-permute-start | bytes 49160 | tf_op jit(solution)/shard_map/ppermute | solution.py:397
  34.0 4.6 %collective-permute-start.12 = (f32[16,256]{1,0:T(8,128)S(1)}, f32[16,256]{1,0:T(8,128)S(1)}, u32[]{:S(2)}, u32[]{:S(2)}) collective-permute-start(f32[16,256]{1,0:T(8,128)S(1)} %get-tuple-element.60), channel_id=1, source_target_pairs={{0,16},{4,20},{8,24},{12,28},{16,0},{20,4},{24,8},{28,12},{1,17},{... | collective-permute-start | bytes 49160 | tf_op jit(solution)/shard_map/ppermute | solution.py:397
  34.0 4.6 %collective-permute-start.11 = (f32[16,256]{1,0:T(8,128)S(1)}, f32[16,256]{1,0:T(8,128)S(1)}, u32[]{:S(2)}, u32[]{:S(2)}) collective-permute-start(f32[16,256]{1,0:T(8,128)S(1)} %get-tuple-element.60), channel_id=1, source_target_pairs={{0,8},{4,12},{8,0},{12,4},{16,24},{20,28},{24,16},{28,20},{1,9},{5... | collective-permute-start | bytes 49160 | tf_op jit(solution)/shard_map/ppermute | solution.py:397
  38.7 3.8 %collective-permute-start.14 = (f32[16,256]{1,0:T(8,128)S(1)}, f32[16,256]{1,0:T(8,128)S(1)}, u32[]{:S(2)}, u32[]{:S(2)}) collective-permute-start(f32[16,256]{1,0:T(8,128)S(1)} %add_add_fusion), channel_id=1, source_target_pairs={{0,4},{4,0},{8,12},{12,8},{16,20},{20,16},{24,28},{28,24},{1,5},{5... | collective-permute-start | bytes 49160 | tf_op jit(solution)/shard_map/ppermute | solution.py:397
  45.3 1.4 %collective-permute-start.15 = (f32[2,32,512]{2,1,0:T(8,128)S(1)}, f32[2,32,512]{2,1,0:T(8,128)S(1)}, u32[]{:S(2)}, u32[]{:S(2)}) collective-permute-start(f32[2,32,512]{2,1,0:T(8,128)S(1)} %get-tuple-element.62), channel_id=1, source_target_pairs={{0,1},{1,0},{2,3},{3,2},{4,5},{5,4},{6,7},{7,6},{8,9},{9,8},{10,11... | collective-permute-start | bytes 393224 | tf_op jit(solution)/shard_map/ppermute | solution.py:397
  46.8 6.0 %collective-permute-start.16 = (f32[72,512]{1,0:T(8,128)S(1)}, f32[72,512]{1,0:T(8,128)S(1)}, u32[]{:S(2)}, u32[]{:S(2)}) collective-permute-start(f32[72,512]{1,0:T(8,128)S(1)} %pad_maximum_fusion.2), channel_id=1, source_target_pairs={{0,2},{1,3},{2,0},{3,1},{4,6},{5,7},{6,4},{7,5},{8,10},{9,11},{10,... | collective-permute-start | bytes 442376 | tf_op jit(solution)/shard_map/ppermute | solution.py:397
  52.9 1.5 %collective-permute-start.17 = (f32[2,40,512]{2,1,0:T(8,128)S(1)}, f32[2,40,512]{2,1,0:T(8,128)S(1)}, u32[]{:S(2)}, u32[]{:S(2)}) collective-permute-start(f32[2,40,512]{2,1,0:T(8,128)S(1)} %pad_maximum_fusion.1.s1_own), channel_id=1, source_target_pairs={{0,1},{1,0},{2,3},{3,2},{4,5},{5,4},{6,7},{7,6},{8,9},{9,8},{10,11... | collective-permute-start | bytes 491528 | tf_op jit(solution)/shard_map/ppermute | solution.py:397
  55.7 8.2 %collective-permute-start.18 = (bf16[4,32,512]{2,1,0:T(8,128)(2,1)S(1)}, bf16[4,32,512]{2,1,0:T(8,128)(2,1)S(1)}, u32[]{:S(2)}, u32[]{:S(2)}) collective-permute-start(bf16[4,32,512]{2,1,0:T(8,128)(2,1)S(1)} %second.3), channel_id=1, source_target_pairs={{0,4},{4,0},{8,12},{12,8},{16,20},{20,16},{24,28},{28,24},{1,5},{5... | collective-permute-start | bytes 393224 | tf_op jit(solution)/shard_map/ppermute | solution.py:397
  57.3 6.0 %collective-permute-start.21 = (bf16[32,512]{1,0:T(8,128)(2,1)S(1)}, bf16[32,512]{1,0:T(8,128)(2,1)S(1)}, u32[]{:S(2)}, u32[]{:S(2)}) collective-permute-start(bf16[32,512]{1,0:T(8,128)(2,1)S(1)} %fusion.2.refs_0_), channel_id=1, source_target_pairs={{0,24},{4,28},{8,16},{12,20},{16,8},{20,12},{24,0},{28,4},{1,25},{... | collective-permute-start | bytes 98312 | tf_op jit(solution)/shard_map/ppermute | solution.py:397
  58.7 4.9 %collective-permute-start.20 = (bf16[32,512]{1,0:T(8,128)(2,1)S(1)}, bf16[32,512]{1,0:T(8,128)(2,1)S(1)}, u32[]{:S(2)}, u32[]{:S(2)}) collective-permute-start(bf16[32,512]{1,0:T(8,128)(2,1)S(1)} %fusion.2.refs_0_), channel_id=1, source_target_pairs={{0,16},{4,20},{8,24},{12,28},{16,0},{20,4},{24,8},{28,12},{1,17},{... | collective-permute-start | bytes 98312 | tf_op jit(solution)/shard_map/ppermute | solution.py:397
  59.3 4.7 %collective-permute-start.19 = (bf16[32,512]{1,0:T(8,128)(2,1)S(1)}, bf16[32,512]{1,0:T(8,128)(2,1)S(1)}, u32[]{:S(2)}, u32[]{:S(2)}) collective-permute-start(bf16[32,512]{1,0:T(8,128)(2,1)S(1)} %fusion.2.refs_0_), channel_id=1, source_target_pairs={{0,8},{4,12},{8,0},{12,4},{16,24},{20,28},{24,16},{28,20},{1,9},{5... | collective-permute-start | bytes 98312 | tf_op jit(solution)/shard_map/ppermute | solution.py:397
  64.7 4.5 %collective-permute-start.22 = (bf16[32,640]{1,0:T(8,128)(2,1)S(1)}, bf16[32,640]{1,0:T(8,128)(2,1)S(1)}, u32[]{:S(2)}, u32[]{:S(2)}) collective-permute-start(bf16[32,640]{1,0:T(8,128)(2,1)S(1)} %get-tuple-element.75), channel_id=1, source_target_pairs={{0,8},{4,12},{8,0},{12,4},{16,24},{20,28},{24,16},{28,20},{1,9},{5... | collective-permute-start | bytes 122888 | tf_op jit(solution)/shard_map/ppermute | solution.py:397
  66.4 5.2 %collective-permute-start.23 = (bf16[32,640]{1,0:T(8,128)(2,1)S(1)}, bf16[32,640]{1,0:T(8,128)(2,1)S(1)}, u32[]{:S(2)}, u32[]{:S(2)}) collective-permute-start(bf16[32,640]{1,0:T(8,128)(2,1)S(1)} %get-tuple-element.76), channel_id=1, source_target_pairs={{0,16},{4,20},{8,24},{12,28},{16,0},{20,4},{24,8},{28,12},{1,17},{... | collective-permute-start | bytes 122888 | tf_op jit(solution)/shard_map/ppermute | solution.py:397
  67.7 5.8 %collective-permute-start.24 = (bf16[32,640]{1,0:T(8,128)(2,1)S(1)}, bf16[32,640]{1,0:T(8,128)(2,1)S(1)}, u32[]{:S(2)}, u32[]{:S(2)}) collective-permute-start(bf16[32,640]{1,0:T(8,128)(2,1)S(1)} %get-tuple-element.77), channel_id=1, source_target_pairs={{0,24},{4,28},{8,16},{12,20},{16,8},{20,12},{24,0},{28,4},{1,25},{... | collective-permute-start | bytes 122888 | tf_op jit(solution)/shard_map/ppermute | solution.py:397
  73.6 5.2 %collective-permute-start.25 = (f32[32,512]{1,0:T(8,128)S(1)}, f32[32,512]{1,0:T(8,128)S(1)}, u32[]{:S(2)}, u32[]{:S(2)}) collective-permute-start(f32[32,512]{1,0:T(8,128)S(1)} %get-tuple-element.78), channel_id=1, source_target_pairs={{0,2},{1,3},{2,0},{3,1},{4,6},{5,7},{6,4},{7,5},{8,10},{9,11},{10,... | collective-permute-start | bytes 196616 | tf_op jit(solution)/shard_map/ppermute | solution.py:397
  75.0 3.7 %collective-permute-start.26 = (f32[32,128]{1,0:T(8,128)S(1)}, f32[32,128]{1,0:T(8,128)S(1)}, u32[]{:S(2)}, u32[]{:S(2)}) collective-permute-start(f32[32,128]{1,0:T(8,128)S(1)} %get-tuple-element.79), channel_id=1, source_target_pairs={{0,4},{4,0},{8,12},{12,8},{16,20},{20,16},{24,28},{28,24},{1,5},{5... | collective-permute-start | bytes 49160 | tf_op jit(solution)/shard_map/ppermute | solution.py:397
  78.8 4.6 %collective-permute-start.27 = (f32[2,32,512]{2,1,0:T(8,128)S(1)}, f32[2,32,512]{2,1,0:T(8,128)S(1)}, u32[]{:S(2)}, u32[]{:S(2)}) collective-permute-start(f32[2,32,512]{2,1,0:T(8,128)S(1)} %pad_maximum_fusion.3.refs_0_), channel_id=1, source_target_pairs={{0,1},{1,0},{2,3},{3,2},{4,5},{5,4},{6,7},{7,6},{8,9},{9,8},{10,11... | collective-permute-start | bytes 393224 | tf_op jit(solution)/shard_map/ppermute | solution.py:397
  78.8 3.2 %collective-permute-start.30 = (f32[32,128]{1,0:T(8,128)S(1)}, f32[32,128]{1,0:T(8,128)S(1)}, u32[]{:S(2)}, u32[]{:S(2)}) collective-permute-start(f32[32,128]{1,0:T(8,128)S(1)} %add.62.refs_2_), channel_id=1, source_target_pairs={{0,3},{1,2},{2,1},{3,0},{4,7},{5,6},{6,5},{7,4},{8,11},{9,10},{10,... | collective-permute-start | bytes 49160 | tf_op jit(solution)/shard_map/ppermute | solution.py:397
  79.6 3.7 %collective-permute-start.29 = (f32[32,128]{1,0:T(8,128)S(1)}, f32[32,128]{1,0:T(8,128)S(1)}, u32[]{:S(2)}, u32[]{:S(2)}) collective-permute-start(f32[32,128]{1,0:T(8,128)S(1)} %add.62.refs_2_), channel_id=1, source_target_pairs={{0,2},{1,3},{2,0},{3,1},{4,6},{5,7},{6,4},{7,5},{8,10},{9,11},{10,... | collective-permute-start | bytes 49160 | tf_op jit(solution)/shard_map/ppermute | solution.py:397
  81.0 2.4 %collective-permute-start.28 = (f32[32,128]{1,0:T(8,128)S(1)}, f32[32,128]{1,0:T(8,128)S(1)}, u32[]{:S(2)}, u32[]{:S(2)}) collective-permute-start(f32[32,128]{1,0:T(8,128)S(1)} %add.62.refs_2_), channel_id=1, source_target_pairs={{0,1},{1,0},{2,3},{3,2},{4,5},{5,4},{6,7},{7,6},{8,9},{9,8},{10,11... | collective-permute-start | bytes 49160 | tf_op jit(solution)/shard_map/ppermute | solution.py:397

commit v11 on v10

--- a/solution.py
+++ b/solution.py
@@ -22,7 +22,6 @@
 DIRECT_ROWS = 8
 RESIDENT_BYTES = 20 * 1024 * 1024
 
-SMEM = pl.BlockSpec(memory_space=pltpu.SMEM)
 VMEM = pl.BlockSpec(memory_space=pltpu.VMEM)
 HBM = pl.BlockSpec(memory_space=pltpu.HBM)
 F32 = jnp.float32
@@ -33,6 +32,10 @@
     while len(parts) > 1:
         parts = [a + b for a, b in zip(parts[::2], parts[1::2])]
     return parts[0]
+
+
+def position():
+    return lax.axis_index("rows"), lax.axis_index("cols")
 
 
 class Sizes(NamedTuple):
@@ -73,20 +76,23 @@
     return n if cfg.parts == 1 else lax.shift_right_logical(place[0], 1) ^ n
 
 
-def build_kernel(cfg, part, place, direct, *refs):
+def build_kernel(cfg, part, direct_v, *refs):
     last = part == cfg.parts - 1
+    place = position()
     if part == 0:
         near_hbm, piece, refs = refs[0], refs[1], refs[2:]
-        k_mat, listed, deg_ref, lhs = refs[:4]
+        k_mat, list_v, deg_ref, lhs = refs[:4]
         near_ref, near_sem, refs = refs[4], refs[5], refs[6:]
         near_copy = pltpu.make_async_copy(near_hbm, near_ref, near_sem)
         near_copy.start()
     else:
         lhs, first_deg, piece, _ = refs[:4]
-        k_mat, listed, deg_ref = refs[4:7]
+        k_mat, list_v, deg_ref = refs[4:7]
         refs = refs[7:]
-    mlist, acc, rhs, dist, counts_v, counts, count_sem = refs[:7]
-    kbuf, sems = (None, None) if cfg.resident else refs[7:]
+    listed, mlist, acc, rhs, dist, direct, counts_v, counts, copy_sems = refs[:9]
+    kbuf, sems = (None, None) if cfg.resident else refs[9:]
+    direct_copy = pltpu.make_async_copy(direct_v, direct, copy_sems.at[0])
+    direct_copy.start()
     row, col = place[0], place[1]
     own_rows, block_len, nb = cfg.own_rows, cfg.block_len, cfg.nb
     own_len = own_rows * block_len
@@ -107,7 +113,7 @@
         return carry
 
     lax.fori_loop(0, held, count, 0, unroll=held <= 4)
-    fetch = pltpu.make_async_copy(counts_v, counts, count_sem)
+    fetch = pltpu.make_async_copy(counts_v, counts, copy_sems.at[1])
     fetch.start()
     lax.fori_loop(0, held, prepare, 0, unroll=held <= 4)
     acc[...] = jnp.zeros_like(acc)
@@ -117,6 +123,7 @@
             near = near_ref[:, i * block_len:(i + 1) * block_len].astype(F32)
             full = jnp.concatenate([near * (-2.0 * scale), augment(near, True)], axis=0)
             lhs[i] = full.T.astype(BF16)
+    direct_copy.wait()
     fetch.wait()
 
     pos = jnp.int32(0)
@@ -129,7 +136,7 @@
             for k in range(own_rows):
                 name = row_of(cfg, place, part, z) * cfg.block_rows + col * own_rows + k
                 m = direct[i, name] + jnp.where(name == me, 0, counts[z, spots[k][0], spots[k][1]])
-                listed[at + 1] = i * CODE + z * own_rows + k
+                listed[0, at + 1] = i * CODE + z * own_rows + k
                 mlist[at] = m
                 at = at + jnp.where(m > 0, 1, 0)
             return at
@@ -140,10 +147,12 @@
         else:
             pos = lax.fori_loop(0, held, note, pos, unroll=4)
     for u in range(GROUP):
-        listed[pos + u + 1] = 0
+        listed[0, pos + u + 1] = 0
         mlist[pos + u] = 0
     total = lax.shift_right_logical(pos + (GROUP - 1), GROUP_BITS)
-    listed[0] = total
+    listed[0, 0] = total
+    list_copy = pltpu.make_async_copy(listed, list_v, copy_sems.at[2])
+    list_copy.start()
 
     def copy_out(g):
         slot = lax.rem(g, RING)
@@ -152,7 +161,7 @@
     base = part * cfg.part_groups
 
     def distances(e, slot):
-        code = listed[e + 1]
+        code = listed[0, e + 1]
         i, j = lax.shift_right_logical(code, CODE_BITS), code & (CODE - 1)
         dist[slot] = jnp.dot(lhs[i], rhs[j], preferred_element_type=F32)
 
@@ -168,7 +177,7 @@
 
         for u in range(GROUP):
             distances(g * GROUP + u + 1, (u + 1) % 2)
-            j = listed[g * GROUP + u + 1] & (CODE - 1)
+            j = listed[0, g * GROUP + u + 1] & (CODE - 1)
             m = mlist[g * GROUP + u].astype(F32)
             sums = jnp.zeros((8, block_len), F32)
             for s in range(block_len // STRIP):
@@ -204,6 +213,7 @@
 
     if not cfg.resident:
         lax.fori_loop(jnp.maximum(total - RING, 0), total, drain, 0)
+    list_copy.wait()
 
 
 def pieces_of(own, got):
@@ -211,7 +221,7 @@
 
 
 def walk(cfg, part, listed, k_mat, kbuf, sems, product, total_ref, by_row):
-    total = listed[0]
+    total = listed[0, 0]
     base = part * cfg.part_groups
 
     def copy_in(g):
@@ -234,7 +244,7 @@
                 copy_in(g + (RING - 1)).start()
 
             copy_in(g).wait()
-        codes = [listed[g * GROUP + u + 1] for u in range(GROUP)]
+        codes = [listed[0, g * GROUP + u + 1] for u in range(GROUP)]
         pairs = [(lax.shift_right_logical(code, CODE_BITS), code & (CODE - 1)) for code in codes]
         terms = [product(i, j, source[slot, u]) for u, (i, j) in enumerate(pairs)]
         for (i, j), term in zip(pairs, terms):
@@ -244,15 +254,21 @@
     lax.fori_loop(0, total, step, 0)
 
 
-def first_kernel(cfg, place, k_mat, *refs):
+def first_kernel(cfg, k_mat, *refs):
     n = cfg.parts
     lists, pieces, inv_ref, refs = refs[:n], refs[n:2 * n], refs[2 * n], refs[2 * n + 1:]
-    near, near_y, cross, own_inv, z_acc, w_all, *ring = refs
+    near, near_y, cross, own_inv, z_acc, w_all, listed, list_sems, *ring = refs
     kbuf, sems = ring or (None, None)
+    place = position()
     col = place[1]
+    copies = [
+        pltpu.make_async_copy(lists[p], listed.at[p], list_sems.at[p]) for p in range(n)
+    ]
+    for copy in copies:
+        copy.start()
     own_rows, block_len = cfg.own_rows, cfg.block_len
     z_acc[...] = jnp.zeros_like(z_acc)
-    for part, (listed, piece) in enumerate(zip(lists, pieces)):
+    for part, piece in enumerate(pieces):
         held = piece.shape[0]
 
         def prepare(m, carry, part=part, piece=piece):
@@ -270,7 +286,8 @@
                 w_all[j], block, (((1,), (1,)), ((), ())), preferred_element_type=F32
             )
 
-        walk(cfg, part, listed, k_mat, kbuf, sems, product, z_acc, True)
+        copies[part].wait()
+        walk(cfg, part, listed.at[part], k_mat, kbuf, sems, product, z_acc, True)
     for k in range(own_rows):
         cols = slice(k * block_len, (k + 1) * block_len)
         mine = inv_ref[pl.ds(place[0] * own_rows + k, 1), :]
@@ -279,10 +296,13 @@
             ref[:, cols] = z_acc[(col ^ e) * own_rows + k]
 
 
-def second_kernel(cfg, part, place, k_mat, listed, t_ref, s1_own, s1_got, out, z_acc, w_all, *ring):
+def second_kernel(cfg, part, k_mat, list_v, t_ref, s1_own, s1_got, out, z_acc, w_all, listed, list_sem, *ring):
     kbuf, sems = ring or (None, None)
+    place = position()
     own_rows, block_len = cfg.own_rows, cfg.block_len
     outputs = t_ref.shape[0]
+    list_copy = pltpu.make_async_copy(list_v, listed, list_sem)
+    list_copy.start()
     for e, packed in enumerate(pieces_of(s1_own, s1_got)):
         share = place[1] ^ e
         for k in range(own_rows):
@@ -296,6 +316,7 @@
     def product(i, j, block):
         return jnp.dot(w_all[i], block, preferred_element_type=F32)
 
+    list_copy.wait()
     walk(cfg, part, listed, k_mat, kbuf, sems, product, z_acc, False)
 
     def hand_out(m, carry):
@@ -311,10 +332,11 @@
 N_DOTS = 5
 
 
-def meet_kernel(cfg, place, z_same, z_other, t_same, inv_ref, s1_own, *refs):
+def meet_kernel(cfg, z_same, z_other, t_same, inv_ref, s1_own, *refs):
     gs, (own_z, own_dots, *outs) = refs[:4], refs[4:]
     own_rows, block_len = cfg.own_rows, cfg.block_len
     outputs, own_len = own_z.shape
+    place = position()
     tz = jnp.zeros((outputs, 1), F32)
     gz = jnp.zeros((outputs, 1), F32)
     for n in range(4):
@@ -361,11 +383,12 @@
     dot_ref[...] = out
 
 
-def final_kernel(place, t_ref, s1_own, s1_got, *refs):
+def final_kernel(t_ref, s1_own, s1_got, *refs):
     grown, all_dots = pieces_of(refs[0], refs[1]), refs[2:6]
     sol_hbm, res_hbm, sol_ref, res_ref, sems = refs[6:]
     s1s = pieces_of(s1_own, s1_got)
     outputs, own_len = grown[0].shape
+    place = position()
     dots = pair_sum([ref[...] for ref in all_dots])
     tt, ts1, s1s1, ts2, s1s2 = (dots[:, n:n + 1] for n in range(5))
     a1 = tt / (REG * tt + ts1)
@@ -428,8 +451,7 @@
     n_part = n_sub // parts
     bound = min(block_rows * n_part, n_cols * capacity * (n_rows + 1))
     n_groups = -(-bound // GROUP)
-    list_len = n_groups * GROUP + GROUP + 1
-    place = jnp.stack([row, col])
+    list_len = -(-(n_groups * GROUP + GROUP + 1) // LANES) * LANES
     resident = parts * 2 * n_groups * GROUP * block_len * block_len <= RESIDENT_BYTES
     k_shape = (parts * n_groups, GROUP, block_len, block_len)
     limit = pltpu.CompilerParams(vmem_limit_bytes=(8 if resident else 32) * 1024 * 1024)
@@ -466,37 +488,39 @@
         first, last = part == 0, part == parts - 1
         out = [
             pltpu.VMEM(k_shape, BF16) if resident else shape(*k_shape, dtype=BF16),
-            shape(list_len, dtype=jnp.int32),
+            shape(1, list_len, dtype=jnp.int32),
             shape(n_sub if last else n_part, block_len),
         ]
         out += [shape(block_rows, block_len, 2 * dim, dtype=BF16)] if first else []
         k_mat, *rest = pl.pallas_call(
             functools.partial(build_kernel, cfg, part),
             out_shape=out,
-            in_specs=[SMEM, SMEM] + ([HBM, VMEM] if first else [VMEM] * 3 + [k_spec]),
-            out_specs=[k_spec, SMEM] + [VMEM] * (len(out) - 2),
+            in_specs=[VMEM] + ([HBM, VMEM] if first else [VMEM] * 3 + [k_spec]),
+            out_specs=[k_spec] + [VMEM] * (len(out) - 1),
             scratch_shapes=([
                 pltpu.VMEM((dim, npoints), BF16),
                 pltpu.SemaphoreType.DMA,
             ] if first else []) + [
+                pltpu.SMEM((1, list_len), jnp.int32),
                 pltpu.SMEM((list_len,), jnp.int32),
                 pltpu.VMEM((n_part, 8, block_len), F32),
                 pltpu.VMEM((n_part, 2 * dim, block_len), BF16),
                 pltpu.VMEM((2, block_len, block_len), F32),
+                pltpu.SMEM((block_rows, nb), jnp.int32),
                 pltpu.VMEM((n_part // own_rows, cfg.count_rows, LANES), jnp.int32),
                 pltpu.SMEM((n_part // own_rows, cfg.count_rows, LANES), jnp.int32),
-                pltpu.SemaphoreType.DMA,
+                pltpu.SemaphoreType.DMA((3,)),
                 *ring,
             ],
             compiler_params=limit,
-            input_output_aliases={} if first else {5: 0},
+            input_output_aliases={} if first else {4: 0},
             cost_estimate=pl.CostEstimate(
                 flops=2 * 2 * dim * bound * block_len * block_len,
                 bytes_accessed=2 * bound * block_len * block_len,
                 transcendentals=bound * block_len * block_len,
             ),
             name="build",
-        )(place, direct, *operands)
+        )(direct, *operands)
         if resident:
             k_mat = pltpu.with_memory_space_constraint(k_mat, pltpu.VMEM)
         return k_mat, *rest
@@ -528,17 +552,19 @@
     near_z, near_y, cross_z, tail = pl.pallas_call(
         functools.partial(first_kernel, cfg),
         out_shape=[shape(outputs, own_len)] * 2 + [shape(2, outputs, own_len), shape(8, own_len)],
-        in_specs=[SMEM, k_spec] + [SMEM] * parts + [VMEM] * (parts + 1),
+        in_specs=[k_spec] + [VMEM] * (2 * parts + 1),
         out_specs=[VMEM] * 4,
         scratch_shapes=[
             pltpu.VMEM((block_rows, outputs, block_len), F32),
             pltpu.VMEM((n_part, outputs, block_len), BF16),
+            pltpu.SMEM((parts, 1, list_len), jnp.int32),
+            pltpu.SemaphoreType.DMA((parts,)),
             *ring,
         ],
         compiler_params=limit,
         cost_estimate=cost(parts),
         name="first",
-    )(place, k_mat, *k_lists, *t_pieces, inv)
+    )(k_mat, *k_lists, *t_pieces, inv)
 
     got = swap(cross_z, "cols", 1)
     half = jnp.concatenate([near_z + got[0], near_y + got[1], tail], axis=0)
@@ -555,17 +581,19 @@
         return pl.pallas_call(
             functools.partial(second_kernel, cfg, part),
             out_shape=shape(n_part // own_rows, outputs, own_len, dtype=dtype),
-            in_specs=[SMEM, k_spec, SMEM] + [VMEM] * 3,
+            in_specs=[k_spec] + [VMEM] * 4,
             out_specs=VMEM,
             scratch_shapes=[
                 pltpu.VMEM((n_part, outputs, block_len), F32),
                 pltpu.VMEM((block_rows, outputs, block_len), BF16),
+                pltpu.SMEM((1, list_len), jnp.int32),
+                pltpu.SemaphoreType.DMA,
                 *ring,
             ],
             compiler_params=limit,
             cost_estimate=cost(1),
             name="second",
-        )(place, k_mat, k_lists[part], held_t, s1_own, s1_got)
+        )(k_mat, k_lists[part], held_t, s1_own, s1_got)
 
     if direct_rows:
         g = ((s1_own[0, :outputs] - SHIFT * own_t) * tail[:1]).astype(BF16)
@@ -578,11 +606,12 @@
         own_z, own_dots, *sends = pl.pallas_call(
             functools.partial(meet_kernel, cfg),
             out_shape=[shape(outputs, own_len), shape(outputs, LANES, dtype=BF16)] + [row_piece] * 3,
-            in_specs=[SMEM] + [VMEM] * 9,
+            in_specs=[VMEM] * 9,
             out_specs=[VMEM] * 5,
             compiler_params=limit,
             name="meet",
-        )(place, z2_same, z2_other, t_pieces[0], inv, s1_own, *gs)
+        )(z2_same, z2_other, t_pieces[0], inv, s1_own, *gs)
+        got = [swap(sends[n], "rows", 2 * n + 2) for n in (2, 1, 0)][::-1]
         grown, dots = pl.pallas_call(
             product_kernel,
             out_shape=(shape(outputs, own_len), shape(outputs, LANES)),
@@ -590,7 +619,7 @@
             out_specs=(VMEM, VMEM),
             compiler_params=limit,
             name="products",
-        )(own_z, own_dots, s1_own, *[swap(x, "rows", 2 * n + 2) for n, x in enumerate(sends)])
+        )(own_z, own_dots, s1_own, *got)
         dots = pair_sum(across_x(dots))
     else:
         z2 = lax.psum_scatter(second(0, F32), "rows", scatter_dimension=0)
@@ -608,7 +637,7 @@
     return pl.pallas_call(
         final_kernel,
         out_shape=(shape(outputs, npoints), shape(outputs, npoints)),
-        in_specs=[SMEM] + [VMEM] * 9,
+        in_specs=[VMEM] * 9,
         out_specs=(HBM, HBM),
         scratch_shapes=[
             pltpu.VMEM((4, outputs, own_len), F32),
@@ -617,7 +646,7 @@
         ],
         compiler_params=limit,
         name="final",
-    )(place, held_t, *ends)
+    )(held_t, *ends)
 
 
 def solution(mesh):

time: 85.2 us -> 84.5 us (level)
  starting transfers between devices: 37.6 us -> 35.2 us
  waiting for transfers between devices: 25.6 us -> 27.8 us
    ppermute x31, starting transfers between devices: 37.6 us -> 35.2 us  [swap(): return lax.ppermute(x, axis, [(i, i ^ d) for i in range(size)])]
    ppermute x31, waiting for transfers between devices: 25.6 us -> 27.8 us  [swap(): return lax.ppermute(x, axis, [(i, i ^ d) for i in range(size)])]
  transfers between devices with their start and end apart: 31 -> 31, of which waited for: 16 -> 18; matrix products, arithmetic and copies ran while one was open for 3% -> 3% of each run, Pallas kernels for 13% -> 12%
where the time goes in v11:
time: 84.5 us; the launch traced here: 84.3 us
  starting transfers between devices  35.2 us (42%)
  waiting for transfers between devices  27.8 us (33%)
  Pallas kernels  17.2 us (20%)
  local copies, waits for them, and re-layouts  2.74 us (3%)
  between operations  0.86 us (1%)
    ppermute x31, starting transfers between devices, swap(): return lax.ppermute(x, axis, [(i, i ^ d) for i in range(size)])  35.2 us
    ppermute x31, waiting for transfers between devices, swap(): return lax.ppermute(x, axis, [(i, i ^ d) for i in range(size)])  27.8 us
    pallas_call x2, Pallas kernels, build(): pl.pallas_call(functools.partial(build_kernel, cfg, part), out_shape=out,...  8.76 us
    pallas_call x1, Pallas kernels, local(): pl.pallas_call(functools.partial(first_kernel, cfg), out_shape=[shape(out...  3.62 us
    pallas_call x2, Pallas kernels, second(): pl.pallas_call(functools.partial(second_kernel, cfg, part), out_shape=sha...  3.41 us
  transfers between devices with their start and end apart: 31, of which 18 were waited for; matrix products, arithmetic and copies ran while one was open for 3% of the time, Pallas kernels for 12%

profile of v11, /device:TPU:0, one launch (start us, length us, event | category | flops | bytes accessed | tf_op | source)
XLA Modules:
  0.0 84.3 jit_solution(7728476446881335717)
XLA Ops:
  0.6 0.5 collective-permute-start
  1.1 2.6 %collective-permute-start.2 = (s32[8,6]{1,0:T(8,128)}, s32[8,6]{1,0:T(8,128)S(1)}, u32[]{:S(2)}, u32[]{:S(2)}) collective-permute-start(s32[8,6]{1,0:T(8,128)} %param.3), channel_id=1, source_target_pairs={{0,3},{1,2},{2,1},{3,0},{4,7},{5,6},{6,5},{7,4},{8,11},{9,10},{10,... | collective-permute-start | bytes 584 | tf_op jit(solution)/shard_map/ppermute | solution.py:420
  3.8 0.8 copy.6
  4.7 0.7 constant_dynamic-slice_fusion.1
  5.5 0.8 %constant_dynamic-slice_fusion = f32[32,512]{1,0:T(8,128)S(1)} fusion(f32[32,2048]{1,0:T(8,128)} %t_ref.5, s32[]{:T(128)S(6)} %select_n.7), kind=kLoop, calls=%fused_computation.33 | loop fusion | bytes 131076 | tf_op jit(solution)/shard_map/dynamic_slice | solution.py:471
  6.6 1.0 %collective-permute-done.1 = s32[8,6]{1,0:T(8,128)S(1)} collective-permute-done((s32[8,6]{1,0:T(8,128)}, s32[8,6]{1,0:T(8,128)S(1)}, u32[]{:S(2)}, u32[]{:S(2)}) %collective-permute-start.1) | collective-permute-done | bytes 224 | tf_op jit(solution)/shard_map/ppermute | solution.py:420
  7.9 3.7 %collective-permute-start.5 = (bf16[16,640]{1,0:T(8,128)(2,1)S(1)}, bf16[16,640]{1,0:T(8,128)(2,1)S(1)}, u32[]{:S(2)}, u32[]{:S(2)}) collective-permute-start(bf16[16,640]{1,0:T(8,128)(2,1)S(1)} %pad_maximum_fusion.5), channel_id=1, source_target_pairs={{0,24},{4,28},{8,16},{12,20},{16,8},{20,12},{24,0},{28,4},{1,25},{... | collective-permute-start | bytes 61448 | tf_op jit(solution)/shard_map/ppermute | solution.py:420
  11.6 0.8 collective-permute-start.3
  12.3 1.2 %collective-permute-done.5 = bf16[16,640]{1,0:T(8,128)(2,1)S(1)} collective-permute-done((bf16[16,640]{1,0:T(8,128)(2,1)S(1)}, bf16[16,640]{1,0:T(8,128)(2,1)S(1)}, u32[]{:S(2)}, u32[]{:S(2)}) %collective-permute-start.5) | collective-permute-done | bytes 20512 | tf_op jit(solution)/shard_map/ppermute | solution.py:420
  13.6 2.7 %collective-permute-done.4 = bf16[16,640]{1,0:T(8,128)(2,1)S(1)} collective-permute-done((bf16[16,640]{1,0:T(8,128)(2,1)S(1)}, bf16[16,640]{1,0:T(8,128)(2,1)S(1)}, u32[]{:S(2)}, u32[]{:S(2)}) %collective-permute-start.4) | collective-permute-done | bytes 20512 | tf_op jit(solution)/shard_map/ppermute | solution.py:420
  16.3 1.6 %collective-permute-start.6 = (bf16[4,16,640]{2,1,0:T(8,128)(2,1)S(1)}, bf16[4,16,640]{2,1,0:T(8,128)(2,1)S(1)}, u32[]{:S(2)}, u32[]{:S(2)}) collective-permute-start(bf16[4,16,640]{2,1,0:T(8,128)(2,1)S(1)} %pad_maximum_fusion.4.refs_1_), channel_id=1, source_target_pairs={{0,4},{4,0},{8,12},{12,8},{16,20},{20,16},{24,28},{28,24},{1,5},{5... | collective-permute-start | bytes 245768 | tf_op jit(solution)/shard_map/ppermute | solution.py:420
  17.8 1.5 %collective-permute-start.9 = (f32[32,512]{1,0:T(8,128)S(1)}, f32[32,512]{1,0:T(8,128)S(1)}, u32[]{:S(2)}, u32[]{:S(2)}) collective-permute-start(f32[32,512]{1,0:T(8,128)S(1)} %constant_dynamic-slice_fusion), channel_id=1, source_target_pairs={{0,24},{4,28},{8,16},{12,20},{16,8},{20,12},{24,0},{28,4},{1,25},{... | collective-permute-start | bytes 196616 | tf_op jit(solution)/shard_map/ppermute | solution.py:420
  19.3 0.6 collective-permute-start.8
  19.8 2.4 %collective-permute-start.7 = (f32[32,512]{1,0:T(8,128)S(1)}, f32[32,512]{1,0:T(8,128)S(1)}, u32[]{:S(2)}, u32[]{:S(2)}) collective-permute-start(f32[32,512]{1,0:T(8,128)S(1)} %constant_dynamic-slice_fusion), channel_id=1, source_target_pairs={{0,8},{4,12},{8,0},{12,4},{16,24},{20,28},{24,16},{28,20},{1,9},{5... | collective-permute-start | bytes 196616 | tf_op jit(solution)/shard_map/ppermute | solution.py:420
  22.2 4.4 %build.2 = (bf16[32,4,256,256]{3,2,1,0:T(8,128)(2,1)S(1)}, s32[1,128]{1,0:T(1,128)S(1)}, f32[8,256]{1,0:T(8,128)S(1)}, bf16[8,256,32]{2,1,0:T(8,128)(2,1)S(1)}) custom-call(s32[8,64]{1,0:T(8,128)S(1)} %add_add_fusion.1.direct_v, bf16[16,2048]{1,0:T(8,128)(2,1)} %refs_0_.1, bf16[4,16,640]{2,1,0:T(8,128)(2,1)S(1)} %pad_maximum_fusion.4.refs_1_), custom_call_target="tpu_custom_call" | custom-call | flops 268435456 | bytes 8388608 | tf_op jit(solution)/shard_map/build/pallas_call | solution.py:495
  26.6 0.6 collective-permute-start.10
  27.2 4.4 %build.3 = (bf16[32,4,256,256]{3,2,1,0:T(8,128)(2,1)S(1)}, s32[1,128]{1,0:T(1,128)S(1)}, f32[16,256]{1,0:T(8,128)S(1)}) custom-call(s32[8,64]{1,0:T(8,128)S(1)} %add_add_fusion.1.direct_v, bf16[8,256,32]{2,1,0:T(8,128)(2,1)S(1)} %get-tuple-element.43.refs_0_, f32[8,256]{1,0:T(8,128)S(1)} %get-tuple-element.46.refs_1_, ...), custom_call_target="tpu_custom_call", output_to_operand_aliasing={{0}: (4, {})} | custom-call | flops 268435456 | bytes 8388608 | tf_op jit(solution)/shard_map/build/pallas_call | solution.py:495
  31.7 1.4 %collective-permute-done.10.refs_3_ = f32[4,32,512]{2,1,0:T(8,128)S(1)} collective-permute-done((f32[4,32,512]{2,1,0:T(8,128)S(1)}, f32[4,32,512]{2,1,0:T(8,128)S(1)}, u32[]{:S(2)}, u32[]{:S(2)}) %collective-permute-start.10) | collective-permute-done | bytes 262176 | tf_op jit(solution)/shard_map/ppermute | solution.py:420
  33.1 1.5 %collective-permute-start.13 = (f32[16,256]{1,0:T(8,128)S(1)}, f32[16,256]{1,0:T(8,128)S(1)}, u32[]{:S(2)}, u32[]{:S(2)}) collective-permute-start(f32[16,256]{1,0:T(8,128)S(1)} %get-tuple-element.60), channel_id=1, source_target_pairs={{0,24},{4,28},{8,16},{12,20},{16,8},{20,12},{24,0},{28,4},{1,25},{... | collective-permute-start | bytes 49160 | tf_op jit(solution)/shard_map/ppermute | solution.py:420
  34.5 0.5 collective-permute-start.12
  35.1 2.4 %collective-permute-start.11 = (f32[16,256]{1,0:T(8,128)S(1)}, f32[16,256]{1,0:T(8,128)S(1)}, u32[]{:S(2)}, u32[]{:S(2)}) collective-permute-start(f32[16,256]{1,0:T(8,128)S(1)} %get-tuple-element.60), channel_id=1, source_target_pairs={{0,8},{4,12},{8,0},{12,4},{16,24},{20,28},{24,16},{28,20},{1,9},{5... | collective-permute-start | bytes 49160 | tf_op jit(solution)/shard_map/ppermute | solution.py:420
  37.5 1.1 %collective-permute-done.13 = f32[16,256]{1,0:T(8,128)S(1)} collective-permute-done((f32[16,256]{1,0:T(8,128)S(1)}, f32[16,256]{1,0:T(8,128)S(1)}, u32[]{:S(2)}, u32[]{:S(2)}) %collective-permute-start.13) | collective-permute-done | bytes 16416 | tf_op jit(solution)/shard_map/ppermute | solution.py:420
  38.6 0.6 collective-permute-done.12
  39.8 3.4 %collective-permute-done.14 = f32[16,256]{1,0:T(8,128)S(1)} collective-permute-done((f32[16,256]{1,0:T(8,128)S(1)}, f32[16,256]{1,0:T(8,128)S(1)}, u32[]{:S(2)}, u32[]{:S(2)}) %collective-permute-start.14) | collective-permute-done | bytes 16416 | tf_op jit(solution)/shard_map/ppermute | solution.py:420
  43.2 3.6 %first.1 = (f32[32,512]{1,0:T(8,128)S(1)}, f32[32,512]{1,0:T(8,128)S(1)}, f32[2,32,512]{2,1,0:T(8,128)S(1)}, f32[8,512]{1,0:T(8,128)S(1)}) custom-call(bf16[32,4,256,256]{3,2,1,0:T(8,128)(2,1)S(1)} %get-tuple-element.54.k_mat, s32[1,128]{1,0:T(1,128)S(1)} %get-tuple-element.55.refs_0_.list_v, s32[1,128]{1,0:T(1,128)S(1)} %get-tuple-element.56.refs_1_.list_v, ...), custom_call_target="tpu_custom_call" | custom-call | flops 536870912 | bytes 8388608 | tf_op jit(solution)/shard_map/first/pallas_call | solution.py:552
  46.9 1.3 %collective-permute-done.15 = f32[2,32,512]{2,1,0:T(8,128)S(1)} collective-permute-done((f32[2,32,512]{2,1,0:T(8,128)S(1)}, f32[2,32,512]{2,1,0:T(8,128)S(1)}, u32[]{:S(2)}, u32[]{:S(2)}) %collective-permute-start.15) | collective-permute-done | bytes 131104 | tf_op jit(solution)/shard_map/ppermute | solution.py:420
  48.3 1.3 %collective-permute-start.16 = (f32[72,512]{1,0:T(8,128)S(1)}, f32[72,512]{1,0:T(8,128)S(1)}, u32[]{:S(2)}, u32[]{:S(2)}) collective-permute-start(f32[72,512]{1,0:T(8,128)S(1)} %pad_maximum_fusion.2), channel_id=1, source_target_pairs={{0,2},{1,3},{2,0},{3,1},{4,6},{5,7},{6,4},{7,5},{8,10},{9,11},{10,... | collective-permute-start | bytes 442376 | tf_op jit(solution)/shard_map/ppermute | solution.py:420
  49.6 4.6 %collective-permute-done.16 = f32[72,512]{1,0:T(8,128)S(1)} collective-permute-done((f32[72,512]{1,0:T(8,128)S(1)}, f32[72,512]{1,0:T(8,128)S(1)}, u32[]{:S(2)}, u32[]{:S(2)}) %collective-permute-start.16) | collective-permute-done | bytes 147488 | tf_op jit(solution)/shard_map/ppermute | solution.py:420
  54.4 1.3 %collective-permute-done.17.s1_got = f32[2,40,512]{2,1,0:T(8,128)S(1)} collective-permute-done((f32[2,40,512]{2,1,0:T(8,128)S(1)}, f32[2,40,512]{2,1,0:T(8,128)S(1)}, u32[]{:S(2)}, u32[]{:S(2)}) %collective-permute-start.17) | collective-permute-done | bytes 163872 | tf_op jit(solution)/shard_map/ppermute | solution.py:420
  55.8 1.8 %second.3 = bf16[4,32,512]{2,1,0:T(8,128)(2,1)S(1)} custom-call(bf16[32,4,256,256]{3,2,1,0:T(8,128)(2,1)S(1)} %get-tuple-element.54.k_mat, s32[1,128]{1,0:T(1,128)S(1)} %get-tuple-element.56.refs_1_.list_v, f32[32,2048]{1,0:T(8,128)S(1)} %copy-done, f32[2,40,512]{2,1,0:T(8,128)S(1)} %pad_maximum_fusion.1.s1_own, f32[2,40,512]{2,1,0:T(8,128)S(1)} %collective-permute-done.17.s1_got), custom_call_target="tpu_custom_call" | custom-call | flops 268435456 | bytes 4194304 | tf_op jit(solution)/shard_map/second/pallas_call | solution.py:581
  57.7 2.0 %collective-permute-start.21 = (bf16[32,512]{1,0:T(8,128)(2,1)S(1)}, bf16[32,512]{1,0:T(8,128)(2,1)S(1)}, u32[]{:S(2)}, u32[]{:S(2)}) collective-permute-start(bf16[32,512]{1,0:T(8,128)(2,1)S(1)} %fusion.2.refs_0_), channel_id=1, source_target_pairs={{0,24},{4,28},{8,16},{12,20},{16,8},{20,12},{24,0},{28,4},{1,25},{... | collective-permute-start | bytes 98312 | tf_op jit(solution)/shard_map/ppermute | solution.py:420
  59.6 1.4 %collective-permute-start.20 = (bf16[32,512]{1,0:T(8,128)(2,1)S(1)}, bf16[32,512]{1,0:T(8,128)(2,1)S(1)}, u32[]{:S(2)}, u32[]{:S(2)}) collective-permute-start(bf16[32,512]{1,0:T(8,128)(2,1)S(1)} %fusion.2.refs_0_), channel_id=1, source_target_pairs={{0,16},{4,20},{8,24},{12,28},{16,0},{20,4},{24,8},{28,12},{1,17},{... | collective-permute-start | bytes 98312 | tf_op jit(solution)/shard_map/ppermute | solution.py:420
  61.0 1.1 %collective-permute-start.19 = (bf16[32,512]{1,0:T(8,128)(2,1)S(1)}, bf16[32,512]{1,0:T(8,128)(2,1)S(1)}, u32[]{:S(2)}, u32[]{:S(2)}) collective-permute-start(bf16[32,512]{1,0:T(8,128)(2,1)S(1)} %fusion.2.refs_0_), channel_id=1, source_target_pairs={{0,8},{4,12},{8,0},{12,4},{16,24},{20,28},{24,16},{28,20},{1,9},{5... | collective-permute-start | bytes 98312 | tf_op jit(solution)/shard_map/ppermute | solution.py:420
  62.1 1.6 %second.2.z_same = f32[4,32,512]{2,1,0:T(8,128)S(1)} custom-call(bf16[32,4,256,256]{3,2,1,0:T(8,128)(2,1)S(1)} %get-tuple-element.54.k_mat, s32[1,128]{1,0:T(1,128)S(1)} %get-tuple-element.55.refs_0_.list_v, f32[32,2048]{1,0:T(8,128)S(1)} %copy-done, f32[2,40,512]{2,1,0:T(8,128)S(1)} %pad_maximum_fusion.1.s1_own, ...), custom_call_target="tpu_custom_call" | custom-call | flops 268435456 | bytes 4194304 | tf_op jit(solution)/shard_map/second/pallas_call | solution.py:581
  63.7 0.9 %collective-permute-done.20.refs_2_ = bf16[32,512]{1,0:T(8,128)(2,1)S(1)} collective-permute-done((bf16[32,512]{1,0:T(8,128)(2,1)S(1)}, bf16[32,512]{1,0:T(8,128)(2,1)S(1)}, u32[]{:S(2)}, u32[]{:S(2)}) %collective-permute-start.20) | collective-permute-done | bytes 32800 | tf_op jit(solution)/shard_map/ppermute | solution.py:420
  65.2 1.1 %collective-permute-start.22 = (bf16[32,640]{1,0:T(8,128)(2,1)S(1)}, bf16[32,640]{1,0:T(8,128)(2,1)S(1)}, u32[]{:S(2)}, u32[]{:S(2)}) collective-permute-start(bf16[32,640]{1,0:T(8,128)(2,1)S(1)} %get-tuple-element.75), channel_id=1, source_target_pairs={{0,8},{4,12},{8,0},{12,4},{16,24},{20,28},{24,16},{28,20},{1,9},{5... | collective-permute-start | bytes 122888 | tf_op jit(solution)/shard_map/ppermute | solution.py:420
  66.3 0.9 %collective-permute-start.23 = (bf16[32,640]{1,0:T(8,128)(2,1)S(1)}, bf16[32,640]{1,0:T(8,128)(2,1)S(1)}, u32[]{:S(2)}, u32[]{:S(2)}) collective-permute-start(bf16[32,640]{1,0:T(8,128)(2,1)S(1)} %get-tuple-element.76), channel_id=1, source_target_pairs={{0,16},{4,20},{8,24},{12,28},{16,0},{20,4},{24,8},{28,12},{1,17},{... | collective-permute-start | bytes 122888 | tf_op jit(solution)/shard_map/ppermute | solution.py:420
  67.2 2.4 %collective-permute-start.24 = (bf16[32,640]{1,0:T(8,128)(2,1)S(1)}, bf16[32,640]{1,0:T(8,128)(2,1)S(1)}, u32[]{:S(2)}, u32[]{:S(2)}) collective-permute-start(bf16[32,640]{1,0:T(8,128)(2,1)S(1)} %get-tuple-element.77), channel_id=1, source_target_pairs={{0,24},{4,28},{8,16},{12,20},{16,8},{20,12},{24,0},{28,4},{1,25},{... | collective-permute-start | bytes 122888 | tf_op jit(solution)/shard_map/ppermute | solution.py:420
  69.6 1.6 %collective-permute-done.23.refs_1_ = bf16[32,640]{1,0:T(8,128)(2,1)S(1)} collective-permute-done((bf16[32,640]{1,0:T(8,128)(2,1)S(1)}, bf16[32,640]{1,0:T(8,128)(2,1)S(1)}, u32[]{:S(2)}, u32[]{:S(2)}) %collective-permute-start.23) | collective-permute-done | bytes 40992 | tf_op jit(solution)/shard_map/ppermute | solution.py:420
  71.2 1.8 %collective-permute-done.24.refs_2_ = bf16[32,640]{1,0:T(8,128)(2,1)S(1)} collective-permute-done((bf16[32,640]{1,0:T(8,128)(2,1)S(1)}, bf16[32,640]{1,0:T(8,128)(2,1)S(1)}, u32[]{:S(2)}, u32[]{:S(2)}) %collective-permute-start.24) | collective-permute-done | bytes 40992 | tf_op jit(solution)/shard_map/ppermute | solution.py:420
  73.1 1.6 %collective-permute-start.25 = (f32[32,512]{1,0:T(8,128)S(1)}, f32[32,512]{1,0:T(8,128)S(1)}, u32[]{:S(2)}, u32[]{:S(2)}) collective-permute-start(f32[32,512]{1,0:T(8,128)S(1)} %get-tuple-element.78), channel_id=1, source_target_pairs={{0,2},{1,3},{2,0},{3,1},{4,6},{5,7},{6,4},{7,5},{8,10},{9,11},{10,... | collective-permute-start | bytes 196616 | tf_op jit(solution)/shard_map/ppermute | solution.py:420
  74.7 1.9 %collective-permute-start.26 = (f32[32,128]{1,0:T(8,128)S(1)}, f32[32,128]{1,0:T(8,128)S(1)}, u32[]{:S(2)}, u32[]{:S(2)}) collective-permute-start(f32[32,128]{1,0:T(8,128)S(1)} %get-tuple-element.79), channel_id=1, source_target_pairs={{0,4},{4,0},{8,12},{12,8},{16,20},{20,16},{24,28},{28,24},{1,5},{5... | collective-permute-start | bytes 49160 | tf_op jit(solution)/shard_map/ppermute | solution.py:420
  76.6 1.9 %collective-permute-done.26 = f32[32,128]{1,0:T(8,128)S(1)} collective-permute-done((f32[32,128]{1,0:T(8,128)S(1)}, f32[32,128]{1,0:T(8,128)S(1)}, u32[]{:S(2)}, u32[]{:S(2)}) %collective-permute-start.26) | collective-permute-done | bytes 16416 | tf_op jit(solution)/shard_map/ppermute | solution.py:420
  78.6 0.8 collective-permute-start.30
  79.4 1.3 %collective-permute-start.29 = (f32[32,128]{1,0:T(8,128)S(1)}, f32[32,128]{1,0:T(8,128)S(1)}, u32[]{:S(2)}, u32[]{:S(2)}) collective-permute-start(f32[32,128]{1,0:T(8,128)S(1)} %add.62.refs_2_), channel_id=1, source_target_pairs={{0,2},{1,3},{2,0},{3,1},{4,6},{5,7},{6,4},{7,5},{8,10},{9,11},{10,... | collective-permute-start | bytes 49160 | tf_op jit(solution)/shard_map/ppermute | solution.py:420
  80.7 1.1 %collective-permute-done.30.refs_5_ = f32[32,128]{1,0:T(8,128)S(1)} collective-permute-done((f32[32,128]{1,0:T(8,128)S(1)}, f32[32,128]{1,0:T(8,128)S(1)}, u32[]{:S(2)}, u32[]{:S(2)}) %collective-permute-start.30) | collective-permute-done | bytes 16416 | tf_op jit(solution)/shard_map/ppermute | solution.py:420
  81.8 1.3 %collective-permute-done.29.refs_4_ = f32[32,128]{1,0:T(8,128)S(1)} collective-permute-done((f32[32,128]{1,0:T(8,128)S(1)}, f32[32,128]{1,0:T(8,128)S(1)}, u32[]{:S(2)}, u32[]{:S(2)}) %collective-permute-start.29) | collective-permute-done | bytes 16416 | tf_op jit(solution)/shard_map/ppermute | solution.py:420
  83.1 1.2 %final.1 = (f32[32,2048]{1,0:T(8,128)}, f32[32,2048]{1,0:T(8,128)}) custom-call(f32[32,2048]{1,0:T(8,128)S(1)} %copy-done, f32[2,40,512]{2,1,0:T(8,128)S(1)} %pad_maximum_fusion.1.s1_own, f32[2,40,512]{2,1,0:T(8,128)S(1)} %collective-permute-done.17.s1_got, f32[2,32,512]{2,1,0:T(8,128)S(1)} %pad_maximum_fusion.3.refs_0_, ...), custom_call_target="tpu_custom_call" | custom-call | tf_op jit(solution)/shard_map/final/pallas_call | solution.py:637
  (54 shorter events, 2.4 us)
Async XLA Ops:
  0.6 5.7 %collective-permute-start = (s32[8,6]{1,0:T(8,128)}, s32[8,6]{1,0:T(8,128)S(1)}, u32[]{:S(2)}, u32[]{:S(2)}) collective-permute-start(s32[8,6]{1,0:T(8,128)} %param.3), channel_id=1, source_target_pairs={{0,1},{1,0},{2,3},{3,2},{4,5},{5,4},{6,7},{7,6},{8,9},{9,8},{10,11... | collective-permute-start | bytes 584 | tf_op jit(solution)/shard_map/ppermute | solution.py:420
  1.1 5.3 %collective-permute-start.2 = (s32[8,6]{1,0:T(8,128)}, s32[8,6]{1,0:T(8,128)S(1)}, u32[]{:S(2)}, u32[]{:S(2)}) collective-permute-start(s32[8,6]{1,0:T(8,128)} %param.3), channel_id=1, source_target_pairs={{0,3},{1,2},{2,1},{3,0},{4,7},{5,6},{6,5},{7,4},{8,11},{9,10},{10,... | collective-permute-start | bytes 584 | tf_op jit(solution)/shard_map/ppermute | solution.py:420
  3.8 3.8 %collective-permute-start.1 = (s32[8,6]{1,0:T(8,128)}, s32[8,6]{1,0:T(8,128)S(1)}, u32[]{:S(2)}, u32[]{:S(2)}) collective-permute-start(s32[8,6]{1,0:T(8,128)} %param.3), channel_id=1, source_target_pairs={{0,2},{1,3},{2,0},{3,1},{4,6},{5,7},{6,4},{7,5},{8,10},{9,11},{10,... | collective-permute-start | bytes 584 | tf_op jit(solution)/shard_map/ppermute | solution.py:420
  7.9 5.7 %collective-permute-start.5 = (bf16[16,640]{1,0:T(8,128)(2,1)S(1)}, bf16[16,640]{1,0:T(8,128)(2,1)S(1)}, u32[]{:S(2)}, u32[]{:S(2)}) collective-permute-start(bf16[16,640]{1,0:T(8,128)(2,1)S(1)} %pad_maximum_fusion.5), channel_id=1, source_target_pairs={{0,24},{4,28},{8,16},{12,20},{16,8},{20,12},{24,0},{28,4},{1,25},{... | collective-permute-start | bytes 61448 | tf_op jit(solution)/shard_map/ppermute | solution.py:420
  11.6 4.7 %collective-permute-start.4 = (bf16[16,640]{1,0:T(8,128)(2,1)S(1)}, bf16[16,640]{1,0:T(8,128)(2,1)S(1)}, u32[]{:S(2)}, u32[]{:S(2)}) collective-permute-start(bf16[16,640]{1,0:T(8,128)(2,1)S(1)} %pad_maximum_fusion.5), channel_id=1, source_target_pairs={{0,16},{4,20},{8,24},{12,28},{16,0},{20,4},{24,8},{28,12},{1,17},{... | collective-permute-start | bytes 61448 | tf_op jit(solution)/shard_map/ppermute | solution.py:420
  11.6 4.7 %collective-permute-start.3 = (bf16[16,640]{1,0:T(8,128)(2,1)S(1)}, bf16[16,640]{1,0:T(8,128)(2,1)S(1)}, u32[]{:S(2)}, u32[]{:S(2)}) collective-permute-start(bf16[16,640]{1,0:T(8,128)(2,1)S(1)} %pad_maximum_fusion.5), channel_id=1, source_target_pairs={{0,8},{4,12},{8,0},{12,4},{16,24},{20,28},{24,16},{28,20},{1,9},{5... | collective-permute-start | bytes 61448 | tf_op jit(solution)/shard_map/ppermute | solution.py:420
  16.3 10.3 %collective-permute-start.6 = (bf16[4,16,640]{2,1,0:T(8,128)(2,1)S(1)}, bf16[4,16,640]{2,1,0:T(8,128)(2,1)S(1)}, u32[]{:S(2)}, u32[]{:S(2)}) collective-permute-start(bf16[4,16,640]{2,1,0:T(8,128)(2,1)S(1)} %pad_maximum_fusion.4.refs_1_), channel_id=1, source_target_pairs={{0,4},{4,0},{8,12},{12,8},{16,20},{20,16},{24,28},{28,24},{1,5},{5... | collective-permute-start | bytes 245768 | tf_op jit(solution)/shard_map/ppermute | solution.py:420
  17.8 8.8 %collective-permute-start.9 = (f32[32,512]{1,0:T(8,128)S(1)}, f32[32,512]{1,0:T(8,128)S(1)}, u32[]{:S(2)}, u32[]{:S(2)}) collective-permute-start(f32[32,512]{1,0:T(8,128)S(1)} %constant_dynamic-slice_fusion), channel_id=1, source_target_pairs={{0,24},{4,28},{8,16},{12,20},{16,8},{20,12},{24,0},{28,4},{1,25},{... | collective-permute-start | bytes 196616 | tf_op jit(solution)/shard_map/ppermute | solution.py:420
  19.3 7.3 %collective-permute-start.8 = (f32[32,512]{1,0:T(8,128)S(1)}, f32[32,512]{1,0:T(8,128)S(1)}, u32[]{:S(2)}, u32[]{:S(2)}) collective-permute-start(f32[32,512]{1,0:T(8,128)S(1)} %constant_dynamic-slice_fusion), channel_id=1, source_target_pairs={{0,16},{4,20},{8,24},{12,28},{16,0},{20,4},{24,8},{28,12},{1,17},{... | collective-permute-start | bytes 196616 | tf_op jit(solution)/shard_map/ppermute | solution.py:420
  19.8 6.8 %collective-permute-start.7 = (f32[32,512]{1,0:T(8,128)S(1)}, f32[32,512]{1,0:T(8,128)S(1)}, u32[]{:S(2)}, u32[]{:S(2)}) collective-permute-start(f32[32,512]{1,0:T(8,128)S(1)} %constant_dynamic-slice_fusion), channel_id=1, source_target_pairs={{0,8},{4,12},{8,0},{12,4},{16,24},{20,28},{24,16},{28,20},{1,9},{5... | collective-permute-start | bytes 196616 | tf_op jit(solution)/shard_map/ppermute | solution.py:420
  26.6 6.4 %collective-permute-start.10 = (f32[4,32,512]{2,1,0:T(8,128)S(1)}, f32[4,32,512]{2,1,0:T(8,128)S(1)}, u32[]{:S(2)}, u32[]{:S(2)}) collective-permute-start(f32[4,32,512]{2,1,0:T(8,128)S(1)} %pad_maximum_fusion.refs_2_.t_same), channel_id=1, source_target_pairs={{0,4},{4,0},{8,12},{12,8},{16,20},{20,16},{24,28},{28,24},{1,5},{5... | collective-permute-start | bytes 786440 | tf_op jit(solution)/shard_map/ppermute | solution.py:420
  27.2 27.1 %copy-start = (f32[32,2048]{1,0:T(8,128)S(1)}, f32[32,2048]{1,0:T(8,128)}, u32[]{:S(2)}) copy-start(f32[32,2048]{1,0:T(8,128)} %t_ref.5) | copy-start | bytes 786436
  33.1 5.5 %collective-permute-start.13 = (f32[16,256]{1,0:T(8,128)S(1)}, f32[16,256]{1,0:T(8,128)S(1)}, u32[]{:S(2)}, u32[]{:S(2)}) collective-permute-start(f32[16,256]{1,0:T(8,128)S(1)} %get-tuple-element.60), channel_id=1, source_target_pairs={{0,24},{4,28},{8,16},{12,20},{16,8},{20,12},{24,0},{28,4},{1,25},{... | collective-permute-start | bytes 49160 | tf_op jit(solution)/shard_map/ppermute | solution.py:420
  34.5 4.7 %collective-permute-start.12 = (f32[16,256]{1,0:T(8,128)S(1)}, f32[16,256]{1,0:T(8,128)S(1)}, u32[]{:S(2)}, u32[]{:S(2)}) collective-permute-start(f32[16,256]{1,0:T(8,128)S(1)} %get-tuple-element.60), channel_id=1, source_target_pairs={{0,16},{4,20},{8,24},{12,28},{16,0},{20,4},{24,8},{28,12},{1,17},{... | collective-permute-start | bytes 49160 | tf_op jit(solution)/shard_map/ppermute | solution.py:420
  35.1 4.3 %collective-permute-start.11 = (f32[16,256]{1,0:T(8,128)S(1)}, f32[16,256]{1,0:T(8,128)S(1)}, u32[]{:S(2)}, u32[]{:S(2)}) collective-permute-start(f32[16,256]{1,0:T(8,128)S(1)} %get-tuple-element.60), channel_id=1, source_target_pairs={{0,8},{4,12},{8,0},{12,4},{16,24},{20,28},{24,16},{28,20},{1,9},{5... | collective-permute-start | bytes 49160 | tf_op jit(solution)/shard_map/ppermute | solution.py:420
  39.4 3.8 %collective-permute-start.14 = (f32[16,256]{1,0:T(8,128)S(1)}, f32[16,256]{1,0:T(8,128)S(1)}, u32[]{:S(2)}, u32[]{:S(2)}) collective-permute-start(f32[16,256]{1,0:T(8,128)S(1)} %add_add_fusion), channel_id=1, source_target_pairs={{0,4},{4,0},{8,12},{12,8},{16,20},{20,16},{24,28},{28,24},{1,5},{5... | collective-permute-start | bytes 49160 | tf_op jit(solution)/shard_map/ppermute | solution.py:420
  46.8 1.4 %collective-permute-start.15 = (f32[2,32,512]{2,1,0:T(8,128)S(1)}, f32[2,32,512]{2,1,0:T(8,128)S(1)}, u32[]{:S(2)}, u32[]{:S(2)}) collective-permute-start(f32[2,32,512]{2,1,0:T(8,128)S(1)} %get-tuple-element.62), channel_id=1, source_target_pairs={{0,1},{1,0},{2,3},{3,2},{4,5},{5,4},{6,7},{7,6},{8,9},{9,8},{10,11... | collective-permute-start | bytes 393224 | tf_op jit(solution)/shard_map/ppermute | solution.py:420
  48.3 6.0 %collective-permute-start.16 = (f32[72,512]{1,0:T(8,128)S(1)}, f32[72,512]{1,0:T(8,128)S(1)}, u32[]{:S(2)}, u32[]{:S(2)}) collective-permute-start(f32[72,512]{1,0:T(8,128)S(1)} %pad_maximum_fusion.2), channel_id=1, source_target_pairs={{0,2},{1,3},{2,0},{3,1},{4,6},{5,7},{6,4},{7,5},{8,10},{9,11},{10,... | collective-permute-start | bytes 442376 | tf_op jit(solution)/shard_map/ppermute | solution.py:420
  54.3 1.5 %collective-permute-start.17 = (f32[2,40,512]{2,1,0:T(8,128)S(1)}, f32[2,40,512]{2,1,0:T(8,128)S(1)}, u32[]{:S(2)}, u32[]{:S(2)}) collective-permute-start(f32[2,40,512]{2,1,0:T(8,128)S(1)} %pad_maximum_fusion.1.s1_own), channel_id=1, source_target_pairs={{0,1},{1,0},{2,3},{3,2},{4,5},{5,4},{6,7},{7,6},{8,9},{9,8},{10,11... | collective-permute-start | bytes 491528 | tf_op jit(solution)/shard_map/ppermute | solution.py:420
  57.6 7.4 %collective-permute-start.18 = (bf16[4,32,512]{2,1,0:T(8,128)(2,1)S(1)}, bf16[4,32,512]{2,1,0:T(8,128)(2,1)S(1)}, u32[]{:S(2)}, u32[]{:S(2)}) collective-permute-start(bf16[4,32,512]{2,1,0:T(8,128)(2,1)S(1)} %second.3), channel_id=1, source_target_pairs={{0,4},{4,0},{8,12},{12,8},{16,20},{20,16},{24,28},{28,24},{1,5},{5... | collective-permute-start | bytes 393224 | tf_op jit(solution)/shard_map/ppermute | solution.py:420
  57.7 6.1 %collective-permute-start.21 = (bf16[32,512]{1,0:T(8,128)(2,1)S(1)}, bf16[32,512]{1,0:T(8,128)(2,1)S(1)}, u32[]{:S(2)}, u32[]{:S(2)}) collective-permute-start(bf16[32,512]{1,0:T(8,128)(2,1)S(1)} %fusion.2.refs_0_), channel_id=1, source_target_pairs={{0,24},{4,28},{8,16},{12,20},{16,8},{20,12},{24,0},{28,4},{1,25},{... | collective-permute-start | bytes 98312 | tf_op jit(solution)/shard_map/ppermute | solution.py:420
  59.6 5.0 %collective-permute-start.20 = (bf16[32,512]{1,0:T(8,128)(2,1)S(1)}, bf16[32,512]{1,0:T(8,128)(2,1)S(1)}, u32[]{:S(2)}, u32[]{:S(2)}) collective-permute-start(bf16[32,512]{1,0:T(8,128)(2,1)S(1)} %fusion.2.refs_0_), channel_id=1, source_target_pairs={{0,16},{4,20},{8,24},{12,28},{16,0},{20,4},{24,8},{28,12},{1,17},{... | collective-permute-start | bytes 98312 | tf_op jit(solution)/shard_map/ppermute | solution.py:420
  61.0 4.0 %collective-permute-start.19 = (bf16[32,512]{1,0:T(8,128)(2,1)S(1)}, bf16[32,512]{1,0:T(8,128)(2,1)S(1)}, u32[]{:S(2)}, u32[]{:S(2)}) collective-permute-start(bf16[32,512]{1,0:T(8,128)(2,1)S(1)} %fusion.2.refs_0_), channel_id=1, source_target_pairs={{0,8},{4,12},{8,0},{12,4},{16,24},{20,28},{24,16},{28,20},{1,9},{5... | collective-permute-start | bytes 98312 | tf_op jit(solution)/shard_map/ppermute | solution.py:420
  65.2 4.5 %collective-permute-start.22 = (bf16[32,640]{1,0:T(8,128)(2,1)S(1)}, bf16[32,640]{1,0:T(8,128)(2,1)S(1)}, u32[]{:S(2)}, u32[]{:S(2)}) collective-permute-start(bf16[32,640]{1,0:T(8,128)(2,1)S(1)} %get-tuple-element.75), channel_id=1, source_target_pairs={{0,8},{4,12},{8,0},{12,4},{16,24},{20,28},{24,16},{28,20},{1,9},{5... | collective-permute-start | bytes 122888 | tf_op jit(solution)/shard_map/ppermute | solution.py:420
  66.3 4.9 %collective-permute-start.23 = (bf16[32,640]{1,0:T(8,128)(2,1)S(1)}, bf16[32,640]{1,0:T(8,128)(2,1)S(1)}, u32[]{:S(2)}, u32[]{:S(2)}) collective-permute-start(bf16[32,640]{1,0:T(8,128)(2,1)S(1)} %get-tuple-element.76), channel_id=1, source_target_pairs={{0,16},{4,20},{8,24},{12,28},{16,0},{20,4},{24,8},{28,12},{1,17},{... | collective-permute-start | bytes 122888 | tf_op jit(solution)/shard_map/ppermute | solution.py:420
  67.2 5.8 %collective-permute-start.24 = (bf16[32,640]{1,0:T(8,128)(2,1)S(1)}, bf16[32,640]{1,0:T(8,128)(2,1)S(1)}, u32[]{:S(2)}, u32[]{:S(2)}) collective-permute-start(bf16[32,640]{1,0:T(8,128)(2,1)S(1)} %get-tuple-element.77), channel_id=1, source_target_pairs={{0,24},{4,28},{8,16},{12,20},{16,8},{20,12},{24,0},{28,4},{1,25},{... | collective-permute-start | bytes 122888 | tf_op jit(solution)/shard_map/ppermute | solution.py:420
  73.1 5.4 %collective-permute-start.25 = (f32[32,512]{1,0:T(8,128)S(1)}, f32[32,512]{1,0:T(8,128)S(1)}, u32[]{:S(2)}, u32[]{:S(2)}) collective-permute-start(f32[32,512]{1,0:T(8,128)S(1)} %get-tuple-element.78), channel_id=1, source_target_pairs={{0,2},{1,3},{2,0},{3,1},{4,6},{5,7},{6,4},{7,5},{8,10},{9,11},{10,... | collective-permute-start | bytes 196616 | tf_op jit(solution)/shard_map/ppermute | solution.py:420
  74.7 3.7 %collective-permute-start.26 = (f32[32,128]{1,0:T(8,128)S(1)}, f32[32,128]{1,0:T(8,128)S(1)}, u32[]{:S(2)}, u32[]{:S(2)}) collective-permute-start(f32[32,128]{1,0:T(8,128)S(1)} %get-tuple-element.79), channel_id=1, source_target_pairs={{0,4},{4,0},{8,12},{12,8},{16,20},{20,16},{24,28},{28,24},{1,5},{5... | collective-permute-start | bytes 49160 | tf_op jit(solution)/shard_map/ppermute | solution.py:420
  78.5 4.6 %collective-permute-start.27 = (f32[2,32,512]{2,1,0:T(8,128)S(1)}, f32[2,32,512]{2,1,0:T(8,128)S(1)}, u32[]{:S(2)}, u32[]{:S(2)}) collective-permute-start(f32[2,32,512]{2,1,0:T(8,128)S(1)} %pad_maximum_fusion.3.refs_0_), channel_id=1, source_target_pairs={{0,1},{1,0},{2,3},{3,2},{4,5},{5,4},{6,7},{7,6},{8,9},{9,8},{10,11... | collective-permute-start | bytes 393224 | tf_op jit(solution)/shard_map/ppermute | solution.py:420
  78.6 3.2 %collective-permute-start.30 = (f32[32,128]{1,0:T(8,128)S(1)}, f32[32,128]{1,0:T(8,128)S(1)}, u32[]{:S(2)}, u32[]{:S(2)}) collective-permute-start(f32[32,128]{1,0:T(8,128)S(1)} %add.62.refs_2_), channel_id=1, source_target_pairs={{0,3},{1,2},{2,1},{3,0},{4,7},{5,6},{6,5},{7,4},{8,11},{9,10},{10,... | collective-permute-start | bytes 49160 | tf_op jit(solution)/shard_map/ppermute | solution.py:420
  79.4 3.7 %collective-permute-start.29 = (f32[32,128]{1,0:T(8,128)S(1)}, f32[32,128]{1,0:T(8,128)S(1)}, u32[]{:S(2)}, u32[]{:S(2)}) collective-permute-start(f32[32,128]{1,0:T(8,128)S(1)} %add.62.refs_2_), channel_id=1, source_target_pairs={{0,2},{1,3},{2,0},{3,1},{4,6},{5,7},{6,4},{7,5},{8,10},{9,11},{10,... | collective-permute-start | bytes 49160 | tf_op jit(solution)/shard_map/ppermute | solution.py:420
  80.7 2.4 %collective-permute-start.28 = (f32[32,128]{1,0:T(8,128)S(1)}, f32[32,128]{1,0:T(8,128)S(1)}, u32[]{:S(2)}, u32[]{:S(2)}) collective-permute-start(f32[32,128]{1,0:T(8,128)S(1)} %add.62.refs_2_), channel_id=1, source_target_pairs={{0,1},{1,0},{2,3},{3,2},{4,5},{5,4},{6,7},{7,6},{8,9},{9,8},{10,11... | collective-permute-start | bytes 49160 | tf_op jit(solution)/shard_map/ppermute | solution.py:420

commit v12 on v11

--- a/solution.py
+++ b/solution.py
@@ -369,7 +369,7 @@
 
 
 def product_kernel(own_z, own_dots, s1_own, *refs):
-    got, grown_ref, dot_ref = refs[:3], refs[3], refs[4]
+    got, grown_ref, dot_ref = refs[2::-1], refs[3], refs[4]
     outputs, own_len = grown_ref.shape
     z = own_z[...]
     for ref in got:
@@ -384,8 +384,8 @@
 
 
 def final_kernel(t_ref, s1_own, s1_got, *refs):
-    grown, all_dots = pieces_of(refs[0], refs[1]), refs[2:6]
-    sol_hbm, res_hbm, sol_ref, res_ref, sems = refs[6:]
+    grown, all_dots = pieces_of(refs[0], refs[1]), refs[2:4]
+    sol_hbm, res_hbm, sol_ref, res_ref, sems = refs[4:]
     s1s = pieces_of(s1_own, s1_got)
     outputs, own_len = grown[0].shape
     place = position()
@@ -418,6 +418,16 @@
 def swap(x, axis, d):
     size = lax.axis_size(axis)
     return lax.ppermute(x, axis, [(i, i ^ d) for i in range(size)])
+
+
+def both_swap(x, row_d, col_d):
+    n_rows, n_cols = lax.axis_size("rows"), lax.axis_size("cols")
+    pairs = [
+        (r * n_cols + c, (r ^ row_d) * n_cols + (c ^ col_d))
+        for r in range(n_rows)
+        for c in range(n_cols)
+    ]
+    return lax.ppermute(x, ("rows", "cols"), pairs)
 
 
 def along_z(x):
@@ -472,7 +482,8 @@
 
     def total_rows(x):
         if direct_rows:
-            return pair_sum(across_x(pair_sum(along_z(x))))
+            near = pair_sum([x] + [swap(x, "rows", d) for d in range(1, 4)])
+            return near + swap(near, "rows", 4)
         return lax.psum(x, "rows")
 
     lists = direct_cols(block_list)
@@ -515,9 +526,9 @@
             compiler_params=limit,
             input_output_aliases={} if first else {4: 0},
             cost_estimate=pl.CostEstimate(
-                flops=2 * 2 * dim * bound * block_len * block_len,
-                bytes_accessed=2 * bound * block_len * block_len,
-                transcendentals=bound * block_len * block_len,
+                flops=10 * 2 * 2 * dim * bound * block_len * block_len,
+                bytes_accessed=10 * 2 * bound * block_len * block_len,
+                transcendentals=10 * bound * block_len * block_len,
             ),
             name="build",
         )(direct, *operands)
@@ -611,7 +622,7 @@
             compiler_params=limit,
             name="meet",
         )(z2_same, z2_other, t_pieces[0], inv, s1_own, *gs)
-        got = [swap(sends[n], "rows", 2 * n + 2) for n in (2, 1, 0)][::-1]
+        got = [swap(sends[n], "rows", 2 * n + 2) for n in (2, 1, 0)]
         grown, dots = pl.pallas_call(
             product_kernel,
             out_shape=(shape(outputs, own_len), shape(outputs, LANES)),
@@ -620,7 +631,8 @@
             compiler_params=limit,
             name="products",
         )(own_z, own_dots, s1_own, *got)
-        dots = pair_sum(across_x(dots))
+        far = both_swap(dots, 1, 2)
+        dots = pair_sum([dots, swap(dots, "rows", 1), swap(dots, "cols", 2), far])
     else:
         z2 = lax.psum_scatter(second(0, F32), "rows", scatter_dimension=0)
         grown = z2 * tail[:1]
@@ -629,15 +641,16 @@
         dots = [(own_t, own_t), (own_t, own_s1), (own_s1, own_s1), (own_t, s2), (own_s1, s2)]
         dots = jnp.stack([jnp.sum(x * y, axis=1) for x, y in dots], axis=1)
         dots = lax.psum(jnp.pad(dots, ((0, 0), (0, LANES - N_DOTS))), "rows")
+        dots = dots + swap(dots, "cols", 2)
     grown = jnp.stack([grown, swap(grown, "cols", 2)])
     grown, dots = lax.optimization_barrier((grown, dots))
-    ends = (s1_own, s1_got, grown, swap(grown, "cols", 1), *direct_cols(dots))
+    ends = (s1_own, s1_got, grown, swap(grown, "cols", 1), dots, swap(dots, "cols", 1))
     ends = [pltpu.with_memory_space_constraint(x, pltpu.VMEM) for x in ends]
 
     return pl.pallas_call(
         final_kernel,
         out_shape=(shape(outputs, npoints), shape(outputs, npoints)),
-        in_specs=[VMEM] * 9,
+        in_specs=[VMEM] * 7,
         out_specs=(HBM, HBM),
         scratch_shapes=[
             pltpu.VMEM((4, outputs, own_len), F32),

time: 84.5 us -> 81.8 us (0.968)
  waiting for transfers between devices: 27.8 us -> 24.4 us
  starting transfers between devices: 35.2 us -> 37.1 us
  Pallas kernels: 17.2 us -> 16.2 us
    ppermute x31 -> x30, waiting for transfers between devices: 27.8 us -> 23.4 us  [swap(): return lax.ppermute(x, axis, [(i, i ^ d) for i in range(size)])]
    ppermute x31 -> x30, starting transfers between devices: 35.2 us -> 36.3 us  [swap(): return lax.ppermute(x, axis, [(i, i ^ d) for i in range(size)])]
    ppermute x0 -> x1, waiting for transfers between devices: none -> 0.93 us  [both_swap(): return lax.ppermute(x, ('rows', 'cols'), pairs)]
  transfers between devices with their start and end apart: 31 -> 31, of which waited for: 18 -> 16; matrix products, arithmetic and copies ran while one was open for 3% -> 3% of each run, Pallas kernels for 12% -> 12%
where the time goes in v12:
time: 81.8 us
  starting transfers between devices  37.1 us (45%)
  waiting for transfers between devices  24.4 us (30%)
  Pallas kernels  16.2 us (20%)
  local copies, waits for them, and re-layouts  2.74 us (3%)
  between operations  0.86 us (1%)
    ppermute x30, starting transfers between devices, swap(): return lax.ppermute(x, axis, [(i, i ^ d) for i in range(size)])  36.3 us
    ppermute x30, waiting for transfers between devices, swap(): return lax.ppermute(x, axis, [(i, i ^ d) for i in range(size)])  23.4 us
    pallas_call x2, Pallas kernels, build(): pl.pallas_call(functools.partial(build_kernel, cfg, part), out_shape=out,...  8.23 us
    pallas_call x1, Pallas kernels, local(): pl.pallas_call(functools.partial(first_kernel, cfg), out_shape=[shape(out...  3.35 us
    pallas_call x2, Pallas kernels, second(): pl.pallas_call(functools.partial(second_kernel, cfg, part), out_shape=sha...  3.2 us
  transfers between devices with their start and end apart: 31, of which 16 were waited for; matrix products, arithmetic and copies ran while one was open for 3% of the time, Pallas kernels for 12%

profile of v12, /device:TPU:0, one launch (start us, length us, event | category | flops | bytes accessed | tf_op | source)
XLA Modules:
  0.0 81.8 jit_solution(15574300687521958232)
XLA Ops:
  0.6 0.5 collective-permute-start
  1.1 2.6 %collective-permute-start.2 = (s32[8,6]{1,0:T(8,128)}, s32[8,6]{1,0:T(8,128)S(1)}, u32[]{:S(2)}, u32[]{:S(2)}) collective-permute-start(s32[8,6]{1,0:T(8,128)} %param.3), channel_id=1, source_target_pairs={{0,3},{1,2},{2,1},{3,0},{4,7},{5,6},{6,5},{7,4},{8,11},{9,10},{10,... | collective-permute-start | bytes 584 | tf_op jit(solution)/shard_map/ppermute | solution.py:420
  3.8 0.8 %copy.6 = s32[8,6]{0,1:T(8,128)S(1)} copy(s32[8,6]{1,0:T(8,128)} %param.3) | data formatting | bytes 384 | tf_op args[0]
  4.7 0.7 constant_dynamic-slice_fusion.1
  5.5 0.8 %constant_dynamic-slice_fusion = f32[32,512]{1,0:T(8,128)S(1)} fusion(f32[32,2048]{1,0:T(8,128)} %t_ref.5, s32[]{:T(128)S(6)} %select_n.7), kind=kLoop, calls=%fused_computation.34 | loop fusion | bytes 131076 | tf_op jit(solution)/shard_map/dynamic_slice | solution.py:481
  6.6 1.0 %collective-permute-done.1 = s32[8,6]{1,0:T(8,128)S(1)} collective-permute-done((s32[8,6]{1,0:T(8,128)}, s32[8,6]{1,0:T(8,128)S(1)}, u32[]{:S(2)}, u32[]{:S(2)}) %collective-permute-start.1) | collective-permute-done | bytes 224 | tf_op jit(solution)/shard_map/ppermute | solution.py:420
  7.9 3.7 %collective-permute-start.5 = (bf16[16,640]{1,0:T(8,128)(2,1)S(1)}, bf16[16,640]{1,0:T(8,128)(2,1)S(1)}, u32[]{:S(2)}, u32[]{:S(2)}) collective-permute-start(bf16[16,640]{1,0:T(8,128)(2,1)S(1)} %pad_maximum_fusion.5), channel_id=1, source_target_pairs={{0,24},{4,28},{8,16},{12,20},{16,8},{20,12},{24,0},{28,4},{1,25},{... | collective-permute-start | bytes 61448 | tf_op jit(solution)/shard_map/ppermute | solution.py:420
  11.6 0.8 collective-permute-start.3
  12.3 3.6 %collective-permute-start.9 = (f32[32,512]{1,0:T(8,128)S(1)}, f32[32,512]{1,0:T(8,128)S(1)}, u32[]{:S(2)}, u32[]{:S(2)}) collective-permute-start(f32[32,512]{1,0:T(8,128)S(1)} %constant_dynamic-slice_fusion), channel_id=1, source_target_pairs={{0,24},{4,28},{8,16},{12,20},{16,8},{20,12},{24,0},{28,4},{1,25},{... | collective-permute-start | bytes 196616 | tf_op jit(solution)/shard_map/ppermute | solution.py:420
  15.9 0.8 collective-permute-start.7
  16.8 1.6 %collective-permute-start.6 = (bf16[4,16,640]{2,1,0:T(8,128)(2,1)S(1)}, bf16[4,16,640]{2,1,0:T(8,128)(2,1)S(1)}, u32[]{:S(2)}, u32[]{:S(2)}) collective-permute-start(bf16[4,16,640]{2,1,0:T(8,128)(2,1)S(1)} %pad_maximum_fusion.4.refs_1_), channel_id=1, source_target_pairs={{0,4},{4,0},{8,12},{12,8},{16,20},{20,16},{24,28},{28,24},{1,5},{5... | collective-permute-start | bytes 245768 | tf_op jit(solution)/shard_map/ppermute | solution.py:420
  18.3 4.4 %build.2 = (bf16[32,4,256,256]{3,2,1,0:T(8,128)(2,1)S(1)}, s32[1,128]{1,0:T(1,128)S(1)}, f32[8,256]{1,0:T(8,128)S(1)}, bf16[8,256,32]{2,1,0:T(8,128)(2,1)S(1)}) custom-call(s32[8,64]{1,0:T(8,128)S(1)} %add_add_fusion.2.direct_v, bf16[16,2048]{1,0:T(8,128)(2,1)} %refs_0_.1, bf16[4,16,640]{2,1,0:T(8,128)(2,1)S(1)} %pad_maximum_fusion.4.refs_1_), custom_call_target="tpu_custom_call" | custom-call | flops 2684354560 | bytes 83886080 | tf_op jit(solution)/shard_map/build/pallas_call | solution.py:506
  22.8 0.6 collective-permute-start.10
  23.4 3.9 %build.3 = (bf16[32,4,256,256]{3,2,1,0:T(8,128)(2,1)S(1)}, s32[1,128]{1,0:T(1,128)S(1)}, f32[16,256]{1,0:T(8,128)S(1)}) custom-call(s32[8,64]{1,0:T(8,128)S(1)} %add_add_fusion.2.direct_v, bf16[8,256,32]{2,1,0:T(8,128)(2,1)S(1)} %get-tuple-element.43.refs_0_, f32[8,256]{1,0:T(8,128)S(1)} %get-tuple-element.46.refs_1_, ...), custom_call_target="tpu_custom_call", output_to_operand_aliasing={{0}: (4, {})} | custom-call | flops 2684354560 | bytes 83886080 | tf_op jit(solution)/shard_map/build/pallas_call | solution.py:506
  27.3 1.9 %collective-permute-done.10.refs_3_ = f32[4,32,512]{2,1,0:T(8,128)S(1)} collective-permute-done((f32[4,32,512]{2,1,0:T(8,128)S(1)}, f32[4,32,512]{2,1,0:T(8,128)S(1)}, u32[]{:S(2)}, u32[]{:S(2)}) %collective-permute-start.10) | collective-permute-done | bytes 262176 | tf_op jit(solution)/shard_map/ppermute | solution.py:420
  29.2 0.8 %collective-permute-start.13 = (f32[16,256]{1,0:T(8,128)S(1)}, f32[16,256]{1,0:T(8,128)S(1)}, u32[]{:S(2)}, u32[]{:S(2)}) collective-permute-start(f32[16,256]{1,0:T(8,128)S(1)} %get-tuple-element.60), channel_id=1, source_target_pairs={{0,12},{4,8},{8,4},{12,0},{16,28},{20,24},{24,20},{28,16},{1,13},{... | collective-permute-start | bytes 49160 | tf_op jit(solution)/shard_map/ppermute | solution.py:420
  30.0 1.2 %collective-permute-start.12 = (f32[16,256]{1,0:T(8,128)S(1)}, f32[16,256]{1,0:T(8,128)S(1)}, u32[]{:S(2)}, u32[]{:S(2)}) collective-permute-start(f32[16,256]{1,0:T(8,128)S(1)} %get-tuple-element.60), channel_id=1, source_target_pairs={{0,8},{4,12},{8,0},{12,4},{16,24},{20,28},{24,16},{28,20},{1,9},{5... | collective-permute-start | bytes 49160 | tf_op jit(solution)/shard_map/ppermute | solution.py:420
  31.2 1.5 %collective-permute-start.11 = (f32[16,256]{1,0:T(8,128)S(1)}, f32[16,256]{1,0:T(8,128)S(1)}, u32[]{:S(2)}, u32[]{:S(2)}) collective-permute-start(f32[16,256]{1,0:T(8,128)S(1)} %get-tuple-element.60), channel_id=1, source_target_pairs={{0,4},{4,0},{8,12},{12,8},{16,20},{20,16},{24,28},{28,24},{1,5},{5... | collective-permute-start | bytes 49160 | tf_op jit(solution)/shard_map/ppermute | solution.py:420
  32.7 1.1 %collective-permute-done.13 = f32[16,256]{1,0:T(8,128)S(1)} collective-permute-done((f32[16,256]{1,0:T(8,128)S(1)}, f32[16,256]{1,0:T(8,128)S(1)}, u32[]{:S(2)}, u32[]{:S(2)}) %collective-permute-start.13) | collective-permute-done | bytes 16416 | tf_op jit(solution)/shard_map/ppermute | solution.py:420
  33.8 1.1 %collective-permute-done.11 = f32[16,256]{1,0:T(8,128)S(1)} collective-permute-done((f32[16,256]{1,0:T(8,128)S(1)}, f32[16,256]{1,0:T(8,128)S(1)}, u32[]{:S(2)}, u32[]{:S(2)}) %collective-permute-start.11) | collective-permute-done | bytes 16416 | tf_op jit(solution)/shard_map/ppermute | solution.py:420
  34.9 2.9 %collective-permute-start.14 = (f32[16,256]{1,0:T(8,128)S(1)}, f32[16,256]{1,0:T(8,128)S(1)}, u32[]{:S(2)}, u32[]{:S(2)}) collective-permute-start(f32[16,256]{1,0:T(8,128)S(1)} %add_add_fusion.1), channel_id=1, source_target_pairs={{0,16},{4,20},{8,24},{12,28},{16,0},{20,4},{24,8},{28,12},{1,17},{... | collective-permute-start | bytes 49160 | tf_op jit(solution)/shard_map/ppermute | solution.py:420
  37.9 1.8 %collective-permute-done.14 = f32[16,256]{1,0:T(8,128)S(1)} collective-permute-done((f32[16,256]{1,0:T(8,128)S(1)}, f32[16,256]{1,0:T(8,128)S(1)}, u32[]{:S(2)}, u32[]{:S(2)}) %collective-permute-start.14) | collective-permute-done | bytes 16416 | tf_op jit(solution)/shard_map/ppermute | solution.py:420
  39.7 3.4 %first.1 = (f32[32,512]{1,0:T(8,128)S(1)}, f32[32,512]{1,0:T(8,128)S(1)}, f32[2,32,512]{2,1,0:T(8,128)S(1)}, f32[8,512]{1,0:T(8,128)S(1)}) custom-call(bf16[32,4,256,256]{3,2,1,0:T(8,128)(2,1)S(1)} %get-tuple-element.54.k_mat, s32[1,128]{1,0:T(1,128)S(1)} %get-tuple-element.55.refs_0_.list_v, s32[1,128]{1,0:T(1,128)S(1)} %get-tuple-element.56.refs_1_.list_v, ...), custom_call_target="tpu_custom_call" | custom-call | flops 536870912 | bytes 8388608 | tf_op jit(solution)/shard_map/first/pallas_call | solution.py:563
  43.1 1.3 %collective-permute-done.15 = f32[2,32,512]{2,1,0:T(8,128)S(1)} collective-permute-done((f32[2,32,512]{2,1,0:T(8,128)S(1)}, f32[2,32,512]{2,1,0:T(8,128)S(1)}, u32[]{:S(2)}, u32[]{:S(2)}) %collective-permute-start.15) | collective-permute-done | bytes 131104 | tf_op jit(solution)/shard_map/ppermute | solution.py:420
  44.5 1.1 %collective-permute-start.16 = (f32[72,512]{1,0:T(8,128)S(1)}, f32[72,512]{1,0:T(8,128)S(1)}, u32[]{:S(2)}, u32[]{:S(2)}) collective-permute-start(f32[72,512]{1,0:T(8,128)S(1)} %pad_maximum_fusion.2), channel_id=1, source_target_pairs={{0,2},{1,3},{2,0},{3,1},{4,6},{5,7},{6,4},{7,5},{8,10},{9,11},{10,... | collective-permute-start | bytes 442376 | tf_op jit(solution)/shard_map/ppermute | solution.py:420
  45.6 4.9 %collective-permute-done.16 = f32[72,512]{1,0:T(8,128)S(1)} collective-permute-done((f32[72,512]{1,0:T(8,128)S(1)}, f32[72,512]{1,0:T(8,128)S(1)}, u32[]{:S(2)}, u32[]{:S(2)}) %collective-permute-start.16) | collective-permute-done | bytes 147488 | tf_op jit(solution)/shard_map/ppermute | solution.py:420
  50.6 1.3 %collective-permute-done.17.s1_got = f32[2,40,512]{2,1,0:T(8,128)S(1)} collective-permute-done((f32[2,40,512]{2,1,0:T(8,128)S(1)}, f32[2,40,512]{2,1,0:T(8,128)S(1)}, u32[]{:S(2)}, u32[]{:S(2)}) %collective-permute-start.17) | collective-permute-done | bytes 163872 | tf_op jit(solution)/shard_map/ppermute | solution.py:420
  52.0 1.6 %second.3 = bf16[4,32,512]{2,1,0:T(8,128)(2,1)S(1)} custom-call(bf16[32,4,256,256]{3,2,1,0:T(8,128)(2,1)S(1)} %get-tuple-element.54.k_mat, s32[1,128]{1,0:T(1,128)S(1)} %get-tuple-element.56.refs_1_.list_v, f32[32,2048]{1,0:T(8,128)S(1)} %copy-done, f32[2,40,512]{2,1,0:T(8,128)S(1)} %pad_maximum_fusion.1.s1_own, f32[2,40,512]{2,1,0:T(8,128)S(1)} %collective-permute-done.17.s1_got), custom_call_target="tpu_custom_call" | custom-call | flops 268435456 | bytes 4194304 | tf_op jit(solution)/shard_map/second/pallas_call | solution.py:592
  53.6 1.5 %collective-permute-start.18 = (bf16[4,32,512]{2,1,0:T(8,128)(2,1)S(1)}, bf16[4,32,512]{2,1,0:T(8,128)(2,1)S(1)}, u32[]{:S(2)}, u32[]{:S(2)}) collective-permute-start(bf16[4,32,512]{2,1,0:T(8,128)(2,1)S(1)} %second.3), channel_id=1, source_target_pairs={{0,4},{4,0},{8,12},{12,8},{16,20},{20,16},{24,28},{28,24},{1,5},{5... | collective-permute-start | bytes 393224 | tf_op jit(solution)/shard_map/ppermute | solution.py:420
  55.1 4.3 %collective-permute-start.21 = (bf16[32,512]{1,0:T(8,128)(2,1)S(1)}, bf16[32,512]{1,0:T(8,128)(2,1)S(1)}, u32[]{:S(2)}, u32[]{:S(2)}) collective-permute-start(bf16[32,512]{1,0:T(8,128)(2,1)S(1)} %fusion.2.refs_0_), channel_id=1, source_target_pairs={{0,24},{4,28},{8,16},{12,20},{16,8},{20,12},{24,0},{28,4},{1,25},{... | collective-permute-start | bytes 98312 | tf_op jit(solution)/shard_map/ppermute | solution.py:420
  59.4 0.6 collective-permute-start.19
  60.0 1.6 %second.2.z_same = f32[4,32,512]{2,1,0:T(8,128)S(1)} custom-call(bf16[32,4,256,256]{3,2,1,0:T(8,128)(2,1)S(1)} %get-tuple-element.54.k_mat, s32[1,128]{1,0:T(1,128)S(1)} %get-tuple-element.55.refs_0_.list_v, f32[32,2048]{1,0:T(8,128)S(1)} %copy-done, f32[2,40,512]{2,1,0:T(8,128)S(1)} %pad_maximum_fusion.1.s1_own, ...), custom_call_target="tpu_custom_call" | custom-call | flops 268435456 | bytes 4194304 | tf_op jit(solution)/shard_map/second/pallas_call | solution.py:592
  61.6 2.6 %collective-permute-done.20.refs_2_ = bf16[32,512]{1,0:T(8,128)(2,1)S(1)} collective-permute-done((bf16[32,512]{1,0:T(8,128)(2,1)S(1)}, bf16[32,512]{1,0:T(8,128)(2,1)S(1)}, u32[]{:S(2)}, u32[]{:S(2)}) %collective-permute-start.20) | collective-permute-done | bytes 32800 | tf_op jit(solution)/shard_map/ppermute | solution.py:420
  64.4 1.5 %collective-permute-start.22 = (bf16[32,640]{1,0:T(8,128)(2,1)S(1)}, bf16[32,640]{1,0:T(8,128)(2,1)S(1)}, u32[]{:S(2)}, u32[]{:S(2)}) collective-permute-start(bf16[32,640]{1,0:T(8,128)(2,1)S(1)} %get-tuple-element.75), channel_id=1, source_target_pairs={{0,24},{4,28},{8,16},{12,20},{16,8},{20,12},{24,0},{28,4},{1,25},{... | collective-permute-start | bytes 122888 | tf_op jit(solution)/shard_map/ppermute | solution.py:420
  66.0 0.6 collective-permute-start.23
  66.6 2.3 %collective-permute-start.24 = (bf16[32,640]{1,0:T(8,128)(2,1)S(1)}, bf16[32,640]{1,0:T(8,128)(2,1)S(1)}, u32[]{:S(2)}, u32[]{:S(2)}) collective-permute-start(bf16[32,640]{1,0:T(8,128)(2,1)S(1)} %get-tuple-element.77), channel_id=1, source_target_pairs={{0,8},{4,12},{8,0},{12,4},{16,24},{20,28},{24,16},{28,20},{1,9},{5... | collective-permute-start | bytes 122888 | tf_op jit(solution)/shard_map/ppermute | solution.py:420
  68.9 1.4 %collective-permute-done.22.refs_0_ = bf16[32,640]{1,0:T(8,128)(2,1)S(1)} collective-permute-done((bf16[32,640]{1,0:T(8,128)(2,1)S(1)}, bf16[32,640]{1,0:T(8,128)(2,1)S(1)}, u32[]{:S(2)}, u32[]{:S(2)}) %collective-permute-start.22) | collective-permute-done | bytes 40992 | tf_op jit(solution)/shard_map/ppermute | solution.py:420
  70.3 0.6 collective-permute-done.23.refs_1_
  70.9 0.4 collective-permute-done.24.refs_2_
  71.4 0.8 collective-permute-start.28
  72.2 0.8 %collective-permute-start.27 = (f32[32,128]{1,0:T(8,128)S(1)}, f32[32,128]{1,0:T(8,128)S(1)}, u32[]{:S(2)}, u32[]{:S(2)}) collective-permute-start(f32[32,128]{1,0:T(8,128)S(1)} %get-tuple-element.79), channel_id=1, source_target_pairs={{0,2},{1,3},{2,0},{3,1},{4,6},{5,7},{6,4},{7,5},{8,10},{9,11},{10,... | collective-permute-start | bytes 49160 | tf_op jit(solution)/shard_map/ppermute | solution.py:420
  73.0 1.9 %collective-permute-start.26 = (f32[32,128]{1,0:T(8,128)S(1)}, f32[32,128]{1,0:T(8,128)S(1)}, u32[]{:S(2)}, u32[]{:S(2)}) collective-permute-start(f32[32,128]{1,0:T(8,128)S(1)} %get-tuple-element.79), channel_id=1, source_target_pairs={{0,4},{4,0},{8,12},{12,8},{16,20},{20,16},{24,28},{28,24},{1,5},{5... | collective-permute-start | bytes 49160 | tf_op jit(solution)/shard_map/ppermute | solution.py:420
  75.2 0.9 %collective-permute-done.28 = f32[32,128]{1,0:T(8,128)S(1)} collective-permute-done((f32[32,128]{1,0:T(8,128)S(1)}, f32[32,128]{1,0:T(8,128)S(1)}, u32[]{:S(2)}, u32[]{:S(2)}) %collective-permute-start.28) | collective-permute-done | bytes 16416 | tf_op jit(solution)/shard_map/ppermute | solution.py:430
  76.1 0.7 collective-permute-done.26
  76.8 2.4 %collective-permute-done.25 = f32[32,512]{1,0:T(8,128)S(1)} collective-permute-done((f32[32,512]{1,0:T(8,128)S(1)}, f32[32,512]{1,0:T(8,128)S(1)}, u32[]{:S(2)}, u32[]{:S(2)}) %collective-permute-start.25) | collective-permute-done | bytes 65568 | tf_op jit(solution)/shard_map/ppermute | solution.py:420
  79.3 0.5 collective-permute-start.30
  79.8 0.9 %collective-permute-done.30.refs_3_ = f32[32,128]{1,0:T(8,128)S(1)} collective-permute-done((f32[32,128]{1,0:T(8,128)S(1)}, f32[32,128]{1,0:T(8,128)S(1)}, u32[]{:S(2)}, u32[]{:S(2)}) %collective-permute-start.30) | collective-permute-done | bytes 16416 | tf_op jit(solution)/shard_map/ppermute | solution.py:420
  80.6 1.2 %final.1 = (f32[32,2048]{1,0:T(8,128)}, f32[32,2048]{1,0:T(8,128)}) custom-call(f32[32,2048]{1,0:T(8,128)S(1)} %copy-done, f32[2,40,512]{2,1,0:T(8,128)S(1)} %pad_maximum_fusion.1.s1_own, f32[2,40,512]{2,1,0:T(8,128)S(1)} %collective-permute-done.17.s1_got, f32[2,32,512]{2,1,0:T(8,128)S(1)} %pad_maximum_fusion.3.refs_0_, ...), custom_call_target="tpu_custom_call" | custom-call | tf_op jit(solution)/shard_map/final/pallas_call | solution.py:650
  (54 shorter events, 1.7 us)
Async XLA Ops:
  0.6 5.7 %collective-permute-start = (s32[8,6]{1,0:T(8,128)}, s32[8,6]{1,0:T(8,128)S(1)}, u32[]{:S(2)}, u32[]{:S(2)}) collective-permute-start(s32[8,6]{1,0:T(8,128)} %param.3), channel_id=1, source_target_pairs={{0,1},{1,0},{2,3},{3,2},{4,5},{5,4},{6,7},{7,6},{8,9},{9,8},{10,11... | collective-permute-start | bytes 584 | tf_op jit(solution)/shard_map/ppermute | solution.py:420
  1.1 5.3 %collective-permute-start.2 = (s32[8,6]{1,0:T(8,128)}, s32[8,6]{1,0:T(8,128)S(1)}, u32[]{:S(2)}, u32[]{:S(2)}) collective-permute-start(s32[8,6]{1,0:T(8,128)} %param.3), channel_id=1, source_target_pairs={{0,3},{1,2},{2,1},{3,0},{4,7},{5,6},{6,5},{7,4},{8,11},{9,10},{10,... | collective-permute-start | bytes 584 | tf_op jit(solution)/shard_map/ppermute | solution.py:420
  3.8 3.8 %collective-permute-start.1 = (s32[8,6]{1,0:T(8,128)}, s32[8,6]{1,0:T(8,128)S(1)}, u32[]{:S(2)}, u32[]{:S(2)}) collective-permute-start(s32[8,6]{1,0:T(8,128)} %param.3), channel_id=1, source_target_pairs={{0,2},{1,3},{2,0},{3,1},{4,6},{5,7},{6,4},{7,5},{8,10},{9,11},{10,... | collective-permute-start | bytes 584 | tf_op jit(solution)/shard_map/ppermute | solution.py:420
  7.9 8.1 %collective-permute-start.5 = (bf16[16,640]{1,0:T(8,128)(2,1)S(1)}, bf16[16,640]{1,0:T(8,128)(2,1)S(1)}, u32[]{:S(2)}, u32[]{:S(2)}) collective-permute-start(bf16[16,640]{1,0:T(8,128)(2,1)S(1)} %pad_maximum_fusion.5), channel_id=1, source_target_pairs={{0,24},{4,28},{8,16},{12,20},{16,8},{20,12},{24,0},{28,4},{1,25},{... | collective-permute-start | bytes 61448 | tf_op jit(solution)/shard_map/ppermute | solution.py:420
  11.6 5.2 %collective-permute-start.4 = (bf16[16,640]{1,0:T(8,128)(2,1)S(1)}, bf16[16,640]{1,0:T(8,128)(2,1)S(1)}, u32[]{:S(2)}, u32[]{:S(2)}) collective-permute-start(bf16[16,640]{1,0:T(8,128)(2,1)S(1)} %pad_maximum_fusion.5), channel_id=1, source_target_pairs={{0,16},{4,20},{8,24},{12,28},{16,0},{20,4},{24,8},{28,12},{1,17},{... | collective-permute-start | bytes 61448 | tf_op jit(solution)/shard_map/ppermute | solution.py:420
  11.6 5.2 %collective-permute-start.3 = (bf16[16,640]{1,0:T(8,128)(2,1)S(1)}, bf16[16,640]{1,0:T(8,128)(2,1)S(1)}, u32[]{:S(2)}, u32[]{:S(2)}) collective-permute-start(bf16[16,640]{1,0:T(8,128)(2,1)S(1)} %pad_maximum_fusion.5), channel_id=1, source_target_pairs={{0,8},{4,12},{8,0},{12,4},{16,24},{20,28},{24,16},{28,20},{1,9},{5... | collective-permute-start | bytes 61448 | tf_op jit(solution)/shard_map/ppermute | solution.py:420
  12.3 10.3 %collective-permute-start.9 = (f32[32,512]{1,0:T(8,128)S(1)}, f32[32,512]{1,0:T(8,128)S(1)}, u32[]{:S(2)}, u32[]{:S(2)}) collective-permute-start(f32[32,512]{1,0:T(8,128)S(1)} %constant_dynamic-slice_fusion), channel_id=1, source_target_pairs={{0,24},{4,28},{8,16},{12,20},{16,8},{20,12},{24,0},{28,4},{1,25},{... | collective-permute-start | bytes 196616 | tf_op jit(solution)/shard_map/ppermute | solution.py:420
  15.9 6.8 %collective-permute-start.8 = (f32[32,512]{1,0:T(8,128)S(1)}, f32[32,512]{1,0:T(8,128)S(1)}, u32[]{:S(2)}, u32[]{:S(2)}) collective-permute-start(f32[32,512]{1,0:T(8,128)S(1)} %constant_dynamic-slice_fusion), channel_id=1, source_target_pairs={{0,16},{4,20},{8,24},{12,28},{16,0},{20,4},{24,8},{28,12},{1,17},{... | collective-permute-start | bytes 196616 | tf_op jit(solution)/shard_map/ppermute | solution.py:420
  15.9 6.8 %collective-permute-start.7 = (f32[32,512]{1,0:T(8,128)S(1)}, f32[32,512]{1,0:T(8,128)S(1)}, u32[]{:S(2)}, u32[]{:S(2)}) collective-permute-start(f32[32,512]{1,0:T(8,128)S(1)} %constant_dynamic-slice_fusion), channel_id=1, source_target_pairs={{0,8},{4,12},{8,0},{12,4},{16,24},{20,28},{24,16},{28,20},{1,9},{5... | collective-permute-start | bytes 196616 | tf_op jit(solution)/shard_map/ppermute | solution.py:420
  16.8 6.0 %collective-permute-start.6 = (bf16[4,16,640]{2,1,0:T(8,128)(2,1)S(1)}, bf16[4,16,640]{2,1,0:T(8,128)(2,1)S(1)}, u32[]{:S(2)}, u32[]{:S(2)}) collective-permute-start(bf16[4,16,640]{2,1,0:T(8,128)(2,1)S(1)} %pad_maximum_fusion.4.refs_1_), channel_id=1, source_target_pairs={{0,4},{4,0},{8,12},{12,8},{16,20},{20,16},{24,28},{28,24},{1,5},{5... | collective-permute-start | bytes 245768 | tf_op jit(solution)/shard_map/ppermute | solution.py:420
  22.8 6.4 %collective-permute-start.10 = (f32[4,32,512]{2,1,0:T(8,128)S(1)}, f32[4,32,512]{2,1,0:T(8,128)S(1)}, u32[]{:S(2)}, u32[]{:S(2)}) collective-permute-start(f32[4,32,512]{2,1,0:T(8,128)S(1)} %pad_maximum_fusion.refs_2_.t_same), channel_id=1, source_target_pairs={{0,4},{4,0},{8,12},{12,8},{16,20},{20,16},{24,28},{28,24},{1,5},{5... | collective-permute-start | bytes 786440 | tf_op jit(solution)/shard_map/ppermute | solution.py:420
  27.2 23.3 %copy-start = (f32[32,2048]{1,0:T(8,128)S(1)}, f32[32,2048]{1,0:T(8,128)}, u32[]{:S(2)}) copy-start(f32[32,2048]{1,0:T(8,128)} %t_ref.5) | copy-start | bytes 786436
  29.2 4.6 %collective-permute-start.13 = (f32[16,256]{1,0:T(8,128)S(1)}, f32[16,256]{1,0:T(8,128)S(1)}, u32[]{:S(2)}, u32[]{:S(2)}) collective-permute-start(f32[16,256]{1,0:T(8,128)S(1)} %get-tuple-element.60), channel_id=1, source_target_pairs={{0,12},{4,8},{8,4},{12,0},{16,28},{20,24},{24,20},{28,16},{1,13},{... | collective-permute-start | bytes 49160 | tf_op jit(solution)/shard_map/ppermute | solution.py:420
  30.0 3.8 %collective-permute-start.12 = (f32[16,256]{1,0:T(8,128)S(1)}, f32[16,256]{1,0:T(8,128)S(1)}, u32[]{:S(2)}, u32[]{:S(2)}) collective-permute-start(f32[16,256]{1,0:T(8,128)S(1)} %get-tuple-element.60), channel_id=1, source_target_pairs={{0,8},{4,12},{8,0},{12,4},{16,24},{20,28},{24,16},{28,20},{1,9},{5... | collective-permute-start | bytes 49160 | tf_op jit(solution)/shard_map/ppermute | solution.py:420
  31.2 3.7 %collective-permute-start.11 = (f32[16,256]{1,0:T(8,128)S(1)}, f32[16,256]{1,0:T(8,128)S(1)}, u32[]{:S(2)}, u32[]{:S(2)}) collective-permute-start(f32[16,256]{1,0:T(8,128)S(1)} %get-tuple-element.60), channel_id=1, source_target_pairs={{0,4},{4,0},{8,12},{12,8},{16,20},{20,16},{24,28},{28,24},{1,5},{5... | collective-permute-start | bytes 49160 | tf_op jit(solution)/shard_map/ppermute | solution.py:420
  34.9 4.7 %collective-permute-start.14 = (f32[16,256]{1,0:T(8,128)S(1)}, f32[16,256]{1,0:T(8,128)S(1)}, u32[]{:S(2)}, u32[]{:S(2)}) collective-permute-start(f32[16,256]{1,0:T(8,128)S(1)} %add_add_fusion.1), channel_id=1, source_target_pairs={{0,16},{4,20},{8,24},{12,28},{16,0},{20,4},{24,8},{28,12},{1,17},{... | collective-permute-start | bytes 49160 | tf_op jit(solution)/shard_map/ppermute | solution.py:420
  43.0 1.4 %collective-permute-start.15 = (f32[2,32,512]{2,1,0:T(8,128)S(1)}, f32[2,32,512]{2,1,0:T(8,128)S(1)}, u32[]{:S(2)}, u32[]{:S(2)}) collective-permute-start(f32[2,32,512]{2,1,0:T(8,128)S(1)} %get-tuple-element.62), channel_id=1, source_target_pairs={{0,1},{1,0},{2,3},{3,2},{4,5},{5,4},{6,7},{7,6},{8,9},{9,8},{10,11... | collective-permute-start | bytes 393224 | tf_op jit(solution)/shard_map/ppermute | solution.py:420
  44.5 6.0 %collective-permute-start.16 = (f32[72,512]{1,0:T(8,128)S(1)}, f32[72,512]{1,0:T(8,128)S(1)}, u32[]{:S(2)}, u32[]{:S(2)}) collective-permute-start(f32[72,512]{1,0:T(8,128)S(1)} %pad_maximum_fusion.2), channel_id=1, source_target_pairs={{0,2},{1,3},{2,0},{3,1},{4,6},{5,7},{6,4},{7,5},{8,10},{9,11},{10,... | collective-permute-start | bytes 442376 | tf_op jit(solution)/shard_map/ppermute | solution.py:420
  50.5 1.5 %collective-permute-start.17 = (f32[2,40,512]{2,1,0:T(8,128)S(1)}, f32[2,40,512]{2,1,0:T(8,128)S(1)}, u32[]{:S(2)}, u32[]{:S(2)}) collective-permute-start(f32[2,40,512]{2,1,0:T(8,128)S(1)} %pad_maximum_fusion.1.s1_own), channel_id=1, source_target_pairs={{0,1},{1,0},{2,3},{3,2},{4,5},{5,4},{6,7},{7,6},{8,9},{9,8},{10,11... | collective-permute-start | bytes 491528 | tf_op jit(solution)/shard_map/ppermute | solution.py:420
  53.6 10.7 %collective-permute-start.18 = (bf16[4,32,512]{2,1,0:T(8,128)(2,1)S(1)}, bf16[4,32,512]{2,1,0:T(8,128)(2,1)S(1)}, u32[]{:S(2)}, u32[]{:S(2)}) collective-permute-start(bf16[4,32,512]{2,1,0:T(8,128)(2,1)S(1)} %second.3), channel_id=1, source_target_pairs={{0,4},{4,0},{8,12},{12,8},{16,20},{20,16},{24,28},{28,24},{1,5},{5... | collective-permute-start | bytes 393224 | tf_op jit(solution)/shard_map/ppermute | solution.py:420
  55.1 6.5 %collective-permute-start.21 = (bf16[32,512]{1,0:T(8,128)(2,1)S(1)}, bf16[32,512]{1,0:T(8,128)(2,1)S(1)}, u32[]{:S(2)}, u32[]{:S(2)}) collective-permute-start(bf16[32,512]{1,0:T(8,128)(2,1)S(1)} %fusion.2.refs_0_), channel_id=1, source_target_pairs={{0,24},{4,28},{8,16},{12,20},{16,8},{20,12},{24,0},{28,4},{1,25},{... | collective-permute-start | bytes 98312 | tf_op jit(solution)/shard_map/ppermute | solution.py:420
  59.4 4.8 %collective-permute-start.20 = (bf16[32,512]{1,0:T(8,128)(2,1)S(1)}, bf16[32,512]{1,0:T(8,128)(2,1)S(1)}, u32[]{:S(2)}, u32[]{:S(2)}) collective-permute-start(bf16[32,512]{1,0:T(8,128)(2,1)S(1)} %fusion.2.refs_0_), channel_id=1, source_target_pairs={{0,16},{4,20},{8,24},{12,28},{16,0},{20,4},{24,8},{28,12},{1,17},{... | collective-permute-start | bytes 98312 | tf_op jit(solution)/shard_map/ppermute | solution.py:420
  59.4 4.8 %collective-permute-start.19 = (bf16[32,512]{1,0:T(8,128)(2,1)S(1)}, bf16[32,512]{1,0:T(8,128)(2,1)S(1)}, u32[]{:S(2)}, u32[]{:S(2)}) collective-permute-start(bf16[32,512]{1,0:T(8,128)(2,1)S(1)} %fusion.2.refs_0_), channel_id=1, source_target_pairs={{0,8},{4,12},{8,0},{12,4},{16,24},{20,28},{24,16},{28,20},{1,9},{5... | collective-permute-start | bytes 98312 | tf_op jit(solution)/shard_map/ppermute | solution.py:420
  64.4 5.9 %collective-permute-start.22 = (bf16[32,640]{1,0:T(8,128)(2,1)S(1)}, bf16[32,640]{1,0:T(8,128)(2,1)S(1)}, u32[]{:S(2)}, u32[]{:S(2)}) collective-permute-start(bf16[32,640]{1,0:T(8,128)(2,1)S(1)} %get-tuple-element.75), channel_id=1, source_target_pairs={{0,24},{4,28},{8,16},{12,20},{16,8},{20,12},{24,0},{28,4},{1,25},{... | collective-permute-start | bytes 122888 | tf_op jit(solution)/shard_map/ppermute | solution.py:420
  66.0 4.9 %collective-permute-start.23 = (bf16[32,640]{1,0:T(8,128)(2,1)S(1)}, bf16[32,640]{1,0:T(8,128)(2,1)S(1)}, u32[]{:S(2)}, u32[]{:S(2)}) collective-permute-start(bf16[32,640]{1,0:T(8,128)(2,1)S(1)} %get-tuple-element.76), channel_id=1, source_target_pairs={{0,16},{4,20},{8,24},{12,28},{16,0},{20,4},{24,8},{28,12},{1,17},{... | collective-permute-start | bytes 122888 | tf_op jit(solution)/shard_map/ppermute | solution.py:420
  66.6 4.7 %collective-permute-start.24 = (bf16[32,640]{1,0:T(8,128)(2,1)S(1)}, bf16[32,640]{1,0:T(8,128)(2,1)S(1)}, u32[]{:S(2)}, u32[]{:S(2)}) collective-permute-start(bf16[32,640]{1,0:T(8,128)(2,1)S(1)} %get-tuple-element.77), channel_id=1, source_target_pairs={{0,8},{4,12},{8,0},{12,4},{16,24},{20,28},{24,16},{28,20},{1,9},{5... | collective-permute-start | bytes 122888 | tf_op jit(solution)/shard_map/ppermute | solution.py:420
  71.4 4.7 %collective-permute-start.28 = (f32[32,128]{1,0:T(8,128)S(1)}, f32[32,128]{1,0:T(8,128)S(1)}, u32[]{:S(2)}, u32[]{:S(2)}) collective-permute-start(f32[32,128]{1,0:T(8,128)S(1)} %get-tuple-element.79), channel_id=1, source_target_pairs={{0,6},{1,7},{2,4},{3,5},{4,2},{5,3},{6,0},{7,1},{8,14},{9,15},{10,... | collective-permute-start | bytes 49160 | tf_op jit(solution)/shard_map/ppermute | solution.py:430
  72.2 3.9 %collective-permute-start.27 = (f32[32,128]{1,0:T(8,128)S(1)}, f32[32,128]{1,0:T(8,128)S(1)}, u32[]{:S(2)}, u32[]{:S(2)}) collective-permute-start(f32[32,128]{1,0:T(8,128)S(1)} %get-tuple-element.79), channel_id=1, source_target_pairs={{0,2},{1,3},{2,0},{3,1},{4,6},{5,7},{6,4},{7,5},{8,10},{9,11},{10,... | collective-permute-start | bytes 49160 | tf_op jit(solution)/shard_map/ppermute | solution.py:420
  73.0 3.7 %collective-permute-start.26 = (f32[32,128]{1,0:T(8,128)S(1)}, f32[32,128]{1,0:T(8,128)S(1)}, u32[]{:S(2)}, u32[]{:S(2)}) collective-permute-start(f32[32,128]{1,0:T(8,128)S(1)} %get-tuple-element.79), channel_id=1, source_target_pairs={{0,4},{4,0},{8,12},{12,8},{16,20},{20,16},{24,28},{28,24},{1,5},{5... | collective-permute-start | bytes 49160 | tf_op jit(solution)/shard_map/ppermute | solution.py:420
  74.9 4.3 %collective-permute-start.25 = (f32[32,512]{1,0:T(8,128)S(1)}, f32[32,512]{1,0:T(8,128)S(1)}, u32[]{:S(2)}, u32[]{:S(2)}) collective-permute-start(f32[32,512]{1,0:T(8,128)S(1)} %get-tuple-element.78), channel_id=1, source_target_pairs={{0,2},{1,3},{2,0},{3,1},{4,6},{5,7},{6,4},{7,5},{8,10},{9,11},{10,... | collective-permute-start | bytes 196616 | tf_op jit(solution)/shard_map/ppermute | solution.py:420
  79.2 1.4 %collective-permute-start.29 = (f32[2,32,512]{2,1,0:T(8,128)S(1)}, f32[2,32,512]{2,1,0:T(8,128)S(1)}, u32[]{:S(2)}, u32[]{:S(2)}) collective-permute-start(f32[2,32,512]{2,1,0:T(8,128)S(1)} %pad_maximum_fusion.3.refs_0_), channel_id=1, source_target_pairs={{0,1},{1,0},{2,3},{3,2},{4,5},{5,4},{6,7},{7,6},{8,9},{9,8},{10,11... | collective-permute-start | bytes 393224 | tf_op jit(solution)/shard_map/ppermute | solution.py:420
  79.3 1.4 %collective-permute-start.30 = (f32[32,128]{1,0:T(8,128)S(1)}, f32[32,128]{1,0:T(8,128)S(1)}, u32[]{:S(2)}, u32[]{:S(2)}) collective-permute-start(f32[32,128]{1,0:T(8,128)S(1)} %add_add_fusion.refs_2_), channel_id=1, source_target_pairs={{0,1},{1,0},{2,3},{3,2},{4,5},{5,4},{6,7},{7,6},{8,9},{9,8},{10,11... | collective-permute-start | bytes 49160 | tf_op jit(solution)/shard_map/ppermute | solution.py:420

commit v13 on v12

--- a/solution.py
+++ b/solution.py
@@ -247,11 +247,15 @@
         codes = [listed[0, g * GROUP + u + 1] for u in range(GROUP)]
         pairs = [(lax.shift_right_logical(code, CODE_BITS), code & (CODE - 1)) for code in codes]
         terms = [product(i, j, source[slot, u]) for u, (i, j) in enumerate(pairs)]
-        for (i, j), term in zip(pairs, terms):
-            total_ref[i if by_row else j] += term
-        return carry
-
-    lax.fori_loop(0, total, step, 0)
+        add(carry)
+        return [i if by_row else j for i, j in pairs], terms
+
+    def add(carry):
+        for at, term in zip(*carry):
+            total_ref[at] += term
+
+    none = [jnp.int32(0)] * GROUP, [jnp.zeros(total_ref.shape[1:], F32)] * GROUP
+    add(lax.fori_loop(0, total, step, none))
 
 
 def first_kernel(cfg, k_mat, *refs):
@@ -546,7 +550,6 @@
         t_same, t_other = across_x(jnp.stack(t_same))
         other, t_same = lax.optimization_barrier((other, t_same))
         k_mat, list1, degree = build(1, lhs, degree, other, k_mat)
-        degree, t_other = lax.optimization_barrier((degree, t_other))
         t_pieces, k_lists = [t_same, t_other], [list0, list1]
     else:
         k_mat, list0, degree, _ = build(0, near, lax.all_gather(packed, "rows"))

time: 81.8 us -> 78.8 us (0.963)
  waiting for transfers between devices: 24.4 us -> 21 us
  starting transfers between devices: 37.1 us -> 38.8 us
  Pallas kernels: 16.2 us -> 15.2 us
    ppermute x30, waiting for transfers between devices: 23.4 us -> 20.8 us  [swap(): return lax.ppermute(x, axis, [(i, i ^ d) for i in range(size)])]
    ppermute x30, starting transfers between devices: 36.3 us -> 37.7 us  [swap(): return lax.ppermute(x, axis, [(i, i ^ d) for i in range(size)])]
  transfers between devices with their start and end apart: 31 -> 31, of which waited for: 16 -> 17; matrix products, arithmetic and copies ran while one was open for 3% -> 4% of each run, Pallas kernels for 12% -> 7%
where the time goes in v13:
time: 78.8 us; the launch traced here: 79 us
  starting transfers between devices  38.8 us (49%)
  waiting for transfers between devices  21 us (27%)
  Pallas kernels  15.2 us (19%)
  local copies, waits for them, and re-layouts  2.74 us (3%)
  between operations  0.86 us (1%)
    ppermute x30, starting transfers between devices, swap(): return lax.ppermute(x, axis, [(i, i ^ d) for i in range(size)])  37.7 us
    ppermute x30, waiting for transfers between devices, swap(): return lax.ppermute(x, axis, [(i, i ^ d) for i in range(size)])  20.8 us
    pallas_call x2, Pallas kernels, build(): pl.pallas_call(functools.partial(build_kernel, cfg, part), out_shape=out,...  7.7 us
    pallas_call x1, Pallas kernels, local(): pl.pallas_call(functools.partial(first_kernel, cfg), out_shape=[shape(out...  3.05 us
    pallas_call x2, Pallas kernels, second(): pl.pallas_call(functools.partial(second_kernel, cfg, part), out_shape=sha...  3 us
  transfers between devices with their start and end apart: 31, of which 17 were waited for; matrix products, arithmetic and copies ran while one was open for 4% of the time, Pallas kernels for 7%

profile of v13, /device:TPU:0, one launch (start us, length us, event | category | flops | bytes accessed | tf_op | source)
XLA Modules:
  0.0 79.0 jit_solution(8268972320827950337)
XLA Ops:
  0.6 0.5 collective-permute-start
  1.1 2.6 %collective-permute-start.2 = (s32[8,6]{1,0:T(8,128)}, s32[8,6]{1,0:T(8,128)S(1)}, u32[]{:S(2)}, u32[]{:S(2)}) collective-permute-start(s32[8,6]{1,0:T(8,128)} %param.3), channel_id=1, source_target_pairs={{0,3},{1,2},{2,1},{3,0},{4,7},{5,6},{6,5},{7,4},{8,11},{9,10},{10,... | collective-permute-start | bytes 584 | tf_op jit(solution)/shard_map/ppermute | solution.py:424
  3.8 0.8 %copy.6 = s32[8,6]{0,1:T(8,128)S(1)} copy(s32[8,6]{1,0:T(8,128)} %param.3) | data formatting | bytes 384 | tf_op args[0]
  4.7 0.7 constant_dynamic-slice_fusion.1
  5.5 0.8 %constant_dynamic-slice_fusion = f32[32,512]{1,0:T(8,128)S(1)} fusion(f32[32,2048]{1,0:T(8,128)} %t_ref.5, s32[]{:T(128)S(6)} %select_n.7), kind=kLoop, calls=%fused_computation.34 | loop fusion | bytes 131076 | tf_op jit(solution)/shard_map/dynamic_slice | solution.py:485
  6.6 1.0 %collective-permute-done.1 = s32[8,6]{1,0:T(8,128)S(1)} collective-permute-done((s32[8,6]{1,0:T(8,128)}, s32[8,6]{1,0:T(8,128)S(1)}, u32[]{:S(2)}, u32[]{:S(2)}) %collective-permute-start.1) | collective-permute-done | bytes 224 | tf_op jit(solution)/shard_map/ppermute | solution.py:424
  7.9 3.7 %collective-permute-start.5 = (bf16[16,640]{1,0:T(8,128)(2,1)S(1)}, bf16[16,640]{1,0:T(8,128)(2,1)S(1)}, u32[]{:S(2)}, u32[]{:S(2)}) collective-permute-start(bf16[16,640]{1,0:T(8,128)(2,1)S(1)} %pad_maximum_fusion.5), channel_id=1, source_target_pairs={{0,24},{4,28},{8,16},{12,20},{16,8},{20,12},{24,0},{28,4},{1,25},{... | collective-permute-start | bytes 61448 | tf_op jit(solution)/shard_map/ppermute | solution.py:424
  11.6 0.8 collective-permute-start.3
  12.3 3.6 %collective-permute-start.9 = (f32[32,512]{1,0:T(8,128)S(1)}, f32[32,512]{1,0:T(8,128)S(1)}, u32[]{:S(2)}, u32[]{:S(2)}) collective-permute-start(f32[32,512]{1,0:T(8,128)S(1)} %constant_dynamic-slice_fusion), channel_id=1, source_target_pairs={{0,24},{4,28},{8,16},{12,20},{16,8},{20,12},{24,0},{28,4},{1,25},{... | collective-permute-start | bytes 196616 | tf_op jit(solution)/shard_map/ppermute | solution.py:424
  15.9 0.8 collective-permute-start.7
  16.8 1.6 %collective-permute-start.6 = (bf16[4,16,640]{2,1,0:T(8,128)(2,1)S(1)}, bf16[4,16,640]{2,1,0:T(8,128)(2,1)S(1)}, u32[]{:S(2)}, u32[]{:S(2)}) collective-permute-start(bf16[4,16,640]{2,1,0:T(8,128)(2,1)S(1)} %pad_maximum_fusion.4.refs_1_), channel_id=1, source_target_pairs={{0,4},{4,0},{8,12},{12,8},{16,20},{20,16},{24,28},{28,24},{1,5},{5... | collective-permute-start | bytes 245768 | tf_op jit(solution)/shard_map/ppermute | solution.py:424
  18.3 3.8 %build.2 = (bf16[32,4,256,256]{3,2,1,0:T(8,128)(2,1)S(1)}, s32[1,128]{1,0:T(1,128)S(1)}, f32[8,256]{1,0:T(8,128)S(1)}, bf16[8,256,32]{2,1,0:T(8,128)(2,1)S(1)}) custom-call(s32[8,64]{1,0:T(8,128)S(1)} %add_add_fusion.2.direct_v, bf16[16,2048]{1,0:T(8,128)(2,1)} %refs_0_.1, bf16[4,16,640]{2,1,0:T(8,128)(2,1)S(1)} %pad_maximum_fusion.4.refs_1_), custom_call_target="tpu_custom_call" | custom-call | flops 2684354560 | bytes 83886080 | tf_op jit(solution)/shard_map/build/pallas_call | solution.py:510
  22.2 3.9 %build.3 = (bf16[32,4,256,256]{3,2,1,0:T(8,128)(2,1)S(1)}, s32[1,128]{1,0:T(1,128)S(1)}, f32[16,256]{1,0:T(8,128)S(1)}) custom-call(s32[8,64]{1,0:T(8,128)S(1)} %add_add_fusion.2.direct_v, bf16[8,256,32]{2,1,0:T(8,128)(2,1)S(1)} %get-tuple-element.41.refs_0_, f32[8,256]{1,0:T(8,128)S(1)} %get-tuple-element.44.refs_1_, ...), custom_call_target="tpu_custom_call", output_to_operand_aliasing={{0}: (4, {})} | custom-call | flops 2684354560 | bytes 83886080 | tf_op jit(solution)/shard_map/build/pallas_call | solution.py:510
  26.1 1.3 %collective-permute-start.13 = (f32[16,256]{1,0:T(8,128)S(1)}, f32[16,256]{1,0:T(8,128)S(1)}, u32[]{:S(2)}, u32[]{:S(2)}) collective-permute-start(f32[16,256]{1,0:T(8,128)S(1)} %get-tuple-element.56), channel_id=1, source_target_pairs={{0,12},{4,8},{8,4},{12,0},{16,28},{20,24},{24,20},{28,16},{1,13},{... | collective-permute-start | bytes 49160 | tf_op jit(solution)/shard_map/ppermute | solution.py:424
  27.4 0.8 collective-permute-start.12
  28.2 1.5 %collective-permute-start.11 = (f32[16,256]{1,0:T(8,128)S(1)}, f32[16,256]{1,0:T(8,128)S(1)}, u32[]{:S(2)}, u32[]{:S(2)}) collective-permute-start(f32[16,256]{1,0:T(8,128)S(1)} %get-tuple-element.56), channel_id=1, source_target_pairs={{0,4},{4,0},{8,12},{12,8},{16,20},{20,16},{24,28},{28,24},{1,5},{5... | collective-permute-start | bytes 49160 | tf_op jit(solution)/shard_map/ppermute | solution.py:424
  29.7 0.6 collective-permute-start.10
  30.2 0.7 collective-permute-done.13
  30.9 0.2 collective-permute-done.12
  31.2 1.0 %collective-permute-done.11 = f32[16,256]{1,0:T(8,128)S(1)} collective-permute-done((f32[16,256]{1,0:T(8,128)S(1)}, f32[16,256]{1,0:T(8,128)S(1)}, u32[]{:S(2)}, u32[]{:S(2)}) %collective-permute-start.11) | collective-permute-done | bytes 16416 | tf_op jit(solution)/shard_map/ppermute | solution.py:424
  32.2 3.0 %collective-permute-start.14 = (f32[16,256]{1,0:T(8,128)S(1)}, f32[16,256]{1,0:T(8,128)S(1)}, u32[]{:S(2)}, u32[]{:S(2)}) collective-permute-start(f32[16,256]{1,0:T(8,128)S(1)} %add_add_fusion.1), channel_id=1, source_target_pairs={{0,16},{4,20},{8,24},{12,28},{16,0},{20,4},{24,8},{28,12},{1,17},{... | collective-permute-start | bytes 49160 | tf_op jit(solution)/shard_map/ppermute | solution.py:424
  35.2 1.7 %collective-permute-done.14 = f32[16,256]{1,0:T(8,128)S(1)} collective-permute-done((f32[16,256]{1,0:T(8,128)S(1)}, f32[16,256]{1,0:T(8,128)S(1)}, u32[]{:S(2)}, u32[]{:S(2)}) %collective-permute-start.14) | collective-permute-done | bytes 16416 | tf_op jit(solution)/shard_map/ppermute | solution.py:424
  36.9 3.1 %first.1 = (f32[32,512]{1,0:T(8,128)S(1)}, f32[32,512]{1,0:T(8,128)S(1)}, f32[2,32,512]{2,1,0:T(8,128)S(1)}, f32[8,512]{1,0:T(8,128)S(1)}) custom-call(bf16[32,4,256,256]{3,2,1,0:T(8,128)(2,1)S(1)} %get-tuple-element.52.k_mat, s32[1,128]{1,0:T(1,128)S(1)} %get-tuple-element.53.refs_0_.list_v, s32[1,128]{1,0:T(1,128)S(1)} %get-tuple-element.54.refs_1_.list_v, ...), custom_call_target="tpu_custom_call" | custom-call | flops 536870912 | bytes 8388608 | tf_op jit(solution)/shard_map/first/pallas_call | solution.py:566
  40.1 1.3 %collective-permute-done.15 = f32[2,32,512]{2,1,0:T(8,128)S(1)} collective-permute-done((f32[2,32,512]{2,1,0:T(8,128)S(1)}, f32[2,32,512]{2,1,0:T(8,128)S(1)}, u32[]{:S(2)}, u32[]{:S(2)}) %collective-permute-start.15) | collective-permute-done | bytes 131104 | tf_op jit(solution)/shard_map/ppermute | solution.py:424
  41.5 1.7 %collective-permute-start.16 = (f32[72,512]{1,0:T(8,128)S(1)}, f32[72,512]{1,0:T(8,128)S(1)}, u32[]{:S(2)}, u32[]{:S(2)}) collective-permute-start(f32[72,512]{1,0:T(8,128)S(1)} %pad_maximum_fusion.2), channel_id=1, source_target_pairs={{0,2},{1,3},{2,0},{3,1},{4,6},{5,7},{6,4},{7,5},{8,10},{9,11},{10,... | collective-permute-start | bytes 442376 | tf_op jit(solution)/shard_map/ppermute | solution.py:424
  43.1 4.3 %collective-permute-done.16 = f32[72,512]{1,0:T(8,128)S(1)} collective-permute-done((f32[72,512]{1,0:T(8,128)S(1)}, f32[72,512]{1,0:T(8,128)S(1)}, u32[]{:S(2)}, u32[]{:S(2)}) %collective-permute-start.16) | collective-permute-done | bytes 147488 | tf_op jit(solution)/shard_map/ppermute | solution.py:424
  47.6 1.3 %collective-permute-done.17.s1_got = f32[2,40,512]{2,1,0:T(8,128)S(1)} collective-permute-done((f32[2,40,512]{2,1,0:T(8,128)S(1)}, f32[2,40,512]{2,1,0:T(8,128)S(1)}, u32[]{:S(2)}, u32[]{:S(2)}) %collective-permute-start.17) | collective-permute-done | bytes 163872 | tf_op jit(solution)/shard_map/ppermute | solution.py:424
  49.0 1.6 %second.3 = bf16[4,32,512]{2,1,0:T(8,128)(2,1)S(1)} custom-call(bf16[32,4,256,256]{3,2,1,0:T(8,128)(2,1)S(1)} %get-tuple-element.52.k_mat, s32[1,128]{1,0:T(1,128)S(1)} %get-tuple-element.54.refs_1_.list_v, f32[32,2048]{1,0:T(8,128)S(1)} %copy-done, f32[2,40,512]{2,1,0:T(8,128)S(1)} %pad_maximum_fusion.1.s1_own, f32[2,40,512]{2,1,0:T(8,128)S(1)} %collective-permute-done.17.s1_got), custom_call_target="tpu_custom_call" | custom-call | flops 268435456 | bytes 4194304 | tf_op jit(solution)/shard_map/second/pallas_call | solution.py:595
  50.6 1.3 %collective-permute-start.18 = (bf16[4,32,512]{2,1,0:T(8,128)(2,1)S(1)}, bf16[4,32,512]{2,1,0:T(8,128)(2,1)S(1)}, u32[]{:S(2)}, u32[]{:S(2)}) collective-permute-start(bf16[4,32,512]{2,1,0:T(8,128)(2,1)S(1)} %second.3), channel_id=1, source_target_pairs={{0,4},{4,0},{8,12},{12,8},{16,20},{20,16},{24,28},{28,24},{1,5},{5... | collective-permute-start | bytes 393224 | tf_op jit(solution)/shard_map/ppermute | solution.py:424
  51.8 4.9 %collective-permute-start.21 = (bf16[32,512]{1,0:T(8,128)(2,1)S(1)}, bf16[32,512]{1,0:T(8,128)(2,1)S(1)}, u32[]{:S(2)}, u32[]{:S(2)}) collective-permute-start(bf16[32,512]{1,0:T(8,128)(2,1)S(1)} %fusion.2.refs_0_), channel_id=1, source_target_pairs={{0,24},{4,28},{8,16},{12,20},{16,8},{20,12},{24,0},{28,4},{1,25},{... | collective-permute-start | bytes 98312 | tf_op jit(solution)/shard_map/ppermute | solution.py:424
  56.7 0.6 collective-permute-start.19
  57.3 1.4 %second.2.z_same = f32[4,32,512]{2,1,0:T(8,128)S(1)} custom-call(bf16[32,4,256,256]{3,2,1,0:T(8,128)(2,1)S(1)} %get-tuple-element.52.k_mat, s32[1,128]{1,0:T(1,128)S(1)} %get-tuple-element.53.refs_0_.list_v, f32[32,2048]{1,0:T(8,128)S(1)} %copy-done, f32[2,40,512]{2,1,0:T(8,128)S(1)} %pad_maximum_fusion.1.s1_own, ...), custom_call_target="tpu_custom_call" | custom-call | flops 268435456 | bytes 4194304 | tf_op jit(solution)/shard_map/second/pallas_call | solution.py:595
  58.7 2.8 %collective-permute-done.20.refs_2_ = bf16[32,512]{1,0:T(8,128)(2,1)S(1)} collective-permute-done((bf16[32,512]{1,0:T(8,128)(2,1)S(1)}, bf16[32,512]{1,0:T(8,128)(2,1)S(1)}, u32[]{:S(2)}, u32[]{:S(2)}) %collective-permute-start.20) | collective-permute-done | bytes 32800 | tf_op jit(solution)/shard_map/ppermute | solution.py:424
  61.7 1.5 %collective-permute-start.22 = (bf16[32,640]{1,0:T(8,128)(2,1)S(1)}, bf16[32,640]{1,0:T(8,128)(2,1)S(1)}, u32[]{:S(2)}, u32[]{:S(2)}) collective-permute-start(bf16[32,640]{1,0:T(8,128)(2,1)S(1)} %get-tuple-element.71), channel_id=1, source_target_pairs={{0,24},{4,28},{8,16},{12,20},{16,8},{20,12},{24,0},{28,4},{1,25},{... | collective-permute-start | bytes 122888 | tf_op jit(solution)/shard_map/ppermute | solution.py:424
  63.2 0.6 collective-permute-start.23
  63.9 2.3 %collective-permute-start.24 = (bf16[32,640]{1,0:T(8,128)(2,1)S(1)}, bf16[32,640]{1,0:T(8,128)(2,1)S(1)}, u32[]{:S(2)}, u32[]{:S(2)}) collective-permute-start(bf16[32,640]{1,0:T(8,128)(2,1)S(1)} %get-tuple-element.73), channel_id=1, source_target_pairs={{0,8},{4,12},{8,0},{12,4},{16,24},{20,28},{24,16},{28,20},{1,9},{5... | collective-permute-start | bytes 122888 | tf_op jit(solution)/shard_map/ppermute | solution.py:424
  66.2 1.4 %collective-permute-done.22.refs_0_ = bf16[32,640]{1,0:T(8,128)(2,1)S(1)} collective-permute-done((bf16[32,640]{1,0:T(8,128)(2,1)S(1)}, bf16[32,640]{1,0:T(8,128)(2,1)S(1)}, u32[]{:S(2)}, u32[]{:S(2)}) %collective-permute-start.22) | collective-permute-done | bytes 40992 | tf_op jit(solution)/shard_map/ppermute | solution.py:424
  67.6 0.6 collective-permute-done.23.refs_1_
  68.2 0.4 collective-permute-done.24.refs_2_
  68.7 1.0 %collective-permute-start.28 = (f32[32,128]{1,0:T(8,128)S(1)}, f32[32,128]{1,0:T(8,128)S(1)}, u32[]{:S(2)}, u32[]{:S(2)}) collective-permute-start(f32[32,128]{1,0:T(8,128)S(1)} %get-tuple-element.75), channel_id=1, source_target_pairs={{0,6},{1,7},{2,4},{3,5},{4,2},{5,3},{6,0},{7,1},{8,14},{9,15},{10,... | collective-permute-start | bytes 49160 | tf_op jit(solution)/shard_map/ppermute | solution.py:434
  69.7 1.0 %collective-permute-start.27 = (f32[32,128]{1,0:T(8,128)S(1)}, f32[32,128]{1,0:T(8,128)S(1)}, u32[]{:S(2)}, u32[]{:S(2)}) collective-permute-start(f32[32,128]{1,0:T(8,128)S(1)} %get-tuple-element.75), channel_id=1, source_target_pairs={{0,2},{1,3},{2,0},{3,1},{4,6},{5,7},{6,4},{7,5},{8,10},{9,11},{10,... | collective-permute-start | bytes 49160 | tf_op jit(solution)/shard_map/ppermute | solution.py:424
  70.7 1.4 %collective-permute-start.26 = (f32[32,128]{1,0:T(8,128)S(1)}, f32[32,128]{1,0:T(8,128)S(1)}, u32[]{:S(2)}, u32[]{:S(2)}) collective-permute-start(f32[32,128]{1,0:T(8,128)S(1)} %get-tuple-element.75), channel_id=1, source_target_pairs={{0,4},{4,0},{8,12},{12,8},{16,20},{20,16},{24,28},{28,24},{1,5},{5... | collective-permute-start | bytes 49160 | tf_op jit(solution)/shard_map/ppermute | solution.py:424
  72.2 1.0 %collective-permute-start.25 = (f32[32,512]{1,0:T(8,128)S(1)}, f32[32,512]{1,0:T(8,128)S(1)}, u32[]{:S(2)}, u32[]{:S(2)}) collective-permute-start(f32[32,512]{1,0:T(8,128)S(1)} %get-tuple-element.74), channel_id=1, source_target_pairs={{0,2},{1,3},{2,0},{3,1},{4,6},{5,7},{6,4},{7,5},{8,10},{9,11},{10,... | collective-permute-start | bytes 196616 | tf_op jit(solution)/shard_map/ppermute | solution.py:424
  73.5 1.0 %collective-permute-done.26 = f32[32,128]{1,0:T(8,128)S(1)} collective-permute-done((f32[32,128]{1,0:T(8,128)S(1)}, f32[32,128]{1,0:T(8,128)S(1)}, u32[]{:S(2)}, u32[]{:S(2)}) %collective-permute-start.26) | collective-permute-done | bytes 16416 | tf_op jit(solution)/shard_map/ppermute | solution.py:424
  74.5 1.9 %collective-permute-done.25 = f32[32,512]{1,0:T(8,128)S(1)} collective-permute-done((f32[32,512]{1,0:T(8,128)S(1)}, f32[32,512]{1,0:T(8,128)S(1)}, u32[]{:S(2)}, u32[]{:S(2)}) %collective-permute-start.25) | collective-permute-done | bytes 65568 | tf_op jit(solution)/shard_map/ppermute | solution.py:424
  76.5 0.5 collective-permute-start.30
  77.0 0.9 %collective-permute-done.30.refs_3_ = f32[32,128]{1,0:T(8,128)S(1)} collective-permute-done((f32[32,128]{1,0:T(8,128)S(1)}, f32[32,128]{1,0:T(8,128)S(1)}, u32[]{:S(2)}, u32[]{:S(2)}) %collective-permute-start.30) | collective-permute-done | bytes 16416 | tf_op jit(solution)/shard_map/ppermute | solution.py:424
  77.9 1.2 %final.1 = (f32[32,2048]{1,0:T(8,128)}, f32[32,2048]{1,0:T(8,128)}) custom-call(f32[32,2048]{1,0:T(8,128)S(1)} %copy-done, f32[2,40,512]{2,1,0:T(8,128)S(1)} %pad_maximum_fusion.1.s1_own, f32[2,40,512]{2,1,0:T(8,128)S(1)} %collective-permute-done.17.s1_got, f32[2,32,512]{2,1,0:T(8,128)S(1)} %pad_maximum_fusion.3.refs_0_, ...), custom_call_target="tpu_custom_call" | custom-call | tf_op jit(solution)/shard_map/final/pallas_call | solution.py:653
  (54 shorter events, 1.8 us)
Async XLA Ops:
  0.6 5.7 %collective-permute-start = (s32[8,6]{1,0:T(8,128)}, s32[8,6]{1,0:T(8,128)S(1)}, u32[]{:S(2)}, u32[]{:S(2)}) collective-permute-start(s32[8,6]{1,0:T(8,128)} %param.3), channel_id=1, source_target_pairs={{0,1},{1,0},{2,3},{3,2},{4,5},{5,4},{6,7},{7,6},{8,9},{9,8},{10,11... | collective-permute-start | bytes 584 | tf_op jit(solution)/shard_map/ppermute | solution.py:424
  1.1 5.3 %collective-permute-start.2 = (s32[8,6]{1,0:T(8,128)}, s32[8,6]{1,0:T(8,128)S(1)}, u32[]{:S(2)}, u32[]{:S(2)}) collective-permute-start(s32[8,6]{1,0:T(8,128)} %param.3), channel_id=1, source_target_pairs={{0,3},{1,2},{2,1},{3,0},{4,7},{5,6},{6,5},{7,4},{8,11},{9,10},{10,... | collective-permute-start | bytes 584 | tf_op jit(solution)/shard_map/ppermute | solution.py:424
  3.8 3.8 %collective-permute-start.1 = (s32[8,6]{1,0:T(8,128)}, s32[8,6]{1,0:T(8,128)S(1)}, u32[]{:S(2)}, u32[]{:S(2)}) collective-permute-start(s32[8,6]{1,0:T(8,128)} %param.3), channel_id=1, source_target_pairs={{0,2},{1,3},{2,0},{3,1},{4,6},{5,7},{6,4},{7,5},{8,10},{9,11},{10,... | collective-permute-start | bytes 584 | tf_op jit(solution)/shard_map/ppermute | solution.py:424
  7.9 8.1 %collective-permute-start.5 = (bf16[16,640]{1,0:T(8,128)(2,1)S(1)}, bf16[16,640]{1,0:T(8,128)(2,1)S(1)}, u32[]{:S(2)}, u32[]{:S(2)}) collective-permute-start(bf16[16,640]{1,0:T(8,128)(2,1)S(1)} %pad_maximum_fusion.5), channel_id=1, source_target_pairs={{0,24},{4,28},{8,16},{12,20},{16,8},{20,12},{24,0},{28,4},{1,25},{... | collective-permute-start | bytes 61448 | tf_op jit(solution)/shard_map/ppermute | solution.py:424
  11.6 5.2 %collective-permute-start.4 = (bf16[16,640]{1,0:T(8,128)(2,1)S(1)}, bf16[16,640]{1,0:T(8,128)(2,1)S(1)}, u32[]{:S(2)}, u32[]{:S(2)}) collective-permute-start(bf16[16,640]{1,0:T(8,128)(2,1)S(1)} %pad_maximum_fusion.5), channel_id=1, source_target_pairs={{0,16},{4,20},{8,24},{12,28},{16,0},{20,4},{24,8},{28,12},{1,17},{... | collective-permute-start | bytes 61448 | tf_op jit(solution)/shard_map/ppermute | solution.py:424
  11.6 5.2 %collective-permute-start.3 = (bf16[16,640]{1,0:T(8,128)(2,1)S(1)}, bf16[16,640]{1,0:T(8,128)(2,1)S(1)}, u32[]{:S(2)}, u32[]{:S(2)}) collective-permute-start(bf16[16,640]{1,0:T(8,128)(2,1)S(1)} %pad_maximum_fusion.5), channel_id=1, source_target_pairs={{0,8},{4,12},{8,0},{12,4},{16,24},{20,28},{24,16},{28,20},{1,9},{5... | collective-permute-start | bytes 61448 | tf_op jit(solution)/shard_map/ppermute | solution.py:424
  12.3 9.8 %collective-permute-start.9 = (f32[32,512]{1,0:T(8,128)S(1)}, f32[32,512]{1,0:T(8,128)S(1)}, u32[]{:S(2)}, u32[]{:S(2)}) collective-permute-start(f32[32,512]{1,0:T(8,128)S(1)} %constant_dynamic-slice_fusion), channel_id=1, source_target_pairs={{0,24},{4,28},{8,16},{12,20},{16,8},{20,12},{24,0},{28,4},{1,25},{... | collective-permute-start | bytes 196616 | tf_op jit(solution)/shard_map/ppermute | solution.py:424
  15.9 6.2 %collective-permute-start.8 = (f32[32,512]{1,0:T(8,128)S(1)}, f32[32,512]{1,0:T(8,128)S(1)}, u32[]{:S(2)}, u32[]{:S(2)}) collective-permute-start(f32[32,512]{1,0:T(8,128)S(1)} %constant_dynamic-slice_fusion), channel_id=1, source_target_pairs={{0,16},{4,20},{8,24},{12,28},{16,0},{20,4},{24,8},{28,12},{1,17},{... | collective-permute-start | bytes 196616 | tf_op jit(solution)/shard_map/ppermute | solution.py:424
  15.9 6.2 %collective-permute-start.7 = (f32[32,512]{1,0:T(8,128)S(1)}, f32[32,512]{1,0:T(8,128)S(1)}, u32[]{:S(2)}, u32[]{:S(2)}) collective-permute-start(f32[32,512]{1,0:T(8,128)S(1)} %constant_dynamic-slice_fusion), channel_id=1, source_target_pairs={{0,8},{4,12},{8,0},{12,4},{16,24},{20,28},{24,16},{28,20},{1,9},{5... | collective-permute-start | bytes 196616 | tf_op jit(solution)/shard_map/ppermute | solution.py:424
  16.8 5.4 %collective-permute-start.6 = (bf16[4,16,640]{2,1,0:T(8,128)(2,1)S(1)}, bf16[4,16,640]{2,1,0:T(8,128)(2,1)S(1)}, u32[]{:S(2)}, u32[]{:S(2)}) collective-permute-start(bf16[4,16,640]{2,1,0:T(8,128)(2,1)S(1)} %pad_maximum_fusion.4.refs_1_), channel_id=1, source_target_pairs={{0,4},{4,0},{8,12},{12,8},{16,20},{20,16},{24,28},{28,24},{1,5},{5... | collective-permute-start | bytes 245768 | tf_op jit(solution)/shard_map/ppermute | solution.py:424
  26.1 21.5 %copy-start = (f32[32,2048]{1,0:T(8,128)S(1)}, f32[32,2048]{1,0:T(8,128)}, u32[]{:S(2)}) copy-start(f32[32,2048]{1,0:T(8,128)} %t_ref.5) | copy-start | bytes 786436
  26.1 4.8 %collective-permute-start.13 = (f32[16,256]{1,0:T(8,128)S(1)}, f32[16,256]{1,0:T(8,128)S(1)}, u32[]{:S(2)}, u32[]{:S(2)}) collective-permute-start(f32[16,256]{1,0:T(8,128)S(1)} %get-tuple-element.56), channel_id=1, source_target_pairs={{0,12},{4,8},{8,4},{12,0},{16,28},{20,24},{24,20},{28,16},{1,13},{... | collective-permute-start | bytes 49160 | tf_op jit(solution)/shard_map/ppermute | solution.py:424
  27.4 3.7 %collective-permute-start.12 = (f32[16,256]{1,0:T(8,128)S(1)}, f32[16,256]{1,0:T(8,128)S(1)}, u32[]{:S(2)}, u32[]{:S(2)}) collective-permute-start(f32[16,256]{1,0:T(8,128)S(1)} %get-tuple-element.56), channel_id=1, source_target_pairs={{0,8},{4,12},{8,0},{12,4},{16,24},{20,28},{24,16},{28,20},{1,9},{5... | collective-permute-start | bytes 49160 | tf_op jit(solution)/shard_map/ppermute | solution.py:424
  28.2 4.0 %collective-permute-start.11 = (f32[16,256]{1,0:T(8,128)S(1)}, f32[16,256]{1,0:T(8,128)S(1)}, u32[]{:S(2)}, u32[]{:S(2)}) collective-permute-start(f32[16,256]{1,0:T(8,128)S(1)} %get-tuple-element.56), channel_id=1, source_target_pairs={{0,4},{4,0},{8,12},{12,8},{16,20},{20,16},{24,28},{28,24},{1,5},{5... | collective-permute-start | bytes 49160 | tf_op jit(solution)/shard_map/ppermute | solution.py:424
  29.7 7.3 %collective-permute-start.10 = (f32[4,32,512]{2,1,0:T(8,128)S(1)}, f32[4,32,512]{2,1,0:T(8,128)S(1)}, u32[]{:S(2)}, u32[]{:S(2)}) collective-permute-start(f32[4,32,512]{2,1,0:T(8,128)S(1)} %pad_maximum_fusion.refs_2_.t_same), channel_id=1, source_target_pairs={{0,4},{4,0},{8,12},{12,8},{16,20},{20,16},{24,28},{28,24},{1,5},{5... | collective-permute-start | bytes 786440 | tf_op jit(solution)/shard_map/ppermute | solution.py:424
  32.2 4.7 %collective-permute-start.14 = (f32[16,256]{1,0:T(8,128)S(1)}, f32[16,256]{1,0:T(8,128)S(1)}, u32[]{:S(2)}, u32[]{:S(2)}) collective-permute-start(f32[16,256]{1,0:T(8,128)S(1)} %add_add_fusion.1), channel_id=1, source_target_pairs={{0,16},{4,20},{8,24},{12,28},{16,0},{20,4},{24,8},{28,12},{1,17},{... | collective-permute-start | bytes 49160 | tf_op jit(solution)/shard_map/ppermute | solution.py:424
  40.0 1.4 %collective-permute-start.15 = (f32[2,32,512]{2,1,0:T(8,128)S(1)}, f32[2,32,512]{2,1,0:T(8,128)S(1)}, u32[]{:S(2)}, u32[]{:S(2)}) collective-permute-start(f32[2,32,512]{2,1,0:T(8,128)S(1)} %get-tuple-element.58), channel_id=1, source_target_pairs={{0,1},{1,0},{2,3},{3,2},{4,5},{5,4},{6,7},{7,6},{8,9},{9,8},{10,11... | collective-permute-start | bytes 393224 | tf_op jit(solution)/shard_map/ppermute | solution.py:424
  41.5 6.0 %collective-permute-start.16 = (f32[72,512]{1,0:T(8,128)S(1)}, f32[72,512]{1,0:T(8,128)S(1)}, u32[]{:S(2)}, u32[]{:S(2)}) collective-permute-start(f32[72,512]{1,0:T(8,128)S(1)} %pad_maximum_fusion.2), channel_id=1, source_target_pairs={{0,2},{1,3},{2,0},{3,1},{4,6},{5,7},{6,4},{7,5},{8,10},{9,11},{10,... | collective-permute-start | bytes 442376 | tf_op jit(solution)/shard_map/ppermute | solution.py:424
  47.5 1.5 %collective-permute-start.17 = (f32[2,40,512]{2,1,0:T(8,128)S(1)}, f32[2,40,512]{2,1,0:T(8,128)S(1)}, u32[]{:S(2)}, u32[]{:S(2)}) collective-permute-start(f32[2,40,512]{2,1,0:T(8,128)S(1)} %pad_maximum_fusion.1.s1_own), channel_id=1, source_target_pairs={{0,1},{1,0},{2,3},{3,2},{4,5},{5,4},{6,7},{7,6},{8,9},{9,8},{10,11... | collective-permute-start | bytes 491528 | tf_op jit(solution)/shard_map/ppermute | solution.py:424
  50.6 11.0 %collective-permute-start.18 = (bf16[4,32,512]{2,1,0:T(8,128)(2,1)S(1)}, bf16[4,32,512]{2,1,0:T(8,128)(2,1)S(1)}, u32[]{:S(2)}, u32[]{:S(2)}) collective-permute-start(bf16[4,32,512]{2,1,0:T(8,128)(2,1)S(1)} %second.3), channel_id=1, source_target_pairs={{0,4},{4,0},{8,12},{12,8},{16,20},{20,16},{24,28},{28,24},{1,5},{5... | collective-permute-start | bytes 393224 | tf_op jit(solution)/shard_map/ppermute | solution.py:424
  51.8 6.8 %collective-permute-start.21 = (bf16[32,512]{1,0:T(8,128)(2,1)S(1)}, bf16[32,512]{1,0:T(8,128)(2,1)S(1)}, u32[]{:S(2)}, u32[]{:S(2)}) collective-permute-start(bf16[32,512]{1,0:T(8,128)(2,1)S(1)} %fusion.2.refs_0_), channel_id=1, source_target_pairs={{0,24},{4,28},{8,16},{12,20},{16,8},{20,12},{24,0},{28,4},{1,25},{... | collective-permute-start | bytes 98312 | tf_op jit(solution)/shard_map/ppermute | solution.py:424
  56.7 4.8 %collective-permute-start.20 = (bf16[32,512]{1,0:T(8,128)(2,1)S(1)}, bf16[32,512]{1,0:T(8,128)(2,1)S(1)}, u32[]{:S(2)}, u32[]{:S(2)}) collective-permute-start(bf16[32,512]{1,0:T(8,128)(2,1)S(1)} %fusion.2.refs_0_), channel_id=1, source_target_pairs={{0,16},{4,20},{8,24},{12,28},{16,0},{20,4},{24,8},{28,12},{1,17},{... | collective-permute-start | bytes 98312 | tf_op jit(solution)/shard_map/ppermute | solution.py:424
  56.7 4.8 %collective-permute-start.19 = (bf16[32,512]{1,0:T(8,128)(2,1)S(1)}, bf16[32,512]{1,0:T(8,128)(2,1)S(1)}, u32[]{:S(2)}, u32[]{:S(2)}) collective-permute-start(bf16[32,512]{1,0:T(8,128)(2,1)S(1)} %fusion.2.refs_0_), channel_id=1, source_target_pairs={{0,8},{4,12},{8,0},{12,4},{16,24},{20,28},{24,16},{28,20},{1,9},{5... | collective-permute-start | bytes 98312 | tf_op jit(solution)/shard_map/ppermute | solution.py:424
  61.7 5.9 %collective-permute-start.22 = (bf16[32,640]{1,0:T(8,128)(2,1)S(1)}, bf16[32,640]{1,0:T(8,128)(2,1)S(1)}, u32[]{:S(2)}, u32[]{:S(2)}) collective-permute-start(bf16[32,640]{1,0:T(8,128)(2,1)S(1)} %get-tuple-element.71), channel_id=1, source_target_pairs={{0,24},{4,28},{8,16},{12,20},{16,8},{20,12},{24,0},{28,4},{1,25},{... | collective-permute-start | bytes 122888 | tf_op jit(solution)/shard_map/ppermute | solution.py:424
  63.2 4.9 %collective-permute-start.23 = (bf16[32,640]{1,0:T(8,128)(2,1)S(1)}, bf16[32,640]{1,0:T(8,128)(2,1)S(1)}, u32[]{:S(2)}, u32[]{:S(2)}) collective-permute-start(bf16[32,640]{1,0:T(8,128)(2,1)S(1)} %get-tuple-element.72), channel_id=1, source_target_pairs={{0,16},{4,20},{8,24},{12,28},{16,0},{20,4},{24,8},{28,12},{1,17},{... | collective-permute-start | bytes 122888 | tf_op jit(solution)/shard_map/ppermute | solution.py:424
  63.9 4.7 %collective-permute-start.24 = (bf16[32,640]{1,0:T(8,128)(2,1)S(1)}, bf16[32,640]{1,0:T(8,128)(2,1)S(1)}, u32[]{:S(2)}, u32[]{:S(2)}) collective-permute-start(bf16[32,640]{1,0:T(8,128)(2,1)S(1)} %get-tuple-element.73), channel_id=1, source_target_pairs={{0,8},{4,12},{8,0},{12,4},{16,24},{20,28},{24,16},{28,20},{1,9},{5... | collective-permute-start | bytes 122888 | tf_op jit(solution)/shard_map/ppermute | solution.py:424
  68.7 4.7 %collective-permute-start.28 = (f32[32,128]{1,0:T(8,128)S(1)}, f32[32,128]{1,0:T(8,128)S(1)}, u32[]{:S(2)}, u32[]{:S(2)}) collective-permute-start(f32[32,128]{1,0:T(8,128)S(1)} %get-tuple-element.75), channel_id=1, source_target_pairs={{0,6},{1,7},{2,4},{3,5},{4,2},{5,3},{6,0},{7,1},{8,14},{9,15},{10,... | collective-permute-start | bytes 49160 | tf_op jit(solution)/shard_map/ppermute | solution.py:434
  69.7 3.8 %collective-permute-start.27 = (f32[32,128]{1,0:T(8,128)S(1)}, f32[32,128]{1,0:T(8,128)S(1)}, u32[]{:S(2)}, u32[]{:S(2)}) collective-permute-start(f32[32,128]{1,0:T(8,128)S(1)} %get-tuple-element.75), channel_id=1, source_target_pairs={{0,2},{1,3},{2,0},{3,1},{4,6},{5,7},{6,4},{7,5},{8,10},{9,11},{10,... | collective-permute-start | bytes 49160 | tf_op jit(solution)/shard_map/ppermute | solution.py:424
  70.7 3.7 %collective-permute-start.26 = (f32[32,128]{1,0:T(8,128)S(1)}, f32[32,128]{1,0:T(8,128)S(1)}, u32[]{:S(2)}, u32[]{:S(2)}) collective-permute-start(f32[32,128]{1,0:T(8,128)S(1)} %get-tuple-element.75), channel_id=1, source_target_pairs={{0,4},{4,0},{8,12},{12,8},{16,20},{20,16},{24,28},{28,24},{1,5},{5... | collective-permute-start | bytes 49160 | tf_op jit(solution)/shard_map/ppermute | solution.py:424
  72.2 4.3 %collective-permute-start.25 = (f32[32,512]{1,0:T(8,128)S(1)}, f32[32,512]{1,0:T(8,128)S(1)}, u32[]{:S(2)}, u32[]{:S(2)}) collective-permute-start(f32[32,512]{1,0:T(8,128)S(1)} %get-tuple-element.74), channel_id=1, source_target_pairs={{0,2},{1,3},{2,0},{3,1},{4,6},{5,7},{6,4},{7,5},{8,10},{9,11},{10,... | collective-permute-start | bytes 196616 | tf_op jit(solution)/shard_map/ppermute | solution.py:424
  76.5 1.4 %collective-permute-start.29 = (f32[2,32,512]{2,1,0:T(8,128)S(1)}, f32[2,32,512]{2,1,0:T(8,128)S(1)}, u32[]{:S(2)}, u32[]{:S(2)}) collective-permute-start(f32[2,32,512]{2,1,0:T(8,128)S(1)} %pad_maximum_fusion.3.refs_0_), channel_id=1, source_target_pairs={{0,1},{1,0},{2,3},{3,2},{4,5},{5,4},{6,7},{7,6},{8,9},{9,8},{10,11... | collective-permute-start | bytes 393224 | tf_op jit(solution)/shard_map/ppermute | solution.py:424
  76.5 1.4 %collective-permute-start.30 = (f32[32,128]{1,0:T(8,128)S(1)}, f32[32,128]{1,0:T(8,128)S(1)}, u32[]{:S(2)}, u32[]{:S(2)}) collective-permute-start(f32[32,128]{1,0:T(8,128)S(1)} %add_add_fusion.refs_2_), channel_id=1, source_target_pairs={{0,1},{1,0},{2,3},{3,2},{4,5},{5,4},{6,7},{7,6},{8,9},{9,8},{10,11... | collective-permute-start | bytes 49160 | tf_op jit(solution)/shard_map/ppermute | solution.py:424

commit v14 on v13

--- a/solution.py
+++ b/solution.py
@@ -166,6 +166,7 @@
         dist[slot] = jnp.dot(lhs[i], rhs[j], preferred_element_type=F32)
 
     distances(0, 0)
+    ones = jnp.ones((8, block_len), BF16)
 
     def step(g, carry):
         slot, target = (base + g, k_mat) if cfg.resident else (lax.rem(g, RING), kbuf)
@@ -179,7 +180,7 @@
             distances(g * GROUP + u + 1, (u + 1) % 2)
             j = listed[0, g * GROUP + u + 1] & (CODE - 1)
             m = mlist[g * GROUP + u].astype(F32)
-            sums = jnp.zeros((8, block_len), F32)
+            strips = []
             for s in range(block_len // STRIP):
                 rows = slice(s * STRIP, (s + 1) * STRIP)
                 d = jnp.maximum(dist[u % 2, rows, :], TINY)
@@ -187,19 +188,19 @@
                 rem = jnp.maximum(1.0 - sc, 0.0)
                 sq = rem * rem
                 val = (sq * sq) * (sc * (4.0 * m) + m)
-                target[slot, u, rows, :] = val.astype(BF16)
-                for h in range(0, STRIP, 8):
-                    sums = sums + val[h:h + 8]
-            acc[j] += sums
+                strips.append(val.astype(BF16))
+                target[slot, u, rows, :] = strips[-1]
+            block = jnp.concatenate(strips, axis=0)
+            acc[j] += jnp.dot(ones, block, preferred_element_type=F32)
         if not cfg.resident:
             copy_out(g).start()
         return carry
 
     lax.fori_loop(0, total, step, 0)
     if cfg.parts == 1 or not last:
-        deg_ref[...] = jnp.sum(acc[...], axis=1)
+        deg_ref[...] = acc[:, 0, :]
     else:
-        second = jnp.sum(acc[...], axis=1)
+        second = acc[:, 0, :]
         for z in range(held):
             rows = slice(z * own_rows, (z + 1) * own_rows)
             for p, deg in enumerate((first_deg[rows, :], second[rows])):
@@ -373,27 +374,28 @@
 
 
 def product_kernel(own_z, own_dots, s1_own, *refs):
-    got, grown_ref, dot_ref = refs[2::-1], refs[3], refs[4]
-    outputs, own_len = grown_ref.shape
+    got, end_ref, dot_ref = refs[2::-1], refs[3], refs[4]
+    outputs, own_len = own_z.shape
     z = own_z[...]
     for ref in got:
         z = z + ref[:, :own_len].astype(F32)
-    grown_ref[...] = z * s1_own[0, outputs:outputs + 1, :]
+    end_ref[:, :own_len] = z * s1_own[0, outputs:outputs + 1, :]
     tiles = [own_dots[...]] + [ref[:, own_len:] for ref in got]
     total = pair_sum([tile.astype(F32) for tile in tiles])
     out = total
     for part in range(1, 3):
         out = out + pltpu.roll(total, LANES - part * N_DOTS, 1)
     dot_ref[...] = out
+    end_ref[:, own_len:] = out
 
 
 def final_kernel(t_ref, s1_own, s1_got, *refs):
-    grown, all_dots = pieces_of(refs[0], refs[1]), refs[2:4]
-    sol_hbm, res_hbm, sol_ref, res_ref, sems = refs[4:]
+    ends = pieces_of(refs[0], refs[1])
+    sol_hbm, res_hbm, sol_ref, res_ref, sems = refs[2:]
     s1s = pieces_of(s1_own, s1_got)
-    outputs, own_len = grown[0].shape
+    outputs, own_len = ends[0].shape[0], ends[0].shape[1] - LANES
     place = position()
-    dots = pair_sum([ref[...] for ref in all_dots])
+    dots = ends[0][:, own_len:] + ends[1][:, own_len:]
     tt, ts1, s1s1, ts2, s1s2 = (dots[:, n:n + 1] for n in range(5))
     a1 = tt / (REG * tt + ts1)
     p = 1.0 - REG * a1
@@ -408,7 +410,7 @@
     for e in range(4):
         at = pl.ds(pl.multiple_of((place[1] ^ e) * own_len, LANES), own_len)
         t, s1 = t_ref[:, at], s1s[e][:outputs, :]
-        s2 = grown[e][...] + SHIFT * s1
+        s2 = ends[e][:, :own_len] + SHIFT * s1
         sol_ref[e] = sol_t * t - sol_1 * s1
         res_ref[e] = res_t * t - res_1 * s1 + sol_1 * s2
         for n, (ref, hbm) in enumerate(((sol_ref, sol_hbm), (res_ref, res_hbm))):
@@ -626,16 +628,18 @@
             name="meet",
         )(z2_same, z2_other, t_pieces[0], inv, s1_own, *gs)
         got = [swap(sends[n], "rows", 2 * n + 2) for n in (2, 1, 0)]
-        grown, dots = pl.pallas_call(
+        ends, dots = pl.pallas_call(
             product_kernel,
-            out_shape=(shape(outputs, own_len), shape(outputs, LANES)),
+            out_shape=(shape(outputs, own_len + LANES), shape(outputs, LANES)),
             in_specs=[VMEM] * 6,
             out_specs=(VMEM, VMEM),
             compiler_params=limit,
             name="products",
         )(own_z, own_dots, s1_own, *got)
         far = both_swap(dots, 1, 2)
-        dots = pair_sum([dots, swap(dots, "rows", 1), swap(dots, "cols", 2), far])
+        across = swap(dots, "rows", 1)
+        ends_y = swap(ends, "cols", 2)
+        dots = (dots + across) + (ends_y[:, own_len:] + far)
     else:
         z2 = lax.psum_scatter(second(0, F32), "rows", scatter_dimension=0)
         grown = z2 * tail[:1]
@@ -644,16 +648,17 @@
         dots = [(own_t, own_t), (own_t, own_s1), (own_s1, own_s1), (own_t, s2), (own_s1, s2)]
         dots = jnp.stack([jnp.sum(x * y, axis=1) for x, y in dots], axis=1)
         dots = lax.psum(jnp.pad(dots, ((0, 0), (0, LANES - N_DOTS))), "rows")
-        dots = dots + swap(dots, "cols", 2)
-    grown = jnp.stack([grown, swap(grown, "cols", 2)])
-    grown, dots = lax.optimization_barrier((grown, dots))
-    ends = (s1_own, s1_got, grown, swap(grown, "cols", 1), dots, swap(dots, "cols", 1))
+        ends = jnp.concatenate([grown, dots], axis=1)
+        ends_y = swap(ends, "cols", 2)
+        dots = dots + ends_y[:, own_len:]
+    ends = jnp.stack([jnp.concatenate([ends[:, :own_len], dots], axis=1), ends_y])
+    ends = (s1_own, s1_got, ends, swap(ends, "cols", 1))
     ends = [pltpu.with_memory_space_constraint(x, pltpu.VMEM) for x in ends]
 
     return pl.pallas_call(
         final_kernel,
         out_shape=(shape(outputs, npoints), shape(outputs, npoints)),
-        in_specs=[VMEM] * 7,
+        in_specs=[VMEM] * 5,
         out_specs=(HBM, HBM),
         scratch_shapes=[
             pltpu.VMEM((4, outputs, own_len), F32),

time: 78.8 us -> 77.3 us (0.981)
  starting transfers between devices: 38.8 us -> 36.8 us
    ppermute x30 -> x28, waiting for transfers between devices: 20.8 us -> 18.1 us  [swap(): return lax.ppermute(x, axis, [(i, i ^ d) for i in range(size)])]
    ppermute x30 -> x28, starting transfers between devices: 37.7 us -> 35.5 us  [swap(): return lax.ppermute(x, axis, [(i, i ^ d) for i in range(size)])]
    ppermute x1, waiting for transfers between devices: 0.15 us -> 2.2 us  [both_swap(): return lax.ppermute(x, ('rows', 'cols'), pairs)]
  transfers between devices with their start and end apart: 31 -> 29, of which waited for: 17 -> 15; matrix products, arithmetic and copies ran while one was open for 4% -> 4% of each run, Pallas kernels for 7% -> 8%
where the time goes in v14:
time: 77.3 us; the launch traced here: 76.9 us
  starting transfers between devices  36.8 us (48%)
  waiting for transfers between devices  20.3 us (26%)
  Pallas kernels  15.7 us (20%)
  local copies, waits for them, and re-layouts  2.75 us (4%)
  between operations  0.88 us (1%)
    ppermute x28, starting transfers between devices, swap(): return lax.ppermute(x, axis, [(i, i ^ d) for i in range(size)])  35.5 us
    ppermute x28, waiting for transfers between devices, swap(): return lax.ppermute(x, axis, [(i, i ^ d) for i in range(size)])  18.1 us
    pallas_call x2, Pallas kernels, build(): pl.pallas_call(functools.partial(build_kernel, cfg, part), out_shape=out,...  8.21 us
    pallas_call x1, Pallas kernels, local(): pl.pallas_call(functools.partial(first_kernel, cfg), out_shape=[shape(out...  3.06 us
    pallas_call x2, Pallas kernels, second(): pl.pallas_call(functools.partial(second_kernel, cfg, part), out_shape=sha...  3.01 us
    ppermute x1, waiting for transfers between devices, both_swap(): return lax.ppermute(x, ('rows', 'cols'), pairs)  2.2 us
    dynamic_slice x2, local copies, waits for them, and re-layouts, own(): return lax.dynamic_slice_in_dim(x, col * own_len, own_len, 1)  1.56 us
  transfers between devices with their start and end apart: 29, of which 15 were waited for; matrix products, arithmetic and copies ran while one was open for 4% of the time, Pallas kernels for 8%

profile of v14, /device:TPU:0, one launch (start us, length us, event | category | flops | bytes accessed | tf_op | source)
XLA Modules:
  0.0 76.9 jit_solution(6837069112722036731)
XLA Ops:
  0.6 0.5 collective-permute-start
  1.1 2.6 %collective-permute-start.2 = (s32[8,6]{1,0:T(8,128)}, s32[8,6]{1,0:T(8,128)S(1)}, u32[]{:S(2)}, u32[]{:S(2)}) collective-permute-start(s32[8,6]{1,0:T(8,128)} %param.3), channel_id=1, source_target_pairs={{0,3},{1,2},{2,1},{3,0},{4,7},{5,6},{6,5},{7,4},{8,11},{9,10},{10,... | collective-permute-start | bytes 584 | tf_op jit(solution)/shard_map/ppermute | solution.py:426
  3.8 0.8 %copy.6 = s32[8,6]{0,1:T(8,128)S(1)} copy(s32[8,6]{1,0:T(8,128)} %param.3) | data formatting | bytes 384 | tf_op args[0]
  4.7 0.7 constant_dynamic-slice_fusion.1
  5.5 0.8 %constant_dynamic-slice_fusion = f32[32,512]{1,0:T(8,128)S(1)} fusion(f32[32,2048]{1,0:T(8,128)} %t_ref.5, s32[]{:T(128)S(6)} %select_n.7), kind=kLoop, calls=%fused_computation.36 | loop fusion | bytes 131076 | tf_op jit(solution)/shard_map/dynamic_slice | solution.py:487
  6.6 1.0 %collective-permute-done.1 = s32[8,6]{1,0:T(8,128)S(1)} collective-permute-done((s32[8,6]{1,0:T(8,128)}, s32[8,6]{1,0:T(8,128)S(1)}, u32[]{:S(2)}, u32[]{:S(2)}) %collective-permute-start.1) | collective-permute-done | bytes 224 | tf_op jit(solution)/shard_map/ppermute | solution.py:426
  7.9 3.7 %collective-permute-start.5 = (bf16[16,640]{1,0:T(8,128)(2,1)S(1)}, bf16[16,640]{1,0:T(8,128)(2,1)S(1)}, u32[]{:S(2)}, u32[]{:S(2)}) collective-permute-start(bf16[16,640]{1,0:T(8,128)(2,1)S(1)} %pad_maximum_fusion.5), channel_id=1, source_target_pairs={{0,24},{4,28},{8,16},{12,20},{16,8},{20,12},{24,0},{28,4},{1,25},{... | collective-permute-start | bytes 61448 | tf_op jit(solution)/shard_map/ppermute | solution.py:426
  11.6 0.8 %collective-permute-start.3 = (bf16[16,640]{1,0:T(8,128)(2,1)S(1)}, bf16[16,640]{1,0:T(8,128)(2,1)S(1)}, u32[]{:S(2)}, u32[]{:S(2)}) collective-permute-start(bf16[16,640]{1,0:T(8,128)(2,1)S(1)} %pad_maximum_fusion.5), channel_id=1, source_target_pairs={{0,8},{4,12},{8,0},{12,4},{16,24},{20,28},{24,16},{28,20},{1,9},{5... | collective-permute-start | bytes 61448 | tf_op jit(solution)/shard_map/ppermute | solution.py:426
  12.3 3.6 %collective-permute-start.9 = (f32[32,512]{1,0:T(8,128)S(1)}, f32[32,512]{1,0:T(8,128)S(1)}, u32[]{:S(2)}, u32[]{:S(2)}) collective-permute-start(f32[32,512]{1,0:T(8,128)S(1)} %constant_dynamic-slice_fusion), channel_id=1, source_target_pairs={{0,24},{4,28},{8,16},{12,20},{16,8},{20,12},{24,0},{28,4},{1,25},{... | collective-permute-start | bytes 196616 | tf_op jit(solution)/shard_map/ppermute | solution.py:426
  15.9 0.8 %collective-permute-start.7 = (f32[32,512]{1,0:T(8,128)S(1)}, f32[32,512]{1,0:T(8,128)S(1)}, u32[]{:S(2)}, u32[]{:S(2)}) collective-permute-start(f32[32,512]{1,0:T(8,128)S(1)} %constant_dynamic-slice_fusion), channel_id=1, source_target_pairs={{0,8},{4,12},{8,0},{12,4},{16,24},{20,28},{24,16},{28,20},{1,9},{5... | collective-permute-start | bytes 196616 | tf_op jit(solution)/shard_map/ppermute | solution.py:426
  16.8 1.6 %collective-permute-start.6 = (bf16[4,16,640]{2,1,0:T(8,128)(2,1)S(1)}, bf16[4,16,640]{2,1,0:T(8,128)(2,1)S(1)}, u32[]{:S(2)}, u32[]{:S(2)}) collective-permute-start(bf16[4,16,640]{2,1,0:T(8,128)(2,1)S(1)} %pad_maximum_fusion.4.refs_1_), channel_id=1, source_target_pairs={{0,4},{4,0},{8,12},{12,8},{16,20},{20,16},{24,28},{28,24},{1,5},{5... | collective-permute-start | bytes 245768 | tf_op jit(solution)/shard_map/ppermute | solution.py:426
  18.3 4.6 %build.2 = (bf16[32,4,256,256]{3,2,1,0:T(8,128)(2,1)S(1)}, s32[1,128]{1,0:T(1,128)S(1)}, f32[8,256]{1,0:T(8,128)S(1)}, bf16[8,256,32]{2,1,0:T(8,128)(2,1)S(1)}) custom-call(s32[8,64]{1,0:T(8,128)S(1)} %add_add_fusion.1.direct_v, bf16[16,2048]{1,0:T(8,128)(2,1)} %refs_0_.1, bf16[4,16,640]{2,1,0:T(8,128)(2,1)S(1)} %pad_maximum_fusion.4.refs_1_), custom_call_target="tpu_custom_call" | custom-call | flops 2684354560 | bytes 83886080 | tf_op jit(solution)/shard_map/build/pallas_call | solution.py:512
  23.0 3.6 %build.3 = (bf16[32,4,256,256]{3,2,1,0:T(8,128)(2,1)S(1)}, s32[1,128]{1,0:T(1,128)S(1)}, f32[16,256]{1,0:T(8,128)S(1)}) custom-call(s32[8,64]{1,0:T(8,128)S(1)} %add_add_fusion.1.direct_v, bf16[8,256,32]{2,1,0:T(8,128)(2,1)S(1)} %get-tuple-element.39.refs_0_, f32[8,256]{1,0:T(8,128)S(1)} %get-tuple-element.42.refs_1_, ...), custom_call_target="tpu_custom_call", output_to_operand_aliasing={{0}: (4, {})} | custom-call | flops 2684354560 | bytes 83886080 | tf_op jit(solution)/shard_map/build/pallas_call | solution.py:512
  26.6 1.3 %collective-permute-start.13 = (f32[16,256]{1,0:T(8,128)S(1)}, f32[16,256]{1,0:T(8,128)S(1)}, u32[]{:S(2)}, u32[]{:S(2)}) collective-permute-start(f32[16,256]{1,0:T(8,128)S(1)} %get-tuple-element.54), channel_id=1, source_target_pairs={{0,12},{4,8},{8,4},{12,0},{16,28},{20,24},{24,20},{28,16},{1,13},{... | collective-permute-start | bytes 49160 | tf_op jit(solution)/shard_map/ppermute | solution.py:426
  27.9 0.6 collective-permute-start.12
  28.5 1.7 %collective-permute-start.11 = (f32[16,256]{1,0:T(8,128)S(1)}, f32[16,256]{1,0:T(8,128)S(1)}, u32[]{:S(2)}, u32[]{:S(2)}) collective-permute-start(f32[16,256]{1,0:T(8,128)S(1)} %get-tuple-element.54), channel_id=1, source_target_pairs={{0,4},{4,0},{8,12},{12,8},{16,20},{20,16},{24,28},{28,24},{1,5},{5... | collective-permute-start | bytes 49160 | tf_op jit(solution)/shard_map/ppermute | solution.py:426
  30.2 0.3 collective-permute-start.10
  30.5 0.9 %collective-permute-done.13 = f32[16,256]{1,0:T(8,128)S(1)} collective-permute-done((f32[16,256]{1,0:T(8,128)S(1)}, f32[16,256]{1,0:T(8,128)S(1)}, u32[]{:S(2)}, u32[]{:S(2)}) %collective-permute-start.13) | collective-permute-done | bytes 16416 | tf_op jit(solution)/shard_map/ppermute | solution.py:426
  31.4 0.2 collective-permute-done.12
  31.6 0.8 %collective-permute-done.11 = f32[16,256]{1,0:T(8,128)S(1)} collective-permute-done((f32[16,256]{1,0:T(8,128)S(1)}, f32[16,256]{1,0:T(8,128)S(1)}, u32[]{:S(2)}, u32[]{:S(2)}) %collective-permute-start.11) | collective-permute-done | bytes 16416 | tf_op jit(solution)/shard_map/ppermute | solution.py:426
  32.5 3.0 %collective-permute-start.14 = (f32[16,256]{1,0:T(8,128)S(1)}, f32[16,256]{1,0:T(8,128)S(1)}, u32[]{:S(2)}, u32[]{:S(2)}) collective-permute-start(f32[16,256]{1,0:T(8,128)S(1)} %add_add_fusion), channel_id=1, source_target_pairs={{0,16},{4,20},{8,24},{12,28},{16,0},{20,4},{24,8},{28,12},{1,17},{... | collective-permute-start | bytes 49160 | tf_op jit(solution)/shard_map/ppermute | solution.py:426
  35.5 1.7 %collective-permute-done.14 = f32[16,256]{1,0:T(8,128)S(1)} collective-permute-done((f32[16,256]{1,0:T(8,128)S(1)}, f32[16,256]{1,0:T(8,128)S(1)}, u32[]{:S(2)}, u32[]{:S(2)}) %collective-permute-start.14) | collective-permute-done | bytes 16416 | tf_op jit(solution)/shard_map/ppermute | solution.py:426
  37.2 3.1 %first.1 = (f32[32,512]{1,0:T(8,128)S(1)}, f32[32,512]{1,0:T(8,128)S(1)}, f32[2,32,512]{2,1,0:T(8,128)S(1)}, f32[8,512]{1,0:T(8,128)S(1)}) custom-call(bf16[32,4,256,256]{3,2,1,0:T(8,128)(2,1)S(1)} %get-tuple-element.50.k_mat, s32[1,128]{1,0:T(1,128)S(1)} %get-tuple-element.51.refs_0_.list_v, s32[1,128]{1,0:T(1,128)S(1)} %get-tuple-element.52.refs_1_.list_v, ...), custom_call_target="tpu_custom_call" | custom-call | flops 536870912 | bytes 8388608 | tf_op jit(solution)/shard_map/first/pallas_call | solution.py:568
  40.4 1.3 %collective-permute-done.15 = f32[2,32,512]{2,1,0:T(8,128)S(1)} collective-permute-done((f32[2,32,512]{2,1,0:T(8,128)S(1)}, f32[2,32,512]{2,1,0:T(8,128)S(1)}, u32[]{:S(2)}, u32[]{:S(2)}) %collective-permute-start.15) | collective-permute-done | bytes 131104 | tf_op jit(solution)/shard_map/ppermute | solution.py:426
  41.7 2.2 %collective-permute-start.16 = (f32[72,512]{1,0:T(8,128)S(1)}, f32[72,512]{1,0:T(8,128)S(1)}, u32[]{:S(2)}, u32[]{:S(2)}) collective-permute-start(f32[72,512]{1,0:T(8,128)S(1)} %pad_maximum_fusion.3), channel_id=1, source_target_pairs={{0,2},{1,3},{2,0},{3,1},{4,6},{5,7},{6,4},{7,5},{8,10},{9,11},{10,... | collective-permute-start | bytes 442376 | tf_op jit(solution)/shard_map/ppermute | solution.py:426
  44.0 4.2 %collective-permute-done.16 = f32[72,512]{1,0:T(8,128)S(1)} collective-permute-done((f32[72,512]{1,0:T(8,128)S(1)}, f32[72,512]{1,0:T(8,128)S(1)}, u32[]{:S(2)}, u32[]{:S(2)}) %collective-permute-start.16) | collective-permute-done | bytes 147488 | tf_op jit(solution)/shard_map/ppermute | solution.py:426
  48.3 1.3 %collective-permute-done.17.s1_got = f32[2,40,512]{2,1,0:T(8,128)S(1)} collective-permute-done((f32[2,40,512]{2,1,0:T(8,128)S(1)}, f32[2,40,512]{2,1,0:T(8,128)S(1)}, u32[]{:S(2)}, u32[]{:S(2)}) %collective-permute-start.17) | collective-permute-done | bytes 163872 | tf_op jit(solution)/shard_map/ppermute | solution.py:426
  49.7 1.4 %second.3 = bf16[4,32,512]{2,1,0:T(8,128)(2,1)S(1)} custom-call(bf16[32,4,256,256]{3,2,1,0:T(8,128)(2,1)S(1)} %get-tuple-element.50.k_mat, s32[1,128]{1,0:T(1,128)S(1)} %get-tuple-element.52.refs_1_.list_v, f32[32,2048]{1,0:T(8,128)S(1)} %copy-done, f32[2,40,512]{2,1,0:T(8,128)S(1)} %pad_maximum_fusion.1.s1_own, f32[2,40,512]{2,1,0:T(8,128)S(1)} %collective-permute-done.17.s1_got), custom_call_target="tpu_custom_call" | custom-call | flops 268435456 | bytes 4194304 | tf_op jit(solution)/shard_map/second/pallas_call | solution.py:597
  51.1 1.5 %collective-permute-start.18 = (bf16[4,32,512]{2,1,0:T(8,128)(2,1)S(1)}, bf16[4,32,512]{2,1,0:T(8,128)(2,1)S(1)}, u32[]{:S(2)}, u32[]{:S(2)}) collective-permute-start(bf16[4,32,512]{2,1,0:T(8,128)(2,1)S(1)} %second.3), channel_id=1, source_target_pairs={{0,4},{4,0},{8,12},{12,8},{16,20},{20,16},{24,28},{28,24},{1,5},{5... | collective-permute-start | bytes 393224 | tf_op jit(solution)/shard_map/ppermute | solution.py:426
  52.6 3.6 %collective-permute-start.21 = (bf16[32,512]{1,0:T(8,128)(2,1)S(1)}, bf16[32,512]{1,0:T(8,128)(2,1)S(1)}, u32[]{:S(2)}, u32[]{:S(2)}) collective-permute-start(bf16[32,512]{1,0:T(8,128)(2,1)S(1)} %fusion.2.refs_0_), channel_id=1, source_target_pairs={{0,24},{4,28},{8,16},{12,20},{16,8},{20,12},{24,0},{28,4},{1,25},{... | collective-permute-start | bytes 98312 | tf_op jit(solution)/shard_map/ppermute | solution.py:426
  56.2 0.8 %collective-permute-start.19 = (bf16[32,512]{1,0:T(8,128)(2,1)S(1)}, bf16[32,512]{1,0:T(8,128)(2,1)S(1)}, u32[]{:S(2)}, u32[]{:S(2)}) collective-permute-start(bf16[32,512]{1,0:T(8,128)(2,1)S(1)} %fusion.2.refs_0_), channel_id=1, source_target_pairs={{0,8},{4,12},{8,0},{12,4},{16,24},{20,28},{24,16},{28,20},{1,9},{5... | collective-permute-start | bytes 98312 | tf_op jit(solution)/shard_map/ppermute | solution.py:426
  57.0 1.6 %second.2.z_same = f32[4,32,512]{2,1,0:T(8,128)S(1)} custom-call(bf16[32,4,256,256]{3,2,1,0:T(8,128)(2,1)S(1)} %get-tuple-element.50.k_mat, s32[1,128]{1,0:T(1,128)S(1)} %get-tuple-element.51.refs_0_.list_v, f32[32,2048]{1,0:T(8,128)S(1)} %copy-done, f32[2,40,512]{2,1,0:T(8,128)S(1)} %pad_maximum_fusion.1.s1_own, ...), custom_call_target="tpu_custom_call" | custom-call | flops 268435456 | bytes 4194304 | tf_op jit(solution)/shard_map/second/pallas_call | solution.py:597
  58.6 2.4 %collective-permute-done.20.refs_2_ = bf16[32,512]{1,0:T(8,128)(2,1)S(1)} collective-permute-done((bf16[32,512]{1,0:T(8,128)(2,1)S(1)}, bf16[32,512]{1,0:T(8,128)(2,1)S(1)}, u32[]{:S(2)}, u32[]{:S(2)}) %collective-permute-start.20) | collective-permute-done | bytes 32800 | tf_op jit(solution)/shard_map/ppermute | solution.py:426
  61.0 0.2 meet.1
  61.2 1.5 %collective-permute-start.22 = (bf16[32,640]{1,0:T(8,128)(2,1)S(1)}, bf16[32,640]{1,0:T(8,128)(2,1)S(1)}, u32[]{:S(2)}, u32[]{:S(2)}) collective-permute-start(bf16[32,640]{1,0:T(8,128)(2,1)S(1)} %get-tuple-element.69), channel_id=1, source_target_pairs={{0,24},{4,28},{8,16},{12,20},{16,8},{20,12},{24,0},{28,4},{1,25},{... | collective-permute-start | bytes 122888 | tf_op jit(solution)/shard_map/ppermute | solution.py:426
  62.7 0.6 collective-permute-start.23
  63.3 2.3 %collective-permute-start.24 = (bf16[32,640]{1,0:T(8,128)(2,1)S(1)}, bf16[32,640]{1,0:T(8,128)(2,1)S(1)}, u32[]{:S(2)}, u32[]{:S(2)}) collective-permute-start(bf16[32,640]{1,0:T(8,128)(2,1)S(1)} %get-tuple-element.71), channel_id=1, source_target_pairs={{0,8},{4,12},{8,0},{12,4},{16,24},{20,28},{24,16},{28,20},{1,9},{5... | collective-permute-start | bytes 122888 | tf_op jit(solution)/shard_map/ppermute | solution.py:426
  65.6 1.4 %collective-permute-done.22.refs_0_ = bf16[32,640]{1,0:T(8,128)(2,1)S(1)} collective-permute-done((bf16[32,640]{1,0:T(8,128)(2,1)S(1)}, bf16[32,640]{1,0:T(8,128)(2,1)S(1)}, u32[]{:S(2)}, u32[]{:S(2)}) %collective-permute-start.22) | collective-permute-done | bytes 40992 | tf_op jit(solution)/shard_map/ppermute | solution.py:426
  67.0 0.6 collective-permute-done.23.refs_1_
  67.6 0.4 collective-permute-done.24.refs_2_
  68.0 0.1 products.1
  68.1 1.1 %collective-permute-start.26 = (f32[32,640]{1,0:T(8,128)S(1)}, f32[32,640]{1,0:T(8,128)S(1)}, u32[]{:S(2)}, u32[]{:S(2)}) collective-permute-start(f32[32,640]{1,0:T(8,128)S(1)} %get-tuple-element.72), channel_id=1, source_target_pairs={{0,2},{1,3},{2,0},{3,1},{4,6},{5,7},{6,4},{7,5},{8,10},{9,11},{10,... | collective-permute-start | bytes 245768 | tf_op jit(solution)/shard_map/ppermute | solution.py:426
  69.2 1.3 %collective-permute-start.27 = (f32[32,128]{1,0:T(8,128)S(1)}, f32[32,128]{1,0:T(8,128)S(1)}, u32[]{:S(2)}, u32[]{:S(2)}) collective-permute-start(f32[32,128]{1,0:T(8,128)S(1)} %get-tuple-element.73), channel_id=1, source_target_pairs={{0,6},{1,7},{2,4},{3,5},{4,2},{5,3},{6,0},{7,1},{8,14},{9,15},{10,... | collective-permute-start | bytes 49160 | tf_op jit(solution)/shard_map/ppermute | solution.py:436
  70.5 1.1 %collective-permute-start.25 = (f32[32,128]{1,0:T(8,128)S(1)}, f32[32,128]{1,0:T(8,128)S(1)}, u32[]{:S(2)}, u32[]{:S(2)}) collective-permute-start(f32[32,128]{1,0:T(8,128)S(1)} %get-tuple-element.73), channel_id=1, source_target_pairs={{0,4},{4,0},{8,12},{12,8},{16,20},{20,16},{24,28},{28,24},{1,5},{5... | collective-permute-start | bytes 49160 | tf_op jit(solution)/shard_map/ppermute | solution.py:426
  71.7 2.2 %collective-permute-done.27 = f32[32,128]{1,0:T(8,128)S(1)} collective-permute-done((f32[32,128]{1,0:T(8,128)S(1)}, f32[32,128]{1,0:T(8,128)S(1)}, u32[]{:S(2)}, u32[]{:S(2)}) %collective-permute-start.27) | collective-permute-done | bytes 16416 | tf_op jit(solution)/shard_map/ppermute | solution.py:436
  73.9 0.4 collective-permute-done.25
  74.4 1.4 %collective-permute-done.28.refs_1_ = f32[2,32,640]{2,1,0:T(8,128)S(1)} collective-permute-done((f32[2,32,640]{2,1,0:T(8,128)S(1)}, f32[2,32,640]{2,1,0:T(8,128)S(1)}, u32[]{:S(2)}, u32[]{:S(2)}) %collective-permute-start.28) | collective-permute-done | bytes 163872 | tf_op jit(solution)/shard_map/ppermute | solution.py:426
  75.8 1.2 %final.1 = (f32[32,2048]{1,0:T(8,128)}, f32[32,2048]{1,0:T(8,128)}) custom-call(f32[32,2048]{1,0:T(8,128)S(1)} %copy-done, f32[2,40,512]{2,1,0:T(8,128)S(1)} %pad_maximum_fusion.1.s1_own, f32[2,40,512]{2,1,0:T(8,128)S(1)} %collective-permute-done.17.s1_got, f32[2,32,640]{2,1,0:T(8,128)S(1)} %pad_maximum_fusion.2.refs_0_, ...), custom_call_target="tpu_custom_call" | custom-call | tf_op jit(solution)/shard_map/final/pallas_call | solution.py:658
  (52 shorter events, 1.2 us)
Async XLA Ops:
  0.6 5.7 %collective-permute-start = (s32[8,6]{1,0:T(8,128)}, s32[8,6]{1,0:T(8,128)S(1)}, u32[]{:S(2)}, u32[]{:S(2)}) collective-permute-start(s32[8,6]{1,0:T(8,128)} %param.3), channel_id=1, source_target_pairs={{0,1},{1,0},{2,3},{3,2},{4,5},{5,4},{6,7},{7,6},{8,9},{9,8},{10,11... | collective-permute-start | bytes 584 | tf_op jit(solution)/shard_map/ppermute | solution.py:426
  1.1 5.3 %collective-permute-start.2 = (s32[8,6]{1,0:T(8,128)}, s32[8,6]{1,0:T(8,128)S(1)}, u32[]{:S(2)}, u32[]{:S(2)}) collective-permute-start(s32[8,6]{1,0:T(8,128)} %param.3), channel_id=1, source_target_pairs={{0,3},{1,2},{2,1},{3,0},{4,7},{5,6},{6,5},{7,4},{8,11},{9,10},{10,... | collective-permute-start | bytes 584 | tf_op jit(solution)/shard_map/ppermute | solution.py:426
  3.8 3.8 %collective-permute-start.1 = (s32[8,6]{1,0:T(8,128)}, s32[8,6]{1,0:T(8,128)S(1)}, u32[]{:S(2)}, u32[]{:S(2)}) collective-permute-start(s32[8,6]{1,0:T(8,128)} %param.3), channel_id=1, source_target_pairs={{0,2},{1,3},{2,0},{3,1},{4,6},{5,7},{6,4},{7,5},{8,10},{9,11},{10,... | collective-permute-start | bytes 584 | tf_op jit(solution)/shard_map/ppermute | solution.py:426
  7.9 8.1 %collective-permute-start.5 = (bf16[16,640]{1,0:T(8,128)(2,1)S(1)}, bf16[16,640]{1,0:T(8,128)(2,1)S(1)}, u32[]{:S(2)}, u32[]{:S(2)}) collective-permute-start(bf16[16,640]{1,0:T(8,128)(2,1)S(1)} %pad_maximum_fusion.5), channel_id=1, source_target_pairs={{0,24},{4,28},{8,16},{12,20},{16,8},{20,12},{24,0},{28,4},{1,25},{... | collective-permute-start | bytes 61448 | tf_op jit(solution)/shard_map/ppermute | solution.py:426
  11.6 5.2 %collective-permute-start.4 = (bf16[16,640]{1,0:T(8,128)(2,1)S(1)}, bf16[16,640]{1,0:T(8,128)(2,1)S(1)}, u32[]{:S(2)}, u32[]{:S(2)}) collective-permute-start(bf16[16,640]{1,0:T(8,128)(2,1)S(1)} %pad_maximum_fusion.5), channel_id=1, source_target_pairs={{0,16},{4,20},{8,24},{12,28},{16,0},{20,4},{24,8},{28,12},{1,17},{... | collective-permute-start | bytes 61448 | tf_op jit(solution)/shard_map/ppermute | solution.py:426
  11.6 5.2 %collective-permute-start.3 = (bf16[16,640]{1,0:T(8,128)(2,1)S(1)}, bf16[16,640]{1,0:T(8,128)(2,1)S(1)}, u32[]{:S(2)}, u32[]{:S(2)}) collective-permute-start(bf16[16,640]{1,0:T(8,128)(2,1)S(1)} %pad_maximum_fusion.5), channel_id=1, source_target_pairs={{0,8},{4,12},{8,0},{12,4},{16,24},{20,28},{24,16},{28,20},{1,9},{5... | collective-permute-start | bytes 61448 | tf_op jit(solution)/shard_map/ppermute | solution.py:426
  12.3 10.6 %collective-permute-start.9 = (f32[32,512]{1,0:T(8,128)S(1)}, f32[32,512]{1,0:T(8,128)S(1)}, u32[]{:S(2)}, u32[]{:S(2)}) collective-permute-start(f32[32,512]{1,0:T(8,128)S(1)} %constant_dynamic-slice_fusion), channel_id=1, source_target_pairs={{0,24},{4,28},{8,16},{12,20},{16,8},{20,12},{24,0},{28,4},{1,25},{... | collective-permute-start | bytes 196616 | tf_op jit(solution)/shard_map/ppermute | solution.py:426
  15.9 7.0 %collective-permute-start.8 = (f32[32,512]{1,0:T(8,128)S(1)}, f32[32,512]{1,0:T(8,128)S(1)}, u32[]{:S(2)}, u32[]{:S(2)}) collective-permute-start(f32[32,512]{1,0:T(8,128)S(1)} %constant_dynamic-slice_fusion), channel_id=1, source_target_pairs={{0,16},{4,20},{8,24},{12,28},{16,0},{20,4},{24,8},{28,12},{1,17},{... | collective-permute-start | bytes 196616 | tf_op jit(solution)/shard_map/ppermute | solution.py:426
  15.9 7.0 %collective-permute-start.7 = (f32[32,512]{1,0:T(8,128)S(1)}, f32[32,512]{1,0:T(8,128)S(1)}, u32[]{:S(2)}, u32[]{:S(2)}) collective-permute-start(f32[32,512]{1,0:T(8,128)S(1)} %constant_dynamic-slice_fusion), channel_id=1, source_target_pairs={{0,8},{4,12},{8,0},{12,4},{16,24},{20,28},{24,16},{28,20},{1,9},{5... | collective-permute-start | bytes 196616 | tf_op jit(solution)/shard_map/ppermute | solution.py:426
  16.8 6.2 %collective-permute-start.6 = (bf16[4,16,640]{2,1,0:T(8,128)(2,1)S(1)}, bf16[4,16,640]{2,1,0:T(8,128)(2,1)S(1)}, u32[]{:S(2)}, u32[]{:S(2)}) collective-permute-start(bf16[4,16,640]{2,1,0:T(8,128)(2,1)S(1)} %pad_maximum_fusion.4.refs_1_), channel_id=1, source_target_pairs={{0,4},{4,0},{8,12},{12,8},{16,20},{20,16},{24,28},{28,24},{1,5},{5... | collective-permute-start | bytes 245768 | tf_op jit(solution)/shard_map/ppermute | solution.py:426
  26.6 21.7 %copy-start = (f32[32,2048]{1,0:T(8,128)S(1)}, f32[32,2048]{1,0:T(8,128)}, u32[]{:S(2)}) copy-start(f32[32,2048]{1,0:T(8,128)} %t_ref.5) | copy-start | bytes 786436
  26.6 4.8 %collective-permute-start.13 = (f32[16,256]{1,0:T(8,128)S(1)}, f32[16,256]{1,0:T(8,128)S(1)}, u32[]{:S(2)}, u32[]{:S(2)}) collective-permute-start(f32[16,256]{1,0:T(8,128)S(1)} %get-tuple-element.54), channel_id=1, source_target_pairs={{0,12},{4,8},{8,4},{12,0},{16,28},{20,24},{24,20},{28,16},{1,13},{... | collective-permute-start | bytes 49160 | tf_op jit(solution)/shard_map/ppermute | solution.py:426
  27.9 3.7 %collective-permute-start.12 = (f32[16,256]{1,0:T(8,128)S(1)}, f32[16,256]{1,0:T(8,128)S(1)}, u32[]{:S(2)}, u32[]{:S(2)}) collective-permute-start(f32[16,256]{1,0:T(8,128)S(1)} %get-tuple-element.54), channel_id=1, source_target_pairs={{0,8},{4,12},{8,0},{12,4},{16,24},{20,28},{24,16},{28,20},{1,9},{5... | collective-permute-start | bytes 49160 | tf_op jit(solution)/shard_map/ppermute | solution.py:426
  28.5 4.0 %collective-permute-start.11 = (f32[16,256]{1,0:T(8,128)S(1)}, f32[16,256]{1,0:T(8,128)S(1)}, u32[]{:S(2)}, u32[]{:S(2)}) collective-permute-start(f32[16,256]{1,0:T(8,128)S(1)} %get-tuple-element.54), channel_id=1, source_target_pairs={{0,4},{4,0},{8,12},{12,8},{16,20},{20,16},{24,28},{28,24},{1,5},{5... | collective-permute-start | bytes 49160 | tf_op jit(solution)/shard_map/ppermute | solution.py:426
  30.2 7.0 %collective-permute-start.10 = (f32[4,32,512]{2,1,0:T(8,128)S(1)}, f32[4,32,512]{2,1,0:T(8,128)S(1)}, u32[]{:S(2)}, u32[]{:S(2)}) collective-permute-start(f32[4,32,512]{2,1,0:T(8,128)S(1)} %pad_maximum_fusion.refs_2_.t_same), channel_id=1, source_target_pairs={{0,4},{4,0},{8,12},{12,8},{16,20},{20,16},{24,28},{28,24},{1,5},{5... | collective-permute-start | bytes 786440 | tf_op jit(solution)/shard_map/ppermute | solution.py:426
  32.5 4.7 %collective-permute-start.14 = (f32[16,256]{1,0:T(8,128)S(1)}, f32[16,256]{1,0:T(8,128)S(1)}, u32[]{:S(2)}, u32[]{:S(2)}) collective-permute-start(f32[16,256]{1,0:T(8,128)S(1)} %add_add_fusion), channel_id=1, source_target_pairs={{0,16},{4,20},{8,24},{12,28},{16,0},{20,4},{24,8},{28,12},{1,17},{... | collective-permute-start | bytes 49160 | tf_op jit(solution)/shard_map/ppermute | solution.py:426
  40.3 1.4 %collective-permute-start.15 = (f32[2,32,512]{2,1,0:T(8,128)S(1)}, f32[2,32,512]{2,1,0:T(8,128)S(1)}, u32[]{:S(2)}, u32[]{:S(2)}) collective-permute-start(f32[2,32,512]{2,1,0:T(8,128)S(1)} %get-tuple-element.56), channel_id=1, source_target_pairs={{0,1},{1,0},{2,3},{3,2},{4,5},{5,4},{6,7},{7,6},{8,9},{9,8},{10,11... | collective-permute-start | bytes 393224 | tf_op jit(solution)/shard_map/ppermute | solution.py:426
  41.7 6.4 %collective-permute-start.16 = (f32[72,512]{1,0:T(8,128)S(1)}, f32[72,512]{1,0:T(8,128)S(1)}, u32[]{:S(2)}, u32[]{:S(2)}) collective-permute-start(f32[72,512]{1,0:T(8,128)S(1)} %pad_maximum_fusion.3), channel_id=1, source_target_pairs={{0,2},{1,3},{2,0},{3,1},{4,6},{5,7},{6,4},{7,5},{8,10},{9,11},{10,... | collective-permute-start | bytes 442376 | tf_op jit(solution)/shard_map/ppermute | solution.py:426
  48.2 1.5 %collective-permute-start.17 = (f32[2,40,512]{2,1,0:T(8,128)S(1)}, f32[2,40,512]{2,1,0:T(8,128)S(1)}, u32[]{:S(2)}, u32[]{:S(2)}) collective-permute-start(f32[2,40,512]{2,1,0:T(8,128)S(1)} %pad_maximum_fusion.1.s1_own), channel_id=1, source_target_pairs={{0,1},{1,0},{2,3},{3,2},{4,5},{5,4},{6,7},{7,6},{8,9},{9,8},{10,11... | collective-permute-start | bytes 491528 | tf_op jit(solution)/shard_map/ppermute | solution.py:426
  51.1 9.9 %collective-permute-start.18 = (bf16[4,32,512]{2,1,0:T(8,128)(2,1)S(1)}, bf16[4,32,512]{2,1,0:T(8,128)(2,1)S(1)}, u32[]{:S(2)}, u32[]{:S(2)}) collective-permute-start(bf16[4,32,512]{2,1,0:T(8,128)(2,1)S(1)} %second.3), channel_id=1, source_target_pairs={{0,4},{4,0},{8,12},{12,8},{16,20},{20,16},{24,28},{28,24},{1,5},{5... | collective-permute-start | bytes 393224 | tf_op jit(solution)/shard_map/ppermute | solution.py:426
  52.6 6.0 %collective-permute-start.21 = (bf16[32,512]{1,0:T(8,128)(2,1)S(1)}, bf16[32,512]{1,0:T(8,128)(2,1)S(1)}, u32[]{:S(2)}, u32[]{:S(2)}) collective-permute-start(bf16[32,512]{1,0:T(8,128)(2,1)S(1)} %fusion.2.refs_0_), channel_id=1, source_target_pairs={{0,24},{4,28},{8,16},{12,20},{16,8},{20,12},{24,0},{28,4},{1,25},{... | collective-permute-start | bytes 98312 | tf_op jit(solution)/shard_map/ppermute | solution.py:426
  56.2 4.8 %collective-permute-start.20 = (bf16[32,512]{1,0:T(8,128)(2,1)S(1)}, bf16[32,512]{1,0:T(8,128)(2,1)S(1)}, u32[]{:S(2)}, u32[]{:S(2)}) collective-permute-start(bf16[32,512]{1,0:T(8,128)(2,1)S(1)} %fusion.2.refs_0_), channel_id=1, source_target_pairs={{0,16},{4,20},{8,24},{12,28},{16,0},{20,4},{24,8},{28,12},{1,17},{... | collective-permute-start | bytes 98312 | tf_op jit(solution)/shard_map/ppermute | solution.py:426
  56.2 4.8 %collective-permute-start.19 = (bf16[32,512]{1,0:T(8,128)(2,1)S(1)}, bf16[32,512]{1,0:T(8,128)(2,1)S(1)}, u32[]{:S(2)}, u32[]{:S(2)}) collective-permute-start(bf16[32,512]{1,0:T(8,128)(2,1)S(1)} %fusion.2.refs_0_), channel_id=1, source_target_pairs={{0,8},{4,12},{8,0},{12,4},{16,24},{20,28},{24,16},{28,20},{1,9},{5... | collective-permute-start | bytes 98312 | tf_op jit(solution)/shard_map/ppermute | solution.py:426
  61.2 5.9 %collective-permute-start.22 = (bf16[32,640]{1,0:T(8,128)(2,1)S(1)}, bf16[32,640]{1,0:T(8,128)(2,1)S(1)}, u32[]{:S(2)}, u32[]{:S(2)}) collective-permute-start(bf16[32,640]{1,0:T(8,128)(2,1)S(1)} %get-tuple-element.69), channel_id=1, source_target_pairs={{0,24},{4,28},{8,16},{12,20},{16,8},{20,12},{24,0},{28,4},{1,25},{... | collective-permute-start | bytes 122888 | tf_op jit(solution)/shard_map/ppermute | solution.py:426
  62.7 4.9 %collective-permute-start.23 = (bf16[32,640]{1,0:T(8,128)(2,1)S(1)}, bf16[32,640]{1,0:T(8,128)(2,1)S(1)}, u32[]{:S(2)}, u32[]{:S(2)}) collective-permute-start(bf16[32,640]{1,0:T(8,128)(2,1)S(1)} %get-tuple-element.70), channel_id=1, source_target_pairs={{0,16},{4,20},{8,24},{12,28},{16,0},{20,4},{24,8},{28,12},{1,17},{... | collective-permute-start | bytes 122888 | tf_op jit(solution)/shard_map/ppermute | solution.py:426
  63.3 4.7 %collective-permute-start.24 = (bf16[32,640]{1,0:T(8,128)(2,1)S(1)}, bf16[32,640]{1,0:T(8,128)(2,1)S(1)}, u32[]{:S(2)}, u32[]{:S(2)}) collective-permute-start(bf16[32,640]{1,0:T(8,128)(2,1)S(1)} %get-tuple-element.71), channel_id=1, source_target_pairs={{0,8},{4,12},{8,0},{12,4},{16,24},{20,28},{24,16},{28,20},{1,9},{5... | collective-permute-start | bytes 122888 | tf_op jit(solution)/shard_map/ppermute | solution.py:426
  68.1 6.1 %collective-permute-start.26 = (f32[32,640]{1,0:T(8,128)S(1)}, f32[32,640]{1,0:T(8,128)S(1)}, u32[]{:S(2)}, u32[]{:S(2)}) collective-permute-start(f32[32,640]{1,0:T(8,128)S(1)} %get-tuple-element.72), channel_id=1, source_target_pairs={{0,2},{1,3},{2,0},{3,1},{4,6},{5,7},{6,4},{7,5},{8,10},{9,11},{10,... | collective-permute-start | bytes 245768 | tf_op jit(solution)/shard_map/ppermute | solution.py:426
  69.2 4.6 %collective-permute-start.27 = (f32[32,128]{1,0:T(8,128)S(1)}, f32[32,128]{1,0:T(8,128)S(1)}, u32[]{:S(2)}, u32[]{:S(2)}) collective-permute-start(f32[32,128]{1,0:T(8,128)S(1)} %get-tuple-element.73), channel_id=1, source_target_pairs={{0,6},{1,7},{2,4},{3,5},{4,2},{5,3},{6,0},{7,1},{8,14},{9,15},{10,... | collective-permute-start | bytes 49160 | tf_op jit(solution)/shard_map/ppermute | solution.py:436
  70.5 3.7 %collective-permute-start.25 = (f32[32,128]{1,0:T(8,128)S(1)}, f32[32,128]{1,0:T(8,128)S(1)}, u32[]{:S(2)}, u32[]{:S(2)}) collective-permute-start(f32[32,128]{1,0:T(8,128)S(1)} %get-tuple-element.73), channel_id=1, source_target_pairs={{0,4},{4,0},{8,12},{12,8},{16,20},{20,16},{24,28},{28,24},{1,5},{5... | collective-permute-start | bytes 49160 | tf_op jit(solution)/shard_map/ppermute | solution.py:426
  74.3 1.5 %collective-permute-start.28 = (f32[2,32,640]{2,1,0:T(8,128)S(1)}, f32[2,32,640]{2,1,0:T(8,128)S(1)}, u32[]{:S(2)}, u32[]{:S(2)}) collective-permute-start(f32[2,32,640]{2,1,0:T(8,128)S(1)} %pad_maximum_fusion.2.refs_0_), channel_id=1, source_target_pairs={{0,1},{1,0},{2,3},{3,2},{4,5},{5,4},{6,7},{7,6},{8,9},{9,8},{10,11... | collective-permute-start | bytes 491528 | tf_op jit(solution)/shard_map/ppermute | solution.py:426

commit v15 on v14

--- a/solution.py
+++ b/solution.py
@@ -15,7 +15,7 @@
 CODE_BITS = 12
 CODE = 1 << CODE_BITS
 RING = 3
-STRIP = 32
+STRIP = 64
 LANES = 128
 TINY = 1e-30
 SHIFT = 0.375
@@ -166,7 +166,6 @@
         dist[slot] = jnp.dot(lhs[i], rhs[j], preferred_element_type=F32)
 
     distances(0, 0)
-    ones = jnp.ones((8, block_len), BF16)
 
     def step(g, carry):
         slot, target = (base + g, k_mat) if cfg.resident else (lax.rem(g, RING), kbuf)
@@ -180,7 +179,7 @@
             distances(g * GROUP + u + 1, (u + 1) % 2)
             j = listed[0, g * GROUP + u + 1] & (CODE - 1)
             m = mlist[g * GROUP + u].astype(F32)
-            strips = []
+            sums = jnp.zeros((8, block_len), F32)
             for s in range(block_len // STRIP):
                 rows = slice(s * STRIP, (s + 1) * STRIP)
                 d = jnp.maximum(dist[u % 2, rows, :], TINY)
@@ -188,19 +187,19 @@
                 rem = jnp.maximum(1.0 - sc, 0.0)
                 sq = rem * rem
                 val = (sq * sq) * (sc * (4.0 * m) + m)
-                strips.append(val.astype(BF16))
-                target[slot, u, rows, :] = strips[-1]
-            block = jnp.concatenate(strips, axis=0)
-            acc[j] += jnp.dot(ones, block, preferred_element_type=F32)
+                target[slot, u, rows, :] = val.astype(BF16)
+                for h in range(0, STRIP, 8):
+                    sums = sums + val[h:h + 8]
+            acc[j] += sums
         if not cfg.resident:
             copy_out(g).start()
         return carry
 
     lax.fori_loop(0, total, step, 0)
     if cfg.parts == 1 or not last:
-        deg_ref[...] = acc[:, 0, :]
+        deg_ref[...] = jnp.sum(acc[...], axis=1)
     else:
-        second = acc[:, 0, :]
+        second = jnp.sum(acc[...], axis=1)
         for z in range(held):
             rows = slice(z * own_rows, (z + 1) * own_rows)
             for p, deg in enumerate((first_deg[rows, :], second[rows])):

time: 77.3 us -> 76.7 us (level)
  starting transfers between devices: 36.8 us -> 35.9 us
    ppermute x1, starting transfers between devices: 1.29 us -> 0.52 us  [both_swap(): return lax.ppermute(x, ('rows', 'cols'), pairs)]
  transfers between devices with their start and end apart: 29 -> 29, of which waited for: 15 -> 15; matrix products, arithmetic and copies ran while one was open for 4% -> 4% of each run, Pallas kernels for 8% -> 7%
where the time goes in v15:
time: 76.7 us; the launch traced here: 76 us
  starting transfers between devices  35.9 us (47%)
  waiting for transfers between devices  20.8 us (27%)
  Pallas kernels  15.2 us (20%)
  local copies, waits for them, and re-layouts  2.75 us (4%)
  between operations  0.87 us (1%)
    ppermute x28, starting transfers between devices, swap(): return lax.ppermute(x, axis, [(i, i ^ d) for i in range(size)])  35.3 us
    ppermute x28, waiting for transfers between devices, swap(): return lax.ppermute(x, axis, [(i, i ^ d) for i in range(size)])  18.5 us
    pallas_call x2, Pallas kernels, build(): pl.pallas_call(functools.partial(build_kernel, cfg, part), out_shape=out,...  7.7 us
    pallas_call x1, Pallas kernels, local(): pl.pallas_call(functools.partial(first_kernel, cfg), out_shape=[shape(out...  3.05 us
    pallas_call x2, Pallas kernels, second(): pl.pallas_call(functools.partial(second_kernel, cfg, part), out_shape=sha...  3 us
    ppermute x1, waiting for transfers between devices, both_swap(): return lax.ppermute(x, ('rows', 'cols'), pairs)  2.37 us
    dynamic_slice x2, local copies, waits for them, and re-layouts, own(): return lax.dynamic_slice_in_dim(x, col * own_len, own_len, 1)  1.56 us
  transfers between devices with their start and end apart: 29, of which 15 were waited for; matrix products, arithmetic and copies ran while one was open for 4% of the time, Pallas kernels for 7%

profile of v15, /device:TPU:0, one launch (start us, length us, event | category | flops | bytes accessed | tf_op | source)
XLA Modules:
  0.0 76.0 jit_solution(3821015306524447894)
XLA Ops:
  0.6 0.5 collective-permute-start
  1.1 2.6 %collective-permute-start.2 = (s32[8,6]{1,0:T(8,128)}, s32[8,6]{1,0:T(8,128)S(1)}, u32[]{:S(2)}, u32[]{:S(2)}) collective-permute-start(s32[8,6]{1,0:T(8,128)} %param.3), channel_id=1, source_target_pairs={{0,3},{1,2},{2,1},{3,0},{4,7},{5,6},{6,5},{7,4},{8,11},{9,10},{10,... | collective-permute-start | bytes 584 | tf_op jit(solution)/shard_map/ppermute | solution.py:425
  3.8 0.8 %copy.6 = s32[8,6]{0,1:T(8,128)S(1)} copy(s32[8,6]{1,0:T(8,128)} %param.3) | data formatting | bytes 384 | tf_op args[0]
  4.7 0.7 constant_dynamic-slice_fusion.1
  5.5 0.8 %constant_dynamic-slice_fusion = f32[32,512]{1,0:T(8,128)S(1)} fusion(f32[32,2048]{1,0:T(8,128)} %t_ref.5, s32[]{:T(128)S(6)} %select_n.7), kind=kLoop, calls=%fused_computation.36 | loop fusion | bytes 131076 | tf_op jit(solution)/shard_map/dynamic_slice | solution.py:486
  6.6 1.0 %collective-permute-done.1 = s32[8,6]{1,0:T(8,128)S(1)} collective-permute-done((s32[8,6]{1,0:T(8,128)}, s32[8,6]{1,0:T(8,128)S(1)}, u32[]{:S(2)}, u32[]{:S(2)}) %collective-permute-start.1) | collective-permute-done | bytes 224 | tf_op jit(solution)/shard_map/ppermute | solution.py:425
  7.9 3.7 %collective-permute-start.5 = (bf16[16,640]{1,0:T(8,128)(2,1)S(1)}, bf16[16,640]{1,0:T(8,128)(2,1)S(1)}, u32[]{:S(2)}, u32[]{:S(2)}) collective-permute-start(bf16[16,640]{1,0:T(8,128)(2,1)S(1)} %pad_maximum_fusion.5), channel_id=1, source_target_pairs={{0,24},{4,28},{8,16},{12,20},{16,8},{20,12},{24,0},{28,4},{1,25},{... | collective-permute-start | bytes 61448 | tf_op jit(solution)/shard_map/ppermute | solution.py:425
  11.6 0.8 %collective-permute-start.3 = (bf16[16,640]{1,0:T(8,128)(2,1)S(1)}, bf16[16,640]{1,0:T(8,128)(2,1)S(1)}, u32[]{:S(2)}, u32[]{:S(2)}) collective-permute-start(bf16[16,640]{1,0:T(8,128)(2,1)S(1)} %pad_maximum_fusion.5), channel_id=1, source_target_pairs={{0,8},{4,12},{8,0},{12,4},{16,24},{20,28},{24,16},{28,20},{1,9},{5... | collective-permute-start | bytes 61448 | tf_op jit(solution)/shard_map/ppermute | solution.py:425
  12.3 3.6 %collective-permute-start.9 = (f32[32,512]{1,0:T(8,128)S(1)}, f32[32,512]{1,0:T(8,128)S(1)}, u32[]{:S(2)}, u32[]{:S(2)}) collective-permute-start(f32[32,512]{1,0:T(8,128)S(1)} %constant_dynamic-slice_fusion), channel_id=1, source_target_pairs={{0,24},{4,28},{8,16},{12,20},{16,8},{20,12},{24,0},{28,4},{1,25},{... | collective-permute-start | bytes 196616 | tf_op jit(solution)/shard_map/ppermute | solution.py:425
  15.9 0.8 %collective-permute-start.7 = (f32[32,512]{1,0:T(8,128)S(1)}, f32[32,512]{1,0:T(8,128)S(1)}, u32[]{:S(2)}, u32[]{:S(2)}) collective-permute-start(f32[32,512]{1,0:T(8,128)S(1)} %constant_dynamic-slice_fusion), channel_id=1, source_target_pairs={{0,8},{4,12},{8,0},{12,4},{16,24},{20,28},{24,16},{28,20},{1,9},{5... | collective-permute-start | bytes 196616 | tf_op jit(solution)/shard_map/ppermute | solution.py:425
  16.8 1.6 %collective-permute-start.6 = (bf16[4,16,640]{2,1,0:T(8,128)(2,1)S(1)}, bf16[4,16,640]{2,1,0:T(8,128)(2,1)S(1)}, u32[]{:S(2)}, u32[]{:S(2)}) collective-permute-start(bf16[4,16,640]{2,1,0:T(8,128)(2,1)S(1)} %pad_maximum_fusion.4.refs_1_), channel_id=1, source_target_pairs={{0,4},{4,0},{8,12},{12,8},{16,20},{20,16},{24,28},{28,24},{1,5},{5... | collective-permute-start | bytes 245768 | tf_op jit(solution)/shard_map/ppermute | solution.py:425
  18.3 3.8 %build.2 = (bf16[32,4,256,256]{3,2,1,0:T(8,128)(2,1)S(1)}, s32[1,128]{1,0:T(1,128)S(1)}, f32[8,256]{1,0:T(8,128)S(1)}, bf16[8,256,32]{2,1,0:T(8,128)(2,1)S(1)}) custom-call(s32[8,64]{1,0:T(8,128)S(1)} %add_add_fusion.1.direct_v, bf16[16,2048]{1,0:T(8,128)(2,1)} %refs_0_.1, bf16[4,16,640]{2,1,0:T(8,128)(2,1)S(1)} %pad_maximum_fusion.4.refs_1_), custom_call_target="tpu_custom_call" | custom-call | flops 2684354560 | bytes 83886080 | tf_op jit(solution)/shard_map/build/pallas_call | solution.py:511
  22.2 3.9 %build.3 = (bf16[32,4,256,256]{3,2,1,0:T(8,128)(2,1)S(1)}, s32[1,128]{1,0:T(1,128)S(1)}, f32[16,256]{1,0:T(8,128)S(1)}) custom-call(s32[8,64]{1,0:T(8,128)S(1)} %add_add_fusion.1.direct_v, bf16[8,256,32]{2,1,0:T(8,128)(2,1)S(1)} %get-tuple-element.39.refs_0_, f32[8,256]{1,0:T(8,128)S(1)} %get-tuple-element.42.refs_1_, ...), custom_call_target="tpu_custom_call", output_to_operand_aliasing={{0}: (4, {})} | custom-call | flops 2684354560 | bytes 83886080 | tf_op jit(solution)/shard_map/build/pallas_call | solution.py:511
  26.1 1.8 %collective-permute-start.13 = (f32[16,256]{1,0:T(8,128)S(1)}, f32[16,256]{1,0:T(8,128)S(1)}, u32[]{:S(2)}, u32[]{:S(2)}) collective-permute-start(f32[16,256]{1,0:T(8,128)S(1)} %get-tuple-element.54), channel_id=1, source_target_pairs={{0,12},{4,8},{8,4},{12,0},{16,28},{20,24},{24,20},{28,16},{1,13},{... | collective-permute-start | bytes 49160 | tf_op jit(solution)/shard_map/ppermute | solution.py:425
  27.9 0.3 collective-permute-start.12
  28.2 1.5 %collective-permute-start.11 = (f32[16,256]{1,0:T(8,128)S(1)}, f32[16,256]{1,0:T(8,128)S(1)}, u32[]{:S(2)}, u32[]{:S(2)}) collective-permute-start(f32[16,256]{1,0:T(8,128)S(1)} %get-tuple-element.54), channel_id=1, source_target_pairs={{0,4},{4,0},{8,12},{12,8},{16,20},{20,16},{24,28},{28,24},{1,5},{5... | collective-permute-start | bytes 49160 | tf_op jit(solution)/shard_map/ppermute | solution.py:425
  29.7 0.6 collective-permute-start.10
  30.2 0.7 collective-permute-done.13
  30.9 0.8 collective-permute-done.12
  31.7 0.5 collective-permute-done.11
  32.2 2.3 %collective-permute-start.14 = (f32[16,256]{1,0:T(8,128)S(1)}, f32[16,256]{1,0:T(8,128)S(1)}, u32[]{:S(2)}, u32[]{:S(2)}) collective-permute-start(f32[16,256]{1,0:T(8,128)S(1)} %add_add_fusion), channel_id=1, source_target_pairs={{0,16},{4,20},{8,24},{12,28},{16,0},{20,4},{24,8},{28,12},{1,17},{... | collective-permute-start | bytes 49160 | tf_op jit(solution)/shard_map/ppermute | solution.py:425
  34.5 2.4 %collective-permute-done.14 = f32[16,256]{1,0:T(8,128)S(1)} collective-permute-done((f32[16,256]{1,0:T(8,128)S(1)}, f32[16,256]{1,0:T(8,128)S(1)}, u32[]{:S(2)}, u32[]{:S(2)}) %collective-permute-start.14) | collective-permute-done | bytes 16416 | tf_op jit(solution)/shard_map/ppermute | solution.py:425
  36.9 3.1 %first.1 = (f32[32,512]{1,0:T(8,128)S(1)}, f32[32,512]{1,0:T(8,128)S(1)}, f32[2,32,512]{2,1,0:T(8,128)S(1)}, f32[8,512]{1,0:T(8,128)S(1)}) custom-call(bf16[32,4,256,256]{3,2,1,0:T(8,128)(2,1)S(1)} %get-tuple-element.50.k_mat, s32[1,128]{1,0:T(1,128)S(1)} %get-tuple-element.51.refs_0_.list_v, s32[1,128]{1,0:T(1,128)S(1)} %get-tuple-element.52.refs_1_.list_v, ...), custom_call_target="tpu_custom_call" | custom-call | flops 536870912 | bytes 8388608 | tf_op jit(solution)/shard_map/first/pallas_call | solution.py:567
  40.0 1.3 %collective-permute-done.15 = f32[2,32,512]{2,1,0:T(8,128)S(1)} collective-permute-done((f32[2,32,512]{2,1,0:T(8,128)S(1)}, f32[2,32,512]{2,1,0:T(8,128)S(1)}, u32[]{:S(2)}, u32[]{:S(2)}) %collective-permute-start.15) | collective-permute-done | bytes 131104 | tf_op jit(solution)/shard_map/ppermute | solution.py:425
  41.4 2.1 %collective-permute-start.16 = (f32[72,512]{1,0:T(8,128)S(1)}, f32[72,512]{1,0:T(8,128)S(1)}, u32[]{:S(2)}, u32[]{:S(2)}) collective-permute-start(f32[72,512]{1,0:T(8,128)S(1)} %pad_maximum_fusion.3), channel_id=1, source_target_pairs={{0,2},{1,3},{2,0},{3,1},{4,6},{5,7},{6,4},{7,5},{8,10},{9,11},{10,... | collective-permute-start | bytes 442376 | tf_op jit(solution)/shard_map/ppermute | solution.py:425
  43.6 4.2 %collective-permute-done.16 = f32[72,512]{1,0:T(8,128)S(1)} collective-permute-done((f32[72,512]{1,0:T(8,128)S(1)}, f32[72,512]{1,0:T(8,128)S(1)}, u32[]{:S(2)}, u32[]{:S(2)}) %collective-permute-start.16) | collective-permute-done | bytes 147488 | tf_op jit(solution)/shard_map/ppermute | solution.py:425
  47.9 1.3 %collective-permute-done.17.s1_got = f32[2,40,512]{2,1,0:T(8,128)S(1)} collective-permute-done((f32[2,40,512]{2,1,0:T(8,128)S(1)}, f32[2,40,512]{2,1,0:T(8,128)S(1)}, u32[]{:S(2)}, u32[]{:S(2)}) %collective-permute-start.17) | collective-permute-done | bytes 163872 | tf_op jit(solution)/shard_map/ppermute | solution.py:425
  49.3 1.6 %second.3 = bf16[4,32,512]{2,1,0:T(8,128)(2,1)S(1)} custom-call(bf16[32,4,256,256]{3,2,1,0:T(8,128)(2,1)S(1)} %get-tuple-element.50.k_mat, s32[1,128]{1,0:T(1,128)S(1)} %get-tuple-element.52.refs_1_.list_v, f32[32,2048]{1,0:T(8,128)S(1)} %copy-done, f32[2,40,512]{2,1,0:T(8,128)S(1)} %pad_maximum_fusion.1.s1_own, f32[2,40,512]{2,1,0:T(8,128)S(1)} %collective-permute-done.17.s1_got), custom_call_target="tpu_custom_call" | custom-call | flops 268435456 | bytes 4194304 | tf_op jit(solution)/shard_map/second/pallas_call | solution.py:596
  50.9 1.2 %collective-permute-start.18 = (bf16[4,32,512]{2,1,0:T(8,128)(2,1)S(1)}, bf16[4,32,512]{2,1,0:T(8,128)(2,1)S(1)}, u32[]{:S(2)}, u32[]{:S(2)}) collective-permute-start(bf16[4,32,512]{2,1,0:T(8,128)(2,1)S(1)} %second.3), channel_id=1, source_target_pairs={{0,4},{4,0},{8,12},{12,8},{16,20},{20,16},{24,28},{28,24},{1,5},{5... | collective-permute-start | bytes 393224 | tf_op jit(solution)/shard_map/ppermute | solution.py:425
  52.0 3.5 %collective-permute-start.21 = (bf16[32,512]{1,0:T(8,128)(2,1)S(1)}, bf16[32,512]{1,0:T(8,128)(2,1)S(1)}, u32[]{:S(2)}, u32[]{:S(2)}) collective-permute-start(bf16[32,512]{1,0:T(8,128)(2,1)S(1)} %fusion.2.refs_0_), channel_id=1, source_target_pairs={{0,24},{4,28},{8,16},{12,20},{16,8},{20,12},{24,0},{28,4},{1,25},{... | collective-permute-start | bytes 98312 | tf_op jit(solution)/shard_map/ppermute | solution.py:425
  55.5 0.9 %collective-permute-start.19 = (bf16[32,512]{1,0:T(8,128)(2,1)S(1)}, bf16[32,512]{1,0:T(8,128)(2,1)S(1)}, u32[]{:S(2)}, u32[]{:S(2)}) collective-permute-start(bf16[32,512]{1,0:T(8,128)(2,1)S(1)} %fusion.2.refs_0_), channel_id=1, source_target_pairs={{0,8},{4,12},{8,0},{12,4},{16,24},{20,28},{24,16},{28,20},{1,9},{5... | collective-permute-start | bytes 98312 | tf_op jit(solution)/shard_map/ppermute | solution.py:425
  56.4 1.4 %second.2.z_same = f32[4,32,512]{2,1,0:T(8,128)S(1)} custom-call(bf16[32,4,256,256]{3,2,1,0:T(8,128)(2,1)S(1)} %get-tuple-element.50.k_mat, s32[1,128]{1,0:T(1,128)S(1)} %get-tuple-element.51.refs_0_.list_v, f32[32,2048]{1,0:T(8,128)S(1)} %copy-done, f32[2,40,512]{2,1,0:T(8,128)S(1)} %pad_maximum_fusion.1.s1_own, ...), custom_call_target="tpu_custom_call" | custom-call | flops 268435456 | bytes 4194304 | tf_op jit(solution)/shard_map/second/pallas_call | solution.py:596
  57.8 0.3 collective-permute-done.21.refs_3_
  58.1 2.2 %collective-permute-done.20.refs_2_ = bf16[32,512]{1,0:T(8,128)(2,1)S(1)} collective-permute-done((bf16[32,512]{1,0:T(8,128)(2,1)S(1)}, bf16[32,512]{1,0:T(8,128)(2,1)S(1)}, u32[]{:S(2)}, u32[]{:S(2)}) %collective-permute-start.20) | collective-permute-done | bytes 32800 | tf_op jit(solution)/shard_map/ppermute | solution.py:425
  60.3 0.2 meet.1
  60.5 1.5 %collective-permute-start.22 = (bf16[32,640]{1,0:T(8,128)(2,1)S(1)}, bf16[32,640]{1,0:T(8,128)(2,1)S(1)}, u32[]{:S(2)}, u32[]{:S(2)}) collective-permute-start(bf16[32,640]{1,0:T(8,128)(2,1)S(1)} %get-tuple-element.69), channel_id=1, source_target_pairs={{0,24},{4,28},{8,16},{12,20},{16,8},{20,12},{24,0},{28,4},{1,25},{... | collective-permute-start | bytes 122888 | tf_op jit(solution)/shard_map/ppermute | solution.py:425
  62.0 0.6 collective-permute-start.23
  62.7 2.3 %collective-permute-start.24 = (bf16[32,640]{1,0:T(8,128)(2,1)S(1)}, bf16[32,640]{1,0:T(8,128)(2,1)S(1)}, u32[]{:S(2)}, u32[]{:S(2)}) collective-permute-start(bf16[32,640]{1,0:T(8,128)(2,1)S(1)} %get-tuple-element.71), channel_id=1, source_target_pairs={{0,8},{4,12},{8,0},{12,4},{16,24},{20,28},{24,16},{28,20},{1,9},{5... | collective-permute-start | bytes 122888 | tf_op jit(solution)/shard_map/ppermute | solution.py:425
  65.0 1.4 %collective-permute-done.22.refs_0_ = bf16[32,640]{1,0:T(8,128)(2,1)S(1)} collective-permute-done((bf16[32,640]{1,0:T(8,128)(2,1)S(1)}, bf16[32,640]{1,0:T(8,128)(2,1)S(1)}, u32[]{:S(2)}, u32[]{:S(2)}) %collective-permute-start.22) | collective-permute-done | bytes 40992 | tf_op jit(solution)/shard_map/ppermute | solution.py:425
  66.4 0.6 collective-permute-done.23.refs_1_
  67.0 0.4 collective-permute-done.24.refs_2_
  67.4 0.1 products.1
  67.5 1.2 %collective-permute-start.26 = (f32[32,640]{1,0:T(8,128)S(1)}, f32[32,640]{1,0:T(8,128)S(1)}, u32[]{:S(2)}, u32[]{:S(2)}) collective-permute-start(f32[32,640]{1,0:T(8,128)S(1)} %get-tuple-element.72), channel_id=1, source_target_pairs={{0,2},{1,3},{2,0},{3,1},{4,6},{5,7},{6,4},{7,5},{8,10},{9,11},{10,... | collective-permute-start | bytes 245768 | tf_op jit(solution)/shard_map/ppermute | solution.py:425
  68.7 0.5 collective-permute-start.27
  69.2 1.7 %collective-permute-start.25 = (f32[32,128]{1,0:T(8,128)S(1)}, f32[32,128]{1,0:T(8,128)S(1)}, u32[]{:S(2)}, u32[]{:S(2)}) collective-permute-start(f32[32,128]{1,0:T(8,128)S(1)} %get-tuple-element.73), channel_id=1, source_target_pairs={{0,4},{4,0},{8,12},{12,8},{16,20},{20,16},{24,28},{28,24},{1,5},{5... | collective-permute-start | bytes 49160 | tf_op jit(solution)/shard_map/ppermute | solution.py:425
  71.0 2.4 %collective-permute-done.27 = f32[32,128]{1,0:T(8,128)S(1)} collective-permute-done((f32[32,128]{1,0:T(8,128)S(1)}, f32[32,128]{1,0:T(8,128)S(1)}, u32[]{:S(2)}, u32[]{:S(2)}) %collective-permute-start.27) | collective-permute-done | bytes 16416 | tf_op jit(solution)/shard_map/ppermute | solution.py:435
  73.5 1.4 %collective-permute-done.28.refs_1_ = f32[2,32,640]{2,1,0:T(8,128)S(1)} collective-permute-done((f32[2,32,640]{2,1,0:T(8,128)S(1)}, f32[2,32,640]{2,1,0:T(8,128)S(1)}, u32[]{:S(2)}, u32[]{:S(2)}) %collective-permute-start.28) | collective-permute-done | bytes 163872 | tf_op jit(solution)/shard_map/ppermute | solution.py:425
  74.9 1.2 %final.1 = (f32[32,2048]{1,0:T(8,128)}, f32[32,2048]{1,0:T(8,128)}) custom-call(f32[32,2048]{1,0:T(8,128)S(1)} %copy-done, f32[2,40,512]{2,1,0:T(8,128)S(1)} %pad_maximum_fusion.1.s1_own, f32[2,40,512]{2,1,0:T(8,128)S(1)} %collective-permute-done.17.s1_got, f32[2,32,640]{2,1,0:T(8,128)S(1)} %pad_maximum_fusion.2.refs_0_, ...), custom_call_target="tpu_custom_call" | custom-call | tf_op jit(solution)/shard_map/final/pallas_call | solution.py:657
  (52 shorter events, 1.2 us)
Async XLA Ops:
  0.6 5.7 %collective-permute-start = (s32[8,6]{1,0:T(8,128)}, s32[8,6]{1,0:T(8,128)S(1)}, u32[]{:S(2)}, u32[]{:S(2)}) collective-permute-start(s32[8,6]{1,0:T(8,128)} %param.3), channel_id=1, source_target_pairs={{0,1},{1,0},{2,3},{3,2},{4,5},{5,4},{6,7},{7,6},{8,9},{9,8},{10,11... | collective-permute-start | bytes 584 | tf_op jit(solution)/shard_map/ppermute | solution.py:425
  1.1 5.3 %collective-permute-start.2 = (s32[8,6]{1,0:T(8,128)}, s32[8,6]{1,0:T(8,128)S(1)}, u32[]{:S(2)}, u32[]{:S(2)}) collective-permute-start(s32[8,6]{1,0:T(8,128)} %param.3), channel_id=1, source_target_pairs={{0,3},{1,2},{2,1},{3,0},{4,7},{5,6},{6,5},{7,4},{8,11},{9,10},{10,... | collective-permute-start | bytes 584 | tf_op jit(solution)/shard_map/ppermute | solution.py:425
  3.8 3.8 %collective-permute-start.1 = (s32[8,6]{1,0:T(8,128)}, s32[8,6]{1,0:T(8,128)S(1)}, u32[]{:S(2)}, u32[]{:S(2)}) collective-permute-start(s32[8,6]{1,0:T(8,128)} %param.3), channel_id=1, source_target_pairs={{0,2},{1,3},{2,0},{3,1},{4,6},{5,7},{6,4},{7,5},{8,10},{9,11},{10,... | collective-permute-start | bytes 584 | tf_op jit(solution)/shard_map/ppermute | solution.py:425
  7.9 8.1 %collective-permute-start.5 = (bf16[16,640]{1,0:T(8,128)(2,1)S(1)}, bf16[16,640]{1,0:T(8,128)(2,1)S(1)}, u32[]{:S(2)}, u32[]{:S(2)}) collective-permute-start(bf16[16,640]{1,0:T(8,128)(2,1)S(1)} %pad_maximum_fusion.5), channel_id=1, source_target_pairs={{0,24},{4,28},{8,16},{12,20},{16,8},{20,12},{24,0},{28,4},{1,25},{... | collective-permute-start | bytes 61448 | tf_op jit(solution)/shard_map/ppermute | solution.py:425
  11.6 5.2 %collective-permute-start.4 = (bf16[16,640]{1,0:T(8,128)(2,1)S(1)}, bf16[16,640]{1,0:T(8,128)(2,1)S(1)}, u32[]{:S(2)}, u32[]{:S(2)}) collective-permute-start(bf16[16,640]{1,0:T(8,128)(2,1)S(1)} %pad_maximum_fusion.5), channel_id=1, source_target_pairs={{0,16},{4,20},{8,24},{12,28},{16,0},{20,4},{24,8},{28,12},{1,17},{... | collective-permute-start | bytes 61448 | tf_op jit(solution)/shard_map/ppermute | solution.py:425
  11.6 5.2 %collective-permute-start.3 = (bf16[16,640]{1,0:T(8,128)(2,1)S(1)}, bf16[16,640]{1,0:T(8,128)(2,1)S(1)}, u32[]{:S(2)}, u32[]{:S(2)}) collective-permute-start(bf16[16,640]{1,0:T(8,128)(2,1)S(1)} %pad_maximum_fusion.5), channel_id=1, source_target_pairs={{0,8},{4,12},{8,0},{12,4},{16,24},{20,28},{24,16},{28,20},{1,9},{5... | collective-permute-start | bytes 61448 | tf_op jit(solution)/shard_map/ppermute | solution.py:425
  12.3 9.8 %collective-permute-start.9 = (f32[32,512]{1,0:T(8,128)S(1)}, f32[32,512]{1,0:T(8,128)S(1)}, u32[]{:S(2)}, u32[]{:S(2)}) collective-permute-start(f32[32,512]{1,0:T(8,128)S(1)} %constant_dynamic-slice_fusion), channel_id=1, source_target_pairs={{0,24},{4,28},{8,16},{12,20},{16,8},{20,12},{24,0},{28,4},{1,25},{... | collective-permute-start | bytes 196616 | tf_op jit(solution)/shard_map/ppermute | solution.py:425
  15.9 6.2 %collective-permute-start.8 = (f32[32,512]{1,0:T(8,128)S(1)}, f32[32,512]{1,0:T(8,128)S(1)}, u32[]{:S(2)}, u32[]{:S(2)}) collective-permute-start(f32[32,512]{1,0:T(8,128)S(1)} %constant_dynamic-slice_fusion), channel_id=1, source_target_pairs={{0,16},{4,20},{8,24},{12,28},{16,0},{20,4},{24,8},{28,12},{1,17},{... | collective-permute-start | bytes 196616 | tf_op jit(solution)/shard_map/ppermute | solution.py:425
  15.9 6.2 %collective-permute-start.7 = (f32[32,512]{1,0:T(8,128)S(1)}, f32[32,512]{1,0:T(8,128)S(1)}, u32[]{:S(2)}, u32[]{:S(2)}) collective-permute-start(f32[32,512]{1,0:T(8,128)S(1)} %constant_dynamic-slice_fusion), channel_id=1, source_target_pairs={{0,8},{4,12},{8,0},{12,4},{16,24},{20,28},{24,16},{28,20},{1,9},{5... | collective-permute-start | bytes 196616 | tf_op jit(solution)/shard_map/ppermute | solution.py:425
  16.8 5.4 %collective-permute-start.6 = (bf16[4,16,640]{2,1,0:T(8,128)(2,1)S(1)}, bf16[4,16,640]{2,1,0:T(8,128)(2,1)S(1)}, u32[]{:S(2)}, u32[]{:S(2)}) collective-permute-start(bf16[4,16,640]{2,1,0:T(8,128)(2,1)S(1)} %pad_maximum_fusion.4.refs_1_), channel_id=1, source_target_pairs={{0,4},{4,0},{8,12},{12,8},{16,20},{20,16},{24,28},{28,24},{1,5},{5... | collective-permute-start | bytes 245768 | tf_op jit(solution)/shard_map/ppermute | solution.py:425
  26.1 21.8 %copy-start = (f32[32,2048]{1,0:T(8,128)S(1)}, f32[32,2048]{1,0:T(8,128)}, u32[]{:S(2)}) copy-start(f32[32,2048]{1,0:T(8,128)} %t_ref.5) | copy-start | bytes 786436
  26.1 4.8 %collective-permute-start.13 = (f32[16,256]{1,0:T(8,128)S(1)}, f32[16,256]{1,0:T(8,128)S(1)}, u32[]{:S(2)}, u32[]{:S(2)}) collective-permute-start(f32[16,256]{1,0:T(8,128)S(1)} %get-tuple-element.54), channel_id=1, source_target_pairs={{0,12},{4,8},{8,4},{12,0},{16,28},{20,24},{24,20},{28,16},{1,13},{... | collective-permute-start | bytes 49160 | tf_op jit(solution)/shard_map/ppermute | solution.py:425
  27.9 3.7 %collective-permute-start.12 = (f32[16,256]{1,0:T(8,128)S(1)}, f32[16,256]{1,0:T(8,128)S(1)}, u32[]{:S(2)}, u32[]{:S(2)}) collective-permute-start(f32[16,256]{1,0:T(8,128)S(1)} %get-tuple-element.54), channel_id=1, source_target_pairs={{0,8},{4,12},{8,0},{12,4},{16,24},{20,28},{24,16},{28,20},{1,9},{5... | collective-permute-start | bytes 49160 | tf_op jit(solution)/shard_map/ppermute | solution.py:425
  28.2 4.0 %collective-permute-start.11 = (f32[16,256]{1,0:T(8,128)S(1)}, f32[16,256]{1,0:T(8,128)S(1)}, u32[]{:S(2)}, u32[]{:S(2)}) collective-permute-start(f32[16,256]{1,0:T(8,128)S(1)} %get-tuple-element.54), channel_id=1, source_target_pairs={{0,4},{4,0},{8,12},{12,8},{16,20},{20,16},{24,28},{28,24},{1,5},{5... | collective-permute-start | bytes 49160 | tf_op jit(solution)/shard_map/ppermute | solution.py:425
  29.7 7.2 %collective-permute-start.10 = (f32[4,32,512]{2,1,0:T(8,128)S(1)}, f32[4,32,512]{2,1,0:T(8,128)S(1)}, u32[]{:S(2)}, u32[]{:S(2)}) collective-permute-start(f32[4,32,512]{2,1,0:T(8,128)S(1)} %pad_maximum_fusion.refs_2_.t_same), channel_id=1, source_target_pairs={{0,4},{4,0},{8,12},{12,8},{16,20},{20,16},{24,28},{28,24},{1,5},{5... | collective-permute-start | bytes 786440 | tf_op jit(solution)/shard_map/ppermute | solution.py:425
  32.2 4.7 %collective-permute-start.14 = (f32[16,256]{1,0:T(8,128)S(1)}, f32[16,256]{1,0:T(8,128)S(1)}, u32[]{:S(2)}, u32[]{:S(2)}) collective-permute-start(f32[16,256]{1,0:T(8,128)S(1)} %add_add_fusion), channel_id=1, source_target_pairs={{0,16},{4,20},{8,24},{12,28},{16,0},{20,4},{24,8},{28,12},{1,17},{... | collective-permute-start | bytes 49160 | tf_op jit(solution)/shard_map/ppermute | solution.py:425
  40.0 1.4 %collective-permute-start.15 = (f32[2,32,512]{2,1,0:T(8,128)S(1)}, f32[2,32,512]{2,1,0:T(8,128)S(1)}, u32[]{:S(2)}, u32[]{:S(2)}) collective-permute-start(f32[2,32,512]{2,1,0:T(8,128)S(1)} %get-tuple-element.56), channel_id=1, source_target_pairs={{0,1},{1,0},{2,3},{3,2},{4,5},{5,4},{6,7},{7,6},{8,9},{9,8},{10,11... | collective-permute-start | bytes 393224 | tf_op jit(solution)/shard_map/ppermute | solution.py:425
  41.4 6.3 %collective-permute-start.16 = (f32[72,512]{1,0:T(8,128)S(1)}, f32[72,512]{1,0:T(8,128)S(1)}, u32[]{:S(2)}, u32[]{:S(2)}) collective-permute-start(f32[72,512]{1,0:T(8,128)S(1)} %pad_maximum_fusion.3), channel_id=1, source_target_pairs={{0,2},{1,3},{2,0},{3,1},{4,6},{5,7},{6,4},{7,5},{8,10},{9,11},{10,... | collective-permute-start | bytes 442376 | tf_op jit(solution)/shard_map/ppermute | solution.py:425
  47.8 1.5 %collective-permute-start.17 = (f32[2,40,512]{2,1,0:T(8,128)S(1)}, f32[2,40,512]{2,1,0:T(8,128)S(1)}, u32[]{:S(2)}, u32[]{:S(2)}) collective-permute-start(f32[2,40,512]{2,1,0:T(8,128)S(1)} %pad_maximum_fusion.1.s1_own), channel_id=1, source_target_pairs={{0,1},{1,0},{2,3},{3,2},{4,5},{5,4},{6,7},{7,6},{8,9},{9,8},{10,11... | collective-permute-start | bytes 491528 | tf_op jit(solution)/shard_map/ppermute | solution.py:425
  50.9 9.5 %collective-permute-start.18 = (bf16[4,32,512]{2,1,0:T(8,128)(2,1)S(1)}, bf16[4,32,512]{2,1,0:T(8,128)(2,1)S(1)}, u32[]{:S(2)}, u32[]{:S(2)}) collective-permute-start(bf16[4,32,512]{2,1,0:T(8,128)(2,1)S(1)} %second.3), channel_id=1, source_target_pairs={{0,4},{4,0},{8,12},{12,8},{16,20},{20,16},{24,28},{28,24},{1,5},{5... | collective-permute-start | bytes 393224 | tf_op jit(solution)/shard_map/ppermute | solution.py:425
  52.0 6.1 %collective-permute-start.21 = (bf16[32,512]{1,0:T(8,128)(2,1)S(1)}, bf16[32,512]{1,0:T(8,128)(2,1)S(1)}, u32[]{:S(2)}, u32[]{:S(2)}) collective-permute-start(bf16[32,512]{1,0:T(8,128)(2,1)S(1)} %fusion.2.refs_0_), channel_id=1, source_target_pairs={{0,24},{4,28},{8,16},{12,20},{16,8},{20,12},{24,0},{28,4},{1,25},{... | collective-permute-start | bytes 98312 | tf_op jit(solution)/shard_map/ppermute | solution.py:425
  55.5 4.8 %collective-permute-start.20 = (bf16[32,512]{1,0:T(8,128)(2,1)S(1)}, bf16[32,512]{1,0:T(8,128)(2,1)S(1)}, u32[]{:S(2)}, u32[]{:S(2)}) collective-permute-start(bf16[32,512]{1,0:T(8,128)(2,1)S(1)} %fusion.2.refs_0_), channel_id=1, source_target_pairs={{0,16},{4,20},{8,24},{12,28},{16,0},{20,4},{24,8},{28,12},{1,17},{... | collective-permute-start | bytes 98312 | tf_op jit(solution)/shard_map/ppermute | solution.py:425
  55.5 4.8 %collective-permute-start.19 = (bf16[32,512]{1,0:T(8,128)(2,1)S(1)}, bf16[32,512]{1,0:T(8,128)(2,1)S(1)}, u32[]{:S(2)}, u32[]{:S(2)}) collective-permute-start(bf16[32,512]{1,0:T(8,128)(2,1)S(1)} %fusion.2.refs_0_), channel_id=1, source_target_pairs={{0,8},{4,12},{8,0},{12,4},{16,24},{20,28},{24,16},{28,20},{1,9},{5... | collective-permute-start | bytes 98312 | tf_op jit(solution)/shard_map/ppermute | solution.py:425
  60.5 5.9 %collective-permute-start.22 = (bf16[32,640]{1,0:T(8,128)(2,1)S(1)}, bf16[32,640]{1,0:T(8,128)(2,1)S(1)}, u32[]{:S(2)}, u32[]{:S(2)}) collective-permute-start(bf16[32,640]{1,0:T(8,128)(2,1)S(1)} %get-tuple-element.69), channel_id=1, source_target_pairs={{0,24},{4,28},{8,16},{12,20},{16,8},{20,12},{24,0},{28,4},{1,25},{... | collective-permute-start | bytes 122888 | tf_op jit(solution)/shard_map/ppermute | solution.py:425
  62.0 4.9 %collective-permute-start.23 = (bf16[32,640]{1,0:T(8,128)(2,1)S(1)}, bf16[32,640]{1,0:T(8,128)(2,1)S(1)}, u32[]{:S(2)}, u32[]{:S(2)}) collective-permute-start(bf16[32,640]{1,0:T(8,128)(2,1)S(1)} %get-tuple-element.70), channel_id=1, source_target_pairs={{0,16},{4,20},{8,24},{12,28},{16,0},{20,4},{24,8},{28,12},{1,17},{... | collective-permute-start | bytes 122888 | tf_op jit(solution)/shard_map/ppermute | solution.py:425
  62.7 4.7 %collective-permute-start.24 = (bf16[32,640]{1,0:T(8,128)(2,1)S(1)}, bf16[32,640]{1,0:T(8,128)(2,1)S(1)}, u32[]{:S(2)}, u32[]{:S(2)}) collective-permute-start(bf16[32,640]{1,0:T(8,128)(2,1)S(1)} %get-tuple-element.71), channel_id=1, source_target_pairs={{0,8},{4,12},{8,0},{12,4},{16,24},{20,28},{24,16},{28,20},{1,9},{5... | collective-permute-start | bytes 122888 | tf_op jit(solution)/shard_map/ppermute | solution.py:425
  67.5 5.9 %collective-permute-start.26 = (f32[32,640]{1,0:T(8,128)S(1)}, f32[32,640]{1,0:T(8,128)S(1)}, u32[]{:S(2)}, u32[]{:S(2)}) collective-permute-start(f32[32,640]{1,0:T(8,128)S(1)} %get-tuple-element.72), channel_id=1, source_target_pairs={{0,2},{1,3},{2,0},{3,1},{4,6},{5,7},{6,4},{7,5},{8,10},{9,11},{10,... | collective-permute-start | bytes 245768 | tf_op jit(solution)/shard_map/ppermute | solution.py:425
  68.7 4.6 %collective-permute-start.27 = (f32[32,128]{1,0:T(8,128)S(1)}, f32[32,128]{1,0:T(8,128)S(1)}, u32[]{:S(2)}, u32[]{:S(2)}) collective-permute-start(f32[32,128]{1,0:T(8,128)S(1)} %get-tuple-element.73), channel_id=1, source_target_pairs={{0,6},{1,7},{2,4},{3,5},{4,2},{5,3},{6,0},{7,1},{8,14},{9,15},{10,... | collective-permute-start | bytes 49160 | tf_op jit(solution)/shard_map/ppermute | solution.py:435
  69.2 4.1 %collective-permute-start.25 = (f32[32,128]{1,0:T(8,128)S(1)}, f32[32,128]{1,0:T(8,128)S(1)}, u32[]{:S(2)}, u32[]{:S(2)}) collective-permute-start(f32[32,128]{1,0:T(8,128)S(1)} %get-tuple-element.73), channel_id=1, source_target_pairs={{0,4},{4,0},{8,12},{12,8},{16,20},{20,16},{24,28},{28,24},{1,5},{5... | collective-permute-start | bytes 49160 | tf_op jit(solution)/shard_map/ppermute | solution.py:425
  73.4 1.5 %collective-permute-start.28 = (f32[2,32,640]{2,1,0:T(8,128)S(1)}, f32[2,32,640]{2,1,0:T(8,128)S(1)}, u32[]{:S(2)}, u32[]{:S(2)}) collective-permute-start(f32[2,32,640]{2,1,0:T(8,128)S(1)} %pad_maximum_fusion.2.refs_0_), channel_id=1, source_target_pairs={{0,1},{1,0},{2,3},{3,2},{4,5},{5,4},{6,7},{7,6},{8,9},{9,8},{10,11... | collective-permute-start | bytes 491528 | tf_op jit(solution)/shard_map/ppermute | solution.py:425

commit v16 on v15

--- a/solution.py
+++ b/solution.py
@@ -337,7 +337,8 @@
 
 
 def meet_kernel(cfg, z_same, z_other, t_same, inv_ref, s1_own, *refs):
-    gs, (own_z, own_dots, *outs) = refs[:4], refs[4:]
+    g_near, g_far, own_z, own_dots, *outs = refs
+    gs = g_near[0], g_near[1], g_far[0], g_far[1]
     own_rows, block_len = cfg.own_rows, cfg.block_len
     outputs, own_len = own_z.shape
     place = position()
@@ -349,7 +350,7 @@
             own_z[...] = z
         else:
             outs[n - 1][:, :own_len] = z.astype(BF16)
-        gz += jnp.sum(gs[n][...].astype(F32) * z, axis=1, keepdims=True)
+        gz += jnp.sum(gs[n].astype(F32) * z, axis=1, keepdims=True)
         at = row_of(cfg, place, 0, slot_of(cfg, place, n)) * own_rows
         for k in range(own_rows):
             cols = slice(k * block_len, (k + 1) * block_len)
@@ -612,20 +613,23 @@
 
     if direct_rows:
         g = ((s1_own[0, :outputs] - SHIFT * own_t) * tail[:1]).astype(BF16)
-        z2_other, g = lax.optimization_barrier((second(1, BF16), g))
+        parts_of_g = (g, swap(g, "rows", 2))
+        z2_other = second(1, BF16)
+        _, *parts_of_g = lax.optimization_barrier((z2_other, *parts_of_g))
+        g = jnp.stack(parts_of_g)
         z2_other = swap(z2_other, "rows", 1)
-        gs = along_z(g)
+        far_g = swap(g, "rows", 4)
         z2_same = second(0, F32)
-        z2_same, z2_other, *gs = lax.optimization_barrier((z2_same, z2_other, *gs))
+        z2_same, z2_other, far_g = lax.optimization_barrier((z2_same, z2_other, far_g))
         row_piece = shape(outputs, own_len + LANES, dtype=BF16)
         own_z, own_dots, *sends = pl.pallas_call(
             functools.partial(meet_kernel, cfg),
             out_shape=[shape(outputs, own_len), shape(outputs, LANES, dtype=BF16)] + [row_piece] * 3,
-            in_specs=[VMEM] * 9,
+            in_specs=[VMEM] * 7,
             out_specs=[VMEM] * 5,
             compiler_params=limit,
             name="meet",
-        )(z2_same, z2_other, t_pieces[0], inv, s1_own, *gs)
+        )(z2_same, z2_other, t_pieces[0], inv, s1_own, g, far_g)
         got = [swap(sends[n], "rows", 2 * n + 2) for n in (2, 1, 0)]
         ends, dots = pl.pallas_call(
             product_kernel,

time: 76.7 us -> 75.9 us (0.990)
  waiting for transfers between devices: 20.8 us -> 23.2 us
  starting transfers between devices: 35.9 us -> 33.9 us
  Pallas kernels: 15.2 us -> 14.2 us
    ppermute x28 -> x27, starting transfers between devices: 35.3 us -> 33.4 us  [swap(): return lax.ppermute(x, axis, [(i, i ^ d) for i in range(size)])]
    ppermute x28 -> x27, waiting for transfers between devices: 18.5 us -> 20.4 us  [swap(): return lax.ppermute(x, axis, [(i, i ^ d) for i in range(size)])]
  transfers between devices with their start and end apart: 29 -> 28, of which waited for: 15 -> 11; matrix products, arithmetic and copies ran while one was open for 4% -> 4% of each run, Pallas kernels for 7% -> 9%
where the time goes in v16:
time: 75.9 us; the launch traced here: 75.4 us
  starting transfers between devices  33.9 us (45%)
  waiting for transfers between devices  23.2 us (31%)
  Pallas kernels  14.2 us (19%)
  local copies, waits for them, and re-layouts  2.75 us (4%)
  between operations  0.87 us (1%)
    ppermute x27, starting transfers between devices, swap(): return lax.ppermute(x, axis, [(i, i ^ d) for i in range(size)])  33.4 us
    ppermute x27, waiting for transfers between devices, swap(): return lax.ppermute(x, axis, [(i, i ^ d) for i in range(size)])  20.4 us
    pallas_call x2, Pallas kernels, build(): pl.pallas_call(functools.partial(build_kernel, cfg, part), out_shape=out,...  7.18 us
    ppermute x1, waiting for transfers between devices, both_swap(): return lax.ppermute(x, ('rows', 'cols'), pairs)  2.86 us
    pallas_call x2, Pallas kernels, second(): pl.pallas_call(functools.partial(second_kernel, cfg, part), out_shape=sha...  2.8 us
    pallas_call x1, Pallas kernels, local(): pl.pallas_call(functools.partial(first_kernel, cfg), out_shape=[shape(out...  2.79 us
    dynamic_slice x2, local copies, waits for them, and re-layouts, own(): return lax.dynamic_slice_in_dim(x, col * own_len, own_len, 1)  1.56 us
  transfers between devices with their start and end apart: 28, of which 11 were waited for; matrix products, arithmetic and copies ran while one was open for 4% of the time, Pallas kernels for 9%

profile of v16, /device:TPU:0, one launch (start us, length us, event | category | flops | bytes accessed | tf_op | source)
XLA Modules:
  0.0 75.4 jit_solution(18298839485295853384)
XLA Ops:
  0.6 0.5 collective-permute-start
  1.1 2.6 %collective-permute-start.2 = (s32[8,6]{1,0:T(8,128)}, s32[8,6]{1,0:T(8,128)S(1)}, u32[]{:S(2)}, u32[]{:S(2)}) collective-permute-start(s32[8,6]{1,0:T(8,128)} %param.3), channel_id=1, source_target_pairs={{0,3},{1,2},{2,1},{3,0},{4,7},{5,6},{6,5},{7,4},{8,11},{9,10},{10,... | collective-permute-start | bytes 584 | tf_op jit(solution)/shard_map/ppermute | solution.py:426
  3.8 0.8 %copy.6 = s32[8,6]{0,1:T(8,128)S(1)} copy(s32[8,6]{1,0:T(8,128)} %param.3) | data formatting | bytes 384 | tf_op args[0]
  4.7 0.7 constant_dynamic-slice_fusion.1
  5.5 0.8 %constant_dynamic-slice_fusion = f32[32,512]{1,0:T(8,128)S(1)} fusion(f32[32,2048]{1,0:T(8,128)} %t_ref.5, s32[]{:T(128)S(6)} %select_n.7), kind=kLoop, calls=%fused_computation.37 | loop fusion | bytes 131076 | tf_op jit(solution)/shard_map/dynamic_slice | solution.py:487
  6.3 0.1 copy.7
  6.4 0.1 convert_reduce_fusion.2
  6.5 0.1 copy.9
  6.6 0.1 convert_reduce_fusion
  6.6 1.0 %collective-permute-done.1 = s32[8,6]{1,0:T(8,128)S(1)} collective-permute-done((s32[8,6]{1,0:T(8,128)}, s32[8,6]{1,0:T(8,128)S(1)}, u32[]{:S(2)}, u32[]{:S(2)}) %collective-permute-start.1) | collective-permute-done | bytes 224 | tf_op jit(solution)/shard_map/ppermute | solution.py:426
  7.6 0.1 copy.8
  7.8 0.1 reshape.14
  7.9 3.7 %collective-permute-start.5 = (bf16[16,640]{1,0:T(8,128)(2,1)S(1)}, bf16[16,640]{1,0:T(8,128)(2,1)S(1)}, u32[]{:S(2)}, u32[]{:S(2)}) collective-permute-start(bf16[16,640]{1,0:T(8,128)(2,1)S(1)} %pad_maximum_fusion.6), channel_id=1, source_target_pairs={{0,24},{4,28},{8,16},{12,20},{16,8},{20,12},{24,0},{28,4},{1,25},{... | collective-permute-start | bytes 61448 | tf_op jit(solution)/shard_map/ppermute | solution.py:426
  11.6 0.8 %collective-permute-start.3 = (bf16[16,640]{1,0:T(8,128)(2,1)S(1)}, bf16[16,640]{1,0:T(8,128)(2,1)S(1)}, u32[]{:S(2)}, u32[]{:S(2)}) collective-permute-start(bf16[16,640]{1,0:T(8,128)(2,1)S(1)} %pad_maximum_fusion.6), channel_id=1, source_target_pairs={{0,8},{4,12},{8,0},{12,4},{16,24},{20,28},{24,16},{28,20},{1,9},{5... | collective-permute-start | bytes 61448 | tf_op jit(solution)/shard_map/ppermute | solution.py:426
  12.3 3.6 %collective-permute-start.9 = (f32[32,512]{1,0:T(8,128)S(1)}, f32[32,512]{1,0:T(8,128)S(1)}, u32[]{:S(2)}, u32[]{:S(2)}) collective-permute-start(f32[32,512]{1,0:T(8,128)S(1)} %constant_dynamic-slice_fusion), channel_id=1, source_target_pairs={{0,24},{4,28},{8,16},{12,20},{16,8},{20,12},{24,0},{28,4},{1,25},{... | collective-permute-start | bytes 196616 | tf_op jit(solution)/shard_map/ppermute | solution.py:426
  15.9 0.8 %collective-permute-start.7 = (f32[32,512]{1,0:T(8,128)S(1)}, f32[32,512]{1,0:T(8,128)S(1)}, u32[]{:S(2)}, u32[]{:S(2)}) collective-permute-start(f32[32,512]{1,0:T(8,128)S(1)} %constant_dynamic-slice_fusion), channel_id=1, source_target_pairs={{0,8},{4,12},{8,0},{12,4},{16,24},{20,28},{24,16},{28,20},{1,9},{5... | collective-permute-start | bytes 196616 | tf_op jit(solution)/shard_map/ppermute | solution.py:426
  16.8 1.6 %collective-permute-start.6 = (bf16[4,16,640]{2,1,0:T(8,128)(2,1)S(1)}, bf16[4,16,640]{2,1,0:T(8,128)(2,1)S(1)}, u32[]{:S(2)}, u32[]{:S(2)}) collective-permute-start(bf16[4,16,640]{2,1,0:T(8,128)(2,1)S(1)} %pad_maximum_fusion.4.refs_1_), channel_id=1, source_target_pairs={{0,4},{4,0},{8,12},{12,8},{16,20},{20,16},{24,28},{28,24},{1,5},{5... | collective-permute-start | bytes 245768 | tf_op jit(solution)/shard_map/ppermute | solution.py:426
  18.3 3.8 %build.2 = (bf16[32,4,256,256]{3,2,1,0:T(8,128)(2,1)S(1)}, s32[1,128]{1,0:T(1,128)S(1)}, f32[8,256]{1,0:T(8,128)S(1)}, bf16[8,256,32]{2,1,0:T(8,128)(2,1)S(1)}) custom-call(s32[8,64]{1,0:T(8,128)S(1)} %add_add_fusion.1.direct_v, bf16[16,2048]{1,0:T(8,128)(2,1)} %refs_0_.1, bf16[4,16,640]{2,1,0:T(8,128)(2,1)S(1)} %pad_maximum_fusion.4.refs_1_), custom_call_target="tpu_custom_call" | custom-call | flops 2684354560 | bytes 83886080 | tf_op jit(solution)/shard_map/build/pallas_call | solution.py:512
  22.2 3.3 %build.3 = (bf16[32,4,256,256]{3,2,1,0:T(8,128)(2,1)S(1)}, s32[1,128]{1,0:T(1,128)S(1)}, f32[16,256]{1,0:T(8,128)S(1)}) custom-call(s32[8,64]{1,0:T(8,128)S(1)} %add_add_fusion.1.direct_v, bf16[8,256,32]{2,1,0:T(8,128)(2,1)S(1)} %get-tuple-element.36.refs_0_, f32[8,256]{1,0:T(8,128)S(1)} %get-tuple-element.39.refs_1_, ...), custom_call_target="tpu_custom_call", output_to_operand_aliasing={{0}: (4, {})} | custom-call | flops 2684354560 | bytes 83886080 | tf_op jit(solution)/shard_map/build/pallas_call | solution.py:512
  25.6 1.8 %collective-permute-start.13 = (f32[16,256]{1,0:T(8,128)S(1)}, f32[16,256]{1,0:T(8,128)S(1)}, u32[]{:S(2)}, u32[]{:S(2)}) collective-permute-start(f32[16,256]{1,0:T(8,128)S(1)} %get-tuple-element.51), channel_id=1, source_target_pairs={{0,12},{4,8},{8,4},{12,0},{16,28},{20,24},{24,20},{28,16},{1,13},{... | collective-permute-start | bytes 49160 | tf_op jit(solution)/shard_map/ppermute | solution.py:426
  27.4 1.8 %collective-permute-start.12 = (f32[16,256]{1,0:T(8,128)S(1)}, f32[16,256]{1,0:T(8,128)S(1)}, u32[]{:S(2)}, u32[]{:S(2)}) collective-permute-start(f32[16,256]{1,0:T(8,128)S(1)} %get-tuple-element.51), channel_id=1, source_target_pairs={{0,8},{4,12},{8,0},{12,4},{16,24},{20,28},{24,16},{28,20},{1,9},{5... | collective-permute-start | bytes 49160 | tf_op jit(solution)/shard_map/ppermute | solution.py:426
  29.3 2.0 %collective-permute-start.10 = (f32[4,32,512]{2,1,0:T(8,128)S(1)}, f32[4,32,512]{2,1,0:T(8,128)S(1)}, u32[]{:S(2)}, u32[]{:S(2)}) collective-permute-start(f32[4,32,512]{2,1,0:T(8,128)S(1)} %pad_maximum_fusion.refs_2_.t_same), channel_id=1, source_target_pairs={{0,4},{4,0},{8,12},{12,8},{16,20},{20,16},{24,28},{28,24},{1,5},{5... | collective-permute-start | bytes 786440 | tf_op jit(solution)/shard_map/ppermute | solution.py:426
  31.3 1.7 %collective-permute-done.11 = f32[16,256]{1,0:T(8,128)S(1)} collective-permute-done((f32[16,256]{1,0:T(8,128)S(1)}, f32[16,256]{1,0:T(8,128)S(1)}, u32[]{:S(2)}, u32[]{:S(2)}) %collective-permute-start.11) | collective-permute-done | bytes 16416 | tf_op jit(solution)/shard_map/ppermute | solution.py:426
  33.0 1.5 %collective-permute-start.14 = (f32[16,256]{1,0:T(8,128)S(1)}, f32[16,256]{1,0:T(8,128)S(1)}, u32[]{:S(2)}, u32[]{:S(2)}) collective-permute-start(f32[16,256]{1,0:T(8,128)S(1)} %add_add_fusion), channel_id=1, source_target_pairs={{0,16},{4,20},{8,24},{12,28},{16,0},{20,4},{24,8},{28,12},{1,17},{... | collective-permute-start | bytes 49160 | tf_op jit(solution)/shard_map/ppermute | solution.py:426
  34.5 3.3 %collective-permute-done.14 = f32[16,256]{1,0:T(8,128)S(1)} collective-permute-done((f32[16,256]{1,0:T(8,128)S(1)}, f32[16,256]{1,0:T(8,128)S(1)}, u32[]{:S(2)}, u32[]{:S(2)}) %collective-permute-start.14) | collective-permute-done | bytes 16416 | tf_op jit(solution)/shard_map/ppermute | solution.py:426
  37.8 2.8 %first.1 = (f32[32,512]{1,0:T(8,128)S(1)}, f32[32,512]{1,0:T(8,128)S(1)}, f32[2,32,512]{2,1,0:T(8,128)S(1)}, f32[8,512]{1,0:T(8,128)S(1)}) custom-call(bf16[32,4,256,256]{3,2,1,0:T(8,128)(2,1)S(1)} %get-tuple-element.47.k_mat, s32[1,128]{1,0:T(1,128)S(1)} %get-tuple-element.48.refs_0_.list_v, s32[1,128]{1,0:T(1,128)S(1)} %get-tuple-element.49.refs_1_.list_v, ...), custom_call_target="tpu_custom_call" | custom-call | flops 536870912 | bytes 8388608 | tf_op jit(solution)/shard_map/first/pallas_call | solution.py:568
  40.6 1.3 %collective-permute-done.15 = f32[2,32,512]{2,1,0:T(8,128)S(1)} collective-permute-done((f32[2,32,512]{2,1,0:T(8,128)S(1)}, f32[2,32,512]{2,1,0:T(8,128)S(1)}, u32[]{:S(2)}, u32[]{:S(2)}) %collective-permute-start.15) | collective-permute-done | bytes 131104 | tf_op jit(solution)/shard_map/ppermute | solution.py:426
  42.0 0.9 %collective-permute-start.16 = (f32[72,512]{1,0:T(8,128)S(1)}, f32[72,512]{1,0:T(8,128)S(1)}, u32[]{:S(2)}, u32[]{:S(2)}) collective-permute-start(f32[72,512]{1,0:T(8,128)S(1)} %pad_maximum_fusion.3), channel_id=1, source_target_pairs={{0,2},{1,3},{2,0},{3,1},{4,6},{5,7},{6,4},{7,5},{8,10},{9,11},{10,... | collective-permute-start | bytes 442376 | tf_op jit(solution)/shard_map/ppermute | solution.py:426
  42.9 5.1 %collective-permute-done.16 = f32[72,512]{1,0:T(8,128)S(1)} collective-permute-done((f32[72,512]{1,0:T(8,128)S(1)}, f32[72,512]{1,0:T(8,128)S(1)}, u32[]{:S(2)}, u32[]{:S(2)}) %collective-permute-start.16) | collective-permute-done | bytes 147488 | tf_op jit(solution)/shard_map/ppermute | solution.py:426
  48.2 0.7 collective-permute-start.19
  48.9 0.6 collective-permute-done.17.s1_got
  49.5 1.4 %second.3 = bf16[4,32,512]{2,1,0:T(8,128)(2,1)S(1)} custom-call(bf16[32,4,256,256]{3,2,1,0:T(8,128)(2,1)S(1)} %get-tuple-element.47.k_mat, s32[1,128]{1,0:T(1,128)S(1)} %get-tuple-element.49.refs_1_.list_v, f32[32,2048]{1,0:T(8,128)S(1)} %copy-done, f32[2,40,512]{2,1,0:T(8,128)S(1)} %pad_maximum_fusion.1.s1_own, f32[2,40,512]{2,1,0:T(8,128)S(1)} %collective-permute-done.17.s1_got), custom_call_target="tpu_custom_call" | custom-call | flops 268435456 | bytes 4194304 | tf_op jit(solution)/shard_map/second/pallas_call | solution.py:597
  50.9 1.3 %collective-permute-start.18 = (bf16[4,32,512]{2,1,0:T(8,128)(2,1)S(1)}, bf16[4,32,512]{2,1,0:T(8,128)(2,1)S(1)}, u32[]{:S(2)}, u32[]{:S(2)}) collective-permute-start(bf16[4,32,512]{2,1,0:T(8,128)(2,1)S(1)} %second.3), channel_id=1, source_target_pairs={{0,4},{4,0},{8,12},{12,8},{16,20},{20,16},{24,28},{28,24},{1,5},{5... | collective-permute-start | bytes 393224 | tf_op jit(solution)/shard_map/ppermute | solution.py:426
  52.2 2.1 %collective-permute-start.20 = (bf16[2,32,512]{2,1,0:T(8,128)(2,1)S(1)}, bf16[2,32,512]{2,1,0:T(8,128)(2,1)S(1)}, u32[]{:S(2)}, u32[]{:S(2)}) collective-permute-start(bf16[2,32,512]{2,1,0:T(8,128)(2,1)S(1)} %pad_maximum_fusion.5.refs_0_), channel_id=1, source_target_pairs={{0,16},{4,20},{8,24},{12,28},{16,0},{20,4},{24,8},{28,12},{1,17},{... | collective-permute-start | bytes 196616 | tf_op jit(solution)/shard_map/ppermute | solution.py:426
  54.3 1.4 %second.2.z_same = f32[4,32,512]{2,1,0:T(8,128)S(1)} custom-call(bf16[32,4,256,256]{3,2,1,0:T(8,128)(2,1)S(1)} %get-tuple-element.47.k_mat, s32[1,128]{1,0:T(1,128)S(1)} %get-tuple-element.48.refs_0_.list_v, f32[32,2048]{1,0:T(8,128)S(1)} %copy-done, f32[2,40,512]{2,1,0:T(8,128)S(1)} %pad_maximum_fusion.1.s1_own, ...), custom_call_target="tpu_custom_call" | custom-call | flops 268435456 | bytes 4194304 | tf_op jit(solution)/shard_map/second/pallas_call | solution.py:597
  55.7 2.7 %collective-permute-done.20.refs_1_ = bf16[2,32,512]{2,1,0:T(8,128)(2,1)S(1)} collective-permute-done((bf16[2,32,512]{2,1,0:T(8,128)(2,1)S(1)}, bf16[2,32,512]{2,1,0:T(8,128)(2,1)S(1)}, u32[]{:S(2)}, u32[]{:S(2)}) %collective-permute-start.20) | collective-permute-done | bytes 65568 | tf_op jit(solution)/shard_map/ppermute | solution.py:426
  58.4 0.2 meet.1
  58.6 2.8 %collective-permute-start.21 = (bf16[32,640]{1,0:T(8,128)(2,1)S(1)}, bf16[32,640]{1,0:T(8,128)(2,1)S(1)}, u32[]{:S(2)}, u32[]{:S(2)}) collective-permute-start(bf16[32,640]{1,0:T(8,128)(2,1)S(1)} %get-tuple-element.63), channel_id=1, source_target_pairs={{0,24},{4,28},{8,16},{12,20},{16,8},{20,12},{24,0},{28,4},{1,25},{... | collective-permute-start | bytes 122888 | tf_op jit(solution)/shard_map/ppermute | solution.py:426
  61.4 1.7 %collective-permute-start.23 = (bf16[32,640]{1,0:T(8,128)(2,1)S(1)}, bf16[32,640]{1,0:T(8,128)(2,1)S(1)}, u32[]{:S(2)}, u32[]{:S(2)}) collective-permute-start(bf16[32,640]{1,0:T(8,128)(2,1)S(1)} %get-tuple-element.65), channel_id=1, source_target_pairs={{0,8},{4,12},{8,0},{12,4},{16,24},{20,28},{24,16},{28,20},{1,9},{5... | collective-permute-start | bytes 122888 | tf_op jit(solution)/shard_map/ppermute | solution.py:426
  63.1 1.4 %collective-permute-done.21.refs_0_ = bf16[32,640]{1,0:T(8,128)(2,1)S(1)} collective-permute-done((bf16[32,640]{1,0:T(8,128)(2,1)S(1)}, bf16[32,640]{1,0:T(8,128)(2,1)S(1)}, u32[]{:S(2)}, u32[]{:S(2)}) %collective-permute-start.21) | collective-permute-done | bytes 40992 | tf_op jit(solution)/shard_map/ppermute | solution.py:426
  64.5 1.8 %collective-permute-done.22.refs_1_ = bf16[32,640]{1,0:T(8,128)(2,1)S(1)} collective-permute-done((bf16[32,640]{1,0:T(8,128)(2,1)S(1)}, bf16[32,640]{1,0:T(8,128)(2,1)S(1)}, u32[]{:S(2)}, u32[]{:S(2)}) %collective-permute-start.22) | collective-permute-done | bytes 40992 | tf_op jit(solution)/shard_map/ppermute | solution.py:426
  66.3 0.1 products.1
  66.4 1.7 %collective-permute-start.25 = (f32[32,640]{1,0:T(8,128)S(1)}, f32[32,640]{1,0:T(8,128)S(1)}, u32[]{:S(2)}, u32[]{:S(2)}) collective-permute-start(f32[32,640]{1,0:T(8,128)S(1)} %get-tuple-element.66), channel_id=1, source_target_pairs={{0,2},{1,3},{2,0},{3,1},{4,6},{5,7},{6,4},{7,5},{8,10},{9,11},{10,... | collective-permute-start | bytes 245768 | tf_op jit(solution)/shard_map/ppermute | solution.py:426
  68.1 0.4 collective-permute-start.26
  68.5 1.4 %collective-permute-start.24 = (f32[32,128]{1,0:T(8,128)S(1)}, f32[32,128]{1,0:T(8,128)S(1)}, u32[]{:S(2)}, u32[]{:S(2)}) collective-permute-start(f32[32,128]{1,0:T(8,128)S(1)} %get-tuple-element.67), channel_id=1, source_target_pairs={{0,4},{4,0},{8,12},{12,8},{16,20},{20,16},{24,28},{28,24},{1,5},{5... | collective-permute-start | bytes 49160 | tf_op jit(solution)/shard_map/ppermute | solution.py:426
  69.9 2.9 %collective-permute-done.26 = f32[32,128]{1,0:T(8,128)S(1)} collective-permute-done((f32[32,128]{1,0:T(8,128)S(1)}, f32[32,128]{1,0:T(8,128)S(1)}, u32[]{:S(2)}, u32[]{:S(2)}) %collective-permute-start.26) | collective-permute-done | bytes 16416 | tf_op jit(solution)/shard_map/ppermute | solution.py:436
  72.9 1.4 %collective-permute-done.27.refs_1_ = f32[2,32,640]{2,1,0:T(8,128)S(1)} collective-permute-done((f32[2,32,640]{2,1,0:T(8,128)S(1)}, f32[2,32,640]{2,1,0:T(8,128)S(1)}, u32[]{:S(2)}, u32[]{:S(2)}) %collective-permute-start.27) | collective-permute-done | bytes 163872 | tf_op jit(solution)/shard_map/ppermute | solution.py:426
  74.3 1.2 %final.1 = (f32[32,2048]{1,0:T(8,128)}, f32[32,2048]{1,0:T(8,128)}) custom-call(f32[32,2048]{1,0:T(8,128)S(1)} %copy-done, f32[2,40,512]{2,1,0:T(8,128)S(1)} %pad_maximum_fusion.1.s1_own, f32[2,40,512]{2,1,0:T(8,128)S(1)} %collective-permute-done.17.s1_got, f32[2,32,640]{2,1,0:T(8,128)S(1)} %pad_maximum_fusion.2.refs_0_, ...), custom_call_target="tpu_custom_call" | custom-call | tf_op jit(solution)/shard_map/final/pallas_call | solution.py:661
  (51 shorter events, 0.7 us)
Async XLA Ops:
  0.6 5.7 %collective-permute-start = (s32[8,6]{1,0:T(8,128)}, s32[8,6]{1,0:T(8,128)S(1)}, u32[]{:S(2)}, u32[]{:S(2)}) collective-permute-start(s32[8,6]{1,0:T(8,128)} %param.3), channel_id=1, source_target_pairs={{0,1},{1,0},{2,3},{3,2},{4,5},{5,4},{6,7},{7,6},{8,9},{9,8},{10,11... | collective-permute-start | bytes 584 | tf_op jit(solution)/shard_map/ppermute | solution.py:426
  1.1 5.3 %collective-permute-start.2 = (s32[8,6]{1,0:T(8,128)}, s32[8,6]{1,0:T(8,128)S(1)}, u32[]{:S(2)}, u32[]{:S(2)}) collective-permute-start(s32[8,6]{1,0:T(8,128)} %param.3), channel_id=1, source_target_pairs={{0,3},{1,2},{2,1},{3,0},{4,7},{5,6},{6,5},{7,4},{8,11},{9,10},{10,... | collective-permute-start | bytes 584 | tf_op jit(solution)/shard_map/ppermute | solution.py:426
  3.8 3.8 %collective-permute-start.1 = (s32[8,6]{1,0:T(8,128)}, s32[8,6]{1,0:T(8,128)S(1)}, u32[]{:S(2)}, u32[]{:S(2)}) collective-permute-start(s32[8,6]{1,0:T(8,128)} %param.3), channel_id=1, source_target_pairs={{0,2},{1,3},{2,0},{3,1},{4,6},{5,7},{6,4},{7,5},{8,10},{9,11},{10,... | collective-permute-start | bytes 584 | tf_op jit(solution)/shard_map/ppermute | solution.py:426
  7.9 8.1 %collective-permute-start.5 = (bf16[16,640]{1,0:T(8,128)(2,1)S(1)}, bf16[16,640]{1,0:T(8,128)(2,1)S(1)}, u32[]{:S(2)}, u32[]{:S(2)}) collective-permute-start(bf16[16,640]{1,0:T(8,128)(2,1)S(1)} %pad_maximum_fusion.6), channel_id=1, source_target_pairs={{0,24},{4,28},{8,16},{12,20},{16,8},{20,12},{24,0},{28,4},{1,25},{... | collective-permute-start | bytes 61448 | tf_op jit(solution)/shard_map/ppermute | solution.py:426
  11.6 5.2 %collective-permute-start.4 = (bf16[16,640]{1,0:T(8,128)(2,1)S(1)}, bf16[16,640]{1,0:T(8,128)(2,1)S(1)}, u32[]{:S(2)}, u32[]{:S(2)}) collective-permute-start(bf16[16,640]{1,0:T(8,128)(2,1)S(1)} %pad_maximum_fusion.6), channel_id=1, source_target_pairs={{0,16},{4,20},{8,24},{12,28},{16,0},{20,4},{24,8},{28,12},{1,17},{... | collective-permute-start | bytes 61448 | tf_op jit(solution)/shard_map/ppermute | solution.py:426
  11.6 5.2 %collective-permute-start.3 = (bf16[16,640]{1,0:T(8,128)(2,1)S(1)}, bf16[16,640]{1,0:T(8,128)(2,1)S(1)}, u32[]{:S(2)}, u32[]{:S(2)}) collective-permute-start(bf16[16,640]{1,0:T(8,128)(2,1)S(1)} %pad_maximum_fusion.6), channel_id=1, source_target_pairs={{0,8},{4,12},{8,0},{12,4},{16,24},{20,28},{24,16},{28,20},{1,9},{5... | collective-permute-start | bytes 61448 | tf_op jit(solution)/shard_map/ppermute | solution.py:426
  12.3 9.8 %collective-permute-start.9 = (f32[32,512]{1,0:T(8,128)S(1)}, f32[32,512]{1,0:T(8,128)S(1)}, u32[]{:S(2)}, u32[]{:S(2)}) collective-permute-start(f32[32,512]{1,0:T(8,128)S(1)} %constant_dynamic-slice_fusion), channel_id=1, source_target_pairs={{0,24},{4,28},{8,16},{12,20},{16,8},{20,12},{24,0},{28,4},{1,25},{... | collective-permute-start | bytes 196616 | tf_op jit(solution)/shard_map/ppermute | solution.py:426
  15.9 6.2 %collective-permute-start.8 = (f32[32,512]{1,0:T(8,128)S(1)}, f32[32,512]{1,0:T(8,128)S(1)}, u32[]{:S(2)}, u32[]{:S(2)}) collective-permute-start(f32[32,512]{1,0:T(8,128)S(1)} %constant_dynamic-slice_fusion), channel_id=1, source_target_pairs={{0,16},{4,20},{8,24},{12,28},{16,0},{20,4},{24,8},{28,12},{1,17},{... | collective-permute-start | bytes 196616 | tf_op jit(solution)/shard_map/ppermute | solution.py:426
  15.9 6.2 %collective-permute-start.7 = (f32[32,512]{1,0:T(8,128)S(1)}, f32[32,512]{1,0:T(8,128)S(1)}, u32[]{:S(2)}, u32[]{:S(2)}) collective-permute-start(f32[32,512]{1,0:T(8,128)S(1)} %constant_dynamic-slice_fusion), channel_id=1, source_target_pairs={{0,8},{4,12},{8,0},{12,4},{16,24},{20,28},{24,16},{28,20},{1,9},{5... | collective-permute-start | bytes 196616 | tf_op jit(solution)/shard_map/ppermute | solution.py:426
  16.8 5.4 %collective-permute-start.6 = (bf16[4,16,640]{2,1,0:T(8,128)(2,1)S(1)}, bf16[4,16,640]{2,1,0:T(8,128)(2,1)S(1)}, u32[]{:S(2)}, u32[]{:S(2)}) collective-permute-start(bf16[4,16,640]{2,1,0:T(8,128)(2,1)S(1)} %pad_maximum_fusion.4.refs_1_), channel_id=1, source_target_pairs={{0,4},{4,0},{8,12},{12,8},{16,20},{20,16},{24,28},{28,24},{1,5},{5... | collective-permute-start | bytes 245768 | tf_op jit(solution)/shard_map/ppermute | solution.py:426
  25.6 22.6 %copy-start = (f32[32,2048]{1,0:T(8,128)S(1)}, f32[32,2048]{1,0:T(8,128)}, u32[]{:S(2)}) copy-start(f32[32,2048]{1,0:T(8,128)} %t_ref.5) | copy-start | bytes 786436
  25.6 5.7 %collective-permute-start.13 = (f32[16,256]{1,0:T(8,128)S(1)}, f32[16,256]{1,0:T(8,128)S(1)}, u32[]{:S(2)}, u32[]{:S(2)}) collective-permute-start(f32[16,256]{1,0:T(8,128)S(1)} %get-tuple-element.51), channel_id=1, source_target_pairs={{0,12},{4,8},{8,4},{12,0},{16,28},{20,24},{24,20},{28,16},{1,13},{... | collective-permute-start | bytes 49160 | tf_op jit(solution)/shard_map/ppermute | solution.py:426
  27.4 3.9 %collective-permute-start.12 = (f32[16,256]{1,0:T(8,128)S(1)}, f32[16,256]{1,0:T(8,128)S(1)}, u32[]{:S(2)}, u32[]{:S(2)}) collective-permute-start(f32[16,256]{1,0:T(8,128)S(1)} %get-tuple-element.51), channel_id=1, source_target_pairs={{0,8},{4,12},{8,0},{12,4},{16,24},{20,28},{24,16},{28,20},{1,9},{5... | collective-permute-start | bytes 49160 | tf_op jit(solution)/shard_map/ppermute | solution.py:426
  29.2 3.7 %collective-permute-start.11 = (f32[16,256]{1,0:T(8,128)S(1)}, f32[16,256]{1,0:T(8,128)S(1)}, u32[]{:S(2)}, u32[]{:S(2)}) collective-permute-start(f32[16,256]{1,0:T(8,128)S(1)} %get-tuple-element.51), channel_id=1, source_target_pairs={{0,4},{4,0},{8,12},{12,8},{16,20},{20,16},{24,28},{28,24},{1,5},{5... | collective-permute-start | bytes 49160 | tf_op jit(solution)/shard_map/ppermute | solution.py:426
  29.3 8.5 %collective-permute-start.10 = (f32[4,32,512]{2,1,0:T(8,128)S(1)}, f32[4,32,512]{2,1,0:T(8,128)S(1)}, u32[]{:S(2)}, u32[]{:S(2)}) collective-permute-start(f32[4,32,512]{2,1,0:T(8,128)S(1)} %pad_maximum_fusion.refs_2_.t_same), channel_id=1, source_target_pairs={{0,4},{4,0},{8,12},{12,8},{16,20},{20,16},{24,28},{28,24},{1,5},{5... | collective-permute-start | bytes 786440 | tf_op jit(solution)/shard_map/ppermute | solution.py:426
  33.0 4.7 %collective-permute-start.14 = (f32[16,256]{1,0:T(8,128)S(1)}, f32[16,256]{1,0:T(8,128)S(1)}, u32[]{:S(2)}, u32[]{:S(2)}) collective-permute-start(f32[16,256]{1,0:T(8,128)S(1)} %add_add_fusion), channel_id=1, source_target_pairs={{0,16},{4,20},{8,24},{12,28},{16,0},{20,4},{24,8},{28,12},{1,17},{... | collective-permute-start | bytes 49160 | tf_op jit(solution)/shard_map/ppermute | solution.py:426
  40.6 1.4 %collective-permute-start.15 = (f32[2,32,512]{2,1,0:T(8,128)S(1)}, f32[2,32,512]{2,1,0:T(8,128)S(1)}, u32[]{:S(2)}, u32[]{:S(2)}) collective-permute-start(f32[2,32,512]{2,1,0:T(8,128)S(1)} %get-tuple-element.53), channel_id=1, source_target_pairs={{0,1},{1,0},{2,3},{3,2},{4,5},{5,4},{6,7},{7,6},{8,9},{9,8},{10,11... | collective-permute-start | bytes 393224 | tf_op jit(solution)/shard_map/ppermute | solution.py:426
  42.0 6.0 %collective-permute-start.16 = (f32[72,512]{1,0:T(8,128)S(1)}, f32[72,512]{1,0:T(8,128)S(1)}, u32[]{:S(2)}, u32[]{:S(2)}) collective-permute-start(f32[72,512]{1,0:T(8,128)S(1)} %pad_maximum_fusion.3), channel_id=1, source_target_pairs={{0,2},{1,3},{2,0},{3,1},{4,6},{5,7},{6,4},{7,5},{8,10},{9,11},{10,... | collective-permute-start | bytes 442376 | tf_op jit(solution)/shard_map/ppermute | solution.py:426
  48.1 1.5 %collective-permute-start.17 = (f32[2,40,512]{2,1,0:T(8,128)S(1)}, f32[2,40,512]{2,1,0:T(8,128)S(1)}, u32[]{:S(2)}, u32[]{:S(2)}) collective-permute-start(f32[2,40,512]{2,1,0:T(8,128)S(1)} %pad_maximum_fusion.1.s1_own), channel_id=1, source_target_pairs={{0,1},{1,0},{2,3},{3,2},{4,5},{5,4},{6,7},{7,6},{8,9},{9,8},{10,11... | collective-permute-start | bytes 491528 | tf_op jit(solution)/shard_map/ppermute | solution.py:426
  48.2 4.0 %collective-permute-start.19 = (bf16[32,512]{1,0:T(8,128)(2,1)S(1)}, bf16[32,512]{1,0:T(8,128)(2,1)S(1)}, u32[]{:S(2)}, u32[]{:S(2)}) collective-permute-start(bf16[32,512]{1,0:T(8,128)(2,1)S(1)} %fusion.2), channel_id=1, source_target_pairs={{0,8},{4,12},{8,0},{12,4},{16,24},{20,28},{24,16},{28,20},{1,9},{5... | collective-permute-start | bytes 98312 | tf_op jit(solution)/shard_map/ppermute | solution.py:426
  50.9 7.5 %collective-permute-start.18 = (bf16[4,32,512]{2,1,0:T(8,128)(2,1)S(1)}, bf16[4,32,512]{2,1,0:T(8,128)(2,1)S(1)}, u32[]{:S(2)}, u32[]{:S(2)}) collective-permute-start(bf16[4,32,512]{2,1,0:T(8,128)(2,1)S(1)} %second.3), channel_id=1, source_target_pairs={{0,4},{4,0},{8,12},{12,8},{16,20},{20,16},{24,28},{28,24},{1,5},{5... | collective-permute-start | bytes 393224 | tf_op jit(solution)/shard_map/ppermute | solution.py:426
  52.2 6.2 %collective-permute-start.20 = (bf16[2,32,512]{2,1,0:T(8,128)(2,1)S(1)}, bf16[2,32,512]{2,1,0:T(8,128)(2,1)S(1)}, u32[]{:S(2)}, u32[]{:S(2)}) collective-permute-start(bf16[2,32,512]{2,1,0:T(8,128)(2,1)S(1)} %pad_maximum_fusion.5.refs_0_), channel_id=1, source_target_pairs={{0,16},{4,20},{8,24},{12,28},{16,0},{20,4},{24,8},{28,12},{1,17},{... | collective-permute-start | bytes 196616 | tf_op jit(solution)/shard_map/ppermute | solution.py:426
  58.6 5.9 %collective-permute-start.21 = (bf16[32,640]{1,0:T(8,128)(2,1)S(1)}, bf16[32,640]{1,0:T(8,128)(2,1)S(1)}, u32[]{:S(2)}, u32[]{:S(2)}) collective-permute-start(bf16[32,640]{1,0:T(8,128)(2,1)S(1)} %get-tuple-element.63), channel_id=1, source_target_pairs={{0,24},{4,28},{8,16},{12,20},{16,8},{20,12},{24,0},{28,4},{1,25},{... | collective-permute-start | bytes 122888 | tf_op jit(solution)/shard_map/ppermute | solution.py:426
  61.4 4.9 %collective-permute-start.22 = (bf16[32,640]{1,0:T(8,128)(2,1)S(1)}, bf16[32,640]{1,0:T(8,128)(2,1)S(1)}, u32[]{:S(2)}, u32[]{:S(2)}) collective-permute-start(bf16[32,640]{1,0:T(8,128)(2,1)S(1)} %get-tuple-element.64), channel_id=1, source_target_pairs={{0,16},{4,20},{8,24},{12,28},{16,0},{20,4},{24,8},{28,12},{1,17},{... | collective-permute-start | bytes 122888 | tf_op jit(solution)/shard_map/ppermute | solution.py:426
  61.4 4.9 %collective-permute-start.23 = (bf16[32,640]{1,0:T(8,128)(2,1)S(1)}, bf16[32,640]{1,0:T(8,128)(2,1)S(1)}, u32[]{:S(2)}, u32[]{:S(2)}) collective-permute-start(bf16[32,640]{1,0:T(8,128)(2,1)S(1)} %get-tuple-element.65), channel_id=1, source_target_pairs={{0,8},{4,12},{8,0},{12,4},{16,24},{20,28},{24,16},{28,20},{1,9},{5... | collective-permute-start | bytes 122888 | tf_op jit(solution)/shard_map/ppermute | solution.py:426
  66.4 6.4 %collective-permute-start.25 = (f32[32,640]{1,0:T(8,128)S(1)}, f32[32,640]{1,0:T(8,128)S(1)}, u32[]{:S(2)}, u32[]{:S(2)}) collective-permute-start(f32[32,640]{1,0:T(8,128)S(1)} %get-tuple-element.66), channel_id=1, source_target_pairs={{0,2},{1,3},{2,0},{3,1},{4,6},{5,7},{6,4},{7,5},{8,10},{9,11},{10,... | collective-permute-start | bytes 245768 | tf_op jit(solution)/shard_map/ppermute | solution.py:426
  68.1 4.6 %collective-permute-start.26 = (f32[32,128]{1,0:T(8,128)S(1)}, f32[32,128]{1,0:T(8,128)S(1)}, u32[]{:S(2)}, u32[]{:S(2)}) collective-permute-start(f32[32,128]{1,0:T(8,128)S(1)} %get-tuple-element.67), channel_id=1, source_target_pairs={{0,6},{1,7},{2,4},{3,5},{4,2},{5,3},{6,0},{7,1},{8,14},{9,15},{10,... | collective-permute-start | bytes 49160 | tf_op jit(solution)/shard_map/ppermute | solution.py:436
  68.5 4.2 %collective-permute-start.24 = (f32[32,128]{1,0:T(8,128)S(1)}, f32[32,128]{1,0:T(8,128)S(1)}, u32[]{:S(2)}, u32[]{:S(2)}) collective-permute-start(f32[32,128]{1,0:T(8,128)S(1)} %get-tuple-element.67), channel_id=1, source_target_pairs={{0,4},{4,0},{8,12},{12,8},{16,20},{20,16},{24,28},{28,24},{1,5},{5... | collective-permute-start | bytes 49160 | tf_op jit(solution)/shard_map/ppermute | solution.py:426
  72.8 1.5 %collective-permute-start.27 = (f32[2,32,640]{2,1,0:T(8,128)S(1)}, f32[2,32,640]{2,1,0:T(8,128)S(1)}, u32[]{:S(2)}, u32[]{:S(2)}) collective-permute-start(f32[2,32,640]{2,1,0:T(8,128)S(1)} %pad_maximum_fusion.2.refs_0_), channel_id=1, source_target_pairs={{0,1},{1,0},{2,3},{3,2},{4,5},{5,4},{6,7},{7,6},{8,9},{9,8},{10,11... | collective-permute-start | bytes 491528 | tf_op jit(solution)/shard_map/ppermute | solution.py:426

commit v17 on v16

--- a/solution.py
+++ b/solution.py
@@ -298,6 +298,43 @@
         own_inv[:, cols] = jnp.broadcast_to(mine, (8, block_len))
         for e, ref in enumerate((near, cross.at[0], near_y, cross.at[1])):
             ref[:, cols] = z_acc[(col ^ e) * own_rows + k]
+
+
+def terms_of(v, n):
+    out = []
+    for _ in range(n):
+        out.append(v.astype(BF16))
+        v = v - out[-1].astype(F32)
+    return out
+
+
+def part_kernel(near, near_y, got, tail, send, lo_ref, hi_ref):
+    outputs = near.shape[0]
+    hi = (near_y[...] + got[1]).astype(BF16)
+    lo = terms_of(near[...] + got[0], 2)
+    for n, v in enumerate((hi, *lo)):
+        send[n * outputs:(n + 1) * outputs, :] = v
+    hi_ref[...] = hi.astype(F32)
+    lo_ref[...] = lo[0].astype(F32) + lo[1].astype(F32)
+    line = lax.broadcasted_iota(jnp.int32, (16, tail.shape[1]), 0)
+    rows = jnp.zeros(line.shape, F32)
+    for n, v in enumerate(terms_of(tail[0:1, :], 3)):
+        rows = jnp.where(line == n, v.astype(F32), rows)
+    send[3 * outputs:, :] = rows.astype(BF16)
+
+
+def join_kernel(lo_ref, hi_ref, tail, far, t_ref, s1_ref, g_ref):
+    outputs = lo_ref.shape[0]
+    far_hi, far_a, far_b = (far[n * outputs:(n + 1) * outputs, :].astype(F32) for n in range(3))
+    rows = far[3 * outputs:, :].astype(F32)
+    far_inv = (rows[0:1] + rows[1:2]) + rows[2:3]
+    inv = tail[0:1, :]
+    s1 = (lo_ref[...] + far_hi) * inv
+    s1_ref[0, :outputs, :] = s1
+    s1_ref[0, outputs:, :] = tail[...]
+    s1_ref[1, :outputs, :] = ((far_a + far_b) + hi_ref[...]) * far_inv
+    s1_ref[1, outputs:, :] = jnp.broadcast_to(far_inv, tail.shape)
+    g_ref[...] = ((s1 - SHIFT * t_ref[...]) * inv).astype(BF16)
 
 
 def second_kernel(cfg, part, k_mat, list_v, t_ref, s1_own, s1_got, out, z_acc, w_all, listed, list_sem, *ring):
@@ -583,13 +620,22 @@
     )(k_mat, *k_lists, *t_pieces, inv)
 
     got = swap(cross_z, "cols", 1)
-    half = jnp.concatenate([near_z + got[0], near_y + got[1], tail], axis=0)
-    far = swap(half, "cols", 2)
-    lo, hi, end = slice(0, outputs), slice(outputs, 2 * outputs), slice(2 * outputs, None)
-    s1_own = jnp.stack([
-        jnp.concatenate([(half[lo] + far[hi]) * tail[:1], tail], axis=0),
-        jnp.concatenate([(half[hi] + far[lo]) * far[end][:1], far[end]], axis=0),
-    ])
+    send, lo, hi = pl.pallas_call(
+        part_kernel,
+        out_shape=[shape(3 * outputs + 16, own_len, dtype=BF16)] + [shape(outputs, own_len)] * 2,
+        in_specs=[VMEM] * 4,
+        out_specs=[VMEM] * 3,
+        compiler_params=limit,
+        name="part",
+    )(near_z, near_y, got, tail)
+    s1_own, g = pl.pallas_call(
+        join_kernel,
+        out_shape=(shape(2, outputs + 8, own_len), shape(outputs, own_len, dtype=BF16)),
+        in_specs=[VMEM] * 5,
+        out_specs=(VMEM, VMEM),
+        compiler_params=limit,
+        name="join",
+    )(lo, hi, tail, swap(send, "cols", 2), own_t)
     s1_got = swap(s1_own, "cols", 1)
     held_t = pltpu.with_memory_space_constraint(targets, pltpu.VMEM)
 
@@ -612,7 +658,6 @@
         )(k_mat, k_lists[part], held_t, s1_own, s1_got)
 
     if direct_rows:
-        g = ((s1_own[0, :outputs] - SHIFT * own_t) * tail[:1]).astype(BF16)
         parts_of_g = (g, swap(g, "rows", 2))
         z2_other = second(1, BF16)
         _, *parts_of_g = lax.optimization_barrier((z2_other, *parts_of_g))
@@ -647,7 +692,7 @@
         z2 = lax.psum_scatter(second(0, F32), "rows", scatter_dimension=0)
         grown = z2 * tail[:1]
         own_s1 = s1_own[0, :outputs]
-        own_t, s2 = own(targets), grown + SHIFT * own_s1
+        s2 = grown + SHIFT * own_s1
         dots = [(own_t, own_t), (own_t, own_s1), (own_s1, own_s1), (own_t, s2), (own_s1, s2)]
         dots = jnp.stack([jnp.sum(x * y, axis=1) for x, y in dots], axis=1)
         dots = lax.psum(jnp.pad(dots, ((0, 0), (0, LANES - N_DOTS))), "rows")

time: 75.9 us -> 75.9 us (level)
  Pallas kernels: 14.2 us -> 16.3 us
  waiting for transfers between devices: 23.2 us -> 21.8 us
    ppermute x27, waiting for transfers between devices: 20.4 us -> 18.7 us  [swap(): return lax.ppermute(x, axis, [(i, i ^ d) for i in range(size)])]
    pallas_call x2, Pallas kernels: 7.18 us -> 8.23 us  [build(): pl.pallas_call(functools.partial(build_kernel, cfg, part), out_shape=out,...]
  transfers between devices with their start and end apart: 28 -> 28, of which waited for: 11 -> 12; matrix products, arithmetic and copies ran while one was open for 4% -> 4% of each run, Pallas kernels for 9% -> 10%
where the time goes in v17:
time: 75.9 us; the launch traced here: 75.6 us
  starting transfers between devices  33.5 us (44%)
  waiting for transfers between devices  21.8 us (29%)
  Pallas kernels  16.3 us (21%)
  local copies, waits for them, and re-layouts  2.74 us (4%)
  between operations  0.84 us (1%)
    ppermute x27, starting transfers between devices, swap(): return lax.ppermute(x, axis, [(i, i ^ d) for i in range(size)])  33.1 us
    ppermute x27, waiting for transfers between devices, swap(): return lax.ppermute(x, axis, [(i, i ^ d) for i in range(size)])  18.7 us
    pallas_call x2, Pallas kernels, build(): pl.pallas_call(functools.partial(build_kernel, cfg, part), out_shape=out,...  8.23 us
    pallas_call x1, Pallas kernels, local(): pl.pallas_call(functools.partial(first_kernel, cfg), out_shape=[shape(out...  3.32 us
    pallas_call x2, Pallas kernels, second(): pl.pallas_call(functools.partial(second_kernel, cfg, part), out_shape=sha...  3.21 us
    ppermute x1, waiting for transfers between devices, both_swap(): return lax.ppermute(x, ('rows', 'cols'), pairs)  3.09 us
    dynamic_slice x2, local copies, waits for them, and re-layouts, own(): return lax.dynamic_slice_in_dim(x, col * own_len, own_len, 1)  1.56 us
  transfers between devices with their start and end apart: 28, of which 12 were waited for; matrix products, arithmetic and copies ran while one was open for 4% of the time, Pallas kernels for 10%

profile of v17, /device:TPU:0, one launch (start us, length us, event | category | flops | bytes accessed | tf_op | source)
XLA Modules:
  0.0 75.6 jit_solution(12169853067419401098)
XLA Ops:
  0.6 0.5 collective-permute-start
  1.1 2.6 %collective-permute-start.2 = (s32[8,6]{1,0:T(8,128)}, s32[8,6]{1,0:T(8,128)S(1)}, u32[]{:S(2)}, u32[]{:S(2)}) collective-permute-start(s32[8,6]{1,0:T(8,128)} %param.3), channel_id=1, source_target_pairs={{0,3},{1,2},{2,1},{3,0},{4,7},{5,6},{6,5},{7,4},{8,11},{9,10},{10,... | collective-permute-start | bytes 584 | tf_op jit(solution)/shard_map/ppermute | solution.py:463
  3.8 0.8 %copy.6 = s32[8,6]{0,1:T(8,128)S(1)} copy(s32[8,6]{1,0:T(8,128)} %param.3) | data formatting | bytes 384 | tf_op args[0]
  4.7 0.7 constant_dynamic-slice_fusion.1
  5.5 0.8 %constant_dynamic-slice_fusion.t_ref = f32[32,512]{1,0:T(8,128)S(1)} fusion(f32[32,2048]{1,0:T(8,128)} %t_ref.5, s32[]{:T(128)S(6)} %select_n.7), kind=kLoop, calls=%fused_computation.21 | loop fusion | bytes 131076 | tf_op jit(solution)/shard_map/dynamic_slice | solution.py:524
  6.3 0.1 copy.7
  6.5 0.1 copy.9
  6.6 1.0 %collective-permute-done.1 = s32[8,6]{1,0:T(8,128)S(1)} collective-permute-done((s32[8,6]{1,0:T(8,128)}, s32[8,6]{1,0:T(8,128)S(1)}, u32[]{:S(2)}, u32[]{:S(2)}) %collective-permute-start.1) | collective-permute-done | bytes 224 | tf_op jit(solution)/shard_map/ppermute | solution.py:463
  7.6 0.1 copy.8
  7.8 0.1 reshape.14
  7.9 3.7 %collective-permute-start.5 = (bf16[16,640]{1,0:T(8,128)(2,1)S(1)}, bf16[16,640]{1,0:T(8,128)(2,1)S(1)}, u32[]{:S(2)}, u32[]{:S(2)}) collective-permute-start(bf16[16,640]{1,0:T(8,128)(2,1)S(1)} %pad_maximum_fusion.4), channel_id=1, source_target_pairs={{0,24},{4,28},{8,16},{12,20},{16,8},{20,12},{24,0},{28,4},{1,25},{... | collective-permute-start | bytes 61448 | tf_op jit(solution)/shard_map/ppermute | solution.py:463
  11.6 0.8 %collective-permute-start.3 = (bf16[16,640]{1,0:T(8,128)(2,1)S(1)}, bf16[16,640]{1,0:T(8,128)(2,1)S(1)}, u32[]{:S(2)}, u32[]{:S(2)}) collective-permute-start(bf16[16,640]{1,0:T(8,128)(2,1)S(1)} %pad_maximum_fusion.4), channel_id=1, source_target_pairs={{0,8},{4,12},{8,0},{12,4},{16,24},{20,28},{24,16},{28,20},{1,9},{5... | collective-permute-start | bytes 61448 | tf_op jit(solution)/shard_map/ppermute | solution.py:463
  12.3 3.6 %collective-permute-start.9 = (f32[32,512]{1,0:T(8,128)S(1)}, f32[32,512]{1,0:T(8,128)S(1)}, u32[]{:S(2)}, u32[]{:S(2)}) collective-permute-start(f32[32,512]{1,0:T(8,128)S(1)} %constant_dynamic-slice_fusion.t_ref), channel_id=1, source_target_pairs={{0,24},{4,28},{8,16},{12,20},{16,8},{20,12},{24,0},{28,4},{1,25},{... | collective-permute-start | bytes 196616 | tf_op jit(solution)/shard_map/ppermute | solution.py:463
  15.9 0.8 %collective-permute-start.7 = (f32[32,512]{1,0:T(8,128)S(1)}, f32[32,512]{1,0:T(8,128)S(1)}, u32[]{:S(2)}, u32[]{:S(2)}) collective-permute-start(f32[32,512]{1,0:T(8,128)S(1)} %constant_dynamic-slice_fusion.t_ref), channel_id=1, source_target_pairs={{0,8},{4,12},{8,0},{12,4},{16,24},{20,28},{24,16},{28,20},{1,9},{5... | collective-permute-start | bytes 196616 | tf_op jit(solution)/shard_map/ppermute | solution.py:463
  16.8 1.6 %collective-permute-start.6 = (bf16[4,16,640]{2,1,0:T(8,128)(2,1)S(1)}, bf16[4,16,640]{2,1,0:T(8,128)(2,1)S(1)}, u32[]{:S(2)}, u32[]{:S(2)}) collective-permute-start(bf16[4,16,640]{2,1,0:T(8,128)(2,1)S(1)} %pad_maximum_fusion.2.refs_1_), channel_id=1, source_target_pairs={{0,4},{4,0},{8,12},{12,8},{16,20},{20,16},{24,28},{28,24},{1,5},{5... | collective-permute-start | bytes 245768 | tf_op jit(solution)/shard_map/ppermute | solution.py:463
  18.3 4.4 %build.2 = (bf16[32,4,256,256]{3,2,1,0:T(8,128)(2,1)S(1)}, s32[1,128]{1,0:T(1,128)S(1)}, f32[8,256]{1,0:T(8,128)S(1)}, bf16[8,256,32]{2,1,0:T(8,128)(2,1)S(1)}) custom-call(s32[8,64]{1,0:T(8,128)S(1)} %add_add_fusion.1.direct_v, bf16[16,2048]{1,0:T(8,128)(2,1)} %refs_0_.1, bf16[4,16,640]{2,1,0:T(8,128)(2,1)S(1)} %pad_maximum_fusion.2.refs_1_), custom_call_target="tpu_custom_call" | custom-call | flops 2684354560 | bytes 83886080 | tf_op jit(solution)/shard_map/build/pallas_call | solution.py:549
  22.8 3.9 %build.3 = (bf16[32,4,256,256]{3,2,1,0:T(8,128)(2,1)S(1)}, s32[1,128]{1,0:T(1,128)S(1)}, f32[16,256]{1,0:T(8,128)S(1)}) custom-call(s32[8,64]{1,0:T(8,128)S(1)} %add_add_fusion.1.direct_v, bf16[8,256,32]{2,1,0:T(8,128)(2,1)S(1)} %get-tuple-element.41.refs_0_, f32[8,256]{1,0:T(8,128)S(1)} %get-tuple-element.44.refs_1_, ...), custom_call_target="tpu_custom_call", output_to_operand_aliasing={{0}: (4, {})} | custom-call | flops 2684354560 | bytes 83886080 | tf_op jit(solution)/shard_map/build/pallas_call | solution.py:549
  26.6 1.8 %collective-permute-start.13 = (f32[16,256]{1,0:T(8,128)S(1)}, f32[16,256]{1,0:T(8,128)S(1)}, u32[]{:S(2)}, u32[]{:S(2)}) collective-permute-start(f32[16,256]{1,0:T(8,128)S(1)} %get-tuple-element.56), channel_id=1, source_target_pairs={{0,12},{4,8},{8,4},{12,0},{16,28},{20,24},{24,20},{28,16},{1,13},{... | collective-permute-start | bytes 49160 | tf_op jit(solution)/shard_map/ppermute | solution.py:463
  28.5 0.2 collective-permute-start.12
  28.7 1.5 %collective-permute-start.11 = (f32[16,256]{1,0:T(8,128)S(1)}, f32[16,256]{1,0:T(8,128)S(1)}, u32[]{:S(2)}, u32[]{:S(2)}) collective-permute-start(f32[16,256]{1,0:T(8,128)S(1)} %get-tuple-element.56), channel_id=1, source_target_pairs={{0,4},{4,0},{8,12},{12,8},{16,20},{20,16},{24,28},{28,24},{1,5},{5... | collective-permute-start | bytes 49160 | tf_op jit(solution)/shard_map/ppermute | solution.py:463
  30.2 0.5 collective-permute-start.10
  30.7 0.7 collective-permute-done.13
  31.5 0.7 collective-permute-done.12
  32.2 0.5 collective-permute-done.11
  32.7 2.2 %collective-permute-start.14 = (f32[16,256]{1,0:T(8,128)S(1)}, f32[16,256]{1,0:T(8,128)S(1)}, u32[]{:S(2)}, u32[]{:S(2)}) collective-permute-start(f32[16,256]{1,0:T(8,128)S(1)} %add_add_fusion), channel_id=1, source_target_pairs={{0,16},{4,20},{8,24},{12,28},{16,0},{20,4},{24,8},{28,12},{1,17},{... | collective-permute-start | bytes 49160 | tf_op jit(solution)/shard_map/ppermute | solution.py:463
  34.9 2.5 %collective-permute-done.14 = f32[16,256]{1,0:T(8,128)S(1)} collective-permute-done((f32[16,256]{1,0:T(8,128)S(1)}, f32[16,256]{1,0:T(8,128)S(1)}, u32[]{:S(2)}, u32[]{:S(2)}) %collective-permute-start.14) | collective-permute-done | bytes 16416 | tf_op jit(solution)/shard_map/ppermute | solution.py:463
  37.4 3.3 %first.1 = (f32[32,512]{1,0:T(8,128)S(1)}, f32[32,512]{1,0:T(8,128)S(1)}, f32[2,32,512]{2,1,0:T(8,128)S(1)}, f32[8,512]{1,0:T(8,128)S(1)}) custom-call(bf16[32,4,256,256]{3,2,1,0:T(8,128)(2,1)S(1)} %get-tuple-element.52.k_mat, s32[1,128]{1,0:T(1,128)S(1)} %get-tuple-element.53.refs_0_.list_v, s32[1,128]{1,0:T(1,128)S(1)} %get-tuple-element.54.refs_1_.list_v, ...), custom_call_target="tpu_custom_call" | custom-call | flops 536870912 | bytes 8388608 | tf_op jit(solution)/shard_map/first/pallas_call | solution.py:605
  40.8 1.3 %collective-permute-done.15.got = f32[2,32,512]{2,1,0:T(8,128)S(1)} collective-permute-done((f32[2,32,512]{2,1,0:T(8,128)S(1)}, f32[2,32,512]{2,1,0:T(8,128)S(1)}, u32[]{:S(2)}, u32[]{:S(2)}) %collective-permute-start.15) | collective-permute-done | bytes 131104 | tf_op jit(solution)/shard_map/ppermute | solution.py:463
  42.2 0.6 collective-permute-start.16
  42.8 4.7 %collective-permute-done.16.far = bf16[112,512]{1,0:T(8,128)(2,1)S(1)} collective-permute-done((bf16[112,512]{1,0:T(8,128)(2,1)S(1)}, bf16[112,512]{1,0:T(8,128)(2,1)S(1)}, u32[]{:S(2)}, u32[]{:S(2)}) %collective-permute-start.16) | collective-permute-done | bytes 114720 | tf_op jit(solution)/shard_map/ppermute | solution.py:463
  47.6 1.6 %collective-permute-start.19 = (bf16[32,512]{1,0:T(8,128)(2,1)S(1)}, bf16[32,512]{1,0:T(8,128)(2,1)S(1)}, u32[]{:S(2)}, u32[]{:S(2)}) collective-permute-start(bf16[32,512]{1,0:T(8,128)(2,1)S(1)} %get-tuple-element.66), channel_id=1, source_target_pairs={{0,8},{4,12},{8,0},{12,4},{16,24},{20,28},{24,16},{28,20},{1,9},{5... | collective-permute-start | bytes 98312 | tf_op jit(solution)/shard_map/ppermute | solution.py:463
  49.2 1.6 %second.3 = bf16[4,32,512]{2,1,0:T(8,128)(2,1)S(1)} custom-call(bf16[32,4,256,256]{3,2,1,0:T(8,128)(2,1)S(1)} %get-tuple-element.52.k_mat, s32[1,128]{1,0:T(1,128)S(1)} %get-tuple-element.54.refs_1_.list_v, f32[32,2048]{1,0:T(8,128)S(1)} %copy-done, f32[2,40,512]{2,1,0:T(8,128)S(1)} %get-tuple-element.64.s1_own, f32[2,40,512]{2,1,0:T(8,128)S(1)} %collective-permute-done.17.s1_got), custom_call_target="tpu_custom_call" | custom-call | flops 268435456 | bytes 4194304 | tf_op jit(solution)/shard_map/second/pallas_call | solution.py:643
  50.8 1.4 %collective-permute-start.18 = (bf16[4,32,512]{2,1,0:T(8,128)(2,1)S(1)}, bf16[4,32,512]{2,1,0:T(8,128)(2,1)S(1)}, u32[]{:S(2)}, u32[]{:S(2)}) collective-permute-start(bf16[4,32,512]{2,1,0:T(8,128)(2,1)S(1)} %second.3), channel_id=1, source_target_pairs={{0,4},{4,0},{8,12},{12,8},{16,20},{20,16},{24,28},{28,24},{1,5},{5... | collective-permute-start | bytes 393224 | tf_op jit(solution)/shard_map/ppermute | solution.py:463
  52.2 2.0 %collective-permute-start.20 = (bf16[2,32,512]{2,1,0:T(8,128)(2,1)S(1)}, bf16[2,32,512]{2,1,0:T(8,128)(2,1)S(1)}, u32[]{:S(2)}, u32[]{:S(2)}) collective-permute-start(bf16[2,32,512]{2,1,0:T(8,128)(2,1)S(1)} %pad_maximum_fusion.3.refs_0_), channel_id=1, source_target_pairs={{0,16},{4,20},{8,24},{12,28},{16,0},{20,4},{24,8},{28,12},{1,17},{... | collective-permute-start | bytes 196616 | tf_op jit(solution)/shard_map/ppermute | solution.py:463
  54.1 1.6 %second.2.z_same = f32[4,32,512]{2,1,0:T(8,128)S(1)} custom-call(bf16[32,4,256,256]{3,2,1,0:T(8,128)(2,1)S(1)} %get-tuple-element.52.k_mat, s32[1,128]{1,0:T(1,128)S(1)} %get-tuple-element.53.refs_0_.list_v, f32[32,2048]{1,0:T(8,128)S(1)} %copy-done, f32[2,40,512]{2,1,0:T(8,128)S(1)} %get-tuple-element.64.s1_own, ...), custom_call_target="tpu_custom_call" | custom-call | flops 268435456 | bytes 4194304 | tf_op jit(solution)/shard_map/second/pallas_call | solution.py:643
  55.8 2.9 %collective-permute-done.20.refs_1_ = bf16[2,32,512]{2,1,0:T(8,128)(2,1)S(1)} collective-permute-done((bf16[2,32,512]{2,1,0:T(8,128)(2,1)S(1)}, bf16[2,32,512]{2,1,0:T(8,128)(2,1)S(1)}, u32[]{:S(2)}, u32[]{:S(2)}) %collective-permute-start.20) | collective-permute-done | bytes 65568 | tf_op jit(solution)/shard_map/ppermute | solution.py:463
  58.6 0.2 meet.1
  58.8 2.5 %collective-permute-start.21 = (bf16[32,640]{1,0:T(8,128)(2,1)S(1)}, bf16[32,640]{1,0:T(8,128)(2,1)S(1)}, u32[]{:S(2)}, u32[]{:S(2)}) collective-permute-start(bf16[32,640]{1,0:T(8,128)(2,1)S(1)} %get-tuple-element.73), channel_id=1, source_target_pairs={{0,24},{4,28},{8,16},{12,20},{16,8},{20,12},{24,0},{28,4},{1,25},{... | collective-permute-start | bytes 122888 | tf_op jit(solution)/shard_map/ppermute | solution.py:463
  61.3 2.0 %collective-permute-start.23 = (bf16[32,640]{1,0:T(8,128)(2,1)S(1)}, bf16[32,640]{1,0:T(8,128)(2,1)S(1)}, u32[]{:S(2)}, u32[]{:S(2)}) collective-permute-start(bf16[32,640]{1,0:T(8,128)(2,1)S(1)} %get-tuple-element.75), channel_id=1, source_target_pairs={{0,8},{4,12},{8,0},{12,4},{16,24},{20,28},{24,16},{28,20},{1,9},{5... | collective-permute-start | bytes 122888 | tf_op jit(solution)/shard_map/ppermute | solution.py:463
  63.3 1.4 %collective-permute-done.21.refs_0_ = bf16[32,640]{1,0:T(8,128)(2,1)S(1)} collective-permute-done((bf16[32,640]{1,0:T(8,128)(2,1)S(1)}, bf16[32,640]{1,0:T(8,128)(2,1)S(1)}, u32[]{:S(2)}, u32[]{:S(2)}) %collective-permute-start.21) | collective-permute-done | bytes 40992 | tf_op jit(solution)/shard_map/ppermute | solution.py:463
  64.7 1.5 %collective-permute-done.22.refs_1_ = bf16[32,640]{1,0:T(8,128)(2,1)S(1)} collective-permute-done((bf16[32,640]{1,0:T(8,128)(2,1)S(1)}, bf16[32,640]{1,0:T(8,128)(2,1)S(1)}, u32[]{:S(2)}, u32[]{:S(2)}) %collective-permute-start.22) | collective-permute-done | bytes 40992 | tf_op jit(solution)/shard_map/ppermute | solution.py:463
  66.2 0.1 products.1
  66.3 2.0 %collective-permute-start.25 = (f32[32,640]{1,0:T(8,128)S(1)}, f32[32,640]{1,0:T(8,128)S(1)}, u32[]{:S(2)}, u32[]{:S(2)}) collective-permute-start(f32[32,640]{1,0:T(8,128)S(1)} %get-tuple-element.76), channel_id=1, source_target_pairs={{0,2},{1,3},{2,0},{3,1},{4,6},{5,7},{6,4},{7,5},{8,10},{9,11},{10,... | collective-permute-start | bytes 245768 | tf_op jit(solution)/shard_map/ppermute | solution.py:463
  68.3 0.5 collective-permute-start.26
  68.7 1.1 %collective-permute-start.24 = (f32[32,128]{1,0:T(8,128)S(1)}, f32[32,128]{1,0:T(8,128)S(1)}, u32[]{:S(2)}, u32[]{:S(2)}) collective-permute-start(f32[32,128]{1,0:T(8,128)S(1)} %get-tuple-element.77), channel_id=1, source_target_pairs={{0,4},{4,0},{8,12},{12,8},{16,20},{20,16},{24,28},{28,24},{1,5},{5... | collective-permute-start | bytes 49160 | tf_op jit(solution)/shard_map/ppermute | solution.py:463
  69.8 3.1 %collective-permute-done.26 = f32[32,128]{1,0:T(8,128)S(1)} collective-permute-done((f32[32,128]{1,0:T(8,128)S(1)}, f32[32,128]{1,0:T(8,128)S(1)}, u32[]{:S(2)}, u32[]{:S(2)}) %collective-permute-start.26) | collective-permute-done | bytes 16416 | tf_op jit(solution)/shard_map/ppermute | solution.py:473
  73.0 1.4 %collective-permute-done.27.refs_1_ = f32[2,32,640]{2,1,0:T(8,128)S(1)} collective-permute-done((f32[2,32,640]{2,1,0:T(8,128)S(1)}, f32[2,32,640]{2,1,0:T(8,128)S(1)}, u32[]{:S(2)}, u32[]{:S(2)}) %collective-permute-start.27) | collective-permute-done | bytes 163872 | tf_op jit(solution)/shard_map/ppermute | solution.py:463
  74.4 1.2 %final.1 = (f32[32,2048]{1,0:T(8,128)}, f32[32,2048]{1,0:T(8,128)}) custom-call(f32[32,2048]{1,0:T(8,128)S(1)} %copy-done, f32[2,40,512]{2,1,0:T(8,128)S(1)} %get-tuple-element.64.s1_own, f32[2,40,512]{2,1,0:T(8,128)S(1)} %collective-permute-done.17.s1_got, f32[2,32,640]{2,1,0:T(8,128)S(1)} %pad_maximum_fusion.1.refs_0_, ...), custom_call_target="tpu_custom_call" | custom-call | tf_op jit(solution)/shard_map/final/pallas_call | solution.py:706
  (44 shorter events, 0.8 us)
Async XLA Ops:
  0.6 5.7 %collective-permute-start = (s32[8,6]{1,0:T(8,128)}, s32[8,6]{1,0:T(8,128)S(1)}, u32[]{:S(2)}, u32[]{:S(2)}) collective-permute-start(s32[8,6]{1,0:T(8,128)} %param.3), channel_id=1, source_target_pairs={{0,1},{1,0},{2,3},{3,2},{4,5},{5,4},{6,7},{7,6},{8,9},{9,8},{10,11... | collective-permute-start | bytes 584 | tf_op jit(solution)/shard_map/ppermute | solution.py:463
  1.1 5.3 %collective-permute-start.2 = (s32[8,6]{1,0:T(8,128)}, s32[8,6]{1,0:T(8,128)S(1)}, u32[]{:S(2)}, u32[]{:S(2)}) collective-permute-start(s32[8,6]{1,0:T(8,128)} %param.3), channel_id=1, source_target_pairs={{0,3},{1,2},{2,1},{3,0},{4,7},{5,6},{6,5},{7,4},{8,11},{9,10},{10,... | collective-permute-start | bytes 584 | tf_op jit(solution)/shard_map/ppermute | solution.py:463
  3.8 3.8 %collective-permute-start.1 = (s32[8,6]{1,0:T(8,128)}, s32[8,6]{1,0:T(8,128)S(1)}, u32[]{:S(2)}, u32[]{:S(2)}) collective-permute-start(s32[8,6]{1,0:T(8,128)} %param.3), channel_id=1, source_target_pairs={{0,2},{1,3},{2,0},{3,1},{4,6},{5,7},{6,4},{7,5},{8,10},{9,11},{10,... | collective-permute-start | bytes 584 | tf_op jit(solution)/shard_map/ppermute | solution.py:463
  7.9 8.1 %collective-permute-start.5 = (bf16[16,640]{1,0:T(8,128)(2,1)S(1)}, bf16[16,640]{1,0:T(8,128)(2,1)S(1)}, u32[]{:S(2)}, u32[]{:S(2)}) collective-permute-start(bf16[16,640]{1,0:T(8,128)(2,1)S(1)} %pad_maximum_fusion.4), channel_id=1, source_target_pairs={{0,24},{4,28},{8,16},{12,20},{16,8},{20,12},{24,0},{28,4},{1,25},{... | collective-permute-start | bytes 61448 | tf_op jit(solution)/shard_map/ppermute | solution.py:463
  11.6 5.2 %collective-permute-start.4 = (bf16[16,640]{1,0:T(8,128)(2,1)S(1)}, bf16[16,640]{1,0:T(8,128)(2,1)S(1)}, u32[]{:S(2)}, u32[]{:S(2)}) collective-permute-start(bf16[16,640]{1,0:T(8,128)(2,1)S(1)} %pad_maximum_fusion.4), channel_id=1, source_target_pairs={{0,16},{4,20},{8,24},{12,28},{16,0},{20,4},{24,8},{28,12},{1,17},{... | collective-permute-start | bytes 61448 | tf_op jit(solution)/shard_map/ppermute | solution.py:463
  11.6 5.2 %collective-permute-start.3 = (bf16[16,640]{1,0:T(8,128)(2,1)S(1)}, bf16[16,640]{1,0:T(8,128)(2,1)S(1)}, u32[]{:S(2)}, u32[]{:S(2)}) collective-permute-start(bf16[16,640]{1,0:T(8,128)(2,1)S(1)} %pad_maximum_fusion.4), channel_id=1, source_target_pairs={{0,8},{4,12},{8,0},{12,4},{16,24},{20,28},{24,16},{28,20},{1,9},{5... | collective-permute-start | bytes 61448 | tf_op jit(solution)/shard_map/ppermute | solution.py:463
  12.3 10.3 %collective-permute-start.9 = (f32[32,512]{1,0:T(8,128)S(1)}, f32[32,512]{1,0:T(8,128)S(1)}, u32[]{:S(2)}, u32[]{:S(2)}) collective-permute-start(f32[32,512]{1,0:T(8,128)S(1)} %constant_dynamic-slice_fusion.t_ref), channel_id=1, source_target_pairs={{0,24},{4,28},{8,16},{12,20},{16,8},{20,12},{24,0},{28,4},{1,25},{... | collective-permute-start | bytes 196616 | tf_op jit(solution)/shard_map/ppermute | solution.py:463
  15.9 6.8 %collective-permute-start.8 = (f32[32,512]{1,0:T(8,128)S(1)}, f32[32,512]{1,0:T(8,128)S(1)}, u32[]{:S(2)}, u32[]{:S(2)}) collective-permute-start(f32[32,512]{1,0:T(8,128)S(1)} %constant_dynamic-slice_fusion.t_ref), channel_id=1, source_target_pairs={{0,16},{4,20},{8,24},{12,28},{16,0},{20,4},{24,8},{28,12},{1,17},{... | collective-permute-start | bytes 196616 | tf_op jit(solution)/shard_map/ppermute | solution.py:463
  15.9 6.8 %collective-permute-start.7 = (f32[32,512]{1,0:T(8,128)S(1)}, f32[32,512]{1,0:T(8,128)S(1)}, u32[]{:S(2)}, u32[]{:S(2)}) collective-permute-start(f32[32,512]{1,0:T(8,128)S(1)} %constant_dynamic-slice_fusion.t_ref), channel_id=1, source_target_pairs={{0,8},{4,12},{8,0},{12,4},{16,24},{20,28},{24,16},{28,20},{1,9},{5... | collective-permute-start | bytes 196616 | tf_op jit(solution)/shard_map/ppermute | solution.py:463
  16.8 6.0 %collective-permute-start.6 = (bf16[4,16,640]{2,1,0:T(8,128)(2,1)S(1)}, bf16[4,16,640]{2,1,0:T(8,128)(2,1)S(1)}, u32[]{:S(2)}, u32[]{:S(2)}) collective-permute-start(bf16[4,16,640]{2,1,0:T(8,128)(2,1)S(1)} %pad_maximum_fusion.2.refs_1_), channel_id=1, source_target_pairs={{0,4},{4,0},{8,12},{12,8},{16,20},{20,16},{24,28},{28,24},{1,5},{5... | collective-permute-start | bytes 245768 | tf_op jit(solution)/shard_map/ppermute | solution.py:463
  26.6 22.5 %copy-start = (f32[32,2048]{1,0:T(8,128)S(1)}, f32[32,2048]{1,0:T(8,128)}, u32[]{:S(2)}) copy-start(f32[32,2048]{1,0:T(8,128)} %t_ref.5) | copy-start | bytes 786436
  26.6 4.8 %collective-permute-start.13 = (f32[16,256]{1,0:T(8,128)S(1)}, f32[16,256]{1,0:T(8,128)S(1)}, u32[]{:S(2)}, u32[]{:S(2)}) collective-permute-start(f32[16,256]{1,0:T(8,128)S(1)} %get-tuple-element.56), channel_id=1, source_target_pairs={{0,12},{4,8},{8,4},{12,0},{16,28},{20,24},{24,20},{28,16},{1,13},{... | collective-permute-start | bytes 49160 | tf_op jit(solution)/shard_map/ppermute | solution.py:463
  28.5 3.7 %collective-permute-start.12 = (f32[16,256]{1,0:T(8,128)S(1)}, f32[16,256]{1,0:T(8,128)S(1)}, u32[]{:S(2)}, u32[]{:S(2)}) collective-permute-start(f32[16,256]{1,0:T(8,128)S(1)} %get-tuple-element.56), channel_id=1, source_target_pairs={{0,8},{4,12},{8,0},{12,4},{16,24},{20,28},{24,16},{28,20},{1,9},{5... | collective-permute-start | bytes 49160 | tf_op jit(solution)/shard_map/ppermute | solution.py:463
  28.7 4.0 %collective-permute-start.11 = (f32[16,256]{1,0:T(8,128)S(1)}, f32[16,256]{1,0:T(8,128)S(1)}, u32[]{:S(2)}, u32[]{:S(2)}) collective-permute-start(f32[16,256]{1,0:T(8,128)S(1)} %get-tuple-element.56), channel_id=1, source_target_pairs={{0,4},{4,0},{8,12},{12,8},{16,20},{20,16},{24,28},{28,24},{1,5},{5... | collective-permute-start | bytes 49160 | tf_op jit(solution)/shard_map/ppermute | solution.py:463
  30.2 7.2 %collective-permute-start.10 = (f32[4,32,512]{2,1,0:T(8,128)S(1)}, f32[4,32,512]{2,1,0:T(8,128)S(1)}, u32[]{:S(2)}, u32[]{:S(2)}) collective-permute-start(f32[4,32,512]{2,1,0:T(8,128)S(1)} %pad_maximum_fusion.refs_2_.t_same), channel_id=1, source_target_pairs={{0,4},{4,0},{8,12},{12,8},{16,20},{20,16},{24,28},{28,24},{1,5},{5... | collective-permute-start | bytes 786440 | tf_op jit(solution)/shard_map/ppermute | solution.py:463
  32.7 4.7 %collective-permute-start.14 = (f32[16,256]{1,0:T(8,128)S(1)}, f32[16,256]{1,0:T(8,128)S(1)}, u32[]{:S(2)}, u32[]{:S(2)}) collective-permute-start(f32[16,256]{1,0:T(8,128)S(1)} %add_add_fusion), channel_id=1, source_target_pairs={{0,16},{4,20},{8,24},{12,28},{16,0},{20,4},{24,8},{28,12},{1,17},{... | collective-permute-start | bytes 49160 | tf_op jit(solution)/shard_map/ppermute | solution.py:463
  40.7 1.4 %collective-permute-start.15 = (f32[2,32,512]{2,1,0:T(8,128)S(1)}, f32[2,32,512]{2,1,0:T(8,128)S(1)}, u32[]{:S(2)}, u32[]{:S(2)}) collective-permute-start(f32[2,32,512]{2,1,0:T(8,128)S(1)} %get-tuple-element.59), channel_id=1, source_target_pairs={{0,1},{1,0},{2,3},{3,2},{4,5},{5,4},{6,7},{7,6},{8,9},{9,8},{10,11... | collective-permute-start | bytes 393224 | tf_op jit(solution)/shard_map/ppermute | solution.py:463
  42.2 5.3 %collective-permute-start.16 = (bf16[112,512]{1,0:T(8,128)(2,1)S(1)}, bf16[112,512]{1,0:T(8,128)(2,1)S(1)}, u32[]{:S(2)}, u32[]{:S(2)}) collective-permute-start(bf16[112,512]{1,0:T(8,128)(2,1)S(1)} %get-tuple-element.63), channel_id=1, source_target_pairs={{0,2},{1,3},{2,0},{3,1},{4,6},{5,7},{6,4},{7,5},{8,10},{9,11},{10,... | collective-permute-start | bytes 344072 | tf_op jit(solution)/shard_map/ppermute | solution.py:463
  47.5 1.7 %collective-permute-start.17 = (f32[2,40,512]{2,1,0:T(8,128)S(1)}, f32[2,40,512]{2,1,0:T(8,128)S(1)}, u32[]{:S(2)}, u32[]{:S(2)}) collective-permute-start(f32[2,40,512]{2,1,0:T(8,128)S(1)} %get-tuple-element.64.s1_own), channel_id=1, source_target_pairs={{0,1},{1,0},{2,3},{3,2},{4,5},{5,4},{6,7},{7,6},{8,9},{9,8},{10,11... | collective-permute-start | bytes 491528 | tf_op jit(solution)/shard_map/ppermute | solution.py:463
  47.6 4.6 %collective-permute-start.19 = (bf16[32,512]{1,0:T(8,128)(2,1)S(1)}, bf16[32,512]{1,0:T(8,128)(2,1)S(1)}, u32[]{:S(2)}, u32[]{:S(2)}) collective-permute-start(bf16[32,512]{1,0:T(8,128)(2,1)S(1)} %get-tuple-element.66), channel_id=1, source_target_pairs={{0,8},{4,12},{8,0},{12,4},{16,24},{20,28},{24,16},{28,20},{1,9},{5... | collective-permute-start | bytes 98312 | tf_op jit(solution)/shard_map/ppermute | solution.py:463
  50.8 7.8 %collective-permute-start.18 = (bf16[4,32,512]{2,1,0:T(8,128)(2,1)S(1)}, bf16[4,32,512]{2,1,0:T(8,128)(2,1)S(1)}, u32[]{:S(2)}, u32[]{:S(2)}) collective-permute-start(bf16[4,32,512]{2,1,0:T(8,128)(2,1)S(1)} %second.3), channel_id=1, source_target_pairs={{0,4},{4,0},{8,12},{12,8},{16,20},{20,16},{24,28},{28,24},{1,5},{5... | collective-permute-start | bytes 393224 | tf_op jit(solution)/shard_map/ppermute | solution.py:463
  52.2 6.5 %collective-permute-start.20 = (bf16[2,32,512]{2,1,0:T(8,128)(2,1)S(1)}, bf16[2,32,512]{2,1,0:T(8,128)(2,1)S(1)}, u32[]{:S(2)}, u32[]{:S(2)}) collective-permute-start(bf16[2,32,512]{2,1,0:T(8,128)(2,1)S(1)} %pad_maximum_fusion.3.refs_0_), channel_id=1, source_target_pairs={{0,16},{4,20},{8,24},{12,28},{16,0},{20,4},{24,8},{28,12},{1,17},{... | collective-permute-start | bytes 196616 | tf_op jit(solution)/shard_map/ppermute | solution.py:463
  58.8 5.9 %collective-permute-start.21 = (bf16[32,640]{1,0:T(8,128)(2,1)S(1)}, bf16[32,640]{1,0:T(8,128)(2,1)S(1)}, u32[]{:S(2)}, u32[]{:S(2)}) collective-permute-start(bf16[32,640]{1,0:T(8,128)(2,1)S(1)} %get-tuple-element.73), channel_id=1, source_target_pairs={{0,24},{4,28},{8,16},{12,20},{16,8},{20,12},{24,0},{28,4},{1,25},{... | collective-permute-start | bytes 122888 | tf_op jit(solution)/shard_map/ppermute | solution.py:463
  61.3 4.9 %collective-permute-start.22 = (bf16[32,640]{1,0:T(8,128)(2,1)S(1)}, bf16[32,640]{1,0:T(8,128)(2,1)S(1)}, u32[]{:S(2)}, u32[]{:S(2)}) collective-permute-start(bf16[32,640]{1,0:T(8,128)(2,1)S(1)} %get-tuple-element.74), channel_id=1, source_target_pairs={{0,16},{4,20},{8,24},{12,28},{16,0},{20,4},{24,8},{28,12},{1,17},{... | collective-permute-start | bytes 122888 | tf_op jit(solution)/shard_map/ppermute | solution.py:463
  61.3 4.9 %collective-permute-start.23 = (bf16[32,640]{1,0:T(8,128)(2,1)S(1)}, bf16[32,640]{1,0:T(8,128)(2,1)S(1)}, u32[]{:S(2)}, u32[]{:S(2)}) collective-permute-start(bf16[32,640]{1,0:T(8,128)(2,1)S(1)} %get-tuple-element.75), channel_id=1, source_target_pairs={{0,8},{4,12},{8,0},{12,4},{16,24},{20,28},{24,16},{28,20},{1,9},{5... | collective-permute-start | bytes 122888 | tf_op jit(solution)/shard_map/ppermute | solution.py:463
  66.3 6.6 %collective-permute-start.25 = (f32[32,640]{1,0:T(8,128)S(1)}, f32[32,640]{1,0:T(8,128)S(1)}, u32[]{:S(2)}, u32[]{:S(2)}) collective-permute-start(f32[32,640]{1,0:T(8,128)S(1)} %get-tuple-element.76), channel_id=1, source_target_pairs={{0,2},{1,3},{2,0},{3,1},{4,6},{5,7},{6,4},{7,5},{8,10},{9,11},{10,... | collective-permute-start | bytes 245768 | tf_op jit(solution)/shard_map/ppermute | solution.py:463
  68.3 4.6 %collective-permute-start.26 = (f32[32,128]{1,0:T(8,128)S(1)}, f32[32,128]{1,0:T(8,128)S(1)}, u32[]{:S(2)}, u32[]{:S(2)}) collective-permute-start(f32[32,128]{1,0:T(8,128)S(1)} %get-tuple-element.77), channel_id=1, source_target_pairs={{0,6},{1,7},{2,4},{3,5},{4,2},{5,3},{6,0},{7,1},{8,14},{9,15},{10,... | collective-permute-start | bytes 49160 | tf_op jit(solution)/shard_map/ppermute | solution.py:473
  68.7 4.2 %collective-permute-start.24 = (f32[32,128]{1,0:T(8,128)S(1)}, f32[32,128]{1,0:T(8,128)S(1)}, u32[]{:S(2)}, u32[]{:S(2)}) collective-permute-start(f32[32,128]{1,0:T(8,128)S(1)} %get-tuple-element.77), channel_id=1, source_target_pairs={{0,4},{4,0},{8,12},{12,8},{16,20},{20,16},{24,28},{28,24},{1,5},{5... | collective-permute-start | bytes 49160 | tf_op jit(solution)/shard_map/ppermute | solution.py:463
  73.0 1.5 %collective-permute-start.27 = (f32[2,32,640]{2,1,0:T(8,128)S(1)}, f32[2,32,640]{2,1,0:T(8,128)S(1)}, u32[]{:S(2)}, u32[]{:S(2)}) collective-permute-start(f32[2,32,640]{2,1,0:T(8,128)S(1)} %pad_maximum_fusion.1.refs_0_), channel_id=1, source_target_pairs={{0,1},{1,0},{2,3},{3,2},{4,5},{5,4},{6,7},{7,6},{8,9},{9,8},{10,11... | collective-permute-start | bytes 491528 | tf_op jit(solution)/shard_map/ppermute | solution.py:463

commit v18 on v17

--- a/solution.py
+++ b/solution.py
@@ -15,7 +15,7 @@
 CODE_BITS = 12
 CODE = 1 << CODE_BITS
 RING = 3
-STRIP = 64
+STRIP = 128
 LANES = 128
 TINY = 1e-30
 SHIFT = 0.375

time: 75.9 us -> 75.6 us (level)
  waiting for transfers between devices: 21.8 us -> 20.2 us
  starting transfers between devices: 33.5 us -> 34.8 us
    ppermute x27, waiting for transfers between devices: 18.7 us -> 17.8 us  [swap(): return lax.ppermute(x, axis, [(i, i ^ d) for i in range(size)])]
  transfers between devices with their start and end apart: 28 -> 28, of which waited for: 12 -> 13; matrix products, arithmetic and copies ran while one was open for 4% -> 4% of each run, Pallas kernels for 10% -> 10%
where the time goes in v18:
time: 75.6 us; the launch traced here: 75.3 us
  starting transfers between devices  34.8 us (46%)
  waiting for transfers between devices  20.2 us (27%)
  Pallas kernels  16.3 us (22%)
  local copies, waits for them, and re-layouts  2.74 us (4%)
  between operations  0.84 us (1%)
    ppermute x27, starting transfers between devices, swap(): return lax.ppermute(x, axis, [(i, i ^ d) for i in range(size)])  33.7 us
    ppermute x27, waiting for transfers between devices, swap(): return lax.ppermute(x, axis, [(i, i ^ d) for i in range(size)])  17.8 us
    pallas_call x2, Pallas kernels, build(): pl.pallas_call(functools.partial(build_kernel, cfg, part), out_shape=out,...  8.24 us
    pallas_call x1, Pallas kernels, local(): pl.pallas_call(functools.partial(first_kernel, cfg), out_shape=[shape(out...  3.32 us
    pallas_call x2, Pallas kernels, second(): pl.pallas_call(functools.partial(second_kernel, cfg, part), out_shape=sha...  3.22 us
    ppermute x1, waiting for transfers between devices, both_swap(): return lax.ppermute(x, ('rows', 'cols'), pairs)  2.41 us
    dynamic_slice x2, local copies, waits for them, and re-layouts, own(): return lax.dynamic_slice_in_dim(x, col * own_len, own_len, 1)  1.56 us
  transfers between devices with their start and end apart: 28, of which 13 were waited for; matrix products, arithmetic and copies ran while one was open for 4% of the time, Pallas kernels for 10%

profile of v18, /device:TPU:0, one launch (start us, length us, event | category | flops | bytes accessed | tf_op | source)
XLA Modules:
  0.0 75.3 jit_solution(2543775968364595026)
XLA Ops:
  0.6 0.5 collective-permute-start
  1.1 2.6 %collective-permute-start.2 = (s32[8,6]{1,0:T(8,128)}, s32[8,6]{1,0:T(8,128)S(1)}, u32[]{:S(2)}, u32[]{:S(2)}) collective-permute-start(s32[8,6]{1,0:T(8,128)} %param.3), channel_id=1, source_target_pairs={{0,3},{1,2},{2,1},{3,0},{4,7},{5,6},{6,5},{7,4},{8,11},{9,10},{10,... | collective-permute-start | bytes 584 | tf_op jit(solution)/shard_map/ppermute | solution.py:463
  3.8 0.8 %copy.6 = s32[8,6]{0,1:T(8,128)S(1)} copy(s32[8,6]{1,0:T(8,128)} %param.3) | data formatting | bytes 384 | tf_op args[0]
  4.7 0.7 constant_dynamic-slice_fusion.1
  5.5 0.8 %constant_dynamic-slice_fusion.t_ref = f32[32,512]{1,0:T(8,128)S(1)} fusion(f32[32,2048]{1,0:T(8,128)} %t_ref.5, s32[]{:T(128)S(6)} %select_n.7), kind=kLoop, calls=%fused_computation.21 | loop fusion | bytes 131076 | tf_op jit(solution)/shard_map/dynamic_slice | solution.py:524
  6.3 0.1 copy.7
  6.5 0.1 copy.9
  6.6 1.0 %collective-permute-done.1 = s32[8,6]{1,0:T(8,128)S(1)} collective-permute-done((s32[8,6]{1,0:T(8,128)}, s32[8,6]{1,0:T(8,128)S(1)}, u32[]{:S(2)}, u32[]{:S(2)}) %collective-permute-start.1) | collective-permute-done | bytes 224 | tf_op jit(solution)/shard_map/ppermute | solution.py:463
  7.6 0.1 copy.8
  7.8 0.1 reshape.14
  7.9 3.7 %collective-permute-start.5 = (bf16[16,640]{1,0:T(8,128)(2,1)S(1)}, bf16[16,640]{1,0:T(8,128)(2,1)S(1)}, u32[]{:S(2)}, u32[]{:S(2)}) collective-permute-start(bf16[16,640]{1,0:T(8,128)(2,1)S(1)} %pad_maximum_fusion.4), channel_id=1, source_target_pairs={{0,24},{4,28},{8,16},{12,20},{16,8},{20,12},{24,0},{28,4},{1,25},{... | collective-permute-start | bytes 61448 | tf_op jit(solution)/shard_map/ppermute | solution.py:463
  11.6 0.8 %collective-permute-start.3 = (bf16[16,640]{1,0:T(8,128)(2,1)S(1)}, bf16[16,640]{1,0:T(8,128)(2,1)S(1)}, u32[]{:S(2)}, u32[]{:S(2)}) collective-permute-start(bf16[16,640]{1,0:T(8,128)(2,1)S(1)} %pad_maximum_fusion.4), channel_id=1, source_target_pairs={{0,8},{4,12},{8,0},{12,4},{16,24},{20,28},{24,16},{28,20},{1,9},{5... | collective-permute-start | bytes 61448 | tf_op jit(solution)/shard_map/ppermute | solution.py:463
  12.3 3.6 %collective-permute-start.9 = (f32[32,512]{1,0:T(8,128)S(1)}, f32[32,512]{1,0:T(8,128)S(1)}, u32[]{:S(2)}, u32[]{:S(2)}) collective-permute-start(f32[32,512]{1,0:T(8,128)S(1)} %constant_dynamic-slice_fusion.t_ref), channel_id=1, source_target_pairs={{0,24},{4,28},{8,16},{12,20},{16,8},{20,12},{24,0},{28,4},{1,25},{... | collective-permute-start | bytes 196616 | tf_op jit(solution)/shard_map/ppermute | solution.py:463
  15.9 0.8 %collective-permute-start.7 = (f32[32,512]{1,0:T(8,128)S(1)}, f32[32,512]{1,0:T(8,128)S(1)}, u32[]{:S(2)}, u32[]{:S(2)}) collective-permute-start(f32[32,512]{1,0:T(8,128)S(1)} %constant_dynamic-slice_fusion.t_ref), channel_id=1, source_target_pairs={{0,8},{4,12},{8,0},{12,4},{16,24},{20,28},{24,16},{28,20},{1,9},{5... | collective-permute-start | bytes 196616 | tf_op jit(solution)/shard_map/ppermute | solution.py:463
  16.8 1.6 %collective-permute-start.6 = (bf16[4,16,640]{2,1,0:T(8,128)(2,1)S(1)}, bf16[4,16,640]{2,1,0:T(8,128)(2,1)S(1)}, u32[]{:S(2)}, u32[]{:S(2)}) collective-permute-start(bf16[4,16,640]{2,1,0:T(8,128)(2,1)S(1)} %pad_maximum_fusion.2.refs_1_), channel_id=1, source_target_pairs={{0,4},{4,0},{8,12},{12,8},{16,20},{20,16},{24,28},{28,24},{1,5},{5... | collective-permute-start | bytes 245768 | tf_op jit(solution)/shard_map/ppermute | solution.py:463
  18.3 4.4 %build.2 = (bf16[32,4,256,256]{3,2,1,0:T(8,128)(2,1)S(1)}, s32[1,128]{1,0:T(1,128)S(1)}, f32[8,256]{1,0:T(8,128)S(1)}, bf16[8,256,32]{2,1,0:T(8,128)(2,1)S(1)}) custom-call(s32[8,64]{1,0:T(8,128)S(1)} %add_add_fusion.1.direct_v, bf16[16,2048]{1,0:T(8,128)(2,1)} %refs_0_.1, bf16[4,16,640]{2,1,0:T(8,128)(2,1)S(1)} %pad_maximum_fusion.2.refs_1_), custom_call_target="tpu_custom_call" | custom-call | flops 2684354560 | bytes 83886080 | tf_op jit(solution)/shard_map/build/pallas_call | solution.py:549
  22.8 3.9 %build.3 = (bf16[32,4,256,256]{3,2,1,0:T(8,128)(2,1)S(1)}, s32[1,128]{1,0:T(1,128)S(1)}, f32[16,256]{1,0:T(8,128)S(1)}) custom-call(s32[8,64]{1,0:T(8,128)S(1)} %add_add_fusion.1.direct_v, bf16[8,256,32]{2,1,0:T(8,128)(2,1)S(1)} %get-tuple-element.41.refs_0_, f32[8,256]{1,0:T(8,128)S(1)} %get-tuple-element.44.refs_1_, ...), custom_call_target="tpu_custom_call", output_to_operand_aliasing={{0}: (4, {})} | custom-call | flops 2684354560 | bytes 83886080 | tf_op jit(solution)/shard_map/build/pallas_call | solution.py:549
  26.7 1.3 %collective-permute-start.13 = (f32[16,256]{1,0:T(8,128)S(1)}, f32[16,256]{1,0:T(8,128)S(1)}, u32[]{:S(2)}, u32[]{:S(2)}) collective-permute-start(f32[16,256]{1,0:T(8,128)S(1)} %get-tuple-element.56), channel_id=1, source_target_pairs={{0,12},{4,8},{8,4},{12,0},{16,28},{20,24},{24,20},{28,16},{1,13},{... | collective-permute-start | bytes 49160 | tf_op jit(solution)/shard_map/ppermute | solution.py:463
  27.9 0.3 collective-permute-start.12
  28.2 2.0 %collective-permute-start.11 = (f32[16,256]{1,0:T(8,128)S(1)}, f32[16,256]{1,0:T(8,128)S(1)}, u32[]{:S(2)}, u32[]{:S(2)}) collective-permute-start(f32[16,256]{1,0:T(8,128)S(1)} %get-tuple-element.56), channel_id=1, source_target_pairs={{0,4},{4,0},{8,12},{12,8},{16,20},{20,16},{24,28},{28,24},{1,5},{5... | collective-permute-start | bytes 49160 | tf_op jit(solution)/shard_map/ppermute | solution.py:463
  30.2 1.2 %collective-permute-done.13 = f32[16,256]{1,0:T(8,128)S(1)} collective-permute-done((f32[16,256]{1,0:T(8,128)S(1)}, f32[16,256]{1,0:T(8,128)S(1)}, u32[]{:S(2)}, u32[]{:S(2)}) %collective-permute-start.13) | collective-permute-done | bytes 16416 | tf_op jit(solution)/shard_map/ppermute | solution.py:463
  31.5 0.2 collective-permute-done.12
  31.7 0.5 collective-permute-done.11
  32.2 2.7 %collective-permute-start.14 = (f32[16,256]{1,0:T(8,128)S(1)}, f32[16,256]{1,0:T(8,128)S(1)}, u32[]{:S(2)}, u32[]{:S(2)}) collective-permute-start(f32[16,256]{1,0:T(8,128)S(1)} %add_add_fusion), channel_id=1, source_target_pairs={{0,16},{4,20},{8,24},{12,28},{16,0},{20,4},{24,8},{28,12},{1,17},{... | collective-permute-start | bytes 49160 | tf_op jit(solution)/shard_map/ppermute | solution.py:463
  34.9 2.0 %collective-permute-done.14 = f32[16,256]{1,0:T(8,128)S(1)} collective-permute-done((f32[16,256]{1,0:T(8,128)S(1)}, f32[16,256]{1,0:T(8,128)S(1)}, u32[]{:S(2)}, u32[]{:S(2)}) %collective-permute-start.14) | collective-permute-done | bytes 16416 | tf_op jit(solution)/shard_map/ppermute | solution.py:463
  36.9 3.3 %first.1 = (f32[32,512]{1,0:T(8,128)S(1)}, f32[32,512]{1,0:T(8,128)S(1)}, f32[2,32,512]{2,1,0:T(8,128)S(1)}, f32[8,512]{1,0:T(8,128)S(1)}) custom-call(bf16[32,4,256,256]{3,2,1,0:T(8,128)(2,1)S(1)} %get-tuple-element.52.k_mat, s32[1,128]{1,0:T(1,128)S(1)} %get-tuple-element.53.refs_0_.list_v, s32[1,128]{1,0:T(1,128)S(1)} %get-tuple-element.54.refs_1_.list_v, ...), custom_call_target="tpu_custom_call" | custom-call | flops 536870912 | bytes 8388608 | tf_op jit(solution)/shard_map/first/pallas_call | solution.py:605
  40.3 1.3 %collective-permute-done.15.got = f32[2,32,512]{2,1,0:T(8,128)S(1)} collective-permute-done((f32[2,32,512]{2,1,0:T(8,128)S(1)}, f32[2,32,512]{2,1,0:T(8,128)S(1)}, u32[]{:S(2)}, u32[]{:S(2)}) %collective-permute-start.15) | collective-permute-done | bytes 131104 | tf_op jit(solution)/shard_map/ppermute | solution.py:463
  41.7 1.3 %collective-permute-start.16 = (bf16[112,512]{1,0:T(8,128)(2,1)S(1)}, bf16[112,512]{1,0:T(8,128)(2,1)S(1)}, u32[]{:S(2)}, u32[]{:S(2)}) collective-permute-start(bf16[112,512]{1,0:T(8,128)(2,1)S(1)} %get-tuple-element.63), channel_id=1, source_target_pairs={{0,2},{1,3},{2,0},{3,1},{4,6},{5,7},{6,4},{7,5},{8,10},{9,11},{10,... | collective-permute-start | bytes 344072 | tf_op jit(solution)/shard_map/ppermute | solution.py:463
  43.0 3.9 %collective-permute-done.16.far = bf16[112,512]{1,0:T(8,128)(2,1)S(1)} collective-permute-done((bf16[112,512]{1,0:T(8,128)(2,1)S(1)}, bf16[112,512]{1,0:T(8,128)(2,1)S(1)}, u32[]{:S(2)}, u32[]{:S(2)}) %collective-permute-start.16) | collective-permute-done | bytes 114720 | tf_op jit(solution)/shard_map/ppermute | solution.py:463
  47.1 1.6 %collective-permute-start.19 = (bf16[32,512]{1,0:T(8,128)(2,1)S(1)}, bf16[32,512]{1,0:T(8,128)(2,1)S(1)}, u32[]{:S(2)}, u32[]{:S(2)}) collective-permute-start(bf16[32,512]{1,0:T(8,128)(2,1)S(1)} %get-tuple-element.66), channel_id=1, source_target_pairs={{0,8},{4,12},{8,0},{12,4},{16,24},{20,28},{24,16},{28,20},{1,9},{5... | collective-permute-start | bytes 98312 | tf_op jit(solution)/shard_map/ppermute | solution.py:463
  48.6 1.6 %second.3 = bf16[4,32,512]{2,1,0:T(8,128)(2,1)S(1)} custom-call(bf16[32,4,256,256]{3,2,1,0:T(8,128)(2,1)S(1)} %get-tuple-element.52.k_mat, s32[1,128]{1,0:T(1,128)S(1)} %get-tuple-element.54.refs_1_.list_v, f32[32,2048]{1,0:T(8,128)S(1)} %copy-done, f32[2,40,512]{2,1,0:T(8,128)S(1)} %get-tuple-element.64.s1_own, f32[2,40,512]{2,1,0:T(8,128)S(1)} %collective-permute-done.17.s1_got), custom_call_target="tpu_custom_call" | custom-call | flops 268435456 | bytes 4194304 | tf_op jit(solution)/shard_map/second/pallas_call | solution.py:643
  50.2 1.6 %collective-permute-start.18 = (bf16[4,32,512]{2,1,0:T(8,128)(2,1)S(1)}, bf16[4,32,512]{2,1,0:T(8,128)(2,1)S(1)}, u32[]{:S(2)}, u32[]{:S(2)}) collective-permute-start(bf16[4,32,512]{2,1,0:T(8,128)(2,1)S(1)} %second.3), channel_id=1, source_target_pairs={{0,4},{4,0},{8,12},{12,8},{16,20},{20,16},{24,28},{28,24},{1,5},{5... | collective-permute-start | bytes 393224 | tf_op jit(solution)/shard_map/ppermute | solution.py:463
  51.8 2.3 %collective-permute-start.20 = (bf16[2,32,512]{2,1,0:T(8,128)(2,1)S(1)}, bf16[2,32,512]{2,1,0:T(8,128)(2,1)S(1)}, u32[]{:S(2)}, u32[]{:S(2)}) collective-permute-start(bf16[2,32,512]{2,1,0:T(8,128)(2,1)S(1)} %pad_maximum_fusion.3.refs_0_), channel_id=1, source_target_pairs={{0,16},{4,20},{8,24},{12,28},{16,0},{20,4},{24,8},{28,12},{1,17},{... | collective-permute-start | bytes 196616 | tf_op jit(solution)/shard_map/ppermute | solution.py:463
  54.1 1.6 %second.2.z_same = f32[4,32,512]{2,1,0:T(8,128)S(1)} custom-call(bf16[32,4,256,256]{3,2,1,0:T(8,128)(2,1)S(1)} %get-tuple-element.52.k_mat, s32[1,128]{1,0:T(1,128)S(1)} %get-tuple-element.53.refs_0_.list_v, f32[32,2048]{1,0:T(8,128)S(1)} %copy-done, f32[2,40,512]{2,1,0:T(8,128)S(1)} %get-tuple-element.64.s1_own, ...), custom_call_target="tpu_custom_call" | custom-call | flops 268435456 | bytes 4194304 | tf_op jit(solution)/shard_map/second/pallas_call | solution.py:643
  55.7 2.4 %collective-permute-done.20.refs_1_ = bf16[2,32,512]{2,1,0:T(8,128)(2,1)S(1)} collective-permute-done((bf16[2,32,512]{2,1,0:T(8,128)(2,1)S(1)}, bf16[2,32,512]{2,1,0:T(8,128)(2,1)S(1)}, u32[]{:S(2)}, u32[]{:S(2)}) %collective-permute-start.20) | collective-permute-done | bytes 65568 | tf_op jit(solution)/shard_map/ppermute | solution.py:463
  58.1 0.2 meet.1
  58.3 3.1 %collective-permute-start.21 = (bf16[32,640]{1,0:T(8,128)(2,1)S(1)}, bf16[32,640]{1,0:T(8,128)(2,1)S(1)}, u32[]{:S(2)}, u32[]{:S(2)}) collective-permute-start(bf16[32,640]{1,0:T(8,128)(2,1)S(1)} %get-tuple-element.73), channel_id=1, source_target_pairs={{0,24},{4,28},{8,16},{12,20},{16,8},{20,12},{24,0},{28,4},{1,25},{... | collective-permute-start | bytes 122888 | tf_op jit(solution)/shard_map/ppermute | solution.py:463
  61.5 1.3 %collective-permute-start.23 = (bf16[32,640]{1,0:T(8,128)(2,1)S(1)}, bf16[32,640]{1,0:T(8,128)(2,1)S(1)}, u32[]{:S(2)}, u32[]{:S(2)}) collective-permute-start(bf16[32,640]{1,0:T(8,128)(2,1)S(1)} %get-tuple-element.75), channel_id=1, source_target_pairs={{0,8},{4,12},{8,0},{12,4},{16,24},{20,28},{24,16},{28,20},{1,9},{5... | collective-permute-start | bytes 122888 | tf_op jit(solution)/shard_map/ppermute | solution.py:463
  62.8 1.5 %collective-permute-done.21.refs_0_ = bf16[32,640]{1,0:T(8,128)(2,1)S(1)} collective-permute-done((bf16[32,640]{1,0:T(8,128)(2,1)S(1)}, bf16[32,640]{1,0:T(8,128)(2,1)S(1)}, u32[]{:S(2)}, u32[]{:S(2)}) %collective-permute-start.21) | collective-permute-done | bytes 40992 | tf_op jit(solution)/shard_map/ppermute | solution.py:463
  64.3 2.1 %collective-permute-done.22.refs_1_ = bf16[32,640]{1,0:T(8,128)(2,1)S(1)} collective-permute-done((bf16[32,640]{1,0:T(8,128)(2,1)S(1)}, bf16[32,640]{1,0:T(8,128)(2,1)S(1)}, u32[]{:S(2)}, u32[]{:S(2)}) %collective-permute-start.22) | collective-permute-done | bytes 40992 | tf_op jit(solution)/shard_map/ppermute | solution.py:463
  66.4 0.1 products.1
  66.5 1.3 %collective-permute-start.25 = (f32[32,640]{1,0:T(8,128)S(1)}, f32[32,640]{1,0:T(8,128)S(1)}, u32[]{:S(2)}, u32[]{:S(2)}) collective-permute-start(f32[32,640]{1,0:T(8,128)S(1)} %get-tuple-element.76), channel_id=1, source_target_pairs={{0,2},{1,3},{2,0},{3,1},{4,6},{5,7},{6,4},{7,5},{8,10},{9,11},{10,... | collective-permute-start | bytes 245768 | tf_op jit(solution)/shard_map/ppermute | solution.py:463
  67.7 1.1 %collective-permute-start.26 = (f32[32,128]{1,0:T(8,128)S(1)}, f32[32,128]{1,0:T(8,128)S(1)}, u32[]{:S(2)}, u32[]{:S(2)}) collective-permute-start(f32[32,128]{1,0:T(8,128)S(1)} %get-tuple-element.77), channel_id=1, source_target_pairs={{0,6},{1,7},{2,4},{3,5},{4,2},{5,3},{6,0},{7,1},{8,14},{9,15},{10,... | collective-permute-start | bytes 49160 | tf_op jit(solution)/shard_map/ppermute | solution.py:473
  68.9 1.1 %collective-permute-start.24 = (f32[32,128]{1,0:T(8,128)S(1)}, f32[32,128]{1,0:T(8,128)S(1)}, u32[]{:S(2)}, u32[]{:S(2)}) collective-permute-start(f32[32,128]{1,0:T(8,128)S(1)} %get-tuple-element.77), channel_id=1, source_target_pairs={{0,4},{4,0},{8,12},{12,8},{16,20},{20,16},{24,28},{28,24},{1,5},{5... | collective-permute-start | bytes 49160 | tf_op jit(solution)/shard_map/ppermute | solution.py:463
  70.0 2.4 %collective-permute-done.26 = f32[32,128]{1,0:T(8,128)S(1)} collective-permute-done((f32[32,128]{1,0:T(8,128)S(1)}, f32[32,128]{1,0:T(8,128)S(1)}, u32[]{:S(2)}, u32[]{:S(2)}) %collective-permute-start.26) | collective-permute-done | bytes 16416 | tf_op jit(solution)/shard_map/ppermute | solution.py:473
  72.4 0.2 collective-permute-done.24
  72.8 1.4 %collective-permute-done.27.refs_1_ = f32[2,32,640]{2,1,0:T(8,128)S(1)} collective-permute-done((f32[2,32,640]{2,1,0:T(8,128)S(1)}, f32[2,32,640]{2,1,0:T(8,128)S(1)}, u32[]{:S(2)}, u32[]{:S(2)}) %collective-permute-start.27) | collective-permute-done | bytes 163872 | tf_op jit(solution)/shard_map/ppermute | solution.py:463
  74.1 1.2 %final.1 = (f32[32,2048]{1,0:T(8,128)}, f32[32,2048]{1,0:T(8,128)}) custom-call(f32[32,2048]{1,0:T(8,128)S(1)} %copy-done, f32[2,40,512]{2,1,0:T(8,128)S(1)} %get-tuple-element.64.s1_own, f32[2,40,512]{2,1,0:T(8,128)S(1)} %collective-permute-done.17.s1_got, f32[2,32,640]{2,1,0:T(8,128)S(1)} %pad_maximum_fusion.1.refs_0_, ...), custom_call_target="tpu_custom_call" | custom-call | tf_op jit(solution)/shard_map/final/pallas_call | solution.py:706
  (44 shorter events, 0.9 us)
Async XLA Ops:
  0.6 5.7 %collective-permute-start = (s32[8,6]{1,0:T(8,128)}, s32[8,6]{1,0:T(8,128)S(1)}, u32[]{:S(2)}, u32[]{:S(2)}) collective-permute-start(s32[8,6]{1,0:T(8,128)} %param.3), channel_id=1, source_target_pairs={{0,1},{1,0},{2,3},{3,2},{4,5},{5,4},{6,7},{7,6},{8,9},{9,8},{10,11... | collective-permute-start | bytes 584 | tf_op jit(solution)/shard_map/ppermute | solution.py:463
  1.1 5.3 %collective-permute-start.2 = (s32[8,6]{1,0:T(8,128)}, s32[8,6]{1,0:T(8,128)S(1)}, u32[]{:S(2)}, u32[]{:S(2)}) collective-permute-start(s32[8,6]{1,0:T(8,128)} %param.3), channel_id=1, source_target_pairs={{0,3},{1,2},{2,1},{3,0},{4,7},{5,6},{6,5},{7,4},{8,11},{9,10},{10,... | collective-permute-start | bytes 584 | tf_op jit(solution)/shard_map/ppermute | solution.py:463
  3.8 3.8 %collective-permute-start.1 = (s32[8,6]{1,0:T(8,128)}, s32[8,6]{1,0:T(8,128)S(1)}, u32[]{:S(2)}, u32[]{:S(2)}) collective-permute-start(s32[8,6]{1,0:T(8,128)} %param.3), channel_id=1, source_target_pairs={{0,2},{1,3},{2,0},{3,1},{4,6},{5,7},{6,4},{7,5},{8,10},{9,11},{10,... | collective-permute-start | bytes 584 | tf_op jit(solution)/shard_map/ppermute | solution.py:463
  7.9 8.1 %collective-permute-start.5 = (bf16[16,640]{1,0:T(8,128)(2,1)S(1)}, bf16[16,640]{1,0:T(8,128)(2,1)S(1)}, u32[]{:S(2)}, u32[]{:S(2)}) collective-permute-start(bf16[16,640]{1,0:T(8,128)(2,1)S(1)} %pad_maximum_fusion.4), channel_id=1, source_target_pairs={{0,24},{4,28},{8,16},{12,20},{16,8},{20,12},{24,0},{28,4},{1,25},{... | collective-permute-start | bytes 61448 | tf_op jit(solution)/shard_map/ppermute | solution.py:463
  11.6 5.2 %collective-permute-start.4 = (bf16[16,640]{1,0:T(8,128)(2,1)S(1)}, bf16[16,640]{1,0:T(8,128)(2,1)S(1)}, u32[]{:S(2)}, u32[]{:S(2)}) collective-permute-start(bf16[16,640]{1,0:T(8,128)(2,1)S(1)} %pad_maximum_fusion.4), channel_id=1, source_target_pairs={{0,16},{4,20},{8,24},{12,28},{16,0},{20,4},{24,8},{28,12},{1,17},{... | collective-permute-start | bytes 61448 | tf_op jit(solution)/shard_map/ppermute | solution.py:463
  11.6 5.2 %collective-permute-start.3 = (bf16[16,640]{1,0:T(8,128)(2,1)S(1)}, bf16[16,640]{1,0:T(8,128)(2,1)S(1)}, u32[]{:S(2)}, u32[]{:S(2)}) collective-permute-start(bf16[16,640]{1,0:T(8,128)(2,1)S(1)} %pad_maximum_fusion.4), channel_id=1, source_target_pairs={{0,8},{4,12},{8,0},{12,4},{16,24},{20,28},{24,16},{28,20},{1,9},{5... | collective-permute-start | bytes 61448 | tf_op jit(solution)/shard_map/ppermute | solution.py:463
  12.3 10.3 %collective-permute-start.9 = (f32[32,512]{1,0:T(8,128)S(1)}, f32[32,512]{1,0:T(8,128)S(1)}, u32[]{:S(2)}, u32[]{:S(2)}) collective-permute-start(f32[32,512]{1,0:T(8,128)S(1)} %constant_dynamic-slice_fusion.t_ref), channel_id=1, source_target_pairs={{0,24},{4,28},{8,16},{12,20},{16,8},{20,12},{24,0},{28,4},{1,25},{... | collective-permute-start | bytes 196616 | tf_op jit(solution)/shard_map/ppermute | solution.py:463
  15.9 6.8 %collective-permute-start.8 = (f32[32,512]{1,0:T(8,128)S(1)}, f32[32,512]{1,0:T(8,128)S(1)}, u32[]{:S(2)}, u32[]{:S(2)}) collective-permute-start(f32[32,512]{1,0:T(8,128)S(1)} %constant_dynamic-slice_fusion.t_ref), channel_id=1, source_target_pairs={{0,16},{4,20},{8,24},{12,28},{16,0},{20,4},{24,8},{28,12},{1,17},{... | collective-permute-start | bytes 196616 | tf_op jit(solution)/shard_map/ppermute | solution.py:463
  15.9 6.8 %collective-permute-start.7 = (f32[32,512]{1,0:T(8,128)S(1)}, f32[32,512]{1,0:T(8,128)S(1)}, u32[]{:S(2)}, u32[]{:S(2)}) collective-permute-start(f32[32,512]{1,0:T(8,128)S(1)} %constant_dynamic-slice_fusion.t_ref), channel_id=1, source_target_pairs={{0,8},{4,12},{8,0},{12,4},{16,24},{20,28},{24,16},{28,20},{1,9},{5... | collective-permute-start | bytes 196616 | tf_op jit(solution)/shard_map/ppermute | solution.py:463
  16.8 6.0 %collective-permute-start.6 = (bf16[4,16,640]{2,1,0:T(8,128)(2,1)S(1)}, bf16[4,16,640]{2,1,0:T(8,128)(2,1)S(1)}, u32[]{:S(2)}, u32[]{:S(2)}) collective-permute-start(bf16[4,16,640]{2,1,0:T(8,128)(2,1)S(1)} %pad_maximum_fusion.2.refs_1_), channel_id=1, source_target_pairs={{0,4},{4,0},{8,12},{12,8},{16,20},{20,16},{24,28},{28,24},{1,5},{5... | collective-permute-start | bytes 245768 | tf_op jit(solution)/shard_map/ppermute | solution.py:463
  26.6 22.0 %copy-start = (f32[32,2048]{1,0:T(8,128)S(1)}, f32[32,2048]{1,0:T(8,128)}, u32[]{:S(2)}) copy-start(f32[32,2048]{1,0:T(8,128)} %t_ref.5) | copy-start | bytes 786436
  26.7 4.8 %collective-permute-start.13 = (f32[16,256]{1,0:T(8,128)S(1)}, f32[16,256]{1,0:T(8,128)S(1)}, u32[]{:S(2)}, u32[]{:S(2)}) collective-permute-start(f32[16,256]{1,0:T(8,128)S(1)} %get-tuple-element.56), channel_id=1, source_target_pairs={{0,12},{4,8},{8,4},{12,0},{16,28},{20,24},{24,20},{28,16},{1,13},{... | collective-permute-start | bytes 49160 | tf_op jit(solution)/shard_map/ppermute | solution.py:463
  27.9 3.7 %collective-permute-start.12 = (f32[16,256]{1,0:T(8,128)S(1)}, f32[16,256]{1,0:T(8,128)S(1)}, u32[]{:S(2)}, u32[]{:S(2)}) collective-permute-start(f32[16,256]{1,0:T(8,128)S(1)} %get-tuple-element.56), channel_id=1, source_target_pairs={{0,8},{4,12},{8,0},{12,4},{16,24},{20,28},{24,16},{28,20},{1,9},{5... | collective-permute-start | bytes 49160 | tf_op jit(solution)/shard_map/ppermute | solution.py:463
  28.2 4.0 %collective-permute-start.11 = (f32[16,256]{1,0:T(8,128)S(1)}, f32[16,256]{1,0:T(8,128)S(1)}, u32[]{:S(2)}, u32[]{:S(2)}) collective-permute-start(f32[16,256]{1,0:T(8,128)S(1)} %get-tuple-element.56), channel_id=1, source_target_pairs={{0,4},{4,0},{8,12},{12,8},{16,20},{20,16},{24,28},{28,24},{1,5},{5... | collective-permute-start | bytes 49160 | tf_op jit(solution)/shard_map/ppermute | solution.py:463
  30.2 6.7 %collective-permute-start.10 = (f32[4,32,512]{2,1,0:T(8,128)S(1)}, f32[4,32,512]{2,1,0:T(8,128)S(1)}, u32[]{:S(2)}, u32[]{:S(2)}) collective-permute-start(f32[4,32,512]{2,1,0:T(8,128)S(1)} %pad_maximum_fusion.refs_2_.t_same), channel_id=1, source_target_pairs={{0,4},{4,0},{8,12},{12,8},{16,20},{20,16},{24,28},{28,24},{1,5},{5... | collective-permute-start | bytes 786440 | tf_op jit(solution)/shard_map/ppermute | solution.py:463
  32.2 4.7 %collective-permute-start.14 = (f32[16,256]{1,0:T(8,128)S(1)}, f32[16,256]{1,0:T(8,128)S(1)}, u32[]{:S(2)}, u32[]{:S(2)}) collective-permute-start(f32[16,256]{1,0:T(8,128)S(1)} %add_add_fusion), channel_id=1, source_target_pairs={{0,16},{4,20},{8,24},{12,28},{16,0},{20,4},{24,8},{28,12},{1,17},{... | collective-permute-start | bytes 49160 | tf_op jit(solution)/shard_map/ppermute | solution.py:463
  40.2 1.4 %collective-permute-start.15 = (f32[2,32,512]{2,1,0:T(8,128)S(1)}, f32[2,32,512]{2,1,0:T(8,128)S(1)}, u32[]{:S(2)}, u32[]{:S(2)}) collective-permute-start(f32[2,32,512]{2,1,0:T(8,128)S(1)} %get-tuple-element.59), channel_id=1, source_target_pairs={{0,1},{1,0},{2,3},{3,2},{4,5},{5,4},{6,7},{7,6},{8,9},{9,8},{10,11... | collective-permute-start | bytes 393224 | tf_op jit(solution)/shard_map/ppermute | solution.py:463
  41.7 5.3 %collective-permute-start.16 = (bf16[112,512]{1,0:T(8,128)(2,1)S(1)}, bf16[112,512]{1,0:T(8,128)(2,1)S(1)}, u32[]{:S(2)}, u32[]{:S(2)}) collective-permute-start(bf16[112,512]{1,0:T(8,128)(2,1)S(1)} %get-tuple-element.63), channel_id=1, source_target_pairs={{0,2},{1,3},{2,0},{3,1},{4,6},{5,7},{6,4},{7,5},{8,10},{9,11},{10,... | collective-permute-start | bytes 344072 | tf_op jit(solution)/shard_map/ppermute | solution.py:463
  47.0 1.6 %collective-permute-start.17 = (f32[2,40,512]{2,1,0:T(8,128)S(1)}, f32[2,40,512]{2,1,0:T(8,128)S(1)}, u32[]{:S(2)}, u32[]{:S(2)}) collective-permute-start(f32[2,40,512]{2,1,0:T(8,128)S(1)} %get-tuple-element.64.s1_own), channel_id=1, source_target_pairs={{0,1},{1,0},{2,3},{3,2},{4,5},{5,4},{6,7},{7,6},{8,9},{9,8},{10,11... | collective-permute-start | bytes 491528 | tf_op jit(solution)/shard_map/ppermute | solution.py:463
  47.1 4.8 %collective-permute-start.19 = (bf16[32,512]{1,0:T(8,128)(2,1)S(1)}, bf16[32,512]{1,0:T(8,128)(2,1)S(1)}, u32[]{:S(2)}, u32[]{:S(2)}) collective-permute-start(bf16[32,512]{1,0:T(8,128)(2,1)S(1)} %get-tuple-element.66), channel_id=1, source_target_pairs={{0,8},{4,12},{8,0},{12,4},{16,24},{20,28},{24,16},{28,20},{1,9},{5... | collective-permute-start | bytes 98312 | tf_op jit(solution)/shard_map/ppermute | solution.py:463
  50.2 7.9 %collective-permute-start.18 = (bf16[4,32,512]{2,1,0:T(8,128)(2,1)S(1)}, bf16[4,32,512]{2,1,0:T(8,128)(2,1)S(1)}, u32[]{:S(2)}, u32[]{:S(2)}) collective-permute-start(bf16[4,32,512]{2,1,0:T(8,128)(2,1)S(1)} %second.3), channel_id=1, source_target_pairs={{0,4},{4,0},{8,12},{12,8},{16,20},{20,16},{24,28},{28,24},{1,5},{5... | collective-permute-start | bytes 393224 | tf_op jit(solution)/shard_map/ppermute | solution.py:463
  51.8 6.3 %collective-permute-start.20 = (bf16[2,32,512]{2,1,0:T(8,128)(2,1)S(1)}, bf16[2,32,512]{2,1,0:T(8,128)(2,1)S(1)}, u32[]{:S(2)}, u32[]{:S(2)}) collective-permute-start(bf16[2,32,512]{2,1,0:T(8,128)(2,1)S(1)} %pad_maximum_fusion.3.refs_0_), channel_id=1, source_target_pairs={{0,16},{4,20},{8,24},{12,28},{16,0},{20,4},{24,8},{28,12},{1,17},{... | collective-permute-start | bytes 196616 | tf_op jit(solution)/shard_map/ppermute | solution.py:463
  58.3 6.0 %collective-permute-start.21 = (bf16[32,640]{1,0:T(8,128)(2,1)S(1)}, bf16[32,640]{1,0:T(8,128)(2,1)S(1)}, u32[]{:S(2)}, u32[]{:S(2)}) collective-permute-start(bf16[32,640]{1,0:T(8,128)(2,1)S(1)} %get-tuple-element.73), channel_id=1, source_target_pairs={{0,24},{4,28},{8,16},{12,20},{16,8},{20,12},{24,0},{28,4},{1,25},{... | collective-permute-start | bytes 122888 | tf_op jit(solution)/shard_map/ppermute | solution.py:463
  61.5 4.9 %collective-permute-start.22 = (bf16[32,640]{1,0:T(8,128)(2,1)S(1)}, bf16[32,640]{1,0:T(8,128)(2,1)S(1)}, u32[]{:S(2)}, u32[]{:S(2)}) collective-permute-start(bf16[32,640]{1,0:T(8,128)(2,1)S(1)} %get-tuple-element.74), channel_id=1, source_target_pairs={{0,16},{4,20},{8,24},{12,28},{16,0},{20,4},{24,8},{28,12},{1,17},{... | collective-permute-start | bytes 122888 | tf_op jit(solution)/shard_map/ppermute | solution.py:463
  61.5 4.9 %collective-permute-start.23 = (bf16[32,640]{1,0:T(8,128)(2,1)S(1)}, bf16[32,640]{1,0:T(8,128)(2,1)S(1)}, u32[]{:S(2)}, u32[]{:S(2)}) collective-permute-start(bf16[32,640]{1,0:T(8,128)(2,1)S(1)} %get-tuple-element.75), channel_id=1, source_target_pairs={{0,8},{4,12},{8,0},{12,4},{16,24},{20,28},{24,16},{28,20},{1,9},{5... | collective-permute-start | bytes 122888 | tf_op jit(solution)/shard_map/ppermute | solution.py:463
  66.5 6.2 %collective-permute-start.25 = (f32[32,640]{1,0:T(8,128)S(1)}, f32[32,640]{1,0:T(8,128)S(1)}, u32[]{:S(2)}, u32[]{:S(2)}) collective-permute-start(f32[32,640]{1,0:T(8,128)S(1)} %get-tuple-element.76), channel_id=1, source_target_pairs={{0,2},{1,3},{2,0},{3,1},{4,6},{5,7},{6,4},{7,5},{8,10},{9,11},{10,... | collective-permute-start | bytes 245768 | tf_op jit(solution)/shard_map/ppermute | solution.py:463
  67.7 4.6 %collective-permute-start.26 = (f32[32,128]{1,0:T(8,128)S(1)}, f32[32,128]{1,0:T(8,128)S(1)}, u32[]{:S(2)}, u32[]{:S(2)}) collective-permute-start(f32[32,128]{1,0:T(8,128)S(1)} %get-tuple-element.77), channel_id=1, source_target_pairs={{0,6},{1,7},{2,4},{3,5},{4,2},{5,3},{6,0},{7,1},{8,14},{9,15},{10,... | collective-permute-start | bytes 49160 | tf_op jit(solution)/shard_map/ppermute | solution.py:473
  68.9 3.7 %collective-permute-start.24 = (f32[32,128]{1,0:T(8,128)S(1)}, f32[32,128]{1,0:T(8,128)S(1)}, u32[]{:S(2)}, u32[]{:S(2)}) collective-permute-start(f32[32,128]{1,0:T(8,128)S(1)} %get-tuple-element.77), channel_id=1, source_target_pairs={{0,4},{4,0},{8,12},{12,8},{16,20},{20,16},{24,28},{28,24},{1,5},{5... | collective-permute-start | bytes 49160 | tf_op jit(solution)/shard_map/ppermute | solution.py:463
  72.7 1.5 %collective-permute-start.27 = (f32[2,32,640]{2,1,0:T(8,128)S(1)}, f32[2,32,640]{2,1,0:T(8,128)S(1)}, u32[]{:S(2)}, u32[]{:S(2)}) collective-permute-start(f32[2,32,640]{2,1,0:T(8,128)S(1)} %pad_maximum_fusion.1.refs_0_), channel_id=1, source_target_pairs={{0,1},{1,0},{2,3},{3,2},{4,5},{5,4},{6,7},{7,6},{8,9},{9,8},{10,11... | collective-permute-start | bytes 491528 | tf_op jit(solution)/shard_map/ppermute | solution.py:463

commit v19 on v18

--- a/solution.py
+++ b/solution.py
@@ -375,7 +375,7 @@
 
 def meet_kernel(cfg, z_same, z_other, t_same, inv_ref, s1_own, *refs):
     g_near, g_far, own_z, own_dots, *outs = refs
-    gs = g_near[0], g_near[1], g_far[0], g_far[1]
+    gs = g_near[0], g_far[0], g_near[1], g_far[1]
     own_rows, block_len = cfg.own_rows, cfg.block_len
     outputs, own_len = own_z.shape
     place = position()
@@ -658,12 +658,12 @@
         )(k_mat, k_lists[part], held_t, s1_own, s1_got)
 
     if direct_rows:
-        parts_of_g = (g, swap(g, "rows", 2))
+        parts_of_g = (g, swap(g, "rows", 4))
         z2_other = second(1, BF16)
         _, *parts_of_g = lax.optimization_barrier((z2_other, *parts_of_g))
         g = jnp.stack(parts_of_g)
         z2_other = swap(z2_other, "rows", 1)
-        far_g = swap(g, "rows", 4)
+        far_g = swap(g, "rows", 2)
         z2_same = second(0, F32)
         z2_same, z2_other, far_g = lax.optimization_barrier((z2_same, z2_other, far_g))
         row_piece = shape(outputs, own_len + LANES, dtype=BF16)

time: 75.6 us -> 75.2 us (level)
  Pallas kernels: 16.3 us -> 15.2 us
  starting transfers between devices: 34.8 us -> 35.7 us
  transfers between devices with their start and end apart: 28 -> 28, of which waited for: 13 -> 12; matrix products, arithmetic and copies ran while one was open for 4% -> 4% of each run, Pallas kernels for 10% -> 9%
where the time goes in v19:
time: 75.2 us; the launch traced here: 74.8 us
  starting transfers between devices  35.7 us (47%)
  waiting for transfers between devices  19.8 us (26%)
  Pallas kernels  15.2 us (20%)
  local copies, waits for them, and re-layouts  2.74 us (4%)
  between operations  0.84 us (1%)
    ppermute x27, starting transfers between devices, swap(): return lax.ppermute(x, axis, [(i, i ^ d) for i in range(size)])  33.9 us
    ppermute x27, waiting for transfers between devices, swap(): return lax.ppermute(x, axis, [(i, i ^ d) for i in range(size)])  17.6 us
    pallas_call x2, Pallas kernels, build(): pl.pallas_call(functools.partial(build_kernel, cfg, part), out_shape=out,...  7.69 us
    pallas_call x1, Pallas kernels, local(): pl.pallas_call(functools.partial(first_kernel, cfg), out_shape=[shape(out...  3.05 us
    pallas_call x2, Pallas kernels, second(): pl.pallas_call(functools.partial(second_kernel, cfg, part), out_shape=sha...  2.99 us
    ppermute x1, waiting for transfers between devices, both_swap(): return lax.ppermute(x, ('rows', 'cols'), pairs)  2.27 us
    ppermute x1, starting transfers between devices, both_swap(): return lax.ppermute(x, ('rows', 'cols'), pairs)  1.81 us
    dynamic_slice x2, local copies, waits for them, and re-layouts, own(): return lax.dynamic_slice_in_dim(x, col * own_len, own_len, 1)  1.56 us
  transfers between devices with their start and end apart: 28, of which 12 were waited for; matrix products, arithmetic and copies ran while one was open for 4% of the time, Pallas kernels for 9%

profile of v19, /device:TPU:0, one launch (start us, length us, event | category | flops | bytes accessed | tf_op | source)
XLA Modules:
  0.0 74.8 jit_solution(14802558454309531059)
XLA Ops:
  0.6 0.5 collective-permute-start
  1.1 2.6 %collective-permute-start.2 = (s32[8,6]{1,0:T(8,128)}, s32[8,6]{1,0:T(8,128)S(1)}, u32[]{:S(2)}, u32[]{:S(2)}) collective-permute-start(s32[8,6]{1,0:T(8,128)} %param.3), channel_id=1, source_target_pairs={{0,3},{1,2},{2,1},{3,0},{4,7},{5,6},{6,5},{7,4},{8,11},{9,10},{10,... | collective-permute-start | bytes 584 | tf_op jit(solution)/shard_map/ppermute | solution.py:463
  3.8 0.8 %copy.6 = s32[8,6]{0,1:T(8,128)S(1)} copy(s32[8,6]{1,0:T(8,128)} %param.3) | data formatting | bytes 384 | tf_op args[0]
  4.7 0.7 constant_dynamic-slice_fusion.1
  5.5 0.8 %constant_dynamic-slice_fusion.t_ref = f32[32,512]{1,0:T(8,128)S(1)} fusion(f32[32,2048]{1,0:T(8,128)} %t_ref.5, s32[]{:T(128)S(6)} %select_n.7), kind=kLoop, calls=%fused_computation.21 | loop fusion | bytes 131076 | tf_op jit(solution)/shard_map/dynamic_slice | solution.py:524
  6.3 0.1 copy.7
  6.5 0.1 copy.9
  6.6 1.0 %collective-permute-done.1 = s32[8,6]{1,0:T(8,128)S(1)} collective-permute-done((s32[8,6]{1,0:T(8,128)}, s32[8,6]{1,0:T(8,128)S(1)}, u32[]{:S(2)}, u32[]{:S(2)}) %collective-permute-start.1) | collective-permute-done | bytes 224 | tf_op jit(solution)/shard_map/ppermute | solution.py:463
  7.6 0.1 copy.8
  7.8 0.1 reshape.14
  7.9 3.7 %collective-permute-start.5 = (bf16[16,640]{1,0:T(8,128)(2,1)S(1)}, bf16[16,640]{1,0:T(8,128)(2,1)S(1)}, u32[]{:S(2)}, u32[]{:S(2)}) collective-permute-start(bf16[16,640]{1,0:T(8,128)(2,1)S(1)} %pad_maximum_fusion.4), channel_id=1, source_target_pairs={{0,24},{4,28},{8,16},{12,20},{16,8},{20,12},{24,0},{28,4},{1,25},{... | collective-permute-start | bytes 61448 | tf_op jit(solution)/shard_map/ppermute | solution.py:463
  11.6 0.8 %collective-permute-start.3 = (bf16[16,640]{1,0:T(8,128)(2,1)S(1)}, bf16[16,640]{1,0:T(8,128)(2,1)S(1)}, u32[]{:S(2)}, u32[]{:S(2)}) collective-permute-start(bf16[16,640]{1,0:T(8,128)(2,1)S(1)} %pad_maximum_fusion.4), channel_id=1, source_target_pairs={{0,8},{4,12},{8,0},{12,4},{16,24},{20,28},{24,16},{28,20},{1,9},{5... | collective-permute-start | bytes 61448 | tf_op jit(solution)/shard_map/ppermute | solution.py:463
  12.3 3.6 %collective-permute-start.9 = (f32[32,512]{1,0:T(8,128)S(1)}, f32[32,512]{1,0:T(8,128)S(1)}, u32[]{:S(2)}, u32[]{:S(2)}) collective-permute-start(f32[32,512]{1,0:T(8,128)S(1)} %constant_dynamic-slice_fusion.t_ref), channel_id=1, source_target_pairs={{0,24},{4,28},{8,16},{12,20},{16,8},{20,12},{24,0},{28,4},{1,25},{... | collective-permute-start | bytes 196616 | tf_op jit(solution)/shard_map/ppermute | solution.py:463
  15.9 0.8 %collective-permute-start.7 = (f32[32,512]{1,0:T(8,128)S(1)}, f32[32,512]{1,0:T(8,128)S(1)}, u32[]{:S(2)}, u32[]{:S(2)}) collective-permute-start(f32[32,512]{1,0:T(8,128)S(1)} %constant_dynamic-slice_fusion.t_ref), channel_id=1, source_target_pairs={{0,8},{4,12},{8,0},{12,4},{16,24},{20,28},{24,16},{28,20},{1,9},{5... | collective-permute-start | bytes 196616 | tf_op jit(solution)/shard_map/ppermute | solution.py:463
  16.8 1.6 %collective-permute-start.6 = (bf16[4,16,640]{2,1,0:T(8,128)(2,1)S(1)}, bf16[4,16,640]{2,1,0:T(8,128)(2,1)S(1)}, u32[]{:S(2)}, u32[]{:S(2)}) collective-permute-start(bf16[4,16,640]{2,1,0:T(8,128)(2,1)S(1)} %pad_maximum_fusion.2.refs_1_), channel_id=1, source_target_pairs={{0,4},{4,0},{8,12},{12,8},{16,20},{20,16},{24,28},{28,24},{1,5},{5... | collective-permute-start | bytes 245768 | tf_op jit(solution)/shard_map/ppermute | solution.py:463
  18.3 3.8 %build.2 = (bf16[32,4,256,256]{3,2,1,0:T(8,128)(2,1)S(1)}, s32[1,128]{1,0:T(1,128)S(1)}, f32[8,256]{1,0:T(8,128)S(1)}, bf16[8,256,32]{2,1,0:T(8,128)(2,1)S(1)}) custom-call(s32[8,64]{1,0:T(8,128)S(1)} %add_add_fusion.1.direct_v, bf16[16,2048]{1,0:T(8,128)(2,1)} %refs_0_.1, bf16[4,16,640]{2,1,0:T(8,128)(2,1)S(1)} %pad_maximum_fusion.2.refs_1_), custom_call_target="tpu_custom_call" | custom-call | flops 2684354560 | bytes 83886080 | tf_op jit(solution)/shard_map/build/pallas_call | solution.py:549
  22.2 3.9 %build.3 = (bf16[32,4,256,256]{3,2,1,0:T(8,128)(2,1)S(1)}, s32[1,128]{1,0:T(1,128)S(1)}, f32[16,256]{1,0:T(8,128)S(1)}) custom-call(s32[8,64]{1,0:T(8,128)S(1)} %add_add_fusion.1.direct_v, bf16[8,256,32]{2,1,0:T(8,128)(2,1)S(1)} %get-tuple-element.41.refs_0_, f32[8,256]{1,0:T(8,128)S(1)} %get-tuple-element.44.refs_1_, ...), custom_call_target="tpu_custom_call", output_to_operand_aliasing={{0}: (4, {})} | custom-call | flops 2684354560 | bytes 83886080 | tf_op jit(solution)/shard_map/build/pallas_call | solution.py:549
  26.1 0.3 collective-permute-start.13
  26.4 2.4 %collective-permute-start.12 = (f32[16,256]{1,0:T(8,128)S(1)}, f32[16,256]{1,0:T(8,128)S(1)}, u32[]{:S(2)}, u32[]{:S(2)}) collective-permute-start(f32[16,256]{1,0:T(8,128)S(1)} %get-tuple-element.56), channel_id=1, source_target_pairs={{0,8},{4,12},{8,0},{12,4},{16,24},{20,28},{24,16},{28,20},{1,9},{5... | collective-permute-start | bytes 49160 | tf_op jit(solution)/shard_map/ppermute | solution.py:463
  28.7 0.9 %collective-permute-start.11 = (f32[16,256]{1,0:T(8,128)S(1)}, f32[16,256]{1,0:T(8,128)S(1)}, u32[]{:S(2)}, u32[]{:S(2)}) collective-permute-start(f32[16,256]{1,0:T(8,128)S(1)} %get-tuple-element.56), channel_id=1, source_target_pairs={{0,4},{4,0},{8,12},{12,8},{16,20},{20,16},{24,28},{28,24},{1,5},{5... | collective-permute-start | bytes 49160 | tf_op jit(solution)/shard_map/ppermute | solution.py:463
  29.7 1.1 %collective-permute-start.10 = (f32[4,32,512]{2,1,0:T(8,128)S(1)}, f32[4,32,512]{2,1,0:T(8,128)S(1)}, u32[]{:S(2)}, u32[]{:S(2)}) collective-permute-start(f32[4,32,512]{2,1,0:T(8,128)S(1)} %pad_maximum_fusion.refs_2_.t_same), channel_id=1, source_target_pairs={{0,4},{4,0},{8,12},{12,8},{16,20},{20,16},{24,28},{28,24},{1,5},{5... | collective-permute-start | bytes 786440 | tf_op jit(solution)/shard_map/ppermute | solution.py:463
  30.8 0.2 collective-permute-done.13
  30.9 1.5 %collective-permute-done.11 = f32[16,256]{1,0:T(8,128)S(1)} collective-permute-done((f32[16,256]{1,0:T(8,128)S(1)}, f32[16,256]{1,0:T(8,128)S(1)}, u32[]{:S(2)}, u32[]{:S(2)}) %collective-permute-start.11) | collective-permute-done | bytes 16416 | tf_op jit(solution)/shard_map/ppermute | solution.py:463
  32.5 2.5 %collective-permute-start.14 = (f32[16,256]{1,0:T(8,128)S(1)}, f32[16,256]{1,0:T(8,128)S(1)}, u32[]{:S(2)}, u32[]{:S(2)}) collective-permute-start(f32[16,256]{1,0:T(8,128)S(1)} %add_add_fusion), channel_id=1, source_target_pairs={{0,16},{4,20},{8,24},{12,28},{16,0},{20,4},{24,8},{28,12},{1,17},{... | collective-permute-start | bytes 49160 | tf_op jit(solution)/shard_map/ppermute | solution.py:463
  34.9 2.3 %collective-permute-done.14 = f32[16,256]{1,0:T(8,128)S(1)} collective-permute-done((f32[16,256]{1,0:T(8,128)S(1)}, f32[16,256]{1,0:T(8,128)S(1)}, u32[]{:S(2)}, u32[]{:S(2)}) %collective-permute-start.14) | collective-permute-done | bytes 16416 | tf_op jit(solution)/shard_map/ppermute | solution.py:463
  37.2 3.0 %first.1 = (f32[32,512]{1,0:T(8,128)S(1)}, f32[32,512]{1,0:T(8,128)S(1)}, f32[2,32,512]{2,1,0:T(8,128)S(1)}, f32[8,512]{1,0:T(8,128)S(1)}) custom-call(bf16[32,4,256,256]{3,2,1,0:T(8,128)(2,1)S(1)} %get-tuple-element.52.k_mat, s32[1,128]{1,0:T(1,128)S(1)} %get-tuple-element.53.refs_0_.list_v, s32[1,128]{1,0:T(1,128)S(1)} %get-tuple-element.54.refs_1_.list_v, ...), custom_call_target="tpu_custom_call" | custom-call | flops 536870912 | bytes 8388608 | tf_op jit(solution)/shard_map/first/pallas_call | solution.py:605
  40.3 1.3 %collective-permute-done.15.got = f32[2,32,512]{2,1,0:T(8,128)S(1)} collective-permute-done((f32[2,32,512]{2,1,0:T(8,128)S(1)}, f32[2,32,512]{2,1,0:T(8,128)S(1)}, u32[]{:S(2)}, u32[]{:S(2)}) %collective-permute-start.15) | collective-permute-done | bytes 131104 | tf_op jit(solution)/shard_map/ppermute | solution.py:463
  41.7 1.4 %collective-permute-start.16 = (bf16[112,512]{1,0:T(8,128)(2,1)S(1)}, bf16[112,512]{1,0:T(8,128)(2,1)S(1)}, u32[]{:S(2)}, u32[]{:S(2)}) collective-permute-start(bf16[112,512]{1,0:T(8,128)(2,1)S(1)} %get-tuple-element.63), channel_id=1, source_target_pairs={{0,2},{1,3},{2,0},{3,1},{4,6},{5,7},{6,4},{7,5},{8,10},{9,11},{10,... | collective-permute-start | bytes 344072 | tf_op jit(solution)/shard_map/ppermute | solution.py:463
  43.1 3.8 %collective-permute-done.16.far = bf16[112,512]{1,0:T(8,128)(2,1)S(1)} collective-permute-done((bf16[112,512]{1,0:T(8,128)(2,1)S(1)}, bf16[112,512]{1,0:T(8,128)(2,1)S(1)}, u32[]{:S(2)}, u32[]{:S(2)}) %collective-permute-start.16) | collective-permute-done | bytes 114720 | tf_op jit(solution)/shard_map/ppermute | solution.py:463
  47.1 2.7 %collective-permute-start.19 = (bf16[32,512]{1,0:T(8,128)(2,1)S(1)}, bf16[32,512]{1,0:T(8,128)(2,1)S(1)}, u32[]{:S(2)}, u32[]{:S(2)}) collective-permute-start(bf16[32,512]{1,0:T(8,128)(2,1)S(1)} %get-tuple-element.66), channel_id=1, source_target_pairs={{0,16},{4,20},{8,24},{12,28},{16,0},{20,4},{24,8},{28,12},{1,17},{... | collective-permute-start | bytes 98312 | tf_op jit(solution)/shard_map/ppermute | solution.py:463
  49.8 1.6 %second.3 = bf16[4,32,512]{2,1,0:T(8,128)(2,1)S(1)} custom-call(bf16[32,4,256,256]{3,2,1,0:T(8,128)(2,1)S(1)} %get-tuple-element.52.k_mat, s32[1,128]{1,0:T(1,128)S(1)} %get-tuple-element.54.refs_1_.list_v, f32[32,2048]{1,0:T(8,128)S(1)} %copy-done, f32[2,40,512]{2,1,0:T(8,128)S(1)} %get-tuple-element.64.s1_own, f32[2,40,512]{2,1,0:T(8,128)S(1)} %collective-permute-done.17.s1_got), custom_call_target="tpu_custom_call" | custom-call | flops 268435456 | bytes 4194304 | tf_op jit(solution)/shard_map/second/pallas_call | solution.py:643
  51.4 1.3 %collective-permute-start.18 = (bf16[4,32,512]{2,1,0:T(8,128)(2,1)S(1)}, bf16[4,32,512]{2,1,0:T(8,128)(2,1)S(1)}, u32[]{:S(2)}, u32[]{:S(2)}) collective-permute-start(bf16[4,32,512]{2,1,0:T(8,128)(2,1)S(1)} %second.3), channel_id=1, source_target_pairs={{0,4},{4,0},{8,12},{12,8},{16,20},{20,16},{24,28},{28,24},{1,5},{5... | collective-permute-start | bytes 393224 | tf_op jit(solution)/shard_map/ppermute | solution.py:463
  52.8 1.4 %collective-permute-start.20 = (bf16[2,32,512]{2,1,0:T(8,128)(2,1)S(1)}, bf16[2,32,512]{2,1,0:T(8,128)(2,1)S(1)}, u32[]{:S(2)}, u32[]{:S(2)}) collective-permute-start(bf16[2,32,512]{2,1,0:T(8,128)(2,1)S(1)} %pad_maximum_fusion.3.refs_0_), channel_id=1, source_target_pairs={{0,8},{4,12},{8,0},{12,4},{16,24},{20,28},{24,16},{28,20},{1,9},{5... | collective-permute-start | bytes 196616 | tf_op jit(solution)/shard_map/ppermute | solution.py:463
  54.2 1.4 %second.2.z_same = f32[4,32,512]{2,1,0:T(8,128)S(1)} custom-call(bf16[32,4,256,256]{3,2,1,0:T(8,128)(2,1)S(1)} %get-tuple-element.52.k_mat, s32[1,128]{1,0:T(1,128)S(1)} %get-tuple-element.53.refs_0_.list_v, f32[32,2048]{1,0:T(8,128)S(1)} %copy-done, f32[2,40,512]{2,1,0:T(8,128)S(1)} %get-tuple-element.64.s1_own, ...), custom_call_target="tpu_custom_call" | custom-call | flops 268435456 | bytes 4194304 | tf_op jit(solution)/shard_map/second/pallas_call | solution.py:643
  55.6 1.5 %collective-permute-done.20.refs_1_ = bf16[2,32,512]{2,1,0:T(8,128)(2,1)S(1)} collective-permute-done((bf16[2,32,512]{2,1,0:T(8,128)(2,1)S(1)}, bf16[2,32,512]{2,1,0:T(8,128)(2,1)S(1)}, u32[]{:S(2)}, u32[]{:S(2)}) %collective-permute-start.20) | collective-permute-done | bytes 65568 | tf_op jit(solution)/shard_map/ppermute | solution.py:463
  57.1 0.2 meet.1
  57.3 3.2 %collective-permute-start.21 = (bf16[32,640]{1,0:T(8,128)(2,1)S(1)}, bf16[32,640]{1,0:T(8,128)(2,1)S(1)}, u32[]{:S(2)}, u32[]{:S(2)}) collective-permute-start(bf16[32,640]{1,0:T(8,128)(2,1)S(1)} %get-tuple-element.73), channel_id=1, source_target_pairs={{0,24},{4,28},{8,16},{12,20},{16,8},{20,12},{24,0},{28,4},{1,25},{... | collective-permute-start | bytes 122888 | tf_op jit(solution)/shard_map/ppermute | solution.py:463
  60.4 1.3 %collective-permute-start.23 = (bf16[32,640]{1,0:T(8,128)(2,1)S(1)}, bf16[32,640]{1,0:T(8,128)(2,1)S(1)}, u32[]{:S(2)}, u32[]{:S(2)}) collective-permute-start(bf16[32,640]{1,0:T(8,128)(2,1)S(1)} %get-tuple-element.75), channel_id=1, source_target_pairs={{0,8},{4,12},{8,0},{12,4},{16,24},{20,28},{24,16},{28,20},{1,9},{5... | collective-permute-start | bytes 122888 | tf_op jit(solution)/shard_map/ppermute | solution.py:463
  61.7 1.5 %collective-permute-done.21.refs_0_ = bf16[32,640]{1,0:T(8,128)(2,1)S(1)} collective-permute-done((bf16[32,640]{1,0:T(8,128)(2,1)S(1)}, bf16[32,640]{1,0:T(8,128)(2,1)S(1)}, u32[]{:S(2)}, u32[]{:S(2)}) %collective-permute-start.21) | collective-permute-done | bytes 40992 | tf_op jit(solution)/shard_map/ppermute | solution.py:463
  63.2 2.1 %collective-permute-done.22.refs_1_ = bf16[32,640]{1,0:T(8,128)(2,1)S(1)} collective-permute-done((bf16[32,640]{1,0:T(8,128)(2,1)S(1)}, bf16[32,640]{1,0:T(8,128)(2,1)S(1)}, u32[]{:S(2)}, u32[]{:S(2)}) %collective-permute-start.22) | collective-permute-done | bytes 40992 | tf_op jit(solution)/shard_map/ppermute | solution.py:463
  65.3 0.1 products.1
  65.4 1.1 %collective-permute-start.25 = (f32[32,640]{1,0:T(8,128)S(1)}, f32[32,640]{1,0:T(8,128)S(1)}, u32[]{:S(2)}, u32[]{:S(2)}) collective-permute-start(f32[32,640]{1,0:T(8,128)S(1)} %get-tuple-element.76), channel_id=1, source_target_pairs={{0,2},{1,3},{2,0},{3,1},{4,6},{5,7},{6,4},{7,5},{8,10},{9,11},{10,... | collective-permute-start | bytes 245768 | tf_op jit(solution)/shard_map/ppermute | solution.py:463
  66.6 1.8 %collective-permute-start.26 = (f32[32,128]{1,0:T(8,128)S(1)}, f32[32,128]{1,0:T(8,128)S(1)}, u32[]{:S(2)}, u32[]{:S(2)}) collective-permute-start(f32[32,128]{1,0:T(8,128)S(1)} %get-tuple-element.77), channel_id=1, source_target_pairs={{0,6},{1,7},{2,4},{3,5},{4,2},{5,3},{6,0},{7,1},{8,14},{9,15},{10,... | collective-permute-start | bytes 49160 | tf_op jit(solution)/shard_map/ppermute | solution.py:473
  68.4 0.6 collective-permute-start.24
  68.9 2.3 %collective-permute-done.26 = f32[32,128]{1,0:T(8,128)S(1)} collective-permute-done((f32[32,128]{1,0:T(8,128)S(1)}, f32[32,128]{1,0:T(8,128)S(1)}, u32[]{:S(2)}, u32[]{:S(2)}) %collective-permute-start.26) | collective-permute-done | bytes 16416 | tf_op jit(solution)/shard_map/ppermute | solution.py:473
  71.2 0.9 %collective-permute-done.24 = f32[32,128]{1,0:T(8,128)S(1)} collective-permute-done((f32[32,128]{1,0:T(8,128)S(1)}, f32[32,128]{1,0:T(8,128)S(1)}, u32[]{:S(2)}, u32[]{:S(2)}) %collective-permute-start.24) | collective-permute-done | bytes 16416 | tf_op jit(solution)/shard_map/ppermute | solution.py:463
  72.2 1.4 %collective-permute-done.27.refs_1_ = f32[2,32,640]{2,1,0:T(8,128)S(1)} collective-permute-done((f32[2,32,640]{2,1,0:T(8,128)S(1)}, f32[2,32,640]{2,1,0:T(8,128)S(1)}, u32[]{:S(2)}, u32[]{:S(2)}) %collective-permute-start.27) | collective-permute-done | bytes 163872 | tf_op jit(solution)/shard_map/ppermute | solution.py:463
  73.6 1.2 %final.1 = (f32[32,2048]{1,0:T(8,128)}, f32[32,2048]{1,0:T(8,128)}) custom-call(f32[32,2048]{1,0:T(8,128)S(1)} %copy-done, f32[2,40,512]{2,1,0:T(8,128)S(1)} %get-tuple-element.64.s1_own, f32[2,40,512]{2,1,0:T(8,128)S(1)} %collective-permute-done.17.s1_got, f32[2,32,640]{2,1,0:T(8,128)S(1)} %pad_maximum_fusion.1.refs_0_, ...), custom_call_target="tpu_custom_call" | custom-call | tf_op jit(solution)/shard_map/final/pallas_call | solution.py:706
  (44 shorter events, 0.8 us)
Async XLA Ops:
  0.6 5.7 %collective-permute-start = (s32[8,6]{1,0:T(8,128)}, s32[8,6]{1,0:T(8,128)S(1)}, u32[]{:S(2)}, u32[]{:S(2)}) collective-permute-start(s32[8,6]{1,0:T(8,128)} %param.3), channel_id=1, source_target_pairs={{0,1},{1,0},{2,3},{3,2},{4,5},{5,4},{6,7},{7,6},{8,9},{9,8},{10,11... | collective-permute-start | bytes 584 | tf_op jit(solution)/shard_map/ppermute | solution.py:463
  1.1 5.3 %collective-permute-start.2 = (s32[8,6]{1,0:T(8,128)}, s32[8,6]{1,0:T(8,128)S(1)}, u32[]{:S(2)}, u32[]{:S(2)}) collective-permute-start(s32[8,6]{1,0:T(8,128)} %param.3), channel_id=1, source_target_pairs={{0,3},{1,2},{2,1},{3,0},{4,7},{5,6},{6,5},{7,4},{8,11},{9,10},{10,... | collective-permute-start | bytes 584 | tf_op jit(solution)/shard_map/ppermute | solution.py:463
  3.8 3.8 %collective-permute-start.1 = (s32[8,6]{1,0:T(8,128)}, s32[8,6]{1,0:T(8,128)S(1)}, u32[]{:S(2)}, u32[]{:S(2)}) collective-permute-start(s32[8,6]{1,0:T(8,128)} %param.3), channel_id=1, source_target_pairs={{0,2},{1,3},{2,0},{3,1},{4,6},{5,7},{6,4},{7,5},{8,10},{9,11},{10,... | collective-permute-start | bytes 584 | tf_op jit(solution)/shard_map/ppermute | solution.py:463
  7.9 8.1 %collective-permute-start.5 = (bf16[16,640]{1,0:T(8,128)(2,1)S(1)}, bf16[16,640]{1,0:T(8,128)(2,1)S(1)}, u32[]{:S(2)}, u32[]{:S(2)}) collective-permute-start(bf16[16,640]{1,0:T(8,128)(2,1)S(1)} %pad_maximum_fusion.4), channel_id=1, source_target_pairs={{0,24},{4,28},{8,16},{12,20},{16,8},{20,12},{24,0},{28,4},{1,25},{... | collective-permute-start | bytes 61448 | tf_op jit(solution)/shard_map/ppermute | solution.py:463
  11.6 5.2 %collective-permute-start.4 = (bf16[16,640]{1,0:T(8,128)(2,1)S(1)}, bf16[16,640]{1,0:T(8,128)(2,1)S(1)}, u32[]{:S(2)}, u32[]{:S(2)}) collective-permute-start(bf16[16,640]{1,0:T(8,128)(2,1)S(1)} %pad_maximum_fusion.4), channel_id=1, source_target_pairs={{0,16},{4,20},{8,24},{12,28},{16,0},{20,4},{24,8},{28,12},{1,17},{... | collective-permute-start | bytes 61448 | tf_op jit(solution)/shard_map/ppermute | solution.py:463
  11.6 5.2 %collective-permute-start.3 = (bf16[16,640]{1,0:T(8,128)(2,1)S(1)}, bf16[16,640]{1,0:T(8,128)(2,1)S(1)}, u32[]{:S(2)}, u32[]{:S(2)}) collective-permute-start(bf16[16,640]{1,0:T(8,128)(2,1)S(1)} %pad_maximum_fusion.4), channel_id=1, source_target_pairs={{0,8},{4,12},{8,0},{12,4},{16,24},{20,28},{24,16},{28,20},{1,9},{5... | collective-permute-start | bytes 61448 | tf_op jit(solution)/shard_map/ppermute | solution.py:463
  12.3 9.8 %collective-permute-start.9 = (f32[32,512]{1,0:T(8,128)S(1)}, f32[32,512]{1,0:T(8,128)S(1)}, u32[]{:S(2)}, u32[]{:S(2)}) collective-permute-start(f32[32,512]{1,0:T(8,128)S(1)} %constant_dynamic-slice_fusion.t_ref), channel_id=1, source_target_pairs={{0,24},{4,28},{8,16},{12,20},{16,8},{20,12},{24,0},{28,4},{1,25},{... | collective-permute-start | bytes 196616 | tf_op jit(solution)/shard_map/ppermute | solution.py:463
  15.9 6.2 %collective-permute-start.8 = (f32[32,512]{1,0:T(8,128)S(1)}, f32[32,512]{1,0:T(8,128)S(1)}, u32[]{:S(2)}, u32[]{:S(2)}) collective-permute-start(f32[32,512]{1,0:T(8,128)S(1)} %constant_dynamic-slice_fusion.t_ref), channel_id=1, source_target_pairs={{0,16},{4,20},{8,24},{12,28},{16,0},{20,4},{24,8},{28,12},{1,17},{... | collective-permute-start | bytes 196616 | tf_op jit(solution)/shard_map/ppermute | solution.py:463
  15.9 6.2 %collective-permute-start.7 = (f32[32,512]{1,0:T(8,128)S(1)}, f32[32,512]{1,0:T(8,128)S(1)}, u32[]{:S(2)}, u32[]{:S(2)}) collective-permute-start(f32[32,512]{1,0:T(8,128)S(1)} %constant_dynamic-slice_fusion.t_ref), channel_id=1, source_target_pairs={{0,8},{4,12},{8,0},{12,4},{16,24},{20,28},{24,16},{28,20},{1,9},{5... | collective-permute-start | bytes 196616 | tf_op jit(solution)/shard_map/ppermute | solution.py:463
  16.8 5.4 %collective-permute-start.6 = (bf16[4,16,640]{2,1,0:T(8,128)(2,1)S(1)}, bf16[4,16,640]{2,1,0:T(8,128)(2,1)S(1)}, u32[]{:S(2)}, u32[]{:S(2)}) collective-permute-start(bf16[4,16,640]{2,1,0:T(8,128)(2,1)S(1)} %pad_maximum_fusion.2.refs_1_), channel_id=1, source_target_pairs={{0,4},{4,0},{8,12},{12,8},{16,20},{20,16},{24,28},{28,24},{1,5},{5... | collective-permute-start | bytes 245768 | tf_op jit(solution)/shard_map/ppermute | solution.py:463
  26.1 23.7 %copy-start = (f32[32,2048]{1,0:T(8,128)S(1)}, f32[32,2048]{1,0:T(8,128)}, u32[]{:S(2)}) copy-start(f32[32,2048]{1,0:T(8,128)} %t_ref.5) | copy-start | bytes 786436
  26.1 4.8 %collective-permute-start.13 = (f32[16,256]{1,0:T(8,128)S(1)}, f32[16,256]{1,0:T(8,128)S(1)}, u32[]{:S(2)}, u32[]{:S(2)}) collective-permute-start(f32[16,256]{1,0:T(8,128)S(1)} %get-tuple-element.56), channel_id=1, source_target_pairs={{0,12},{4,8},{8,4},{12,0},{16,28},{20,24},{24,20},{28,16},{1,13},{... | collective-permute-start | bytes 49160 | tf_op jit(solution)/shard_map/ppermute | solution.py:463
  26.4 4.6 %collective-permute-start.12 = (f32[16,256]{1,0:T(8,128)S(1)}, f32[16,256]{1,0:T(8,128)S(1)}, u32[]{:S(2)}, u32[]{:S(2)}) collective-permute-start(f32[16,256]{1,0:T(8,128)S(1)} %get-tuple-element.56), channel_id=1, source_target_pairs={{0,8},{4,12},{8,0},{12,4},{16,24},{20,28},{24,16},{28,20},{1,9},{5... | collective-permute-start | bytes 49160 | tf_op jit(solution)/shard_map/ppermute | solution.py:463
  28.7 3.7 %collective-permute-start.11 = (f32[16,256]{1,0:T(8,128)S(1)}, f32[16,256]{1,0:T(8,128)S(1)}, u32[]{:S(2)}, u32[]{:S(2)}) collective-permute-start(f32[16,256]{1,0:T(8,128)S(1)} %get-tuple-element.56), channel_id=1, source_target_pairs={{0,4},{4,0},{8,12},{12,8},{16,20},{20,16},{24,28},{28,24},{1,5},{5... | collective-permute-start | bytes 49160 | tf_op jit(solution)/shard_map/ppermute | solution.py:463
  29.7 7.5 %collective-permute-start.10 = (f32[4,32,512]{2,1,0:T(8,128)S(1)}, f32[4,32,512]{2,1,0:T(8,128)S(1)}, u32[]{:S(2)}, u32[]{:S(2)}) collective-permute-start(f32[4,32,512]{2,1,0:T(8,128)S(1)} %pad_maximum_fusion.refs_2_.t_same), channel_id=1, source_target_pairs={{0,4},{4,0},{8,12},{12,8},{16,20},{20,16},{24,28},{28,24},{1,5},{5... | collective-permute-start | bytes 786440 | tf_op jit(solution)/shard_map/ppermute | solution.py:463
  32.5 4.7 %collective-permute-start.14 = (f32[16,256]{1,0:T(8,128)S(1)}, f32[16,256]{1,0:T(8,128)S(1)}, u32[]{:S(2)}, u32[]{:S(2)}) collective-permute-start(f32[16,256]{1,0:T(8,128)S(1)} %add_add_fusion), channel_id=1, source_target_pairs={{0,16},{4,20},{8,24},{12,28},{16,0},{20,4},{24,8},{28,12},{1,17},{... | collective-permute-start | bytes 49160 | tf_op jit(solution)/shard_map/ppermute | solution.py:463
  40.3 1.4 %collective-permute-start.15 = (f32[2,32,512]{2,1,0:T(8,128)S(1)}, f32[2,32,512]{2,1,0:T(8,128)S(1)}, u32[]{:S(2)}, u32[]{:S(2)}) collective-permute-start(f32[2,32,512]{2,1,0:T(8,128)S(1)} %get-tuple-element.59), channel_id=1, source_target_pairs={{0,1},{1,0},{2,3},{3,2},{4,5},{5,4},{6,7},{7,6},{8,9},{9,8},{10,11... | collective-permute-start | bytes 393224 | tf_op jit(solution)/shard_map/ppermute | solution.py:463
  41.7 5.3 %collective-permute-start.16 = (bf16[112,512]{1,0:T(8,128)(2,1)S(1)}, bf16[112,512]{1,0:T(8,128)(2,1)S(1)}, u32[]{:S(2)}, u32[]{:S(2)}) collective-permute-start(bf16[112,512]{1,0:T(8,128)(2,1)S(1)} %get-tuple-element.63), channel_id=1, source_target_pairs={{0,2},{1,3},{2,0},{3,1},{4,6},{5,7},{6,4},{7,5},{8,10},{9,11},{10,... | collective-permute-start | bytes 344072 | tf_op jit(solution)/shard_map/ppermute | solution.py:463
  47.0 2.8 %collective-permute-start.17 = (f32[2,40,512]{2,1,0:T(8,128)S(1)}, f32[2,40,512]{2,1,0:T(8,128)S(1)}, u32[]{:S(2)}, u32[]{:S(2)}) collective-permute-start(f32[2,40,512]{2,1,0:T(8,128)S(1)} %get-tuple-element.64.s1_own), channel_id=1, source_target_pairs={{0,1},{1,0},{2,3},{3,2},{4,5},{5,4},{6,7},{7,6},{8,9},{9,8},{10,11... | collective-permute-start | bytes 491528 | tf_op jit(solution)/shard_map/ppermute | solution.py:463
  47.1 5.6 %collective-permute-start.19 = (bf16[32,512]{1,0:T(8,128)(2,1)S(1)}, bf16[32,512]{1,0:T(8,128)(2,1)S(1)}, u32[]{:S(2)}, u32[]{:S(2)}) collective-permute-start(bf16[32,512]{1,0:T(8,128)(2,1)S(1)} %get-tuple-element.66), channel_id=1, source_target_pairs={{0,16},{4,20},{8,24},{12,28},{16,0},{20,4},{24,8},{28,12},{1,17},{... | collective-permute-start | bytes 98312 | tf_op jit(solution)/shard_map/ppermute | solution.py:463
  51.4 5.6 %collective-permute-start.18 = (bf16[4,32,512]{2,1,0:T(8,128)(2,1)S(1)}, bf16[4,32,512]{2,1,0:T(8,128)(2,1)S(1)}, u32[]{:S(2)}, u32[]{:S(2)}) collective-permute-start(bf16[4,32,512]{2,1,0:T(8,128)(2,1)S(1)} %second.3), channel_id=1, source_target_pairs={{0,4},{4,0},{8,12},{12,8},{16,20},{20,16},{24,28},{28,24},{1,5},{5... | collective-permute-start | bytes 393224 | tf_op jit(solution)/shard_map/ppermute | solution.py:463
  52.8 4.3 %collective-permute-start.20 = (bf16[2,32,512]{2,1,0:T(8,128)(2,1)S(1)}, bf16[2,32,512]{2,1,0:T(8,128)(2,1)S(1)}, u32[]{:S(2)}, u32[]{:S(2)}) collective-permute-start(bf16[2,32,512]{2,1,0:T(8,128)(2,1)S(1)} %pad_maximum_fusion.3.refs_0_), channel_id=1, source_target_pairs={{0,8},{4,12},{8,0},{12,4},{16,24},{20,28},{24,16},{28,20},{1,9},{5... | collective-permute-start | bytes 196616 | tf_op jit(solution)/shard_map/ppermute | solution.py:463
  57.3 6.0 %collective-permute-start.21 = (bf16[32,640]{1,0:T(8,128)(2,1)S(1)}, bf16[32,640]{1,0:T(8,128)(2,1)S(1)}, u32[]{:S(2)}, u32[]{:S(2)}) collective-permute-start(bf16[32,640]{1,0:T(8,128)(2,1)S(1)} %get-tuple-element.73), channel_id=1, source_target_pairs={{0,24},{4,28},{8,16},{12,20},{16,8},{20,12},{24,0},{28,4},{1,25},{... | collective-permute-start | bytes 122888 | tf_op jit(solution)/shard_map/ppermute | solution.py:463
  60.4 4.9 %collective-permute-start.22 = (bf16[32,640]{1,0:T(8,128)(2,1)S(1)}, bf16[32,640]{1,0:T(8,128)(2,1)S(1)}, u32[]{:S(2)}, u32[]{:S(2)}) collective-permute-start(bf16[32,640]{1,0:T(8,128)(2,1)S(1)} %get-tuple-element.74), channel_id=1, source_target_pairs={{0,16},{4,20},{8,24},{12,28},{16,0},{20,4},{24,8},{28,12},{1,17},{... | collective-permute-start | bytes 122888 | tf_op jit(solution)/shard_map/ppermute | solution.py:463
  60.4 4.9 %collective-permute-start.23 = (bf16[32,640]{1,0:T(8,128)(2,1)S(1)}, bf16[32,640]{1,0:T(8,128)(2,1)S(1)}, u32[]{:S(2)}, u32[]{:S(2)}) collective-permute-start(bf16[32,640]{1,0:T(8,128)(2,1)S(1)} %get-tuple-element.75), channel_id=1, source_target_pairs={{0,8},{4,12},{8,0},{12,4},{16,24},{20,28},{24,16},{28,20},{1,9},{5... | collective-permute-start | bytes 122888 | tf_op jit(solution)/shard_map/ppermute | solution.py:463
  65.4 6.7 %collective-permute-start.25 = (f32[32,640]{1,0:T(8,128)S(1)}, f32[32,640]{1,0:T(8,128)S(1)}, u32[]{:S(2)}, u32[]{:S(2)}) collective-permute-start(f32[32,640]{1,0:T(8,128)S(1)} %get-tuple-element.76), channel_id=1, source_target_pairs={{0,2},{1,3},{2,0},{3,1},{4,6},{5,7},{6,4},{7,5},{8,10},{9,11},{10,... | collective-permute-start | bytes 245768 | tf_op jit(solution)/shard_map/ppermute | solution.py:463
  66.6 4.6 %collective-permute-start.26 = (f32[32,128]{1,0:T(8,128)S(1)}, f32[32,128]{1,0:T(8,128)S(1)}, u32[]{:S(2)}, u32[]{:S(2)}) collective-permute-start(f32[32,128]{1,0:T(8,128)S(1)} %get-tuple-element.77), channel_id=1, source_target_pairs={{0,6},{1,7},{2,4},{3,5},{4,2},{5,3},{6,0},{7,1},{8,14},{9,15},{10,... | collective-permute-start | bytes 49160 | tf_op jit(solution)/shard_map/ppermute | solution.py:473
  68.4 3.7 %collective-permute-start.24 = (f32[32,128]{1,0:T(8,128)S(1)}, f32[32,128]{1,0:T(8,128)S(1)}, u32[]{:S(2)}, u32[]{:S(2)}) collective-permute-start(f32[32,128]{1,0:T(8,128)S(1)} %get-tuple-element.77), channel_id=1, source_target_pairs={{0,4},{4,0},{8,12},{12,8},{16,20},{20,16},{24,28},{28,24},{1,5},{5... | collective-permute-start | bytes 49160 | tf_op jit(solution)/shard_map/ppermute | solution.py:463
  72.2 1.5 %collective-permute-start.27 = (f32[2,32,640]{2,1,0:T(8,128)S(1)}, f32[2,32,640]{2,1,0:T(8,128)S(1)}, u32[]{:S(2)}, u32[]{:S(2)}) collective-permute-start(f32[2,32,640]{2,1,0:T(8,128)S(1)} %pad_maximum_fusion.1.refs_0_), channel_id=1, source_target_pairs={{0,1},{1,0},{2,3},{3,2},{4,5},{5,4},{6,7},{7,6},{8,9},{9,8},{10,11... | collective-permute-start | bytes 491528 | tf_op jit(solution)/shard_map/ppermute | solution.py:463

commit v20 on v19

--- a/solution.py
+++ b/solution.py
@@ -10,7 +10,7 @@
 
 REG = 1.5
 RADIUS = 0.25
-GROUP_BITS = 2
+GROUP_BITS = 1
 GROUP = 1 << GROUP_BITS
 CODE_BITS = 12
 CODE = 1 << CODE_BITS

time: 75.2 us -> 76.9 us (1.023)
  Pallas kernels: 15.2 us -> 17.7 us
  waiting for transfers between devices: 19.8 us -> 19 us
    pallas_call x2, Pallas kernels: 7.69 us -> 8.51 us  [build(): pl.pallas_call(functools.partial(build_kernel, cfg, part), out_shape=out,...]
    pallas_call x1, Pallas kernels: 3.05 us -> 3.86 us  [local(): pl.pallas_call(functools.partial(first_kernel, cfg), out_shape=[shape(out...]
    pallas_call x2, Pallas kernels: 2.99 us -> 3.79 us  [second(): pl.pallas_call(functools.partial(second_kernel, cfg, part), out_shape=sha...]
  transfers between devices with their start and end apart: 28 -> 28, of which waited for: 12 -> 14; matrix products, arithmetic and copies ran while one was open for 4% -> 4% of each run, Pallas kernels for 9% -> 11%
where the time goes in v20:
time: 76.9 us; the launch traced here: 77.1 us
  starting transfers between devices  36.4 us (47%)
  waiting for transfers between devices  19 us (25%)
  Pallas kernels  17.7 us (23%)
  local copies, waits for them, and re-layouts  2.74 us (4%)
  between operations  0.84 us (1%)
    ppermute x27, starting transfers between devices, swap(): return lax.ppermute(x, axis, [(i, i ^ d) for i in range(size)])  34.2 us
    ppermute x27, waiting for transfers between devices, swap(): return lax.ppermute(x, axis, [(i, i ^ d) for i in range(size)])  17.5 us
    pallas_call x2, Pallas kernels, build(): pl.pallas_call(functools.partial(build_kernel, cfg, part), out_shape=out,...  8.51 us
    pallas_call x1, Pallas kernels, local(): pl.pallas_call(functools.partial(first_kernel, cfg), out_shape=[shape(out...  3.86 us
    pallas_call x2, Pallas kernels, second(): pl.pallas_call(functools.partial(second_kernel, cfg, part), out_shape=sha...  3.79 us
    ppermute x1, starting transfers between devices, both_swap(): return lax.ppermute(x, ('rows', 'cols'), pairs)  2.24 us
    dynamic_slice x2, local copies, waits for them, and re-layouts, own(): return lax.dynamic_slice_in_dim(x, col * own_len, own_len, 1)  1.56 us
    ppermute x1, waiting for transfers between devices, both_swap(): return lax.ppermute(x, ('rows', 'cols'), pairs)  1.56 us
  transfers between devices with their start and end apart: 28, of which 14 were waited for; matrix products, arithmetic and copies ran while one was open for 4% of the time, Pallas kernels for 11%

profile of v20, /device:TPU:0, one launch (start us, length us, event | category | flops | bytes accessed | tf_op | source)
XLA Modules:
  0.0 77.1 jit_solution(14921552352351848694)
XLA Ops:
  0.6 0.5 collective-permute-start
  1.1 2.6 %collective-permute-start.2 = (s32[8,6]{1,0:T(8,128)}, s32[8,6]{1,0:T(8,128)S(1)}, u32[]{:S(2)}, u32[]{:S(2)}) collective-permute-start(s32[8,6]{1,0:T(8,128)} %param.3), channel_id=1, source_target_pairs={{0,3},{1,2},{2,1},{3,0},{4,7},{5,6},{6,5},{7,4},{8,11},{9,10},{10,... | collective-permute-start | bytes 584 | tf_op jit(solution)/shard_map/ppermute | solution.py:463
  3.8 0.8 %copy.6 = s32[8,6]{0,1:T(8,128)S(1)} copy(s32[8,6]{1,0:T(8,128)} %param.3) | data formatting | bytes 384 | tf_op args[0]
  4.7 0.7 constant_dynamic-slice_fusion.1
  5.5 0.8 %constant_dynamic-slice_fusion.t_ref = f32[32,512]{1,0:T(8,128)S(1)} fusion(f32[32,2048]{1,0:T(8,128)} %t_ref.5, s32[]{:T(128)S(6)} %select_n.7), kind=kLoop, calls=%fused_computation.21 | loop fusion | bytes 131076 | tf_op jit(solution)/shard_map/dynamic_slice | solution.py:524
  6.5 0.1 copy.9
  6.6 1.0 %collective-permute-done.1 = s32[8,6]{1,0:T(8,128)S(1)} collective-permute-done((s32[8,6]{1,0:T(8,128)}, s32[8,6]{1,0:T(8,128)S(1)}, u32[]{:S(2)}, u32[]{:S(2)}) %collective-permute-start.1) | collective-permute-done | bytes 224 | tf_op jit(solution)/shard_map/ppermute | solution.py:463
  7.8 0.1 reshape.14
  7.9 3.7 %collective-permute-start.5 = (bf16[16,640]{1,0:T(8,128)(2,1)S(1)}, bf16[16,640]{1,0:T(8,128)(2,1)S(1)}, u32[]{:S(2)}, u32[]{:S(2)}) collective-permute-start(bf16[16,640]{1,0:T(8,128)(2,1)S(1)} %pad_maximum_fusion.4), channel_id=1, source_target_pairs={{0,24},{4,28},{8,16},{12,20},{16,8},{20,12},{24,0},{28,4},{1,25},{... | collective-permute-start | bytes 61448 | tf_op jit(solution)/shard_map/ppermute | solution.py:463
  11.6 0.8 %collective-permute-start.3 = (bf16[16,640]{1,0:T(8,128)(2,1)S(1)}, bf16[16,640]{1,0:T(8,128)(2,1)S(1)}, u32[]{:S(2)}, u32[]{:S(2)}) collective-permute-start(bf16[16,640]{1,0:T(8,128)(2,1)S(1)} %pad_maximum_fusion.4), channel_id=1, source_target_pairs={{0,8},{4,12},{8,0},{12,4},{16,24},{20,28},{24,16},{28,20},{1,9},{5... | collective-permute-start | bytes 61448 | tf_op jit(solution)/shard_map/ppermute | solution.py:463
  12.3 3.6 %collective-permute-start.9 = (f32[32,512]{1,0:T(8,128)S(1)}, f32[32,512]{1,0:T(8,128)S(1)}, u32[]{:S(2)}, u32[]{:S(2)}) collective-permute-start(f32[32,512]{1,0:T(8,128)S(1)} %constant_dynamic-slice_fusion.t_ref), channel_id=1, source_target_pairs={{0,24},{4,28},{8,16},{12,20},{16,8},{20,12},{24,0},{28,4},{1,25},{... | collective-permute-start | bytes 196616 | tf_op jit(solution)/shard_map/ppermute | solution.py:463
  15.9 0.8 %collective-permute-start.7 = (f32[32,512]{1,0:T(8,128)S(1)}, f32[32,512]{1,0:T(8,128)S(1)}, u32[]{:S(2)}, u32[]{:S(2)}) collective-permute-start(f32[32,512]{1,0:T(8,128)S(1)} %constant_dynamic-slice_fusion.t_ref), channel_id=1, source_target_pairs={{0,8},{4,12},{8,0},{12,4},{16,24},{20,28},{24,16},{28,20},{1,9},{5... | collective-permute-start | bytes 196616 | tf_op jit(solution)/shard_map/ppermute | solution.py:463
  16.8 1.6 %collective-permute-start.6 = (bf16[4,16,640]{2,1,0:T(8,128)(2,1)S(1)}, bf16[4,16,640]{2,1,0:T(8,128)(2,1)S(1)}, u32[]{:S(2)}, u32[]{:S(2)}) collective-permute-start(bf16[4,16,640]{2,1,0:T(8,128)(2,1)S(1)} %pad_maximum_fusion.2.refs_1_), channel_id=1, source_target_pairs={{0,4},{4,0},{8,12},{12,8},{16,20},{20,16},{24,28},{28,24},{1,5},{5... | collective-permute-start | bytes 245768 | tf_op jit(solution)/shard_map/ppermute | solution.py:463
  18.3 4.3 %build.2 = (bf16[64,2,256,256]{3,2,1,0:T(8,128)(2,1)S(1)}, s32[1,128]{1,0:T(1,128)S(1)}, f32[8,256]{1,0:T(8,128)S(1)}, bf16[8,256,32]{2,1,0:T(8,128)(2,1)S(1)}) custom-call(s32[8,64]{1,0:T(8,128)S(1)} %add_add_fusion.1.direct_v, bf16[16,2048]{1,0:T(8,128)(2,1)} %refs_0_.1, bf16[4,16,640]{2,1,0:T(8,128)(2,1)S(1)} %pad_maximum_fusion.2.refs_1_), custom_call_target="tpu_custom_call" | custom-call | flops 2684354560 | bytes 83886080 | tf_op jit(solution)/shard_map/build/pallas_call | solution.py:549
  22.7 4.2 %build.3 = (bf16[64,2,256,256]{3,2,1,0:T(8,128)(2,1)S(1)}, s32[1,128]{1,0:T(1,128)S(1)}, f32[16,256]{1,0:T(8,128)S(1)}) custom-call(s32[8,64]{1,0:T(8,128)S(1)} %add_add_fusion.1.direct_v, bf16[8,256,32]{2,1,0:T(8,128)(2,1)S(1)} %get-tuple-element.41.refs_0_, f32[8,256]{1,0:T(8,128)S(1)} %get-tuple-element.44.refs_1_, ...), custom_call_target="tpu_custom_call", output_to_operand_aliasing={{0}: (4, {})} | custom-call | flops 2684354560 | bytes 83886080 | tf_op jit(solution)/shard_map/build/pallas_call | solution.py:549
  26.9 1.6 %collective-permute-start.13 = (f32[16,256]{1,0:T(8,128)S(1)}, f32[16,256]{1,0:T(8,128)S(1)}, u32[]{:S(2)}, u32[]{:S(2)}) collective-permute-start(f32[16,256]{1,0:T(8,128)S(1)} %get-tuple-element.56), channel_id=1, source_target_pairs={{0,12},{4,8},{8,4},{12,0},{16,28},{20,24},{24,20},{28,16},{1,13},{... | collective-permute-start | bytes 49160 | tf_op jit(solution)/shard_map/ppermute | solution.py:463
  28.5 1.1 %collective-permute-start.12 = (f32[16,256]{1,0:T(8,128)S(1)}, f32[16,256]{1,0:T(8,128)S(1)}, u32[]{:S(2)}, u32[]{:S(2)}) collective-permute-start(f32[16,256]{1,0:T(8,128)S(1)} %get-tuple-element.56), channel_id=1, source_target_pairs={{0,8},{4,12},{8,0},{12,4},{16,24},{20,28},{24,16},{28,20},{1,9},{5... | collective-permute-start | bytes 49160 | tf_op jit(solution)/shard_map/ppermute | solution.py:463
  29.6 0.8 %collective-permute-start.11 = (f32[16,256]{1,0:T(8,128)S(1)}, f32[16,256]{1,0:T(8,128)S(1)}, u32[]{:S(2)}, u32[]{:S(2)}) collective-permute-start(f32[16,256]{1,0:T(8,128)S(1)} %get-tuple-element.56), channel_id=1, source_target_pairs={{0,4},{4,0},{8,12},{12,8},{16,20},{20,16},{24,28},{28,24},{1,5},{5... | collective-permute-start | bytes 49160 | tf_op jit(solution)/shard_map/ppermute | solution.py:463
  30.5 1.2 %collective-permute-start.10 = (f32[4,32,512]{2,1,0:T(8,128)S(1)}, f32[4,32,512]{2,1,0:T(8,128)S(1)}, u32[]{:S(2)}, u32[]{:S(2)}) collective-permute-start(f32[4,32,512]{2,1,0:T(8,128)S(1)} %pad_maximum_fusion.refs_2_.t_same), channel_id=1, source_target_pairs={{0,4},{4,0},{8,12},{12,8},{16,20},{20,16},{24,28},{28,24},{1,5},{5... | collective-permute-start | bytes 786440 | tf_op jit(solution)/shard_map/ppermute | solution.py:463
  31.7 0.5 collective-permute-done.12
  32.3 1.3 %collective-permute-done.11 = f32[16,256]{1,0:T(8,128)S(1)} collective-permute-done((f32[16,256]{1,0:T(8,128)S(1)}, f32[16,256]{1,0:T(8,128)S(1)}, u32[]{:S(2)}, u32[]{:S(2)}) %collective-permute-start.11) | collective-permute-done | bytes 16416 | tf_op jit(solution)/shard_map/ppermute | solution.py:463
  33.6 2.4 %collective-permute-start.14 = (f32[16,256]{1,0:T(8,128)S(1)}, f32[16,256]{1,0:T(8,128)S(1)}, u32[]{:S(2)}, u32[]{:S(2)}) collective-permute-start(f32[16,256]{1,0:T(8,128)S(1)} %add_add_fusion), channel_id=1, source_target_pairs={{0,16},{4,20},{8,24},{12,28},{16,0},{20,4},{24,8},{28,12},{1,17},{... | collective-permute-start | bytes 49160 | tf_op jit(solution)/shard_map/ppermute | solution.py:463
  36.0 2.3 %collective-permute-done.14 = f32[16,256]{1,0:T(8,128)S(1)} collective-permute-done((f32[16,256]{1,0:T(8,128)S(1)}, f32[16,256]{1,0:T(8,128)S(1)}, u32[]{:S(2)}, u32[]{:S(2)}) %collective-permute-start.14) | collective-permute-done | bytes 16416 | tf_op jit(solution)/shard_map/ppermute | solution.py:463
  38.4 3.9 %first.1 = (f32[32,512]{1,0:T(8,128)S(1)}, f32[32,512]{1,0:T(8,128)S(1)}, f32[2,32,512]{2,1,0:T(8,128)S(1)}, f32[8,512]{1,0:T(8,128)S(1)}) custom-call(bf16[64,2,256,256]{3,2,1,0:T(8,128)(2,1)S(1)} %get-tuple-element.52.k_mat, s32[1,128]{1,0:T(1,128)S(1)} %get-tuple-element.53.refs_0_.list_v, s32[1,128]{1,0:T(1,128)S(1)} %get-tuple-element.54.refs_1_.list_v, ...), custom_call_target="tpu_custom_call" | custom-call | flops 536870912 | bytes 8388608 | tf_op jit(solution)/shard_map/first/pallas_call | solution.py:605
  42.3 1.3 %collective-permute-done.15.got = f32[2,32,512]{2,1,0:T(8,128)S(1)} collective-permute-done((f32[2,32,512]{2,1,0:T(8,128)S(1)}, f32[2,32,512]{2,1,0:T(8,128)S(1)}, u32[]{:S(2)}, u32[]{:S(2)}) %collective-permute-start.15) | collective-permute-done | bytes 131104 | tf_op jit(solution)/shard_map/ppermute | solution.py:463
  43.7 1.1 %collective-permute-start.16 = (bf16[112,512]{1,0:T(8,128)(2,1)S(1)}, bf16[112,512]{1,0:T(8,128)(2,1)S(1)}, u32[]{:S(2)}, u32[]{:S(2)}) collective-permute-start(bf16[112,512]{1,0:T(8,128)(2,1)S(1)} %get-tuple-element.63), channel_id=1, source_target_pairs={{0,2},{1,3},{2,0},{3,1},{4,6},{5,7},{6,4},{7,5},{8,10},{9,11},{10,... | collective-permute-start | bytes 344072 | tf_op jit(solution)/shard_map/ppermute | solution.py:463
  44.7 4.2 %collective-permute-done.16.far = bf16[112,512]{1,0:T(8,128)(2,1)S(1)} collective-permute-done((bf16[112,512]{1,0:T(8,128)(2,1)S(1)}, bf16[112,512]{1,0:T(8,128)(2,1)S(1)}, u32[]{:S(2)}, u32[]{:S(2)}) %collective-permute-start.16) | collective-permute-done | bytes 114720 | tf_op jit(solution)/shard_map/ppermute | solution.py:463
  49.1 2.6 %collective-permute-start.19 = (bf16[32,512]{1,0:T(8,128)(2,1)S(1)}, bf16[32,512]{1,0:T(8,128)(2,1)S(1)}, u32[]{:S(2)}, u32[]{:S(2)}) collective-permute-start(bf16[32,512]{1,0:T(8,128)(2,1)S(1)} %get-tuple-element.66), channel_id=1, source_target_pairs={{0,16},{4,20},{8,24},{12,28},{16,0},{20,4},{24,8},{28,12},{1,17},{... | collective-permute-start | bytes 98312 | tf_op jit(solution)/shard_map/ppermute | solution.py:463
  51.7 2.0 %second.3 = bf16[4,32,512]{2,1,0:T(8,128)(2,1)S(1)} custom-call(bf16[64,2,256,256]{3,2,1,0:T(8,128)(2,1)S(1)} %get-tuple-element.52.k_mat, s32[1,128]{1,0:T(1,128)S(1)} %get-tuple-element.54.refs_1_.list_v, f32[32,2048]{1,0:T(8,128)S(1)} %copy-done, f32[2,40,512]{2,1,0:T(8,128)S(1)} %get-tuple-element.64.s1_own, f32[2,40,512]{2,1,0:T(8,128)S(1)} %collective-permute-done.17.s1_got), custom_call_target="tpu_custom_call" | custom-call | flops 268435456 | bytes 4194304 | tf_op jit(solution)/shard_map/second/pallas_call | solution.py:643
  53.6 1.6 %collective-permute-start.18 = (bf16[4,32,512]{2,1,0:T(8,128)(2,1)S(1)}, bf16[4,32,512]{2,1,0:T(8,128)(2,1)S(1)}, u32[]{:S(2)}, u32[]{:S(2)}) collective-permute-start(bf16[4,32,512]{2,1,0:T(8,128)(2,1)S(1)} %second.3), channel_id=1, source_target_pairs={{0,4},{4,0},{8,12},{12,8},{16,20},{20,16},{24,28},{28,24},{1,5},{5... | collective-permute-start | bytes 393224 | tf_op jit(solution)/shard_map/ppermute | solution.py:463
  55.3 2.2 %collective-permute-start.20 = (bf16[2,32,512]{2,1,0:T(8,128)(2,1)S(1)}, bf16[2,32,512]{2,1,0:T(8,128)(2,1)S(1)}, u32[]{:S(2)}, u32[]{:S(2)}) collective-permute-start(bf16[2,32,512]{2,1,0:T(8,128)(2,1)S(1)} %pad_maximum_fusion.3.refs_0_), channel_id=1, source_target_pairs={{0,8},{4,12},{8,0},{12,4},{16,24},{20,28},{24,16},{28,20},{1,9},{5... | collective-permute-start | bytes 196616 | tf_op jit(solution)/shard_map/ppermute | solution.py:463
  57.5 1.8 %second.2.z_same = f32[4,32,512]{2,1,0:T(8,128)S(1)} custom-call(bf16[64,2,256,256]{3,2,1,0:T(8,128)(2,1)S(1)} %get-tuple-element.52.k_mat, s32[1,128]{1,0:T(1,128)S(1)} %get-tuple-element.53.refs_0_.list_v, f32[32,2048]{1,0:T(8,128)S(1)} %copy-done, f32[2,40,512]{2,1,0:T(8,128)S(1)} %get-tuple-element.64.s1_own, ...), custom_call_target="tpu_custom_call" | custom-call | flops 268435456 | bytes 4194304 | tf_op jit(solution)/shard_map/second/pallas_call | solution.py:643
  59.4 0.4 collective-permute-done.20.refs_1_
  59.8 0.2 meet.1
  60.0 2.7 %collective-permute-start.21 = (bf16[32,640]{1,0:T(8,128)(2,1)S(1)}, bf16[32,640]{1,0:T(8,128)(2,1)S(1)}, u32[]{:S(2)}, u32[]{:S(2)}) collective-permute-start(bf16[32,640]{1,0:T(8,128)(2,1)S(1)} %get-tuple-element.73), channel_id=1, source_target_pairs={{0,24},{4,28},{8,16},{12,20},{16,8},{20,12},{24,0},{28,4},{1,25},{... | collective-permute-start | bytes 122888 | tf_op jit(solution)/shard_map/ppermute | solution.py:463
  62.7 0.9 %collective-permute-start.22 = (bf16[32,640]{1,0:T(8,128)(2,1)S(1)}, bf16[32,640]{1,0:T(8,128)(2,1)S(1)}, u32[]{:S(2)}, u32[]{:S(2)}) collective-permute-start(bf16[32,640]{1,0:T(8,128)(2,1)S(1)} %get-tuple-element.74), channel_id=1, source_target_pairs={{0,16},{4,20},{8,24},{12,28},{16,0},{20,4},{24,8},{28,12},{1,17},{... | collective-permute-start | bytes 122888 | tf_op jit(solution)/shard_map/ppermute | solution.py:463
  63.5 0.9 %collective-permute-start.23 = (bf16[32,640]{1,0:T(8,128)(2,1)S(1)}, bf16[32,640]{1,0:T(8,128)(2,1)S(1)}, u32[]{:S(2)}, u32[]{:S(2)}) collective-permute-start(bf16[32,640]{1,0:T(8,128)(2,1)S(1)} %get-tuple-element.75), channel_id=1, source_target_pairs={{0,8},{4,12},{8,0},{12,4},{16,24},{20,28},{24,16},{28,20},{1,9},{5... | collective-permute-start | bytes 122888 | tf_op jit(solution)/shard_map/ppermute | solution.py:463
  64.4 1.6 %collective-permute-done.21.refs_0_ = bf16[32,640]{1,0:T(8,128)(2,1)S(1)} collective-permute-done((bf16[32,640]{1,0:T(8,128)(2,1)S(1)}, bf16[32,640]{1,0:T(8,128)(2,1)S(1)}, u32[]{:S(2)}, u32[]{:S(2)}) %collective-permute-start.21) | collective-permute-done | bytes 40992 | tf_op jit(solution)/shard_map/ppermute | solution.py:463
  66.0 1.7 %collective-permute-done.22.refs_1_ = bf16[32,640]{1,0:T(8,128)(2,1)S(1)} collective-permute-done((bf16[32,640]{1,0:T(8,128)(2,1)S(1)}, bf16[32,640]{1,0:T(8,128)(2,1)S(1)}, u32[]{:S(2)}, u32[]{:S(2)}) %collective-permute-start.22) | collective-permute-done | bytes 40992 | tf_op jit(solution)/shard_map/ppermute | solution.py:463
  67.7 0.3 collective-permute-done.23.refs_2_
  68.0 0.1 products.1
  68.1 0.4 collective-permute-start.25
  68.5 2.2 %collective-permute-start.26 = (f32[32,128]{1,0:T(8,128)S(1)}, f32[32,128]{1,0:T(8,128)S(1)}, u32[]{:S(2)}, u32[]{:S(2)}) collective-permute-start(f32[32,128]{1,0:T(8,128)S(1)} %get-tuple-element.77), channel_id=1, source_target_pairs={{0,6},{1,7},{2,4},{3,5},{4,2},{5,3},{6,0},{7,1},{8,14},{9,15},{10,... | collective-permute-start | bytes 49160 | tf_op jit(solution)/shard_map/ppermute | solution.py:473
  70.7 0.8 %collective-permute-start.24 = (f32[32,128]{1,0:T(8,128)S(1)}, f32[32,128]{1,0:T(8,128)S(1)}, u32[]{:S(2)}, u32[]{:S(2)}) collective-permute-start(f32[32,128]{1,0:T(8,128)S(1)} %get-tuple-element.77), channel_id=1, source_target_pairs={{0,4},{4,0},{8,12},{12,8},{16,20},{20,16},{24,28},{28,24},{1,5},{5... | collective-permute-start | bytes 49160 | tf_op jit(solution)/shard_map/ppermute | solution.py:463
  71.6 1.6 %collective-permute-done.26 = f32[32,128]{1,0:T(8,128)S(1)} collective-permute-done((f32[32,128]{1,0:T(8,128)S(1)}, f32[32,128]{1,0:T(8,128)S(1)}, u32[]{:S(2)}, u32[]{:S(2)}) %collective-permute-start.26) | collective-permute-done | bytes 16416 | tf_op jit(solution)/shard_map/ppermute | solution.py:473
  73.1 1.3 %collective-permute-done.24 = f32[32,128]{1,0:T(8,128)S(1)} collective-permute-done((f32[32,128]{1,0:T(8,128)S(1)}, f32[32,128]{1,0:T(8,128)S(1)}, u32[]{:S(2)}, u32[]{:S(2)}) %collective-permute-start.24) | collective-permute-done | bytes 16416 | tf_op jit(solution)/shard_map/ppermute | solution.py:463
  74.6 1.4 %collective-permute-done.27.refs_1_ = f32[2,32,640]{2,1,0:T(8,128)S(1)} collective-permute-done((f32[2,32,640]{2,1,0:T(8,128)S(1)}, f32[2,32,640]{2,1,0:T(8,128)S(1)}, u32[]{:S(2)}, u32[]{:S(2)}) %collective-permute-start.27) | collective-permute-done | bytes 163872 | tf_op jit(solution)/shard_map/ppermute | solution.py:463
  76.0 1.2 %final.1 = (f32[32,2048]{1,0:T(8,128)}, f32[32,2048]{1,0:T(8,128)}) custom-call(f32[32,2048]{1,0:T(8,128)S(1)} %copy-done, f32[2,40,512]{2,1,0:T(8,128)S(1)} %get-tuple-element.64.s1_own, f32[2,40,512]{2,1,0:T(8,128)S(1)} %collective-permute-done.17.s1_got, f32[2,32,640]{2,1,0:T(8,128)S(1)} %pad_maximum_fusion.1.refs_0_, ...), custom_call_target="tpu_custom_call" | custom-call | tf_op jit(solution)/shard_map/final/pallas_call | solution.py:706
  (44 shorter events, 1.1 us)
Async XLA Ops:
  0.6 5.7 %collective-permute-start = (s32[8,6]{1,0:T(8,128)}, s32[8,6]{1,0:T(8,128)S(1)}, u32[]{:S(2)}, u32[]{:S(2)}) collective-permute-start(s32[8,6]{1,0:T(8,128)} %param.3), channel_id=1, source_target_pairs={{0,1},{1,0},{2,3},{3,2},{4,5},{5,4},{6,7},{7,6},{8,9},{9,8},{10,11... | collective-permute-start | bytes 584 | tf_op jit(solution)/shard_map/ppermute | solution.py:463
  1.1 5.3 %collective-permute-start.2 = (s32[8,6]{1,0:T(8,128)}, s32[8,6]{1,0:T(8,128)S(1)}, u32[]{:S(2)}, u32[]{:S(2)}) collective-permute-start(s32[8,6]{1,0:T(8,128)} %param.3), channel_id=1, source_target_pairs={{0,3},{1,2},{2,1},{3,0},{4,7},{5,6},{6,5},{7,4},{8,11},{9,10},{10,... | collective-permute-start | bytes 584 | tf_op jit(solution)/shard_map/ppermute | solution.py:463
  3.8 3.8 %collective-permute-start.1 = (s32[8,6]{1,0:T(8,128)}, s32[8,6]{1,0:T(8,128)S(1)}, u32[]{:S(2)}, u32[]{:S(2)}) collective-permute-start(s32[8,6]{1,0:T(8,128)} %param.3), channel_id=1, source_target_pairs={{0,2},{1,3},{2,0},{3,1},{4,6},{5,7},{6,4},{7,5},{8,10},{9,11},{10,... | collective-permute-start | bytes 584 | tf_op jit(solution)/shard_map/ppermute | solution.py:463
  7.9 8.1 %collective-permute-start.5 = (bf16[16,640]{1,0:T(8,128)(2,1)S(1)}, bf16[16,640]{1,0:T(8,128)(2,1)S(1)}, u32[]{:S(2)}, u32[]{:S(2)}) collective-permute-start(bf16[16,640]{1,0:T(8,128)(2,1)S(1)} %pad_maximum_fusion.4), channel_id=1, source_target_pairs={{0,24},{4,28},{8,16},{12,20},{16,8},{20,12},{24,0},{28,4},{1,25},{... | collective-permute-start | bytes 61448 | tf_op jit(solution)/shard_map/ppermute | solution.py:463
  11.6 5.2 %collective-permute-start.4 = (bf16[16,640]{1,0:T(8,128)(2,1)S(1)}, bf16[16,640]{1,0:T(8,128)(2,1)S(1)}, u32[]{:S(2)}, u32[]{:S(2)}) collective-permute-start(bf16[16,640]{1,0:T(8,128)(2,1)S(1)} %pad_maximum_fusion.4), channel_id=1, source_target_pairs={{0,16},{4,20},{8,24},{12,28},{16,0},{20,4},{24,8},{28,12},{1,17},{... | collective-permute-start | bytes 61448 | tf_op jit(solution)/shard_map/ppermute | solution.py:463
  11.6 5.2 %collective-permute-start.3 = (bf16[16,640]{1,0:T(8,128)(2,1)S(1)}, bf16[16,640]{1,0:T(8,128)(2,1)S(1)}, u32[]{:S(2)}, u32[]{:S(2)}) collective-permute-start(bf16[16,640]{1,0:T(8,128)(2,1)S(1)} %pad_maximum_fusion.4), channel_id=1, source_target_pairs={{0,8},{4,12},{8,0},{12,4},{16,24},{20,28},{24,16},{28,20},{1,9},{5... | collective-permute-start | bytes 61448 | tf_op jit(solution)/shard_map/ppermute | solution.py:463
  12.3 10.3 %collective-permute-start.9 = (f32[32,512]{1,0:T(8,128)S(1)}, f32[32,512]{1,0:T(8,128)S(1)}, u32[]{:S(2)}, u32[]{:S(2)}) collective-permute-start(f32[32,512]{1,0:T(8,128)S(1)} %constant_dynamic-slice_fusion.t_ref), channel_id=1, source_target_pairs={{0,24},{4,28},{8,16},{12,20},{16,8},{20,12},{24,0},{28,4},{1,25},{... | collective-permute-start | bytes 196616 | tf_op jit(solution)/shard_map/ppermute | solution.py:463
  15.9 6.7 %collective-permute-start.8 = (f32[32,512]{1,0:T(8,128)S(1)}, f32[32,512]{1,0:T(8,128)S(1)}, u32[]{:S(2)}, u32[]{:S(2)}) collective-permute-start(f32[32,512]{1,0:T(8,128)S(1)} %constant_dynamic-slice_fusion.t_ref), channel_id=1, source_target_pairs={{0,16},{4,20},{8,24},{12,28},{16,0},{20,4},{24,8},{28,12},{1,17},{... | collective-permute-start | bytes 196616 | tf_op jit(solution)/shard_map/ppermute | solution.py:463
  15.9 6.7 %collective-permute-start.7 = (f32[32,512]{1,0:T(8,128)S(1)}, f32[32,512]{1,0:T(8,128)S(1)}, u32[]{:S(2)}, u32[]{:S(2)}) collective-permute-start(f32[32,512]{1,0:T(8,128)S(1)} %constant_dynamic-slice_fusion.t_ref), channel_id=1, source_target_pairs={{0,8},{4,12},{8,0},{12,4},{16,24},{20,28},{24,16},{28,20},{1,9},{5... | collective-permute-start | bytes 196616 | tf_op jit(solution)/shard_map/ppermute | solution.py:463
  16.8 5.9 %collective-permute-start.6 = (bf16[4,16,640]{2,1,0:T(8,128)(2,1)S(1)}, bf16[4,16,640]{2,1,0:T(8,128)(2,1)S(1)}, u32[]{:S(2)}, u32[]{:S(2)}) collective-permute-start(bf16[4,16,640]{2,1,0:T(8,128)(2,1)S(1)} %pad_maximum_fusion.2.refs_1_), channel_id=1, source_target_pairs={{0,4},{4,0},{8,12},{12,8},{16,20},{20,16},{24,28},{28,24},{1,5},{5... | collective-permute-start | bytes 245768 | tf_op jit(solution)/shard_map/ppermute | solution.py:463
  26.9 24.7 %copy-start = (f32[32,2048]{1,0:T(8,128)S(1)}, f32[32,2048]{1,0:T(8,128)}, u32[]{:S(2)}) copy-start(f32[32,2048]{1,0:T(8,128)} %t_ref.5) | copy-start | bytes 786436
  26.9 4.8 %collective-permute-start.13 = (f32[16,256]{1,0:T(8,128)S(1)}, f32[16,256]{1,0:T(8,128)S(1)}, u32[]{:S(2)}, u32[]{:S(2)}) collective-permute-start(f32[16,256]{1,0:T(8,128)S(1)} %get-tuple-element.56), channel_id=1, source_target_pairs={{0,12},{4,8},{8,4},{12,0},{16,28},{20,24},{24,20},{28,16},{1,13},{... | collective-permute-start | bytes 49160 | tf_op jit(solution)/shard_map/ppermute | solution.py:463
  28.5 3.7 %collective-permute-start.12 = (f32[16,256]{1,0:T(8,128)S(1)}, f32[16,256]{1,0:T(8,128)S(1)}, u32[]{:S(2)}, u32[]{:S(2)}) collective-permute-start(f32[16,256]{1,0:T(8,128)S(1)} %get-tuple-element.56), channel_id=1, source_target_pairs={{0,8},{4,12},{8,0},{12,4},{16,24},{20,28},{24,16},{28,20},{1,9},{5... | collective-permute-start | bytes 49160 | tf_op jit(solution)/shard_map/ppermute | solution.py:463
  29.6 4.0 %collective-permute-start.11 = (f32[16,256]{1,0:T(8,128)S(1)}, f32[16,256]{1,0:T(8,128)S(1)}, u32[]{:S(2)}, u32[]{:S(2)}) collective-permute-start(f32[16,256]{1,0:T(8,128)S(1)} %get-tuple-element.56), channel_id=1, source_target_pairs={{0,4},{4,0},{8,12},{12,8},{16,20},{20,16},{24,28},{28,24},{1,5},{5... | collective-permute-start | bytes 49160 | tf_op jit(solution)/shard_map/ppermute | solution.py:463
  30.5 7.9 %collective-permute-start.10 = (f32[4,32,512]{2,1,0:T(8,128)S(1)}, f32[4,32,512]{2,1,0:T(8,128)S(1)}, u32[]{:S(2)}, u32[]{:S(2)}) collective-permute-start(f32[4,32,512]{2,1,0:T(8,128)S(1)} %pad_maximum_fusion.refs_2_.t_same), channel_id=1, source_target_pairs={{0,4},{4,0},{8,12},{12,8},{16,20},{20,16},{24,28},{28,24},{1,5},{5... | collective-permute-start | bytes 786440 | tf_op jit(solution)/shard_map/ppermute | solution.py:463
  33.6 4.7 %collective-permute-start.14 = (f32[16,256]{1,0:T(8,128)S(1)}, f32[16,256]{1,0:T(8,128)S(1)}, u32[]{:S(2)}, u32[]{:S(2)}) collective-permute-start(f32[16,256]{1,0:T(8,128)S(1)} %add_add_fusion), channel_id=1, source_target_pairs={{0,16},{4,20},{8,24},{12,28},{16,0},{20,4},{24,8},{28,12},{1,17},{... | collective-permute-start | bytes 49160 | tf_op jit(solution)/shard_map/ppermute | solution.py:463
  42.2 1.4 %collective-permute-start.15 = (f32[2,32,512]{2,1,0:T(8,128)S(1)}, f32[2,32,512]{2,1,0:T(8,128)S(1)}, u32[]{:S(2)}, u32[]{:S(2)}) collective-permute-start(f32[2,32,512]{2,1,0:T(8,128)S(1)} %get-tuple-element.59), channel_id=1, source_target_pairs={{0,1},{1,0},{2,3},{3,2},{4,5},{5,4},{6,7},{7,6},{8,9},{9,8},{10,11... | collective-permute-start | bytes 393224 | tf_op jit(solution)/shard_map/ppermute | solution.py:463
  43.7 5.3 %collective-permute-start.16 = (bf16[112,512]{1,0:T(8,128)(2,1)S(1)}, bf16[112,512]{1,0:T(8,128)(2,1)S(1)}, u32[]{:S(2)}, u32[]{:S(2)}) collective-permute-start(bf16[112,512]{1,0:T(8,128)(2,1)S(1)} %get-tuple-element.63), channel_id=1, source_target_pairs={{0,2},{1,3},{2,0},{3,1},{4,6},{5,7},{6,4},{7,5},{8,10},{9,11},{10,... | collective-permute-start | bytes 344072 | tf_op jit(solution)/shard_map/ppermute | solution.py:463
  49.0 2.7 %collective-permute-start.17 = (f32[2,40,512]{2,1,0:T(8,128)S(1)}, f32[2,40,512]{2,1,0:T(8,128)S(1)}, u32[]{:S(2)}, u32[]{:S(2)}) collective-permute-start(f32[2,40,512]{2,1,0:T(8,128)S(1)} %get-tuple-element.64.s1_own), channel_id=1, source_target_pairs={{0,1},{1,0},{2,3},{3,2},{4,5},{5,4},{6,7},{7,6},{8,9},{9,8},{10,11... | collective-permute-start | bytes 491528 | tf_op jit(solution)/shard_map/ppermute | solution.py:463
  49.1 6.2 %collective-permute-start.19 = (bf16[32,512]{1,0:T(8,128)(2,1)S(1)}, bf16[32,512]{1,0:T(8,128)(2,1)S(1)}, u32[]{:S(2)}, u32[]{:S(2)}) collective-permute-start(bf16[32,512]{1,0:T(8,128)(2,1)S(1)} %get-tuple-element.66), channel_id=1, source_target_pairs={{0,16},{4,20},{8,24},{12,28},{16,0},{20,4},{24,8},{28,12},{1,17},{... | collective-permute-start | bytes 98312 | tf_op jit(solution)/shard_map/ppermute | solution.py:463
  53.6 6.1 %collective-permute-start.18 = (bf16[4,32,512]{2,1,0:T(8,128)(2,1)S(1)}, bf16[4,32,512]{2,1,0:T(8,128)(2,1)S(1)}, u32[]{:S(2)}, u32[]{:S(2)}) collective-permute-start(bf16[4,32,512]{2,1,0:T(8,128)(2,1)S(1)} %second.3), channel_id=1, source_target_pairs={{0,4},{4,0},{8,12},{12,8},{16,20},{20,16},{24,28},{28,24},{1,5},{5... | collective-permute-start | bytes 393224 | tf_op jit(solution)/shard_map/ppermute | solution.py:463
  55.3 4.5 %collective-permute-start.20 = (bf16[2,32,512]{2,1,0:T(8,128)(2,1)S(1)}, bf16[2,32,512]{2,1,0:T(8,128)(2,1)S(1)}, u32[]{:S(2)}, u32[]{:S(2)}) collective-permute-start(bf16[2,32,512]{2,1,0:T(8,128)(2,1)S(1)} %pad_maximum_fusion.3.refs_0_), channel_id=1, source_target_pairs={{0,8},{4,12},{8,0},{12,4},{16,24},{20,28},{24,16},{28,20},{1,9},{5... | collective-permute-start | bytes 196616 | tf_op jit(solution)/shard_map/ppermute | solution.py:463
  60.0 6.0 %collective-permute-start.21 = (bf16[32,640]{1,0:T(8,128)(2,1)S(1)}, bf16[32,640]{1,0:T(8,128)(2,1)S(1)}, u32[]{:S(2)}, u32[]{:S(2)}) collective-permute-start(bf16[32,640]{1,0:T(8,128)(2,1)S(1)} %get-tuple-element.73), channel_id=1, source_target_pairs={{0,24},{4,28},{8,16},{12,20},{16,8},{20,12},{24,0},{28,4},{1,25},{... | collective-permute-start | bytes 122888 | tf_op jit(solution)/shard_map/ppermute | solution.py:463
  62.7 5.0 %collective-permute-start.22 = (bf16[32,640]{1,0:T(8,128)(2,1)S(1)}, bf16[32,640]{1,0:T(8,128)(2,1)S(1)}, u32[]{:S(2)}, u32[]{:S(2)}) collective-permute-start(bf16[32,640]{1,0:T(8,128)(2,1)S(1)} %get-tuple-element.74), channel_id=1, source_target_pairs={{0,16},{4,20},{8,24},{12,28},{16,0},{20,4},{24,8},{28,12},{1,17},{... | collective-permute-start | bytes 122888 | tf_op jit(solution)/shard_map/ppermute | solution.py:463
  63.5 4.4 %collective-permute-start.23 = (bf16[32,640]{1,0:T(8,128)(2,1)S(1)}, bf16[32,640]{1,0:T(8,128)(2,1)S(1)}, u32[]{:S(2)}, u32[]{:S(2)}) collective-permute-start(bf16[32,640]{1,0:T(8,128)(2,1)S(1)} %get-tuple-element.75), channel_id=1, source_target_pairs={{0,8},{4,12},{8,0},{12,4},{16,24},{20,28},{24,16},{28,20},{1,9},{5... | collective-permute-start | bytes 122888 | tf_op jit(solution)/shard_map/ppermute | solution.py:463
  68.1 6.4 %collective-permute-start.25 = (f32[32,640]{1,0:T(8,128)S(1)}, f32[32,640]{1,0:T(8,128)S(1)}, u32[]{:S(2)}, u32[]{:S(2)}) collective-permute-start(f32[32,640]{1,0:T(8,128)S(1)} %get-tuple-element.76), channel_id=1, source_target_pairs={{0,2},{1,3},{2,0},{3,1},{4,6},{5,7},{6,4},{7,5},{8,10},{9,11},{10,... | collective-permute-start | bytes 245768 | tf_op jit(solution)/shard_map/ppermute | solution.py:463
  68.5 4.6 %collective-permute-start.26 = (f32[32,128]{1,0:T(8,128)S(1)}, f32[32,128]{1,0:T(8,128)S(1)}, u32[]{:S(2)}, u32[]{:S(2)}) collective-permute-start(f32[32,128]{1,0:T(8,128)S(1)} %get-tuple-element.77), channel_id=1, source_target_pairs={{0,6},{1,7},{2,4},{3,5},{4,2},{5,3},{6,0},{7,1},{8,14},{9,15},{10,... | collective-permute-start | bytes 49160 | tf_op jit(solution)/shard_map/ppermute | solution.py:473
  70.7 3.7 %collective-permute-start.24 = (f32[32,128]{1,0:T(8,128)S(1)}, f32[32,128]{1,0:T(8,128)S(1)}, u32[]{:S(2)}, u32[]{:S(2)}) collective-permute-start(f32[32,128]{1,0:T(8,128)S(1)} %get-tuple-element.77), channel_id=1, source_target_pairs={{0,4},{4,0},{8,12},{12,8},{16,20},{20,16},{24,28},{28,24},{1,5},{5... | collective-permute-start | bytes 49160 | tf_op jit(solution)/shard_map/ppermute | solution.py:463
  74.5 1.5 %collective-permute-start.27 = (f32[2,32,640]{2,1,0:T(8,128)S(1)}, f32[2,32,640]{2,1,0:T(8,128)S(1)}, u32[]{:S(2)}, u32[]{:S(2)}) collective-permute-start(f32[2,32,640]{2,1,0:T(8,128)S(1)} %pad_maximum_fusion.1.refs_0_), channel_id=1, source_target_pairs={{0,1},{1,0},{2,3},{3,2},{4,5},{5,4},{6,7},{7,6},{8,9},{9,8},{10,11... | collective-permute-start | bytes 491528 | tf_op jit(solution)/shard_map/ppermute | solution.py:463

commit v21 on v20

--- a/solution.py
+++ b/solution.py
@@ -10,7 +10,7 @@
 
 REG = 1.5
 RADIUS = 0.25
-GROUP_BITS = 1
+GROUP_BITS = 3
 GROUP = 1 << GROUP_BITS
 CODE_BITS = 12
 CODE = 1 << CODE_BITS

time: 76.9 us -> 75.4 us (0.980); the launches traced: 77.1 us -> 74.7 us
  starting transfers between devices: 36.4 us -> 35.1 us
  Pallas kernels: 17.7 us -> 16.7 us
    ppermute x1, starting transfers between devices: 2.24 us -> 1.42 us  [both_swap(): return lax.ppermute(x, ('rows', 'cols'), pairs)]
  transfers between devices with their start and end apart: 28 -> 28, of which waited for: 14 -> 14; matrix products, arithmetic and copies ran while one was open for 4% -> 4% of each run, Pallas kernels for 11% -> 10%
where the time goes in v21:
time: 75.4 us; the launch traced here: 74.7 us
  starting transfers between devices  35.1 us (47%)
  waiting for transfers between devices  19 us (25%)
  Pallas kernels  16.7 us (22%)
  local copies, waits for them, and re-layouts  2.74 us (4%)
  between operations  0.84 us (1%)
    ppermute x27, starting transfers between devices, swap(): return lax.ppermute(x, axis, [(i, i ^ d) for i in range(size)])  33.6 us
    ppermute x27, waiting for transfers between devices, swap(): return lax.ppermute(x, axis, [(i, i ^ d) for i in range(size)])  16.8 us
    pallas_call x2, Pallas kernels, build(): pl.pallas_call(functools.partial(build_kernel, cfg, part), out_shape=out,...  8.82 us
    pallas_call x1, Pallas kernels, local(): pl.pallas_call(functools.partial(first_kernel, cfg), out_shape=[shape(out...  3.32 us
    pallas_call x2, Pallas kernels, second(): pl.pallas_call(functools.partial(second_kernel, cfg, part), out_shape=sha...  3.05 us
    ppermute x1, waiting for transfers between devices, both_swap(): return lax.ppermute(x, ('rows', 'cols'), pairs)  2.19 us
    dynamic_slice x2, local copies, waits for them, and re-layouts, own(): return lax.dynamic_slice_in_dim(x, col * own_len, own_len, 1)  1.56 us
  transfers between devices with their start and end apart: 28, of which 14 were waited for; matrix products, arithmetic and copies ran while one was open for 4% of the time, Pallas kernels for 10%

profile of v21, /device:TPU:0, one launch (start us, length us, event | category | flops | bytes accessed | tf_op | source)
XLA Modules:
  0.0 74.7 jit_solution(5460140292682456172)
XLA Ops:
  0.6 0.5 collective-permute-start
  1.1 2.6 %collective-permute-start.2 = (s32[8,6]{1,0:T(8,128)}, s32[8,6]{1,0:T(8,128)S(1)}, u32[]{:S(2)}, u32[]{:S(2)}) collective-permute-start(s32[8,6]{1,0:T(8,128)} %param.3), channel_id=1, source_target_pairs={{0,3},{1,2},{2,1},{3,0},{4,7},{5,6},{6,5},{7,4},{8,11},{9,10},{10,... | collective-permute-start | bytes 584 | tf_op jit(solution)/shard_map/ppermute | solution.py:463
  3.8 0.8 %copy.6 = s32[8,6]{0,1:T(8,128)S(1)} copy(s32[8,6]{1,0:T(8,128)} %param.3) | data formatting | bytes 384 | tf_op args[0]
  4.7 0.7 constant_dynamic-slice_fusion.1
  5.5 0.8 %constant_dynamic-slice_fusion.t_ref = f32[32,512]{1,0:T(8,128)S(1)} fusion(f32[32,2048]{1,0:T(8,128)} %t_ref.5, s32[]{:T(128)S(6)} %select_n.7), kind=kLoop, calls=%fused_computation.21 | loop fusion | bytes 131076 | tf_op jit(solution)/shard_map/dynamic_slice | solution.py:524
  6.3 0.1 copy.7
  6.5 0.1 copy.9
  6.6 1.0 %collective-permute-done.1 = s32[8,6]{1,0:T(8,128)S(1)} collective-permute-done((s32[8,6]{1,0:T(8,128)}, s32[8,6]{1,0:T(8,128)S(1)}, u32[]{:S(2)}, u32[]{:S(2)}) %collective-permute-start.1) | collective-permute-done | bytes 224 | tf_op jit(solution)/shard_map/ppermute | solution.py:463
  7.6 0.1 copy.8
  7.8 0.1 reshape.14
  7.9 3.7 %collective-permute-start.5 = (bf16[16,640]{1,0:T(8,128)(2,1)S(1)}, bf16[16,640]{1,0:T(8,128)(2,1)S(1)}, u32[]{:S(2)}, u32[]{:S(2)}) collective-permute-start(bf16[16,640]{1,0:T(8,128)(2,1)S(1)} %pad_maximum_fusion.4), channel_id=1, source_target_pairs={{0,24},{4,28},{8,16},{12,20},{16,8},{20,12},{24,0},{28,4},{1,25},{... | collective-permute-start | bytes 61448 | tf_op jit(solution)/shard_map/ppermute | solution.py:463
  11.6 0.8 %collective-permute-start.3 = (bf16[16,640]{1,0:T(8,128)(2,1)S(1)}, bf16[16,640]{1,0:T(8,128)(2,1)S(1)}, u32[]{:S(2)}, u32[]{:S(2)}) collective-permute-start(bf16[16,640]{1,0:T(8,128)(2,1)S(1)} %pad_maximum_fusion.4), channel_id=1, source_target_pairs={{0,8},{4,12},{8,0},{12,4},{16,24},{20,28},{24,16},{28,20},{1,9},{5... | collective-permute-start | bytes 61448 | tf_op jit(solution)/shard_map/ppermute | solution.py:463
  12.3 3.6 %collective-permute-start.9 = (f32[32,512]{1,0:T(8,128)S(1)}, f32[32,512]{1,0:T(8,128)S(1)}, u32[]{:S(2)}, u32[]{:S(2)}) collective-permute-start(f32[32,512]{1,0:T(8,128)S(1)} %constant_dynamic-slice_fusion.t_ref), channel_id=1, source_target_pairs={{0,24},{4,28},{8,16},{12,20},{16,8},{20,12},{24,0},{28,4},{1,25},{... | collective-permute-start | bytes 196616 | tf_op jit(solution)/shard_map/ppermute | solution.py:463
  15.9 0.8 %collective-permute-start.7 = (f32[32,512]{1,0:T(8,128)S(1)}, f32[32,512]{1,0:T(8,128)S(1)}, u32[]{:S(2)}, u32[]{:S(2)}) collective-permute-start(f32[32,512]{1,0:T(8,128)S(1)} %constant_dynamic-slice_fusion.t_ref), channel_id=1, source_target_pairs={{0,8},{4,12},{8,0},{12,4},{16,24},{20,28},{24,16},{28,20},{1,9},{5... | collective-permute-start | bytes 196616 | tf_op jit(solution)/shard_map/ppermute | solution.py:463
  16.8 1.6 %collective-permute-start.6 = (bf16[4,16,640]{2,1,0:T(8,128)(2,1)S(1)}, bf16[4,16,640]{2,1,0:T(8,128)(2,1)S(1)}, u32[]{:S(2)}, u32[]{:S(2)}) collective-permute-start(bf16[4,16,640]{2,1,0:T(8,128)(2,1)S(1)} %pad_maximum_fusion.2.refs_1_), channel_id=1, source_target_pairs={{0,4},{4,0},{8,12},{12,8},{16,20},{20,16},{24,28},{28,24},{1,5},{5... | collective-permute-start | bytes 245768 | tf_op jit(solution)/shard_map/ppermute | solution.py:463
  18.3 4.6 %build.2 = (bf16[16,8,256,256]{3,2,1,0:T(8,128)(2,1)S(1)}, s32[1,128]{1,0:T(1,128)S(1)}, f32[8,256]{1,0:T(8,128)S(1)}, bf16[8,256,32]{2,1,0:T(8,128)(2,1)S(1)}) custom-call(s32[8,64]{1,0:T(8,128)S(1)} %add_add_fusion.1.direct_v, bf16[16,2048]{1,0:T(8,128)(2,1)} %refs_0_.1, bf16[4,16,640]{2,1,0:T(8,128)(2,1)S(1)} %pad_maximum_fusion.2.refs_1_), custom_call_target="tpu_custom_call" | custom-call | flops 2684354560 | bytes 83886080 | tf_op jit(solution)/shard_map/build/pallas_call | solution.py:549
  23.0 4.2 %build.3 = (bf16[16,8,256,256]{3,2,1,0:T(8,128)(2,1)S(1)}, s32[1,128]{1,0:T(1,128)S(1)}, f32[16,256]{1,0:T(8,128)S(1)}) custom-call(s32[8,64]{1,0:T(8,128)S(1)} %add_add_fusion.1.direct_v, bf16[8,256,32]{2,1,0:T(8,128)(2,1)S(1)} %get-tuple-element.41.refs_0_, f32[8,256]{1,0:T(8,128)S(1)} %get-tuple-element.44.refs_1_, ...), custom_call_target="tpu_custom_call", output_to_operand_aliasing={{0}: (4, {})} | custom-call | flops 2684354560 | bytes 83886080 | tf_op jit(solution)/shard_map/build/pallas_call | solution.py:549
  27.2 1.3 %collective-permute-start.13 = (f32[16,256]{1,0:T(8,128)S(1)}, f32[16,256]{1,0:T(8,128)S(1)}, u32[]{:S(2)}, u32[]{:S(2)}) collective-permute-start(f32[16,256]{1,0:T(8,128)S(1)} %get-tuple-element.56), channel_id=1, source_target_pairs={{0,12},{4,8},{8,4},{12,0},{16,28},{20,24},{24,20},{28,16},{1,13},{... | collective-permute-start | bytes 49160 | tf_op jit(solution)/shard_map/ppermute | solution.py:463
  28.5 0.1 collective-permute-start.12
  28.6 2.2 %collective-permute-start.11 = (f32[16,256]{1,0:T(8,128)S(1)}, f32[16,256]{1,0:T(8,128)S(1)}, u32[]{:S(2)}, u32[]{:S(2)}) collective-permute-start(f32[16,256]{1,0:T(8,128)S(1)} %get-tuple-element.56), channel_id=1, source_target_pairs={{0,4},{4,0},{8,12},{12,8},{16,20},{20,16},{24,28},{28,24},{1,5},{5... | collective-permute-start | bytes 49160 | tf_op jit(solution)/shard_map/ppermute | solution.py:463
  30.8 1.2 %collective-permute-done.13 = f32[16,256]{1,0:T(8,128)S(1)} collective-permute-done((f32[16,256]{1,0:T(8,128)S(1)}, f32[16,256]{1,0:T(8,128)S(1)}, u32[]{:S(2)}, u32[]{:S(2)}) %collective-permute-start.13) | collective-permute-done | bytes 16416 | tf_op jit(solution)/shard_map/ppermute | solution.py:463
  32.0 0.3 collective-permute-done.12
  32.3 0.2 collective-permute-done.11
  32.5 3.0 %collective-permute-start.14 = (f32[16,256]{1,0:T(8,128)S(1)}, f32[16,256]{1,0:T(8,128)S(1)}, u32[]{:S(2)}, u32[]{:S(2)}) collective-permute-start(f32[16,256]{1,0:T(8,128)S(1)} %add_add_fusion), channel_id=1, source_target_pairs={{0,16},{4,20},{8,24},{12,28},{16,0},{20,4},{24,8},{28,12},{1,17},{... | collective-permute-start | bytes 49160 | tf_op jit(solution)/shard_map/ppermute | solution.py:463
  35.5 1.7 %collective-permute-done.14 = f32[16,256]{1,0:T(8,128)S(1)} collective-permute-done((f32[16,256]{1,0:T(8,128)S(1)}, f32[16,256]{1,0:T(8,128)S(1)}, u32[]{:S(2)}, u32[]{:S(2)}) %collective-permute-start.14) | collective-permute-done | bytes 16416 | tf_op jit(solution)/shard_map/ppermute | solution.py:463
  37.2 3.3 %first.1 = (f32[32,512]{1,0:T(8,128)S(1)}, f32[32,512]{1,0:T(8,128)S(1)}, f32[2,32,512]{2,1,0:T(8,128)S(1)}, f32[8,512]{1,0:T(8,128)S(1)}) custom-call(bf16[16,8,256,256]{3,2,1,0:T(8,128)(2,1)S(1)} %get-tuple-element.52.k_mat, s32[1,128]{1,0:T(1,128)S(1)} %get-tuple-element.53.refs_0_.list_v, s32[1,128]{1,0:T(1,128)S(1)} %get-tuple-element.54.refs_1_.list_v, ...), custom_call_target="tpu_custom_call" | custom-call | flops 536870912 | bytes 8388608 | tf_op jit(solution)/shard_map/first/pallas_call | solution.py:605
  40.6 1.3 %collective-permute-done.15.got = f32[2,32,512]{2,1,0:T(8,128)S(1)} collective-permute-done((f32[2,32,512]{2,1,0:T(8,128)S(1)}, f32[2,32,512]{2,1,0:T(8,128)S(1)}, u32[]{:S(2)}, u32[]{:S(2)}) %collective-permute-start.15) | collective-permute-done | bytes 131104 | tf_op jit(solution)/shard_map/ppermute | solution.py:463
  42.0 1.5 %collective-permute-start.16 = (bf16[112,512]{1,0:T(8,128)(2,1)S(1)}, bf16[112,512]{1,0:T(8,128)(2,1)S(1)}, u32[]{:S(2)}, u32[]{:S(2)}) collective-permute-start(bf16[112,512]{1,0:T(8,128)(2,1)S(1)} %get-tuple-element.63), channel_id=1, source_target_pairs={{0,2},{1,3},{2,0},{3,1},{4,6},{5,7},{6,4},{7,5},{8,10},{9,11},{10,... | collective-permute-start | bytes 344072 | tf_op jit(solution)/shard_map/ppermute | solution.py:463
  43.6 3.7 %collective-permute-done.16.far = bf16[112,512]{1,0:T(8,128)(2,1)S(1)} collective-permute-done((bf16[112,512]{1,0:T(8,128)(2,1)S(1)}, bf16[112,512]{1,0:T(8,128)(2,1)S(1)}, u32[]{:S(2)}, u32[]{:S(2)}) %collective-permute-start.16) | collective-permute-done | bytes 114720 | tf_op jit(solution)/shard_map/ppermute | solution.py:463
  47.4 3.0 %collective-permute-start.19 = (bf16[32,512]{1,0:T(8,128)(2,1)S(1)}, bf16[32,512]{1,0:T(8,128)(2,1)S(1)}, u32[]{:S(2)}, u32[]{:S(2)}) collective-permute-start(bf16[32,512]{1,0:T(8,128)(2,1)S(1)} %get-tuple-element.66), channel_id=1, source_target_pairs={{0,16},{4,20},{8,24},{12,28},{16,0},{20,4},{24,8},{28,12},{1,17},{... | collective-permute-start | bytes 98312 | tf_op jit(solution)/shard_map/ppermute | solution.py:463
  50.4 1.5 %second.3 = bf16[4,32,512]{2,1,0:T(8,128)(2,1)S(1)} custom-call(bf16[16,8,256,256]{3,2,1,0:T(8,128)(2,1)S(1)} %get-tuple-element.52.k_mat, s32[1,128]{1,0:T(1,128)S(1)} %get-tuple-element.54.refs_1_.list_v, f32[32,2048]{1,0:T(8,128)S(1)} %copy-done, f32[2,40,512]{2,1,0:T(8,128)S(1)} %get-tuple-element.64.s1_own, f32[2,40,512]{2,1,0:T(8,128)S(1)} %collective-permute-done.17.s1_got), custom_call_target="tpu_custom_call" | custom-call | flops 268435456 | bytes 4194304 | tf_op jit(solution)/shard_map/second/pallas_call | solution.py:643
  51.9 0.9 %collective-permute-start.18 = (bf16[4,32,512]{2,1,0:T(8,128)(2,1)S(1)}, bf16[4,32,512]{2,1,0:T(8,128)(2,1)S(1)}, u32[]{:S(2)}, u32[]{:S(2)}) collective-permute-start(bf16[4,32,512]{2,1,0:T(8,128)(2,1)S(1)} %second.3), channel_id=1, source_target_pairs={{0,4},{4,0},{8,12},{12,8},{16,20},{20,16},{24,28},{28,24},{1,5},{5... | collective-permute-start | bytes 393224 | tf_op jit(solution)/shard_map/ppermute | solution.py:463
  52.8 1.3 %collective-permute-start.20 = (bf16[2,32,512]{2,1,0:T(8,128)(2,1)S(1)}, bf16[2,32,512]{2,1,0:T(8,128)(2,1)S(1)}, u32[]{:S(2)}, u32[]{:S(2)}) collective-permute-start(bf16[2,32,512]{2,1,0:T(8,128)(2,1)S(1)} %pad_maximum_fusion.3.refs_0_), channel_id=1, source_target_pairs={{0,8},{4,12},{8,0},{12,4},{16,24},{20,28},{24,16},{28,20},{1,9},{5... | collective-permute-start | bytes 196616 | tf_op jit(solution)/shard_map/ppermute | solution.py:463
  54.2 1.5 %second.2.z_same = f32[4,32,512]{2,1,0:T(8,128)S(1)} custom-call(bf16[16,8,256,256]{3,2,1,0:T(8,128)(2,1)S(1)} %get-tuple-element.52.k_mat, s32[1,128]{1,0:T(1,128)S(1)} %get-tuple-element.53.refs_0_.list_v, f32[32,2048]{1,0:T(8,128)S(1)} %copy-done, f32[2,40,512]{2,1,0:T(8,128)S(1)} %get-tuple-element.64.s1_own, ...), custom_call_target="tpu_custom_call" | custom-call | flops 268435456 | bytes 4194304 | tf_op jit(solution)/shard_map/second/pallas_call | solution.py:643
  55.7 1.5 %collective-permute-done.20.refs_1_ = bf16[2,32,512]{2,1,0:T(8,128)(2,1)S(1)} collective-permute-done((bf16[2,32,512]{2,1,0:T(8,128)(2,1)S(1)}, bf16[2,32,512]{2,1,0:T(8,128)(2,1)S(1)}, u32[]{:S(2)}, u32[]{:S(2)}) %collective-permute-start.20) | collective-permute-done | bytes 65568 | tf_op jit(solution)/shard_map/ppermute | solution.py:463
  57.2 0.2 meet.1
  57.4 3.4 %collective-permute-start.21 = (bf16[32,640]{1,0:T(8,128)(2,1)S(1)}, bf16[32,640]{1,0:T(8,128)(2,1)S(1)}, u32[]{:S(2)}, u32[]{:S(2)}) collective-permute-start(bf16[32,640]{1,0:T(8,128)(2,1)S(1)} %get-tuple-element.73), channel_id=1, source_target_pairs={{0,24},{4,28},{8,16},{12,20},{16,8},{20,12},{24,0},{28,4},{1,25},{... | collective-permute-start | bytes 122888 | tf_op jit(solution)/shard_map/ppermute | solution.py:463
  60.8 1.0 %collective-permute-start.23 = (bf16[32,640]{1,0:T(8,128)(2,1)S(1)}, bf16[32,640]{1,0:T(8,128)(2,1)S(1)}, u32[]{:S(2)}, u32[]{:S(2)}) collective-permute-start(bf16[32,640]{1,0:T(8,128)(2,1)S(1)} %get-tuple-element.75), channel_id=1, source_target_pairs={{0,8},{4,12},{8,0},{12,4},{16,24},{20,28},{24,16},{28,20},{1,9},{5... | collective-permute-start | bytes 122888 | tf_op jit(solution)/shard_map/ppermute | solution.py:463
  61.9 1.5 %collective-permute-done.21.refs_0_ = bf16[32,640]{1,0:T(8,128)(2,1)S(1)} collective-permute-done((bf16[32,640]{1,0:T(8,128)(2,1)S(1)}, bf16[32,640]{1,0:T(8,128)(2,1)S(1)}, u32[]{:S(2)}, u32[]{:S(2)}) %collective-permute-start.21) | collective-permute-done | bytes 40992 | tf_op jit(solution)/shard_map/ppermute | solution.py:463
  63.4 2.4 %collective-permute-done.22.refs_1_ = bf16[32,640]{1,0:T(8,128)(2,1)S(1)} collective-permute-done((bf16[32,640]{1,0:T(8,128)(2,1)S(1)}, bf16[32,640]{1,0:T(8,128)(2,1)S(1)}, u32[]{:S(2)}, u32[]{:S(2)}) %collective-permute-start.22) | collective-permute-done | bytes 40992 | tf_op jit(solution)/shard_map/ppermute | solution.py:463
  65.7 0.1 products.1
  65.8 1.1 %collective-permute-start.25 = (f32[32,640]{1,0:T(8,128)S(1)}, f32[32,640]{1,0:T(8,128)S(1)}, u32[]{:S(2)}, u32[]{:S(2)}) collective-permute-start(f32[32,640]{1,0:T(8,128)S(1)} %get-tuple-element.76), channel_id=1, source_target_pairs={{0,2},{1,3},{2,0},{3,1},{4,6},{5,7},{6,4},{7,5},{8,10},{9,11},{10,... | collective-permute-start | bytes 245768 | tf_op jit(solution)/shard_map/ppermute | solution.py:463
  66.9 1.4 %collective-permute-start.26 = (f32[32,128]{1,0:T(8,128)S(1)}, f32[32,128]{1,0:T(8,128)S(1)}, u32[]{:S(2)}, u32[]{:S(2)}) collective-permute-start(f32[32,128]{1,0:T(8,128)S(1)} %get-tuple-element.77), channel_id=1, source_target_pairs={{0,6},{1,7},{2,4},{3,5},{4,2},{5,3},{6,0},{7,1},{8,14},{9,15},{10,... | collective-permute-start | bytes 49160 | tf_op jit(solution)/shard_map/ppermute | solution.py:473
  68.3 1.0 %collective-permute-start.24 = (f32[32,128]{1,0:T(8,128)S(1)}, f32[32,128]{1,0:T(8,128)S(1)}, u32[]{:S(2)}, u32[]{:S(2)}) collective-permute-start(f32[32,128]{1,0:T(8,128)S(1)} %get-tuple-element.77), channel_id=1, source_target_pairs={{0,4},{4,0},{8,12},{12,8},{16,20},{20,16},{24,28},{28,24},{1,5},{5... | collective-permute-start | bytes 49160 | tf_op jit(solution)/shard_map/ppermute | solution.py:463
  69.4 2.2 %collective-permute-done.26 = f32[32,128]{1,0:T(8,128)S(1)} collective-permute-done((f32[32,128]{1,0:T(8,128)S(1)}, f32[32,128]{1,0:T(8,128)S(1)}, u32[]{:S(2)}, u32[]{:S(2)}) %collective-permute-start.26) | collective-permute-done | bytes 16416 | tf_op jit(solution)/shard_map/ppermute | solution.py:473
  71.6 0.5 collective-permute-done.24
  72.2 1.4 %collective-permute-done.27.refs_1_ = f32[2,32,640]{2,1,0:T(8,128)S(1)} collective-permute-done((f32[2,32,640]{2,1,0:T(8,128)S(1)}, f32[2,32,640]{2,1,0:T(8,128)S(1)}, u32[]{:S(2)}, u32[]{:S(2)}) %collective-permute-start.27) | collective-permute-done | bytes 163872 | tf_op jit(solution)/shard_map/ppermute | solution.py:463
  73.6 1.2 %final.1 = (f32[32,2048]{1,0:T(8,128)}, f32[32,2048]{1,0:T(8,128)}) custom-call(f32[32,2048]{1,0:T(8,128)S(1)} %copy-done, f32[2,40,512]{2,1,0:T(8,128)S(1)} %get-tuple-element.64.s1_own, f32[2,40,512]{2,1,0:T(8,128)S(1)} %collective-permute-done.17.s1_got, f32[2,32,640]{2,1,0:T(8,128)S(1)} %pad_maximum_fusion.1.refs_0_, ...), custom_call_target="tpu_custom_call" | custom-call | tf_op jit(solution)/shard_map/final/pallas_call | solution.py:706
  (44 shorter events, 0.9 us)
Async XLA Ops:
  0.6 5.7 %collective-permute-start = (s32[8,6]{1,0:T(8,128)}, s32[8,6]{1,0:T(8,128)S(1)}, u32[]{:S(2)}, u32[]{:S(2)}) collective-permute-start(s32[8,6]{1,0:T(8,128)} %param.3), channel_id=1, source_target_pairs={{0,1},{1,0},{2,3},{3,2},{4,5},{5,4},{6,7},{7,6},{8,9},{9,8},{10,11... | collective-permute-start | bytes 584 | tf_op jit(solution)/shard_map/ppermute | solution.py:463
  1.1 5.3 %collective-permute-start.2 = (s32[8,6]{1,0:T(8,128)}, s32[8,6]{1,0:T(8,128)S(1)}, u32[]{:S(2)}, u32[]{:S(2)}) collective-permute-start(s32[8,6]{1,0:T(8,128)} %param.3), channel_id=1, source_target_pairs={{0,3},{1,2},{2,1},{3,0},{4,7},{5,6},{6,5},{7,4},{8,11},{9,10},{10,... | collective-permute-start | bytes 584 | tf_op jit(solution)/shard_map/ppermute | solution.py:463
  3.8 3.8 %collective-permute-start.1 = (s32[8,6]{1,0:T(8,128)}, s32[8,6]{1,0:T(8,128)S(1)}, u32[]{:S(2)}, u32[]{:S(2)}) collective-permute-start(s32[8,6]{1,0:T(8,128)} %param.3), channel_id=1, source_target_pairs={{0,2},{1,3},{2,0},{3,1},{4,6},{5,7},{6,4},{7,5},{8,10},{9,11},{10,... | collective-permute-start | bytes 584 | tf_op jit(solution)/shard_map/ppermute | solution.py:463
  7.9 8.1 %collective-permute-start.5 = (bf16[16,640]{1,0:T(8,128)(2,1)S(1)}, bf16[16,640]{1,0:T(8,128)(2,1)S(1)}, u32[]{:S(2)}, u32[]{:S(2)}) collective-permute-start(bf16[16,640]{1,0:T(8,128)(2,1)S(1)} %pad_maximum_fusion.4), channel_id=1, source_target_pairs={{0,24},{4,28},{8,16},{12,20},{16,8},{20,12},{24,0},{28,4},{1,25},{... | collective-permute-start | bytes 61448 | tf_op jit(solution)/shard_map/ppermute | solution.py:463
  11.6 5.2 %collective-permute-start.4 = (bf16[16,640]{1,0:T(8,128)(2,1)S(1)}, bf16[16,640]{1,0:T(8,128)(2,1)S(1)}, u32[]{:S(2)}, u32[]{:S(2)}) collective-permute-start(bf16[16,640]{1,0:T(8,128)(2,1)S(1)} %pad_maximum_fusion.4), channel_id=1, source_target_pairs={{0,16},{4,20},{8,24},{12,28},{16,0},{20,4},{24,8},{28,12},{1,17},{... | collective-permute-start | bytes 61448 | tf_op jit(solution)/shard_map/ppermute | solution.py:463
  11.6 5.2 %collective-permute-start.3 = (bf16[16,640]{1,0:T(8,128)(2,1)S(1)}, bf16[16,640]{1,0:T(8,128)(2,1)S(1)}, u32[]{:S(2)}, u32[]{:S(2)}) collective-permute-start(bf16[16,640]{1,0:T(8,128)(2,1)S(1)} %pad_maximum_fusion.4), channel_id=1, source_target_pairs={{0,8},{4,12},{8,0},{12,4},{16,24},{20,28},{24,16},{28,20},{1,9},{5... | collective-permute-start | bytes 61448 | tf_op jit(solution)/shard_map/ppermute | solution.py:463
  12.3 10.6 %collective-permute-start.9 = (f32[32,512]{1,0:T(8,128)S(1)}, f32[32,512]{1,0:T(8,128)S(1)}, u32[]{:S(2)}, u32[]{:S(2)}) collective-permute-start(f32[32,512]{1,0:T(8,128)S(1)} %constant_dynamic-slice_fusion.t_ref), channel_id=1, source_target_pairs={{0,24},{4,28},{8,16},{12,20},{16,8},{20,12},{24,0},{28,4},{1,25},{... | collective-permute-start | bytes 196616 | tf_op jit(solution)/shard_map/ppermute | solution.py:463
  15.9 7.0 %collective-permute-start.8 = (f32[32,512]{1,0:T(8,128)S(1)}, f32[32,512]{1,0:T(8,128)S(1)}, u32[]{:S(2)}, u32[]{:S(2)}) collective-permute-start(f32[32,512]{1,0:T(8,128)S(1)} %constant_dynamic-slice_fusion.t_ref), channel_id=1, source_target_pairs={{0,16},{4,20},{8,24},{12,28},{16,0},{20,4},{24,8},{28,12},{1,17},{... | collective-permute-start | bytes 196616 | tf_op jit(solution)/shard_map/ppermute | solution.py:463
  15.9 7.0 %collective-permute-start.7 = (f32[32,512]{1,0:T(8,128)S(1)}, f32[32,512]{1,0:T(8,128)S(1)}, u32[]{:S(2)}, u32[]{:S(2)}) collective-permute-start(f32[32,512]{1,0:T(8,128)S(1)} %constant_dynamic-slice_fusion.t_ref), channel_id=1, source_target_pairs={{0,8},{4,12},{8,0},{12,4},{16,24},{20,28},{24,16},{28,20},{1,9},{5... | collective-permute-start | bytes 196616 | tf_op jit(solution)/shard_map/ppermute | solution.py:463
  16.8 6.2 %collective-permute-start.6 = (bf16[4,16,640]{2,1,0:T(8,128)(2,1)S(1)}, bf16[4,16,640]{2,1,0:T(8,128)(2,1)S(1)}, u32[]{:S(2)}, u32[]{:S(2)}) collective-permute-start(bf16[4,16,640]{2,1,0:T(8,128)(2,1)S(1)} %pad_maximum_fusion.2.refs_1_), channel_id=1, source_target_pairs={{0,4},{4,0},{8,12},{12,8},{16,20},{20,16},{24,28},{28,24},{1,5},{5... | collective-permute-start | bytes 245768 | tf_op jit(solution)/shard_map/ppermute | solution.py:463
  27.2 23.2 %copy-start = (f32[32,2048]{1,0:T(8,128)S(1)}, f32[32,2048]{1,0:T(8,128)}, u32[]{:S(2)}) copy-start(f32[32,2048]{1,0:T(8,128)} %t_ref.5) | copy-start | bytes 786436
  27.2 4.7 %collective-permute-start.13 = (f32[16,256]{1,0:T(8,128)S(1)}, f32[16,256]{1,0:T(8,128)S(1)}, u32[]{:S(2)}, u32[]{:S(2)}) collective-permute-start(f32[16,256]{1,0:T(8,128)S(1)} %get-tuple-element.56), channel_id=1, source_target_pairs={{0,12},{4,8},{8,4},{12,0},{16,28},{20,24},{24,20},{28,16},{1,13},{... | collective-permute-start | bytes 49160 | tf_op jit(solution)/shard_map/ppermute | solution.py:463
  28.5 3.7 %collective-permute-start.12 = (f32[16,256]{1,0:T(8,128)S(1)}, f32[16,256]{1,0:T(8,128)S(1)}, u32[]{:S(2)}, u32[]{:S(2)}) collective-permute-start(f32[16,256]{1,0:T(8,128)S(1)} %get-tuple-element.56), channel_id=1, source_target_pairs={{0,8},{4,12},{8,0},{12,4},{16,24},{20,28},{24,16},{28,20},{1,9},{5... | collective-permute-start | bytes 49160 | tf_op jit(solution)/shard_map/ppermute | solution.py:463
  28.6 3.9 %collective-permute-start.11 = (f32[16,256]{1,0:T(8,128)S(1)}, f32[16,256]{1,0:T(8,128)S(1)}, u32[]{:S(2)}, u32[]{:S(2)}) collective-permute-start(f32[16,256]{1,0:T(8,128)S(1)} %get-tuple-element.56), channel_id=1, source_target_pairs={{0,4},{4,0},{8,12},{12,8},{16,20},{20,16},{24,28},{28,24},{1,5},{5... | collective-permute-start | bytes 49160 | tf_op jit(solution)/shard_map/ppermute | solution.py:463
  30.8 6.4 %collective-permute-start.10 = (f32[4,32,512]{2,1,0:T(8,128)S(1)}, f32[4,32,512]{2,1,0:T(8,128)S(1)}, u32[]{:S(2)}, u32[]{:S(2)}) collective-permute-start(f32[4,32,512]{2,1,0:T(8,128)S(1)} %pad_maximum_fusion.refs_2_.t_same), channel_id=1, source_target_pairs={{0,4},{4,0},{8,12},{12,8},{16,20},{20,16},{24,28},{28,24},{1,5},{5... | collective-permute-start | bytes 786440 | tf_op jit(solution)/shard_map/ppermute | solution.py:463
  32.5 4.7 %collective-permute-start.14 = (f32[16,256]{1,0:T(8,128)S(1)}, f32[16,256]{1,0:T(8,128)S(1)}, u32[]{:S(2)}, u32[]{:S(2)}) collective-permute-start(f32[16,256]{1,0:T(8,128)S(1)} %add_add_fusion), channel_id=1, source_target_pairs={{0,16},{4,20},{8,24},{12,28},{16,0},{20,4},{24,8},{28,12},{1,17},{... | collective-permute-start | bytes 49160 | tf_op jit(solution)/shard_map/ppermute | solution.py:463
  40.6 1.4 %collective-permute-start.15 = (f32[2,32,512]{2,1,0:T(8,128)S(1)}, f32[2,32,512]{2,1,0:T(8,128)S(1)}, u32[]{:S(2)}, u32[]{:S(2)}) collective-permute-start(f32[2,32,512]{2,1,0:T(8,128)S(1)} %get-tuple-element.59), channel_id=1, source_target_pairs={{0,1},{1,0},{2,3},{3,2},{4,5},{5,4},{6,7},{7,6},{8,9},{9,8},{10,11... | collective-permute-start | bytes 393224 | tf_op jit(solution)/shard_map/ppermute | solution.py:463
  42.0 5.3 %collective-permute-start.16 = (bf16[112,512]{1,0:T(8,128)(2,1)S(1)}, bf16[112,512]{1,0:T(8,128)(2,1)S(1)}, u32[]{:S(2)}, u32[]{:S(2)}) collective-permute-start(bf16[112,512]{1,0:T(8,128)(2,1)S(1)} %get-tuple-element.63), channel_id=1, source_target_pairs={{0,2},{1,3},{2,0},{3,1},{4,6},{5,7},{6,4},{7,5},{8,10},{9,11},{10,... | collective-permute-start | bytes 344072 | tf_op jit(solution)/shard_map/ppermute | solution.py:463
  47.3 3.1 %collective-permute-start.17 = (f32[2,40,512]{2,1,0:T(8,128)S(1)}, f32[2,40,512]{2,1,0:T(8,128)S(1)}, u32[]{:S(2)}, u32[]{:S(2)}) collective-permute-start(f32[2,40,512]{2,1,0:T(8,128)S(1)} %get-tuple-element.64.s1_own), channel_id=1, source_target_pairs={{0,1},{1,0},{2,3},{3,2},{4,5},{5,4},{6,7},{7,6},{8,9},{9,8},{10,11... | collective-permute-start | bytes 491528 | tf_op jit(solution)/shard_map/ppermute | solution.py:463
  47.4 5.4 %collective-permute-start.19 = (bf16[32,512]{1,0:T(8,128)(2,1)S(1)}, bf16[32,512]{1,0:T(8,128)(2,1)S(1)}, u32[]{:S(2)}, u32[]{:S(2)}) collective-permute-start(bf16[32,512]{1,0:T(8,128)(2,1)S(1)} %get-tuple-element.66), channel_id=1, source_target_pairs={{0,16},{4,20},{8,24},{12,28},{16,0},{20,4},{24,8},{28,12},{1,17},{... | collective-permute-start | bytes 98312 | tf_op jit(solution)/shard_map/ppermute | solution.py:463
  51.9 5.3 %collective-permute-start.18 = (bf16[4,32,512]{2,1,0:T(8,128)(2,1)S(1)}, bf16[4,32,512]{2,1,0:T(8,128)(2,1)S(1)}, u32[]{:S(2)}, u32[]{:S(2)}) collective-permute-start(bf16[4,32,512]{2,1,0:T(8,128)(2,1)S(1)} %second.3), channel_id=1, source_target_pairs={{0,4},{4,0},{8,12},{12,8},{16,20},{20,16},{24,28},{28,24},{1,5},{5... | collective-permute-start | bytes 393224 | tf_op jit(solution)/shard_map/ppermute | solution.py:463
  52.8 4.3 %collective-permute-start.20 = (bf16[2,32,512]{2,1,0:T(8,128)(2,1)S(1)}, bf16[2,32,512]{2,1,0:T(8,128)(2,1)S(1)}, u32[]{:S(2)}, u32[]{:S(2)}) collective-permute-start(bf16[2,32,512]{2,1,0:T(8,128)(2,1)S(1)} %pad_maximum_fusion.3.refs_0_), channel_id=1, source_target_pairs={{0,8},{4,12},{8,0},{12,4},{16,24},{20,28},{24,16},{28,20},{1,9},{5... | collective-permute-start | bytes 196616 | tf_op jit(solution)/shard_map/ppermute | solution.py:463
  57.4 5.9 %collective-permute-start.21 = (bf16[32,640]{1,0:T(8,128)(2,1)S(1)}, bf16[32,640]{1,0:T(8,128)(2,1)S(1)}, u32[]{:S(2)}, u32[]{:S(2)}) collective-permute-start(bf16[32,640]{1,0:T(8,128)(2,1)S(1)} %get-tuple-element.73), channel_id=1, source_target_pairs={{0,24},{4,28},{8,16},{12,20},{16,8},{20,12},{24,0},{28,4},{1,25},{... | collective-permute-start | bytes 122888 | tf_op jit(solution)/shard_map/ppermute | solution.py:463
  60.8 4.9 %collective-permute-start.22 = (bf16[32,640]{1,0:T(8,128)(2,1)S(1)}, bf16[32,640]{1,0:T(8,128)(2,1)S(1)}, u32[]{:S(2)}, u32[]{:S(2)}) collective-permute-start(bf16[32,640]{1,0:T(8,128)(2,1)S(1)} %get-tuple-element.74), channel_id=1, source_target_pairs={{0,16},{4,20},{8,24},{12,28},{16,0},{20,4},{24,8},{28,12},{1,17},{... | collective-permute-start | bytes 122888 | tf_op jit(solution)/shard_map/ppermute | solution.py:463
  60.8 4.9 %collective-permute-start.23 = (bf16[32,640]{1,0:T(8,128)(2,1)S(1)}, bf16[32,640]{1,0:T(8,128)(2,1)S(1)}, u32[]{:S(2)}, u32[]{:S(2)}) collective-permute-start(bf16[32,640]{1,0:T(8,128)(2,1)S(1)} %get-tuple-element.75), channel_id=1, source_target_pairs={{0,8},{4,12},{8,0},{12,4},{16,24},{20,28},{24,16},{28,20},{1,9},{5... | collective-permute-start | bytes 122888 | tf_op jit(solution)/shard_map/ppermute | solution.py:463
  65.8 6.2 %collective-permute-start.25 = (f32[32,640]{1,0:T(8,128)S(1)}, f32[32,640]{1,0:T(8,128)S(1)}, u32[]{:S(2)}, u32[]{:S(2)}) collective-permute-start(f32[32,640]{1,0:T(8,128)S(1)} %get-tuple-element.76), channel_id=1, source_target_pairs={{0,2},{1,3},{2,0},{3,1},{4,6},{5,7},{6,4},{7,5},{8,10},{9,11},{10,... | collective-permute-start | bytes 245768 | tf_op jit(solution)/shard_map/ppermute | solution.py:463
  66.9 4.6 %collective-permute-start.26 = (f32[32,128]{1,0:T(8,128)S(1)}, f32[32,128]{1,0:T(8,128)S(1)}, u32[]{:S(2)}, u32[]{:S(2)}) collective-permute-start(f32[32,128]{1,0:T(8,128)S(1)} %get-tuple-element.77), channel_id=1, source_target_pairs={{0,6},{1,7},{2,4},{3,5},{4,2},{5,3},{6,0},{7,1},{8,14},{9,15},{10,... | collective-permute-start | bytes 49160 | tf_op jit(solution)/shard_map/ppermute | solution.py:473
  68.3 3.7 %collective-permute-start.24 = (f32[32,128]{1,0:T(8,128)S(1)}, f32[32,128]{1,0:T(8,128)S(1)}, u32[]{:S(2)}, u32[]{:S(2)}) collective-permute-start(f32[32,128]{1,0:T(8,128)S(1)} %get-tuple-element.77), channel_id=1, source_target_pairs={{0,4},{4,0},{8,12},{12,8},{16,20},{20,16},{24,28},{28,24},{1,5},{5... | collective-permute-start | bytes 49160 | tf_op jit(solution)/shard_map/ppermute | solution.py:463
  72.1 1.5 %collective-permute-start.27 = (f32[2,32,640]{2,1,0:T(8,128)S(1)}, f32[2,32,640]{2,1,0:T(8,128)S(1)}, u32[]{:S(2)}, u32[]{:S(2)}) collective-permute-start(f32[2,32,640]{2,1,0:T(8,128)S(1)} %pad_maximum_fusion.1.refs_0_), channel_id=1, source_target_pairs={{0,1},{1,0},{2,3},{3,2},{4,5},{5,4},{6,7},{7,6},{8,9},{9,8},{10,11... | collective-permute-start | bytes 491528 | tf_op jit(solution)/shard_map/ppermute | solution.py:463
